TPU v7x, 32 devices: a whole 2x2x4 slice. The times are simulated.
32 devices in a mesh: runs: 2 (over x), line: 16 (over z, y, core).
Axes of the slice: x: 2, y: 2, z: 4, core: 2. Of those that a mesh axis runs over, the one named last changes fastest.
Arguments:
- velocity: float32 [3, 64, 128, 128], P(None, ('runs', 'line')), parts along dimension 1, may hold values from -6 to 6
- stress: float32 [6, 64, 128, 128], P(None, ('runs', 'line')), parts along dimension 1, may hold values from -6 to 6
- memory: float32 [6, 64, 128, 128], P(None, ('runs', 'line')), parts along dimension 1, may hold values from -4 to 4
- truck_loads: float32 [512, 128], P(('runs', 'line')), parts along dimension 0, may hold values from -8 to 8
- pier_panels: float32 [16, 16, 1536], P('line', 'runs'), parts along dimension 1, may hold values from -8 to 8
- lame_lambda: float32 [8], replicated, may hold values from 0.3 to 1
- lame_mu: float32 [8], replicated, may hold values from 0.2 to 0.6
- buoyancy: float32 [8], replicated, may hold values from 0.5 to 1.5
- relax_rate: float32 [8], replicated, may hold values from 0.3 to 3
- defect_mu: float32 [8], replicated, may hold values from 0.05 to 0.4
- layer: int32 [128], replicated, may hold values from 0 to 7, never falling along the last dimension, each value on 1 to 32 neighbouring positions
- truck_entry: int32 [6, 512], P(None, ('runs', 'line')), parts along dimension 1, may hold values from -1 to 15
- truck_cell: int32 [6, 512], P(None, ('runs', 'line')), parts along dimension 1, may hold values from 0 to 1
- pier_cell: int32 [8], replicated, may hold values from 0 to 31
Outputs:
- velocity_out: float32 [3, 64, 128, 128], P(None, ('runs', 'line')), parts along dimension 1
- stress_out: float32 [6, 64, 128, 128], P(None, ('runs', 'line')), parts along dimension 1
- memory_out: float32 [6, 64, 128, 128], P(None, ('runs', 'line')), parts along dimension 1
There are 2 independent parts, one for each index of `runs`. A program takes and returns all parts, laid end to end along the dimension named above; an argument that names none is the same for every part. Nothing has to cross between parts.
Inputs may be any that keep to these rules, and one draw needn't show every extreme that they name: `truck_entry`: -1 keeps a slot's own truck; k takes slot k of the tile behind. `truck_cell`: A cell within the tile. `layer`: never falls with depth.
All inputs are finite; a program needn't handle non-finite values.
Results may differ from a plain program's by a relative error of at most 0.0001.
Values sent between devices are 32-bit elements; how exact they have to be, the bound alone decides.
No kernel may reach another device: no remote copies, remote signals or barrier semaphores. Data moves between devices by JAX's collectives and lax.ppermute only.
A program may use at most 64 MiB of HBM per device.

v0:
```python
import jax
import jax.numpy as jnp
from jax import lax
from jax.sharding import PartitionSpec as P

STEPS = 6
FY = 8
FZ = 64


time_step = 0.25


def passed_along(block, axis, distance):
    devices = range(lax.axis_size(axis))
    route = [(i - distance, i) for i in devices if i - distance in devices]
    return lax.ppermute(block, axis, route)


def from_root(block, axis, owner):
    block = jnp.where(lax.axis_index(axis) == owner, block, jnp.zeros_like(block))
    return lax.psum(block, axis)


def behind(field, axis):
    size = field.shape[axis]
    head = jnp.zeros_like(lax.slice_in_dim(field, 0, 1, axis=axis))
    return jnp.concatenate([head, lax.slice_in_dim(field, 0, size - 1, axis=axis)], axis=axis)


def ahead(field, axis):
    size = field.shape[axis]
    tail = jnp.zeros_like(lax.slice_in_dim(field, 0, 1, axis=axis))
    return jnp.concatenate([lax.slice_in_dim(field, 1, size, axis=axis), tail], axis=axis)


def per_depth(layer, table):
    levels = jnp.arange(table.shape[0], dtype=jnp.int32)
    return jnp.sum(
        jnp.where(layer[:, None] == levels[None, :], table[None, :], jnp.float32(0.0)), axis=1
    )


def velocity_rates(stresses, ahead_xx, behind_xy, behind_xz):
    s_xx, s_yy, s_zz, s_xy, s_xz, s_yz = stresses
    rate_x = ahead_xx - s_xx + (s_xy - behind(s_xy, 1)) + (s_xz - behind(s_xz, 2))
    rate_y = s_xy - behind_xy + (ahead(s_yy, 1) - s_yy) + (s_yz - behind(s_yz, 2))
    rate_z = s_xz - behind_xz + (s_yz - behind(s_yz, 1)) + (ahead(s_zz, 2) - s_zz)
    return (rate_x, rate_y, rate_z)


def strain_rates(speeds, behind_ux, ahead_uy, ahead_uz):
    u_x, u_y, u_z = speeds
    e_xx = u_x - behind_ux
    e_yy = u_y - behind(u_y, 1)
    e_zz = u_z - behind(u_z, 2)
    e_xy = 0.5 * (ahead(u_x, 1) - u_x + (ahead_uy - u_y))
    e_xz = 0.5 * (ahead(u_x, 2) - u_x + (ahead_uz - u_z))
    e_yz = 0.5 * (ahead(u_y, 2) - u_y + (ahead(u_z, 1) - u_z))
    return (e_xx, e_yy, e_zz, e_xy, e_xz, e_yz)


def relax(stresses, memories, strains, lambda_z, shear_z, decay_z, defect_z):
    trace = strains[0] + strains[1] + strains[2]
    new_stress = []
    new_memory = []
    for comp in range(6):
        drive = 2.0 * shear_z * strains[comp] + memories[comp]
        if comp < 3:
            drive = drive + lambda_z * trace
        new_stress.append(stresses[comp] + time_step * drive)
        new_memory.append(
            memories[comp] * (1.0 - time_step * decay_z)
            - time_step * decay_z * 2.0 * defect_z * strains[comp]
        )
    return (new_stress, new_memory)


def body(
    velocity,
    stress,
    memory,
    truck_loads,
    pier_panels,
    lame_lambda,
    lame_mu,
    buoyancy,
    relax_rate,
    defect_mu,
    layer,
    truck_entry,
    truck_cell,
    pier_cell,
):
    width_x = velocity.shape[1]
    across = velocity.shape[2]
    slots = truck_loads.shape[0]
    lambda_z = per_depth(layer, lame_lambda)
    shear_z = per_depth(layer, lame_mu)
    buoy_z = per_depth(layer, buoyancy)
    decay_z = per_depth(layer, relax_rate)
    defect_z = per_depth(layer, defect_mu)
    speeds = [velocity[0], velocity[1], velocity[2]]
    stresses = [stress[comp] for comp in range(6)]
    memories = [memory[comp] for comp in range(6)]
    slot_ids = jnp.arange(slots, dtype=jnp.int32)
    local_cells = jnp.arange(width_x, dtype=jnp.int32)
    tile_index = lax.axis_index("line")
    global_cells = local_cells + tile_index * width_x
    pier_hit = (pier_cell[None, :] == global_cells[:, None]).astype(jnp.float32)
    corner = (across - FY) // 2
    truck_rows = truck_loads
    for step_index in range(STEPS):
        incoming = passed_along(truck_rows, "line", 1)
        entry = truck_entry[step_index]
        match = entry[:, None] == slot_ids[None, :]
        picked = jnp.sum(
            jnp.where(match[:, :, None], incoming[None, :, :], jnp.float32(0.0)), axis=1
        )
        truck_rows = jnp.where((entry >= 0)[:, None], picked, truck_rows)
        record = from_root(pier_panels, "line", step_index)[0]
        pier_flat = jnp.dot(pier_hit, record, precision=lax.Precision.HIGHEST)
        plane_xx = passed_along(stresses[0][0:1], "line", -1)
        plane_xy, plane_xz = passed_along((stresses[3][-1:], stresses[4][-1:]), "line", 1)
        ahead_xx = jnp.concatenate([stresses[0][1:], plane_xx], axis=0)
        behind_xy = jnp.concatenate([plane_xy, stresses[3][:-1]], axis=0)
        behind_xz = jnp.concatenate([plane_xz, stresses[4][:-1]], axis=0)
        rates = velocity_rates(stresses, ahead_xx, behind_xy, behind_xz)
        pier_force = pier_flat.reshape(width_x, 3, FY, FZ)
        for comp in range(3):
            moved = speeds[comp] + time_step * buoy_z * rates[comp]
            speeds[comp] = moved.at[:, corner : corner + FY, 0:FZ].add(
                time_step * pier_force[:, comp]
            )
        plane_ux = passed_along(speeds[0][-1:], "line", 1)
        plane_uy, plane_uz = passed_along((speeds[1][0:1], speeds[2][0:1]), "line", -1)
        behind_ux = jnp.concatenate([plane_ux, speeds[0][:-1]], axis=0)
        ahead_uy = jnp.concatenate([speeds[1][1:], plane_uy], axis=0)
        ahead_uz = jnp.concatenate([speeds[2][1:], plane_uz], axis=0)
        strains = strain_rates(speeds, behind_ux, ahead_uy, ahead_uz)
        stresses, memories = relax(
            stresses, memories, strains, lambda_z, shear_z, decay_z, defect_z
        )
        truck_hit = (truck_cell[step_index][None, :] == local_cells[:, None]).astype(jnp.float32)
        surface = jnp.dot(truck_hit, truck_rows, precision=lax.Precision.HIGHEST)
        stresses[2] = stresses[2].at[:, :, 0].add(time_step * surface)
    return (jnp.stack(speeds), jnp.stack(stresses), jnp.stack(memories))


def solution(mesh):
    placed = (
        P(None, ("runs", "line"), None, None),
        P(None, ("runs", "line"), None, None),
        P(None, ("runs", "line"), None, None),
        P(("runs", "line"), None),
        P("line", "runs", None),
        P(),
        P(),
        P(),
        P(),
        P(),
        P(),
        P(None, ("runs", "line")),
        P(None, ("runs", "line")),
        P(),
    )
    return jax.shard_map(
        body,
        mesh=mesh,
        in_specs=placed,
        out_specs=(
            P(None, ("runs", "line"), None, None),
            P(None, ("runs", "line"), None, None),
            P(None, ("runs", "line"), None, None),
        ),
        check_vma=False,
    )
```

profile of v0, /device:TPU:17, one launch (start us, length us, event | category | flops | bytes accessed | tf_op | source)
XLA Modules:
  0.0 301.8 jit_solution(15321346041309461195)
XLA Ops:
  8.3 2.6 collective-permute-start
  10.9 3.0 %collective-permute-start.2 = (f32[1,128,128]{2,1,0:T(8,128)S(1)}, f32[1,128,128]{2,1,0:T(8,128)S(1)}, u32[]{:S(2)}, u32[]{:S(2)}) collective-permute-start(f32[1,128,128]{2,1,0:T(8,128)S(1)} %get-tuple-element.423), channel_id=1, source_target_pairs={{0,1},{1,2},{2,3},{3,4},{4,5},{5,6},{6,7},{7,8},{8,9},{9,10},{10,1... | collective-permute-start | bytes 196616 | tf_op jit(solution)/shard_map/ppermute | solution.py:17
  13.9 2.4 collective-permute-start.3
  16.3 3.9 %collective-permute-start.10 = (f32[16,128]{1,0:T(8,128)S(1)}, f32[16,128]{1,0:T(8,128)S(1)}, u32[]{:S(2)}, u32[]{:S(2)}) collective-permute-start(f32[16,128]{1,0:T(8,128)S(1)} %copy-done.113), channel_id=1, source_target_pairs={{0,1},{1,2},{2,3},{3,4},{4,5},{5,6},{6,7},{7,8},{8,9},{9,10},{10,1... | collective-permute-start | bytes 24584 | tf_op jit(solution)/shard_map/ppermute | solution.py:17
  28.2 1.9 collective-permute-start.17
  31.4 3.8 %collective-permute-start.24 = (f32[16,128]{1,0:T(8,128)S(1)}, f32[16,128]{1,0:T(8,128)S(1)}, u32[]{:S(2)}, u32[]{:S(2)}) collective-permute-start(f32[16,128]{1,0:T(8,128)S(1)} %broadcast_select_fusion.3), channel_id=1, source_target_pairs={{0,1},{1,2},{2,3},{3,4},{4,5},{5,6},{6,7},{7,8},{8,9},{9,10},{10,1... | collective-permute-start | bytes 24584 | tf_op jit(solution)/shard_map/ppermute | solution.py:17
  36.4 4.1 %collective-permute-start.31 = (f32[16,128]{1,0:T(8,128)S(1)}, f32[16,128]{1,0:T(8,128)S(1)}, u32[]{:S(2)}, u32[]{:S(2)}) collective-permute-start(f32[16,128]{1,0:T(8,128)S(1)} %broadcast_select_fusion.2), channel_id=1, source_target_pairs={{0,1},{1,2},{2,3},{3,4},{4,5},{5,6},{6,7},{7,8},{8,9},{9,10},{10,1... | collective-permute-start | bytes 24584 | tf_op jit(solution)/shard_map/ppermute | solution.py:17
  41.8 3.9 %collective-permute-start.37 = (f32[16,128]{1,0:T(8,128)S(1)}, f32[16,128]{1,0:T(8,128)S(1)}, u32[]{:S(2)}, u32[]{:S(2)}) collective-permute-start(f32[16,128]{1,0:T(8,128)S(1)} %broadcast_select_fusion.1), channel_id=1, source_target_pairs={{0,1},{1,2},{2,3},{3,4},{4,5},{5,6},{6,7},{7,8},{8,9},{9,10},{10,1... | collective-permute-start | bytes 24584 | tf_op jit(solution)/shard_map/ppermute | solution.py:17
  48.0 2.9 collective-permute-start.39
  51.8 2.0 collective-permute-done.39
  55.2 59.2 %all-reduce.75.cloned.1.call-done = (f32[3,8,64,8]{2,3,1,0:T(8,128)}, f32[3,8,64,8]{2,3,1,0:T(8,128)}, f32[3,8,64,8]{2,3,1,0:T(8,128)}, f32[3,8,64,8]{2,3,1,0:T(...) async-done(((f32[3,8,64,8]{2,3,1,0:T(8,128)}, f32[3,8,64,8]{2,3,1,0:T(8,128)}, f32[3,8,64,8]{2,3,1,0:T(8,128)}, f32[3,8,64,8]{2,3,1,0:T(8,128)}, ...) | async-done | bytes 294928 | tf_op jit(solution)/shard_map/psum | solution.py:22
  114.4 1.1 fusion.142
  116.1 5.0 %collective-permute-start.1 = (f32[1,128,128]{2,1,0:T(8,128)S(1)}, f32[1,128,128]{2,1,0:T(8,128)}, u32[]{:S(2)}, u32[]{:S(2)}) collective-permute-start(f32[1,128,128]{2,1,0:T(8,128)S(1)} %get-tuple-element.503), channel_id=1, source_target_pairs={{0,1},{1,2},{2,3},{3,4},{4,5},{5,6},{6,7},{7,8},{8,9},{9,10},{10,1... | collective-permute-start | bytes 196616 | tf_op jit(solution)/shard_map/ppermute | solution.py:17
  121.6 1.9 collective-permute-start.5
  124.0 3.6 %collective-permute-start.6 = (f32[1,128,128]{2,1,0:T(8,128)S(1)}, f32[1,128,128]{2,1,0:T(8,128)S(1)}, u32[]{:S(2)}, u32[]{:S(2)}) collective-permute-start(f32[1,128,128]{2,1,0:T(8,128)S(1)} %get-tuple-element.508), channel_id=1, source_target_pairs={{1,0},{2,1},{3,2},{4,3},{5,4},{6,5},{7,6},{8,7},{9,8},{10,9},{11,1... | collective-permute-start | bytes 196616 | tf_op jit(solution)/shard_map/ppermute | solution.py:17
  132.9 2.1 collective-permute-start.9
  137.4 2.4 collective-permute-start.8
  141.8 2.1 collective-permute-start.4
  149.9 2.7 collective-permute-start.7
  152.6 2.6 collective-permute-start.13
  155.2 4.5 %collective-permute-start.12 = (f32[1,128,128]{2,1,0:T(8,128)S(1)}, f32[1,128,128]{2,1,0:T(8,128)S(1)}, u32[]{:S(2)}, u32[]{:S(2)}) collective-permute-start(f32[1,128,128]{2,1,0:T(8,128)S(1)} %get-tuple-element.486), channel_id=1, source_target_pairs={{1,0},{2,1},{3,2},{4,3},{5,4},{6,5},{7,6},{8,7},{9,8},{10,9},{11,1... | collective-permute-start | bytes 196616 | tf_op jit(solution)/shard_map/ppermute | solution.py:17
  162.2 1.9 collective-permute-start.15
  164.7 5.1 %collective-permute-start.16 = (f32[1,128,128]{2,1,0:T(8,128)}, f32[1,128,128]{2,1,0:T(8,128)}, u32[]{:S(2)}, u32[]{:S(2)}) collective-permute-start(f32[1,128,128]{2,1,0:T(8,128)} %get-tuple-element.495), channel_id=1, source_target_pairs={{0,1},{1,2},{2,3},{3,4},{4,5},{5,6},{6,7},{7,8},{8,9},{9,10},{10,1... | collective-permute-start | bytes 196616 | tf_op jit(solution)/shard_map/ppermute | solution.py:17
  173.4 1.9 collective-permute-start.11
  177.5 2.2 collective-permute-start.20
  183.2 3.3 %collective-permute-start.14 = (f32[1,128,128]{2,1,0:T(8,128)}, f32[1,128,128]{2,1,0:T(8,128)S(1)}, u32[]{:S(2)}, u32[]{:S(2)}) collective-permute-start(f32[1,128,128]{2,1,0:T(8,128)} %get-tuple-element.479), channel_id=1, source_target_pairs={{0,1},{1,2},{2,3},{3,4},{4,5},{5,6},{6,7},{7,8},{8,9},{9,10},{10,1... | collective-permute-start | bytes 196616 | tf_op jit(solution)/shard_map/ppermute | solution.py:17
  186.5 1.9 collective-permute-start.19
  189.8 3.6 %collective-permute-start.23 = (f32[1,128,128]{2,1,0:T(8,128)}, f32[1,128,128]{2,1,0:T(8,128)}, u32[]{:S(2)}, u32[]{:S(2)}) collective-permute-start(f32[1,128,128]{2,1,0:T(8,128)} %get-tuple-element.483), channel_id=1, source_target_pairs={{0,1},{1,2},{2,3},{3,4},{4,5},{5,6},{6,7},{7,8},{8,9},{9,10},{10,1... | collective-permute-start | bytes 196616 | tf_op jit(solution)/shard_map/ppermute | solution.py:17
  195.0 1.9 collective-permute-start.22
  200.5 2.5 collective-permute-start.18
  207.1 4.2 %collective-permute-start.27 = (f32[1,128,128]{2,1,0:T(8,128)}, f32[1,128,128]{2,1,0:T(8,128)}, u32[]{:S(2)}, u32[]{:S(2)}) collective-permute-start(f32[1,128,128]{2,1,0:T(8,128)} %get-tuple-element.478), channel_id=1, source_target_pairs={{1,0},{2,1},{3,2},{4,3},{5,4},{6,5},{7,6},{8,7},{9,8},{10,9},{11,1... | collective-permute-start | bytes 196616 | tf_op jit(solution)/shard_map/ppermute | solution.py:17
  213.4 2.1 collective-permute-start.21
  215.4 2.4 collective-permute-start.26
  219.0 1.6 multiply_add_fusion.10
  221.3 3.1 %collective-permute-start.30 = (f32[1,128,128]{2,1,0:T(8,128)}, f32[1,128,128]{2,1,0:T(8,128)}, u32[]{:S(2)}, u32[]{:S(2)}) collective-permute-start(f32[1,128,128]{2,1,0:T(8,128)} %get-tuple-element.471), channel_id=1, source_target_pairs={{0,1},{1,2},{2,3},{3,4},{4,5},{5,6},{6,7},{7,8},{8,9},{9,10},{10,1... | collective-permute-start | bytes 196616 | tf_op jit(solution)/shard_map/ppermute | solution.py:17
  225.3 3.0 collective-permute-start.29
  231.6 2.3 collective-permute-start.25
  239.3 3.3 %collective-permute-start.28 = (f32[1,128,128]{2,1,0:T(8,128)S(1)}, f32[1,128,128]{2,1,0:T(8,128)S(1)}, u32[]{:S(2)}, u32[]{:S(2)}) collective-permute-start(f32[1,128,128]{2,1,0:T(8,128)S(1)} %get-tuple-element.455), channel_id=1, source_target_pairs={{0,1},{1,2},{2,3},{3,4},{4,5},{5,6},{6,7},{7,8},{8,9},{9,10},{10,1... | collective-permute-start | bytes 196616 | tf_op jit(solution)/shard_map/ppermute | solution.py:17
  242.6 2.2 collective-permute-start.33
  245.7 4.5 %collective-permute-start.34 = (f32[1,128,128]{2,1,0:T(8,128)S(1)}, f32[1,128,128]{2,1,0:T(8,128)S(1)}, u32[]{:S(2)}, u32[]{:S(2)}) collective-permute-start(f32[1,128,128]{2,1,0:T(8,128)S(1)} %get-tuple-element.466), channel_id=1, source_target_pairs={{1,0},{2,1},{3,2},{4,3},{5,4},{6,5},{7,6},{8,7},{9,8},{10,9},{11,1... | collective-permute-start | bytes 196616 | tf_op jit(solution)/shard_map/ppermute | solution.py:17
  251.7 1.9 collective-permute-start.32
  255.1 3.6 %collective-permute-start.35 = (f32[1,128,128]{2,1,0:T(8,128)}, f32[1,128,128]{2,1,0:T(8,128)}, u32[]{:S(2)}, u32[]{:S(2)}) collective-permute-start(f32[1,128,128]{2,1,0:T(8,128)} %get-tuple-element.451), channel_id=1, source_target_pairs={{0,1},{1,2},{2,3},{3,4},{4,5},{5,6},{6,7},{7,8},{8,9},{9,10},{10,1... | collective-permute-start | bytes 196616 | tf_op jit(solution)/shard_map/ppermute | solution.py:17
  261.4 1.9 collective-permute-start.36
  273.4 2.5 collective-permute-start.38
  275.9 1.9 collective-permute-start.40
  277.9 4.4 %collective-permute-start.41 = (f32[1,128,128]{2,1,0:T(8,128)}, f32[1,128,128]{2,1,0:T(8,128)}, u32[]{:S(2)}, u32[]{:S(2)}) collective-permute-start(f32[1,128,128]{2,1,0:T(8,128)} %get-tuple-element.444), channel_id=1, source_target_pairs={{1,0},{2,1},{3,2},{4,3},{5,4},{6,5},{7,6},{8,7},{9,8},{10,9},{11,1... | collective-permute-start | bytes 196616 | tf_op jit(solution)/shard_map/ppermute | solution.py:17
  288.6 1.6 bitcast_dynamic-update-slice_fusion.2
  291.1 1.6 bitcast_dynamic-update-slice_fusion.1
  (507 shorter events, 94.7 us)
Async XLA Ops:
  7.2 107.3 %all-reduce.75.cloned.1.call-start = ((), (), s32[]{:S(2)}) async-start(), calls=%async_computation | async-start | bytes 1179648 | tf_op jit(solution)/shard_map/psum | solution.py:22
  7.2 13.0 %copy-start.94 = (f32[1,8,1536]{2,1,0:T(8,128)S(1)}, f32[1,8,1536]{2,1,0:T(8,128)}, u32[]{:S(2)}) copy-start(f32[1,8,1536]{2,1,0:T(8,128)} %param.66) | copy-start | bytes 147460
  8.3 46.7 %collective-permute-start = (f32[1,128,128]{2,1,0:T(8,128)S(1)}, f32[1,128,128]{2,1,0:T(8,128)S(1)}, u32[]{:S(2)}, u32[]{:S(2)}) collective-permute-start(f32[1,128,128]{2,1,0:T(8,128)S(1)} %get-tuple-element.426), channel_id=1, source_target_pairs={{1,0},{2,1},{3,2},{4,3},{5,4},{6,5},{7,6},{8,7},{9,8},{10,9},{11,1... | collective-permute-start | bytes 196616 | tf_op jit(solution)/shard_map/ppermute | solution.py:17
  10.9 44.1 %collective-permute-start.2 = (f32[1,128,128]{2,1,0:T(8,128)S(1)}, f32[1,128,128]{2,1,0:T(8,128)S(1)}, u32[]{:S(2)}, u32[]{:S(2)}) collective-permute-start(f32[1,128,128]{2,1,0:T(8,128)S(1)} %get-tuple-element.423), channel_id=1, source_target_pairs={{0,1},{1,2},{2,3},{3,4},{4,5},{5,6},{6,7},{7,8},{8,9},{9,10},{10,1... | collective-permute-start | bytes 196616 | tf_op jit(solution)/shard_map/ppermute | solution.py:17
  13.9 41.2 %collective-permute-start.3 = (f32[1,128,128]{2,1,0:T(8,128)S(1)}, f32[1,128,128]{2,1,0:T(8,128)S(1)}, u32[]{:S(2)}, u32[]{:S(2)}) collective-permute-start(f32[1,128,128]{2,1,0:T(8,128)S(1)} %get-tuple-element.424), channel_id=1, source_target_pairs={{0,1},{1,2},{2,3},{3,4},{4,5},{5,6},{6,7},{7,8},{8,9},{9,10},{10,1... | collective-permute-start | bytes 196616 | tf_op jit(solution)/shard_map/ppermute | solution.py:17
  16.3 11.7 %collective-permute-start.10 = (f32[16,128]{1,0:T(8,128)S(1)}, f32[16,128]{1,0:T(8,128)S(1)}, u32[]{:S(2)}, u32[]{:S(2)}) collective-permute-start(f32[16,128]{1,0:T(8,128)S(1)} %copy-done.113), channel_id=1, source_target_pairs={{0,1},{1,2},{2,3},{3,4},{4,5},{5,6},{6,7},{7,8},{8,9},{9,10},{10,1... | collective-permute-start | bytes 24584 | tf_op jit(solution)/shard_map/ppermute | solution.py:17
  26.8 28.3 %copy-start.83 = (f32[128]{0:T(128)}, f32[128]{0:T(128)S(1)}, u32[]{:S(2)}) copy-start(f32[128]{0:T(128)S(1)} %broadcast_multiply_fusion.2) | copy-start | bytes 1540
  28.2 3.1 %collective-permute-start.17 = (f32[16,128]{1,0:T(8,128)S(1)}, f32[16,128]{1,0:T(8,128)S(1)}, u32[]{:S(2)}, u32[]{:S(2)}) collective-permute-start(f32[16,128]{1,0:T(8,128)S(1)} %broadcast_select_fusion.4), channel_id=1, source_target_pairs={{0,1},{1,2},{2,3},{3,4},{4,5},{5,6},{6,7},{7,8},{8,9},{9,10},{10,1... | collective-permute-start | bytes 24584 | tf_op jit(solution)/shard_map/ppermute | solution.py:17
  31.4 4.8 %collective-permute-start.24 = (f32[16,128]{1,0:T(8,128)S(1)}, f32[16,128]{1,0:T(8,128)S(1)}, u32[]{:S(2)}, u32[]{:S(2)}) collective-permute-start(f32[16,128]{1,0:T(8,128)S(1)} %broadcast_select_fusion.3), channel_id=1, source_target_pairs={{0,1},{1,2},{2,3},{3,4},{4,5},{5,6},{6,7},{7,8},{8,9},{9,10},{10,1... | collective-permute-start | bytes 24584 | tf_op jit(solution)/shard_map/ppermute | solution.py:17
  36.3 18.6 %copy-start.47 = (f32[3,2,128,128]{3,2,1,0:T(8,128)S(1)}, f32[3,2,128,128]{3,2,1,0:T(8,128)}, u32[]{:S(2)}) copy-start(f32[3,2,128,128]{3,2,1,0:T(8,128)} %param.62) | copy-start | bytes 1179652
  36.4 5.2 %collective-permute-start.31 = (f32[16,128]{1,0:T(8,128)S(1)}, f32[16,128]{1,0:T(8,128)S(1)}, u32[]{:S(2)}, u32[]{:S(2)}) collective-permute-start(f32[16,128]{1,0:T(8,128)S(1)} %broadcast_select_fusion.2), channel_id=1, source_target_pairs={{0,1},{1,2},{2,3},{3,4},{4,5},{5,6},{6,7},{7,8},{8,9},{9,10},{10,1... | collective-permute-start | bytes 24584 | tf_op jit(solution)/shard_map/ppermute | solution.py:17
  41.8 6.0 %collective-permute-start.37 = (f32[16,128]{1,0:T(8,128)S(1)}, f32[16,128]{1,0:T(8,128)S(1)}, u32[]{:S(2)}, u32[]{:S(2)}) collective-permute-start(f32[16,128]{1,0:T(8,128)S(1)} %broadcast_select_fusion.1), channel_id=1, source_target_pairs={{0,1},{1,2},{2,3},{3,4},{4,5},{5,6},{6,7},{7,8},{8,9},{9,10},{10,1... | collective-permute-start | bytes 24584 | tf_op jit(solution)/shard_map/ppermute | solution.py:17
  48.0 5.9 %collective-permute-start.39 = (f32[16,128]{1,0:T(8,128)S(1)}, f32[16,128]{1,0:T(8,128)S(1)}, u32[]{:S(2)}, u32[]{:S(2)}) collective-permute-start(f32[16,128]{1,0:T(8,128)S(1)} %broadcast_select_fusion), channel_id=1, source_target_pairs={{0,1},{1,2},{2,3},{3,4},{4,5},{5,6},{6,7},{7,8},{8,9},{9,10},{10,1... | collective-permute-start | bytes 24584 | tf_op jit(solution)/shard_map/ppermute | solution.py:17
  55.2 59.2 %copy-start.111 = (s32[8]{0:T(128)S(1)}, s32[8]{0:T(128)}, u32[]{:S(2)}) copy-start(s32[8]{0:T(128)} %param.75) | copy-start | bytes 100
  116.1 19.0 %collective-permute-start.1 = (f32[1,128,128]{2,1,0:T(8,128)S(1)}, f32[1,128,128]{2,1,0:T(8,128)}, u32[]{:S(2)}, u32[]{:S(2)}) collective-permute-start(f32[1,128,128]{2,1,0:T(8,128)S(1)} %get-tuple-element.503), channel_id=1, source_target_pairs={{0,1},{1,2},{2,3},{3,4},{4,5},{5,6},{6,7},{7,8},{8,9},{9,10},{10,1... | collective-permute-start | bytes 196616 | tf_op jit(solution)/shard_map/ppermute | solution.py:17
  121.6 13.5 %collective-permute-start.5 = (f32[1,128,128]{2,1,0:T(8,128)S(1)}, f32[1,128,128]{2,1,0:T(8,128)}, u32[]{:S(2)}, u32[]{:S(2)}) collective-permute-start(f32[1,128,128]{2,1,0:T(8,128)S(1)} %get-tuple-element.498), channel_id=1, source_target_pairs={{1,0},{2,1},{3,2},{4,3},{5,4},{6,5},{7,6},{8,7},{9,8},{10,9},{11,1... | collective-permute-start | bytes 196616 | tf_op jit(solution)/shard_map/ppermute | solution.py:17
  124.0 8.1 %collective-permute-start.6 = (f32[1,128,128]{2,1,0:T(8,128)S(1)}, f32[1,128,128]{2,1,0:T(8,128)S(1)}, u32[]{:S(2)}, u32[]{:S(2)}) collective-permute-start(f32[1,128,128]{2,1,0:T(8,128)S(1)} %get-tuple-element.508), channel_id=1, source_target_pairs={{1,0},{2,1},{3,2},{4,3},{5,4},{6,5},{7,6},{8,7},{9,8},{10,9},{11,1... | collective-permute-start | bytes 196616 | tf_op jit(solution)/shard_map/ppermute | solution.py:17
  132.9 11.0 %collective-permute-start.9 = (f32[1,128,128]{2,1,0:T(8,128)}, f32[1,128,128]{2,1,0:T(8,128)}, u32[]{:S(2)}, u32[]{:S(2)}) collective-permute-start(f32[1,128,128]{2,1,0:T(8,128)} %get-tuple-element.505), channel_id=1, source_target_pairs={{0,1},{1,2},{2,3},{3,4},{4,5},{5,6},{6,7},{7,8},{8,9},{9,10},{10,1... | collective-permute-start | bytes 196616 | tf_op jit(solution)/shard_map/ppermute | solution.py:17
  137.4 6.5 %collective-permute-start.8 = (f32[1,128,128]{2,1,0:T(8,128)}, f32[1,128,128]{2,1,0:T(8,128)}, u32[]{:S(2)}, u32[]{:S(2)}) collective-permute-start(f32[1,128,128]{2,1,0:T(8,128)} %get-tuple-element.493), channel_id=1, source_target_pairs={{0,1},{1,2},{2,3},{3,4},{4,5},{5,6},{6,7},{7,8},{8,9},{9,10},{10,1... | collective-permute-start | bytes 196616 | tf_op jit(solution)/shard_map/ppermute | solution.py:17
  141.8 6.0 %collective-permute-start.4 = (f32[1,128,128]{2,1,0:T(8,128)}, f32[1,128,128]{2,1,0:T(8,128)}, u32[]{:S(2)}, u32[]{:S(2)}) collective-permute-start(f32[1,128,128]{2,1,0:T(8,128)} %get-tuple-element.500), channel_id=1, source_target_pairs={{1,0},{2,1},{3,2},{4,3},{5,4},{6,5},{7,6},{8,7},{9,8},{10,9},{11,1... | collective-permute-start | bytes 196616 | tf_op jit(solution)/shard_map/ppermute | solution.py:17
  149.9 20.0 %collective-permute-start.7 = (f32[1,128,128]{2,1,0:T(8,128)S(1)}, f32[1,128,128]{2,1,0:T(8,128)S(1)}, u32[]{:S(2)}, u32[]{:S(2)}) collective-permute-start(f32[1,128,128]{2,1,0:T(8,128)S(1)} %get-tuple-element.491), channel_id=1, source_target_pairs={{0,1},{1,2},{2,3},{3,4},{4,5},{5,6},{6,7},{7,8},{8,9},{9,10},{10,1... | collective-permute-start | bytes 196616 | tf_op jit(solution)/shard_map/ppermute | solution.py:17
  152.6 8.0 %collective-permute-start.13 = (f32[1,128,128]{2,1,0:T(8,128)S(1)}, f32[1,128,128]{2,1,0:T(8,128)S(1)}, u32[]{:S(2)}, u32[]{:S(2)}) collective-permute-start(f32[1,128,128]{2,1,0:T(8,128)S(1)} %get-tuple-element.502), channel_id=1, source_target_pairs={{1,0},{2,1},{3,2},{4,3},{5,4},{6,5},{7,6},{8,7},{9,8},{10,9},{11,1... | collective-permute-start | bytes 196616 | tf_op jit(solution)/shard_map/ppermute | solution.py:17
  155.2 5.6 %collective-permute-start.12 = (f32[1,128,128]{2,1,0:T(8,128)S(1)}, f32[1,128,128]{2,1,0:T(8,128)S(1)}, u32[]{:S(2)}, u32[]{:S(2)}) collective-permute-start(f32[1,128,128]{2,1,0:T(8,128)S(1)} %get-tuple-element.486), channel_id=1, source_target_pairs={{1,0},{2,1},{3,2},{4,3},{5,4},{6,5},{7,6},{8,7},{9,8},{10,9},{11,1... | collective-permute-start | bytes 196616 | tf_op jit(solution)/shard_map/ppermute | solution.py:17
  162.2 13.2 %collective-permute-start.15 = (f32[1,128,128]{2,1,0:T(8,128)}, f32[1,128,128]{2,1,0:T(8,128)}, u32[]{:S(2)}, u32[]{:S(2)}) collective-permute-start(f32[1,128,128]{2,1,0:T(8,128)} %get-tuple-element.481), channel_id=1, source_target_pairs={{0,1},{1,2},{2,3},{3,4},{4,5},{5,6},{6,7},{7,8},{8,9},{9,10},{10,1... | collective-permute-start | bytes 196616 | tf_op jit(solution)/shard_map/ppermute | solution.py:17
  164.7 10.6 %collective-permute-start.16 = (f32[1,128,128]{2,1,0:T(8,128)}, f32[1,128,128]{2,1,0:T(8,128)}, u32[]{:S(2)}, u32[]{:S(2)}) collective-permute-start(f32[1,128,128]{2,1,0:T(8,128)} %get-tuple-element.495), channel_id=1, source_target_pairs={{0,1},{1,2},{2,3},{3,4},{4,5},{5,6},{6,7},{7,8},{8,9},{9,10},{10,1... | collective-permute-start | bytes 196616 | tf_op jit(solution)/shard_map/ppermute | solution.py:17
  170.7 26.2 %copy-start.3 = (f32[2,128,128]{2,1,0:T(8,128)}, f32[2,128,128]{2,1,0:T(8,128)S(1)}, u32[]{:S(2)}) copy-start(f32[2,128,128]{2,1,0:T(8,128)S(1)} %get-tuple-element.375) | copy-start | bytes 393220
  173.4 6.3 %collective-permute-start.11 = (f32[1,128,128]{2,1,0:T(8,128)}, f32[1,128,128]{2,1,0:T(8,128)}, u32[]{:S(2)}, u32[]{:S(2)}) collective-permute-start(f32[1,128,128]{2,1,0:T(8,128)} %get-tuple-element.488), channel_id=1, source_target_pairs={{1,0},{2,1},{3,2},{4,3},{5,4},{6,5},{7,6},{8,7},{9,8},{10,9},{11,1... | collective-permute-start | bytes 196616 | tf_op jit(solution)/shard_map/ppermute | solution.py:17
  177.5 11.0 %collective-permute-start.20 = (f32[1,128,128]{2,1,0:T(8,128)S(1)}, f32[1,128,128]{2,1,0:T(8,128)S(1)}, u32[]{:S(2)}, u32[]{:S(2)}) collective-permute-start(f32[1,128,128]{2,1,0:T(8,128)S(1)} %get-tuple-element.490), channel_id=1, source_target_pairs={{1,0},{2,1},{3,2},{4,3},{5,4},{6,5},{7,6},{8,7},{9,8},{10,9},{11,1... | collective-permute-start | bytes 196616 | tf_op jit(solution)/shard_map/ppermute | solution.py:17
  183.2 13.8 %collective-permute-start.14 = (f32[1,128,128]{2,1,0:T(8,128)}, f32[1,128,128]{2,1,0:T(8,128)S(1)}, u32[]{:S(2)}, u32[]{:S(2)}) collective-permute-start(f32[1,128,128]{2,1,0:T(8,128)} %get-tuple-element.479), channel_id=1, source_target_pairs={{0,1},{1,2},{2,3},{3,4},{4,5},{5,6},{6,7},{7,8},{8,9},{9,10},{10,1... | collective-permute-start | bytes 196616 | tf_op jit(solution)/shard_map/ppermute | solution.py:17
  186.5 7.0 %collective-permute-start.19 = (f32[1,128,128]{2,1,0:T(8,128)S(1)}, f32[1,128,128]{2,1,0:T(8,128)S(1)}, u32[]{:S(2)}, u32[]{:S(2)}) collective-permute-start(f32[1,128,128]{2,1,0:T(8,128)S(1)} %get-tuple-element.474), channel_id=1, source_target_pairs={{1,0},{2,1},{3,2},{4,3},{5,4},{6,5},{7,6},{8,7},{9,8},{10,9},{11,1... | collective-permute-start | bytes 196616 | tf_op jit(solution)/shard_map/ppermute | solution.py:17
  189.8 13.2 %collective-permute-start.23 = (f32[1,128,128]{2,1,0:T(8,128)}, f32[1,128,128]{2,1,0:T(8,128)}, u32[]{:S(2)}, u32[]{:S(2)}) collective-permute-start(f32[1,128,128]{2,1,0:T(8,128)} %get-tuple-element.483), channel_id=1, source_target_pairs={{0,1},{1,2},{2,3},{3,4},{4,5},{5,6},{6,7},{7,8},{8,9},{9,10},{10,1... | collective-permute-start | bytes 196616 | tf_op jit(solution)/shard_map/ppermute | solution.py:17
  195.0 8.1 %collective-permute-start.22 = (f32[1,128,128]{2,1,0:T(8,128)}, f32[1,128,128]{2,1,0:T(8,128)}, u32[]{:S(2)}, u32[]{:S(2)}) collective-permute-start(f32[1,128,128]{2,1,0:T(8,128)} %get-tuple-element.469), channel_id=1, source_target_pairs={{0,1},{1,2},{2,3},{3,4},{4,5},{5,6},{6,7},{7,8},{8,9},{9,10},{10,1... | collective-permute-start | bytes 196616 | tf_op jit(solution)/shard_map/ppermute | solution.py:17
  200.5 10.7 %collective-permute-start.18 = (f32[1,128,128]{2,1,0:T(8,128)S(1)}, f32[1,128,128]{2,1,0:T(8,128)}, u32[]{:S(2)}, u32[]{:S(2)}) collective-permute-start(f32[1,128,128]{2,1,0:T(8,128)S(1)} %get-tuple-element.476), channel_id=1, source_target_pairs={{1,0},{2,1},{3,2},{4,3},{5,4},{6,5},{7,6},{8,7},{9,8},{10,9},{11,1... | collective-permute-start | bytes 196616 | tf_op jit(solution)/shard_map/ppermute | solution.py:17
  207.1 11.0 %collective-permute-start.27 = (f32[1,128,128]{2,1,0:T(8,128)}, f32[1,128,128]{2,1,0:T(8,128)}, u32[]{:S(2)}, u32[]{:S(2)}) collective-permute-start(f32[1,128,128]{2,1,0:T(8,128)} %get-tuple-element.478), channel_id=1, source_target_pairs={{1,0},{2,1},{3,2},{4,3},{5,4},{6,5},{7,6},{8,7},{9,8},{10,9},{11,1... | collective-permute-start | bytes 196616 | tf_op jit(solution)/shard_map/ppermute | solution.py:17
  213.4 14.9 %collective-permute-start.21 = (f32[1,128,128]{2,1,0:T(8,128)S(1)}, f32[1,128,128]{2,1,0:T(8,128)S(1)}, u32[]{:S(2)}, u32[]{:S(2)}) collective-permute-start(f32[1,128,128]{2,1,0:T(8,128)S(1)} %get-tuple-element.467), channel_id=1, source_target_pairs={{0,1},{1,2},{2,3},{3,4},{4,5},{5,6},{6,7},{7,8},{8,9},{9,10},{10,1... | collective-permute-start | bytes 196616 | tf_op jit(solution)/shard_map/ppermute | solution.py:17
  215.4 9.0 %collective-permute-start.26 = (f32[1,128,128]{2,1,0:T(8,128)}, f32[1,128,128]{2,1,0:T(8,128)S(1)}, u32[]{:S(2)}, u32[]{:S(2)}) collective-permute-start(f32[1,128,128]{2,1,0:T(8,128)} %get-tuple-element.462), channel_id=1, source_target_pairs={{1,0},{2,1},{3,2},{4,3},{5,4},{6,5},{7,6},{8,7},{9,8},{10,9},{11,1... | collective-permute-start | bytes 196616 | tf_op jit(solution)/shard_map/ppermute | solution.py:17
  221.3 12.6 %collective-permute-start.30 = (f32[1,128,128]{2,1,0:T(8,128)}, f32[1,128,128]{2,1,0:T(8,128)}, u32[]{:S(2)}, u32[]{:S(2)}) collective-permute-start(f32[1,128,128]{2,1,0:T(8,128)} %get-tuple-element.471), channel_id=1, source_target_pairs={{0,1},{1,2},{2,3},{3,4},{4,5},{5,6},{6,7},{7,8},{8,9},{9,10},{10,1... | collective-permute-start | bytes 196616 | tf_op jit(solution)/shard_map/ppermute | solution.py:17
  225.3 8.7 %collective-permute-start.29 = (f32[1,128,128]{2,1,0:T(8,128)}, f32[1,128,128]{2,1,0:T(8,128)}, u32[]{:S(2)}, u32[]{:S(2)}) collective-permute-start(f32[1,128,128]{2,1,0:T(8,128)} %get-tuple-element.457), channel_id=1, source_target_pairs={{0,1},{1,2},{2,3},{3,4},{4,5},{5,6},{6,7},{7,8},{8,9},{9,10},{10,1... | collective-permute-start | bytes 196616 | tf_op jit(solution)/shard_map/ppermute | solution.py:17
  231.6 6.6 %collective-permute-start.25 = (f32[1,128,128]{2,1,0:T(8,128)S(1)}, f32[1,128,128]{2,1,0:T(8,128)S(1)}, u32[]{:S(2)}, u32[]{:S(2)}) collective-permute-start(f32[1,128,128]{2,1,0:T(8,128)S(1)} %get-tuple-element.464), channel_id=1, source_target_pairs={{1,0},{2,1},{3,2},{4,3},{5,4},{6,5},{7,6},{8,7},{9,8},{10,9},{11,1... | collective-permute-start | bytes 196616 | tf_op jit(solution)/shard_map/ppermute | solution.py:17
  239.3 10.9 %collective-permute-start.28 = (f32[1,128,128]{2,1,0:T(8,128)S(1)}, f32[1,128,128]{2,1,0:T(8,128)S(1)}, u32[]{:S(2)}, u32[]{:S(2)}) collective-permute-start(f32[1,128,128]{2,1,0:T(8,128)S(1)} %get-tuple-element.455), channel_id=1, source_target_pairs={{0,1},{1,2},{2,3},{3,4},{4,5},{5,6},{6,7},{7,8},{8,9},{9,10},{10,1... | collective-permute-start | bytes 196616 | tf_op jit(solution)/shard_map/ppermute | solution.py:17
  242.6 11.0 %collective-permute-start.33 = (f32[1,128,128]{2,1,0:T(8,128)S(1)}, f32[1,128,128]{2,1,0:T(8,128)S(1)}, u32[]{:S(2)}, u32[]{:S(2)}) collective-permute-start(f32[1,128,128]{2,1,0:T(8,128)S(1)} %get-tuple-element.454), channel_id=1, source_target_pairs={{1,0},{2,1},{3,2},{4,3},{5,4},{6,5},{7,6},{8,7},{9,8},{10,9},{11,1... | collective-permute-start | bytes 196616 | tf_op jit(solution)/shard_map/ppermute | solution.py:17
  245.7 8.0 %collective-permute-start.34 = (f32[1,128,128]{2,1,0:T(8,128)S(1)}, f32[1,128,128]{2,1,0:T(8,128)S(1)}, u32[]{:S(2)}, u32[]{:S(2)}) collective-permute-start(f32[1,128,128]{2,1,0:T(8,128)S(1)} %get-tuple-element.466), channel_id=1, source_target_pairs={{1,0},{2,1},{3,2},{4,3},{5,4},{6,5},{7,6},{8,7},{9,8},{10,9},{11,1... | collective-permute-start | bytes 196616 | tf_op jit(solution)/shard_map/ppermute | solution.py:17
  251.7 11.6 %collective-permute-start.32 = (f32[1,128,128]{2,1,0:T(8,128)}, f32[1,128,128]{2,1,0:T(8,128)}, u32[]{:S(2)}, u32[]{:S(2)}) collective-permute-start(f32[1,128,128]{2,1,0:T(8,128)} %get-tuple-element.450), channel_id=1, source_target_pairs={{1,0},{2,1},{3,2},{4,3},{5,4},{6,5},{7,6},{8,7},{9,8},{10,9},{11,1... | collective-permute-start | bytes 196616 | tf_op jit(solution)/shard_map/ppermute | solution.py:17
  255.1 8.3 %collective-permute-start.35 = (f32[1,128,128]{2,1,0:T(8,128)}, f32[1,128,128]{2,1,0:T(8,128)}, u32[]{:S(2)}, u32[]{:S(2)}) collective-permute-start(f32[1,128,128]{2,1,0:T(8,128)} %get-tuple-element.451), channel_id=1, source_target_pairs={{0,1},{1,2},{2,3},{3,4},{4,5},{5,6},{6,7},{7,8},{8,9},{9,10},{10,1... | collective-permute-start | bytes 196616 | tf_op jit(solution)/shard_map/ppermute | solution.py:17
  261.4 8.5 %collective-permute-start.36 = (f32[1,128,128]{2,1,0:T(8,128)}, f32[1,128,128]{2,1,0:T(8,128)}, u32[]{:S(2)}, u32[]{:S(2)}) collective-permute-start(f32[1,128,128]{2,1,0:T(8,128)} %get-tuple-element.459), channel_id=1, source_target_pairs={{0,1},{1,2},{2,3},{3,4},{4,5},{5,6},{6,7},{7,8},{8,9},{9,10},{10,1... | collective-permute-start | bytes 196616 | tf_op jit(solution)/shard_map/ppermute | solution.py:17
  273.4 9.7 %collective-permute-start.38 = (f32[1,128,128]{2,1,0:T(8,128)S(1)}, f32[1,128,128]{2,1,0:T(8,128)S(1)}, u32[]{:S(2)}, u32[]{:S(2)}) collective-permute-start(f32[1,128,128]{2,1,0:T(8,128)S(1)} %copy-done.93), channel_id=1, source_target_pairs={{0,1},{1,2},{2,3},{3,4},{4,5},{5,6},{6,7},{7,8},{8,9},{9,10},{10,1... | collective-permute-start | bytes 196616 | tf_op jit(solution)/shard_map/ppermute | solution.py:17
  275.9 12.0 %collective-permute-start.40 = (f32[1,128,128]{2,1,0:T(8,128)}, f32[1,128,128]{2,1,0:T(8,128)}, u32[]{:S(2)}, u32[]{:S(2)}) collective-permute-start(f32[1,128,128]{2,1,0:T(8,128)} %get-tuple-element.446), channel_id=1, source_target_pairs={{1,0},{2,1},{3,2},{4,3},{5,4},{6,5},{7,6},{8,7},{9,8},{10,9},{11,1... | collective-permute-start | bytes 196616 | tf_op jit(solution)/shard_map/ppermute | solution.py:17
  277.9 13.0 %collective-permute-start.41 = (f32[1,128,128]{2,1,0:T(8,128)}, f32[1,128,128]{2,1,0:T(8,128)}, u32[]{:S(2)}, u32[]{:S(2)}) collective-permute-start(f32[1,128,128]{2,1,0:T(8,128)} %get-tuple-element.444), channel_id=1, source_target_pairs={{1,0},{2,1},{3,2},{4,3},{5,4},{6,5},{7,6},{8,7},{9,8},{10,9},{11,1... | collective-permute-start | bytes 196616 | tf_op jit(solution)/shard_map/ppermute | solution.py:17
  (116 other events, 212.6 us)
Sparse Core Ops, SparseCore 0:
  24.9 89.5 all-reduce.74
where the time goes:
time: 305 us; the launch traced here: 302 us
  starting transfers between devices  124 us (41%)
  waiting for transfers between devices  65 us (21%)
  local copies, waits for them, and re-layouts  64.6 us (21%)
  other arithmetic  29.1 us (10%)
  between operations  16.5 us (5%)
  matrix products  3.09 us (1%)
    ppermute x42, starting transfers between devices, passed_along(): return lax.ppermute(block, axis, route)  124 us
    psum x1, waiting for transfers between devices, from_root(): return lax.psum(block, axis)  59.2 us
    unnamed x243, local copies, waits for them, and re-layouts  23 us
    add x21, other arithmetic, relax(): new_stress.append(stresses[comp] + time_step * drive)  9.74 us
    add x12, other arithmetic, body(): moved = speeds[comp] + time_step * buoy_z * rates[comp]  9.12 us
    scatter-add x18, local copies, waits for them, and re-layouts, body(): moved.at[:, corner:corner + FY, 0:FZ].add(time_step * pier_force[:, comp])  7.7 us
  transfers between devices with their start and end apart: 43, of which 8 were waited for; matrix products, arithmetic and copies ran while one was open for 21% of the time, Pallas kernels for 0%

commit v1 on v0

v1 whole, which is shorter than its diff:
```python
import functools

import jax
import jax.numpy as jnp
from jax import lax
from jax.experimental import pallas as pl
from jax.experimental.pallas import tpu as pltpu
from jax.sharding import PartitionSpec as P

STEPS = 6
FY = 8
FZ = 64
DT = 0.25
PAD = 8
ROWS = 16
VMEM_LIMIT = 32 * 1024 * 1024

C_B, C_B0, C_B1, C_M0, C_M1, C_LAM, C_MU2, C_MU, C_K1, C_K2, C_K2H, C_L0 = range(12)
N_COEF = 16

VX, VY, VZ = range(3)
XX, YY, ZZ, XY, XZ, YZ = range(6)


def lane_roll(x, shift):
    return pltpu.roll(x, shift % x.shape[-1], x.ndim - 1)


def before(x):
    return lane_roll(x, 1)


def after(x):
    return lane_roll(x, -1)


def over_rows(count, work):
    def step(i, carry):
        work(pl.multiple_of(i * ROWS, ROWS))
        return carry

    lax.fori_loop(0, count // ROWS, step, 0)


def coefs(coef_ref, ids):
    return [coef_ref[i : i + 1, :] for i in ids]


def place():
    index = lax.axis_index("line")
    return lax.rem(index, 2) == 0, index > 0, index < lax.axis_size("line") - 1


def pre_ahead(V, S, coef_ref, msg):
    b, b0 = coefs(coef_ref, (C_B, C_B0))

    def work(r):
        here, up = pl.ds(PAD + r, ROWS), pl.ds(PAD + r - 1, ROWS)
        sxy, sxz = S[XY, 1, here], S[XZ, 1, here]
        px = V[VX, 1, here] + b * (sxy - S[XY, 1, up] + sxz - S[XX, 1, here]) - b0 * before(sxz)
        V[VX, 1, here] = px
        out = pl.ds(r, ROWS)
        msg[0, out] = sxy
        msg[1, out] = sxz
        msg[2, out] = px

    over_rows(msg.shape[1], work)


def pre_behind(V, S, coef_ref, msg):
    b, b0, b1 = coefs(coef_ref, (C_B, C_B0, C_B1))

    def work(r):
        here, up, down = pl.ds(PAD + r, ROWS), pl.ds(PAD + r - 1, ROWS), pl.ds(PAD + r + 1, ROWS)
        syz, szz = S[YZ, 0, here], S[ZZ, 0, here]
        qy = V[VY, 0, here] + b * (S[XY, 0, here] + S[YY, 0, down] - S[YY, 0, here] + syz) - b0 * before(syz)
        qz = V[VZ, 0, here] + b * (S[XZ, 0, here] + syz - S[YZ, 0, up] - szz) + b1 * after(szz)
        V[VY, 0, here] = qy
        V[VZ, 0, here] = qz
        out = pl.ds(r, ROWS)
        msg[0, out] = S[XX, 0, here]
        msg[1, out] = qy
        msg[2, out] = qz

    over_rows(msg.shape[1], work)


def add_force(ref, index, force, which, corner_rows):
    rows = pl.ds(corner_rows, 16)
    ref[(*index, rows)] = ref[(*index, rows)] + force[which]


def inner(V, S, coef_ref, force, window, depth_rows):
    b, b0, b1 = coefs(coef_ref, (C_B, C_B0, C_B1))

    def work(r):
        here, up, down = pl.ds(PAD + r, ROWS), pl.ds(PAD + r - 1, ROWS), pl.ds(PAD + r + 1, ROWS)
        sxy, sxz = S[XY, 0, here], S[XZ, 0, here]
        V[VX, 0, here] = (
            V[VX, 0, here]
            + b * (S[XX, 1, here] - S[XX, 0, here] + sxy - S[XY, 0, up] + sxz)
            - b0 * before(sxz)
        )
        syz, szz = S[YZ, 1, here], S[ZZ, 1, here]
        V[VY, 1, here] = (
            V[VY, 1, here]
            + b * (S[XY, 1, here] - sxy + S[YY, 1, down] - S[YY, 1, here] + syz)
            - b0 * before(syz)
        )
        V[VZ, 1, here] = (
            V[VZ, 1, here]
            + b * (S[XZ, 1, here] - sxz + syz - S[YZ, 1, up] - szz)
            + b1 * after(szz)
        )

    over_rows(depth_rows, work)
    add_force(V, (VX, 0), force, (VX, 1), PAD + window)
    add_force(V, (VY, 1), force, (VY, 1), PAD + window)
    add_force(V, (VZ, 1), force, (VZ, 1), PAD + window)


def post(V, S, R, coef_ref, surface, cell, column, behind_x, ahead_y, ahead_z):
    m0, m1, lam, mu2, mu, k1, k2, k2h, l0 = coefs(
        coef_ref, (C_M0, C_M1, C_LAM, C_MU2, C_MU, C_K1, C_K2, C_K2H, C_L0)
    )

    def work(r):
        here, up, down = pl.ds(PAD + r, ROWS), pl.ds(PAD + r - 1, ROWS), pl.ds(PAD + r + 1, ROWS)
        out = pl.ds(r, ROWS)
        vx, vy, vz = V[VX, cell, here], V[VY, cell, here], V[VZ, cell, here]
        exx = vx - behind_x(r)
        eyy = vy - V[VY, cell, up]
        ezz = vz - m0 * before(vz)
        exy = V[VX, cell, down] - vx + (ahead_y(r) - vy)
        exz = m1 * after(vx) - vx + (ahead_z(r) - vz)
        eyz = m1 * after(vy) - vy + (V[VZ, cell, down] - vz)
        volume = lam * (exx + eyy + ezz)
        for comp, e in ((XX, exx), (YY, eyy), (ZZ, ezz)):
            old = R[comp, cell, out]
            new = S[comp, cell, here] + (volume + mu2 * e) + DT * old
            if comp == ZZ:
                new = new + l0 * lane_roll(surface[out, :], -column)
            S[comp, cell, here] = new
            R[comp, cell, out] = k1 * old - k2 * e
        for comp, e in ((XY, exy), (XZ, exz), (YZ, eyz)):
            old = R[comp, cell, out]
            S[comp, cell, here] = S[comp, cell, here] + mu * e + DT * old
            R[comp, cell, out] = k1 * old - k2h * e

    over_rows(R.shape[2], work)


def ahead_bond(V, S, R, coef_ref, force, surface, msg, G, step, window, has_ahead):
    (b,) = coefs(coef_ref, (C_B,))
    keep = jnp.where(has_ahead, 1.0, 0.0).astype(jnp.float32)

    def work(r):
        here, out = pl.ds(PAD + r, ROWS), pl.ds(r, ROWS)
        V[VX, 1, here] = V[VX, 1, here] + b * msg[0, out]
        G[0, out] = keep * (msg[1, out] - b * S[XY, 1, here])
        G[1, out] = keep * (msg[2, out] - b * S[XZ, 1, here])

    over_rows(R.shape[2], work)
    add_force(V, (VX, 1), force, (VX, 2), PAD + window)
    add_force(G, (0,), force, (VY, 2), window)
    add_force(G, (1,), force, (VZ, 2), window)
    post(
        V, S, R, coef_ref, surface, 1, 2 * step + 1,
        lambda r: V[VX, 0, pl.ds(PAD + r, ROWS)],
        lambda r: G[0, pl.ds(r, ROWS)],
        lambda r: G[1, pl.ds(r, ROWS)],
    )


def behind_bond(V, S, R, coef_ref, force, surface, msg, G, step, window, has_behind):
    (b,) = coefs(coef_ref, (C_B,))
    keep = jnp.where(has_behind, 1.0, 0.0).astype(jnp.float32)

    def work(r):
        here, out = pl.ds(PAD + r, ROWS), pl.ds(r, ROWS)
        V[VY, 0, here] = V[VY, 0, here] - b * msg[0, out]
        V[VZ, 0, here] = V[VZ, 0, here] - b * msg[1, out]
        G[0, out] = keep * (msg[2, out] + b * S[XX, 0, here])

    over_rows(R.shape[2], work)
    add_force(V, (VY, 0), force, (VY, 0), PAD + window)
    add_force(V, (VZ, 0), force, (VZ, 0), PAD + window)
    add_force(G, (0,), force, (VX, 0), window)
    post(
        V, S, R, coef_ref, surface, 0, 2 * step,
        lambda r: G[0, pl.ds(r, ROWS)],
        lambda r: V[VY, 1, pl.ds(PAD + r, ROWS)],
        lambda r: V[VZ, 1, pl.ds(PAD + r, ROWS)],
    )


def start_kernel(
    velocity, stress, layer_ref, lam, mu, buoy, rate, defect,
    V, S, coef_ref, msg_near, msg_far, sems,
):
    across = velocity.shape[2]
    inside = pl.ds(PAD, across)
    load_v = pltpu.make_async_copy(velocity, V.at[:, :, inside], sems.at[0])
    load_s = pltpu.make_async_copy(stress, S.at[:, :, inside], sems.at[1])
    load_v.start()
    load_s.start()
    edge = jnp.zeros((PAD, V.shape[3]), jnp.float32)
    for ref in (V, S):
        for comp in range(ref.shape[0]):
            for cell in range(ref.shape[1]):
                ref[comp, cell, pl.ds(0, PAD)] = edge
                ref[comp, cell, pl.ds(PAD + across, PAD)] = edge
    layer = layer_ref[...]

    def per_depth(table):
        row = jnp.zeros(layer.shape, jnp.float32)
        for level in range(table.shape[0]):
            row = jnp.where(layer == level, table[level], row)
        return row

    lane = lax.broadcasted_iota(jnp.int32, layer.shape, 1)
    not_first = jnp.where(lane > 0, 1.0, 0.0).astype(jnp.float32)
    not_last = jnp.where(lane < layer.shape[1] - 1, 1.0, 0.0).astype(jnp.float32)
    b = DT * per_depth(buoy)
    two_mu = (2.0 * DT) * per_depth(mu)
    decay = DT * per_depth(rate)
    drop = 2.0 * decay * per_depth(defect)
    for row, value in (
        (C_B, b),
        (C_B0, b * not_first),
        (C_B1, b * not_last),
        (C_M0, not_first),
        (C_M1, not_last),
        (C_LAM, DT * per_depth(lam)),
        (C_MU2, two_mu),
        (C_MU, 0.5 * two_mu),
        (C_K1, 1.0 - decay),
        (C_K2, drop),
        (C_K2H, 0.5 * drop),
        (C_L0, DT * (1.0 - not_first)),
    ):
        coef_ref[row : row + 1, :] = value
    coef_ref[12:16, :] = jnp.zeros((4, layer.shape[1]), jnp.float32)
    load_v.wait()
    load_s.wait()
    even, _, _ = place()

    @pl.when(even)
    def _():
        pre_ahead(V, S, coef_ref, msg_near)
        pre_behind(V, S, coef_ref, msg_far)

    @pl.when(jnp.logical_not(even))
    def _():
        pre_behind(V, S, coef_ref, msg_near)
        pre_ahead(V, S, coef_ref, msg_far)


def near_kernel(step, window, V0, S0, R0, coef_ref, force, surface, msg, V, S, R, *rest):
    G = rest[-1]
    even, has_behind, has_ahead = place()
    here = force.at[step]
    inner(V, S, coef_ref, here, window, R.shape[2])

    @pl.when(even)
    def _():
        ahead_bond(V, S, R, coef_ref, here, surface, msg, G, step, window, has_ahead)
        if step < STEPS - 1:
            pre_ahead(V, S, coef_ref, rest[0])

    @pl.when(jnp.logical_not(even))
    def _():
        behind_bond(V, S, R, coef_ref, here, surface, msg, G, step, window, has_behind)
        if step < STEPS - 1:
            pre_behind(V, S, coef_ref, rest[0])


def far_kernel(step, window, V0, S0, R0, coef_ref, force, surface, msg, V, S, R, *rest):
    G = rest[-1]
    even, has_behind, has_ahead = place()
    here = force.at[step]

    @pl.when(even)
    def _():
        behind_bond(V, S, R, coef_ref, here, surface, msg, G, step, window, has_behind)
        if step < STEPS - 1:
            pre_behind(V, S, coef_ref, rest[0])

    @pl.when(jnp.logical_not(even))
    def _():
        ahead_bond(V, S, R, coef_ref, here, surface, msg, G, step, window, has_ahead)
        if step < STEPS - 1:
            pre_ahead(V, S, coef_ref, rest[0])


def last_kernel(
    step, window, V0, S0, R0, coef_ref, force, surface, msg, V, S, R, v_out, s_out, r_out, G, sems
):
    even, has_behind, has_ahead = place()
    here = force.at[step]

    @pl.when(even)
    def _():
        behind_bond(V, S, R, coef_ref, here, surface, msg, G, step, window, has_behind)

    @pl.when(jnp.logical_not(even))
    def _():
        ahead_bond(V, S, R, coef_ref, here, surface, msg, G, step, window, has_ahead)

    inside = pl.ds(PAD, R.shape[2])
    copies = [
        pltpu.make_async_copy(V.at[:, :, inside], v_out, sems.at[0]),
        pltpu.make_async_copy(S.at[:, :, inside], s_out, sems.at[1]),
        pltpu.make_async_copy(R, r_out, sems.at[2]),
    ]
    for copy in copies:
        copy.start()
    for copy in copies:
        copy.wait()


def split_kernel(record, cells, out):
    tiles = out.shape[0]
    lanes = out.shape[2]
    pieces = record.shape[1] // lanes
    third = pieces // 3
    cell_of = cells[...]
    row = lax.broadcasted_iota(jnp.int32, (3 * tiles, cell_of.shape[1]), 0)
    first = lax.div(row, 3) * 2 + lax.rem(row, 3)
    hit_x = jnp.where(first - 1 == cell_of, 1.0, 0.0).astype(jnp.float32)
    hit_yz = jnp.where(first == cell_of, 1.0, 0.0).astype(jnp.float32)
    for m in range(pieces):
        panel = record[:, m * lanes : (m + 1) * lanes]
        part = jnp.dot(
            hit_x if m < third else hit_yz, panel,
            precision=lax.Precision.HIGHEST, preferred_element_type=jnp.float32,
        )
        for tile in range(tiles):
            out[tile, 3 * m : 3 * m + 3, :] = part[3 * tile : 3 * tile + 3, :]


def force_kernel(parts, force):
    steps, comps, cells = force.shape[:3]
    force[...] = jnp.zeros(force.shape, jnp.float32)
    per = parts.shape[1] // (comps * cells)
    lane = lax.broadcasted_iota(jnp.int32, (per, parts.shape[2]), 1)
    scale = jnp.where(lane < FZ, DT, 0.0).astype(jnp.float32)
    for s in range(steps):
        for comp in range(comps):
            for cell in range(cells):
                panel = parts[s, pl.ds(comp * per * cells + cell, per, stride=cells), :]
                force[s, comp, cell, pl.ds(4, per, stride=2), :] = scale * panel
                force[s, comp, cell, pl.ds(5, per, stride=2), :] = scale * lane_roll(panel, FZ)


def truck_kernel(slots, own, one, two, four, cells, out, table, rows_out):
    table[...] = jnp.zeros(table.shape, jnp.float32)
    rows = []
    for k in range(STEPS + 1):
        source, at = ((own, 0), (one, 0), (two, 0), (two, 1), (four, 0), (four, 1), (four, 2))[k]
        base = at * (slots + 8)
        rows.append(source[base : base + slots, :])
        table[8 * k : 8 * k + 8, :] = source[base + slots : base + slots + 8, :]
    table[8 * (STEPS + 1) : 8 * (STEPS + 1) + 8, :] = cells[...]
    columns = table[...].T
    rows_out[...] = jnp.zeros(rows_out.shape, jnp.float32)
    for s in range(STEPS):
        moved = []
        for k in range(STEPS - s):
            at = 8 * k + s
            entry = jnp.broadcast_to(columns[0:slots, at : at + 1], rows[k].shape)
            new = rows[k]
            for slot in range(slots):
                new = jnp.where(entry == float(slot), rows[k + 1][slot : slot + 1, :], new)
            moved.append(new)
        rows = moved
        at = 8 * (STEPS + 1) + s
        cell = jnp.broadcast_to(columns[0:slots, at : at + 1], rows[0].shape)
        for c in range(2):
            load = jnp.sum(jnp.where(cell == float(c), rows[0], 0.0), axis=0, keepdims=True)
            rows_out[2 * s + c : 2 * s + c + 1, :] = load
    out[...] = rows_out[...].T


def in_vmem(x):
    return pltpu.with_memory_space_constraint(x, pltpu.VMEM)


WHOLE = pl.BlockSpec(memory_space=pltpu.VMEM)
SCALARS = pl.BlockSpec(memory_space=pltpu.SMEM)
ANYWHERE = pl.BlockSpec(memory_space=pl.ANY)


def call(kernel, ins, specs, outs, out_specs, scratch=(), aliases=None, name=None):
    return pl.pallas_call(
        kernel,
        out_shape=outs,
        in_specs=specs,
        out_specs=out_specs,
        scratch_shapes=list(scratch),
        input_output_aliases=aliases or {},
        compiler_params=pltpu.CompilerParams(vmem_limit_bytes=VMEM_LIMIT),
        name=name,
    )(*ins)


def body(
    velocity, stress, memory, truck_loads, pier_panels,
    lame_lambda, lame_mu, buoyancy, relax_rate, defect_mu, layer,
    truck_entry, truck_cell, pier_cell,
):
    tiles = lax.axis_size("line")
    width_x, across, depth = velocity.shape[1:]
    slots = truck_loads.shape[0]
    window = (across - FY) // 2 - 4
    f32 = jnp.float32

    near = [(i, i ^ 1) for i in range(tiles) if (i ^ 1) < tiles]
    far = [(i, i + 1) for i in range(1, tiles - 1, 2)] + [(i + 1, i) for i in range(1, tiles - 1, 2)]

    def ahead_by(x, distance):
        return lax.ppermute(x, "line", [(i, i + distance) for i in range(tiles - distance)])

    padded = across + 2 * PAD
    v_type = pltpu.VMEM((3, width_x, padded, depth), f32)
    s_type = pltpu.VMEM((6, width_x, padded, depth), f32)
    r_type = pltpu.VMEM((6, width_x, across, depth), f32)
    c_type = pltpu.VMEM((N_COEF, depth), f32)
    m_type = pltpu.VMEM((3, across, depth), f32)

    V, S, coef, msg_near, msg_far = call(
        start_kernel,
        (velocity, stress, layer[None, :], lame_lambda, lame_mu, buoyancy, relax_rate, defect_mu),
        (ANYWHERE, ANYWHERE, WHOLE, SCALARS, SCALARS, SCALARS, SCALARS, SCALARS),
        (v_type, s_type, c_type, m_type, m_type),
        (WHOLE,) * 5,
        scratch=(pltpu.SemaphoreType.DMA((2,)),),
        name="start",
    )
    msg_far = lax.ppermute(msg_far, "line", far)
    msg_near = lax.ppermute(msg_near, "line", near)

    pieces = pier_panels.shape[2] // depth
    parts = call(
        split_kernel,
        (pier_panels[0], pier_cell[None, :]),
        (WHOLE, WHOLE),
        jax.ShapeDtypeStruct((tiles, 3 * pieces, depth), f32),
        WHOLE,
        name="split",
    )
    parts = lax.all_to_all(parts, "line", 0, 0, tiled=True)
    force = call(
        force_kernel,
        (parts[:STEPS],),
        (WHOLE,),
        pltpu.VMEM((STEPS, 3, 3, 16, depth), f32),
        WHOLE,
        name="force",
    )

    entries = jnp.pad(truck_entry.astype(f32), ((0, 8 - STEPS), (0, depth - slots)))
    cells = jnp.pad(truck_cell.astype(f32), ((0, 8 - STEPS), (0, depth - slots)))
    own = jnp.concatenate([truck_loads, entries], axis=0)
    one = ahead_by(own, 1)
    pair = jnp.concatenate([own, one], axis=0)
    two = ahead_by(pair, 2)
    four = ahead_by(jnp.concatenate([pair, two[: slots + 8]], axis=0), 4)
    surface = call(
        functools.partial(truck_kernel, slots),
        (own, one, two, four, cells),
        (WHOLE,) * 5,
        pltpu.VMEM((across, depth), f32),
        WHOLE,
        scratch=(pltpu.VMEM((depth, depth), f32), pltpu.VMEM((depth, across), f32)),
        name="trucks",
    )

    R = memory
    ghost = pltpu.VMEM((2, across, depth), f32)
    for step in range(STEPS):
        for far_side in (False, True):
            final = far_side and step == STEPS - 1
            sends = step < STEPS - 1
            ins = (V, S, R, coef, force, surface, msg_far if far_side else msg_near)
            ins = tuple(in_vmem(x) for x in ins)
            if final:
                return call(
                    functools.partial(last_kernel, step, window),
                    ins,
                    (WHOLE,) * len(ins),
                    (
                        v_type,
                        s_type,
                        r_type,
                        jax.ShapeDtypeStruct(velocity.shape, f32),
                        jax.ShapeDtypeStruct(stress.shape, f32),
                        jax.ShapeDtypeStruct(memory.shape, f32),
                    ),
                    (WHOLE,) * 3 + (ANYWHERE,) * 3,
                    scratch=(ghost, pltpu.SemaphoreType.DMA((3,))),
                    aliases={0: 0, 1: 1, 2: 2},
                    name="last",
                )[3:]
            outs = (v_type, s_type, r_type) + ((m_type,) if sends else ())
            kernel = far_kernel if far_side else near_kernel
            V, S, R, *msg = call(
                functools.partial(kernel, step, window),
                ins,
                (WHOLE,) * len(ins),
                outs,
                (WHOLE,) * len(outs),
                scratch=(ghost,),
                aliases={0: 0, 1: 1, 2: 2},
                name=("far" if far_side else "near") + str(step),
            )
            if sends and far_side:
                msg_far = lax.ppermute(msg[0], "line", far)
            elif sends:
                msg_near = lax.ppermute(msg[0], "line", near)


def solution(mesh):
    placed = (
        P(None, ("runs", "line"), None, None),
        P(None, ("runs", "line"), None, None),
        P(None, ("runs", "line"), None, None),
        P(("runs", "line"), None),
        P("line", "runs", None),
        P(),
        P(),
        P(),
        P(),
        P(),
        P(),
        P(None, ("runs", "line")),
        P(None, ("runs", "line")),
        P(),
    )
    return jax.shard_map(
        body,
        mesh=mesh,
        in_specs=placed,
        out_specs=(
            P(None, ("runs", "line"), None, None),
            P(None, ("runs", "line"), None, None),
            P(None, ("runs", "line"), None, None),
        ),
        check_vma=False,
    )
```

time: 305 us -> 87.1 us (0.29)
  starting transfers between devices: 124 us -> 37.3 us
  local copies, waits for them, and re-layouts: 64.6 us -> 2.83 us
  waiting for transfers between devices: 65 us -> 20.7 us
  other arithmetic: 29.1 us -> 0.02 us
  Pallas kernels: 0 us -> 24.6 us
  between operations: 16.5 us -> 1.01 us
  matrix products: 3.09 us -> 0 us
    ppermute x42 -> x15, starting transfers between devices: 124 us -> 30.7 us  [the longest x5 15.6 us: body(): msg_far = lax.ppermute(msg[0], 'line', far)]
    psum x1 -> x0, waiting for transfers between devices: 59.2 us -> none  [from_root(): return lax.psum(block, axis)]
    pallas_call x0 -> x16, Pallas kernels: none -> 24.6 us  [call(): pl.pallas_call(kernel, out_shape=outs, in_specs=specs, out_specs=out_spec...]
    slice x76 -> x2, local copies, waits for them, and re-layouts: 23 us -> 0.91 us  [the longest x1 0.91 us: body(): parts[:STEPS]]
    unnamed x243 -> x27, local copies, waits for them, and re-layouts: 23 us -> 1.91 us
    add x57 -> x0, other arithmetic: 19.8 us -> none  [the longest x21 9.74 us: relax(): new_stress.append(stresses[comp] + time_step * drive)]
    ppermute x42 -> x15, waiting for transfers between devices: 5.75 us -> 20.7 us  [the longest x5 15.8 us: body(): msg_far = lax.ppermute(msg[0], 'line', far)]
    scatter-add x24 -> x0, local copies, waits for them, and re-layouts: 9.22 us -> none  [the longest x18 7.7 us: body(): moved.at[:, corner:corner + FY, 0:FZ].add(time_step * pier_force[:, comp])]
  transfers between devices with their start and end apart: 43 -> 16, of which waited for: 8 -> 7; matrix products, arithmetic and copies ran while one was open for 21% -> 1% of each run, Pallas kernels for 0% -> 25%
where the time goes in v1:
time: 87.1 us; the launch traced here: 86.4 us
  starting transfers between devices  37.3 us (43%)
  Pallas kernels  24.6 us (28%)
  waiting for transfers between devices  20.7 us (24%)
  local copies, waits for them, and re-layouts  2.83 us (3%)
  between operations  1.01 us (1%)
    pallas_call x16, Pallas kernels, call(): pl.pallas_call(kernel, out_shape=outs, in_specs=specs, out_specs=out_spec...  24.6 us
    ppermute x5, waiting for transfers between devices, body(): msg_far = lax.ppermute(msg[0], 'line', far)  15.8 us
    ppermute x5, starting transfers between devices, body(): msg_far = lax.ppermute(msg[0], 'line', far)  15.6 us
    ppermute x3, starting transfers between devices, ahead_by(): lax.ppermute(x, 'line', [(i, i + distance) for i in range(tiles - distanc...  8.85 us
    all_to_all x1, starting transfers between devices, body(): parts = lax.all_to_all(parts, 'line', 0, 0, tiled=True)  6.63 us
    ppermute x3, waiting for transfers between devices, ahead_by(): lax.ppermute(x, 'line', [(i, i + distance) for i in range(tiles - distanc...  4.85 us
    ppermute x1, starting transfers between devices, body(): msg_far = lax.ppermute(msg_far, 'line', far)  3.46 us
    ppermute x5, starting transfers between devices, body(): msg_near = lax.ppermute(msg[0], 'line', near)  2.67 us
  transfers between devices with their start and end apart: 16, of which 7 were waited for; matrix products, arithmetic and copies ran while one was open for 1% of the time, Pallas kernels for 25%

profile of v1, /device:TPU:17, one launch (start us, length us, event | category | flops | bytes accessed | tf_op | source)
XLA Modules:
  0.0 86.4 jit_solution(2334152198716260938)
XLA Ops:
  0.7 1.2 %copy.90.R0 = f32[6,2,128,128]{3,2,1,0:T(8,128)S(1)} copy(f32[6,2,128,128]{3,2,1,0:T(8,128)} %param.16) | data formatting | bytes 1572864
  1.9 1.2 %split.1 = f32[16,36,128]{2,1,0:T(8,128)} custom-call(f32[8,1536]{1,0:T(8,128)S(1)} %bitcast.3, s32[1,8]{1,0:T(1,128)S(1)} %bitcast.4), custom_call_target="tpu_custom_call" | custom-call | tf_op jit(solution)/shard_map/split/pallas_call | solution.py:395
  3.0 6.6 %all-to-all-start = ((f32[16,36,128]{2,1,0:T(8,128)}), f32[16,36,128]{2,1,0:T(8,128)}, u32[]{:S(2)}, u32[]{:S(2)}) async-start(f32[16,36,128]{2,1,0:T(8,128)} %split.1), calls=%async_computation | async-start | bytes 655360 | tf_op jit(solution)/shard_map/all_to_all | solution.py:452
  9.6 0.0 copy-start.10
  9.7 0.7 copy-done.10
  10.4 0.0 copy-start.4
  10.4 0.0 copy-start.5
  10.4 0.0 copy-start.6
  10.4 3.5 %collective-permute-start = (f32[24,128]{1,0:T(8,128)S(1)}, f32[24,128]{1,0:T(8,128)S(1)}, u32[]{:S(2)}, u32[]{:S(2)}) collective-permute-start(f32[24,128]{1,0:T(8,128)S(1)} %pad_maximum_fusion.2.own), channel_id=1, source_target_pairs={{0,1},{1,2},{2,3},{3,4},{4,5},{5,6},{6,7},{7,8},{8,9},{9,10},{10,1... | collective-permute-start | bytes 36872 | tf_op jit(solution)/shard_map/ppermute | solution.py:422
  14.0 2.7 %start.1 = (f32[3,2,144,128]{3,2,1,0:T(8,128)S(1)}, f32[6,2,144,128]{3,2,1,0:T(8,128)S(1)}, f32[16,128]{1,0:T(8,128)S(1)}, f32[3,128,128]{2,1,0:T(8,128)}, f32[3,128,128]{2,1,0:T(8,128)}) custom-call(f32[3,2,128,128]{3,2,1,0:T(8,128)S(1)} %copy-done.1, f32[6,2,128,128]{3,2,1,0:T(8,128)S(1)} %copy-done, s32[1,128]{1,0:T(1,128)S(1)} %bitcast.5, ...), custom_call_target="tpu_custom_call" | custom-call | tf_op jit(solution)/shard_map/start/pallas_call | solution.py:395
  16.6 0.1 collective-permute-start.3
  16.7 3.5 %collective-permute-start.4 = (f32[3,128,128]{2,1,0:T(8,128)}, f32[3,128,128]{2,1,0:T(8,128)S(1)}, u32[]{:S(2)}, u32[]{:S(2)}) collective-permute-start(f32[3,128,128]{2,1,0:T(8,128)} %get-tuple-element.61), channel_id=1, source_target_pairs={{1,2},{3,4},{5,6},{7,8},{9,10},{11,12},{13,14},{2,1},{4,3},{6,5},{... | collective-permute-start | bytes 589832 | tf_op jit(solution)/shard_map/ppermute | solution.py:440
  20.2 0.0 collective-permute-done.one
  20.2 3.1 %collective-permute-start.1 = (f32[48,128]{1,0:T(8,128)S(1)}, f32[48,128]{1,0:T(8,128)S(1)}, u32[]{:S(2)}, u32[]{:S(2)}) collective-permute-start(f32[48,128]{1,0:T(8,128)S(1)} %pad_maximum_fusion.1), channel_id=1, source_target_pairs={{0,2},{1,3},{2,4},{3,5},{4,6},{5,7},{6,8},{7,9},{8,10},{9,11},{10,... | collective-permute-start | bytes 73736 | tf_op jit(solution)/shard_map/ppermute | solution.py:422
  23.3 2.5 %collective-permute-done.1.two = f32[48,128]{1,0:T(8,128)S(1)} collective-permute-done((f32[48,128]{1,0:T(8,128)S(1)}, f32[48,128]{1,0:T(8,128)S(1)}, u32[]{:S(2)}, u32[]{:S(2)}) %collective-permute-start.1) | collective-permute-done | bytes 24608 | tf_op jit(solution)/shard_map/ppermute | solution.py:422
  25.8 2.3 %collective-permute-start.2 = (f32[72,128]{1,0:T(8,128)S(1)}, f32[72,128]{1,0:T(8,128)S(1)}, u32[]{:S(2)}, u32[]{:S(2)}) collective-permute-start(f32[72,128]{1,0:T(8,128)S(1)} %pad_maximum_fusion), channel_id=1, source_target_pairs={{0,4},{1,5},{2,6},{3,7},{4,8},{5,9},{6,10},{7,11},{8,12},{9,13},{1... | collective-permute-start | bytes 110600 | tf_op jit(solution)/shard_map/ppermute | solution.py:422
  28.1 2.4 %collective-permute-done.2.four = f32[72,128]{1,0:T(8,128)S(1)} collective-permute-done((f32[72,128]{1,0:T(8,128)S(1)}, f32[72,128]{1,0:T(8,128)S(1)}, u32[]{:S(2)}, u32[]{:S(2)}) %collective-permute-start.2) | collective-permute-done | bytes 36896 | tf_op jit(solution)/shard_map/ppermute | solution.py:422
  30.5 0.5 trucks.1.surface
  31.0 0.9 %slice.8.parts = f32[6,36,128]{2,1,0:T(8,128)S(1)} slice(f32[16,36,128]{2,1,0:T(8,128)} %all-to-all-done), slice={[0:6], [0:36], [0:128]} | slice | bytes 221184 | tf_op jit(solution)/shard_map/slice | solution.py:455
  31.9 0.1 force.1
  32.0 0.0 collective-permute-done.3.msg
  32.0 2.0 %near0.1 = (f32[3,2,144,128]{3,2,1,0:T(8,128)S(1)}, f32[6,2,144,128]{3,2,1,0:T(8,128)S(1)}, f32[6,2,128,128]{3,2,1,0:T(8,128)S(1)}, f32[3,128,128]{2,1,0:T(8,128)S(1)}) custom-call(f32[3,2,144,128]{3,2,1,0:T(8,128)S(1)} %get-tuple-element.54.V0, ...), custom_call_target="tpu_custom_call", output_to_operand_aliasing={{0}: (0, {}), {1}: (1, {}), {2}: (2, {})} | custom-call | tf_op jit(solution)/shard_map/near0/pallas_call | solution.py:395
  34.0 2.2 %collective-permute-start.5 = (f32[3,128,128]{2,1,0:T(8,128)S(1)}, f32[3,128,128]{2,1,0:T(8,128)S(1)}, u32[]{:S(2)}, u32[]{:S(2)}) collective-permute-start(f32[3,128,128]{2,1,0:T(8,128)S(1)} %get-tuple-element.65), channel_id=1, source_target_pairs={{0,1},{1,0},{2,3},{3,2},{4,5},{5,4},{6,7},{7,6},{8,9},{9,8},{10,11... | collective-permute-start | bytes 589832 | tf_op jit(solution)/shard_map/ppermute | solution.py:520
  36.2 1.3 %far0.1 = (f32[3,2,144,128]{3,2,1,0:T(8,128)S(1)}, f32[6,2,144,128]{3,2,1,0:T(8,128)S(1)}, f32[6,2,128,128]{3,2,1,0:T(8,128)S(1)}, f32[3,128,128]{2,1,0:T(8,128)S(1)}) custom-call(f32[3,2,144,128]{3,2,1,0:T(8,128)S(1)} %get-tuple-element.58.V0, ...), custom_call_target="tpu_custom_call", output_to_operand_aliasing={{0}: (0, {}), {1}: (1, {}), {2}: (2, {})} | custom-call | tf_op jit(solution)/shard_map/far0/pallas_call | solution.py:395
  37.6 2.5 %collective-permute-start.6 = (f32[3,128,128]{2,1,0:T(8,128)S(1)}, f32[3,128,128]{2,1,0:T(8,128)S(1)}, u32[]{:S(2)}, u32[]{:S(2)}) collective-permute-start(f32[3,128,128]{2,1,0:T(8,128)S(1)} %get-tuple-element.69), channel_id=1, source_target_pairs={{1,2},{3,4},{5,6},{7,8},{9,10},{11,12},{13,14},{2,1},{4,3},{6,5},{... | collective-permute-start | bytes 589832 | tf_op jit(solution)/shard_map/ppermute | solution.py:518
  40.1 2.0 %near1.1 = (f32[3,2,144,128]{3,2,1,0:T(8,128)S(1)}, f32[6,2,144,128]{3,2,1,0:T(8,128)S(1)}, f32[6,2,128,128]{3,2,1,0:T(8,128)S(1)}, f32[3,128,128]{2,1,0:T(8,128)S(1)}) custom-call(f32[3,2,144,128]{3,2,1,0:T(8,128)S(1)} %get-tuple-element.62.V0, ...), custom_call_target="tpu_custom_call", output_to_operand_aliasing={{0}: (0, {}), {1}: (1, {}), {2}: (2, {})} | custom-call | tf_op jit(solution)/shard_map/near1/pallas_call | solution.py:395
  42.1 0.4 collective-permute-start.7
  42.5 4.2 %collective-permute-done.6.msg = f32[3,128,128]{2,1,0:T(8,128)S(1)} collective-permute-done((f32[3,128,128]{2,1,0:T(8,128)S(1)}, f32[3,128,128]{2,1,0:T(8,128)S(1)}, u32[]{:S(2)}, u32[]{:S(2)}) %collective-permute-start.6) | collective-permute-done | bytes 196640 | tf_op jit(solution)/shard_map/ppermute | solution.py:518
  46.7 1.3 %far1.1 = (f32[3,2,144,128]{3,2,1,0:T(8,128)S(1)}, f32[6,2,144,128]{3,2,1,0:T(8,128)S(1)}, f32[6,2,128,128]{3,2,1,0:T(8,128)S(1)}, f32[3,128,128]{2,1,0:T(8,128)S(1)}) custom-call(f32[3,2,144,128]{3,2,1,0:T(8,128)S(1)} %get-tuple-element.66.V0, ...), custom_call_target="tpu_custom_call", output_to_operand_aliasing={{0}: (0, {}), {1}: (1, {}), {2}: (2, {})} | custom-call | tf_op jit(solution)/shard_map/far1/pallas_call | solution.py:395
  48.0 2.5 %collective-permute-start.8 = (f32[3,128,128]{2,1,0:T(8,128)S(1)}, f32[3,128,128]{2,1,0:T(8,128)S(1)}, u32[]{:S(2)}, u32[]{:S(2)}) collective-permute-start(f32[3,128,128]{2,1,0:T(8,128)S(1)} %get-tuple-element.77), channel_id=1, source_target_pairs={{1,2},{3,4},{5,6},{7,8},{9,10},{11,12},{13,14},{2,1},{4,3},{6,5},{... | collective-permute-start | bytes 589832 | tf_op jit(solution)/shard_map/ppermute | solution.py:518
  50.5 2.0 %near2.1 = (f32[3,2,144,128]{3,2,1,0:T(8,128)S(1)}, f32[6,2,144,128]{3,2,1,0:T(8,128)S(1)}, f32[6,2,128,128]{3,2,1,0:T(8,128)S(1)}, f32[3,128,128]{2,1,0:T(8,128)S(1)}) custom-call(f32[3,2,144,128]{3,2,1,0:T(8,128)S(1)} %get-tuple-element.70.V0, ...), custom_call_target="tpu_custom_call", output_to_operand_aliasing={{0}: (0, {}), {1}: (1, {}), {2}: (2, {})} | custom-call | tf_op jit(solution)/shard_map/near2/pallas_call | solution.py:395
  52.5 0.0 collective-permute-start.9
  52.6 3.8 %collective-permute-done.8.msg = f32[3,128,128]{2,1,0:T(8,128)S(1)} collective-permute-done((f32[3,128,128]{2,1,0:T(8,128)S(1)}, f32[3,128,128]{2,1,0:T(8,128)S(1)}, u32[]{:S(2)}, u32[]{:S(2)}) %collective-permute-start.8) | collective-permute-done | bytes 196640 | tf_op jit(solution)/shard_map/ppermute | solution.py:518
  56.3 1.3 %far2.1 = (f32[3,2,144,128]{3,2,1,0:T(8,128)S(1)}, f32[6,2,144,128]{3,2,1,0:T(8,128)S(1)}, f32[6,2,128,128]{3,2,1,0:T(8,128)S(1)}, f32[3,128,128]{2,1,0:T(8,128)S(1)}) custom-call(f32[3,2,144,128]{3,2,1,0:T(8,128)S(1)} %get-tuple-element.74.V0, ...), custom_call_target="tpu_custom_call", output_to_operand_aliasing={{0}: (0, {}), {1}: (1, {}), {2}: (2, {})} | custom-call | tf_op jit(solution)/shard_map/far2/pallas_call | solution.py:395
  57.7 3.3 %collective-permute-start.10 = (f32[3,128,128]{2,1,0:T(8,128)S(1)}, f32[3,128,128]{2,1,0:T(8,128)S(1)}, u32[]{:S(2)}, u32[]{:S(2)}) collective-permute-start(f32[3,128,128]{2,1,0:T(8,128)S(1)} %get-tuple-element.85), channel_id=1, source_target_pairs={{1,2},{3,4},{5,6},{7,8},{9,10},{11,12},{13,14},{2,1},{4,3},{6,5},{... | collective-permute-start | bytes 589832 | tf_op jit(solution)/shard_map/ppermute | solution.py:518
  61.0 2.0 %near3.1 = (f32[3,2,144,128]{3,2,1,0:T(8,128)S(1)}, f32[6,2,144,128]{3,2,1,0:T(8,128)S(1)}, f32[6,2,128,128]{3,2,1,0:T(8,128)S(1)}, f32[3,128,128]{2,1,0:T(8,128)S(1)}) custom-call(f32[3,2,144,128]{3,2,1,0:T(8,128)S(1)} %get-tuple-element.78.V0, ...), custom_call_target="tpu_custom_call", output_to_operand_aliasing={{0}: (0, {}), {1}: (1, {}), {2}: (2, {})} | custom-call | tf_op jit(solution)/shard_map/near3/pallas_call | solution.py:395
  63.0 0.0 collective-permute-start.11
  63.0 2.6 %collective-permute-done.10.msg = f32[3,128,128]{2,1,0:T(8,128)S(1)} collective-permute-done((f32[3,128,128]{2,1,0:T(8,128)S(1)}, f32[3,128,128]{2,1,0:T(8,128)S(1)}, u32[]{:S(2)}, u32[]{:S(2)}) %collective-permute-start.10) | collective-permute-done | bytes 196640 | tf_op jit(solution)/shard_map/ppermute | solution.py:518
  65.7 1.3 %far3.1 = (f32[3,2,144,128]{3,2,1,0:T(8,128)S(1)}, f32[6,2,144,128]{3,2,1,0:T(8,128)S(1)}, f32[6,2,128,128]{3,2,1,0:T(8,128)S(1)}, f32[3,128,128]{2,1,0:T(8,128)S(1)}) custom-call(f32[3,2,144,128]{3,2,1,0:T(8,128)S(1)} %get-tuple-element.82.V0, ...), custom_call_target="tpu_custom_call", output_to_operand_aliasing={{0}: (0, {}), {1}: (1, {}), {2}: (2, {})} | custom-call | tf_op jit(solution)/shard_map/far3/pallas_call | solution.py:395
  67.0 3.7 %collective-permute-start.12 = (f32[3,128,128]{2,1,0:T(8,128)S(1)}, f32[3,128,128]{2,1,0:T(8,128)S(1)}, u32[]{:S(2)}, u32[]{:S(2)}) collective-permute-start(f32[3,128,128]{2,1,0:T(8,128)S(1)} %get-tuple-element.93), channel_id=1, source_target_pairs={{1,2},{3,4},{5,6},{7,8},{9,10},{11,12},{13,14},{2,1},{4,3},{6,5},{... | collective-permute-start | bytes 589832 | tf_op jit(solution)/shard_map/ppermute | solution.py:518
  70.7 2.0 %near4.1 = (f32[3,2,144,128]{3,2,1,0:T(8,128)S(1)}, f32[6,2,144,128]{3,2,1,0:T(8,128)S(1)}, f32[6,2,128,128]{3,2,1,0:T(8,128)S(1)}, f32[3,128,128]{2,1,0:T(8,128)S(1)}) custom-call(f32[3,2,144,128]{3,2,1,0:T(8,128)S(1)} %get-tuple-element.86.V0, ...), custom_call_target="tpu_custom_call", output_to_operand_aliasing={{0}: (0, {}), {1}: (1, {}), {2}: (2, {})} | custom-call | tf_op jit(solution)/shard_map/near4/pallas_call | solution.py:395
  72.7 0.0 collective-permute-start.13
  72.7 2.3 %collective-permute-done.12.msg = f32[3,128,128]{2,1,0:T(8,128)S(1)} collective-permute-done((f32[3,128,128]{2,1,0:T(8,128)S(1)}, f32[3,128,128]{2,1,0:T(8,128)S(1)}, u32[]{:S(2)}, u32[]{:S(2)}) %collective-permute-start.12) | collective-permute-done | bytes 196640 | tf_op jit(solution)/shard_map/ppermute | solution.py:518
  75.0 1.3 %far4.1 = (f32[3,2,144,128]{3,2,1,0:T(8,128)S(1)}, f32[6,2,144,128]{3,2,1,0:T(8,128)S(1)}, f32[6,2,128,128]{3,2,1,0:T(8,128)S(1)}, f32[3,128,128]{2,1,0:T(8,128)S(1)}) custom-call(f32[3,2,144,128]{3,2,1,0:T(8,128)S(1)} %get-tuple-element.90.V0, ...), custom_call_target="tpu_custom_call", output_to_operand_aliasing={{0}: (0, {}), {1}: (1, {}), {2}: (2, {})} | custom-call | tf_op jit(solution)/shard_map/far4/pallas_call | solution.py:395
  76.4 3.6 %collective-permute-start.14 = (f32[3,128,128]{2,1,0:T(8,128)S(1)}, f32[3,128,128]{2,1,0:T(8,128)S(1)}, u32[]{:S(2)}, u32[]{:S(2)}) collective-permute-start(f32[3,128,128]{2,1,0:T(8,128)S(1)} %get-tuple-element.101), channel_id=1, source_target_pairs={{1,2},{3,4},{5,6},{7,8},{9,10},{11,12},{13,14},{2,1},{4,3},{6,5},{... | collective-permute-start | bytes 589832 | tf_op jit(solution)/shard_map/ppermute | solution.py:518
  80.0 1.4 %near5.1 = (f32[3,2,144,128]{3,2,1,0:T(8,128)S(1)}, f32[6,2,144,128]{3,2,1,0:T(8,128)S(1)}, f32[6,2,128,128]{3,2,1,0:T(8,128)S(1)}) custom-call(f32[3,2,144,128]{3,2,1,0:T(8,128)S(1)} %get-tuple-element.94.V0, f32[6,2,144,128]{3,2,1,0:T(8,128)S(1)} %get-tuple-element.95.S0, ...), custom_call_target="tpu_custom_call", output_to_operand_aliasing={{0}: (0, {}), {1}: (1, {}), {2}: (2, {})} | custom-call | tf_op jit(solution)/shard_map/near5/pallas_call | solution.py:395
  81.4 3.0 %collective-permute-done.14.msg = f32[3,128,128]{2,1,0:T(8,128)S(1)} collective-permute-done((f32[3,128,128]{2,1,0:T(8,128)S(1)}, f32[3,128,128]{2,1,0:T(8,128)S(1)}, u32[]{:S(2)}, u32[]{:S(2)}) %collective-permute-start.14) | collective-permute-done | bytes 196640 | tf_op jit(solution)/shard_map/ppermute | solution.py:518
  84.4 2.1 %last.1 = (f32[3,2,144,128]{3,2,1,0:T(8,128)S(1)}, f32[6,2,144,128]{3,2,1,0:T(8,128)S(1)}, f32[6,2,128,128]{3,2,1,0:T(8,128)S(1)}, f32[3,2,128,128]{3,2,1,0:T(8,...) custom-call(f32[3,2,144,128]{3,2,1,0:T(8,128)S(1)} %get-tuple-elemen, ...), custom_call_target="tpu_custom_call", output_to_operand_aliasing={{0}: (0, {}), {1}: (1, {}), {2}: (2, {})} | custom-call | tf_op jit(solution)/shard_map/last/pallas_call | solution.py:395
  (36 shorter events, 0.1 us)
Async XLA Ops:
  0.6 1.2 %copy-start.2 = (f32[1,8,1536]{2,1,0:T(8,128)S(1)}, f32[1,8,1536]{2,1,0:T(8,128)}, u32[]{:S(2)}) copy-start(f32[1,8,1536]{2,1,0:T(8,128)} %param.18) | copy-start | bytes 147460
  0.6 1.2 %copy-start.3 = (s32[8]{0:T(128)S(1)}, s32[8]{0:T(128)}, u32[]{:S(2)}) copy-start(s32[8]{0:T(128)} %param.27) | copy-start | bytes 100
  0.7 13.2 %copy-start.1 = (f32[3,2,128,128]{3,2,1,0:T(8,128)S(1)}, f32[3,2,128,128]{3,2,1,0:T(8,128)}, u32[]{:S(2)}) copy-start(f32[3,2,128,128]{3,2,1,0:T(8,128)} %velocity.1) | copy-start | bytes 1179652
  1.8 12.0 %copy-start = (f32[6,2,128,128]{3,2,1,0:T(8,128)S(1)}, f32[6,2,128,128]{3,2,1,0:T(8,128)}, u32[]{:S(2)}) copy-start(f32[6,2,128,128]{3,2,1,0:T(8,128)} %stress.1) | copy-start | bytes 2359300
  3.0 6.6 %copy-start.11 = (s32[6,16]{1,0:T(8,128)S(1)}, s32[6,16]{1,0:T(8,128)}, u32[]{:S(2)}) copy-start(s32[6,16]{1,0:T(8,128)} %param.25) | copy-start | bytes 1156
  3.0 27.9 %all-to-all-start = ((f32[16,36,128]{2,1,0:T(8,128)}), f32[16,36,128]{2,1,0:T(8,128)}, u32[]{:S(2)}, u32[]{:S(2)}) async-start(f32[16,36,128]{2,1,0:T(8,128)} %split.1), calls=%async_computation | async-start | bytes 655360 | tf_op jit(solution)/shard_map/all_to_all | solution.py:452
  9.6 0.7 copy-start.10
  10.3 3.5 %copy-start.7 = (f32[8]{0:T(128)S(1)}, f32[8]{0:T(128)}, u32[]{:S(2)}) copy-start(f32[8]{0:T(128)} %buoy.1) | copy-start | bytes 100
  10.4 3.6 %copy-start.8 = (f32[8]{0:T(128)S(1)}, f32[8]{0:T(128)}, u32[]{:S(2)}) copy-start(f32[8]{0:T(128)} %rate.1) | copy-start | bytes 100
  10.4 3.6 %copy-start.9 = (f32[8]{0:T(128)S(1)}, f32[8]{0:T(128)}, u32[]{:S(2)}) copy-start(f32[8]{0:T(128)} %defect.1) | copy-start | bytes 100
  10.4 3.6 %copy-start.4 = (s32[128]{0:T(128)S(1)}, s32[128]{0:T(128)}, u32[]{:S(2)}) copy-start(s32[128]{0:T(128)} %param.24) | copy-start | bytes 1540
  10.4 3.6 %copy-start.5 = (f32[8]{0:T(128)S(1)}, f32[8]{0:T(128)}, u32[]{:S(2)}) copy-start(f32[8]{0:T(128)} %lam.1) | copy-start | bytes 100
  10.4 3.6 %copy-start.6 = (f32[8]{0:T(128)S(1)}, f32[8]{0:T(128)}, u32[]{:S(2)}) copy-start(f32[8]{0:T(128)} %mu.1) | copy-start | bytes 100
  10.4 9.8 %collective-permute-start = (f32[24,128]{1,0:T(8,128)S(1)}, f32[24,128]{1,0:T(8,128)S(1)}, u32[]{:S(2)}, u32[]{:S(2)}) collective-permute-start(f32[24,128]{1,0:T(8,128)S(1)} %pad_maximum_fusion.2.own), channel_id=1, source_target_pairs={{0,1},{1,2},{2,3},{3,4},{4,5},{5,6},{6,7},{7,8},{8,9},{9,10},{10,1... | collective-permute-start | bytes 36872 | tf_op jit(solution)/shard_map/ppermute | solution.py:422
  16.6 15.4 %collective-permute-start.3 = (f32[3,128,128]{2,1,0:T(8,128)}, f32[3,128,128]{2,1,0:T(8,128)S(1)}, u32[]{:S(2)}, u32[]{:S(2)}) collective-permute-start(f32[3,128,128]{2,1,0:T(8,128)} %get-tuple-element.57), channel_id=1, source_target_pairs={{0,1},{1,0},{2,3},{3,2},{4,5},{5,4},{6,7},{7,6},{8,9},{9,8},{10,11... | collective-permute-start | bytes 589832 | tf_op jit(solution)/shard_map/ppermute | solution.py:441
  16.7 19.5 %collective-permute-start.4 = (f32[3,128,128]{2,1,0:T(8,128)}, f32[3,128,128]{2,1,0:T(8,128)S(1)}, u32[]{:S(2)}, u32[]{:S(2)}) collective-permute-start(f32[3,128,128]{2,1,0:T(8,128)} %get-tuple-element.61), channel_id=1, source_target_pairs={{1,2},{3,4},{5,6},{7,8},{9,10},{11,12},{13,14},{2,1},{4,3},{6,5},{... | collective-permute-start | bytes 589832 | tf_op jit(solution)/shard_map/ppermute | solution.py:440
  20.2 5.6 %collective-permute-start.1 = (f32[48,128]{1,0:T(8,128)S(1)}, f32[48,128]{1,0:T(8,128)S(1)}, u32[]{:S(2)}, u32[]{:S(2)}) collective-permute-start(f32[48,128]{1,0:T(8,128)S(1)} %pad_maximum_fusion.1), channel_id=1, source_target_pairs={{0,2},{1,3},{2,4},{3,5},{4,6},{5,7},{6,8},{7,9},{8,10},{9,11},{10,... | collective-permute-start | bytes 73736 | tf_op jit(solution)/shard_map/ppermute | solution.py:422
  25.8 2.3 %copy-start.12 = (s32[6,16]{1,0:T(8,128)S(1)}, s32[6,16]{1,0:T(8,128)}, u32[]{:S(2)}) copy-start(s32[6,16]{1,0:T(8,128)} %param.26) | copy-start | bytes 1156
  25.8 4.7 %collective-permute-start.2 = (f32[72,128]{1,0:T(8,128)S(1)}, f32[72,128]{1,0:T(8,128)S(1)}, u32[]{:S(2)}, u32[]{:S(2)}) collective-permute-start(f32[72,128]{1,0:T(8,128)S(1)} %pad_maximum_fusion), channel_id=1, source_target_pairs={{0,4},{1,5},{2,6},{3,7},{4,8},{5,9},{6,10},{7,11},{8,12},{9,13},{1... | collective-permute-start | bytes 110600 | tf_op jit(solution)/shard_map/ppermute | solution.py:422
  34.0 6.0 %collective-permute-start.5 = (f32[3,128,128]{2,1,0:T(8,128)S(1)}, f32[3,128,128]{2,1,0:T(8,128)S(1)}, u32[]{:S(2)}, u32[]{:S(2)}) collective-permute-start(f32[3,128,128]{2,1,0:T(8,128)S(1)} %get-tuple-element.65), channel_id=1, source_target_pairs={{0,1},{1,0},{2,3},{3,2},{4,5},{5,4},{6,7},{7,6},{8,9},{9,8},{10,11... | collective-permute-start | bytes 589832 | tf_op jit(solution)/shard_map/ppermute | solution.py:520
  37.6 9.1 %collective-permute-start.6 = (f32[3,128,128]{2,1,0:T(8,128)S(1)}, f32[3,128,128]{2,1,0:T(8,128)S(1)}, u32[]{:S(2)}, u32[]{:S(2)}) collective-permute-start(f32[3,128,128]{2,1,0:T(8,128)S(1)} %get-tuple-element.69), channel_id=1, source_target_pairs={{1,2},{3,4},{5,6},{7,8},{9,10},{11,12},{13,14},{2,1},{4,3},{6,5},{... | collective-permute-start | bytes 589832 | tf_op jit(solution)/shard_map/ppermute | solution.py:518
  42.1 8.5 %collective-permute-start.7 = (f32[3,128,128]{2,1,0:T(8,128)S(1)}, f32[3,128,128]{2,1,0:T(8,128)S(1)}, u32[]{:S(2)}, u32[]{:S(2)}) collective-permute-start(f32[3,128,128]{2,1,0:T(8,128)S(1)} %get-tuple-element.73), channel_id=1, source_target_pairs={{0,1},{1,0},{2,3},{3,2},{4,5},{5,4},{6,7},{7,6},{8,9},{9,8},{10,11... | collective-permute-start | bytes 589832 | tf_op jit(solution)/shard_map/ppermute | solution.py:520
  48.0 8.3 %collective-permute-start.8 = (f32[3,128,128]{2,1,0:T(8,128)S(1)}, f32[3,128,128]{2,1,0:T(8,128)S(1)}, u32[]{:S(2)}, u32[]{:S(2)}) collective-permute-start(f32[3,128,128]{2,1,0:T(8,128)S(1)} %get-tuple-element.77), channel_id=1, source_target_pairs={{1,2},{3,4},{5,6},{7,8},{9,10},{11,12},{13,14},{2,1},{4,3},{6,5},{... | collective-permute-start | bytes 589832 | tf_op jit(solution)/shard_map/ppermute | solution.py:518
  52.5 8.4 %collective-permute-start.9 = (f32[3,128,128]{2,1,0:T(8,128)S(1)}, f32[3,128,128]{2,1,0:T(8,128)S(1)}, u32[]{:S(2)}, u32[]{:S(2)}) collective-permute-start(f32[3,128,128]{2,1,0:T(8,128)S(1)} %get-tuple-element.81), channel_id=1, source_target_pairs={{0,1},{1,0},{2,3},{3,2},{4,5},{5,4},{6,7},{7,6},{8,9},{9,8},{10,11... | collective-permute-start | bytes 589832 | tf_op jit(solution)/shard_map/ppermute | solution.py:520
  57.7 8.0 %collective-permute-start.10 = (f32[3,128,128]{2,1,0:T(8,128)S(1)}, f32[3,128,128]{2,1,0:T(8,128)S(1)}, u32[]{:S(2)}, u32[]{:S(2)}) collective-permute-start(f32[3,128,128]{2,1,0:T(8,128)S(1)} %get-tuple-element.85), channel_id=1, source_target_pairs={{1,2},{3,4},{5,6},{7,8},{9,10},{11,12},{13,14},{2,1},{4,3},{6,5},{... | collective-permute-start | bytes 589832 | tf_op jit(solution)/shard_map/ppermute | solution.py:518
  63.0 7.7 %collective-permute-start.11 = (f32[3,128,128]{2,1,0:T(8,128)S(1)}, f32[3,128,128]{2,1,0:T(8,128)S(1)}, u32[]{:S(2)}, u32[]{:S(2)}) collective-permute-start(f32[3,128,128]{2,1,0:T(8,128)S(1)} %get-tuple-element.89), channel_id=1, source_target_pairs={{0,1},{1,0},{2,3},{3,2},{4,5},{5,4},{6,7},{7,6},{8,9},{9,8},{10,11... | collective-permute-start | bytes 589832 | tf_op jit(solution)/shard_map/ppermute | solution.py:520
  67.0 8.0 %collective-permute-start.12 = (f32[3,128,128]{2,1,0:T(8,128)S(1)}, f32[3,128,128]{2,1,0:T(8,128)S(1)}, u32[]{:S(2)}, u32[]{:S(2)}) collective-permute-start(f32[3,128,128]{2,1,0:T(8,128)S(1)} %get-tuple-element.93), channel_id=1, source_target_pairs={{1,2},{3,4},{5,6},{7,8},{9,10},{11,12},{13,14},{2,1},{4,3},{6,5},{... | collective-permute-start | bytes 589832 | tf_op jit(solution)/shard_map/ppermute | solution.py:518
  72.7 7.3 %collective-permute-start.13 = (f32[3,128,128]{2,1,0:T(8,128)S(1)}, f32[3,128,128]{2,1,0:T(8,128)S(1)}, u32[]{:S(2)}, u32[]{:S(2)}) collective-permute-start(f32[3,128,128]{2,1,0:T(8,128)S(1)} %get-tuple-element.97), channel_id=1, source_target_pairs={{0,1},{1,0},{2,3},{3,2},{4,5},{5,4},{6,7},{7,6},{8,9},{9,8},{10,11... | collective-permute-start | bytes 589832 | tf_op jit(solution)/shard_map/ppermute | solution.py:520
  76.4 8.0 %collective-permute-start.14 = (f32[3,128,128]{2,1,0:T(8,128)S(1)}, f32[3,128,128]{2,1,0:T(8,128)S(1)}, u32[]{:S(2)}, u32[]{:S(2)}) collective-permute-start(f32[3,128,128]{2,1,0:T(8,128)S(1)} %get-tuple-element.101), channel_id=1, source_target_pairs={{1,2},{3,4},{5,6},{7,8},{9,10},{11,12},{13,14},{2,1},{4,3},{6,5},{... | collective-permute-start | bytes 589832 | tf_op jit(solution)/shard_map/ppermute | solution.py:518

commit v2 on v1

v2 whole, which is shorter than its diff:
```python
import functools

import jax
import jax.numpy as jnp
import numpy as np
from jax import lax
from jax.experimental import pallas as pl
from jax.experimental.pallas import tpu as pltpu
from jax.sharding import PartitionSpec as P

STEPS = 6
FY = 8
FZ = 64
DT = 0.25
PAD = 8
ROWS = 16
UNROLL = 4
VMEM_LIMIT = 32 * 1024 * 1024

C_B, C_B0, C_B1, C_M0, C_M1, C_LAM, C_MU2, C_MU, C_K1, C_K2, C_K2H, C_L0 = range(12)
N_COEF = 16

VX, VY, VZ = range(3)
XX, YY, ZZ, XY, XZ, YZ = range(6)


def lane_roll(x, shift):
    return pltpu.roll(x, shift % x.shape[-1], x.ndim - 1)


def before(x):
    return lane_roll(x, 1)


def after(x):
    return lane_roll(x, -1)


def over_rows(count, work):
    def step(i, carry):
        work(pl.multiple_of(i * ROWS, ROWS))
        return carry

    lax.fori_loop(0, count // ROWS, step, 0, unroll=UNROLL)


def coefs(coef_ref, ids):
    return [coef_ref[i : i + 1, :] for i in ids]


def place():
    index = lax.axis_index("line")
    return lax.rem(index, 2) == 0, index > 0, index < lax.axis_size("line") - 1


def spans(r):
    return pl.ds(PAD + r, ROWS), pl.ds(PAD + r - 1, ROWS), pl.ds(PAD + r + 1, ROWS), pl.ds(r, ROWS)


def zero_edges(ref):
    across = ref.shape[-2] - 2 * PAD
    edge = jnp.zeros((PAD, ref.shape[-1]), jnp.float32)
    for where in np.ndindex(*ref.shape[:-2]):
        ref[(*where, pl.ds(0, PAD))] = edge
        ref[(*where, pl.ds(PAD + across, PAD))] = edge


def add_force(ref, index, force, which, first_row):
    rows = pl.ds(first_row, 16)
    ref[(*index, rows)] = ref[(*index, rows)] + force[which]


def pre_ahead(V, S, coef_ref, msg, force, window):
    b, b0 = coefs(coef_ref, (C_B, C_B0))

    def work(r):
        here, up, _, out = spans(r)
        sxy, sxz = S[XY, 1, here], S[XZ, 1, here]
        px = V[VX, 1, here] + b * (sxy - S[XY, 1, up] + sxz - S[XX, 1, here]) - b0 * before(sxz)
        V[VX, 1, here] = px
        if msg is not None:
            msg[0, out] = sxy
            msg[1, out] = sxz
            msg[2, out] = px

    over_rows(V.shape[2] - 2 * PAD, work)
    if force is not None:
        add_force(V, (VX, 1), force, (VX, 2), PAD + window)
        if msg is not None:
            add_force(msg, (2,), force, (VX, 2), window)


def pre_behind(V, S, coef_ref, msg, force, window):
    b, b0, b1 = coefs(coef_ref, (C_B, C_B0, C_B1))

    def work(r):
        here, up, down, out = spans(r)
        syz, szz = S[YZ, 0, here], S[ZZ, 0, here]
        qy = V[VY, 0, here] + b * (S[XY, 0, here] + S[YY, 0, down] - S[YY, 0, here] + syz) - b0 * before(syz)
        qz = V[VZ, 0, here] + b * (S[XZ, 0, here] + syz - S[YZ, 0, up] - szz) + b1 * after(szz)
        V[VY, 0, here] = qy
        V[VZ, 0, here] = qz
        if msg is not None:
            msg[0, out] = S[XX, 0, here]
            msg[1, out] = qy
            msg[2, out] = qz

    over_rows(V.shape[2] - 2 * PAD, work)
    if force is not None:
        add_force(V, (VY, 0), force, (VY, 0), PAD + window)
        add_force(V, (VZ, 0), force, (VZ, 0), PAD + window)
        if msg is not None:
            add_force(msg, (1,), force, (VY, 0), window)
            add_force(msg, (2,), force, (VZ, 0), window)


def inner(V, S, coef_ref, force, window):
    b, b0, b1 = coefs(coef_ref, (C_B, C_B0, C_B1))

    def work(r):
        here, up, down, _ = spans(r)
        sxy, sxz = S[XY, 0, here], S[XZ, 0, here]
        V[VX, 0, here] = (
            V[VX, 0, here]
            + b * (S[XX, 1, here] - S[XX, 0, here] + sxy - S[XY, 0, up] + sxz)
            - b0 * before(sxz)
        )
        syz, szz = S[YZ, 1, here], S[ZZ, 1, here]
        V[VY, 1, here] = (
            V[VY, 1, here]
            + b * (S[XY, 1, here] - sxy + S[YY, 1, down] - S[YY, 1, here] + syz)
            - b0 * before(syz)
        )
        V[VZ, 1, here] = (
            V[VZ, 1, here]
            + b * (S[XZ, 1, here] - sxz + syz - S[YZ, 1, up] - szz)
            + b1 * after(szz)
        )

    over_rows(V.shape[2] - 2 * PAD, work)
    add_force(V, (VX, 0), force, (VX, 1), PAD + window)
    add_force(V, (VY, 1), force, (VY, 1), PAD + window)
    add_force(V, (VZ, 1), force, (VZ, 1), PAD + window)


def post(V, S, R, coef_ref, surface, cell, column, behind_x, ahead_y, ahead_z):
    m0, m1, lam, mu2, mu, k1, k2, k2h, l0 = coefs(
        coef_ref, (C_M0, C_M1, C_LAM, C_MU2, C_MU, C_K1, C_K2, C_K2H, C_L0)
    )

    def work(r):
        here, up, down, out = spans(r)
        vx, vy, vz = V[VX, cell, here], V[VY, cell, here], V[VZ, cell, here]
        exx = vx - behind_x(r)
        eyy = vy - V[VY, cell, up]
        ezz = vz - m0 * before(vz)
        exy = V[VX, cell, down] - vx + (ahead_y(r) - vy)
        exz = m1 * after(vx) - vx + (ahead_z(r) - vz)
        eyz = m1 * after(vy) - vy + (V[VZ, cell, down] - vz)
        volume = lam * (exx + eyy + ezz)
        for comp, e in ((XX, exx), (YY, eyy), (ZZ, ezz)):
            old = R[comp, cell, out]
            new = S[comp, cell, here] + (volume + mu2 * e) + DT * old
            if comp == ZZ:
                new = new + l0 * lane_roll(surface[out, :], -column)
            S[comp, cell, here] = new
            R[comp, cell, out] = k1 * old - k2 * e
        for comp, e in ((XY, exy), (XZ, exz), (YZ, eyz)):
            old = R[comp, cell, out]
            S[comp, cell, here] = S[comp, cell, here] + mu * e + DT * old
            R[comp, cell, out] = k1 * old - k2h * e

    over_rows(R.shape[2], work)


def response_behind(V, S, coef_ref, D, W):
    b, b0, b1, m0, m1, lam, mu2, mu = coefs(coef_ref, (C_B, C_B0, C_B1, C_M0, C_M1, C_LAM, C_MU2, C_MU))

    def work(r):
        here, up, down, out = spans(r)
        sxy = S[XY, 1, here]
        vy, vz = -b * sxy, -b * S[XZ, 1, here]
        exx = -V[VX, 1, here]
        eyy = b * (S[XY, 1, up] - sxy)
        ezz = vz - m0 * before(vz)
        volume = lam * (exx + eyy + ezz)
        dyy, dzz = volume + mu2 * eyy, volume + mu2 * ezz
        dyz = mu * (m1 * after(vy) - vy - b * S[XZ, 1, down] - vz)
        W[0, here] = dyy
        W[1, here] = dyz
        D[0, out] = volume + mu2 * exx
        D[1, out] = vy + b * (dyz - mu * vy - dyy) - b0 * before(dyz)
        D[2, out] = vz + b * (dyz - mu * vz - dzz) + b1 * after(dzz)

    over_rows(D.shape[1], work)

    def rest(r):
        _, up, down, out = spans(r)
        D[1, out] = D[1, out] + b * W[0, down]
        D[2, out] = D[2, out] - b * W[1, up]

    over_rows(D.shape[1], rest)


def response_ahead(V, S, coef_ref, D, W):
    b, b0, m1, lam, mu2, mu = coefs(coef_ref, (C_B, C_B0, C_M1, C_LAM, C_MU2, C_MU))

    def work(r):
        here, _, down, out = spans(r)
        vx = b * S[XX, 0, here]
        dxy = mu * (b * S[XX, 0, down] - vx + V[VY, 0, here])
        dxz = mu * (m1 * after(vx) - vx + V[VZ, 0, here])
        W[0, here] = dxy
        D[0, out] = dxy
        D[1, out] = dxz
        D[2, out] = vx + b * (dxy + dxz - (lam + mu2) * vx) - b0 * before(dxz)

    over_rows(D.shape[1], work)

    def rest(r):
        _, up, _, out = spans(r)
        D[2, out] = D[2, out] - b * W[0, up]

    over_rows(D.shape[1], rest)


def early_ahead(V, S, R, coef_ref, msg, W, force, window):
    b, b0, m0, m1, lam, mu2, mu = coefs(coef_ref, (C_B, C_B0, C_M0, C_M1, C_LAM, C_MU2, C_MU))

    def work(r):
        here, up, down, out = spans(r)
        vx, vy, vz = V[VX, 1, here], V[VY, 1, here], V[VZ, 1, here]
        exx = vx - V[VX, 0, here]
        volume = lam * (exx + (vy - V[VY, 1, up]) + (vz - m0 * before(vz)))
        sxx = S[XX, 1, here] + (volume + mu2 * exx) + DT * R[XX, 1, out]
        sxy = S[XY, 1, here] + mu * (V[VX, 1, down] - vx - vy) + DT * R[XY, 1, out]
        sxz = S[XZ, 1, here] + mu * (m1 * after(vx) - vx - vz) + DT * R[XZ, 1, out]
        W[0, here] = sxy
        msg[0, out] = sxy
        msg[1, out] = sxz
        msg[2, out] = vx + b * (sxy + sxz - sxx) - b0 * before(sxz)

    over_rows(msg.shape[1], work)

    def rest(r):
        _, up, _, out = spans(r)
        msg[2, out] = msg[2, out] - b * W[0, up]

    over_rows(msg.shape[1], rest)
    add_force(msg, (2,), force, (VX, 2), window)


def early_behind(V, S, R, coef_ref, surface, column, msg, W, force, window):
    b, b0, b1, m0, m1, lam, mu2, mu, l0 = coefs(
        coef_ref, (C_B, C_B0, C_B1, C_M0, C_M1, C_LAM, C_MU2, C_MU, C_L0)
    )

    def work(r):
        here, up, down, out = spans(r)
        vx, vy, vz = V[VX, 0, here], V[VY, 0, here], V[VZ, 0, here]
        eyy = vy - V[VY, 0, up]
        ezz = vz - m0 * before(vz)
        volume = lam * (vx + eyy + ezz)
        sxx = S[XX, 0, here] + (volume + mu2 * vx) + DT * R[XX, 0, out]
        syy = S[YY, 0, here] + (volume + mu2 * eyy) + DT * R[YY, 0, out]
        szz = S[ZZ, 0, here] + (volume + mu2 * ezz) + DT * R[ZZ, 0, out]
        szz = szz + l0 * lane_roll(surface[out, :], -column)
        sxy = S[XY, 0, here] + mu * (V[VX, 0, down] - vx + (V[VY, 1, here] - vy)) + DT * R[XY, 0, out]
        sxz = S[XZ, 0, here] + mu * (m1 * after(vx) - vx + (V[VZ, 1, here] - vz)) + DT * R[XZ, 0, out]
        syz = S[YZ, 0, here] + mu * (m1 * after(vy) - vy + (V[VZ, 0, down] - vz)) + DT * R[YZ, 0, out]
        W[0, here] = syy
        W[1, here] = syz
        msg[0, out] = sxx
        msg[1, out] = vy + b * (sxy - syy + syz) - b0 * before(syz)
        msg[2, out] = vz + b * (sxz + syz - szz) + b1 * after(szz)

    over_rows(msg.shape[1], work)

    def rest(r):
        _, up, down, out = spans(r)
        msg[1, out] = msg[1, out] + b * W[0, down]
        msg[2, out] = msg[2, out] - b * W[1, up]

    over_rows(msg.shape[1], rest)
    add_force(msg, (1,), force, (VY, 0), window)
    add_force(msg, (2,), force, (VZ, 0), window)


def ahead_bond(V, S, R, coef_ref, force, surface, msg, missing, G, step, window, respond=None):
    (b,) = coefs(coef_ref, (C_B,))
    _, _, has_ahead = place()
    keep = jnp.where(has_ahead, 1.0, 0.0).astype(jnp.float32)

    def got(i, out):
        return msg[i, out] if missing is None else msg[i, out] + missing[i, out]

    def work(r):
        here, _, _, out = spans(r)
        V[VX, 1, here] = V[VX, 1, here] + (keep * b) * got(0, out)
        G[0, out] = keep * (got(1, out) - b * S[XY, 1, here])
        G[1, out] = keep * (got(2, out) - b * S[XZ, 1, here])

    over_rows(R.shape[2], work)
    if step == 0:
        add_force(G, (0,), force, (VY, 2), window)
        add_force(G, (1,), force, (VZ, 2), window)
    if respond is not None:
        respond()
    post(
        V, S, R, coef_ref, surface, 1, 2 * step + 1,
        lambda r: V[VX, 0, pl.ds(PAD + r, ROWS)],
        lambda r: G[0, pl.ds(r, ROWS)],
        lambda r: G[1, pl.ds(r, ROWS)],
    )


def behind_bond(V, S, R, coef_ref, force, surface, msg, missing, G, step, window, respond=None):
    (b,) = coefs(coef_ref, (C_B,))
    _, has_behind, _ = place()
    keep = jnp.where(has_behind, 1.0, 0.0).astype(jnp.float32)

    def got(i, out):
        return msg[i, out] if missing is None else msg[i, out] + missing[i, out]

    def work(r):
        here, _, _, out = spans(r)
        V[VY, 0, here] = V[VY, 0, here] - (keep * b) * got(0, out)
        V[VZ, 0, here] = V[VZ, 0, here] - (keep * b) * got(1, out)
        G[0, out] = keep * (got(2, out) + b * S[XX, 0, here])

    over_rows(R.shape[2], work)
    if step == 0:
        add_force(G, (0,), force, (VX, 0), window)
    if respond is not None:
        respond()
    post(
        V, S, R, coef_ref, surface, 0, 2 * step,
        lambda r: G[0, pl.ds(r, ROWS)],
        lambda r: V[VY, 1, pl.ds(PAD + r, ROWS)],
        lambda r: V[VZ, 1, pl.ds(PAD + r, ROWS)],
    )


def start_kernel(
    velocity, stress, memory, layer_ref, lam, mu, buoy, rate, defect,
    V, S, R, coef_ref, msg_near, msg_far, sems,
):
    across = velocity.shape[2]
    inside = pl.ds(PAD, across)
    copies = [pltpu.make_async_copy(stress.at[i], S.at[i, :, inside], sems.at[i]) for i in range(6)]
    copies += [pltpu.make_async_copy(velocity.at[i], V.at[i, :, inside], sems.at[6 + i]) for i in range(3)]
    late = [pltpu.make_async_copy(memory.at[i], R.at[i], sems.at[9 + i]) for i in range(6)]
    for copy in copies + late:
        copy.start()
    zero_edges(V)
    zero_edges(S)
    layer = layer_ref[...]

    def per_depth(table):
        row = jnp.zeros(layer.shape, jnp.float32)
        for level in range(table.shape[0]):
            row = jnp.where(layer == level, table[level], row)
        return row

    lane = lax.broadcasted_iota(jnp.int32, layer.shape, 1)
    not_first = jnp.where(lane > 0, 1.0, 0.0).astype(jnp.float32)
    not_last = jnp.where(lane < layer.shape[1] - 1, 1.0, 0.0).astype(jnp.float32)
    b = DT * per_depth(buoy)
    two_mu = (2.0 * DT) * per_depth(mu)
    decay = DT * per_depth(rate)
    drop = 2.0 * decay * per_depth(defect)
    for row, value in (
        (C_B, b),
        (C_B0, b * not_first),
        (C_B1, b * not_last),
        (C_M0, not_first),
        (C_M1, not_last),
        (C_LAM, DT * per_depth(lam)),
        (C_MU2, two_mu),
        (C_MU, 0.5 * two_mu),
        (C_K1, 1.0 - decay),
        (C_K2, drop),
        (C_K2H, 0.5 * drop),
        (C_L0, DT * (1.0 - not_first)),
    ):
        coef_ref[row : row + 1, :] = value
    coef_ref[12:16, :] = jnp.zeros((4, layer.shape[1]), jnp.float32)
    for copy in copies:
        copy.wait()
    even, _, _ = place()

    @pl.when(even)
    def _():
        pre_ahead(V, S, coef_ref, msg_near, None, 0)
        pre_behind(V, S, coef_ref, msg_far, None, 0)

    @pl.when(jnp.logical_not(even))
    def _():
        pre_behind(V, S, coef_ref, msg_near, None, 0)
        pre_ahead(V, S, coef_ref, msg_far, None, 0)

    for copy in late:
        copy.wait()


def first_kernel(window, V0, S, R, coef_ref, force, surface, V, msg, W):
    even, _, _ = place()
    zero_edges(W)
    now, then = force.at[0], force.at[1]
    add_force(V, (VX, 1), now, (VX, 2), PAD + window)
    add_force(V, (VY, 0), now, (VY, 0), PAD + window)
    add_force(V, (VZ, 0), now, (VZ, 0), PAD + window)
    inner(V, S, coef_ref, now, window)

    @pl.when(even)
    def _():
        early_behind(V, S, R, coef_ref, surface, 0, msg, W, then, window)

    @pl.when(jnp.logical_not(even))
    def _():
        early_ahead(V, S, R, coef_ref, msg, W, then, window)


def near_kernel(step, window, V0, S0, R0, coef_ref, force, surface, msg, V, S, R, *rest):
    G = rest[-1]
    even, _, _ = place()
    more = step < STEPS - 1

    @pl.when(even)
    def _():
        ahead_bond(V, S, R, coef_ref, force.at[step], surface, msg, None, G, step, window)
        if more:
            pre_ahead(V, S, coef_ref, rest[0], force.at[step + 1], window)

    @pl.when(jnp.logical_not(even))
    def _():
        behind_bond(V, S, R, coef_ref, force.at[step], surface, msg, None, G, step, window)
        if more:
            pre_behind(V, S, coef_ref, rest[0], force.at[step + 1], window)


def far_kernel(step, window, V0, S0, R0, coef_ref, force, surface, msg, *rest):
    rest = list(rest)
    missing = rest.pop(0) if step > 0 else None
    V, S, R, D = rest[:4]
    G, W = rest[-2:]
    early = rest[4] if step < STEPS - 2 else None
    even, _, _ = place()
    zero_edges(W)
    here, then = force.at[step], force.at[step + 1]

    @pl.when(even)
    def _():
        behind_bond(
            V, S, R, coef_ref, here, surface, msg, missing, G, step, window,
            lambda: response_ahead(V, S, coef_ref, D, W),
        )
        pre_behind(V, S, coef_ref, None, then, window)

    @pl.when(jnp.logical_not(even))
    def _():
        ahead_bond(
            V, S, R, coef_ref, here, surface, msg, missing, G, step, window,
            lambda: response_behind(V, S, coef_ref, D, W),
        )
        pre_ahead(V, S, coef_ref, None, then, window)

    inner(V, S, coef_ref, then, window)
    if early is not None:
        later = force.at[step + 2]

        @pl.when(even)
        def _():
            early_behind(V, S, R, coef_ref, surface, 2 * (step + 1), early, W, later, window)

        @pl.when(jnp.logical_not(even))
        def _():
            early_ahead(V, S, R, coef_ref, early, W, later, window)


def last_kernel(
    step, window, V0, S0, R0, coef_ref, force, surface, msg, missing, V, S, R, v_out, s_out, r_out, G, sems
):
    even, _, _ = place()
    here = force.at[step]
    inside = pl.ds(PAD, R.shape[2])

    def copies(cell):
        return [
            pltpu.make_async_copy(V.at[:, cell, inside], v_out.at[:, cell], sems.at[cell, 0]),
            pltpu.make_async_copy(S.at[:, cell, inside], s_out.at[:, cell], sems.at[cell, 1]),
            pltpu.make_async_copy(R.at[:, cell], r_out.at[:, cell], sems.at[cell, 2]),
        ]

    def finish(cell, bond):
        done, other = copies(1 - cell), copies(cell)
        for copy in done:
            copy.start()
        bond(V, S, R, coef_ref, here, surface, msg, missing, G, step, window)
        for copy in other:
            copy.start()
        for copy in done + other:
            copy.wait()

    @pl.when(even)
    def _():
        finish(0, behind_bond)

    @pl.when(jnp.logical_not(even))
    def _():
        finish(1, ahead_bond)


ENTRY_ROW, TRUCK_ROW = 36, 40


def lane_blocks(table, width):
    return sum(lane_roll(table[s : s + 1, :], s * width) for s in range(STEPS))


def split_kernel(record, cells, loads, entries, out):
    tiles, _, lanes = out.shape
    slots = loads.shape[0]
    pieces = record.shape[1] // lanes
    third = pieces // 3
    cell_of = cells[...]
    row = lax.broadcasted_iota(jnp.int32, (3 * tiles, cell_of.shape[1]), 0)
    first = lax.div(row, 3) * 2 + lax.rem(row, 3)

    def share(cell, columns):
        hit = jnp.where(cell == cell_of, 1.0, 0.0).astype(jnp.float32)
        return jnp.dot(
            hit, record[:, columns], precision=lax.Precision.HIGHEST, preferred_element_type=jnp.float32
        )

    part_x = share(first - 1, slice(0, third * lanes))
    part_yz = share(first, slice(third * lanes, pieces * lanes))
    rows, entry = loads[...], lane_blocks(entries[...], slots)
    for tile in range(tiles):
        mine = slice(3 * tile, 3 * tile + 3)
        for m in range(pieces):
            part, at = (part_x, m) if m < third else (part_yz, m - third)
            out[tile, 3 * m : 3 * m + 3, :] = part[mine, at * lanes : (at + 1) * lanes]
        out[tile, ENTRY_ROW : ENTRY_ROW + 1, :] = entry
        out[tile, TRUCK_ROW : TRUCK_ROW + slots, :] = rows


def prepare_kernel(parts, loads, entries, cells, force, surface, table, rows_out):
    steps, comps, width = force.shape[:3]
    lanes = parts.shape[2]
    force[...] = jnp.zeros(force.shape, jnp.float32)
    per = ENTRY_ROW // (comps * width)
    lane = lax.broadcasted_iota(jnp.int32, (per, lanes), 1)
    scale = jnp.where(lane < FZ, DT, 0.0).astype(jnp.float32)
    for s in range(steps):
        for comp in range(comps):
            for cell in range(width):
                panel = parts[s, pl.ds(comp * per * width + cell, per, stride=width), :]
                force[s, comp, cell, pl.ds(4, per, stride=2), :] = scale * panel
                force[s, comp, cell, pl.ds(5, per, stride=2), :] = scale * lane_roll(panel, FZ)

    slots = loads.shape[0]
    me = lax.axis_index("line")
    table[...] = jnp.zeros(table.shape, jnp.float32)
    table[0:1, :] = lane_blocks(entries[...], slots)
    table[STEPS + 1 : STEPS + 2, :] = lane_blocks(cells[...], slots)
    rows = [loads[...]]
    for k in range(1, STEPS + 1):
        source = jnp.maximum(me - k, 0)
        there = jnp.where(me >= k, 1.0, 0.0).astype(jnp.float32)
        rows.append(there * parts[source, TRUCK_ROW : TRUCK_ROW + slots, :])
        table[k : k + 1, :] = parts[source, ENTRY_ROW : ENTRY_ROW + 1, :]
    columns = table[...].T
    rows_out[...] = jnp.zeros(rows_out.shape, jnp.float32)
    for s in range(STEPS):
        block = slice(s * slots, (s + 1) * slots)
        moved = []
        for k in range(STEPS - s):
            entry = jnp.broadcast_to(columns[block, k : k + 1], rows[k].shape)
            new = rows[k]
            for slot in range(slots):
                new = jnp.where(entry == float(slot), rows[k + 1][slot : slot + 1, :], new)
            moved.append(new)
        rows = moved
        cell = jnp.broadcast_to(columns[block, STEPS + 1 : STEPS + 2], rows[0].shape)
        for c in range(2):
            load = jnp.sum(jnp.where(cell == float(c), rows[0], 0.0), axis=0, keepdims=True)
            rows_out[2 * s + c : 2 * s + c + 1, :] = load
    surface[...] = rows_out[...].T


def in_vmem(x):
    return pltpu.with_memory_space_constraint(x, pltpu.VMEM)


WHOLE = pl.BlockSpec(memory_space=pltpu.VMEM)
SCALARS = pl.BlockSpec(memory_space=pltpu.SMEM)
ANYWHERE = pl.BlockSpec(memory_space=pl.ANY)


def call(kernel, ins, specs, outs, out_specs, scratch=(), aliases=None, name=None):
    size = sum(x.size * 4 for x in ins)
    return pl.pallas_call(
        kernel,
        out_shape=outs,
        in_specs=specs,
        out_specs=out_specs,
        scratch_shapes=list(scratch),
        input_output_aliases=aliases or {},
        compiler_params=pltpu.CompilerParams(vmem_limit_bytes=VMEM_LIMIT),
        cost_estimate=pl.CostEstimate(flops=8 * size, bytes_accessed=2 * size, transcendentals=0),
        name=name,
    )(*ins)


def body(
    velocity, stress, memory, truck_loads, pier_panels,
    lame_lambda, lame_mu, buoyancy, relax_rate, defect_mu, layer,
    truck_entry, truck_cell, pier_cell,
):
    tiles = lax.axis_size("line")
    width_x, across, depth = velocity.shape[1:]
    slots = truck_loads.shape[0]
    window = (across - FY) // 2 - 4
    f32 = jnp.float32

    near = [(i, i ^ 1) for i in range(tiles) if (i ^ 1) < tiles]
    far = [(i, i + 1) for i in range(1, tiles - 1, 2)] + [(i + 1, i) for i in range(1, tiles - 1, 2)]

    padded = across + 2 * PAD
    v_type = pltpu.VMEM((3, width_x, padded, depth), f32)
    s_type = pltpu.VMEM((6, width_x, padded, depth), f32)
    r_type = pltpu.VMEM((6, width_x, across, depth), f32)
    c_type = pltpu.VMEM((N_COEF, depth), f32)
    m_type = pltpu.VMEM((3, across, depth), f32)
    ghost = pltpu.VMEM((2, across, depth), f32)
    work = pltpu.VMEM((2, padded, depth), f32)

    def as_rows(table):
        return jnp.pad(table.astype(f32), ((0, 8 - STEPS), (0, depth - slots)))

    entries, cells = as_rows(truck_entry), as_rows(truck_cell)
    parts = call(
        split_kernel,
        (pier_panels[0], pier_cell[None, :], truck_loads, entries),
        (WHOLE,) * 4,
        jax.ShapeDtypeStruct((tiles, TRUCK_ROW + slots, depth), f32),
        WHOLE,
        name="split",
    )
    parts = lax.all_to_all(parts, "line", 0, 0, tiled=True)

    V, S, R, coef, msg_near, msg_far = call(
        start_kernel,
        (
            *(pltpu.with_memory_space_constraint(x, pltpu.HBM) for x in (velocity, stress, memory)),
            layer[None, :], lame_lambda, lame_mu, buoyancy, relax_rate, defect_mu,
        ),
        (ANYWHERE,) * 3 + (WHOLE,) + (SCALARS,) * 5,
        (v_type, s_type, r_type, c_type, m_type, m_type),
        (WHOLE,) * 6,
        scratch=(pltpu.SemaphoreType.DMA((15,)),),
        name="start",
    )
    msg_far = lax.ppermute(msg_far, "line", far)
    msg_near = lax.ppermute(msg_near, "line", near)

    force, surface = call(
        prepare_kernel,
        (parts, truck_loads, entries, cells),
        (WHOLE,) * 4,
        (pltpu.VMEM((STEPS, 3, 3, 16, depth), f32), pltpu.VMEM((across, depth), f32)),
        (WHOLE,) * 2,
        scratch=(pltpu.VMEM((depth, depth), f32), pltpu.VMEM((depth, across), f32)),
        name="prepare",
    )
    V, early = call(
        functools.partial(first_kernel, window),
        tuple(in_vmem(x) for x in (V, S, R, coef, force, surface)),
        (WHOLE,) * 6,
        (v_type, m_type),
        (WHOLE,) * 2,
        scratch=(work,),
        aliases={0: 0},
        name="first",
    )
    early = lax.ppermute(early, "line", far)
    state = (v_type, s_type, r_type)
    same = {0: 0, 1: 1, 2: 2}
    missing = None
    for step in range(STEPS):
        more = step < STEPS - 1
        ins = tuple(in_vmem(x) for x in (V, S, R, coef, force, surface, msg_near))
        outs = state + ((m_type,) if more else ())
        V, S, R, *msg = call(
            functools.partial(near_kernel, step, window),
            ins,
            (WHOLE,) * len(ins),
            outs,
            (WHOLE,) * len(outs),
            scratch=(ghost,),
            aliases=same,
            name="near" + str(step),
        )
        if more:
            msg_near = lax.ppermute(msg[0], "line", near)
        ins = (V, S, R, coef, force, surface, msg_far) + ((missing,) if step else ())
        ins = tuple(in_vmem(x) for x in ins)
        if more:
            outs = state + (m_type,) + ((m_type,) if step < STEPS - 2 else ())
            V, S, R, missing, *msg = call(
                functools.partial(far_kernel, step, window),
                ins,
                (WHOLE,) * len(ins),
                outs,
                (WHOLE,) * len(outs),
                scratch=(ghost, work),
                aliases=same,
                name="far" + str(step),
            )
            msg_far = early
            if msg:
                early = lax.ppermute(msg[0], "line", far)
    results = call(
        functools.partial(last_kernel, STEPS - 1, window),
        ins,
        (WHOLE,) * len(ins),
        state + tuple(jax.ShapeDtypeStruct(x.shape, f32) for x in (velocity, stress, memory)),
        (WHOLE,) * 3 + (ANYWHERE,) * 3,
        scratch=(ghost, pltpu.SemaphoreType.DMA((2, 3))),
        aliases=same,
        name="last",
    )
    return results[3:]


def solution(mesh):
    placed = (
        P(None, ("runs", "line"), None, None),
        P(None, ("runs", "line"), None, None),
        P(None, ("runs", "line"), None, None),
        P(("runs", "line"), None),
        P("line", "runs", None),
        P(),
        P(),
        P(),
        P(),
        P(),
        P(),
        P(None, ("runs", "line")),
        P(None, ("runs", "line")),
        P(),
    )
    return jax.shard_map(
        body,
        mesh=mesh,
        in_specs=placed,
        out_specs=(
            P(None, ("runs", "line"), None, None),
            P(None, ("runs", "line"), None, None),
            P(None, ("runs", "line"), None, None),
        ),
        check_vma=False,
    )
```

time: 87.1 us -> 58.4 us (0.67)
  starting transfers between devices: 37.3 us -> 24.4 us
  Pallas kernels: 24.6 us -> 14.9 us
  waiting for transfers between devices: 20.7 us -> 14.9 us
    ppermute x8 -> x5, starting transfers between devices: 24.5 us -> 11.4 us  [the longest x4 9.49 us: body(): early = lax.ppermute(msg[0], 'line', far)]
    ppermute x8 -> x5, waiting for transfers between devices: 20.7 us -> 9.69 us  [the longest x4 8.11 us: body(): early = lax.ppermute(msg[0], 'line', far)]
    pallas_call x16, Pallas kernels: 24.6 us -> 14.9 us  [call(): pl.pallas_call(kernel, out_shape=outs, in_specs=specs, out_specs=out_spec...]
    all_to_all x1, waiting for transfers between devices: 0.01 us -> 5.18 us  [body(): parts = lax.all_to_all(parts, 'line', 0, 0, tiled=True)]
    slice x2 -> x0, local copies, waits for them, and re-layouts: 0.91 us -> none  [the longest x1 0.91 us: body(): parts[:STEPS]]
    unnamed x27 -> x20, local copies, waits for them, and re-layouts: 1.91 us -> 2.14 us
  transfers between devices with their start and end apart: 16 -> 13, of which waited for: 7 -> 6; matrix products, arithmetic and copies ran while one was open for 1% -> 0% of each run, Pallas kernels for 25% -> 21%
where the time goes in v2:
time: 58.4 us; the launch traced here: 57.9 us
  starting transfers between devices  24.4 us (42%)
  Pallas kernels  14.9 us (26%)
  waiting for transfers between devices  14.9 us (26%)
  local copies, waits for them, and re-layouts  2.15 us (4%)
  between operations  0.89 us (2%)
  other arithmetic  0.69 us (1%)
    pallas_call x16, Pallas kernels, call(): pl.pallas_call(kernel, out_shape=outs, in_specs=specs, out_specs=out_spec...  14.9 us
    ppermute x4, starting transfers between devices, body(): early = lax.ppermute(msg[0], 'line', far)  9.49 us
    ppermute x4, waiting for transfers between devices, body(): early = lax.ppermute(msg[0], 'line', far)  8.11 us
    all_to_all x1, starting transfers between devices, body(): parts = lax.all_to_all(parts, 'line', 0, 0, tiled=True)  6.63 us
    all_to_all x1, waiting for transfers between devices, body(): parts = lax.all_to_all(parts, 'line', 0, 0, tiled=True)  5.18 us
    ppermute x1, starting transfers between devices, body(): msg_far = lax.ppermute(msg_far, 'line', far)  3.11 us
    ppermute x5, starting transfers between devices, body(): msg_near = lax.ppermute(msg[0], 'line', near)  2.82 us
    unnamed x20, local copies, waits for them, and re-layouts  2.14 us
  transfers between devices with their start and end apart: 13, of which 6 were waited for; matrix products, arithmetic and copies ran while one was open for 0% of the time, Pallas kernels for 21%

profile of v2, /device:TPU:17, one launch (start us, length us, event | category | flops | bytes accessed | tf_op | source)
XLA Modules:
  0.0 57.9 jit_solution(9293590053536523867)
XLA Ops:
  0.6 0.7 %convert_element_type.9 = f32[6,16]{1,0:T(8,128)S(1)} convert(s32[6,16]{1,0:T(8,128)} %param.25) | non-fusion elementwise | flops 96 | bytes 768 | tf_op jit(solution)/shard_map/convert_element_type | solution.py:640
  1.3 0.7 %copy-done.1 = f32[16,128]{1,0:T(8,128)S(1)} copy-done((f32[16,128]{1,0:T(8,128)S(1)}, f32[16,128]{1,0:T(8,128)}, u32[]{:S(2)}) %copy-start.1) | copy-done | bytes 8216
  2.0 0.8 %copy-done = f32[1,8,1536]{2,1,0:T(8,128)S(1)} copy-done((f32[1,8,1536]{2,1,0:T(8,128)S(1)}, f32[1,8,1536]{2,1,0:T(8,128)}, u32[]{:S(2)}) %copy-start) | copy-done | bytes 49176
  2.8 1.2 %split.1 = f32[16,56,128]{2,1,0:T(8,128)} custom-call(f32[8,1536]{1,0:T(8,128)S(1)} %bitcast.3, s32[1,8]{1,0:T(1,128)S(1)} %bitcast.4, f32[16,128]{1,0:T(8,128)S(1)} %copy-done.1, f32[8,128]{1,0:T(8,128)S(1)} %pad.7.entries), custom_call_target="tpu_custom_call" | custom-call | flops 491776 | bytes 122944 | tf_op jit(solution)/shard_map/split/pallas_call | solution.py:603
  4.0 6.6 %all-to-all-start = ((f32[16,56,128]{2,1,0:T(8,128)}), f32[16,56,128]{2,1,0:T(8,128)S(1)}, u32[]{:S(2)}, u32[]{:S(2)}) async-start(f32[16,56,128]{2,1,0:T(8,128)} %split.1), calls=%async_computation | async-start | bytes 917504 | tf_op jit(solution)/shard_map/all_to_all | solution.py:651
  10.6 0.0 copy-start.4
  10.6 0.0 copy-start.5
  10.7 0.6 %copy-done.3 = s32[128]{0:T(128)S(1)} copy-done((s32[128]{0:T(128)S(1)}, s32[128]{0:T(128)}, u32[]{:S(2)}) %copy-start.3) | copy-done | bytes 536
  11.3 0.0 copy-done.4
  11.3 0.0 copy-done.5
  11.3 2.4 %start.1 = (f32[3,2,144,128]{3,2,1,0:T(8,128)S(1)}, f32[6,2,144,128]{3,2,1,0:T(8,128)S(1)}, f32[6,2,128,128]{3,2,1,0:T(8,128)S(1)}, f32[16,128]{1,0:T(8,128)S(1)...) custom-call(f32[3,2,128,128]{3,2,1,0:T(8,128)} %velocity.1, f32[6,2,128,128]{3,2,1,0:T(8,128)} %stress.1, ...), custom_call_target="tpu_custom_call" | custom-call | flops 15734016 | bytes 3933504 | tf_op jit(solution)/shard_map/start/pallas_call | solution.py:603
  13.7 0.4 collective-permute-start
  14.1 3.1 %collective-permute-start.1 = (f32[3,128,128]{2,1,0:T(8,128)S(1)}, f32[3,128,128]{2,1,0:T(8,128)S(1)}, u32[]{:S(2)}, u32[]{:S(2)}) collective-permute-start(f32[3,128,128]{2,1,0:T(8,128)S(1)} %get-tuple-element.74), channel_id=1, source_target_pairs={{1,2},{3,4},{5,6},{7,8},{9,10},{11,12},{13,14},{2,1},{4,3},{6,5},{... | collective-permute-start | bytes 589832 | tf_op jit(solution)/shard_map/ppermute | solution.py:665
  17.3 5.2 %all-to-all-done.parts = f32[16,56,128]{2,1,0:T(8,128)S(1)} async-done(((f32[16,56,128]{2,1,0:T(8,128)}), f32[16,56,128]{2,1,0:T(8,128)S(1)}, u32[]{:S(2)}, u32[]{:S(2)}) %all-to-all-start) | async-done | bytes 458784 | tf_op jit(solution)/shard_map/all_to_all | solution.py:651
  22.4 0.6 %prepare.1 = (f32[6,3,3,16,128]{4,3,2,1,0:T(8,128)S(1)}, f32[128,128]{1,0:T(8,128)S(1)}) custom-call(f32[16,56,128]{2,1,0:T(8,128)S(1)} %all-to-all-done.parts, f32[16,128]{1,0:T(8,128)S(1)} %copy-done.1, f32[8,128]{1,0:T(8,128)S(1)} %pad.7.entries, f32[8,128]{1,0:T(8,128)S(1)} %pad.8.cells), custom_call_target="tpu_custom_call" | custom-call | flops 3801088 | bytes 950272 | tf_op jit(solution)/shard_map/prepare/pallas_call | solution.py:603
  23.0 0.5 first.1
  23.6 0.0 collective-permute-done.msg
  23.6 0.5 near0.1
  24.1 1.5 %collective-permute-start.2 = (f32[3,128,128]{2,1,0:T(8,128)S(1)}, f32[3,128,128]{2,1,0:T(8,128)S(1)}, u32[]{:S(2)}, u32[]{:S(2)}) collective-permute-start(f32[3,128,128]{2,1,0:T(8,128)S(1)} %get-tuple-element.78), channel_id=1, source_target_pairs={{0,1},{1,0},{2,3},{3,2},{4,5},{5,4},{6,7},{7,6},{8,9},{9,8},{10,11... | collective-permute-start | bytes 589832 | tf_op jit(solution)/shard_map/ppermute | solution.py:706
  25.5 1.9 %collective-permute-start.3 = (f32[3,128,128]{2,1,0:T(8,128)S(1)}, f32[3,128,128]{2,1,0:T(8,128)S(1)}, u32[]{:S(2)}, u32[]{:S(2)}) collective-permute-start(f32[3,128,128]{2,1,0:T(8,128)S(1)} %get-tuple-element.82), channel_id=1, source_target_pairs={{1,2},{3,4},{5,6},{7,8},{9,10},{11,12},{13,14},{2,1},{4,3},{6,5},{... | collective-permute-start | bytes 589832 | tf_op jit(solution)/shard_map/ppermute | solution.py:687
  27.5 0.0 collective-permute-done.1.msg
  27.5 1.3 %far0.1 = (f32[3,2,144,128]{3,2,1,0:T(8,128)S(1)}, f32[6,2,144,128]{3,2,1,0:T(8,128)S(1)}, f32[6,2,128,128]{3,2,1,0:T(8,128)S(1)}, f32[3,128,128]{2,1,0:T(8,128)S(1)}, f32[3,128,128]{2,1,0:T(8,128)S(1)}) custom-call(f32[3,2,144,128]{3,2,1,0:T(8,128)S(1)} %get-tuple-element.71.V0, ...), custom_call_target="tpu_custom_call", output_to_operand_aliasing={{0}: (0, {}), {1}: (1, {}), {2}: (2, {})} | custom-call | flops 22609920 | bytes 5652480 | tf_op jit(solution)/shard_map/far0/pallas_call | solution.py:603
  28.8 0.5 near1.1
  29.3 0.8 %collective-permute-start.4 = (f32[3,128,128]{2,1,0:T(8,128)S(1)}, f32[3,128,128]{2,1,0:T(8,128)S(1)}, u32[]{:S(2)}, u32[]{:S(2)}) collective-permute-start(f32[3,128,128]{2,1,0:T(8,128)S(1)} %get-tuple-element.87), channel_id=1, source_target_pairs={{0,1},{1,0},{2,3},{3,2},{4,5},{5,4},{6,7},{7,6},{8,9},{9,8},{10,11... | collective-permute-start | bytes 589832 | tf_op jit(solution)/shard_map/ppermute | solution.py:706
  30.1 2.9 %collective-permute-start.5 = (f32[3,128,128]{2,1,0:T(8,128)S(1)}, f32[3,128,128]{2,1,0:T(8,128)S(1)}, u32[]{:S(2)}, u32[]{:S(2)}) collective-permute-start(f32[3,128,128]{2,1,0:T(8,128)S(1)} %get-tuple-element.91), channel_id=1, source_target_pairs={{1,2},{3,4},{5,6},{7,8},{9,10},{11,12},{13,14},{2,1},{4,3},{6,5},{... | collective-permute-start | bytes 589832 | tf_op jit(solution)/shard_map/ppermute | solution.py:723
  33.0 1.6 %collective-permute-done.3.msg = f32[3,128,128]{2,1,0:T(8,128)S(1)} collective-permute-done((f32[3,128,128]{2,1,0:T(8,128)S(1)}, f32[3,128,128]{2,1,0:T(8,128)S(1)}, u32[]{:S(2)}, u32[]{:S(2)}) %collective-permute-start.3) | collective-permute-done | bytes 196640 | tf_op jit(solution)/shard_map/ppermute | solution.py:687
  34.6 1.3 %far1.1 = (f32[3,2,144,128]{3,2,1,0:T(8,128)S(1)}, f32[6,2,144,128]{3,2,1,0:T(8,128)S(1)}, f32[6,2,128,128]{3,2,1,0:T(8,128)S(1)}, f32[3,128,128]{2,1,0:T(8,128)S(1)}, f32[3,128,128]{2,1,0:T(8,128)S(1)}) custom-call(f32[3,2,144,128]{3,2,1,0:T(8,128)S(1)} %get-tuple-element.79.V0, ...), custom_call_target="tpu_custom_call", output_to_operand_aliasing={{0}: (0, {}), {1}: (1, {}), {2}: (2, {})} | custom-call | flops 24182784 | bytes 6045696 | tf_op jit(solution)/shard_map/far1/pallas_call | solution.py:603
  35.9 0.0 collective-permute-done.4.msg
  36.0 0.5 near2.1
  36.4 0.1 collective-permute-start.6
  36.5 2.0 %collective-permute-start.7 = (f32[3,128,128]{2,1,0:T(8,128)S(1)}, f32[3,128,128]{2,1,0:T(8,128)S(1)}, u32[]{:S(2)}, u32[]{:S(2)}) collective-permute-start(f32[3,128,128]{2,1,0:T(8,128)S(1)} %get-tuple-element.100), channel_id=1, source_target_pairs={{1,2},{3,4},{5,6},{7,8},{9,10},{11,12},{13,14},{2,1},{4,3},{6,5},{... | collective-permute-start | bytes 589832 | tf_op jit(solution)/shard_map/ppermute | solution.py:723
  38.5 0.7 %collective-permute-done.5.msg = f32[3,128,128]{2,1,0:T(8,128)S(1)} collective-permute-done((f32[3,128,128]{2,1,0:T(8,128)S(1)}, f32[3,128,128]{2,1,0:T(8,128)S(1)}, u32[]{:S(2)}, u32[]{:S(2)}) %collective-permute-start.5) | collective-permute-done | bytes 196640 | tf_op jit(solution)/shard_map/ppermute | solution.py:723
  39.2 1.3 %far2.1 = (f32[3,2,144,128]{3,2,1,0:T(8,128)S(1)}, f32[6,2,144,128]{3,2,1,0:T(8,128)S(1)}, f32[6,2,128,128]{3,2,1,0:T(8,128)S(1)}, f32[3,128,128]{2,1,0:T(8,128)S(1)}, f32[3,128,128]{2,1,0:T(8,128)S(1)}) custom-call(f32[3,2,144,128]{3,2,1,0:T(8,128)S(1)} %get-tuple-element.88.V0, ...), custom_call_target="tpu_custom_call", output_to_operand_aliasing={{0}: (0, {}), {1}: (1, {}), {2}: (2, {})} | custom-call | flops 24182784 | bytes 6045696 | tf_op jit(solution)/shard_map/far2/pallas_call | solution.py:603
  40.5 0.0 collective-permute-done.6.msg
  40.6 0.5 near3.1
  41.0 0.4 collective-permute-start.8
  41.4 2.7 %collective-permute-start.9 = (f32[3,128,128]{2,1,0:T(8,128)S(1)}, f32[3,128,128]{2,1,0:T(8,128)S(1)}, u32[]{:S(2)}, u32[]{:S(2)}) collective-permute-start(f32[3,128,128]{2,1,0:T(8,128)S(1)} %get-tuple-element.109), channel_id=1, source_target_pairs={{1,2},{3,4},{5,6},{7,8},{9,10},{11,12},{13,14},{2,1},{4,3},{6,5},{... | collective-permute-start | bytes 589832 | tf_op jit(solution)/shard_map/ppermute | solution.py:723
  44.1 1.6 %collective-permute-done.7.msg = f32[3,128,128]{2,1,0:T(8,128)S(1)} collective-permute-done((f32[3,128,128]{2,1,0:T(8,128)S(1)}, f32[3,128,128]{2,1,0:T(8,128)S(1)}, u32[]{:S(2)}, u32[]{:S(2)}) %collective-permute-start.7) | collective-permute-done | bytes 196640 | tf_op jit(solution)/shard_map/ppermute | solution.py:723
  45.6 1.3 %far3.1 = (f32[3,2,144,128]{3,2,1,0:T(8,128)S(1)}, f32[6,2,144,128]{3,2,1,0:T(8,128)S(1)}, f32[6,2,128,128]{3,2,1,0:T(8,128)S(1)}, f32[3,128,128]{2,1,0:T(8,128)S(1)}, f32[3,128,128]{2,1,0:T(8,128)S(1)}) custom-call(f32[3,2,144,128]{3,2,1,0:T(8,128)S(1)} %get-tuple-element.97.V0, ...), custom_call_target="tpu_custom_call", output_to_operand_aliasing={{0}: (0, {}), {1}: (1, {}), {2}: (2, {})} | custom-call | flops 24182784 | bytes 6045696 | tf_op jit(solution)/shard_map/far3/pallas_call | solution.py:603
  46.9 0.0 collective-permute-done.8.msg
  46.9 0.5 near4.1
  47.4 0.1 collective-permute-start.10
  47.5 2.0 %collective-permute-start.11 = (f32[3,128,128]{2,1,0:T(8,128)S(1)}, f32[3,128,128]{2,1,0:T(8,128)S(1)}, u32[]{:S(2)}, u32[]{:S(2)}) collective-permute-start(f32[3,128,128]{2,1,0:T(8,128)S(1)} %get-tuple-element.118), channel_id=1, source_target_pairs={{1,2},{3,4},{5,6},{7,8},{9,10},{11,12},{13,14},{2,1},{4,3},{6,5},{... | collective-permute-start | bytes 589832 | tf_op jit(solution)/shard_map/ppermute | solution.py:723
  49.5 1.0 %collective-permute-done.9.msg = f32[3,128,128]{2,1,0:T(8,128)S(1)} collective-permute-done((f32[3,128,128]{2,1,0:T(8,128)S(1)}, f32[3,128,128]{2,1,0:T(8,128)S(1)}, u32[]{:S(2)}, u32[]{:S(2)}) %collective-permute-start.9) | collective-permute-done | bytes 196640 | tf_op jit(solution)/shard_map/ppermute | solution.py:723
  50.5 1.0 %far4.1 = (f32[3,2,144,128]{3,2,1,0:T(8,128)S(1)}, f32[6,2,144,128]{3,2,1,0:T(8,128)S(1)}, f32[6,2,128,128]{3,2,1,0:T(8,128)S(1)}, f32[3,128,128]{2,1,0:T(8,128)S(1)}) custom-call(f32[3,2,144,128]{3,2,1,0:T(8,128)S(1)} %get-tuple-element.106.V0, ...), custom_call_target="tpu_custom_call", output_to_operand_aliasing={{0}: (0, {}), {1}: (1, {}), {2}: (2, {})} | custom-call | flops 24182784 | bytes 6045696 | tf_op jit(solution)/shard_map/far4/pallas_call | solution.py:603
  51.5 0.3 near5.1
  51.8 4.8 %collective-permute-done.11.msg = f32[3,128,128]{2,1,0:T(8,128)S(1)} collective-permute-done((f32[3,128,128]{2,1,0:T(8,128)S(1)}, f32[3,128,128]{2,1,0:T(8,128)S(1)}, u32[]{:S(2)}, u32[]{:S(2)}) %collective-permute-start.11) | collective-permute-done | bytes 196640 | tf_op jit(solution)/shard_map/ppermute | solution.py:723
  56.6 1.3 %last.1 = (f32[3,2,144,128]{3,2,1,0:T(8,128)S(1)}, f32[6,2,144,128]{3,2,1,0:T(8,128)S(1)}, f32[6,2,128,128]{3,2,1,0:T(8,128)S(1)}, f32[3,2,128,128]{3,2,1,0:T(8,...) custom-call(f32[3,2,144,128]{3,2,1,0:T(8,128)S(1)} %get-tuple-elemen, ...), custom_call_target="tpu_custom_call", output_to_operand_aliasing={{0}: (0, {}), {1}: (1, {}), {2}: (2, {})} | custom-call | flops 24182784 | bytes 6045696 | tf_op jit(solution)/shard_map/last/pallas_call | solution.py:603
  (18 shorter events, 0.0 us)
Async XLA Ops:
  1.3 0.7 %copy-start.1 = (f32[16,128]{1,0:T(8,128)S(1)}, f32[16,128]{1,0:T(8,128)}, u32[]{:S(2)}) copy-start(f32[16,128]{1,0:T(8,128)} %loads.3) | copy-start | bytes 24580
  1.3 0.7 %copy-start.2 = (s32[8]{0:T(128)S(1)}, s32[8]{0:T(128)}, u32[]{:S(2)}) copy-start(s32[8]{0:T(128)} %param.27) | copy-start | bytes 100
  2.0 0.8 %copy-start = (f32[1,8,1536]{2,1,0:T(8,128)S(1)}, f32[1,8,1536]{2,1,0:T(8,128)}, u32[]{:S(2)}) copy-start(f32[1,8,1536]{2,1,0:T(8,128)} %param.18) | copy-start | bytes 147460
  4.0 6.7 %copy-start.6 = (f32[8]{0:T(128)S(1)}, f32[8]{0:T(128)}, u32[]{:S(2)}) copy-start(f32[8]{0:T(128)} %buoy.1) | copy-start | bytes 100
  4.0 6.7 %copy-start.7 = (f32[8]{0:T(128)S(1)}, f32[8]{0:T(128)}, u32[]{:S(2)}) copy-start(f32[8]{0:T(128)} %rate.1) | copy-start | bytes 100
  4.0 6.7 %copy-start.8 = (f32[8]{0:T(128)S(1)}, f32[8]{0:T(128)}, u32[]{:S(2)}) copy-start(f32[8]{0:T(128)} %defect.1) | copy-start | bytes 100
  4.0 18.5 %all-to-all-start = ((f32[16,56,128]{2,1,0:T(8,128)}), f32[16,56,128]{2,1,0:T(8,128)S(1)}, u32[]{:S(2)}, u32[]{:S(2)}) async-start(f32[16,56,128]{2,1,0:T(8,128)} %split.1), calls=%async_computation | async-start | bytes 917504 | tf_op jit(solution)/shard_map/all_to_all | solution.py:651
  10.6 0.7 %copy-start.3 = (s32[128]{0:T(128)S(1)}, s32[128]{0:T(128)}, u32[]{:S(2)}) copy-start(s32[128]{0:T(128)} %param.24) | copy-start | bytes 1540
  10.6 0.7 %copy-start.4 = (f32[8]{0:T(128)S(1)}, f32[8]{0:T(128)}, u32[]{:S(2)}) copy-start(f32[8]{0:T(128)} %lam.1) | copy-start | bytes 100
  10.6 0.7 %copy-start.5 = (f32[8]{0:T(128)S(1)}, f32[8]{0:T(128)}, u32[]{:S(2)}) copy-start(f32[8]{0:T(128)} %mu.1) | copy-start | bytes 100
  11.3 5.9 %copy-start.9 = (s32[6,16]{1,0:T(8,128)S(1)}, s32[6,16]{1,0:T(8,128)}, u32[]{:S(2)}) copy-start(s32[6,16]{1,0:T(8,128)} %param.26) | copy-start | bytes 1156
  13.7 9.9 %collective-permute-start = (f32[3,128,128]{2,1,0:T(8,128)S(1)}, f32[3,128,128]{2,1,0:T(8,128)S(1)}, u32[]{:S(2)}, u32[]{:S(2)}) collective-permute-start(f32[3,128,128]{2,1,0:T(8,128)S(1)} %get-tuple-element.70), channel_id=1, source_target_pairs={{0,1},{1,0},{2,3},{3,2},{4,5},{5,4},{6,7},{7,6},{8,9},{9,8},{10,11... | collective-permute-start | bytes 589832 | tf_op jit(solution)/shard_map/ppermute | solution.py:666
  14.1 13.4 %collective-permute-start.1 = (f32[3,128,128]{2,1,0:T(8,128)S(1)}, f32[3,128,128]{2,1,0:T(8,128)S(1)}, u32[]{:S(2)}, u32[]{:S(2)}) collective-permute-start(f32[3,128,128]{2,1,0:T(8,128)S(1)} %get-tuple-element.74), channel_id=1, source_target_pairs={{1,2},{3,4},{5,6},{7,8},{9,10},{11,12},{13,14},{2,1},{4,3},{6,5},{... | collective-permute-start | bytes 589832 | tf_op jit(solution)/shard_map/ppermute | solution.py:665
  24.1 4.7 %collective-permute-start.2 = (f32[3,128,128]{2,1,0:T(8,128)S(1)}, f32[3,128,128]{2,1,0:T(8,128)S(1)}, u32[]{:S(2)}, u32[]{:S(2)}) collective-permute-start(f32[3,128,128]{2,1,0:T(8,128)S(1)} %get-tuple-element.78), channel_id=1, source_target_pairs={{0,1},{1,0},{2,3},{3,2},{4,5},{5,4},{6,7},{7,6},{8,9},{9,8},{10,11... | collective-permute-start | bytes 589832 | tf_op jit(solution)/shard_map/ppermute | solution.py:706
  25.5 9.1 %collective-permute-start.3 = (f32[3,128,128]{2,1,0:T(8,128)S(1)}, f32[3,128,128]{2,1,0:T(8,128)S(1)}, u32[]{:S(2)}, u32[]{:S(2)}) collective-permute-start(f32[3,128,128]{2,1,0:T(8,128)S(1)} %get-tuple-element.82), channel_id=1, source_target_pairs={{1,2},{3,4},{5,6},{7,8},{9,10},{11,12},{13,14},{2,1},{4,3},{6,5},{... | collective-permute-start | bytes 589832 | tf_op jit(solution)/shard_map/ppermute | solution.py:687
  29.3 6.7 %collective-permute-start.4 = (f32[3,128,128]{2,1,0:T(8,128)S(1)}, f32[3,128,128]{2,1,0:T(8,128)S(1)}, u32[]{:S(2)}, u32[]{:S(2)}) collective-permute-start(f32[3,128,128]{2,1,0:T(8,128)S(1)} %get-tuple-element.87), channel_id=1, source_target_pairs={{0,1},{1,0},{2,3},{3,2},{4,5},{5,4},{6,7},{7,6},{8,9},{9,8},{10,11... | collective-permute-start | bytes 589832 | tf_op jit(solution)/shard_map/ppermute | solution.py:706
  30.1 9.1 %collective-permute-start.5 = (f32[3,128,128]{2,1,0:T(8,128)S(1)}, f32[3,128,128]{2,1,0:T(8,128)S(1)}, u32[]{:S(2)}, u32[]{:S(2)}) collective-permute-start(f32[3,128,128]{2,1,0:T(8,128)S(1)} %get-tuple-element.91), channel_id=1, source_target_pairs={{1,2},{3,4},{5,6},{7,8},{9,10},{11,12},{13,14},{2,1},{4,3},{6,5},{... | collective-permute-start | bytes 589832 | tf_op jit(solution)/shard_map/ppermute | solution.py:723
  36.4 4.1 %collective-permute-start.6 = (f32[3,128,128]{2,1,0:T(8,128)S(1)}, f32[3,128,128]{2,1,0:T(8,128)S(1)}, u32[]{:S(2)}, u32[]{:S(2)}) collective-permute-start(f32[3,128,128]{2,1,0:T(8,128)S(1)} %get-tuple-element.96), channel_id=1, source_target_pairs={{0,1},{1,0},{2,3},{3,2},{4,5},{5,4},{6,7},{7,6},{8,9},{9,8},{10,11... | collective-permute-start | bytes 589832 | tf_op jit(solution)/shard_map/ppermute | solution.py:706
  36.5 9.1 %collective-permute-start.7 = (f32[3,128,128]{2,1,0:T(8,128)S(1)}, f32[3,128,128]{2,1,0:T(8,128)S(1)}, u32[]{:S(2)}, u32[]{:S(2)}) collective-permute-start(f32[3,128,128]{2,1,0:T(8,128)S(1)} %get-tuple-element.100), channel_id=1, source_target_pairs={{1,2},{3,4},{5,6},{7,8},{9,10},{11,12},{13,14},{2,1},{4,3},{6,5},{... | collective-permute-start | bytes 589832 | tf_op jit(solution)/shard_map/ppermute | solution.py:723
  41.0 5.9 %collective-permute-start.8 = (f32[3,128,128]{2,1,0:T(8,128)S(1)}, f32[3,128,128]{2,1,0:T(8,128)S(1)}, u32[]{:S(2)}, u32[]{:S(2)}) collective-permute-start(f32[3,128,128]{2,1,0:T(8,128)S(1)} %get-tuple-element.105), channel_id=1, source_target_pairs={{0,1},{1,0},{2,3},{3,2},{4,5},{5,4},{6,7},{7,6},{8,9},{9,8},{10,11... | collective-permute-start | bytes 589832 | tf_op jit(solution)/shard_map/ppermute | solution.py:706
  41.4 9.1 %collective-permute-start.9 = (f32[3,128,128]{2,1,0:T(8,128)S(1)}, f32[3,128,128]{2,1,0:T(8,128)S(1)}, u32[]{:S(2)}, u32[]{:S(2)}) collective-permute-start(f32[3,128,128]{2,1,0:T(8,128)S(1)} %get-tuple-element.109), channel_id=1, source_target_pairs={{1,2},{3,4},{5,6},{7,8},{9,10},{11,12},{13,14},{2,1},{4,3},{6,5},{... | collective-permute-start | bytes 589832 | tf_op jit(solution)/shard_map/ppermute | solution.py:723
  47.4 4.0 %collective-permute-start.10 = (f32[3,128,128]{2,1,0:T(8,128)S(1)}, f32[3,128,128]{2,1,0:T(8,128)S(1)}, u32[]{:S(2)}, u32[]{:S(2)}) collective-permute-start(f32[3,128,128]{2,1,0:T(8,128)S(1)} %get-tuple-element.114), channel_id=1, source_target_pairs={{0,1},{1,0},{2,3},{3,2},{4,5},{5,4},{6,7},{7,6},{8,9},{9,8},{10,11... | collective-permute-start | bytes 589832 | tf_op jit(solution)/shard_map/ppermute | solution.py:706
  47.5 9.1 %collective-permute-start.11 = (f32[3,128,128]{2,1,0:T(8,128)S(1)}, f32[3,128,128]{2,1,0:T(8,128)S(1)}, u32[]{:S(2)}, u32[]{:S(2)}) collective-permute-start(f32[3,128,128]{2,1,0:T(8,128)S(1)} %get-tuple-element.118), channel_id=1, source_target_pairs={{1,2},{3,4},{5,6},{7,8},{9,10},{11,12},{13,14},{2,1},{4,3},{6,5},{... | collective-permute-start | bytes 589832 | tf_op jit(solution)/shard_map/ppermute | solution.py:723

commit v3 on v2

--- a/solution.py
+++ b/solution.py
@@ -143,7 +143,7 @@
     add_force(V, (VZ, 1), force, (VZ, 1), PAD + window)
 
 
-def post(V, S, R, coef_ref, surface, cell, column, behind_x, ahead_y, ahead_z):
+def post(V, S, R, old_r, coef_ref, surface, cell, column, behind_x, ahead_y, ahead_z):
     m0, m1, lam, mu2, mu, k1, k2, k2h, l0 = coefs(
         coef_ref, (C_M0, C_M1, C_LAM, C_MU2, C_MU, C_K1, C_K2, C_K2H, C_L0)
     )
@@ -159,14 +159,14 @@
         eyz = m1 * after(vy) - vy + (V[VZ, cell, down] - vz)
         volume = lam * (exx + eyy + ezz)
         for comp, e in ((XX, exx), (YY, eyy), (ZZ, ezz)):
-            old = R[comp, cell, out]
+            old = old_r[comp, cell, out]
             new = S[comp, cell, here] + (volume + mu2 * e) + DT * old
             if comp == ZZ:
                 new = new + l0 * lane_roll(surface[out, :], -column)
             S[comp, cell, here] = new
             R[comp, cell, out] = k1 * old - k2 * e
         for comp, e in ((XY, exy), (XZ, exz), (YZ, eyz)):
-            old = R[comp, cell, out]
+            old = old_r[comp, cell, out]
             S[comp, cell, here] = S[comp, cell, here] + mu * e + DT * old
             R[comp, cell, out] = k1 * old - k2h * e
 
@@ -286,7 +286,7 @@
     add_force(msg, (2,), force, (VZ, 0), window)
 
 
-def ahead_bond(V, S, R, coef_ref, force, surface, msg, missing, G, step, window, respond=None):
+def ahead_bond(V, S, R, old_r, coef_ref, force, surface, msg, missing, G, step, window, respond=None):
     (b,) = coefs(coef_ref, (C_B,))
     _, _, has_ahead = place()
     keep = jnp.where(has_ahead, 1.0, 0.0).astype(jnp.float32)
@@ -307,14 +307,14 @@
     if respond is not None:
         respond()
     post(
-        V, S, R, coef_ref, surface, 1, 2 * step + 1,
+        V, S, R, old_r, coef_ref, surface, 1, 2 * step + 1,
         lambda r: V[VX, 0, pl.ds(PAD + r, ROWS)],
         lambda r: G[0, pl.ds(r, ROWS)],
         lambda r: G[1, pl.ds(r, ROWS)],
     )
 
 
-def behind_bond(V, S, R, coef_ref, force, surface, msg, missing, G, step, window, respond=None):
+def behind_bond(V, S, R, old_r, coef_ref, force, surface, msg, missing, G, step, window, respond=None):
     (b,) = coefs(coef_ref, (C_B,))
     _, has_behind, _ = place()
     keep = jnp.where(has_behind, 1.0, 0.0).astype(jnp.float32)
@@ -334,7 +334,7 @@
     if respond is not None:
         respond()
     post(
-        V, S, R, coef_ref, surface, 0, 2 * step,
+        V, S, R, old_r, coef_ref, surface, 0, 2 * step,
         lambda r: G[0, pl.ds(r, ROWS)],
         lambda r: V[VY, 1, pl.ds(PAD + r, ROWS)],
         lambda r: V[VZ, 1, pl.ds(PAD + r, ROWS)],
@@ -342,18 +342,19 @@
 
 
 def start_kernel(
-    velocity, stress, memory, layer_ref, lam, mu, buoy, rate, defect,
-    V, S, R, coef_ref, msg_near, msg_far, sems,
+    velocity, stress, layer_ref, lam, mu, buoy, rate, defect, after_this, V, S, coef_ref, msg_near, msg_far
 ):
-    across = velocity.shape[2]
-    inside = pl.ds(PAD, across)
-    copies = [pltpu.make_async_copy(stress.at[i], S.at[i, :, inside], sems.at[i]) for i in range(6)]
-    copies += [pltpu.make_async_copy(velocity.at[i], V.at[i, :, inside], sems.at[6 + i]) for i in range(3)]
-    late = [pltpu.make_async_copy(memory.at[i], R.at[i], sems.at[9 + i]) for i in range(6)]
-    for copy in copies + late:
-        copy.start()
+    del after_this
     zero_edges(V)
     zero_edges(S)
+
+    def load(r):
+        here, _, _, out = spans(r)
+        for ref, source in ((V, velocity), (S, stress)):
+            for where in np.ndindex(*source.shape[:2]):
+                ref[(*where, here)] = source[(*where, out)]
+
+    over_rows(velocity.shape[2], load)
     layer = layer_ref[...]
 
     def per_depth(table):
@@ -385,8 +386,6 @@
     ):
         coef_ref[row : row + 1, :] = value
     coef_ref[12:16, :] = jnp.zeros((4, layer.shape[1]), jnp.float32)
-    for copy in copies:
-        copy.wait()
     even, _, _ = place()
 
     @pl.when(even)
@@ -398,9 +397,6 @@
     def _():
         pre_behind(V, S, coef_ref, msg_near, None, 0)
         pre_ahead(V, S, coef_ref, msg_far, None, 0)
-
-    for copy in late:
-        copy.wait()
 
 
 def first_kernel(window, V0, S, R, coef_ref, force, surface, V, msg, W):
@@ -423,26 +419,26 @@
 
 def near_kernel(step, window, V0, S0, R0, coef_ref, force, surface, msg, V, S, R, *rest):
     G = rest[-1]
+    R0 = R0 if step == 0 else R
     even, _, _ = place()
     more = step < STEPS - 1
 
     @pl.when(even)
     def _():
-        ahead_bond(V, S, R, coef_ref, force.at[step], surface, msg, None, G, step, window)
+        ahead_bond(V, S, R, R0, coef_ref, force.at[step], surface, msg, None, G, step, window)
         if more:
             pre_ahead(V, S, coef_ref, rest[0], force.at[step + 1], window)
 
     @pl.when(jnp.logical_not(even))
     def _():
-        behind_bond(V, S, R, coef_ref, force.at[step], surface, msg, None, G, step, window)
+        behind_bond(V, S, R, R0, coef_ref, force.at[step], surface, msg, None, G, step, window)
         if more:
             pre_behind(V, S, coef_ref, rest[0], force.at[step + 1], window)
 
 
-def far_kernel(step, window, V0, S0, R0, coef_ref, force, surface, msg, *rest):
-    rest = list(rest)
-    missing = rest.pop(0) if step > 0 else None
+def far_kernel(step, window, V0, S0, R0, coef_ref, force, surface, msg, other, *rest):
     V, S, R, D = rest[:4]
+    missing, old_r = (other, R) if step > 0 else (None, other)
     G, W = rest[-2:]
     early = rest[4] if step < STEPS - 2 else None
     even, _, _ = place()
@@ -452,7 +448,7 @@
     @pl.when(even)
     def _():
         behind_bond(
-            V, S, R, coef_ref, here, surface, msg, missing, G, step, window,
+            V, S, R, old_r, coef_ref, here, surface, msg, missing, G, step, window,
             lambda: response_ahead(V, S, coef_ref, D, W),
         )
         pre_behind(V, S, coef_ref, None, then, window)
@@ -460,7 +456,7 @@
     @pl.when(jnp.logical_not(even))
     def _():
         ahead_bond(
-            V, S, R, coef_ref, here, surface, msg, missing, G, step, window,
+            V, S, R, old_r, coef_ref, here, surface, msg, missing, G, step, window,
             lambda: response_behind(V, S, coef_ref, D, W),
         )
         pre_ahead(V, S, coef_ref, None, then, window)
@@ -496,7 +492,7 @@
         done, other = copies(1 - cell), copies(cell)
         for copy in done:
             copy.start()
-        bond(V, S, R, coef_ref, here, surface, msg, missing, G, step, window)
+        bond(V, S, R, R, coef_ref, here, surface, msg, missing, G, step, window)
         for copy in other:
             copy.start()
         for copy in done + other:
@@ -512,20 +508,23 @@
 
 
 ENTRY_ROW, TRUCK_ROW = 36, 40
+GROUP = 8
 
 
 def lane_blocks(table, width):
     return sum(lane_roll(table[s : s + 1, :], s * width) for s in range(STEPS))
 
 
-def split_kernel(record, cells, loads, entries, out):
+def split_kernel(panel, slots, own, behind, cells, out):
     tiles, _, lanes = out.shape
-    slots = loads.shape[0]
-    pieces = record.shape[1] // lanes
+    pieces = panel // lanes
     third = pieces // 3
     cell_of = cells[...]
+    me = lax.axis_index("line")
+    group, mine = lax.div(me, tiles), lax.rem(me, tiles)
     row = lax.broadcasted_iota(jnp.int32, (3 * tiles, cell_of.shape[1]), 0)
-    first = lax.div(row, 3) * 2 + lax.rem(row, 3)
+    first = (lax.div(row, 3) + group * tiles) * 2 + lax.rem(row, 3)
+    record = jnp.where(group == 0, own[:, :panel], behind[:, :panel])
 
     def share(cell, columns):
         hit = jnp.where(cell == cell_of, 1.0, 0.0).astype(jnp.float32)
@@ -534,15 +533,24 @@
         )
 
     part_x = share(first - 1, slice(0, third * lanes))
-    part_yz = share(first, slice(third * lanes, pieces * lanes))
-    rows, entry = loads[...], lane_blocks(entries[...], slots)
+    part_yz = share(first, slice(third * lanes, panel))
+
+    def trucks(source):
+        blocks = [source[0:8, panel + i * lanes : panel + (i + 1) * lanes] for i in range(slots // 8 + 1)]
+        return blocks[:-1], lane_blocks(blocks[-1], slots)
+
+    own_rows, own_entry = trucks(own)
+    far_rows, far_entry = trucks(behind)
     for tile in range(tiles):
-        mine = slice(3 * tile, 3 * tile + 3)
+        these = slice(3 * tile, 3 * tile + 3)
         for m in range(pieces):
             part, at = (part_x, m) if m < third else (part_yz, m - third)
-            out[tile, 3 * m : 3 * m + 3, :] = part[mine, at * lanes : (at + 1) * lanes]
-        out[tile, ENTRY_ROW : ENTRY_ROW + 1, :] = entry
-        out[tile, TRUCK_ROW : TRUCK_ROW + slots, :] = rows
+            out[tile, 3 * m : 3 * m + 3, :] = part[these, at * lanes : (at + 1) * lanes]
+        passed = mine < tile
+        out[tile, ENTRY_ROW : ENTRY_ROW + 1, :] = jnp.where(passed, own_entry, far_entry)
+        for i in range(slots // 8):
+            at = TRUCK_ROW + 8 * i
+            out[tile, at : at + 8, :] = jnp.where(passed, own_rows[i], far_rows[i])
 
 
 def prepare_kernel(parts, loads, entries, cells, force, surface, table, rows_out):
@@ -560,15 +568,15 @@
                 force[s, comp, cell, pl.ds(5, per, stride=2), :] = scale * lane_roll(panel, FZ)
 
     slots = loads.shape[0]
-    me = lax.axis_index("line")
+    tiles = parts.shape[0]
+    mine = lax.rem(lax.axis_index("line"), tiles)
     table[...] = jnp.zeros(table.shape, jnp.float32)
     table[0:1, :] = lane_blocks(entries[...], slots)
     table[STEPS + 1 : STEPS + 2, :] = lane_blocks(cells[...], slots)
     rows = [loads[...]]
     for k in range(1, STEPS + 1):
-        source = jnp.maximum(me - k, 0)
-        there = jnp.where(me >= k, 1.0, 0.0).astype(jnp.float32)
-        rows.append(there * parts[source, TRUCK_ROW : TRUCK_ROW + slots, :])
+        source = lax.rem(mine + (tiles - k), tiles)
+        rows.append(parts[source, TRUCK_ROW : TRUCK_ROW + slots, :])
         table[k : k + 1, :] = parts[source, ENTRY_ROW : ENTRY_ROW + 1, :]
     columns = table[...].T
     rows_out[...] = jnp.zeros(rows_out.shape, jnp.float32)
@@ -639,29 +647,44 @@
     def as_rows(table):
         return jnp.pad(table.astype(f32), ((0, 8 - STEPS), (0, depth - slots)))
 
+    def ahead_by(x, distance):
+        return lax.ppermute(x, "line", [(i, i + distance) for i in range(tiles - distance)])
+
     entries, cells = as_rows(truck_entry), as_rows(truck_cell)
+    piers, panel = pier_panels.shape[1:]
+    blocks = [truck_loads[at : at + 8] for at in range(0, slots, 8)] + [entries]
+    blocks = [jnp.pad(block, ((0, piers - 8), (0, 0))) for block in blocks]
+    own = jnp.concatenate([pier_panels[0], *blocks], axis=1)
+    behind = ahead_by(own, GROUP)
+    reach = 2 * GROUP
+    index = lax.axis_index("line")
+    while reach < tiles:
+        record = jnp.where(index < GROUP, own, behind)[:, :panel]
+        record = jnp.where(index < reach, record, ahead_by(record, reach))
+        behind = jnp.concatenate([record, behind[:, panel:]], axis=1)
+        reach *= 2
     parts = call(
-        split_kernel,
-        (pier_panels[0], pier_cell[None, :], truck_loads, entries),
-        (WHOLE,) * 4,
-        jax.ShapeDtypeStruct((tiles, TRUCK_ROW + slots, depth), f32),
+        functools.partial(split_kernel, panel, slots),
+        (own, behind, pier_cell[None, :]),
+        (WHOLE,) * 3,
+        jax.ShapeDtypeStruct((GROUP, TRUCK_ROW + slots, depth), f32),
         WHOLE,
         name="split",
     )
-    parts = lax.all_to_all(parts, "line", 0, 0, tiled=True)
-
-    V, S, R, coef, msg_near, msg_far = call(
+
+    V, S, coef, msg_near, msg_far = call(
         start_kernel,
         (
-            *(pltpu.with_memory_space_constraint(x, pltpu.HBM) for x in (velocity, stress, memory)),
-            layer[None, :], lame_lambda, lame_mu, buoyancy, relax_rate, defect_mu,
+            velocity, stress, layer[None, :], lame_lambda, lame_mu, buoyancy, relax_rate, defect_mu,
+            parts,
         ),
-        (ANYWHERE,) * 3 + (WHOLE,) + (SCALARS,) * 5,
-        (v_type, s_type, r_type, c_type, m_type, m_type),
-        (WHOLE,) * 6,
-        scratch=(pltpu.SemaphoreType.DMA((15,)),),
+        (WHOLE,) * 3 + (SCALARS,) * 5 + (ANYWHERE,),
+        (v_type, s_type, c_type, m_type, m_type),
+        (WHOLE,) * 5,
         name="start",
     )
+    groups = [list(range(at, at + GROUP)) for at in range(0, tiles, GROUP)]
+    parts = lax.all_to_all(parts, "line", 0, 0, axis_index_groups=groups, tiled=True)
     msg_far = lax.ppermute(msg_far, "line", far)
     msg_near = lax.ppermute(msg_near, "line", near)
 
@@ -676,7 +699,7 @@
     )
     V, early = call(
         functools.partial(first_kernel, window),
-        tuple(in_vmem(x) for x in (V, S, R, coef, force, surface)),
+        tuple(in_vmem(x) for x in (V, S)) + (memory,) + tuple(in_vmem(x) for x in (coef, force, surface)),
         (WHOLE,) * 6,
         (v_type, m_type),
         (WHOLE,) * 2,
@@ -687,10 +710,12 @@
     early = lax.ppermute(early, "line", far)
     state = (v_type, s_type, r_type)
     same = {0: 0, 1: 1, 2: 2}
-    missing = None
+    R = missing = None
     for step in range(STEPS):
         more = step < STEPS - 1
-        ins = tuple(in_vmem(x) for x in (V, S, R, coef, force, surface, msg_near))
+        ins = [in_vmem(x) for x in (V, S, R if step else memory, coef, force, surface, msg_near)]
+        if step == 0:
+            ins[2] = memory
         outs = state + ((m_type,) if more else ())
         V, S, R, *msg = call(
             functools.partial(near_kernel, step, window),
@@ -699,13 +724,13 @@
             outs,
             (WHOLE,) * len(outs),
             scratch=(ghost,),
-            aliases=same,
+            aliases=same if step else {0: 0, 1: 1},
             name="near" + str(step),
         )
         if more:
             msg_near = lax.ppermute(msg[0], "line", near)
-        ins = (V, S, R, coef, force, surface, msg_far) + ((missing,) if step else ())
-        ins = tuple(in_vmem(x) for x in ins)
+        ins = tuple(in_vmem(x) for x in (V, S, R, coef, force, surface, msg_far))
+        ins += (in_vmem(missing) if step else memory,)
         if more:
             outs = state + (m_type,) + ((m_type,) if step < STEPS - 2 else ())
             V, S, R, missing, *msg = call(

time: 58.4 us -> 57.9 us (level)
  waiting for transfers between devices: 14.9 us -> 9.17 us
  starting transfers between devices: 24.4 us -> 29.7 us
  Pallas kernels: 14.9 us -> 13.4 us
  other arithmetic: 0.69 us -> 1.57 us
    all_to_all x1, waiting for transfers between devices: 5.18 us -> 0.01 us  [body(): lax.all_to_all(parts, 'line', 0, 0, axis_index_groups=groups, tiled=True)]
    ppermute x4, starting transfers between devices: 9.49 us -> 14.5 us  [body(): early = lax.ppermute(msg[0], 'line', far)]
    ppermute x0 -> x1, waiting for transfers between devices: none -> 4.62 us  [ahead_by(): lax.ppermute(x, 'line', [(i, i + distance) for i in range(tiles - distanc...]
    ppermute x4, waiting for transfers between devices: 8.11 us -> 4.27 us  [body(): early = lax.ppermute(msg[0], 'line', far)]
    ppermute x5, starting transfers between devices: 2.82 us -> 0.36 us  [body(): msg_near = lax.ppermute(msg[0], 'line', near)]
    ppermute x1, waiting for transfers between devices: 1.58 us -> 0.01 us  [body(): early = lax.ppermute(early, 'line', far)]
    ppermute x1, starting transfers between devices: 1.91 us -> 3.46 us  [body(): early = lax.ppermute(early, 'line', far)]
    pallas_call x16, Pallas kernels: 14.9 us -> 13.4 us  [call(): pl.pallas_call(kernel, out_shape=outs, in_specs=specs, out_specs=out_spec...]
  transfers between devices with their start and end apart: 13 -> 14, of which waited for: 6 -> 4; matrix products, arithmetic and copies ran while one was open for 0% -> 0% of each run, Pallas kernels for 21% -> 19%
where the time goes in v3:
time: 57.9 us; the launch traced here: 57.2 us
  starting transfers between devices  29.7 us (51%)
  Pallas kernels  13.4 us (23%)
  waiting for transfers between devices  9.17 us (16%)
  local copies, waits for them, and re-layouts  2.33 us (4%)
  other arithmetic  1.57 us (3%)
  between operations  0.96 us (2%)
    ppermute x4, starting transfers between devices, body(): early = lax.ppermute(msg[0], 'line', far)  14.5 us
    pallas_call x16, Pallas kernels, call(): pl.pallas_call(kernel, out_shape=outs, in_specs=specs, out_specs=out_spec...  13.4 us
    all_to_all x1, starting transfers between devices, body(): lax.all_to_all(parts, 'line', 0, 0, axis_index_groups=groups, tiled=True)  6.43 us
    ppermute x1, waiting for transfers between devices, ahead_by(): lax.ppermute(x, 'line', [(i, i + distance) for i in range(tiles - distanc...  4.62 us
    ppermute x4, waiting for transfers between devices, body(): early = lax.ppermute(msg[0], 'line', far)  4.27 us
    ppermute x1, starting transfers between devices, body(): msg_far = lax.ppermute(msg_far, 'line', far)  3.65 us
    ppermute x1, starting transfers between devices, body(): early = lax.ppermute(early, 'line', far)  3.46 us
    unnamed x24, local copies, waits for them, and re-layouts  2.32 us
  transfers between devices with their start and end apart: 14, of which 4 were waited for; matrix products, arithmetic and copies ran while one was open for 0% of the time, Pallas kernels for 19%

profile of v3, /device:TPU:17, one launch (start us, length us, event | category | flops | bytes accessed | tf_op | source)
XLA Modules:
  0.0 57.2 jit_solution(6923295502997196472)
XLA Ops:
  0.7 0.8 %convert_element_type.9 = f32[6,16]{1,0:T(8,128)S(1)} convert(s32[6,16]{1,0:T(8,128)} %param.25) | non-fusion elementwise | flops 96 | bytes 768 | tf_op jit(solution)/shard_map/convert_element_type | solution.py:648
  1.4 0.8 %pad_maximum_fusion.own = f32[8,1920]{1,0:T(8,128)S(1)} fusion(f32[8,128]{1,0:T(8,128)S(1)} %pad.7.entries, f32[8,128]{1,0:T(8,128)S(1)} %get-tuple-element.122, f32[8,128]{1,0:T(8,128)S(1)} %get-tuple-element.121, f32[8,1536]{1,0:T(8,128)} %bitcast.5), kind=kLoop, calls=%fused_computation | loop fusion | flops 46080 | bytes 122880 | tf_op jit(solution)/shard_map/concatenate | solution.py:657
  2.2 1.3 %collective-permute-start = (f32[8,1920]{1,0:T(8,128)S(1)}, f32[8,1920]{1,0:T(8,128)S(1)}, u32[]{:S(2)}, u32[]{:S(2)}) collective-permute-start(f32[8,1920]{1,0:T(8,128)S(1)} %pad_maximum_fusion.own), channel_id=1, source_target_pairs={{0,8},{1,9},{2,10},{3,11},{4,12},{5,13},{6,14},{7,15},{16,24},{17,... | collective-permute-start | bytes 184328 | tf_op jit(solution)/shard_map/ppermute | solution.py:651
  3.5 4.6 %collective-permute-done.behind = f32[8,1920]{1,0:T(8,128)S(1)} collective-permute-done((f32[8,1920]{1,0:T(8,128)S(1)}, f32[8,1920]{1,0:T(8,128)S(1)}, u32[]{:S(2)}, u32[]{:S(2)}) %collective-permute-start) | collective-permute-done | bytes 61472 | tf_op jit(solution)/shard_map/ppermute | solution.py:651
  8.1 0.7 %copy-done.4 = s32[8]{0:T(128)S(1)} copy-done((s32[8]{0:T(128)S(1)}, s32[8]{0:T(128)}, u32[]{:S(2)}) %copy-start.4) | copy-done | bytes 56
  8.8 1.0 %split.1.after_this = f32[8,56,128]{2,1,0:T(8,128)} custom-call(f32[8,1920]{1,0:T(8,128)S(1)} %pad_maximum_fusion.own, f32[8,1920]{1,0:T(8,128)S(1)} %collective-permute-done.behind, s32[1,8]{1,0:T(1,128)S(1)} %bitcast.3), custom_call_target="tpu_custom_call" | custom-call | flops 983296 | bytes 245824 | tf_op jit(solution)/shard_map/split/pallas_call | solution.py:611
  9.8 6.4 %all-to-all-start = ((f32[8,56,128]{2,1,0:T(8,128)}), f32[8,56,128]{2,1,0:T(8,128)S(1)}, u32[]{:S(2)}, u32[]{:S(2)}) async-start(f32[8,56,128]{2,1,0:T(8,128)} %split.1.after_this), calls=%async_computation | async-start | bytes 458752 | tf_op jit(solution)/shard_map/all_to_all | solution.py:687
  16.3 0.6 %copy-done.5 = s32[128]{0:T(128)S(1)} copy-done((s32[128]{0:T(128)S(1)}, s32[128]{0:T(128)}, u32[]{:S(2)}) %copy-start.5) | copy-done | bytes 536
  16.9 0.0 copy-done.6
  16.9 0.0 copy-done.7
  16.9 1.0 %copy-done.2 = f32[3,2,128,128]{3,2,1,0:T(8,128)S(1)} copy-done((f32[3,2,128,128]{3,2,1,0:T(8,128)S(1)}, f32[3,2,128,128]{3,2,1,0:T(8,128)}, u32[]{:S(2)}) %copy-start.2) | copy-done | bytes 393240
  17.9 1.0 %start.1 = (f32[3,2,144,128]{3,2,1,0:T(8,128)S(1)}, f32[6,2,144,128]{3,2,1,0:T(8,128)S(1)}, f32[16,128]{1,0:T(8,128)S(1)}, f32[3,128,128]{2,1,0:T(8,128)S(1)}, f32[3,128,128]{2,1,0:T(8,128)S(1)}) custom-call(f32[3,2,128,128]{3,2,1,0:T(8,128)S(1)} %copy-done.2, f32[6,2,128,128]{3,2,1,0:T(8,128)S(1)} %copy-done.1, s32[1,128]{1,0:T(1,128)S(1)} %bitcast.4, ...), custom_call_target="tpu_custom_call" | custom-call | flops 11277568 | bytes 2819392 | tf_op jit(solution)/shard_map/start/pallas_call | solution.py:611
  18.9 0.1 collective-permute-start.1
  19.0 3.7 %collective-permute-start.2 = (f32[3,128,128]{2,1,0:T(8,128)S(1)}, f32[3,128,128]{2,1,0:T(8,128)S(1)}, u32[]{:S(2)}, u32[]{:S(2)}) collective-permute-start(f32[3,128,128]{2,1,0:T(8,128)S(1)} %get-tuple-element.72), channel_id=1, source_target_pairs={{1,2},{3,4},{5,6},{7,8},{9,10},{11,12},{13,14},{2,1},{4,3},{6,5},{... | collective-permute-start | bytes 589832 | tf_op jit(solution)/shard_map/ppermute | solution.py:688
  22.7 0.0 all-to-all-done.parts
  22.7 0.6 %prepare.1 = (f32[6,3,3,16,128]{4,3,2,1,0:T(8,128)S(1)}, f32[128,128]{1,0:T(8,128)S(1)}) custom-call(f32[8,56,128]{2,1,0:T(8,128)S(1)} %all-to-all-done.parts, f32[16,128]{1,0:T(8,128)S(1)} %copy-done.3, f32[8,128]{1,0:T(8,128)S(1)} %pad.7.entries, f32[8,128]{1,0:T(8,128)S(1)} %pad.8.cells), custom_call_target="tpu_custom_call" | custom-call | flops 1966080 | bytes 491520 | tf_op jit(solution)/shard_map/prepare/pallas_call | solution.py:611
  23.3 0.5 first.1
  23.8 0.5 near0.1
  24.3 0.1 collective-permute-start.3
  24.4 3.5 %collective-permute-start.4 = (f32[3,128,128]{2,1,0:T(8,128)S(1)}, f32[3,128,128]{2,1,0:T(8,128)S(1)}, u32[]{:S(2)}, u32[]{:S(2)}) collective-permute-start(f32[3,128,128]{2,1,0:T(8,128)S(1)} %get-tuple-element.80), channel_id=1, source_target_pairs={{1,2},{3,4},{5,6},{7,8},{9,10},{11,12},{13,14},{2,1},{4,3},{6,5},{... | collective-permute-start | bytes 589832 | tf_op jit(solution)/shard_map/ppermute | solution.py:710
  27.9 0.3 collective-permute-done.2.msg
  28.1 1.3 %far0.1 = (f32[3,2,144,128]{3,2,1,0:T(8,128)S(1)}, f32[6,2,144,128]{3,2,1,0:T(8,128)S(1)}, f32[6,2,128,128]{3,2,1,0:T(8,128)S(1)}, f32[3,128,128]{2,1,0:T(8,128)S(1)}, f32[3,128,128]{2,1,0:T(8,128)S(1)}) custom-call(f32[3,2,144,128]{3,2,1,0:T(8,128)S(1)} %get-tuple-element.69.V0, ...), custom_call_target="tpu_custom_call", output_to_operand_aliasing={{0}: (0, {}), {1}: (1, {}), {2}: (2, {})} | custom-call | flops 28901376 | bytes 7225344 | tf_op jit(solution)/shard_map/far0/pallas_call | solution.py:611
  29.5 0.0 collective-permute-done.3.msg
  29.5 0.5 near1.1
  29.9 0.1 collective-permute-start.5
  30.0 3.7 %collective-permute-start.6 = (f32[3,128,128]{2,1,0:T(8,128)S(1)}, f32[3,128,128]{2,1,0:T(8,128)S(1)}, u32[]{:S(2)}, u32[]{:S(2)}) collective-permute-start(f32[3,128,128]{2,1,0:T(8,128)S(1)} %get-tuple-element.89), channel_id=1, source_target_pairs={{1,2},{3,4},{5,6},{7,8},{9,10},{11,12},{13,14},{2,1},{4,3},{6,5},{... | collective-permute-start | bytes 589832 | tf_op jit(solution)/shard_map/ppermute | solution.py:748
  33.7 1.3 %far1.1 = (f32[3,2,144,128]{3,2,1,0:T(8,128)S(1)}, f32[6,2,144,128]{3,2,1,0:T(8,128)S(1)}, f32[6,2,128,128]{3,2,1,0:T(8,128)S(1)}, f32[3,128,128]{2,1,0:T(8,128)S(1)}, f32[3,128,128]{2,1,0:T(8,128)S(1)}) custom-call(f32[3,2,144,128]{3,2,1,0:T(8,128)S(1)} %get-tuple-element.77.V0, ...), custom_call_target="tpu_custom_call", output_to_operand_aliasing={{0}: (0, {}), {1}: (1, {}), {2}: (2, {})} | custom-call | flops 24182784 | bytes 6045696 | tf_op jit(solution)/shard_map/far1/pallas_call | solution.py:611
  35.1 0.0 collective-permute-done.5.msg
  35.1 0.5 near2.1
  35.5 0.1 collective-permute-start.7
  35.6 3.8 %collective-permute-start.8 = (f32[3,128,128]{2,1,0:T(8,128)S(1)}, f32[3,128,128]{2,1,0:T(8,128)S(1)}, u32[]{:S(2)}, u32[]{:S(2)}) collective-permute-start(f32[3,128,128]{2,1,0:T(8,128)S(1)} %get-tuple-element.98), channel_id=1, source_target_pairs={{1,2},{3,4},{5,6},{7,8},{9,10},{11,12},{13,14},{2,1},{4,3},{6,5},{... | collective-permute-start | bytes 589832 | tf_op jit(solution)/shard_map/ppermute | solution.py:748
  39.4 0.0 collective-permute-done.6.msg
  39.4 1.3 %far2.1 = (f32[3,2,144,128]{3,2,1,0:T(8,128)S(1)}, f32[6,2,144,128]{3,2,1,0:T(8,128)S(1)}, f32[6,2,128,128]{3,2,1,0:T(8,128)S(1)}, f32[3,128,128]{2,1,0:T(8,128)S(1)}, f32[3,128,128]{2,1,0:T(8,128)S(1)}) custom-call(f32[3,2,144,128]{3,2,1,0:T(8,128)S(1)} %get-tuple-element.86.V0, ...), custom_call_target="tpu_custom_call", output_to_operand_aliasing={{0}: (0, {}), {1}: (1, {}), {2}: (2, {})} | custom-call | flops 24182784 | bytes 6045696 | tf_op jit(solution)/shard_map/far2/pallas_call | solution.py:611
  40.8 0.5 near3.1
  41.3 0.1 collective-permute-start.9
  41.3 3.4 %collective-permute-start.10 = (f32[3,128,128]{2,1,0:T(8,128)S(1)}, f32[3,128,128]{2,1,0:T(8,128)S(1)}, u32[]{:S(2)}, u32[]{:S(2)}) collective-permute-start(f32[3,128,128]{2,1,0:T(8,128)S(1)} %get-tuple-element.107), channel_id=1, source_target_pairs={{1,2},{3,4},{5,6},{7,8},{9,10},{11,12},{13,14},{2,1},{4,3},{6,5},{... | collective-permute-start | bytes 589832 | tf_op jit(solution)/shard_map/ppermute | solution.py:748
  44.7 0.2 collective-permute-done.8.msg
  44.9 1.3 %far3.1 = (f32[3,2,144,128]{3,2,1,0:T(8,128)S(1)}, f32[6,2,144,128]{3,2,1,0:T(8,128)S(1)}, f32[6,2,128,128]{3,2,1,0:T(8,128)S(1)}, f32[3,128,128]{2,1,0:T(8,128)S(1)}, f32[3,128,128]{2,1,0:T(8,128)S(1)}) custom-call(f32[3,2,144,128]{3,2,1,0:T(8,128)S(1)} %get-tuple-element.95.V0, ...), custom_call_target="tpu_custom_call", output_to_operand_aliasing={{0}: (0, {}), {1}: (1, {}), {2}: (2, {})} | custom-call | flops 24182784 | bytes 6045696 | tf_op jit(solution)/shard_map/far3/pallas_call | solution.py:611
  46.2 0.0 collective-permute-done.9.msg
  46.2 0.5 near4.1
  46.7 0.1 collective-permute-start.11
  46.8 3.7 %collective-permute-start.12 = (f32[3,128,128]{2,1,0:T(8,128)S(1)}, f32[3,128,128]{2,1,0:T(8,128)S(1)}, u32[]{:S(2)}, u32[]{:S(2)}) collective-permute-start(f32[3,128,128]{2,1,0:T(8,128)S(1)} %get-tuple-element.116), channel_id=1, source_target_pairs={{1,2},{3,4},{5,6},{7,8},{9,10},{11,12},{13,14},{2,1},{4,3},{6,5},{... | collective-permute-start | bytes 589832 | tf_op jit(solution)/shard_map/ppermute | solution.py:748
  50.4 0.0 collective-permute-done.10.msg
  50.4 1.0 %far4.1 = (f32[3,2,144,128]{3,2,1,0:T(8,128)S(1)}, f32[6,2,144,128]{3,2,1,0:T(8,128)S(1)}, f32[6,2,128,128]{3,2,1,0:T(8,128)S(1)}, f32[3,128,128]{2,1,0:T(8,128)S(1)}) custom-call(f32[3,2,144,128]{3,2,1,0:T(8,128)S(1)} %get-tuple-element.104.V0, ...), custom_call_target="tpu_custom_call", output_to_operand_aliasing={{0}: (0, {}), {1}: (1, {}), {2}: (2, {})} | custom-call | flops 24182784 | bytes 6045696 | tf_op jit(solution)/shard_map/far4/pallas_call | solution.py:611
  51.5 0.0 collective-permute-done.11.msg
  51.5 0.3 near5.1
  51.8 4.1 %collective-permute-done.12.msg = f32[3,128,128]{2,1,0:T(8,128)S(1)} collective-permute-done((f32[3,128,128]{2,1,0:T(8,128)S(1)}, f32[3,128,128]{2,1,0:T(8,128)S(1)}, u32[]{:S(2)}, u32[]{:S(2)}) %collective-permute-start.12) | collective-permute-done | bytes 196640 | tf_op jit(solution)/shard_map/ppermute | solution.py:748
  55.9 1.3 %last.1 = (f32[3,2,144,128]{3,2,1,0:T(8,128)S(1)}, f32[6,2,144,128]{3,2,1,0:T(8,128)S(1)}, f32[6,2,128,128]{3,2,1,0:T(8,128)S(1)}, f32[3,2,128,128]{3,2,1,0:T(8,...) custom-call(f32[3,2,144,128]{3,2,1,0:T(8,128)S(1)} %get-tuple-elemen, ...), custom_call_target="tpu_custom_call", output_to_operand_aliasing={{0}: (0, {}), {1}: (1, {}), {2}: (2, {})} | custom-call | flops 24182784 | bytes 6045696 | tf_op jit(solution)/shard_map/last/pallas_call | solution.py:611
  (26 shorter events, 0.1 us)
Async XLA Ops:
  0.6 0.8 %copy-start.3 = (f32[16,128]{1,0:T(8,128)S(1)}, f32[16,128]{1,0:T(8,128)}, u32[]{:S(2)}) copy-start(f32[16,128]{1,0:T(8,128)} %loads.1) | copy-start | bytes 24580
  0.6 15.6 %copy-start.1 = (f32[6,2,128,128]{3,2,1,0:T(8,128)S(1)}, f32[6,2,128,128]{3,2,1,0:T(8,128)}, u32[]{:S(2)}) copy-start(f32[6,2,128,128]{3,2,1,0:T(8,128)} %stress.1) | copy-start | bytes 2359300
  2.2 5.9 %collective-permute-start = (f32[8,1920]{1,0:T(8,128)S(1)}, f32[8,1920]{1,0:T(8,128)S(1)}, u32[]{:S(2)}, u32[]{:S(2)}) collective-permute-start(f32[8,1920]{1,0:T(8,128)S(1)} %pad_maximum_fusion.own), channel_id=1, source_target_pairs={{0,8},{1,9},{2,10},{3,11},{4,12},{5,13},{6,14},{7,15},{16,24},{17,... | collective-permute-start | bytes 184328 | tf_op jit(solution)/shard_map/ppermute | solution.py:651
  8.1 0.7 %copy-start.4 = (s32[8]{0:T(128)S(1)}, s32[8]{0:T(128)}, u32[]{:S(2)}) copy-start(s32[8]{0:T(128)} %param.27) | copy-start | bytes 100
  9.8 6.5 %copy-start.8 = (f32[8]{0:T(128)S(1)}, f32[8]{0:T(128)}, u32[]{:S(2)}) copy-start(f32[8]{0:T(128)} %buoy.1) | copy-start | bytes 100
  9.8 6.5 %copy-start.9 = (f32[8]{0:T(128)S(1)}, f32[8]{0:T(128)}, u32[]{:S(2)}) copy-start(f32[8]{0:T(128)} %rate.1) | copy-start | bytes 100
  9.8 6.5 %copy-start.10 = (f32[8]{0:T(128)S(1)}, f32[8]{0:T(128)}, u32[]{:S(2)}) copy-start(f32[8]{0:T(128)} %defect.1) | copy-start | bytes 100
  9.8 12.9 %all-to-all-start = ((f32[8,56,128]{2,1,0:T(8,128)}), f32[8,56,128]{2,1,0:T(8,128)S(1)}, u32[]{:S(2)}, u32[]{:S(2)}) async-start(f32[8,56,128]{2,1,0:T(8,128)} %split.1.after_this), calls=%async_computation | async-start | bytes 458752 | tf_op jit(solution)/shard_map/all_to_all | solution.py:687
  16.2 0.7 %copy-start.5 = (s32[128]{0:T(128)S(1)}, s32[128]{0:T(128)}, u32[]{:S(2)}) copy-start(s32[128]{0:T(128)} %param.24) | copy-start | bytes 1540
  16.2 0.7 %copy-start.6 = (f32[8]{0:T(128)S(1)}, f32[8]{0:T(128)}, u32[]{:S(2)}) copy-start(f32[8]{0:T(128)} %lam.1) | copy-start | bytes 100
  16.2 0.7 %copy-start.7 = (f32[8]{0:T(128)S(1)}, f32[8]{0:T(128)}, u32[]{:S(2)}) copy-start(f32[8]{0:T(128)} %mu.1) | copy-start | bytes 100
  16.9 1.0 %copy-start.2 = (f32[3,2,128,128]{3,2,1,0:T(8,128)S(1)}, f32[3,2,128,128]{3,2,1,0:T(8,128)}, u32[]{:S(2)}) copy-start(f32[3,2,128,128]{3,2,1,0:T(8,128)} %velocity.1) | copy-start | bytes 1179652
  17.9 1.1 %copy-start.11 = (s32[6,16]{1,0:T(8,128)S(1)}, s32[6,16]{1,0:T(8,128)}, u32[]{:S(2)}) copy-start(s32[6,16]{1,0:T(8,128)} %param.26) | copy-start | bytes 1156
  17.9 5.4 %copy-start = (f32[6,2,128,128]{3,2,1,0:T(8,128)S(1)}, f32[6,2,128,128]{3,2,1,0:T(8,128)}, u32[]{:S(2)}) copy-start(f32[6,2,128,128]{3,2,1,0:T(8,128)} %other.1) | copy-start | bytes 2359300
  18.9 4.9 %collective-permute-start.1 = (f32[3,128,128]{2,1,0:T(8,128)S(1)}, f32[3,128,128]{2,1,0:T(8,128)S(1)}, u32[]{:S(2)}, u32[]{:S(2)}) collective-permute-start(f32[3,128,128]{2,1,0:T(8,128)S(1)} %get-tuple-element.68), channel_id=1, source_target_pairs={{0,1},{1,0},{2,3},{3,2},{4,5},{5,4},{6,7},{7,6},{8,9},{9,8},{10,11... | collective-permute-start | bytes 589832 | tf_op jit(solution)/shard_map/ppermute | solution.py:689
  19.0 9.1 %collective-permute-start.2 = (f32[3,128,128]{2,1,0:T(8,128)S(1)}, f32[3,128,128]{2,1,0:T(8,128)S(1)}, u32[]{:S(2)}, u32[]{:S(2)}) collective-permute-start(f32[3,128,128]{2,1,0:T(8,128)S(1)} %get-tuple-element.72), channel_id=1, source_target_pairs={{1,2},{3,4},{5,6},{7,8},{9,10},{11,12},{13,14},{2,1},{4,3},{6,5},{... | collective-permute-start | bytes 589832 | tf_op jit(solution)/shard_map/ppermute | solution.py:688
  24.3 5.1 %collective-permute-start.3 = (f32[3,128,128]{2,1,0:T(8,128)S(1)}, f32[3,128,128]{2,1,0:T(8,128)S(1)}, u32[]{:S(2)}, u32[]{:S(2)}) collective-permute-start(f32[3,128,128]{2,1,0:T(8,128)S(1)} %get-tuple-element.76), channel_id=1, source_target_pairs={{0,1},{1,0},{2,3},{3,2},{4,5},{5,4},{6,7},{7,6},{8,9},{9,8},{10,11... | collective-permute-start | bytes 589832 | tf_op jit(solution)/shard_map/ppermute | solution.py:731
  24.4 9.3 %collective-permute-start.4 = (f32[3,128,128]{2,1,0:T(8,128)S(1)}, f32[3,128,128]{2,1,0:T(8,128)S(1)}, u32[]{:S(2)}, u32[]{:S(2)}) collective-permute-start(f32[3,128,128]{2,1,0:T(8,128)S(1)} %get-tuple-element.80), channel_id=1, source_target_pairs={{1,2},{3,4},{5,6},{7,8},{9,10},{11,12},{13,14},{2,1},{4,3},{6,5},{... | collective-permute-start | bytes 589832 | tf_op jit(solution)/shard_map/ppermute | solution.py:710
  29.9 5.1 %collective-permute-start.5 = (f32[3,128,128]{2,1,0:T(8,128)S(1)}, f32[3,128,128]{2,1,0:T(8,128)S(1)}, u32[]{:S(2)}, u32[]{:S(2)}) collective-permute-start(f32[3,128,128]{2,1,0:T(8,128)S(1)} %get-tuple-element.85), channel_id=1, source_target_pairs={{0,1},{1,0},{2,3},{3,2},{4,5},{5,4},{6,7},{7,6},{8,9},{9,8},{10,11... | collective-permute-start | bytes 589832 | tf_op jit(solution)/shard_map/ppermute | solution.py:731
  30.0 9.4 %collective-permute-start.6 = (f32[3,128,128]{2,1,0:T(8,128)S(1)}, f32[3,128,128]{2,1,0:T(8,128)S(1)}, u32[]{:S(2)}, u32[]{:S(2)}) collective-permute-start(f32[3,128,128]{2,1,0:T(8,128)S(1)} %get-tuple-element.89), channel_id=1, source_target_pairs={{1,2},{3,4},{5,6},{7,8},{9,10},{11,12},{13,14},{2,1},{4,3},{6,5},{... | collective-permute-start | bytes 589832 | tf_op jit(solution)/shard_map/ppermute | solution.py:748
  35.5 5.2 %collective-permute-start.7 = (f32[3,128,128]{2,1,0:T(8,128)S(1)}, f32[3,128,128]{2,1,0:T(8,128)S(1)}, u32[]{:S(2)}, u32[]{:S(2)}) collective-permute-start(f32[3,128,128]{2,1,0:T(8,128)S(1)} %get-tuple-element.94), channel_id=1, source_target_pairs={{0,1},{1,0},{2,3},{3,2},{4,5},{5,4},{6,7},{7,6},{8,9},{9,8},{10,11... | collective-permute-start | bytes 589832 | tf_op jit(solution)/shard_map/ppermute | solution.py:731
  35.6 9.2 %collective-permute-start.8 = (f32[3,128,128]{2,1,0:T(8,128)S(1)}, f32[3,128,128]{2,1,0:T(8,128)S(1)}, u32[]{:S(2)}, u32[]{:S(2)}) collective-permute-start(f32[3,128,128]{2,1,0:T(8,128)S(1)} %get-tuple-element.98), channel_id=1, source_target_pairs={{1,2},{3,4},{5,6},{7,8},{9,10},{11,12},{13,14},{2,1},{4,3},{6,5},{... | collective-permute-start | bytes 589832 | tf_op jit(solution)/shard_map/ppermute | solution.py:748
  41.3 4.9 %collective-permute-start.9 = (f32[3,128,128]{2,1,0:T(8,128)S(1)}, f32[3,128,128]{2,1,0:T(8,128)S(1)}, u32[]{:S(2)}, u32[]{:S(2)}) collective-permute-start(f32[3,128,128]{2,1,0:T(8,128)S(1)} %get-tuple-element.103), channel_id=1, source_target_pairs={{0,1},{1,0},{2,3},{3,2},{4,5},{5,4},{6,7},{7,6},{8,9},{9,8},{10,11... | collective-permute-start | bytes 589832 | tf_op jit(solution)/shard_map/ppermute | solution.py:731
  41.3 9.1 %collective-permute-start.10 = (f32[3,128,128]{2,1,0:T(8,128)S(1)}, f32[3,128,128]{2,1,0:T(8,128)S(1)}, u32[]{:S(2)}, u32[]{:S(2)}) collective-permute-start(f32[3,128,128]{2,1,0:T(8,128)S(1)} %get-tuple-element.107), channel_id=1, source_target_pairs={{1,2},{3,4},{5,6},{7,8},{9,10},{11,12},{13,14},{2,1},{4,3},{6,5},{... | collective-permute-start | bytes 589832 | tf_op jit(solution)/shard_map/ppermute | solution.py:748
  46.7 4.8 %collective-permute-start.11 = (f32[3,128,128]{2,1,0:T(8,128)S(1)}, f32[3,128,128]{2,1,0:T(8,128)S(1)}, u32[]{:S(2)}, u32[]{:S(2)}) collective-permute-start(f32[3,128,128]{2,1,0:T(8,128)S(1)} %get-tuple-element.112), channel_id=1, source_target_pairs={{0,1},{1,0},{2,3},{3,2},{4,5},{5,4},{6,7},{7,6},{8,9},{9,8},{10,11... | collective-permute-start | bytes 589832 | tf_op jit(solution)/shard_map/ppermute | solution.py:731
  46.8 9.1 %collective-permute-start.12 = (f32[3,128,128]{2,1,0:T(8,128)S(1)}, f32[3,128,128]{2,1,0:T(8,128)S(1)}, u32[]{:S(2)}, u32[]{:S(2)}) collective-permute-start(f32[3,128,128]{2,1,0:T(8,128)S(1)} %get-tuple-element.116), channel_id=1, source_target_pairs={{1,2},{3,4},{5,6},{7,8},{9,10},{11,12},{13,14},{2,1},{4,3},{6,5},{... | collective-permute-start | bytes 589832 | tf_op jit(solution)/shard_map/ppermute | solution.py:748

commit v4 on v3

--- a/solution.py
+++ b/solution.py
@@ -44,6 +44,21 @@
     lax.fori_loop(0, count // ROWS, step, 0, unroll=UNROLL)
 
 
+class Planes:
+    def __init__(self, ref, first, across):
+        self.ref, self.first, self.shape = ref, first, (3, across, ref.shape[1])
+
+    def rows(self, at):
+        plane, out = at
+        return pl.ds((self.first + plane) * self.shape[1] + out.start, out.size)
+
+    def __getitem__(self, at):
+        return self.ref[self.rows(at)]
+
+    def __setitem__(self, at, value):
+        self.ref[self.rows(at)] = value
+
+
 def coefs(coef_ref, ids):
     return [coef_ref[i : i + 1, :] for i in ids]
 
@@ -85,9 +100,9 @@
 
     over_rows(V.shape[2] - 2 * PAD, work)
     if force is not None:
-        add_force(V, (VX, 1), force, (VX, 2), PAD + window)
+        add_force(V, (VX, 1), force, (VX, 1), PAD + window)
         if msg is not None:
-            add_force(msg, (2,), force, (VX, 2), window)
+            add_force(msg, (2,), force, (VX, 1), window)
 
 
 def pre_behind(V, S, coef_ref, msg, force, window):
@@ -138,9 +153,10 @@
         )
 
     over_rows(V.shape[2] - 2 * PAD, work)
-    add_force(V, (VX, 0), force, (VX, 1), PAD + window)
-    add_force(V, (VY, 1), force, (VY, 1), PAD + window)
-    add_force(V, (VZ, 1), force, (VZ, 1), PAD + window)
+    if force is not None:
+        add_force(V, (VX, 0), force, (VX, 0), PAD + window)
+        add_force(V, (VY, 1), force, (VY, 1), PAD + window)
+        add_force(V, (VZ, 1), force, (VZ, 1), PAD + window)
 
 
 def post(V, S, R, old_r, coef_ref, surface, cell, column, behind_x, ahead_y, ahead_z):
@@ -224,6 +240,82 @@
     over_rows(D.shape[1], rest)
 
 
+def first_response_behind(V, S, coef_ref, force, load, D, W, A, window):
+    b, b0, b1, m0, m1, lam, mu2, mu, l0 = coefs(
+        coef_ref, (C_B, C_B0, C_B1, C_M0, C_M1, C_LAM, C_MU2, C_MU, C_L0)
+    )
+    A[...] = jnp.zeros(A.shape, jnp.float32)
+
+    def given(r):
+        here, _, _, _ = spans(r)
+        A[1, here] = -b * S[XY, 1, here]
+        A[2, here] = -b * S[XZ, 1, here]
+
+    over_rows(D.shape[1], given)
+    for i, which in enumerate(((VX, 3), (VY, 2), (VZ, 2), (VY, 3), (VZ, 3))):
+        add_force(A, (i,), force, which, PAD + window)
+
+    def work(r):
+        here, up, down, out = spans(r)
+        vx, vy, vz = A[0, here], A[1, here], A[2, here]
+        exx = vx - V[VX, 1, here]
+        eyy = vy - A[1, up]
+        ezz = vz - m0 * before(vz)
+        volume = lam * (exx + eyy + ezz)
+        dyy = volume + mu2 * eyy
+        dzz = volume + mu2 * ezz + l0 * load[out, :]
+        dxy = mu * (A[0, down] - vx + (A[3, here] - vy))
+        dxz = mu * (m1 * after(vx) - vx + (A[4, here] - vz))
+        dyz = mu * (m1 * after(vy) - vy + (A[2, down] - vz))
+        W[0, here] = dyy
+        W[1, here] = dyz
+        D[0, out] = volume + mu2 * exx
+        D[1, out] = vy + b * (dxy - dyy + dyz) - b0 * before(dyz)
+        D[2, out] = vz + b * (dxz + dyz - dzz) + b1 * after(dzz)
+
+    over_rows(D.shape[1], work)
+
+    def rest(r):
+        _, up, down, out = spans(r)
+        D[1, out] = D[1, out] + b * W[0, down]
+        D[2, out] = D[2, out] - b * W[1, up]
+
+    over_rows(D.shape[1], rest)
+
+
+def first_response_ahead(V, S, coef_ref, force, D, W, A, window):
+    b, b0, m0, m1, lam, mu2, mu = coefs(coef_ref, (C_B, C_B0, C_M0, C_M1, C_LAM, C_MU2, C_MU))
+    A[...] = jnp.zeros(A.shape, jnp.float32)
+
+    def given(r):
+        here, _, _, _ = spans(r)
+        A[0, here] = b * S[XX, 0, here]
+
+    over_rows(D.shape[1], given)
+    for i, which in enumerate(((VX, 2), (VY, 3), (VZ, 3), (VX, 3))):
+        add_force(A, (i,), force, which, PAD + window)
+
+    def work(r):
+        here, up, down, out = spans(r)
+        vx, vy, vz = A[0, here], A[1, here], A[2, here]
+        exx = vx - A[3, here]
+        dxx = lam * (exx + (vy - A[1, up]) + (vz - m0 * before(vz))) + mu2 * exx
+        dxy = mu * (A[0, down] - vx + (V[VY, 0, here] - vy))
+        dxz = mu * (m1 * after(vx) - vx + (V[VZ, 0, here] - vz))
+        W[0, here] = dxy
+        D[0, out] = dxy
+        D[1, out] = dxz
+        D[2, out] = vx + b * (dxy + dxz - dxx) - b0 * before(dxz)
+
+    over_rows(D.shape[1], work)
+
+    def rest(r):
+        _, up, _, out = spans(r)
+        D[2, out] = D[2, out] - b * W[0, up]
+
+    over_rows(D.shape[1], rest)
+
+
 def early_ahead(V, S, R, coef_ref, msg, W, force, window):
     b, b0, m0, m1, lam, mu2, mu = coefs(coef_ref, (C_B, C_B0, C_M0, C_M1, C_LAM, C_MU2, C_MU))
 
@@ -247,7 +339,8 @@
         msg[2, out] = msg[2, out] - b * W[0, up]
 
     over_rows(msg.shape[1], rest)
-    add_force(msg, (2,), force, (VX, 2), window)
+    if force is not None:
+        add_force(msg, (2,), force, (VX, 1), window)
 
 
 def early_behind(V, S, R, coef_ref, surface, column, msg, W, force, window):
@@ -264,7 +357,8 @@
         sxx = S[XX, 0, here] + (volume + mu2 * vx) + DT * R[XX, 0, out]
         syy = S[YY, 0, here] + (volume + mu2 * eyy) + DT * R[YY, 0, out]
         szz = S[ZZ, 0, here] + (volume + mu2 * ezz) + DT * R[ZZ, 0, out]
-        szz = szz + l0 * lane_roll(surface[out, :], -column)
+        if surface is not None:
+            szz = szz + l0 * lane_roll(surface[out, :], -column)
         sxy = S[XY, 0, here] + mu * (V[VX, 0, down] - vx + (V[VY, 1, here] - vy)) + DT * R[XY, 0, out]
         sxz = S[XZ, 0, here] + mu * (m1 * after(vx) - vx + (V[VZ, 1, here] - vz)) + DT * R[XZ, 0, out]
         syz = S[YZ, 0, here] + mu * (m1 * after(vy) - vy + (V[VZ, 0, down] - vz)) + DT * R[YZ, 0, out]
@@ -282,11 +376,12 @@
         msg[2, out] = msg[2, out] - b * W[1, up]
 
     over_rows(msg.shape[1], rest)
-    add_force(msg, (1,), force, (VY, 0), window)
-    add_force(msg, (2,), force, (VZ, 0), window)
-
-
-def ahead_bond(V, S, R, old_r, coef_ref, force, surface, msg, missing, G, step, window, respond=None):
+    if force is not None:
+        add_force(msg, (1,), force, (VY, 0), window)
+        add_force(msg, (2,), force, (VZ, 0), window)
+
+
+def ahead_bond(V, S, R, old_r, coef_ref, force, surface, msg, missing, G, step, window, unforced=0, respond=None):
     (b,) = coefs(coef_ref, (C_B,))
     _, _, has_ahead = place()
     keep = jnp.where(has_ahead, 1.0, 0.0).astype(jnp.float32)
@@ -301,7 +396,7 @@
         G[1, out] = keep * (got(2, out) - b * S[XZ, 1, here])
 
     over_rows(R.shape[2], work)
-    if step == 0:
+    if step < unforced:
         add_force(G, (0,), force, (VY, 2), window)
         add_force(G, (1,), force, (VZ, 2), window)
     if respond is not None:
@@ -314,7 +409,7 @@
     )
 
 
-def behind_bond(V, S, R, old_r, coef_ref, force, surface, msg, missing, G, step, window, respond=None):
+def behind_bond(V, S, R, old_r, coef_ref, force, surface, msg, missing, G, step, window, unforced=0, respond=None):
     (b,) = coefs(coef_ref, (C_B,))
     _, has_behind, _ = place()
     keep = jnp.where(has_behind, 1.0, 0.0).astype(jnp.float32)
@@ -329,8 +424,8 @@
         G[0, out] = keep * (got(2, out) + b * S[XX, 0, here])
 
     over_rows(R.shape[2], work)
-    if step == 0:
-        add_force(G, (0,), force, (VX, 0), window)
+    if step < unforced:
+        add_force(G, (0,), force, (VX, 2), window)
     if respond is not None:
         respond()
     post(
@@ -341,12 +436,30 @@
     )
 
 
+def step_table(table, entries, cells):
+    table[...] = jnp.zeros(table.shape, jnp.float32)
+    steps, slots = entries.shape
+    table[0:steps, 0:slots] = entries[...].astype(jnp.float32)
+    table[8 : 8 + steps, 0:slots] = cells[...].astype(jnp.float32)
+
+
 def start_kernel(
-    velocity, stress, layer_ref, lam, mu, buoy, rate, defect, after_this, V, S, coef_ref, msg_near, msg_far
+    velocity, stress, memory, layer_ref, lam, mu, buoy, rate, defect, loads, entries, cells,
+    V, S, coef_ref, msg_near, msg_far, W, table,
 ):
-    del after_this
+    across = velocity.shape[2]
+    slots = loads.shape[0]
     zero_edges(V)
     zero_edges(S)
+    zero_edges(W)
+    step_table(table, entries, cells)
+    columns = table[...].T
+    trucks = 6 * across
+    msg_far[trucks : trucks + slots, :] = loads[...]
+    for i, at in enumerate((0, 8)):
+        first_row = trucks + (1 + i) * slots
+        column = columns[0:slots, at : at + 1]
+        msg_far[first_row : first_row + slots, :] = jnp.broadcast_to(column, loads.shape)
 
     def load(r):
         here, _, _, out = spans(r)
@@ -387,77 +500,100 @@
         coef_ref[row : row + 1, :] = value
     coef_ref[12:16, :] = jnp.zeros((4, layer.shape[1]), jnp.float32)
     even, _, _ = place()
+    now, then = Planes(msg_far, 0, across), Planes(msg_far, 3, across)
 
     @pl.when(even)
     def _():
         pre_ahead(V, S, coef_ref, msg_near, None, 0)
-        pre_behind(V, S, coef_ref, msg_far, None, 0)
+        pre_behind(V, S, coef_ref, now, None, 0)
 
     @pl.when(jnp.logical_not(even))
     def _():
         pre_behind(V, S, coef_ref, msg_near, None, 0)
-        pre_ahead(V, S, coef_ref, msg_far, None, 0)
-
-
-def first_kernel(window, V0, S, R, coef_ref, force, surface, V, msg, W):
-    even, _, _ = place()
-    zero_edges(W)
-    now, then = force.at[0], force.at[1]
-    add_force(V, (VX, 1), now, (VX, 2), PAD + window)
-    add_force(V, (VY, 0), now, (VY, 0), PAD + window)
-    add_force(V, (VZ, 0), now, (VZ, 0), PAD + window)
-    inner(V, S, coef_ref, now, window)
+        pre_ahead(V, S, coef_ref, now, None, 0)
+
+    inner(V, S, coef_ref, None, 0)
 
     @pl.when(even)
     def _():
-        early_behind(V, S, R, coef_ref, surface, 0, msg, W, then, window)
+        early_behind(V, S, memory, coef_ref, None, 0, then, W, None, 0)
 
     @pl.when(jnp.logical_not(even))
     def _():
-        early_ahead(V, S, R, coef_ref, msg, W, then, window)
+        early_ahead(V, S, memory, coef_ref, then, W, None, 0)
 
 
 def near_kernel(step, window, V0, S0, R0, coef_ref, force, surface, msg, V, S, R, *rest):
     G = rest[-1]
     R0 = R0 if step == 0 else R
+    if step == 0:
+        for comp in range(3):
+            for cell in range(2):
+                add_force(V, (comp, cell), force, (0, comp, cell), PAD + window)
     even, _, _ = place()
     more = step < STEPS - 1
 
     @pl.when(even)
     def _():
-        ahead_bond(V, S, R, R0, coef_ref, force.at[step], surface, msg, None, G, step, window)
+        ahead_bond(V, S, R, R0, coef_ref, force.at[step], surface, msg, None, G, step, window, 1)
         if more:
             pre_ahead(V, S, coef_ref, rest[0], force.at[step + 1], window)
 
     @pl.when(jnp.logical_not(even))
     def _():
-        behind_bond(V, S, R, R0, coef_ref, force.at[step], surface, msg, None, G, step, window)
+        behind_bond(V, S, R, R0, coef_ref, force.at[step], surface, msg, None, G, step, window, 1)
         if more:
             pre_behind(V, S, coef_ref, rest[0], force.at[step + 1], window)
 
 
-def far_kernel(step, window, V0, S0, R0, coef_ref, force, surface, msg, other, *rest):
+def load_ahead(msg, loads, across, rows_out, load):
+    slots = loads.shape[0]
+    rows, entry, cell = (msg[6 * across + i * slots : 6 * across + (i + 1) * slots, :] for i in range(3))
+    for slot in range(slots):
+        rows = jnp.where(entry == float(slot), loads[slot : slot + 1, :], rows)
+    rows_out[...] = jnp.zeros(rows_out.shape, jnp.float32)
+    rows_out[0:1, :] = jnp.sum(jnp.where(cell == 0.0, rows, 0.0), axis=0, keepdims=True)
+    load[...] = rows_out[...].T
+
+
+def far_kernel(step, window, V0, S0, R0, coef_ref, force, surface, msg, *rest):
+    rest = list(rest)
+    extra = [rest.pop(0) for _ in range(2 if step == 0 else 1)]
     V, S, R, D = rest[:4]
-    missing, old_r = (other, R) if step > 0 else (None, other)
-    G, W = rest[-2:]
     early = rest[4] if step < STEPS - 2 else None
+    across = R.shape[2]
     even, _, _ = place()
+    here, then = force.at[step], force.at[step + 1]
+    got = Planes(msg, 3 * step, across) if step < 2 else msg
+    if step == 0:
+        memory, loads = extra
+        missing, old_r = None, memory
+        G, W, A, load, rows_out = rest[-5:]
+    else:
+        missing, old_r = extra[0], R
+        G, W = rest[-2:]
     zero_edges(W)
-    here, then = force.at[step], force.at[step + 1]
 
     @pl.when(even)
     def _():
+        if step == 0:
+            respond = lambda: first_response_ahead(V, S, coef_ref, here, D, W, A, window)
+        else:
+            respond = lambda: response_ahead(V, S, coef_ref, D, W)
         behind_bond(
-            V, S, R, old_r, coef_ref, here, surface, msg, missing, G, step, window,
-            lambda: response_ahead(V, S, coef_ref, D, W),
+            V, S, R, old_r, coef_ref, here, surface, got, missing, G, step, window, 2, respond
         )
         pre_behind(V, S, coef_ref, None, then, window)
 
     @pl.when(jnp.logical_not(even))
     def _():
+        if step == 0:
+            load_ahead(msg, loads, across, rows_out, load)
+            respond = lambda: first_response_behind(V, S, coef_ref, here, load, D, W, A, window)
+        else:
+            respond = lambda: response_behind(V, S, coef_ref, D, W)
         ahead_bond(
-            V, S, R, old_r, coef_ref, here, surface, msg, missing, G, step, window,
-            lambda: response_behind(V, S, coef_ref, D, W),
+            V, S, R, old_r, coef_ref, here, surface, got, missing, G, step, window, 2, respond
         )
         pre_ahead(V, S, coef_ref, None, then, window)
 
@@ -507,8 +643,20 @@
         finish(1, ahead_bond)
 
 
-ENTRY_ROW, TRUCK_ROW = 36, 40
+ENTRY_ROW, TRUCK_ROW = 48, 56
 GROUP = 8
+
+
+def pack_kernel(record, loads, entries, own):
+    panel = record.shape[1]
+    slots, lanes = loads.shape
+    steps = entries.shape[0]
+    own[...] = jnp.zeros(own.shape, jnp.float32)
+    own[:, 0:panel] = record[...]
+    for i in range(slots // 8):
+        own[0:8, panel + i * lanes : panel + (i + 1) * lanes] = loads[8 * i : 8 * i + 8, :]
+    at = panel + slots // 8 * lanes
+    own[0:steps, at : at + slots] = entries[...].astype(jnp.float32)
 
 
 def lane_blocks(table, width):
@@ -522,8 +670,12 @@
     cell_of = cells[...]
     me = lax.axis_index("line")
     group, mine = lax.div(me, tiles), lax.rem(me, tiles)
-    row = lax.broadcasted_iota(jnp.int32, (3 * tiles, cell_of.shape[1]), 0)
-    first = (lax.div(row, 3) + group * tiles) * 2 + lax.rem(row, 3)
+    row = lax.broadcasted_iota(jnp.int32, (4 * tiles, cell_of.shape[1]), 0)
+    tile, j = lax.div(row, 4), lax.rem(row, 4)
+    odd = lax.rem(tile, 2)
+    first = (tile + group * tiles) * 2
+    cell_x = first + jnp.where(j == 2, -1, jnp.where(j == 3, 4 * odd - 2, j))
+    cell_yz = first + jnp.where(j == 3, 4 * odd - 1, j)
     record = jnp.where(group == 0, own[:, :panel], behind[:, :panel])
 
     def share(cell, columns):
@@ -532,8 +684,8 @@
             hit, record[:, columns], precision=lax.Precision.HIGHEST, preferred_element_type=jnp.float32
         )
 
-    part_x = share(first - 1, slice(0, third * lanes))
-    part_yz = share(first, slice(third * lanes, panel))
+    part_x = share(cell_x, slice(0, third * lanes))
+    part_yz = share(cell_yz, slice(third * lanes, panel))
 
     def trucks(source):
         blocks = [source[0:8, panel + i * lanes : panel + (i + 1) * lanes] for i in range(slots // 8 + 1)]
@@ -542,10 +694,10 @@
     own_rows, own_entry = trucks(own)
     far_rows, far_entry = trucks(behind)
     for tile in range(tiles):
-        these = slice(3 * tile, 3 * tile + 3)
+        these = slice(4 * tile, 4 * tile + 4)
         for m in range(pieces):
             part, at = (part_x, m) if m < third else (part_yz, m - third)
-            out[tile, 3 * m : 3 * m + 3, :] = part[these, at * lanes : (at + 1) * lanes]
+            out[tile, 4 * m : 4 * m + 4, :] = part[these, at * lanes : (at + 1) * lanes]
         passed = mine < tile
         out[tile, ENTRY_ROW : ENTRY_ROW + 1, :] = jnp.where(passed, own_entry, far_entry)
         for i in range(slots // 8):
@@ -570,9 +722,10 @@
     slots = loads.shape[0]
     tiles = parts.shape[0]
     mine = lax.rem(lax.axis_index("line"), tiles)
-    table[...] = jnp.zeros(table.shape, jnp.float32)
-    table[0:1, :] = lane_blocks(entries[...], slots)
-    table[STEPS + 1 : STEPS + 2, :] = lane_blocks(cells[...], slots)
+    step_table(table, entries, cells)
+    own_entry, own_cell = lane_blocks(table[0:8, :], slots), lane_blocks(table[8:16, :], slots)
+    table[0:1, :] = own_entry
+    table[STEPS + 1 : STEPS + 2, :] = own_cell
     rows = [loads[...]]
     for k in range(1, STEPS + 1):
         source = lax.rem(mine + (tiles - k), tiles)
@@ -643,18 +796,20 @@
     m_type = pltpu.VMEM((3, across, depth), f32)
     ghost = pltpu.VMEM((2, across, depth), f32)
     work = pltpu.VMEM((2, padded, depth), f32)
-
-    def as_rows(table):
-        return jnp.pad(table.astype(f32), ((0, 8 - STEPS), (0, depth - slots)))
+    square = pltpu.VMEM((across, depth), f32)
 
     def ahead_by(x, distance):
         return lax.ppermute(x, "line", [(i, i + distance) for i in range(tiles - distance)])
 
-    entries, cells = as_rows(truck_entry), as_rows(truck_cell)
     piers, panel = pier_panels.shape[1:]
-    blocks = [truck_loads[at : at + 8] for at in range(0, slots, 8)] + [entries]
-    blocks = [jnp.pad(block, ((0, piers - 8), (0, 0))) for block in blocks]
-    own = jnp.concatenate([pier_panels[0], *blocks], axis=1)
+    own = call(
+        pack_kernel,
+        (pier_panels[0], truck_loads, truck_entry),
+        (WHOLE,) * 3,
+        jax.ShapeDtypeStruct((piers, panel + (slots // 8 + 1) * depth), f32),
+        WHOLE,
+        name="pack",
+    )
     behind = ahead_by(own, GROUP)
     reach = 2 * GROUP
     index = lax.axis_index("line")
@@ -675,12 +830,13 @@
     V, S, coef, msg_near, msg_far = call(
         start_kernel,
         (
-            velocity, stress, layer[None, :], lame_lambda, lame_mu, buoyancy, relax_rate, defect_mu,
-            parts,
+            velocity, stress, memory, layer[None, :], lame_lambda, lame_mu, buoyancy, relax_rate, defect_mu,
+            truck_loads, truck_entry, truck_cell,
         ),
-        (WHOLE,) * 3 + (SCALARS,) * 5 + (ANYWHERE,),
-        (v_type, s_type, c_type, m_type, m_type),
+        (WHOLE,) * 4 + (SCALARS,) * 5 + (WHOLE,) * 3,
+        (v_type, s_type, c_type, m_type, pltpu.VMEM((6 * across + 3 * slots, depth), f32)),
         (WHOLE,) * 5,
+        scratch=(work, pltpu.VMEM((depth, depth), f32)),
         name="start",
     )
     groups = [list(range(at, at + GROUP)) for at in range(0, tiles, GROUP)]
@@ -690,24 +846,13 @@
 
     force, surface = call(
         prepare_kernel,
-        (parts, truck_loads, entries, cells),
+        (parts, truck_loads, truck_entry, truck_cell),
         (WHOLE,) * 4,
-        (pltpu.VMEM((STEPS, 3, 3, 16, depth), f32), pltpu.VMEM((across, depth), f32)),
+        (pltpu.VMEM((STEPS, 3, 4, 16, depth), f32), pltpu.VMEM((across, depth), f32)),
         (WHOLE,) * 2,
         scratch=(pltpu.VMEM((depth, depth), f32), pltpu.VMEM((depth, across), f32)),
         name="prepare",
     )
-    V, early = call(
-        functools.partial(first_kernel, window),
-        tuple(in_vmem(x) for x in (V, S)) + (memory,) + tuple(in_vmem(x) for x in (coef, force, surface)),
-        (WHOLE,) * 6,
-        (v_type, m_type),
-        (WHOLE,) * 2,
-        scratch=(work,),
-        aliases={0: 0},
-        name="first",
-    )
-    early = lax.ppermute(early, "line", far)
     state = (v_type, s_type, r_type)
     same = {0: 0, 1: 1, 2: 2}
     R = missing = None
@@ -730,7 +875,7 @@
         if more:
             msg_near = lax.ppermute(msg[0], "line", near)
         ins = tuple(in_vmem(x) for x in (V, S, R, coef, force, surface, msg_far))
-        ins += (in_vmem(missing) if step else memory,)
+        ins += (in_vmem(missing),) if step else (memory, truck_loads)
         if more:
             outs = state + (m_type,) + ((m_type,) if step < STEPS - 2 else ())
             V, S, R, missing, *msg = call(
@@ -739,11 +884,12 @@
                 (WHOLE,) * len(ins),
                 outs,
                 (WHOLE,) * len(outs),
-                scratch=(ghost, work),
+                scratch=(ghost, work) + (() if step else (pltpu.VMEM((5, padded, depth), f32),) + (square,) * 2),
                 aliases=same,
                 name="far" + str(step),
             )
-            msg_far = early
+            if step > 0:
+                msg_far = early
             if msg:
                 early = lax.ppermute(msg[0], "line", far)
     results = call(

time: 57.9 us -> 65.9 us (1.14)
  waiting for transfers between devices: 9.17 us -> 17.6 us
  starting transfers between devices: 29.7 us -> 26.1 us
  local copies, waits for them, and re-layouts: 2.33 us -> 5.67 us
  other arithmetic: 1.57 us -> 0 us
  Pallas kernels: 13.4 us -> 14.6 us
    ppermute x1, waiting for transfers between devices: 0.26 us -> 7.86 us  [body(): msg_far = lax.ppermute(msg_far, 'line', far)]
    ppermute x1 -> x0, starting transfers between devices: 3.46 us -> none  [body(): early = lax.ppermute(early, 'line', far)]
    unnamed x24 -> x32, local copies, waits for them, and re-layouts: 2.32 us -> 5.67 us
    pallas_call x16, Pallas kernels: 13.4 us -> 14.6 us  [call(): pl.pallas_call(kernel, out_shape=outs, in_specs=specs, out_specs=out_spec...]
    ppermute x1, waiting for transfers between devices: 0.01 us -> 1 us  [body(): msg_near = lax.ppermute(msg_near, 'line', near)]
    concatenate x1 -> x0, other arithmetic: 0.81 us -> none  [body(): own = jnp.concatenate([pier_panels[0], *blocks], axis=1)]
    convert_element_type x2 -> x0, other arithmetic: 0.77 us -> none  [as_rows(): return jnp.pad(table.astype(f32), ((0, 8 - STEPS), (0, depth - slots)))]
  transfers between devices with their start and end apart: 14 -> 13, of which waited for: 4 -> 4; matrix products, arithmetic and copies ran while one was open for 0% -> 0% of each run, Pallas kernels for 19% -> 18%
where the time goes in v4:
time: 65.9 us; the launch traced here: 64.9 us
  starting transfers between devices  26.1 us (40%)
  waiting for transfers between devices  17.6 us (27%)
  Pallas kernels  14.6 us (22%)
  local copies, waits for them, and re-layouts  5.67 us (9%)
  between operations  0.95 us (1%)
    pallas_call x16, Pallas kernels, call(): pl.pallas_call(kernel, out_shape=outs, in_specs=specs, out_specs=out_spec...  14.6 us
    ppermute x4, starting transfers between devices, body(): early = lax.ppermute(msg[0], 'line', far)  14.2 us
    ppermute x1, waiting for transfers between devices, body(): msg_far = lax.ppermute(msg_far, 'line', far)  7.86 us
    all_to_all x1, starting transfers between devices, body(): lax.all_to_all(parts, 'line', 0, 0, axis_index_groups=groups, tiled=True)  6.46 us
    unnamed x32, local copies, waits for them, and re-layouts  5.67 us
    ppermute x1, waiting for transfers between devices, ahead_by(): lax.ppermute(x, 'line', [(i, i + distance) for i in range(tiles - distanc...  4.62 us
    ppermute x4, waiting for transfers between devices, body(): early = lax.ppermute(msg[0], 'line', far)  4.13 us
    ppermute x1, starting transfers between devices, body(): msg_far = lax.ppermute(msg_far, 'line', far)  3.58 us
  transfers between devices with their start and end apart: 13, of which 4 were waited for; matrix products, arithmetic and copies ran while one was open for 0% of the time, Pallas kernels for 18%

profile of v4, /device:TPU:17, one launch (start us, length us, event | category | flops | bytes accessed | tf_op | source)
XLA Modules:
  0.0 64.9 jit_solution(13231430491459968684)
XLA Ops:
  0.6 0.0 copy-start.3
  0.7 0.8 %copy-done.3 = f32[16,128]{1,0:T(8,128)S(1)} copy-done((f32[16,128]{1,0:T(8,128)S(1)}, f32[16,128]{1,0:T(8,128)}, u32[]{:S(2)}) %copy-start.3) | copy-done | bytes 8216
  1.4 0.8 %copy-done.5 = f32[1,8,1536]{2,1,0:T(8,128)S(1)} copy-done((f32[1,8,1536]{2,1,0:T(8,128)S(1)}, f32[1,8,1536]{2,1,0:T(8,128)}, u32[]{:S(2)}) %copy-start.5) | copy-done | bytes 49176
  2.2 0.7 %copy-done.6 = s32[6,16]{1,0:T(8,128)S(1)} copy-done((s32[6,16]{1,0:T(8,128)S(1)}, s32[6,16]{1,0:T(8,128)}, u32[]{:S(2)}) %copy-start.6) | copy-done | bytes 408
  2.9 1.3 %collective-permute-start = (f32[8,1920]{1,0:T(8,128)S(1)}, f32[8,1920]{1,0:T(8,128)S(1)}, u32[]{:S(2)}, u32[]{:S(2)}) collective-permute-start(f32[8,1920]{1,0:T(8,128)S(1)} %pack.1.own), channel_id=1, source_target_pairs={{0,8},{1,9},{2,10},{3,11},{4,12},{5,13},{6,14},{7,15},{16,24},{17,... | collective-permute-start | bytes 184328 | tf_op jit(solution)/shard_map/ppermute | solution.py:802
  4.2 4.6 %collective-permute-done.behind = f32[8,1920]{1,0:T(8,128)S(1)} collective-permute-done((f32[8,1920]{1,0:T(8,128)S(1)}, f32[8,1920]{1,0:T(8,128)S(1)}, u32[]{:S(2)}, u32[]{:S(2)}) %collective-permute-start) | collective-permute-done | bytes 61472 | tf_op jit(solution)/shard_map/ppermute | solution.py:802
  8.8 0.7 %copy-done.9 = s32[8]{0:T(128)S(1)} copy-done((s32[8]{0:T(128)S(1)}, s32[8]{0:T(128)}, u32[]{:S(2)}) %copy-start.9) | copy-done | bytes 56
  9.5 1.0 %split.1 = f32[8,72,128]{2,1,0:T(8,128)} custom-call(f32[8,1920]{1,0:T(8,128)S(1)} %pack.1.own, f32[8,1920]{1,0:T(8,128)S(1)} %collective-permute-done.behind, s32[1,8]{1,0:T(1,128)S(1)} %bitcast.4), custom_call_target="tpu_custom_call" | custom-call | flops 983296 | bytes 245824 | tf_op jit(solution)/shard_map/split/pallas_call | solution.py:764
  10.5 0.0 copy-start.14
  10.5 0.0 copy-start.15
  10.5 6.5 %all-to-all-start = ((f32[8,72,128]{2,1,0:T(8,128)}), f32[8,72,128]{2,1,0:T(8,128)S(1)}, u32[]{:S(2)}, u32[]{:S(2)}) async-start(f32[8,72,128]{2,1,0:T(8,128)} %split.1), calls=%async_computation | async-start | bytes 589824 | tf_op jit(solution)/shard_map/all_to_all | solution.py:843
  17.1 0.6 copy-done.10
  17.6 0.0 copy-done.11
  17.7 0.0 copy-done.12
  17.7 1.1 %copy-done.1 = f32[6,2,128,128]{3,2,1,0:T(8,128)S(1)} copy-done((f32[6,2,128,128]{3,2,1,0:T(8,128)S(1)}, f32[6,2,128,128]{3,2,1,0:T(8,128)}, u32[]{:S(2)}) %copy-start.1) | copy-done | bytes 786456
  18.8 1.0 %copy-done.2 = f32[3,2,128,128]{3,2,1,0:T(8,128)S(1)} copy-done((f32[3,2,128,128]{3,2,1,0:T(8,128)S(1)}, f32[3,2,128,128]{3,2,1,0:T(8,128)}, u32[]{:S(2)}) %copy-start.2) | copy-done | bytes 393240
  19.8 2.4 %start.1 = (f32[3,2,144,128]{3,2,1,0:T(8,128)S(1)}, f32[6,2,144,128]{3,2,1,0:T(8,128)S(1)}, f32[16,128]{1,0:T(8,128)S(1)}, f32[3,128,128]{2,1,0:T(8,128)}, f32[816,128]{1,0:T(8,128)S(1)}) custom-call(f32[3,2,128,128]{3,2,1,0:T(8,128)S(1)} %copy-done.2, f32[6,2,128,128]{3,2,1,0:T(8,128)S(1)} %copy-done.1, f32[6,2,128,128]{3,2,1,0:T(8,128)S(1)} %copy-done, ...), custom_call_target="tpu_custom_call" | custom-call | flops 15805696 | bytes 3951424 | tf_op jit(solution)/shard_map/start/pallas_call | solution.py:764
  22.1 3.6 %collective-permute-start.2 = (f32[816,128]{1,0:T(8,128)S(1)}, f32[816,128]{1,0:T(8,128)S(1)}, u32[]{:S(2)}, u32[]{:S(2)}) collective-permute-start(f32[816,128]{1,0:T(8,128)S(1)} %get-tuple-element.69), channel_id=1, source_target_pairs={{1,2},{3,4},{5,6},{7,8},{9,10},{11,12},{13,14},{2,1},{4,3},{6,5},{... | collective-permute-start | bytes 1253384 | tf_op jit(solution)/shard_map/ppermute | solution.py:844
  25.7 0.1 collective-permute-start.1
  25.8 0.0 all-to-all-done.parts
  25.8 0.6 prepare.1
  26.5 1.0 %collective-permute-done.1.msg = f32[3,128,128]{2,1,0:T(8,128)S(1)} collective-permute-done((f32[3,128,128]{2,1,0:T(8,128)}, f32[3,128,128]{2,1,0:T(8,128)S(1)}, u32[]{:S(2)}, u32[]{:S(2)}) %collective-permute-start.1) | collective-permute-done | bytes 196640 | tf_op jit(solution)/shard_map/ppermute | solution.py:845
  27.5 0.5 near0.1
  27.9 0.2 collective-permute-start.3
  28.1 7.9 %collective-permute-done.2.msg = f32[816,128]{1,0:T(8,128)S(1)} collective-permute-done((f32[816,128]{1,0:T(8,128)S(1)}, f32[816,128]{1,0:T(8,128)S(1)}, u32[]{:S(2)}, u32[]{:S(2)}) %collective-permute-start.2) | collective-permute-done | bytes 417824 | tf_op jit(solution)/shard_map/ppermute | solution.py:844
  36.0 1.5 %far0.1 = (f32[3,2,144,128]{3,2,1,0:T(8,128)S(1)}, f32[6,2,144,128]{3,2,1,0:T(8,128)S(1)}, f32[6,2,128,128]{3,2,1,0:T(8,128)S(1)}, f32[3,128,128]{2,1,0:T(8,128)S(1)}, f32[3,128,128]{2,1,0:T(8,128)S(1)}) custom-call(f32[3,2,144,128]{3,2,1,0:T(8,128)S(1)} %get-tuple-element.66.V0, ...), custom_call_target="tpu_custom_call", output_to_operand_aliasing={{0}: (0, {}), {1}: (1, {}), {2}: (2, {})} | custom-call | flops 31916032 | bytes 7979008 | tf_op jit(solution)/shard_map/far0/pallas_call | solution.py:764
  37.5 0.0 collective-permute-done.3.msg
  37.5 0.5 near1.1
  38.0 0.1 collective-permute-start.4
  38.0 3.5 %collective-permute-start.5 = (f32[3,128,128]{2,1,0:T(8,128)S(1)}, f32[3,128,128]{2,1,0:T(8,128)S(1)}, u32[]{:S(2)}, u32[]{:S(2)}) collective-permute-start(f32[3,128,128]{2,1,0:T(8,128)S(1)} %get-tuple-element.85), channel_id=1, source_target_pairs={{1,2},{3,4},{5,6},{7,8},{9,10},{11,12},{13,14},{2,1},{4,3},{6,5},{... | collective-permute-start | bytes 589832 | tf_op jit(solution)/shard_map/ppermute | solution.py:894
  41.5 1.4 %far1.1 = (f32[3,2,144,128]{3,2,1,0:T(8,128)S(1)}, f32[6,2,144,128]{3,2,1,0:T(8,128)S(1)}, f32[6,2,128,128]{3,2,1,0:T(8,128)S(1)}, f32[3,128,128]{2,1,0:T(8,128)S(1)}, f32[3,128,128]{2,1,0:T(8,128)S(1)}) custom-call(f32[3,2,144,128]{3,2,1,0:T(8,128)S(1)} %get-tuple-element.74.V0, ...), custom_call_target="tpu_custom_call", output_to_operand_aliasing={{0}: (0, {}), {1}: (1, {}), {2}: (2, {})} | custom-call | flops 27131904 | bytes 6782976 | tf_op jit(solution)/shard_map/far1/pallas_call | solution.py:764
  42.9 0.5 near2.1
  43.4 0.1 collective-permute-start.6
  43.5 3.6 %collective-permute-start.7 = (f32[3,128,128]{2,1,0:T(8,128)S(1)}, f32[3,128,128]{2,1,0:T(8,128)S(1)}, u32[]{:S(2)}, u32[]{:S(2)}) collective-permute-start(f32[3,128,128]{2,1,0:T(8,128)S(1)} %get-tuple-element.94), channel_id=1, source_target_pairs={{1,2},{3,4},{5,6},{7,8},{9,10},{11,12},{13,14},{2,1},{4,3},{6,5},{... | collective-permute-start | bytes 589832 | tf_op jit(solution)/shard_map/ppermute | solution.py:894
  47.1 0.0 collective-permute-done.5.msg
  47.1 1.4 %far2.1 = (f32[3,2,144,128]{3,2,1,0:T(8,128)S(1)}, f32[6,2,144,128]{3,2,1,0:T(8,128)S(1)}, f32[6,2,128,128]{3,2,1,0:T(8,128)S(1)}, f32[3,128,128]{2,1,0:T(8,128)S(1)}, f32[3,128,128]{2,1,0:T(8,128)S(1)}) custom-call(f32[3,2,144,128]{3,2,1,0:T(8,128)S(1)} %get-tuple-element.82.V0, ...), custom_call_target="tpu_custom_call", output_to_operand_aliasing={{0}: (0, {}), {1}: (1, {}), {2}: (2, {})} | custom-call | flops 25362432 | bytes 6340608 | tf_op jit(solution)/shard_map/far2/pallas_call | solution.py:764
  48.5 0.5 near3.1
  49.0 0.1 collective-permute-start.8
  49.1 3.5 %collective-permute-start.9 = (f32[3,128,128]{2,1,0:T(8,128)S(1)}, f32[3,128,128]{2,1,0:T(8,128)S(1)}, u32[]{:S(2)}, u32[]{:S(2)}) collective-permute-start(f32[3,128,128]{2,1,0:T(8,128)S(1)} %get-tuple-element.103), channel_id=1, source_target_pairs={{1,2},{3,4},{5,6},{7,8},{9,10},{11,12},{13,14},{2,1},{4,3},{6,5},{... | collective-permute-start | bytes 589832 | tf_op jit(solution)/shard_map/ppermute | solution.py:894
  52.6 1.4 %far3.1 = (f32[3,2,144,128]{3,2,1,0:T(8,128)S(1)}, f32[6,2,144,128]{3,2,1,0:T(8,128)S(1)}, f32[6,2,128,128]{3,2,1,0:T(8,128)S(1)}, f32[3,128,128]{2,1,0:T(8,128)S(1)}, f32[3,128,128]{2,1,0:T(8,128)S(1)}) custom-call(f32[3,2,144,128]{3,2,1,0:T(8,128)S(1)} %get-tuple-element.91.V0, ...), custom_call_target="tpu_custom_call", output_to_operand_aliasing={{0}: (0, {}), {1}: (1, {}), {2}: (2, {})} | custom-call | flops 25362432 | bytes 6340608 | tf_op jit(solution)/shard_map/far3/pallas_call | solution.py:764
  54.0 0.5 near4.1
  54.5 0.1 collective-permute-start.10
  54.5 3.6 %collective-permute-start.11 = (f32[3,128,128]{2,1,0:T(8,128)S(1)}, f32[3,128,128]{2,1,0:T(8,128)S(1)}, u32[]{:S(2)}, u32[]{:S(2)}) collective-permute-start(f32[3,128,128]{2,1,0:T(8,128)S(1)} %get-tuple-element.112), channel_id=1, source_target_pairs={{1,2},{3,4},{5,6},{7,8},{9,10},{11,12},{13,14},{2,1},{4,3},{6,5},{... | collective-permute-start | bytes 589832 | tf_op jit(solution)/shard_map/ppermute | solution.py:894
  58.2 0.0 collective-permute-done.9.msg
  58.2 1.0 %far4.1 = (f32[3,2,144,128]{3,2,1,0:T(8,128)S(1)}, f32[6,2,144,128]{3,2,1,0:T(8,128)S(1)}, f32[6,2,128,128]{3,2,1,0:T(8,128)S(1)}, f32[3,128,128]{2,1,0:T(8,128)S(1)}) custom-call(f32[3,2,144,128]{3,2,1,0:T(8,128)S(1)} %get-tuple-element.100.V0, ...), custom_call_target="tpu_custom_call", output_to_operand_aliasing={{0}: (0, {}), {1}: (1, {}), {2}: (2, {})} | custom-call | flops 25362432 | bytes 6340608 | tf_op jit(solution)/shard_map/far4/pallas_call | solution.py:764
  59.2 0.3 near5.1
  59.5 4.1 %collective-permute-done.11.msg = f32[3,128,128]{2,1,0:T(8,128)S(1)} collective-permute-done((f32[3,128,128]{2,1,0:T(8,128)S(1)}, f32[3,128,128]{2,1,0:T(8,128)S(1)}, u32[]{:S(2)}, u32[]{:S(2)}) %collective-permute-start.11) | collective-permute-done | bytes 196640 | tf_op jit(solution)/shard_map/ppermute | solution.py:894
  63.6 1.3 %last.1 = (f32[3,2,144,128]{3,2,1,0:T(8,128)S(1)}, f32[6,2,144,128]{3,2,1,0:T(8,128)S(1)}, f32[6,2,128,128]{3,2,1,0:T(8,128)S(1)}, f32[3,2,128,128]{3,2,1,0:T(8,...) custom-call(f32[3,2,144,128]{3,2,1,0:T(8,128)S(1)} %get-tuple-elemen, ...), custom_call_target="tpu_custom_call", output_to_operand_aliasing={{0}: (0, {}), {1}: (1, {}), {2}: (2, {})} | custom-call | flops 25362432 | bytes 6340608 | tf_op jit(solution)/shard_map/last/pallas_call | solution.py:764
  (26 shorter events, 0.1 us)
Async XLA Ops:
  0.6 16.4 %copy-start = (f32[6,2,128,128]{3,2,1,0:T(8,128)S(1)}, f32[6,2,128,128]{3,2,1,0:T(8,128)}, u32[]{:S(2)}) copy-start(f32[6,2,128,128]{3,2,1,0:T(8,128)} %rest_0_.1) | copy-start | bytes 2359300
  0.6 0.8 %copy-start.3 = (f32[16,128]{1,0:T(8,128)S(1)}, f32[16,128]{1,0:T(8,128)}, u32[]{:S(2)}) copy-start(f32[16,128]{1,0:T(8,128)} %rest_1_.1) | copy-start | bytes 24580
  1.4 0.8 %copy-start.5 = (f32[1,8,1536]{2,1,0:T(8,128)S(1)}, f32[1,8,1536]{2,1,0:T(8,128)}, u32[]{:S(2)}) copy-start(f32[1,8,1536]{2,1,0:T(8,128)} %param.18) | copy-start | bytes 147460
  2.2 0.7 %copy-start.6 = (s32[6,16]{1,0:T(8,128)S(1)}, s32[6,16]{1,0:T(8,128)}, u32[]{:S(2)}) copy-start(s32[6,16]{1,0:T(8,128)} %entries.5) | copy-start | bytes 1156
  2.9 5.9 %collective-permute-start = (f32[8,1920]{1,0:T(8,128)S(1)}, f32[8,1920]{1,0:T(8,128)S(1)}, u32[]{:S(2)}, u32[]{:S(2)}) collective-permute-start(f32[8,1920]{1,0:T(8,128)S(1)} %pack.1.own), channel_id=1, source_target_pairs={{0,8},{1,9},{2,10},{3,11},{4,12},{5,13},{6,14},{7,15},{16,24},{17,... | collective-permute-start | bytes 184328 | tf_op jit(solution)/shard_map/ppermute | solution.py:802
  8.8 0.7 %copy-start.9 = (s32[8]{0:T(128)S(1)}, s32[8]{0:T(128)}, u32[]{:S(2)}) copy-start(s32[8]{0:T(128)} %param.27) | copy-start | bytes 100
  10.5 6.5 %copy-start.4 = (f32[16,128]{1,0:T(8,128)S(1)}, f32[16,128]{1,0:T(8,128)}, u32[]{:S(2)}) copy-start(f32[16,128]{1,0:T(8,128)} %rest_1_.1) | copy-start | bytes 24580
  10.5 6.5 %copy-start.7 = (s32[6,16]{1,0:T(8,128)S(1)}, s32[6,16]{1,0:T(8,128)}, u32[]{:S(2)}) copy-start(s32[6,16]{1,0:T(8,128)} %entries.5) | copy-start | bytes 1156
  10.5 6.5 %copy-start.8 = (s32[6,16]{1,0:T(8,128)S(1)}, s32[6,16]{1,0:T(8,128)}, u32[]{:S(2)}) copy-start(s32[6,16]{1,0:T(8,128)} %cells.3) | copy-start | bytes 1156
  10.5 6.5 %copy-start.13 = (f32[8]{0:T(128)S(1)}, f32[8]{0:T(128)}, u32[]{:S(2)}) copy-start(f32[8]{0:T(128)} %buoy.1) | copy-start | bytes 100
  10.5 6.5 %copy-start.14 = (f32[8]{0:T(128)S(1)}, f32[8]{0:T(128)}, u32[]{:S(2)}) copy-start(f32[8]{0:T(128)} %rate.1) | copy-start | bytes 100
  10.5 6.5 %copy-start.15 = (f32[8]{0:T(128)S(1)}, f32[8]{0:T(128)}, u32[]{:S(2)}) copy-start(f32[8]{0:T(128)} %defect.1) | copy-start | bytes 100
  10.5 15.3 %all-to-all-start = ((f32[8,72,128]{2,1,0:T(8,128)}), f32[8,72,128]{2,1,0:T(8,128)S(1)}, u32[]{:S(2)}, u32[]{:S(2)}) async-start(f32[8,72,128]{2,1,0:T(8,128)} %split.1), calls=%async_computation | async-start | bytes 589824 | tf_op jit(solution)/shard_map/all_to_all | solution.py:843
  17.0 0.7 %copy-start.10 = (s32[128]{0:T(128)S(1)}, s32[128]{0:T(128)}, u32[]{:S(2)}) copy-start(s32[128]{0:T(128)} %param.24) | copy-start | bytes 1540
  17.0 0.7 %copy-start.11 = (f32[8]{0:T(128)S(1)}, f32[8]{0:T(128)}, u32[]{:S(2)}) copy-start(f32[8]{0:T(128)} %lam.1) | copy-start | bytes 100
  17.0 0.7 %copy-start.12 = (f32[8]{0:T(128)S(1)}, f32[8]{0:T(128)}, u32[]{:S(2)}) copy-start(f32[8]{0:T(128)} %mu.1) | copy-start | bytes 100
  17.7 1.1 %copy-start.1 = (f32[6,2,128,128]{3,2,1,0:T(8,128)S(1)}, f32[6,2,128,128]{3,2,1,0:T(8,128)}, u32[]{:S(2)}) copy-start(f32[6,2,128,128]{3,2,1,0:T(8,128)} %stress.1) | copy-start | bytes 2359300
  18.8 1.0 %copy-start.2 = (f32[3,2,128,128]{3,2,1,0:T(8,128)S(1)}, f32[3,2,128,128]{3,2,1,0:T(8,128)}, u32[]{:S(2)}) copy-start(f32[3,2,128,128]{3,2,1,0:T(8,128)} %velocity.1) | copy-start | bytes 1179652
  22.1 13.8 %collective-permute-start.2 = (f32[816,128]{1,0:T(8,128)S(1)}, f32[816,128]{1,0:T(8,128)S(1)}, u32[]{:S(2)}, u32[]{:S(2)}) collective-permute-start(f32[816,128]{1,0:T(8,128)S(1)} %get-tuple-element.69), channel_id=1, source_target_pairs={{1,2},{3,4},{5,6},{7,8},{9,10},{11,12},{13,14},{2,1},{4,3},{6,5},{... | collective-permute-start | bytes 1253384 | tf_op jit(solution)/shard_map/ppermute | solution.py:844
  25.7 1.7 %collective-permute-start.1 = (f32[3,128,128]{2,1,0:T(8,128)}, f32[3,128,128]{2,1,0:T(8,128)S(1)}, u32[]{:S(2)}, u32[]{:S(2)}) collective-permute-start(f32[3,128,128]{2,1,0:T(8,128)} %get-tuple-element.65), channel_id=1, source_target_pairs={{0,1},{1,0},{2,3},{3,2},{4,5},{5,4},{6,7},{7,6},{8,9},{9,8},{10,11... | collective-permute-start | bytes 589832 | tf_op jit(solution)/shard_map/ppermute | solution.py:845
  27.9 9.5 %collective-permute-start.3 = (f32[3,128,128]{2,1,0:T(8,128)S(1)}, f32[3,128,128]{2,1,0:T(8,128)S(1)}, u32[]{:S(2)}, u32[]{:S(2)}) collective-permute-start(f32[3,128,128]{2,1,0:T(8,128)S(1)} %get-tuple-element.73), channel_id=1, source_target_pairs={{0,1},{1,0},{2,3},{3,2},{4,5},{5,4},{6,7},{7,6},{8,9},{9,8},{10,11... | collective-permute-start | bytes 589832 | tf_op jit(solution)/shard_map/ppermute | solution.py:876
  38.0 4.9 %collective-permute-start.4 = (f32[3,128,128]{2,1,0:T(8,128)S(1)}, f32[3,128,128]{2,1,0:T(8,128)S(1)}, u32[]{:S(2)}, u32[]{:S(2)}) collective-permute-start(f32[3,128,128]{2,1,0:T(8,128)S(1)} %get-tuple-element.81), channel_id=1, source_target_pairs={{0,1},{1,0},{2,3},{3,2},{4,5},{5,4},{6,7},{7,6},{8,9},{9,8},{10,11... | collective-permute-start | bytes 589832 | tf_op jit(solution)/shard_map/ppermute | solution.py:876
  38.0 9.1 %collective-permute-start.5 = (f32[3,128,128]{2,1,0:T(8,128)S(1)}, f32[3,128,128]{2,1,0:T(8,128)S(1)}, u32[]{:S(2)}, u32[]{:S(2)}) collective-permute-start(f32[3,128,128]{2,1,0:T(8,128)S(1)} %get-tuple-element.85), channel_id=1, source_target_pairs={{1,2},{3,4},{5,6},{7,8},{9,10},{11,12},{13,14},{2,1},{4,3},{6,5},{... | collective-permute-start | bytes 589832 | tf_op jit(solution)/shard_map/ppermute | solution.py:894
  43.4 5.1 %collective-permute-start.6 = (f32[3,128,128]{2,1,0:T(8,128)S(1)}, f32[3,128,128]{2,1,0:T(8,128)S(1)}, u32[]{:S(2)}, u32[]{:S(2)}) collective-permute-start(f32[3,128,128]{2,1,0:T(8,128)S(1)} %get-tuple-element.90), channel_id=1, source_target_pairs={{0,1},{1,0},{2,3},{3,2},{4,5},{5,4},{6,7},{7,6},{8,9},{9,8},{10,11... | collective-permute-start | bytes 589832 | tf_op jit(solution)/shard_map/ppermute | solution.py:876
  43.5 9.1 %collective-permute-start.7 = (f32[3,128,128]{2,1,0:T(8,128)S(1)}, f32[3,128,128]{2,1,0:T(8,128)S(1)}, u32[]{:S(2)}, u32[]{:S(2)}) collective-permute-start(f32[3,128,128]{2,1,0:T(8,128)S(1)} %get-tuple-element.94), channel_id=1, source_target_pairs={{1,2},{3,4},{5,6},{7,8},{9,10},{11,12},{13,14},{2,1},{4,3},{6,5},{... | collective-permute-start | bytes 589832 | tf_op jit(solution)/shard_map/ppermute | solution.py:894
  49.0 5.0 %collective-permute-start.8 = (f32[3,128,128]{2,1,0:T(8,128)S(1)}, f32[3,128,128]{2,1,0:T(8,128)S(1)}, u32[]{:S(2)}, u32[]{:S(2)}) collective-permute-start(f32[3,128,128]{2,1,0:T(8,128)S(1)} %get-tuple-element.99), channel_id=1, source_target_pairs={{0,1},{1,0},{2,3},{3,2},{4,5},{5,4},{6,7},{7,6},{8,9},{9,8},{10,11... | collective-permute-start | bytes 589832 | tf_op jit(solution)/shard_map/ppermute | solution.py:876
  49.1 9.1 %collective-permute-start.9 = (f32[3,128,128]{2,1,0:T(8,128)S(1)}, f32[3,128,128]{2,1,0:T(8,128)S(1)}, u32[]{:S(2)}, u32[]{:S(2)}) collective-permute-start(f32[3,128,128]{2,1,0:T(8,128)S(1)} %get-tuple-element.103), channel_id=1, source_target_pairs={{1,2},{3,4},{5,6},{7,8},{9,10},{11,12},{13,14},{2,1},{4,3},{6,5},{... | collective-permute-start | bytes 589832 | tf_op jit(solution)/shard_map/ppermute | solution.py:894
  54.5 4.8 %collective-permute-start.10 = (f32[3,128,128]{2,1,0:T(8,128)S(1)}, f32[3,128,128]{2,1,0:T(8,128)S(1)}, u32[]{:S(2)}, u32[]{:S(2)}) collective-permute-start(f32[3,128,128]{2,1,0:T(8,128)S(1)} %get-tuple-element.108), channel_id=1, source_target_pairs={{0,1},{1,0},{2,3},{3,2},{4,5},{5,4},{6,7},{7,6},{8,9},{9,8},{10,11... | collective-permute-start | bytes 589832 | tf_op jit(solution)/shard_map/ppermute | solution.py:876
  54.5 9.1 %collective-permute-start.11 = (f32[3,128,128]{2,1,0:T(8,128)S(1)}, f32[3,128,128]{2,1,0:T(8,128)S(1)}, u32[]{:S(2)}, u32[]{:S(2)}) collective-permute-start(f32[3,128,128]{2,1,0:T(8,128)S(1)} %get-tuple-element.112), channel_id=1, source_target_pairs={{1,2},{3,4},{5,6},{7,8},{9,10},{11,12},{13,14},{2,1},{4,3},{6,5},{... | collective-permute-start | bytes 589832 | tf_op jit(solution)/shard_map/ppermute | solution.py:894

commit v5 on v4

--- a/solution.py
+++ b/solution.py
@@ -159,7 +159,7 @@
         add_force(V, (VZ, 1), force, (VZ, 1), PAD + window)
 
 
-def post(V, S, R, old_r, coef_ref, surface, cell, column, behind_x, ahead_y, ahead_z):
+def post(V, S, R, coef_ref, surface, cell, column, behind_x, ahead_y, ahead_z):
     m0, m1, lam, mu2, mu, k1, k2, k2h, l0 = coefs(
         coef_ref, (C_M0, C_M1, C_LAM, C_MU2, C_MU, C_K1, C_K2, C_K2H, C_L0)
     )
@@ -175,14 +175,14 @@
         eyz = m1 * after(vy) - vy + (V[VZ, cell, down] - vz)
         volume = lam * (exx + eyy + ezz)
         for comp, e in ((XX, exx), (YY, eyy), (ZZ, ezz)):
-            old = old_r[comp, cell, out]
+            old = R[comp, cell, out]
             new = S[comp, cell, here] + (volume + mu2 * e) + DT * old
             if comp == ZZ:
                 new = new + l0 * lane_roll(surface[out, :], -column)
             S[comp, cell, here] = new
             R[comp, cell, out] = k1 * old - k2 * e
         for comp, e in ((XY, exy), (XZ, exz), (YZ, eyz)):
-            old = old_r[comp, cell, out]
+            old = R[comp, cell, out]
             S[comp, cell, here] = S[comp, cell, here] + mu * e + DT * old
             R[comp, cell, out] = k1 * old - k2h * e
 
@@ -381,7 +381,7 @@
         add_force(msg, (2,), force, (VZ, 0), window)
 
 
-def ahead_bond(V, S, R, old_r, coef_ref, force, surface, msg, missing, G, step, window, unforced=0, respond=None):
+def ahead_bond(V, S, R, coef_ref, force, surface, msg, missing, G, step, window, unforced=0, respond=None):
     (b,) = coefs(coef_ref, (C_B,))
     _, _, has_ahead = place()
     keep = jnp.where(has_ahead, 1.0, 0.0).astype(jnp.float32)
@@ -402,14 +402,14 @@
     if respond is not None:
         respond()
     post(
-        V, S, R, old_r, coef_ref, surface, 1, 2 * step + 1,
+        V, S, R, coef_ref, surface, 1, 2 * step + 1,
         lambda r: V[VX, 0, pl.ds(PAD + r, ROWS)],
         lambda r: G[0, pl.ds(r, ROWS)],
         lambda r: G[1, pl.ds(r, ROWS)],
     )
 
 
-def behind_bond(V, S, R, old_r, coef_ref, force, surface, msg, missing, G, step, window, unforced=0, respond=None):
+def behind_bond(V, S, R, coef_ref, force, surface, msg, missing, G, step, window, unforced=0, respond=None):
     (b,) = coefs(coef_ref, (C_B,))
     _, has_behind, _ = place()
     keep = jnp.where(has_behind, 1.0, 0.0).astype(jnp.float32)
@@ -429,30 +429,34 @@
     if respond is not None:
         respond()
     post(
-        V, S, R, old_r, coef_ref, surface, 0, 2 * step,
+        V, S, R, coef_ref, surface, 0, 2 * step,
         lambda r: G[0, pl.ds(r, ROWS)],
         lambda r: V[VY, 1, pl.ds(PAD + r, ROWS)],
         lambda r: V[VZ, 1, pl.ds(PAD + r, ROWS)],
     )
 
 
-def step_table(table, entries, cells):
-    table[...] = jnp.zeros(table.shape, jnp.float32)
-    steps, slots = entries.shape
-    table[0:steps, 0:slots] = entries[...].astype(jnp.float32)
-    table[8 : 8 + steps, 0:slots] = cells[...].astype(jnp.float32)
-
-
 def start_kernel(
-    velocity, stress, memory, layer_ref, lam, mu, buoy, rate, defect, loads, entries, cells,
-    V, S, coef_ref, msg_near, msg_far, W, table,
+    velocity, stress, memory, layer_in, lam_in, mu_in, buoy_in, rate_in, defect_in, loads, steps_table,
+    V, S, R, coef_ref, msg_near, msg_far, W, table, layer_ref, lam, mu, buoy, rate, defect, sems,
 ):
     across = velocity.shape[2]
+    inside = pl.ds(PAD, across)
+    pairs = [
+        (layer_in, layer_ref), (lam_in, lam), (mu_in, mu), (buoy_in, buoy), (rate_in, rate), (defect_in, defect),
+    ]
+    pairs += [(stress.at[i], S.at[i, :, inside]) for i in range(6)]
+    pairs += [(velocity.at[i], V.at[i, :, inside]) for i in range(3)]
+    pairs += [(memory.at[i], R.at[i]) for i in range(6)]
+    copies = [pltpu.make_async_copy(*pair, sems.at[i]) for i, pair in enumerate(pairs)]
+    for copy in copies:
+        copy.start()
     slots = loads.shape[0]
     zero_edges(V)
     zero_edges(S)
     zero_edges(W)
-    step_table(table, entries, cells)
+    table[...] = jnp.zeros(table.shape, jnp.float32)
+    table[0:16, :] = steps_table[...]
     columns = table[...].T
     trucks = 6 * across
     msg_far[trucks : trucks + slots, :] = loads[...]
@@ -460,14 +464,8 @@
         first_row = trucks + (1 + i) * slots
         column = columns[0:slots, at : at + 1]
         msg_far[first_row : first_row + slots, :] = jnp.broadcast_to(column, loads.shape)
-
-    def load(r):
-        here, _, _, out = spans(r)
-        for ref, source in ((V, velocity), (S, stress)):
-            for where in np.ndindex(*source.shape[:2]):
-                ref[(*where, here)] = source[(*where, out)]
-
-    over_rows(velocity.shape[2], load)
+    for copy in copies[:6]:
+        copy.wait()
     layer = layer_ref[...]
 
     def per_depth(table):
@@ -499,6 +497,8 @@
     ):
         coef_ref[row : row + 1, :] = value
     coef_ref[12:16, :] = jnp.zeros((4, layer.shape[1]), jnp.float32)
+    for copy in copies[6:15]:
+        copy.wait()
     even, _, _ = place()
     now, then = Planes(msg_far, 0, across), Planes(msg_far, 3, across)
 
@@ -513,19 +513,20 @@
         pre_ahead(V, S, coef_ref, now, None, 0)
 
     inner(V, S, coef_ref, None, 0)
+    for copy in copies[15:]:
+        copy.wait()
 
     @pl.when(even)
     def _():
-        early_behind(V, S, memory, coef_ref, None, 0, then, W, None, 0)
+        early_behind(V, S, R, coef_ref, None, 0, then, W, None, 0)
 
     @pl.when(jnp.logical_not(even))
     def _():
-        early_ahead(V, S, memory, coef_ref, then, W, None, 0)
+        early_ahead(V, S, R, coef_ref, then, W, None, 0)
 
 
 def near_kernel(step, window, V0, S0, R0, coef_ref, force, surface, msg, V, S, R, *rest):
     G = rest[-1]
-    R0 = R0 if step == 0 else R
     if step == 0:
         for comp in range(3):
             for cell in range(2):
@@ -535,13 +536,13 @@
 
     @pl.when(even)
     def _():
-        ahead_bond(V, S, R, R0, coef_ref, force.at[step], surface, msg, None, G, step, window, 1)
+        ahead_bond(V, S, R, coef_ref, force.at[step], surface, msg, None, G, step, window, 1)
         if more:
             pre_ahead(V, S, coef_ref, rest[0], force.at[step + 1], window)
 
     @pl.when(jnp.logical_not(even))
     def _():
-        behind_bond(V, S, R, R0, coef_ref, force.at[step], surface, msg, None, G, step, window, 1)
+        behind_bond(V, S, R, coef_ref, force.at[step], surface, msg, None, G, step, window, 1)
         if more:
             pre_behind(V, S, coef_ref, rest[0], force.at[step + 1], window)
 
@@ -558,7 +559,7 @@
 
 def far_kernel(step, window, V0, S0, R0, coef_ref, force, surface, msg, *rest):
     rest = list(rest)
-    extra = [rest.pop(0) for _ in range(2 if step == 0 else 1)]
+    other = rest.pop(0)
     V, S, R, D = rest[:4]
     early = rest[4] if step < STEPS - 2 else None
     across = R.shape[2]
@@ -566,11 +567,10 @@
     here, then = force.at[step], force.at[step + 1]
     got = Planes(msg, 3 * step, across) if step < 2 else msg
     if step == 0:
-        memory, loads = extra
-        missing, old_r = None, memory
+        missing, loads = None, other
         G, W, A, load, rows_out = rest[-5:]
     else:
-        missing, old_r = extra[0], R
+        missing = other
         G, W = rest[-2:]
     zero_edges(W)
 
@@ -581,7 +581,7 @@
         else:
             respond = lambda: response_ahead(V, S, coef_ref, D, W)
         behind_bond(
-            V, S, R, old_r, coef_ref, here, surface, got, missing, G, step, window, 2, respond
+            V, S, R, coef_ref, here, surface, got, missing, G, step, window, 2, respond
         )
         pre_behind(V, S, coef_ref, None, then, window)
 
@@ -593,7 +593,7 @@
         else:
             respond = lambda: response_behind(V, S, coef_ref, D, W)
         ahead_bond(
-            V, S, R, old_r, coef_ref, here, surface, got, missing, G, step, window, 2, respond
+            V, S, R, coef_ref, here, surface, got, missing, G, step, window, 2, respond
         )
         pre_ahead(V, S, coef_ref, None, then, window)
 
@@ -628,7 +628,7 @@
         done, other = copies(1 - cell), copies(cell)
         for copy in done:
             copy.start()
-        bond(V, S, R, R, coef_ref, here, surface, msg, missing, G, step, window)
+        bond(V, S, R, coef_ref, here, surface, msg, missing, G, step, window)
         for copy in other:
             copy.start()
         for copy in done + other:
@@ -647,23 +647,34 @@
 GROUP = 8
 
 
-def pack_kernel(record, loads, entries, own):
+def pack_kernel(
+    record, loads_in, entries_in, cells_in, piers_in, own, loads, steps_table, piers, entries, cells, sems
+):
     panel = record.shape[1]
     slots, lanes = loads.shape
     steps = entries.shape[0]
-    own[...] = jnp.zeros(own.shape, jnp.float32)
-    own[:, 0:panel] = record[...]
-    for i in range(slots // 8):
-        own[0:8, panel + i * lanes : panel + (i + 1) * lanes] = loads[8 * i : 8 * i + 8, :]
-    at = panel + slots // 8 * lanes
-    own[0:steps, at : at + slots] = entries[...].astype(jnp.float32)
+    pairs = [(record, own.at[:, pl.ds(0, panel)]), (loads_in, loads), (entries_in, entries), (cells_in, cells)]
+    pairs.append((piers_in, piers))
+    copies = [pltpu.make_async_copy(*pair, sems.at[i]) for i, pair in enumerate(pairs)]
+    for copy in copies:
+        copy.start()
+    own[:, panel:] = jnp.zeros((own.shape[0], own.shape[1] - panel), jnp.float32)
+    steps_table[...] = jnp.zeros(steps_table.shape, jnp.float32)
+    for copy in copies:
+        copy.wait()
+    steps_table[0:steps, 0:slots] = entries[...].astype(jnp.float32)
+    steps_table[8 : 8 + steps, 0:slots] = cells[...].astype(jnp.float32)
+    blocks = [loads[8 * i : 8 * i + 8, :] for i in range(slots // 8)] + [steps_table[0:8, :]]
+    for i, block in enumerate(blocks):
+        own[0:8, panel + i * lanes : panel + (i + 1) * lanes] = block
 
 
 def lane_blocks(table, width):
     return sum(lane_roll(table[s : s + 1, :], s * width) for s in range(STEPS))
 
 
-def split_kernel(panel, slots, own, behind, cells, out):
+def split_kernel(panel, slots, own, behind, cells, after_this, out):
+    del after_this
     tiles, _, lanes = out.shape
     pieces = panel // lanes
     third = pieces // 3
@@ -705,7 +716,7 @@
             out[tile, at : at + 8, :] = jnp.where(passed, own_rows[i], far_rows[i])
 
 
-def prepare_kernel(parts, loads, entries, cells, force, surface, table, rows_out):
+def prepare_kernel(parts, loads, steps_table, force, surface, table, rows_out):
     steps, comps, width = force.shape[:3]
     lanes = parts.shape[2]
     force[...] = jnp.zeros(force.shape, jnp.float32)
@@ -722,10 +733,9 @@
     slots = loads.shape[0]
     tiles = parts.shape[0]
     mine = lax.rem(lax.axis_index("line"), tiles)
-    step_table(table, entries, cells)
-    own_entry, own_cell = lane_blocks(table[0:8, :], slots), lane_blocks(table[8:16, :], slots)
-    table[0:1, :] = own_entry
-    table[STEPS + 1 : STEPS + 2, :] = own_cell
+    table[...] = jnp.zeros(table.shape, jnp.float32)
+    table[0:1, :] = lane_blocks(steps_table[0:8, :], slots)
+    table[STEPS + 1 : STEPS + 2, :] = lane_blocks(steps_table[8:16, :], slots)
     rows = [loads[...]]
     for k in range(1, STEPS + 1):
         source = lax.rem(mine + (tiles - k), tiles)
@@ -760,7 +770,6 @@
 
 
 def call(kernel, ins, specs, outs, out_specs, scratch=(), aliases=None, name=None):
-    size = sum(x.size * 4 for x in ins)
     return pl.pallas_call(
         kernel,
         out_shape=outs,
@@ -769,7 +778,6 @@
         scratch_shapes=list(scratch),
         input_output_aliases=aliases or {},
         compiler_params=pltpu.CompilerParams(vmem_limit_bytes=VMEM_LIMIT),
-        cost_estimate=pl.CostEstimate(flops=8 * size, bytes_accessed=2 * size, transcendentals=0),
         name=name,
     )(*ins)
 
@@ -801,13 +809,23 @@
     def ahead_by(x, distance):
         return lax.ppermute(x, "line", [(i, i + distance) for i in range(tiles - distance)])
 
+    def in_hbm(*arrays):
+        return tuple(pltpu.with_memory_space_constraint(x, pltpu.HBM) for x in arrays)
+
+    dma = pltpu.SemaphoreType.DMA
     piers, panel = pier_panels.shape[1:]
-    own = call(
+    own, loads, steps_table, pier_row = call(
         pack_kernel,
-        (pier_panels[0], truck_loads, truck_entry),
-        (WHOLE,) * 3,
-        jax.ShapeDtypeStruct((piers, panel + (slots // 8 + 1) * depth), f32),
-        WHOLE,
+        in_hbm(pier_panels[0], truck_loads, truck_entry, truck_cell, pier_cell[None, :]),
+        (ANYWHERE,) * 5,
+        (
+            pltpu.VMEM((piers, panel + (slots // 8 + 1) * depth), f32),
+            pltpu.VMEM((slots, depth), f32),
+            pltpu.VMEM((16, depth), f32),
+            pltpu.VMEM((1, piers), jnp.int32),
+        ),
+        (WHOLE,) * 4,
+        scratch=(pltpu.VMEM(truck_entry.shape, jnp.int32), pltpu.VMEM(truck_cell.shape, jnp.int32), dma((5,))),
         name="pack",
     )
     behind = ahead_by(own, GROUP)
@@ -818,36 +836,35 @@
         record = jnp.where(index < reach, record, ahead_by(record, reach))
         behind = jnp.concatenate([record, behind[:, panel:]], axis=1)
         reach *= 2
+    tables = (lame_lambda, lame_mu, buoyancy, relax_rate, defect_mu)
+    V, S, R, coef, msg_near, msg_far = call(
+        start_kernel,
+        in_hbm(velocity, stress, memory, layer[None, :], *tables) + (in_vmem(loads), in_vmem(steps_table)),
+        (ANYWHERE,) * 9 + (WHOLE,) * 2,
+        (v_type, s_type, r_type, c_type, m_type, pltpu.VMEM((6 * across + 3 * slots, depth), f32)),
+        (WHOLE,) * 6,
+        scratch=(
+            work, pltpu.VMEM((depth, depth), f32), pltpu.VMEM((1, depth), jnp.int32),
+            *(pltpu.SMEM(table.shape, f32) for table in tables), dma((21,)),
+        ),
+        name="start",
+    )
+    msg_far = lax.ppermute(msg_far, "line", far)
+    msg_near = lax.ppermute(msg_near, "line", near)
     parts = call(
         functools.partial(split_kernel, panel, slots),
-        (own, behind, pier_cell[None, :]),
-        (WHOLE,) * 3,
+        (own, behind, in_vmem(pier_row), msg_near),
+        (WHOLE,) * 3 + (ANYWHERE,),
         jax.ShapeDtypeStruct((GROUP, TRUCK_ROW + slots, depth), f32),
         WHOLE,
         name="split",
     )
-
-    V, S, coef, msg_near, msg_far = call(
-        start_kernel,
-        (
-            velocity, stress, memory, layer[None, :], lame_lambda, lame_mu, buoyancy, relax_rate, defect_mu,
-            truck_loads, truck_entry, truck_cell,
-        ),
-        (WHOLE,) * 4 + (SCALARS,) * 5 + (WHOLE,) * 3,
-        (v_type, s_type, c_type, m_type, pltpu.VMEM((6 * across + 3 * slots, depth), f32)),
-        (WHOLE,) * 5,
-        scratch=(work, pltpu.VMEM((depth, depth), f32)),
-        name="start",
-    )
     groups = [list(range(at, at + GROUP)) for at in range(0, tiles, GROUP)]
     parts = lax.all_to_all(parts, "line", 0, 0, axis_index_groups=groups, tiled=True)
-    msg_far = lax.ppermute(msg_far, "line", far)
-    msg_near = lax.ppermute(msg_near, "line", near)
-
     force, surface = call(
         prepare_kernel,
-        (parts, truck_loads, truck_entry, truck_cell),
-        (WHOLE,) * 4,
+        (parts, in_vmem(loads), in_vmem(steps_table)),
+        (WHOLE,) * 3,
         (pltpu.VMEM((STEPS, 3, 4, 16, depth), f32), pltpu.VMEM((across, depth), f32)),
         (WHOLE,) * 2,
         scratch=(pltpu.VMEM((depth, depth), f32), pltpu.VMEM((depth, across), f32)),
@@ -855,12 +872,10 @@
     )
     state = (v_type, s_type, r_type)
     same = {0: 0, 1: 1, 2: 2}
-    R = missing = None
+    missing = None
     for step in range(STEPS):
         more = step < STEPS - 1
-        ins = [in_vmem(x) for x in (V, S, R if step else memory, coef, force, surface, msg_near)]
-        if step == 0:
-            ins[2] = memory
+        ins = tuple(in_vmem(x) for x in (V, S, R, coef, force, surface, msg_near))
         outs = state + ((m_type,) if more else ())
         V, S, R, *msg = call(
             functools.partial(near_kernel, step, window),
@@ -869,13 +884,13 @@
             outs,
             (WHOLE,) * len(outs),
             scratch=(ghost,),
-            aliases=same if step else {0: 0, 1: 1},
+            aliases=same,
             name="near" + str(step),
         )
         if more:
             msg_near = lax.ppermute(msg[0], "line", near)
-        ins = tuple(in_vmem(x) for x in (V, S, R, coef, force, surface, msg_far))
-        ins += (in_vmem(missing),) if step else (memory, truck_loads)
+        ins = (V, S, R, coef, force, surface, msg_far, missing if step else loads)
+        ins = tuple(in_vmem(x) for x in ins)
         if more:
             outs = state + (m_type,) + ((m_type,) if step < STEPS - 2 else ())
             V, S, R, missing, *msg = call(

time: 65.9 us -> 61.7 us (0.936)
  local copies, waits for them, and re-layouts: 5.67 us -> 0 us
  starting transfers between devices: 26.1 us -> 30.2 us
  waiting for transfers between devices: 17.6 us -> 14.9 us
  Pallas kernels: 14.6 us -> 15.3 us
    unnamed x32 -> x0, local copies, waits for them, and re-layouts: 5.67 us -> none
    ppermute x1, waiting for transfers between devices: 7.86 us -> 2.64 us  [body(): msg_far = lax.ppermute(msg_far, 'line', far)]
    ppermute x5, starting transfers between devices: 0.48 us -> 5.57 us  [body(): msg_near = lax.ppermute(msg[0], 'line', near)]
    all_to_all x1, waiting for transfers between devices: 0.01 us -> 2.09 us  [body(): lax.all_to_all(parts, 'line', 0, 0, axis_index_groups=groups, tiled=True)]
    ppermute x4, starting transfers between devices: 14.2 us -> 13.2 us  [body(): early = lax.ppermute(msg[0], 'line', far)]
    ppermute x1, waiting for transfers between devices: 1 us -> 0.01 us  [body(): msg_near = lax.ppermute(msg_near, 'line', near)]
    ppermute x4, waiting for transfers between devices: 4.13 us -> 5.06 us  [body(): early = lax.ppermute(msg[0], 'line', far)]
    ppermute x1, starting transfers between devices: 0.07 us -> 0.8 us  [body(): msg_near = lax.ppermute(msg_near, 'line', near)]
  transfers between devices with their start and end apart: 13 -> 13, of which waited for: 4 -> 7; matrix products, arithmetic and copies ran while one was open for 0% -> 0% of each run, Pallas kernels for 18% -> 15%
where the time goes in v5:
time: 61.7 us; the launch traced here: 61.3 us
  starting transfers between devices  30.2 us (49%)
  Pallas kernels  15.3 us (25%)
  waiting for transfers between devices  14.9 us (24%)
  between operations  0.82 us (1%)
    pallas_call x16, Pallas kernels, call(): pl.pallas_call(kernel, out_shape=outs, in_specs=specs, out_specs=out_spec...  15.3 us
    ppermute x4, starting transfers between devices, body(): early = lax.ppermute(msg[0], 'line', far)  13.2 us
    all_to_all x1, starting transfers between devices, body(): lax.all_to_all(parts, 'line', 0, 0, axis_index_groups=groups, tiled=True)  5.83 us
    ppermute x5, starting transfers between devices, body(): msg_near = lax.ppermute(msg[0], 'line', near)  5.57 us
    ppermute x1, waiting for transfers between devices, ahead_by(): lax.ppermute(x, 'line', [(i, i + distance) for i in range(tiles - distanc...  5.11 us
    ppermute x4, waiting for transfers between devices, body(): early = lax.ppermute(msg[0], 'line', far)  5.06 us
    ppermute x1, starting transfers between devices, body(): msg_far = lax.ppermute(msg_far, 'line', far)  3.53 us
    ppermute x1, waiting for transfers between devices, body(): msg_far = lax.ppermute(msg_far, 'line', far)  2.64 us
  transfers between devices with their start and end apart: 13, of which 7 were waited for; matrix products, arithmetic and copies ran while one was open for 0% of the time, Pallas kernels for 15%

profile of v5, /device:TPU:17, one launch (start us, length us, event | category | flops | bytes accessed | tf_op | source)
XLA Modules:
  0.0 61.3 jit_solution(6541228930782613963)
XLA Ops:
  0.6 0.9 %pack.1 = (f32[8,1920]{1,0:T(8,128)S(1)}, f32[16,128]{1,0:T(8,128)S(1)}, f32[16,128]{1,0:T(8,128)S(1)}, s32[1,8]{1,0:T(1,128)S(1)}) custom-call(f32[8,1536]{1,0:T(8,128)} %bitcast.3, f32[16,128]{1,0:T(8,128)} %loads_in.1, s32[6,16]{1,0:T(8,128)} %entries_in.1, s32[6,16]{1,0:T(8,128)} %cells_in.1, s32[1,8]{1,0:T(1,128)} %bitcast.4), custom_call_target="tpu_custom_call" | custom-call | tf_op jit(solution)/shard_map/pack/pallas_call | solution.py:773
  1.5 2.4 %start.1 = (f32[3,2,144,128]{3,2,1,0:T(8,128)S(1)}, f32[6,2,144,128]{3,2,1,0:T(8,128)S(1)}, f32[6,2,128,128]{3,2,1,0:T(8,128)S(1)}, f32[16,128]{1,0:T(8,128)S(1)...) custom-call(f32[3,2,128,128]{3,2,1,0:T(8,128)} %velocity.1, f32[6,2,128,128]{3,2,1,0:T(8,128)} %stress.1, ...), custom_call_target="tpu_custom_call" | custom-call | tf_op jit(solution)/shard_map/start/pallas_call | solution.py:773
  3.9 0.8 %collective-permute-start.1 = (f32[3,128,128]{2,1,0:T(8,128)S(1)}, f32[3,128,128]{2,1,0:T(8,128)S(1)}, u32[]{:S(2)}, u32[]{:S(2)}) collective-permute-start(f32[3,128,128]{2,1,0:T(8,128)S(1)} %get-tuple-element.73), channel_id=1, source_target_pairs={{0,1},{1,0},{2,3},{3,2},{4,5},{5,4},{6,7},{7,6},{8,9},{9,8},{10,11... | collective-permute-start | bytes 589832 | tf_op jit(solution)/shard_map/ppermute | solution.py:853
  4.7 1.3 %collective-permute-start = (f32[8,1920]{1,0:T(8,128)S(1)}, f32[8,1920]{1,0:T(8,128)S(1)}, u32[]{:S(2)}, u32[]{:S(2)}) collective-permute-start(f32[8,1920]{1,0:T(8,128)S(1)} %get-tuple-element.71.own), channel_id=1, source_target_pairs={{0,8},{1,9},{2,10},{3,11},{4,12},{5,13},{6,14},{7,15},{16,24},{17,... | collective-permute-start | bytes 184328 | tf_op jit(solution)/shard_map/ppermute | solution.py:810
  6.0 5.1 %collective-permute-done.behind = f32[8,1920]{1,0:T(8,128)S(1)} collective-permute-done((f32[8,1920]{1,0:T(8,128)S(1)}, f32[8,1920]{1,0:T(8,128)S(1)}, u32[]{:S(2)}, u32[]{:S(2)}) %collective-permute-start) | collective-permute-done | bytes 61472 | tf_op jit(solution)/shard_map/ppermute | solution.py:810
  11.1 0.0 collective-permute-done.1.after_this.msg
  11.1 1.0 %split.1 = f32[8,72,128]{2,1,0:T(8,128)} custom-call(f32[8,1920]{1,0:T(8,128)S(1)} %get-tuple-element.71.own, f32[8,1920]{1,0:T(8,128)S(1)} %collective-permute-done.behind, s32[1,8]{1,0:T(1,128)S(1)} %get-tuple-element.72.cells, f32[3,128,128]{2,1,0:T(8,128)S(1)} %collective-permute-done.1.after_this.msg), custom_call_target="tpu_custom_call" | custom-call | tf_op jit(solution)/shard_map/split/pallas_call | solution.py:773
  12.1 5.8 %all-to-all-start = ((f32[8,72,128]{2,1,0:T(8,128)}), f32[8,72,128]{2,1,0:T(8,128)S(1)}, u32[]{:S(2)}, u32[]{:S(2)}) async-start(f32[8,72,128]{2,1,0:T(8,128)} %split.1), calls=%async_computation | async-start | bytes 589824 | tf_op jit(solution)/shard_map/all_to_all | solution.py:863
  17.9 3.5 %collective-permute-start.2 = (f32[816,128]{1,0:T(8,128)S(1)}, f32[816,128]{1,0:T(8,128)S(1)}, u32[]{:S(2)}, u32[]{:S(2)}) collective-permute-start(f32[816,128]{1,0:T(8,128)S(1)} %get-tuple-element.79), channel_id=1, source_target_pairs={{1,2},{3,4},{5,6},{7,8},{9,10},{11,12},{13,14},{2,1},{4,3},{6,5},{... | collective-permute-start | bytes 1253384 | tf_op jit(solution)/shard_map/ppermute | solution.py:852
  21.5 2.1 %all-to-all-done.parts = f32[8,72,128]{2,1,0:T(8,128)S(1)} async-done(((f32[8,72,128]{2,1,0:T(8,128)}), f32[8,72,128]{2,1,0:T(8,128)S(1)}, u32[]{:S(2)}, u32[]{:S(2)}) %all-to-all-start) | async-done | bytes 294944 | tf_op jit(solution)/shard_map/all_to_all | solution.py:863
  23.6 0.6 %prepare.1 = (f32[6,3,4,16,128]{4,3,2,1,0:T(8,128)S(1)}, f32[128,128]{1,0:T(8,128)S(1)}) custom-call(f32[8,72,128]{2,1,0:T(8,128)S(1)} %all-to-all-done.parts, f32[16,128]{1,0:T(8,128)S(1)} %get-tuple-element.65.loads.rest_0_, f32[16,128]{1,0:T(8,128)S(1)} %get-tuple-element.66.steps_table), custom_call_target="tpu_custom_call" | custom-call | tf_op jit(solution)/shard_map/prepare/pallas_call | solution.py:773
  24.2 0.5 near0.1
  24.7 5.3 %collective-permute-start.3 = (f32[3,128,128]{2,1,0:T(8,128)S(1)}, f32[3,128,128]{2,1,0:T(8,128)S(1)}, u32[]{:S(2)}, u32[]{:S(2)}) collective-permute-start(f32[3,128,128]{2,1,0:T(8,128)S(1)} %get-tuple-element.83), channel_id=1, source_target_pairs={{0,1},{1,0},{2,3},{3,2},{4,5},{5,4},{6,7},{7,6},{8,9},{9,8},{10,11... | collective-permute-start | bytes 589832 | tf_op jit(solution)/shard_map/ppermute | solution.py:891
  29.9 2.6 %collective-permute-done.2.msg = f32[816,128]{1,0:T(8,128)S(1)} collective-permute-done((f32[816,128]{1,0:T(8,128)S(1)}, f32[816,128]{1,0:T(8,128)S(1)}, u32[]{:S(2)}, u32[]{:S(2)}) %collective-permute-start.2) | collective-permute-done | bytes 417824 | tf_op jit(solution)/shard_map/ppermute | solution.py:852
  32.6 1.5 %far0.1 = (f32[3,2,144,128]{3,2,1,0:T(8,128)S(1)}, f32[6,2,144,128]{3,2,1,0:T(8,128)S(1)}, f32[6,2,128,128]{3,2,1,0:T(8,128)S(1)}, f32[3,128,128]{2,1,0:T(8,128)S(1)}, f32[3,128,128]{2,1,0:T(8,128)S(1)}) custom-call(f32[3,2,144,128]{3,2,1,0:T(8,128)S(1)} %get-tuple-element.76.V0, ...), custom_call_target="tpu_custom_call", output_to_operand_aliasing={{0}: (0, {}), {1}: (1, {}), {2}: (2, {})} | custom-call | tf_op jit(solution)/shard_map/far0/pallas_call | solution.py:773
  34.1 0.0 collective-permute-done.3.msg
  34.1 0.5 near1.1
  34.6 0.1 collective-permute-start.4
  34.6 2.6 %collective-permute-start.5 = (f32[3,128,128]{2,1,0:T(8,128)S(1)}, f32[3,128,128]{2,1,0:T(8,128)S(1)}, u32[]{:S(2)}, u32[]{:S(2)}) collective-permute-start(f32[3,128,128]{2,1,0:T(8,128)S(1)} %get-tuple-element.95), channel_id=1, source_target_pairs={{1,2},{3,4},{5,6},{7,8},{9,10},{11,12},{13,14},{2,1},{4,3},{6,5},{... | collective-permute-start | bytes 589832 | tf_op jit(solution)/shard_map/ppermute | solution.py:909
  37.2 1.3 %far1.1 = (f32[3,2,144,128]{3,2,1,0:T(8,128)S(1)}, f32[6,2,144,128]{3,2,1,0:T(8,128)S(1)}, f32[6,2,128,128]{3,2,1,0:T(8,128)S(1)}, f32[3,128,128]{2,1,0:T(8,128)S(1)}, f32[3,128,128]{2,1,0:T(8,128)S(1)}) custom-call(f32[3,2,144,128]{3,2,1,0:T(8,128)S(1)} %get-tuple-element.84.V0, ...), custom_call_target="tpu_custom_call", output_to_operand_aliasing={{0}: (0, {}), {1}: (1, {}), {2}: (2, {})} | custom-call | tf_op jit(solution)/shard_map/far1/pallas_call | solution.py:773
  38.6 0.0 collective-permute-done.4.msg
  38.6 0.5 near2.1
  39.1 0.1 collective-permute-start.6
  39.2 4.3 %collective-permute-start.7 = (f32[3,128,128]{2,1,0:T(8,128)S(1)}, f32[3,128,128]{2,1,0:T(8,128)S(1)}, u32[]{:S(2)}, u32[]{:S(2)}) collective-permute-start(f32[3,128,128]{2,1,0:T(8,128)S(1)} %get-tuple-element.104), channel_id=1, source_target_pairs={{1,2},{3,4},{5,6},{7,8},{9,10},{11,12},{13,14},{2,1},{4,3},{6,5},{... | collective-permute-start | bytes 589832 | tf_op jit(solution)/shard_map/ppermute | solution.py:909
  43.5 0.2 collective-permute-done.5.msg
  43.7 1.3 %far2.1 = (f32[3,2,144,128]{3,2,1,0:T(8,128)S(1)}, f32[6,2,144,128]{3,2,1,0:T(8,128)S(1)}, f32[6,2,128,128]{3,2,1,0:T(8,128)S(1)}, f32[3,128,128]{2,1,0:T(8,128)S(1)}, f32[3,128,128]{2,1,0:T(8,128)S(1)}) custom-call(f32[3,2,144,128]{3,2,1,0:T(8,128)S(1)} %get-tuple-element.92.V0, ...), custom_call_target="tpu_custom_call", output_to_operand_aliasing={{0}: (0, {}), {1}: (1, {}), {2}: (2, {})} | custom-call | tf_op jit(solution)/shard_map/far2/pallas_call | solution.py:773
  45.1 0.0 collective-permute-done.6.msg
  45.1 0.5 near3.1
  45.5 0.1 collective-permute-start.8
  45.6 2.6 %collective-permute-start.9 = (f32[3,128,128]{2,1,0:T(8,128)S(1)}, f32[3,128,128]{2,1,0:T(8,128)S(1)}, u32[]{:S(2)}, u32[]{:S(2)}) collective-permute-start(f32[3,128,128]{2,1,0:T(8,128)S(1)} %get-tuple-element.113), channel_id=1, source_target_pairs={{1,2},{3,4},{5,6},{7,8},{9,10},{11,12},{13,14},{2,1},{4,3},{6,5},{... | collective-permute-start | bytes 589832 | tf_op jit(solution)/shard_map/ppermute | solution.py:909
  48.3 0.7 %collective-permute-done.7.msg = f32[3,128,128]{2,1,0:T(8,128)S(1)} collective-permute-done((f32[3,128,128]{2,1,0:T(8,128)S(1)}, f32[3,128,128]{2,1,0:T(8,128)S(1)}, u32[]{:S(2)}, u32[]{:S(2)}) %collective-permute-start.7) | collective-permute-done | bytes 196640 | tf_op jit(solution)/shard_map/ppermute | solution.py:909
  48.9 1.3 %far3.1 = (f32[3,2,144,128]{3,2,1,0:T(8,128)S(1)}, f32[6,2,144,128]{3,2,1,0:T(8,128)S(1)}, f32[6,2,128,128]{3,2,1,0:T(8,128)S(1)}, f32[3,128,128]{2,1,0:T(8,128)S(1)}, f32[3,128,128]{2,1,0:T(8,128)S(1)}) custom-call(f32[3,2,144,128]{3,2,1,0:T(8,128)S(1)} %get-tuple-element.101.V0, ...), custom_call_target="tpu_custom_call", output_to_operand_aliasing={{0}: (0, {}), {1}: (1, {}), {2}: (2, {})} | custom-call | tf_op jit(solution)/shard_map/far3/pallas_call | solution.py:773
  50.3 0.0 collective-permute-done.8.msg
  50.3 0.5 near4.1
  50.7 0.1 collective-permute-start.10
  50.8 3.7 %collective-permute-start.11 = (f32[3,128,128]{2,1,0:T(8,128)S(1)}, f32[3,128,128]{2,1,0:T(8,128)S(1)}, u32[]{:S(2)}, u32[]{:S(2)}) collective-permute-start(f32[3,128,128]{2,1,0:T(8,128)S(1)} %get-tuple-element.122), channel_id=1, source_target_pairs={{1,2},{3,4},{5,6},{7,8},{9,10},{11,12},{13,14},{2,1},{4,3},{6,5},{... | collective-permute-start | bytes 589832 | tf_op jit(solution)/shard_map/ppermute | solution.py:909
  54.5 0.2 collective-permute-done.9.msg
  54.7 1.0 %far4.1 = (f32[3,2,144,128]{3,2,1,0:T(8,128)S(1)}, f32[6,2,144,128]{3,2,1,0:T(8,128)S(1)}, f32[6,2,128,128]{3,2,1,0:T(8,128)S(1)}, f32[3,128,128]{2,1,0:T(8,128)S(1)}) custom-call(f32[3,2,144,128]{3,2,1,0:T(8,128)S(1)} %get-tuple-element.110.V0, ...), custom_call_target="tpu_custom_call", output_to_operand_aliasing={{0}: (0, {}), {1}: (1, {}), {2}: (2, {})} | custom-call | tf_op jit(solution)/shard_map/far4/pallas_call | solution.py:773
  55.7 0.0 collective-permute-done.10.msg
  55.7 0.3 near5.1
  56.0 3.9 %collective-permute-done.11.msg = f32[3,128,128]{2,1,0:T(8,128)S(1)} collective-permute-done((f32[3,128,128]{2,1,0:T(8,128)S(1)}, f32[3,128,128]{2,1,0:T(8,128)S(1)}, u32[]{:S(2)}, u32[]{:S(2)}) %collective-permute-start.11) | collective-permute-done | bytes 196640 | tf_op jit(solution)/shard_map/ppermute | solution.py:909
  60.0 1.3 %last.1 = (f32[3,2,144,128]{3,2,1,0:T(8,128)S(1)}, f32[6,2,144,128]{3,2,1,0:T(8,128)S(1)}, f32[6,2,128,128]{3,2,1,0:T(8,128)S(1)}, f32[3,2,128,128]{3,2,1,0:T(8,...) custom-call(f32[3,2,144,128]{3,2,1,0:T(8,128)S(1)} %get-tuple-elemen, ...), custom_call_target="tpu_custom_call", output_to_operand_aliasing={{0}: (0, {}), {1}: (1, {}), {2}: (2, {})} | custom-call | tf_op jit(solution)/shard_map/last/pallas_call | solution.py:773
Async XLA Ops:
  3.9 7.2 %collective-permute-start.1 = (f32[3,128,128]{2,1,0:T(8,128)S(1)}, f32[3,128,128]{2,1,0:T(8,128)S(1)}, u32[]{:S(2)}, u32[]{:S(2)}) collective-permute-start(f32[3,128,128]{2,1,0:T(8,128)S(1)} %get-tuple-element.73), channel_id=1, source_target_pairs={{0,1},{1,0},{2,3},{3,2},{4,5},{5,4},{6,7},{7,6},{8,9},{9,8},{10,11... | collective-permute-start | bytes 589832 | tf_op jit(solution)/shard_map/ppermute | solution.py:853
  4.7 6.4 %collective-permute-start = (f32[8,1920]{1,0:T(8,128)S(1)}, f32[8,1920]{1,0:T(8,128)S(1)}, u32[]{:S(2)}, u32[]{:S(2)}) collective-permute-start(f32[8,1920]{1,0:T(8,128)S(1)} %get-tuple-element.71.own), channel_id=1, source_target_pairs={{0,8},{1,9},{2,10},{3,11},{4,12},{5,13},{6,14},{7,15},{16,24},{17,... | collective-permute-start | bytes 184328 | tf_op jit(solution)/shard_map/ppermute | solution.py:810
  12.1 11.5 %all-to-all-start = ((f32[8,72,128]{2,1,0:T(8,128)}), f32[8,72,128]{2,1,0:T(8,128)S(1)}, u32[]{:S(2)}, u32[]{:S(2)}) async-start(f32[8,72,128]{2,1,0:T(8,128)} %split.1), calls=%async_computation | async-start | bytes 589824 | tf_op jit(solution)/shard_map/all_to_all | solution.py:863
  17.9 14.7 %collective-permute-start.2 = (f32[816,128]{1,0:T(8,128)S(1)}, f32[816,128]{1,0:T(8,128)S(1)}, u32[]{:S(2)}, u32[]{:S(2)}) collective-permute-start(f32[816,128]{1,0:T(8,128)S(1)} %get-tuple-element.79), channel_id=1, source_target_pairs={{1,2},{3,4},{5,6},{7,8},{9,10},{11,12},{13,14},{2,1},{4,3},{6,5},{... | collective-permute-start | bytes 1253384 | tf_op jit(solution)/shard_map/ppermute | solution.py:852
  24.7 9.4 %collective-permute-start.3 = (f32[3,128,128]{2,1,0:T(8,128)S(1)}, f32[3,128,128]{2,1,0:T(8,128)S(1)}, u32[]{:S(2)}, u32[]{:S(2)}) collective-permute-start(f32[3,128,128]{2,1,0:T(8,128)S(1)} %get-tuple-element.83), channel_id=1, source_target_pairs={{0,1},{1,0},{2,3},{3,2},{4,5},{5,4},{6,7},{7,6},{8,9},{9,8},{10,11... | collective-permute-start | bytes 589832 | tf_op jit(solution)/shard_map/ppermute | solution.py:891
  34.6 4.0 %collective-permute-start.4 = (f32[3,128,128]{2,1,0:T(8,128)S(1)}, f32[3,128,128]{2,1,0:T(8,128)S(1)}, u32[]{:S(2)}, u32[]{:S(2)}) collective-permute-start(f32[3,128,128]{2,1,0:T(8,128)S(1)} %get-tuple-element.91), channel_id=1, source_target_pairs={{0,1},{1,0},{2,3},{3,2},{4,5},{5,4},{6,7},{7,6},{8,9},{9,8},{10,11... | collective-permute-start | bytes 589832 | tf_op jit(solution)/shard_map/ppermute | solution.py:891
  34.6 9.1 %collective-permute-start.5 = (f32[3,128,128]{2,1,0:T(8,128)S(1)}, f32[3,128,128]{2,1,0:T(8,128)S(1)}, u32[]{:S(2)}, u32[]{:S(2)}) collective-permute-start(f32[3,128,128]{2,1,0:T(8,128)S(1)} %get-tuple-element.95), channel_id=1, source_target_pairs={{1,2},{3,4},{5,6},{7,8},{9,10},{11,12},{13,14},{2,1},{4,3},{6,5},{... | collective-permute-start | bytes 589832 | tf_op jit(solution)/shard_map/ppermute | solution.py:909
  39.1 6.0 %collective-permute-start.6 = (f32[3,128,128]{2,1,0:T(8,128)S(1)}, f32[3,128,128]{2,1,0:T(8,128)S(1)}, u32[]{:S(2)}, u32[]{:S(2)}) collective-permute-start(f32[3,128,128]{2,1,0:T(8,128)S(1)} %get-tuple-element.100), channel_id=1, source_target_pairs={{0,1},{1,0},{2,3},{3,2},{4,5},{5,4},{6,7},{7,6},{8,9},{9,8},{10,11... | collective-permute-start | bytes 589832 | tf_op jit(solution)/shard_map/ppermute | solution.py:891
  39.2 9.8 %collective-permute-start.7 = (f32[3,128,128]{2,1,0:T(8,128)S(1)}, f32[3,128,128]{2,1,0:T(8,128)S(1)}, u32[]{:S(2)}, u32[]{:S(2)}) collective-permute-start(f32[3,128,128]{2,1,0:T(8,128)S(1)} %get-tuple-element.104), channel_id=1, source_target_pairs={{1,2},{3,4},{5,6},{7,8},{9,10},{11,12},{13,14},{2,1},{4,3},{6,5},{... | collective-permute-start | bytes 589832 | tf_op jit(solution)/shard_map/ppermute | solution.py:909
  45.5 4.7 %collective-permute-start.8 = (f32[3,128,128]{2,1,0:T(8,128)S(1)}, f32[3,128,128]{2,1,0:T(8,128)S(1)}, u32[]{:S(2)}, u32[]{:S(2)}) collective-permute-start(f32[3,128,128]{2,1,0:T(8,128)S(1)} %get-tuple-element.109), channel_id=1, source_target_pairs={{0,1},{1,0},{2,3},{3,2},{4,5},{5,4},{6,7},{7,6},{8,9},{9,8},{10,11... | collective-permute-start | bytes 589832 | tf_op jit(solution)/shard_map/ppermute | solution.py:891
  45.6 9.1 %collective-permute-start.9 = (f32[3,128,128]{2,1,0:T(8,128)S(1)}, f32[3,128,128]{2,1,0:T(8,128)S(1)}, u32[]{:S(2)}, u32[]{:S(2)}) collective-permute-start(f32[3,128,128]{2,1,0:T(8,128)S(1)} %get-tuple-element.113), channel_id=1, source_target_pairs={{1,2},{3,4},{5,6},{7,8},{9,10},{11,12},{13,14},{2,1},{4,3},{6,5},{... | collective-permute-start | bytes 589832 | tf_op jit(solution)/shard_map/ppermute | solution.py:909
  50.7 5.0 %collective-permute-start.10 = (f32[3,128,128]{2,1,0:T(8,128)S(1)}, f32[3,128,128]{2,1,0:T(8,128)S(1)}, u32[]{:S(2)}, u32[]{:S(2)}) collective-permute-start(f32[3,128,128]{2,1,0:T(8,128)S(1)} %get-tuple-element.118), channel_id=1, source_target_pairs={{0,1},{1,0},{2,3},{3,2},{4,5},{5,4},{6,7},{7,6},{8,9},{9,8},{10,11... | collective-permute-start | bytes 589832 | tf_op jit(solution)/shard_map/ppermute | solution.py:891
  50.8 9.1 %collective-permute-start.11 = (f32[3,128,128]{2,1,0:T(8,128)S(1)}, f32[3,128,128]{2,1,0:T(8,128)S(1)}, u32[]{:S(2)}, u32[]{:S(2)}) collective-permute-start(f32[3,128,128]{2,1,0:T(8,128)S(1)} %get-tuple-element.122), channel_id=1, source_target_pairs={{1,2},{3,4},{5,6},{7,8},{9,10},{11,12},{13,14},{2,1},{4,3},{6,5},{... | collective-permute-start | bytes 589832 | tf_op jit(solution)/shard_map/ppermute | solution.py:909

commit v6 on v5

--- a/solution.py
+++ b/solution.py
@@ -769,7 +769,7 @@
 ANYWHERE = pl.BlockSpec(memory_space=pl.ANY)
 
 
-def call(kernel, ins, specs, outs, out_specs, scratch=(), aliases=None, name=None):
+def call(kernel, ins, specs, outs, out_specs, scratch=(), aliases=None, name=None, cost=1):
     return pl.pallas_call(
         kernel,
         out_shape=outs,
@@ -778,6 +778,7 @@
         scratch_shapes=list(scratch),
         input_output_aliases=aliases or {},
         compiler_params=pltpu.CompilerParams(vmem_limit_bytes=VMEM_LIMIT),
+        cost_estimate=pl.CostEstimate(flops=cost, bytes_accessed=cost, transcendentals=0),
         name=name,
     )(*ins)
 
@@ -848,12 +849,13 @@
             *(pltpu.SMEM(table.shape, f32) for table in tables), dma((21,)),
         ),
         name="start",
+        cost=8 * 1024 * 1024,
     )
     msg_far = lax.ppermute(msg_far, "line", far)
     msg_near = lax.ppermute(msg_near, "line", near)
     parts = call(
         functools.partial(split_kernel, panel, slots),
-        (own, behind, in_vmem(pier_row), msg_near),
+        (own, behind, in_vmem(pier_row), coef),
         (WHOLE,) * 3 + (ANYWHERE,),
         jax.ShapeDtypeStruct((GROUP, TRUCK_ROW + slots, depth), f32),
         WHOLE,

time: 61.7 us -> 58.6 us (0.950)
  waiting for transfers between devices: 14.9 us -> 11.9 us
    ppermute x1, waiting for transfers between devices: 5.11 us -> 2.21 us  [ahead_by(): lax.ppermute(x, 'line', [(i, i + distance) for i in range(tiles - distanc...]
    ppermute x1, starting transfers between devices: 0.8 us -> 0.07 us  [body(): msg_near = lax.ppermute(msg_near, 'line', near)]
  transfers between devices with their start and end apart: 13 -> 13, of which waited for: 7 -> 7; matrix products, arithmetic and copies ran while one was open for 0% -> 0% of each run, Pallas kernels for 15% -> 20%
where the time goes in v6:
time: 58.6 us; the launch traced here: 58.1 us
  starting transfers between devices  30 us (51%)
  Pallas kernels  15.4 us (26%)
  waiting for transfers between devices  11.9 us (20%)
  between operations  0.85 us (1%)
    pallas_call x16, Pallas kernels, call(): pl.pallas_call(kernel, out_shape=outs, in_specs=specs, out_specs=out_spec...  15.4 us
    ppermute x4, starting transfers between devices, body(): early = lax.ppermute(msg[0], 'line', far)  13.2 us
    all_to_all x1, starting transfers between devices, body(): lax.all_to_all(parts, 'line', 0, 0, axis_index_groups=groups, tiled=True)  6.29 us
    ppermute x5, starting transfers between devices, body(): msg_near = lax.ppermute(msg[0], 'line', near)  5.57 us
    ppermute x4, waiting for transfers between devices, body(): early = lax.ppermute(msg[0], 'line', far)  5.03 us
    ppermute x1, starting transfers between devices, body(): msg_far = lax.ppermute(msg_far, 'line', far)  3.53 us
    ppermute x1, waiting for transfers between devices, body(): msg_far = lax.ppermute(msg_far, 'line', far)  2.62 us
    ppermute x1, waiting for transfers between devices, ahead_by(): lax.ppermute(x, 'line', [(i, i + distance) for i in range(tiles - distanc...  2.21 us
  transfers between devices with their start and end apart: 13, of which 7 were waited for; matrix products, arithmetic and copies ran while one was open for 0% of the time, Pallas kernels for 20%

profile of v6, /device:TPU:17, one launch (start us, length us, event | category | flops | bytes accessed | tf_op | source)
XLA Modules:
  0.0 58.1 jit_solution(15145467753303141055)
XLA Ops:
  0.6 0.9 %pack.1 = (f32[8,1920]{1,0:T(8,128)S(1)}, f32[16,128]{1,0:T(8,128)S(1)}, f32[16,128]{1,0:T(8,128)S(1)}, s32[1,8]{1,0:T(1,128)S(1)}) custom-call(f32[8,1536]{1,0:T(8,128)} %bitcast.3, f32[16,128]{1,0:T(8,128)} %loads_in.1, s32[6,16]{1,0:T(8,128)} %entries_in.1, s32[6,16]{1,0:T(8,128)} %cells_in.1, s32[1,8]{1,0:T(1,128)} %bitcast.4), custom_call_target="tpu_custom_call" | custom-call | flops 1 | bytes 1 | tf_op jit(solution)/shard_map/pack/pallas_call | solution.py:773
  1.5 1.3 %collective-permute-start = (f32[8,1920]{1,0:T(8,128)S(1)}, f32[8,1920]{1,0:T(8,128)S(1)}, u32[]{:S(2)}, u32[]{:S(2)}) collective-permute-start(f32[8,1920]{1,0:T(8,128)S(1)} %get-tuple-element.71.own), channel_id=1, source_target_pairs={{0,8},{1,9},{2,10},{3,11},{4,12},{5,13},{6,14},{7,15},{16,24},{17,... | collective-permute-start | bytes 184328 | tf_op jit(solution)/shard_map/ppermute | solution.py:811
  2.8 2.4 %start.1 = (f32[3,2,144,128]{3,2,1,0:T(8,128)S(1)}, f32[6,2,144,128]{3,2,1,0:T(8,128)S(1)}, f32[6,2,128,128]{3,2,1,0:T(8,128)S(1)}, f32[16,128]{1,0:T(8,128)S(1)...) custom-call(f32[3,2,128,128]{3,2,1,0:T(8,128)} %velocity.1, f32[6,2,128,128]{3,2,1,0:T(8,128)} %stress.1, ...), custom_call_target="tpu_custom_call" | custom-call | flops 8388608 | bytes 8388608 | tf_op jit(solution)/shard_map/start/pallas_call | solution.py:773
  5.2 0.0 copy-start
  5.2 2.2 %collective-permute-done.behind = f32[8,1920]{1,0:T(8,128)S(1)} collective-permute-done((f32[8,1920]{1,0:T(8,128)S(1)}, f32[8,1920]{1,0:T(8,128)S(1)}, u32[]{:S(2)}, u32[]{:S(2)}) %collective-permute-start) | collective-permute-done | bytes 61472 | tf_op jit(solution)/shard_map/ppermute | solution.py:811
  7.4 1.0 %split.1 = f32[8,72,128]{2,1,0:T(8,128)} custom-call(f32[8,1920]{1,0:T(8,128)S(1)} %get-tuple-element.71.own, f32[8,1920]{1,0:T(8,128)S(1)} %collective-permute-done.behind, s32[1,8]{1,0:T(1,128)S(1)} %get-tuple-element.72.cells, f32[16,128]{1,0:T(8,128)S(1)} %get-tuple-element.70.after_this.coef_ref), custom_call_target="tpu_custom_call" | custom-call | flops 1 | bytes 1 | tf_op jit(solution)/shard_map/split/pallas_call | solution.py:773
  8.4 0.0 copy-done
  8.5 6.3 %all-to-all-start = ((f32[8,72,128]{2,1,0:T(8,128)}), f32[8,72,128]{2,1,0:T(8,128)S(1)}, u32[]{:S(2)}, u32[]{:S(2)}) async-start(f32[8,72,128]{2,1,0:T(8,128)} %split.1), calls=%async_computation | async-start | bytes 589824 | tf_op jit(solution)/shard_map/all_to_all | solution.py:865
  14.7 3.5 %collective-permute-start.2 = (f32[816,128]{1,0:T(8,128)S(1)}, f32[816,128]{1,0:T(8,128)S(1)}, u32[]{:S(2)}, u32[]{:S(2)}) collective-permute-start(f32[816,128]{1,0:T(8,128)S(1)} %get-tuple-element.79), channel_id=1, source_target_pairs={{1,2},{3,4},{5,6},{7,8},{9,10},{11,12},{13,14},{2,1},{4,3},{6,5},{... | collective-permute-start | bytes 1253384 | tf_op jit(solution)/shard_map/ppermute | solution.py:854
  18.3 0.1 collective-permute-start.1
  18.4 2.0 %all-to-all-done.parts = f32[8,72,128]{2,1,0:T(8,128)S(1)} async-done(((f32[8,72,128]{2,1,0:T(8,128)}), f32[8,72,128]{2,1,0:T(8,128)S(1)}, u32[]{:S(2)}, u32[]{:S(2)}) %all-to-all-start) | async-done | bytes 294944 | tf_op jit(solution)/shard_map/all_to_all | solution.py:865
  20.4 0.6 %prepare.1 = (f32[6,3,4,16,128]{4,3,2,1,0:T(8,128)S(1)}, f32[128,128]{1,0:T(8,128)S(1)}) custom-call(f32[8,72,128]{2,1,0:T(8,128)S(1)} %all-to-all-done.parts, f32[16,128]{1,0:T(8,128)S(1)} %get-tuple-element.65.loads.rest_0_, f32[16,128]{1,0:T(8,128)S(1)} %get-tuple-element.66.steps_table), custom_call_target="tpu_custom_call" | custom-call | flops 1 | bytes 1 | tf_op jit(solution)/shard_map/prepare/pallas_call | solution.py:773
  21.0 0.0 collective-permute-done.1.msg
  21.0 0.5 near0.1
  21.5 5.3 %collective-permute-start.3 = (f32[3,128,128]{2,1,0:T(8,128)S(1)}, f32[3,128,128]{2,1,0:T(8,128)S(1)}, u32[]{:S(2)}, u32[]{:S(2)}) collective-permute-start(f32[3,128,128]{2,1,0:T(8,128)S(1)} %get-tuple-element.83), channel_id=1, source_target_pairs={{0,1},{1,0},{2,3},{3,2},{4,5},{5,4},{6,7},{7,6},{8,9},{9,8},{10,11... | collective-permute-start | bytes 589832 | tf_op jit(solution)/shard_map/ppermute | solution.py:893
  26.8 2.6 %collective-permute-done.2.msg = f32[816,128]{1,0:T(8,128)S(1)} collective-permute-done((f32[816,128]{1,0:T(8,128)S(1)}, f32[816,128]{1,0:T(8,128)S(1)}, u32[]{:S(2)}, u32[]{:S(2)}) %collective-permute-start.2) | collective-permute-done | bytes 417824 | tf_op jit(solution)/shard_map/ppermute | solution.py:854
  29.4 1.5 %far0.1 = (f32[3,2,144,128]{3,2,1,0:T(8,128)S(1)}, f32[6,2,144,128]{3,2,1,0:T(8,128)S(1)}, f32[6,2,128,128]{3,2,1,0:T(8,128)S(1)}, f32[3,128,128]{2,1,0:T(8,128)S(1)}, f32[3,128,128]{2,1,0:T(8,128)S(1)}) custom-call(f32[3,2,144,128]{3,2,1,0:T(8,128)S(1)} %get-tuple-element.76.V0, ...), custom_call_target="tpu_custom_call", output_to_operand_aliasing={{0}: (0, {}), {1}: (1, {}), {2}: (2, {})} | custom-call | flops 1 | bytes 1 | tf_op jit(solution)/shard_map/far0/pallas_call | solution.py:773
  30.9 0.0 collective-permute-done.3.msg
  30.9 0.5 near1.1
  31.4 0.1 collective-permute-start.4
  31.5 2.6 %collective-permute-start.5 = (f32[3,128,128]{2,1,0:T(8,128)S(1)}, f32[3,128,128]{2,1,0:T(8,128)S(1)}, u32[]{:S(2)}, u32[]{:S(2)}) collective-permute-start(f32[3,128,128]{2,1,0:T(8,128)S(1)} %get-tuple-element.95), channel_id=1, source_target_pairs={{1,2},{3,4},{5,6},{7,8},{9,10},{11,12},{13,14},{2,1},{4,3},{6,5},{... | collective-permute-start | bytes 589832 | tf_op jit(solution)/shard_map/ppermute | solution.py:911
  34.1 1.3 %far1.1 = (f32[3,2,144,128]{3,2,1,0:T(8,128)S(1)}, f32[6,2,144,128]{3,2,1,0:T(8,128)S(1)}, f32[6,2,128,128]{3,2,1,0:T(8,128)S(1)}, f32[3,128,128]{2,1,0:T(8,128)S(1)}, f32[3,128,128]{2,1,0:T(8,128)S(1)}) custom-call(f32[3,2,144,128]{3,2,1,0:T(8,128)S(1)} %get-tuple-element.84.V0, ...), custom_call_target="tpu_custom_call", output_to_operand_aliasing={{0}: (0, {}), {1}: (1, {}), {2}: (2, {})} | custom-call | flops 1 | bytes 1 | tf_op jit(solution)/shard_map/far1/pallas_call | solution.py:773
  35.4 0.0 collective-permute-done.4.msg
  35.4 0.5 near2.1
  35.9 0.1 collective-permute-start.6
  36.0 4.3 %collective-permute-start.7 = (f32[3,128,128]{2,1,0:T(8,128)S(1)}, f32[3,128,128]{2,1,0:T(8,128)S(1)}, u32[]{:S(2)}, u32[]{:S(2)}) collective-permute-start(f32[3,128,128]{2,1,0:T(8,128)S(1)} %get-tuple-element.104), channel_id=1, source_target_pairs={{1,2},{3,4},{5,6},{7,8},{9,10},{11,12},{13,14},{2,1},{4,3},{6,5},{... | collective-permute-start | bytes 589832 | tf_op jit(solution)/shard_map/ppermute | solution.py:911
  40.3 0.2 collective-permute-done.5.msg
  40.6 1.3 %far2.1 = (f32[3,2,144,128]{3,2,1,0:T(8,128)S(1)}, f32[6,2,144,128]{3,2,1,0:T(8,128)S(1)}, f32[6,2,128,128]{3,2,1,0:T(8,128)S(1)}, f32[3,128,128]{2,1,0:T(8,128)S(1)}, f32[3,128,128]{2,1,0:T(8,128)S(1)}) custom-call(f32[3,2,144,128]{3,2,1,0:T(8,128)S(1)} %get-tuple-element.92.V0, ...), custom_call_target="tpu_custom_call", output_to_operand_aliasing={{0}: (0, {}), {1}: (1, {}), {2}: (2, {})} | custom-call | flops 1 | bytes 1 | tf_op jit(solution)/shard_map/far2/pallas_call | solution.py:773
  41.9 0.0 collective-permute-done.6.msg
  41.9 0.5 near3.1
  42.4 0.1 collective-permute-start.8
  42.5 2.6 %collective-permute-start.9 = (f32[3,128,128]{2,1,0:T(8,128)S(1)}, f32[3,128,128]{2,1,0:T(8,128)S(1)}, u32[]{:S(2)}, u32[]{:S(2)}) collective-permute-start(f32[3,128,128]{2,1,0:T(8,128)S(1)} %get-tuple-element.113), channel_id=1, source_target_pairs={{1,2},{3,4},{5,6},{7,8},{9,10},{11,12},{13,14},{2,1},{4,3},{6,5},{... | collective-permute-start | bytes 589832 | tf_op jit(solution)/shard_map/ppermute | solution.py:911
  45.1 0.7 %collective-permute-done.7.msg = f32[3,128,128]{2,1,0:T(8,128)S(1)} collective-permute-done((f32[3,128,128]{2,1,0:T(8,128)S(1)}, f32[3,128,128]{2,1,0:T(8,128)S(1)}, u32[]{:S(2)}, u32[]{:S(2)}) %collective-permute-start.7) | collective-permute-done | bytes 196640 | tf_op jit(solution)/shard_map/ppermute | solution.py:911
  45.8 1.3 %far3.1 = (f32[3,2,144,128]{3,2,1,0:T(8,128)S(1)}, f32[6,2,144,128]{3,2,1,0:T(8,128)S(1)}, f32[6,2,128,128]{3,2,1,0:T(8,128)S(1)}, f32[3,128,128]{2,1,0:T(8,128)S(1)}, f32[3,128,128]{2,1,0:T(8,128)S(1)}) custom-call(f32[3,2,144,128]{3,2,1,0:T(8,128)S(1)} %get-tuple-element.101.V0, ...), custom_call_target="tpu_custom_call", output_to_operand_aliasing={{0}: (0, {}), {1}: (1, {}), {2}: (2, {})} | custom-call | flops 1 | bytes 1 | tf_op jit(solution)/shard_map/far3/pallas_call | solution.py:773
  47.1 0.0 collective-permute-done.8.msg
  47.1 0.5 near4.1
  47.6 0.1 collective-permute-start.10
  47.7 3.7 %collective-permute-start.11 = (f32[3,128,128]{2,1,0:T(8,128)S(1)}, f32[3,128,128]{2,1,0:T(8,128)S(1)}, u32[]{:S(2)}, u32[]{:S(2)}) collective-permute-start(f32[3,128,128]{2,1,0:T(8,128)S(1)} %get-tuple-element.122), channel_id=1, source_target_pairs={{1,2},{3,4},{5,6},{7,8},{9,10},{11,12},{13,14},{2,1},{4,3},{6,5},{... | collective-permute-start | bytes 589832 | tf_op jit(solution)/shard_map/ppermute | solution.py:911
  51.4 0.2 collective-permute-done.9.msg
  51.6 1.0 %far4.1 = (f32[3,2,144,128]{3,2,1,0:T(8,128)S(1)}, f32[6,2,144,128]{3,2,1,0:T(8,128)S(1)}, f32[6,2,128,128]{3,2,1,0:T(8,128)S(1)}, f32[3,128,128]{2,1,0:T(8,128)S(1)}) custom-call(f32[3,2,144,128]{3,2,1,0:T(8,128)S(1)} %get-tuple-element.110.V0, ...), custom_call_target="tpu_custom_call", output_to_operand_aliasing={{0}: (0, {}), {1}: (1, {}), {2}: (2, {})} | custom-call | flops 1 | bytes 1 | tf_op jit(solution)/shard_map/far4/pallas_call | solution.py:773
  52.6 0.0 collective-permute-done.10.msg
  52.6 0.3 near5.1
  52.9 3.9 %collective-permute-done.11.msg = f32[3,128,128]{2,1,0:T(8,128)S(1)} collective-permute-done((f32[3,128,128]{2,1,0:T(8,128)S(1)}, f32[3,128,128]{2,1,0:T(8,128)S(1)}, u32[]{:S(2)}, u32[]{:S(2)}) %collective-permute-start.11) | collective-permute-done | bytes 196640 | tf_op jit(solution)/shard_map/ppermute | solution.py:911
  56.8 1.3 %last.1 = (f32[3,2,144,128]{3,2,1,0:T(8,128)S(1)}, f32[6,2,144,128]{3,2,1,0:T(8,128)S(1)}, f32[6,2,128,128]{3,2,1,0:T(8,128)S(1)}, f32[3,2,128,128]{3,2,1,0:T(8,...) custom-call(f32[3,2,144,128]{3,2,1,0:T(8,128)S(1)} %get-tuple-elemen, ...), custom_call_target="tpu_custom_call", output_to_operand_aliasing={{0}: (0, {}), {1}: (1, {}), {2}: (2, {})} | custom-call | flops 1 | bytes 1 | tf_op jit(solution)/shard_map/last/pallas_call | solution.py:773
Async XLA Ops:
  1.5 5.9 %collective-permute-start = (f32[8,1920]{1,0:T(8,128)S(1)}, f32[8,1920]{1,0:T(8,128)S(1)}, u32[]{:S(2)}, u32[]{:S(2)}) collective-permute-start(f32[8,1920]{1,0:T(8,128)S(1)} %get-tuple-element.71.own), channel_id=1, source_target_pairs={{0,8},{1,9},{2,10},{3,11},{4,12},{5,13},{6,14},{7,15},{16,24},{17,... | collective-permute-start | bytes 184328 | tf_op jit(solution)/shard_map/ppermute | solution.py:811
  5.2 3.3 %copy-start = (f32[3,128,128]{2,1,0:T(8,128)}, f32[3,128,128]{2,1,0:T(8,128)S(1)}, u32[]{:S(2)}) copy-start(f32[3,128,128]{2,1,0:T(8,128)S(1)} %get-tuple-element.75) | copy-start | bytes 589828
  8.5 11.9 %all-to-all-start = ((f32[8,72,128]{2,1,0:T(8,128)}), f32[8,72,128]{2,1,0:T(8,128)S(1)}, u32[]{:S(2)}, u32[]{:S(2)}) async-start(f32[8,72,128]{2,1,0:T(8,128)} %split.1), calls=%async_computation | async-start | bytes 589824 | tf_op jit(solution)/shard_map/all_to_all | solution.py:865
  14.7 14.7 %collective-permute-start.2 = (f32[816,128]{1,0:T(8,128)S(1)}, f32[816,128]{1,0:T(8,128)S(1)}, u32[]{:S(2)}, u32[]{:S(2)}) collective-permute-start(f32[816,128]{1,0:T(8,128)S(1)} %get-tuple-element.79), channel_id=1, source_target_pairs={{1,2},{3,4},{5,6},{7,8},{9,10},{11,12},{13,14},{2,1},{4,3},{6,5},{... | collective-permute-start | bytes 1253384 | tf_op jit(solution)/shard_map/ppermute | solution.py:854
  18.3 2.7 %collective-permute-start.1 = (f32[3,128,128]{2,1,0:T(8,128)}, f32[3,128,128]{2,1,0:T(8,128)S(1)}, u32[]{:S(2)}, u32[]{:S(2)}) collective-permute-start(f32[3,128,128]{2,1,0:T(8,128)} %copy-done), channel_id=1, source_target_pairs={{0,1},{1,0},{2,3},{3,2},{4,5},{5,4},{6,7},{7,6},{8,9},{9,8},{10,11... | collective-permute-start | bytes 589832 | tf_op jit(solution)/shard_map/ppermute | solution.py:855
  21.5 9.4 %collective-permute-start.3 = (f32[3,128,128]{2,1,0:T(8,128)S(1)}, f32[3,128,128]{2,1,0:T(8,128)S(1)}, u32[]{:S(2)}, u32[]{:S(2)}) collective-permute-start(f32[3,128,128]{2,1,0:T(8,128)S(1)} %get-tuple-element.83), channel_id=1, source_target_pairs={{0,1},{1,0},{2,3},{3,2},{4,5},{5,4},{6,7},{7,6},{8,9},{9,8},{10,11... | collective-permute-start | bytes 589832 | tf_op jit(solution)/shard_map/ppermute | solution.py:893
  31.4 4.0 %collective-permute-start.4 = (f32[3,128,128]{2,1,0:T(8,128)S(1)}, f32[3,128,128]{2,1,0:T(8,128)S(1)}, u32[]{:S(2)}, u32[]{:S(2)}) collective-permute-start(f32[3,128,128]{2,1,0:T(8,128)S(1)} %get-tuple-element.91), channel_id=1, source_target_pairs={{0,1},{1,0},{2,3},{3,2},{4,5},{5,4},{6,7},{7,6},{8,9},{9,8},{10,11... | collective-permute-start | bytes 589832 | tf_op jit(solution)/shard_map/ppermute | solution.py:893
  31.5 9.1 %collective-permute-start.5 = (f32[3,128,128]{2,1,0:T(8,128)S(1)}, f32[3,128,128]{2,1,0:T(8,128)S(1)}, u32[]{:S(2)}, u32[]{:S(2)}) collective-permute-start(f32[3,128,128]{2,1,0:T(8,128)S(1)} %get-tuple-element.95), channel_id=1, source_target_pairs={{1,2},{3,4},{5,6},{7,8},{9,10},{11,12},{13,14},{2,1},{4,3},{6,5},{... | collective-permute-start | bytes 589832 | tf_op jit(solution)/shard_map/ppermute | solution.py:911
  35.9 6.0 %collective-permute-start.6 = (f32[3,128,128]{2,1,0:T(8,128)S(1)}, f32[3,128,128]{2,1,0:T(8,128)S(1)}, u32[]{:S(2)}, u32[]{:S(2)}) collective-permute-start(f32[3,128,128]{2,1,0:T(8,128)S(1)} %get-tuple-element.100), channel_id=1, source_target_pairs={{0,1},{1,0},{2,3},{3,2},{4,5},{5,4},{6,7},{7,6},{8,9},{9,8},{10,11... | collective-permute-start | bytes 589832 | tf_op jit(solution)/shard_map/ppermute | solution.py:893
  36.0 9.8 %collective-permute-start.7 = (f32[3,128,128]{2,1,0:T(8,128)S(1)}, f32[3,128,128]{2,1,0:T(8,128)S(1)}, u32[]{:S(2)}, u32[]{:S(2)}) collective-permute-start(f32[3,128,128]{2,1,0:T(8,128)S(1)} %get-tuple-element.104), channel_id=1, source_target_pairs={{1,2},{3,4},{5,6},{7,8},{9,10},{11,12},{13,14},{2,1},{4,3},{6,5},{... | collective-permute-start | bytes 589832 | tf_op jit(solution)/shard_map/ppermute | solution.py:911
  42.4 4.7 %collective-permute-start.8 = (f32[3,128,128]{2,1,0:T(8,128)S(1)}, f32[3,128,128]{2,1,0:T(8,128)S(1)}, u32[]{:S(2)}, u32[]{:S(2)}) collective-permute-start(f32[3,128,128]{2,1,0:T(8,128)S(1)} %get-tuple-element.109), channel_id=1, source_target_pairs={{0,1},{1,0},{2,3},{3,2},{4,5},{5,4},{6,7},{7,6},{8,9},{9,8},{10,11... | collective-permute-start | bytes 589832 | tf_op jit(solution)/shard_map/ppermute | solution.py:893
  42.5 9.1 %collective-permute-start.9 = (f32[3,128,128]{2,1,0:T(8,128)S(1)}, f32[3,128,128]{2,1,0:T(8,128)S(1)}, u32[]{:S(2)}, u32[]{:S(2)}) collective-permute-start(f32[3,128,128]{2,1,0:T(8,128)S(1)} %get-tuple-element.113), channel_id=1, source_target_pairs={{1,2},{3,4},{5,6},{7,8},{9,10},{11,12},{13,14},{2,1},{4,3},{6,5},{... | collective-permute-start | bytes 589832 | tf_op jit(solution)/shard_map/ppermute | solution.py:911
  47.6 5.0 %collective-permute-start.10 = (f32[3,128,128]{2,1,0:T(8,128)S(1)}, f32[3,128,128]{2,1,0:T(8,128)S(1)}, u32[]{:S(2)}, u32[]{:S(2)}) collective-permute-start(f32[3,128,128]{2,1,0:T(8,128)S(1)} %get-tuple-element.118), channel_id=1, source_target_pairs={{0,1},{1,0},{2,3},{3,2},{4,5},{5,4},{6,7},{7,6},{8,9},{9,8},{10,11... | collective-permute-start | bytes 589832 | tf_op jit(solution)/shard_map/ppermute | solution.py:893
  47.7 9.1 %collective-permute-start.11 = (f32[3,128,128]{2,1,0:T(8,128)S(1)}, f32[3,128,128]{2,1,0:T(8,128)S(1)}, u32[]{:S(2)}, u32[]{:S(2)}) collective-permute-start(f32[3,128,128]{2,1,0:T(8,128)S(1)} %get-tuple-element.122), channel_id=1, source_target_pairs={{1,2},{3,4},{5,6},{7,8},{9,10},{11,12},{13,14},{2,1},{4,3},{6,5},{... | collective-permute-start | bytes 589832 | tf_op jit(solution)/shard_map/ppermute | solution.py:911

commit v7 on v6

--- a/solution.py
+++ b/solution.py
@@ -14,7 +14,7 @@
 DT = 0.25
 PAD = 8
 ROWS = 16
-UNROLL = 4
+UNROLL = 8
 VMEM_LIMIT = 32 * 1024 * 1024
 
 C_B, C_B0, C_B1, C_M0, C_M1, C_LAM, C_MU2, C_MU, C_K1, C_K2, C_K2H, C_L0 = range(12)
@@ -547,7 +547,7 @@
             pre_behind(V, S, coef_ref, rest[0], force.at[step + 1], window)
 
 
-def load_ahead(msg, loads, across, rows_out, load):
+def meet_kernel(across, msg, loads, load, rows_out):
     slots = loads.shape[0]
     rows, entry, cell = (msg[6 * across + i * slots : 6 * across + (i + 1) * slots, :] for i in range(3))
     for slot in range(slots):
@@ -567,8 +567,8 @@
     here, then = force.at[step], force.at[step + 1]
     got = Planes(msg, 3 * step, across) if step < 2 else msg
     if step == 0:
-        missing, loads = None, other
-        G, W, A, load, rows_out = rest[-5:]
+        missing, load = None, other
+        G, W, A = rest[-3:]
     else:
         missing = other
         G, W = rest[-2:]
@@ -588,7 +588,6 @@
     @pl.when(jnp.logical_not(even))
     def _():
         if step == 0:
-            load_ahead(msg, loads, across, rows_out, load)
             respond = lambda: first_response_behind(V, S, coef_ref, here, load, D, W, A, window)
         else:
             respond = lambda: response_behind(V, S, coef_ref, D, W)
@@ -681,7 +680,8 @@
     cell_of = cells[...]
     me = lax.axis_index("line")
     group, mine = lax.div(me, tiles), lax.rem(me, tiles)
-    row = lax.broadcasted_iota(jnp.int32, (4 * tiles, cell_of.shape[1]), 0)
+    piers = cell_of.shape[1]
+    row = lax.broadcasted_iota(jnp.int32, (4 * tiles, lanes), 0)
     tile, j = lax.div(row, 4), lax.rem(row, 4)
     odd = lax.rem(tile, 2)
     first = (tile + group * tiles) * 2
@@ -689,14 +689,16 @@
     cell_yz = first + jnp.where(j == 3, 4 * odd - 1, j)
     record = jnp.where(group == 0, own[:, :panel], behind[:, :panel])
 
-    def share(cell, columns):
-        hit = jnp.where(cell == cell_of, 1.0, 0.0).astype(jnp.float32)
-        return jnp.dot(
-            hit, record[:, columns], precision=lax.Precision.HIGHEST, preferred_element_type=jnp.float32
-        )
-
-    part_x = share(cell_x, slice(0, third * lanes))
-    part_yz = share(cell_yz, slice(third * lanes, panel))
+    def hits(cell):
+        return [jnp.where(cell == cell_of[0:1, p : p + 1], 1.0, 0.0).astype(jnp.float32) for p in range(piers)]
+
+    hit_x, hit_yz = hits(cell_x), hits(cell_yz)
+
+    def share(m):
+        hit = hit_x if m < third else hit_yz
+        return sum(hit[p] * record[p : p + 1, m * lanes : (m + 1) * lanes] for p in range(piers))
+
+    parts = [share(m) for m in range(pieces)]
 
     def trucks(source):
         blocks = [source[0:8, panel + i * lanes : panel + (i + 1) * lanes] for i in range(slots // 8 + 1)]
@@ -707,8 +709,7 @@
     for tile in range(tiles):
         these = slice(4 * tile, 4 * tile + 4)
         for m in range(pieces):
-            part, at = (part_x, m) if m < third else (part_yz, m - third)
-            out[tile, 4 * m : 4 * m + 4, :] = part[these, at * lanes : (at + 1) * lanes]
+            out[tile, 4 * m : 4 * m + 4, :] = parts[m][these, :]
         passed = mine < tile
         out[tile, ENTRY_ROW : ENTRY_ROW + 1, :] = jnp.where(passed, own_entry, far_entry)
         for i in range(slots // 8):
@@ -716,7 +717,8 @@
             out[tile, at : at + 8, :] = jnp.where(passed, own_rows[i], far_rows[i])
 
 
-def prepare_kernel(parts, loads, steps_table, force, surface, table, rows_out):
+def prepare_kernel(parts, loads, steps_table, after_this, force, surface, table, rows_out):
+    del after_this
     steps, comps, width = force.shape[:3]
     lanes = parts.shape[2]
     force[...] = jnp.zeros(force.shape, jnp.float32)
@@ -863,10 +865,20 @@
     )
     groups = [list(range(at, at + GROUP)) for at in range(0, tiles, GROUP)]
     parts = lax.all_to_all(parts, "line", 0, 0, axis_index_groups=groups, tiled=True)
+    load = call(
+        functools.partial(meet_kernel, across),
+        (in_vmem(msg_far), in_vmem(loads)),
+        (WHOLE,) * 2,
+        square,
+        WHOLE,
+        scratch=(pltpu.VMEM((depth, across), f32),),
+        name="meet",
+        cost=64 * 1024 * 1024,
+    )
     force, surface = call(
         prepare_kernel,
-        (parts, in_vmem(loads), in_vmem(steps_table)),
-        (WHOLE,) * 3,
+        (parts, in_vmem(loads), in_vmem(steps_table), load),
+        (WHOLE,) * 3 + (ANYWHERE,),
         (pltpu.VMEM((STEPS, 3, 4, 16, depth), f32), pltpu.VMEM((across, depth), f32)),
         (WHOLE,) * 2,
         scratch=(pltpu.VMEM((depth, depth), f32), pltpu.VMEM((depth, across), f32)),
@@ -891,7 +903,7 @@
         )
         if more:
             msg_near = lax.ppermute(msg[0], "line", near)
-        ins = (V, S, R, coef, force, surface, msg_far, missing if step else loads)
+        ins = (V, S, R, coef, force, surface, msg_far, missing if step else load)
         ins = tuple(in_vmem(x) for x in ins)
         if more:
             outs = state + (m_type,) + ((m_type,) if step < STEPS - 2 else ())
@@ -901,7 +913,7 @@
                 (WHOLE,) * len(ins),
                 outs,
                 (WHOLE,) * len(outs),
-                scratch=(ghost, work) + (() if step else (pltpu.VMEM((5, padded, depth), f32),) + (square,) * 2),
+                scratch=(ghost, work) + (() if step else (pltpu.VMEM((5, padded, depth), f32),)),
                 aliases=same,
                 name="far" + str(step),
             )

time: 58.6 us -> 57.6 us (0.983)
  waiting for transfers between devices: 11.9 us -> 20.3 us
  starting transfers between devices: 30 us -> 24.9 us
  Pallas kernels: 15.4 us -> 10.3 us
  local copies, waits for them, and re-layouts: 0.01 us -> 0.67 us
    ppermute x1, waiting for transfers between devices: 2.62 us -> 11 us  [body(): msg_far = lax.ppermute(msg_far, 'line', far)]
    ppermute x5, starting transfers between devices: 5.57 us -> 0.45 us  [body(): msg_near = lax.ppermute(msg[0], 'line', near)]
    pallas_call x16 -> x17, Pallas kernels: 15.4 us -> 10.3 us  [call(): pl.pallas_call(kernel, out_shape=outs, in_specs=specs, out_specs=out_spec...]
    all_to_all x1, waiting for transfers between devices: 2.02 us -> 0.01 us  [body(): lax.all_to_all(parts, 'line', 0, 0, axis_index_groups=groups, tiled=True)]
    ppermute x4, waiting for transfers between devices: 5.03 us -> 6.49 us  [body(): early = lax.ppermute(msg[0], 'line', far)]
    ppermute x5, waiting for transfers between devices: 0.01 us -> 0.79 us  [body(): msg_near = lax.ppermute(msg[0], 'line', near)]
    unnamed x2, local copies, waits for them, and re-layouts: 0.01 us -> 0.67 us
  transfers between devices with their start and end apart: 13 -> 13, of which waited for: 7 -> 7; matrix products, arithmetic and copies ran while one was open for 0% -> 0% of each run, Pallas kernels for 20% -> 12%
where the time goes in v7:
time: 57.6 us; the launch traced here: 57.1 us
  starting transfers between devices  24.9 us (43%)
  waiting for transfers between devices  20.3 us (35%)
  Pallas kernels  10.3 us (18%)
  between operations  0.87 us (2%)
  local copies, waits for them, and re-layouts  0.67 us (1%)
    ppermute x4, starting transfers between devices, body(): early = lax.ppermute(msg[0], 'line', far)  13.3 us
    ppermute x1, waiting for transfers between devices, body(): msg_far = lax.ppermute(msg_far, 'line', far)  11 us
    pallas_call x17, Pallas kernels, call(): pl.pallas_call(kernel, out_shape=outs, in_specs=specs, out_specs=out_spec...  10.3 us
    ppermute x4, waiting for transfers between devices, body(): early = lax.ppermute(msg[0], 'line', far)  6.49 us
    all_to_all x1, starting transfers between devices, body(): lax.all_to_all(parts, 'line', 0, 0, axis_index_groups=groups, tiled=True)  6.3 us
    ppermute x1, starting transfers between devices, body(): msg_far = lax.ppermute(msg_far, 'line', far)  3.53 us
    ppermute x1, waiting for transfers between devices, ahead_by(): lax.ppermute(x, 'line', [(i, i + distance) for i in range(tiles - distanc...  1.99 us
    ppermute x1, starting transfers between devices, ahead_by(): lax.ppermute(x, 'line', [(i, i + distance) for i in range(tiles - distanc...  1.29 us
  transfers between devices with their start and end apart: 13, of which 7 were waited for; matrix products, arithmetic and copies ran while one was open for 0% of the time, Pallas kernels for 12%

profile of v7, /device:TPU:17, one launch (start us, length us, event | category | flops | bytes accessed | tf_op | source)
XLA Modules:
  0.0 57.1 jit_solution(6629539685676320640)
XLA Ops:
  0.6 0.9 %pack.1 = (f32[8,1920]{1,0:T(8,128)S(1)}, f32[16,128]{1,0:T(8,128)S(1)}, f32[16,128]{1,0:T(8,128)S(1)}, s32[1,8]{1,0:T(1,128)S(1)}) custom-call(f32[8,1536]{1,0:T(8,128)} %bitcast.3, f32[16,128]{1,0:T(8,128)} %loads_in.1, s32[6,16]{1,0:T(8,128)} %entries_in.1, s32[6,16]{1,0:T(8,128)} %cells_in.1, s32[1,8]{1,0:T(1,128)} %bitcast.4), custom_call_target="tpu_custom_call" | custom-call | flops 1 | bytes 1 | tf_op jit(solution)/shard_map/pack/pallas_call | solution.py:775
  1.5 1.3 %collective-permute-start = (f32[8,1920]{1,0:T(8,128)S(1)}, f32[8,1920]{1,0:T(8,128)S(1)}, u32[]{:S(2)}, u32[]{:S(2)}) collective-permute-start(f32[8,1920]{1,0:T(8,128)S(1)} %get-tuple-element.71.own), channel_id=1, source_target_pairs={{0,8},{1,9},{2,10},{3,11},{4,12},{5,13},{6,14},{7,15},{16,24},{17,... | collective-permute-start | bytes 184328 | tf_op jit(solution)/shard_map/ppermute | solution.py:813
  2.8 1.9 %start.1 = (f32[3,2,144,128]{3,2,1,0:T(8,128)S(1)}, f32[6,2,144,128]{3,2,1,0:T(8,128)S(1)}, f32[6,2,128,128]{3,2,1,0:T(8,128)S(1)}, f32[16,128]{1,0:T(8,128)S(1)...) custom-call(f32[3,2,128,128]{3,2,1,0:T(8,128)} %velocity.1, f32[6,2,128,128]{3,2,1,0:T(8,128)} %stress.1, ...), custom_call_target="tpu_custom_call" | custom-call | flops 8388608 | bytes 8388608 | tf_op jit(solution)/shard_map/start/pallas_call | solution.py:775
  4.7 0.0 copy-start
  4.8 0.7 %copy-done = f32[3,128,128]{2,1,0:T(8,128)} copy-done((f32[3,128,128]{2,1,0:T(8,128)}, f32[3,128,128]{2,1,0:T(8,128)S(1)}, u32[]{:S(2)}) %copy-start) | copy-done | bytes 196632
  5.4 2.0 %collective-permute-done.behind = f32[8,1920]{1,0:T(8,128)S(1)} collective-permute-done((f32[8,1920]{1,0:T(8,128)S(1)}, f32[8,1920]{1,0:T(8,128)S(1)}, u32[]{:S(2)}, u32[]{:S(2)}) %collective-permute-start) | collective-permute-done | bytes 61472 | tf_op jit(solution)/shard_map/ppermute | solution.py:813
  7.4 0.9 %split.1 = f32[8,72,128]{2,1,0:T(8,128)} custom-call(f32[8,1920]{1,0:T(8,128)S(1)} %get-tuple-element.71.own, f32[8,1920]{1,0:T(8,128)S(1)} %collective-permute-done.behind, s32[1,8]{1,0:T(1,128)S(1)} %get-tuple-element.72.cells, f32[16,128]{1,0:T(8,128)S(1)} %get-tuple-element.70.after_this.coef_ref), custom_call_target="tpu_custom_call" | custom-call | flops 1 | bytes 1 | tf_op jit(solution)/shard_map/split/pallas_call | solution.py:775
  8.3 6.3 %all-to-all-start = ((f32[8,72,128]{2,1,0:T(8,128)}), f32[8,72,128]{2,1,0:T(8,128)S(1)}, u32[]{:S(2)}, u32[]{:S(2)}) async-start(f32[8,72,128]{2,1,0:T(8,128)} %split.1), calls=%async_computation | async-start | bytes 589824 | tf_op jit(solution)/shard_map/all_to_all | solution.py:867
  14.6 3.5 %collective-permute-start.1 = (f32[816,128]{1,0:T(8,128)S(1)}, f32[816,128]{1,0:T(8,128)S(1)}, u32[]{:S(2)}, u32[]{:S(2)}) collective-permute-start(f32[816,128]{1,0:T(8,128)S(1)} %get-tuple-element.73), channel_id=1, source_target_pairs={{1,2},{3,4},{5,6},{7,8},{9,10},{11,12},{13,14},{2,1},{4,3},{6,5},{... | collective-permute-start | bytes 1253384 | tf_op jit(solution)/shard_map/ppermute | solution.py:856
  18.2 0.1 collective-permute-start.2
  18.3 11.0 %collective-permute-done.1.msg = f32[816,128]{1,0:T(8,128)S(1)} collective-permute-done((f32[816,128]{1,0:T(8,128)S(1)}, f32[816,128]{1,0:T(8,128)S(1)}, u32[]{:S(2)}, u32[]{:S(2)}) %collective-permute-start.1) | collective-permute-done | bytes 417824 | tf_op jit(solution)/shard_map/ppermute | solution.py:856
  29.3 0.1 meet.1.after_this.rest_0_
  29.4 0.0 all-to-all-done.parts
  29.4 0.6 %prepare.1 = (f32[6,3,4,16,128]{4,3,2,1,0:T(8,128)S(1)}, f32[128,128]{1,0:T(8,128)S(1)}) custom-call(f32[8,72,128]{2,1,0:T(8,128)S(1)} %all-to-all-done.parts, f32[16,128]{1,0:T(8,128)S(1)} %get-tuple-element.65.loads, f32[16,128]{1,0:T(8,128)S(1)} %get-tuple-element.66.steps_table, f32[128,128]{1,0:T(8,128)S(1)} %meet.1.after_this.rest_0_), custom_call_target="tpu_custom_call" | custom-call | flops 1 | bytes 1 | tf_op jit(solution)/shard_map/prepare/pallas_call | solution.py:775
  30.1 0.0 collective-permute-done.2.msg
  30.1 0.3 near0.1
  30.3 0.1 collective-permute-start.3
  30.4 0.6 %far0.1 = (f32[3,2,144,128]{3,2,1,0:T(8,128)S(1)}, f32[6,2,144,128]{3,2,1,0:T(8,128)S(1)}, f32[6,2,128,128]{3,2,1,0:T(8,128)S(1)}, f32[3,128,128]{2,1,0:T(8,128)S(1)}, f32[3,128,128]{2,1,0:T(8,128)S(1)}) custom-call(f32[3,2,144,128]{3,2,1,0:T(8,128)S(1)} %get-tuple-element.77.V0, ...), custom_call_target="tpu_custom_call", output_to_operand_aliasing={{0}: (0, {}), {1}: (1, {}), {2}: (2, {})} | custom-call | flops 1 | bytes 1 | tf_op jit(solution)/shard_map/far0/pallas_call | solution.py:775
  31.1 0.8 %collective-permute-done.3.msg = f32[3,128,128]{2,1,0:T(8,128)S(1)} collective-permute-done((f32[3,128,128]{2,1,0:T(8,128)S(1)}, f32[3,128,128]{2,1,0:T(8,128)S(1)}, u32[]{:S(2)}, u32[]{:S(2)}) %collective-permute-start.3) | collective-permute-done | bytes 196640 | tf_op jit(solution)/shard_map/ppermute | solution.py:905
  31.9 0.3 near1.1
  32.1 0.2 collective-permute-start.4
  32.3 2.7 %collective-permute-start.5 = (f32[3,128,128]{2,1,0:T(8,128)S(1)}, f32[3,128,128]{2,1,0:T(8,128)S(1)}, u32[]{:S(2)}, u32[]{:S(2)}) collective-permute-start(f32[3,128,128]{2,1,0:T(8,128)S(1)} %get-tuple-element.95), channel_id=1, source_target_pairs={{1,2},{3,4},{5,6},{7,8},{9,10},{11,12},{13,14},{2,1},{4,3},{6,5},{... | collective-permute-start | bytes 589832 | tf_op jit(solution)/shard_map/ppermute | solution.py:923
  35.0 0.6 %far1.1 = (f32[3,2,144,128]{3,2,1,0:T(8,128)S(1)}, f32[6,2,144,128]{3,2,1,0:T(8,128)S(1)}, f32[6,2,128,128]{3,2,1,0:T(8,128)S(1)}, f32[3,128,128]{2,1,0:T(8,128)S(1)}, f32[3,128,128]{2,1,0:T(8,128)S(1)}) custom-call(f32[3,2,144,128]{3,2,1,0:T(8,128)S(1)} %get-tuple-element.84.V0, ...), custom_call_target="tpu_custom_call", output_to_operand_aliasing={{0}: (0, {}), {1}: (1, {}), {2}: (2, {})} | custom-call | flops 1 | bytes 1 | tf_op jit(solution)/shard_map/far1/pallas_call | solution.py:775
  35.6 0.0 collective-permute-done.4.msg
  35.6 0.3 near2.1
  35.9 0.1 collective-permute-start.6
  36.0 4.1 %collective-permute-start.7 = (f32[3,128,128]{2,1,0:T(8,128)S(1)}, f32[3,128,128]{2,1,0:T(8,128)S(1)}, u32[]{:S(2)}, u32[]{:S(2)}) collective-permute-start(f32[3,128,128]{2,1,0:T(8,128)S(1)} %get-tuple-element.104), channel_id=1, source_target_pairs={{1,2},{3,4},{5,6},{7,8},{9,10},{11,12},{13,14},{2,1},{4,3},{6,5},{... | collective-permute-start | bytes 589832 | tf_op jit(solution)/shard_map/ppermute | solution.py:923
  40.1 1.2 %collective-permute-done.5.msg = f32[3,128,128]{2,1,0:T(8,128)S(1)} collective-permute-done((f32[3,128,128]{2,1,0:T(8,128)S(1)}, f32[3,128,128]{2,1,0:T(8,128)S(1)}, u32[]{:S(2)}, u32[]{:S(2)}) %collective-permute-start.5) | collective-permute-done | bytes 196640 | tf_op jit(solution)/shard_map/ppermute | solution.py:923
  41.4 0.6 %far2.1 = (f32[3,2,144,128]{3,2,1,0:T(8,128)S(1)}, f32[6,2,144,128]{3,2,1,0:T(8,128)S(1)}, f32[6,2,128,128]{3,2,1,0:T(8,128)S(1)}, f32[3,128,128]{2,1,0:T(8,128)S(1)}, f32[3,128,128]{2,1,0:T(8,128)S(1)}) custom-call(f32[3,2,144,128]{3,2,1,0:T(8,128)S(1)} %get-tuple-element.92.V0, ...), custom_call_target="tpu_custom_call", output_to_operand_aliasing={{0}: (0, {}), {1}: (1, {}), {2}: (2, {})} | custom-call | flops 1 | bytes 1 | tf_op jit(solution)/shard_map/far2/pallas_call | solution.py:775
  42.0 0.0 collective-permute-done.6.msg
  42.0 0.3 near3.1
  42.3 0.1 collective-permute-start.8
  42.4 2.7 %collective-permute-start.9 = (f32[3,128,128]{2,1,0:T(8,128)S(1)}, f32[3,128,128]{2,1,0:T(8,128)S(1)}, u32[]{:S(2)}, u32[]{:S(2)}) collective-permute-start(f32[3,128,128]{2,1,0:T(8,128)S(1)} %get-tuple-element.113), channel_id=1, source_target_pairs={{1,2},{3,4},{5,6},{7,8},{9,10},{11,12},{13,14},{2,1},{4,3},{6,5},{... | collective-permute-start | bytes 589832 | tf_op jit(solution)/shard_map/ppermute | solution.py:923
  45.1 0.5 collective-permute-done.7.msg
  45.6 0.6 %far3.1 = (f32[3,2,144,128]{3,2,1,0:T(8,128)S(1)}, f32[6,2,144,128]{3,2,1,0:T(8,128)S(1)}, f32[6,2,128,128]{3,2,1,0:T(8,128)S(1)}, f32[3,128,128]{2,1,0:T(8,128)S(1)}, f32[3,128,128]{2,1,0:T(8,128)S(1)}) custom-call(f32[3,2,144,128]{3,2,1,0:T(8,128)S(1)} %get-tuple-element.101.V0, ...), custom_call_target="tpu_custom_call", output_to_operand_aliasing={{0}: (0, {}), {1}: (1, {}), {2}: (2, {})} | custom-call | flops 1 | bytes 1 | tf_op jit(solution)/shard_map/far3/pallas_call | solution.py:775
  46.2 0.0 collective-permute-done.8.msg
  46.2 0.3 near4.1
  46.5 0.1 collective-permute-start.10
  46.6 3.7 %collective-permute-start.11 = (f32[3,128,128]{2,1,0:T(8,128)S(1)}, f32[3,128,128]{2,1,0:T(8,128)S(1)}, u32[]{:S(2)}, u32[]{:S(2)}) collective-permute-start(f32[3,128,128]{2,1,0:T(8,128)S(1)} %get-tuple-element.122), channel_id=1, source_target_pairs={{1,2},{3,4},{5,6},{7,8},{9,10},{11,12},{13,14},{2,1},{4,3},{6,5},{... | collective-permute-start | bytes 589832 | tf_op jit(solution)/shard_map/ppermute | solution.py:923
  50.3 1.1 %collective-permute-done.9.msg = f32[3,128,128]{2,1,0:T(8,128)S(1)} collective-permute-done((f32[3,128,128]{2,1,0:T(8,128)S(1)}, f32[3,128,128]{2,1,0:T(8,128)S(1)}, u32[]{:S(2)}, u32[]{:S(2)}) %collective-permute-start.9) | collective-permute-done | bytes 196640 | tf_op jit(solution)/shard_map/ppermute | solution.py:923
  51.5 0.4 far4.1
  51.9 0.0 collective-permute-done.10.msg
  51.9 0.2 near5.1
  52.1 3.6 %collective-permute-done.11.msg = f32[3,128,128]{2,1,0:T(8,128)S(1)} collective-permute-done((f32[3,128,128]{2,1,0:T(8,128)S(1)}, f32[3,128,128]{2,1,0:T(8,128)S(1)}, u32[]{:S(2)}, u32[]{:S(2)}) %collective-permute-start.11) | collective-permute-done | bytes 196640 | tf_op jit(solution)/shard_map/ppermute | solution.py:923
  55.8 1.3 %last.1 = (f32[3,2,144,128]{3,2,1,0:T(8,128)S(1)}, f32[6,2,144,128]{3,2,1,0:T(8,128)S(1)}, f32[6,2,128,128]{3,2,1,0:T(8,128)S(1)}, f32[3,2,128,128]{3,2,1,0:T(8,...) custom-call(f32[3,2,144,128]{3,2,1,0:T(8,128)S(1)} %get-tuple-elemen, ...), custom_call_target="tpu_custom_call", output_to_operand_aliasing={{0}: (0, {}), {1}: (1, {}), {2}: (2, {})} | custom-call | flops 1 | bytes 1 | tf_op jit(solution)/shard_map/last/pallas_call | solution.py:775
Async XLA Ops:
  1.5 5.9 %collective-permute-start = (f32[8,1920]{1,0:T(8,128)S(1)}, f32[8,1920]{1,0:T(8,128)S(1)}, u32[]{:S(2)}, u32[]{:S(2)}) collective-permute-start(f32[8,1920]{1,0:T(8,128)S(1)} %get-tuple-element.71.own), channel_id=1, source_target_pairs={{0,8},{1,9},{2,10},{3,11},{4,12},{5,13},{6,14},{7,15},{16,24},{17,... | collective-permute-start | bytes 184328 | tf_op jit(solution)/shard_map/ppermute | solution.py:813
  4.7 0.7 %copy-start = (f32[3,128,128]{2,1,0:T(8,128)}, f32[3,128,128]{2,1,0:T(8,128)S(1)}, u32[]{:S(2)}) copy-start(f32[3,128,128]{2,1,0:T(8,128)S(1)} %get-tuple-element.76) | copy-start | bytes 589828
  8.3 21.1 %all-to-all-start = ((f32[8,72,128]{2,1,0:T(8,128)}), f32[8,72,128]{2,1,0:T(8,128)S(1)}, u32[]{:S(2)}, u32[]{:S(2)}) async-start(f32[8,72,128]{2,1,0:T(8,128)} %split.1), calls=%async_computation | async-start | bytes 589824 | tf_op jit(solution)/shard_map/all_to_all | solution.py:867
  14.6 14.7 %collective-permute-start.1 = (f32[816,128]{1,0:T(8,128)S(1)}, f32[816,128]{1,0:T(8,128)S(1)}, u32[]{:S(2)}, u32[]{:S(2)}) collective-permute-start(f32[816,128]{1,0:T(8,128)S(1)} %get-tuple-element.73), channel_id=1, source_target_pairs={{1,2},{3,4},{5,6},{7,8},{9,10},{11,12},{13,14},{2,1},{4,3},{6,5},{... | collective-permute-start | bytes 1253384 | tf_op jit(solution)/shard_map/ppermute | solution.py:856
  18.2 11.9 %collective-permute-start.2 = (f32[3,128,128]{2,1,0:T(8,128)}, f32[3,128,128]{2,1,0:T(8,128)S(1)}, u32[]{:S(2)}, u32[]{:S(2)}) collective-permute-start(f32[3,128,128]{2,1,0:T(8,128)} %copy-done), channel_id=1, source_target_pairs={{0,1},{1,0},{2,3},{3,2},{4,5},{5,4},{6,7},{7,6},{8,9},{9,8},{10,11... | collective-permute-start | bytes 589832 | tf_op jit(solution)/shard_map/ppermute | solution.py:857
  30.3 1.5 %collective-permute-start.3 = (f32[3,128,128]{2,1,0:T(8,128)S(1)}, f32[3,128,128]{2,1,0:T(8,128)S(1)}, u32[]{:S(2)}, u32[]{:S(2)}) collective-permute-start(f32[3,128,128]{2,1,0:T(8,128)S(1)} %get-tuple-element.83), channel_id=1, source_target_pairs={{0,1},{1,0},{2,3},{3,2},{4,5},{5,4},{6,7},{7,6},{8,9},{9,8},{10,11... | collective-permute-start | bytes 589832 | tf_op jit(solution)/shard_map/ppermute | solution.py:905
  32.1 3.5 %collective-permute-start.4 = (f32[3,128,128]{2,1,0:T(8,128)S(1)}, f32[3,128,128]{2,1,0:T(8,128)S(1)}, u32[]{:S(2)}, u32[]{:S(2)}) collective-permute-start(f32[3,128,128]{2,1,0:T(8,128)S(1)} %get-tuple-element.91), channel_id=1, source_target_pairs={{0,1},{1,0},{2,3},{3,2},{4,5},{5,4},{6,7},{7,6},{8,9},{9,8},{10,11... | collective-permute-start | bytes 589832 | tf_op jit(solution)/shard_map/ppermute | solution.py:905
  32.3 9.1 %collective-permute-start.5 = (f32[3,128,128]{2,1,0:T(8,128)S(1)}, f32[3,128,128]{2,1,0:T(8,128)S(1)}, u32[]{:S(2)}, u32[]{:S(2)}) collective-permute-start(f32[3,128,128]{2,1,0:T(8,128)S(1)} %get-tuple-element.95), channel_id=1, source_target_pairs={{1,2},{3,4},{5,6},{7,8},{9,10},{11,12},{13,14},{2,1},{4,3},{6,5},{... | collective-permute-start | bytes 589832 | tf_op jit(solution)/shard_map/ppermute | solution.py:923
  35.9 6.1 %collective-permute-start.6 = (f32[3,128,128]{2,1,0:T(8,128)S(1)}, f32[3,128,128]{2,1,0:T(8,128)S(1)}, u32[]{:S(2)}, u32[]{:S(2)}) collective-permute-start(f32[3,128,128]{2,1,0:T(8,128)S(1)} %get-tuple-element.100), channel_id=1, source_target_pairs={{0,1},{1,0},{2,3},{3,2},{4,5},{5,4},{6,7},{7,6},{8,9},{9,8},{10,11... | collective-permute-start | bytes 589832 | tf_op jit(solution)/shard_map/ppermute | solution.py:905
  36.0 9.6 %collective-permute-start.7 = (f32[3,128,128]{2,1,0:T(8,128)S(1)}, f32[3,128,128]{2,1,0:T(8,128)S(1)}, u32[]{:S(2)}, u32[]{:S(2)}) collective-permute-start(f32[3,128,128]{2,1,0:T(8,128)S(1)} %get-tuple-element.104), channel_id=1, source_target_pairs={{1,2},{3,4},{5,6},{7,8},{9,10},{11,12},{13,14},{2,1},{4,3},{6,5},{... | collective-permute-start | bytes 589832 | tf_op jit(solution)/shard_map/ppermute | solution.py:923
  42.3 3.9 %collective-permute-start.8 = (f32[3,128,128]{2,1,0:T(8,128)S(1)}, f32[3,128,128]{2,1,0:T(8,128)S(1)}, u32[]{:S(2)}, u32[]{:S(2)}) collective-permute-start(f32[3,128,128]{2,1,0:T(8,128)S(1)} %get-tuple-element.109), channel_id=1, source_target_pairs={{0,1},{1,0},{2,3},{3,2},{4,5},{5,4},{6,7},{7,6},{8,9},{9,8},{10,11... | collective-permute-start | bytes 589832 | tf_op jit(solution)/shard_map/ppermute | solution.py:905
  42.4 9.1 %collective-permute-start.9 = (f32[3,128,128]{2,1,0:T(8,128)S(1)}, f32[3,128,128]{2,1,0:T(8,128)S(1)}, u32[]{:S(2)}, u32[]{:S(2)}) collective-permute-start(f32[3,128,128]{2,1,0:T(8,128)S(1)} %get-tuple-element.113), channel_id=1, source_target_pairs={{1,2},{3,4},{5,6},{7,8},{9,10},{11,12},{13,14},{2,1},{4,3},{6,5},{... | collective-permute-start | bytes 589832 | tf_op jit(solution)/shard_map/ppermute | solution.py:923
  46.5 5.4 %collective-permute-start.10 = (f32[3,128,128]{2,1,0:T(8,128)S(1)}, f32[3,128,128]{2,1,0:T(8,128)S(1)}, u32[]{:S(2)}, u32[]{:S(2)}) collective-permute-start(f32[3,128,128]{2,1,0:T(8,128)S(1)} %get-tuple-element.118), channel_id=1, source_target_pairs={{0,1},{1,0},{2,3},{3,2},{4,5},{5,4},{6,7},{7,6},{8,9},{9,8},{10,11... | collective-permute-start | bytes 589832 | tf_op jit(solution)/shard_map/ppermute | solution.py:905
  46.6 9.2 %collective-permute-start.11 = (f32[3,128,128]{2,1,0:T(8,128)S(1)}, f32[3,128,128]{2,1,0:T(8,128)S(1)}, u32[]{:S(2)}, u32[]{:S(2)}) collective-permute-start(f32[3,128,128]{2,1,0:T(8,128)S(1)} %get-tuple-element.122), channel_id=1, source_target_pairs={{1,2},{3,4},{5,6},{7,8},{9,10},{11,12},{13,14},{2,1},{4,3},{6,5},{... | collective-permute-start | bytes 589832 | tf_op jit(solution)/shard_map/ppermute | solution.py:923

commit v8 on v7

--- a/solution.py
+++ b/solution.py
@@ -50,7 +50,7 @@
 
     def rows(self, at):
         plane, out = at
-        return pl.ds((self.first + plane) * self.shape[1] + out.start, out.size)
+        return pl.ds(self.first * self.shape[1] + plane * self.shape[1] + out.start, out.size)
 
     def __getitem__(self, at):
         return self.ref[self.rows(at)]
@@ -458,12 +458,7 @@
     table[...] = jnp.zeros(table.shape, jnp.float32)
     table[0:16, :] = steps_table[...]
     columns = table[...].T
-    trucks = 6 * across
-    msg_far[trucks : trucks + slots, :] = loads[...]
-    for i, at in enumerate((0, 8)):
-        first_row = trucks + (1 + i) * slots
-        column = columns[0:slots, at : at + 1]
-        msg_far[first_row : first_row + slots, :] = jnp.broadcast_to(column, loads.shape)
+    entry, cell = (jnp.broadcast_to(columns[0:slots, at : at + 1], loads.shape) for at in (0, 8))
     for copy in copies[:6]:
         copy.wait()
     layer = layer_ref[...]
@@ -500,29 +495,32 @@
     for copy in copies[6:15]:
         copy.wait()
     even, _, _ = place()
-    now, then = Planes(msg_far, 0, across), Planes(msg_far, 3, across)
+
+    def send(side, near, far, early):
+        to = msg_far.at[side]
+        near(V, S, coef_ref, msg_near, None, 0)
+        far(V, S, coef_ref, Planes(to, 0, across), None, 0)
+        inner(V, S, coef_ref, None, 0)
+        for i, block in enumerate((loads[...], entry, cell)):
+            first_row = 6 * across + i * slots
+            to[first_row : first_row + slots, :] = block
+        for copy in copies[15:]:
+            copy.wait()
+        early(Planes(to, 3, across))
 
     @pl.when(even)
     def _():
-        pre_ahead(V, S, coef_ref, msg_near, None, 0)
-        pre_behind(V, S, coef_ref, now, None, 0)
+        send(
+            0, pre_ahead, pre_behind,
+            lambda out: early_behind(V, S, R, coef_ref, None, 0, out, W, None, 0),
+        )
 
     @pl.when(jnp.logical_not(even))
     def _():
-        pre_behind(V, S, coef_ref, msg_near, None, 0)
-        pre_ahead(V, S, coef_ref, now, None, 0)
-
-    inner(V, S, coef_ref, None, 0)
-    for copy in copies[15:]:
-        copy.wait()
-
-    @pl.when(even)
-    def _():
-        early_behind(V, S, R, coef_ref, None, 0, then, W, None, 0)
-
-    @pl.when(jnp.logical_not(even))
-    def _():
-        early_ahead(V, S, R, coef_ref, then, W, None, 0)
+        send(
+            1, pre_behind, pre_ahead,
+            lambda out: early_ahead(V, S, R, coef_ref, out, W, None, 0),
+        )
 
 
 def near_kernel(step, window, V0, S0, R0, coef_ref, force, surface, msg, V, S, R, *rest):
@@ -549,7 +547,7 @@
 
 def meet_kernel(across, msg, loads, load, rows_out):
     slots = loads.shape[0]
-    rows, entry, cell = (msg[6 * across + i * slots : 6 * across + (i + 1) * slots, :] for i in range(3))
+    rows, entry, cell = (msg[1, 6 * across + i * slots : 6 * across + (i + 1) * slots, :] for i in range(3))
     for slot in range(slots):
         rows = jnp.where(entry == float(slot), loads[slot : slot + 1, :], rows)
     rows_out[...] = jnp.zeros(rows_out.shape, jnp.float32)
@@ -565,7 +563,10 @@
     across = R.shape[2]
     even, _, _ = place()
     here, then = force.at[step], force.at[step + 1]
-    got = Planes(msg, 3 * step, across) if step < 2 else msg
+
+    def got(side):
+        return Planes(msg.at[side], 3 * step, across) if step < 2 else msg
+
     if step == 0:
         missing, load = None, other
         G, W, A = rest[-3:]
@@ -581,7 +582,7 @@
         else:
             respond = lambda: response_ahead(V, S, coef_ref, D, W)
         behind_bond(
-            V, S, R, coef_ref, here, surface, got, missing, G, step, window, 2, respond
+            V, S, R, coef_ref, here, surface, got(0), missing, G, step, window, 2, respond
         )
         pre_behind(V, S, coef_ref, None, then, window)
 
@@ -592,7 +593,7 @@
         else:
             respond = lambda: response_behind(V, S, coef_ref, D, W)
         ahead_bond(
-            V, S, R, coef_ref, here, surface, got, missing, G, step, window, 2, respond
+            V, S, R, coef_ref, here, surface, got(1), missing, G, step, window, 2, respond
         )
         pre_ahead(V, S, coef_ref, None, then, window)
 
@@ -844,7 +845,7 @@
         start_kernel,
         in_hbm(velocity, stress, memory, layer[None, :], *tables) + (in_vmem(loads), in_vmem(steps_table)),
         (ANYWHERE,) * 9 + (WHOLE,) * 2,
-        (v_type, s_type, r_type, c_type, m_type, pltpu.VMEM((6 * across + 3 * slots, depth), f32)),
+        (v_type, s_type, r_type, c_type, m_type, pltpu.VMEM((2, 6 * across + 3 * slots, depth), f32)),
         (WHOLE,) * 6,
         scratch=(
             work, pltpu.VMEM((depth, depth), f32), pltpu.VMEM((1, depth), jnp.int32),
@@ -853,7 +854,8 @@
         name="start",
         cost=8 * 1024 * 1024,
     )
-    msg_far = lax.ppermute(msg_far, "line", far)
+    pairs = [[i, (i + 1) % tiles] for i in range(1, tiles, 2)]
+    msg_far = lax.all_to_all(msg_far, "line", 0, 0, axis_index_groups=pairs, tiled=True)
     msg_near = lax.ppermute(msg_near, "line", near)
     parts = call(
         functools.partial(split_kernel, panel, slots),

time: 57.6 us -> 59.9 us (1.040)
  waiting for transfers between devices: 20.3 us -> 21.5 us
  local copies, waits for them, and re-layouts: 0.67 us -> 1.59 us
    ppermute x1 -> x0, waiting for transfers between devices: 11 us -> none  [body(): msg_far = lax.ppermute(msg_far, 'line', far)]
    all_to_all x1, waiting for transfers between devices: 0.01 us -> 5.51 us  [body(): lax.all_to_all(parts, 'line', 0, 0, axis_index_groups=groups, tiled=True)]
    all_to_all x0 -> x1, waiting for transfers between devices: none -> 4.39 us  [body(): lax.all_to_all(msg_far, 'line', 0, 0, axis_index_groups=pairs, tiled=True)]
    all_to_all x0 -> x1, starting transfers between devices: none -> 3.54 us  [body(): lax.all_to_all(msg_far, 'line', 0, 0, axis_index_groups=pairs, tiled=True)]
    ppermute x1 -> x0, starting transfers between devices: 3.53 us -> none  [body(): msg_far = lax.ppermute(msg_far, 'line', far)]
    ppermute x1, waiting for transfers between devices: 1.99 us -> 4.86 us  [ahead_by(): lax.ppermute(x, 'line', [(i, i + distance) for i in range(tiles - distanc...]
    all_to_all x1, starting transfers between devices: 6.3 us -> 5.19 us  [body(): lax.all_to_all(parts, 'line', 0, 0, axis_index_groups=groups, tiled=True)]
    ppermute x5, starting transfers between devices: 0.45 us -> 1.44 us  [body(): msg_near = lax.ppermute(msg[0], 'line', near)]
  transfers between devices with their start and end apart: 13 -> 13, of which waited for: 7 -> 7; matrix products, arithmetic and copies ran while one was open for 0% -> 0% of each run, Pallas kernels for 12% -> 10%
where the time goes in v8:
time: 59.9 us; the launch traced here: 59.1 us
  starting transfers between devices  24.9 us (42%)
  waiting for transfers between devices  21.5 us (36%)
  Pallas kernels  10.3 us (17%)
  local copies, waits for them, and re-layouts  1.59 us (3%)
  between operations  0.85 us (1%)
    ppermute x4, starting transfers between devices, body(): early = lax.ppermute(msg[0], 'line', far)  13.5 us
    pallas_call x17, Pallas kernels, call(): pl.pallas_call(kernel, out_shape=outs, in_specs=specs, out_specs=out_spec...  10.3 us
    ppermute x4, waiting for transfers between devices, body(): early = lax.ppermute(msg[0], 'line', far)  6.28 us
    all_to_all x1, waiting for transfers between devices, body(): lax.all_to_all(parts, 'line', 0, 0, axis_index_groups=groups, tiled=True)  5.51 us
    all_to_all x1, starting transfers between devices, body(): lax.all_to_all(parts, 'line', 0, 0, axis_index_groups=groups, tiled=True)  5.19 us
    ppermute x1, waiting for transfers between devices, ahead_by(): lax.ppermute(x, 'line', [(i, i + distance) for i in range(tiles - distanc...  4.86 us
    all_to_all x1, waiting for transfers between devices, body(): lax.all_to_all(msg_far, 'line', 0, 0, axis_index_groups=pairs, tiled=True)  4.39 us
    all_to_all x1, starting transfers between devices, body(): lax.all_to_all(msg_far, 'line', 0, 0, axis_index_groups=pairs, tiled=True)  3.54 us
  transfers between devices with their start and end apart: 13, of which 7 were waited for; matrix products, arithmetic and copies ran while one was open for 0% of the time, Pallas kernels for 10%

profile of v8, /device:TPU:17, one launch (start us, length us, event | category | flops | bytes accessed | tf_op | source)
XLA Modules:
  0.0 59.1 jit_solution(9602972999524777492)
XLA Ops:
  0.6 0.9 %pack.1 = (f32[8,1920]{1,0:T(8,128)S(1)}, f32[16,128]{1,0:T(8,128)S(1)}, f32[16,128]{1,0:T(8,128)S(1)}, s32[1,8]{1,0:T(1,128)S(1)}) custom-call(f32[8,1536]{1,0:T(8,128)} %bitcast.3, f32[16,128]{1,0:T(8,128)} %loads_in.1, s32[6,16]{1,0:T(8,128)} %entries_in.1, s32[6,16]{1,0:T(8,128)} %cells_in.1, s32[1,8]{1,0:T(1,128)} %bitcast.4), custom_call_target="tpu_custom_call" | custom-call | flops 1 | bytes 1 | tf_op jit(solution)/shard_map/pack/pallas_call | solution.py:776
  1.5 1.9 %start.1 = (f32[3,2,144,128]{3,2,1,0:T(8,128)S(1)}, f32[6,2,144,128]{3,2,1,0:T(8,128)S(1)}, f32[6,2,128,128]{3,2,1,0:T(8,128)S(1)}, f32[16,128]{1,0:T(8,128)S(1)...) custom-call(f32[3,2,128,128]{3,2,1,0:T(8,128)} %velocity.1, f32[6,2,128,128]{3,2,1,0:T(8,128)} %stress.1, ...), custom_call_target="tpu_custom_call" | custom-call | flops 8388608 | bytes 8388608 | tf_op jit(solution)/shard_map/start/pallas_call | solution.py:776
  3.4 0.0 copy-start
  3.4 0.9 %copy-done = f32[2,816,128]{2,1,0:T(8,128)} copy-done((f32[2,816,128]{2,1,0:T(8,128)}, f32[2,816,128]{2,1,0:T(8,128)S(1)}, u32[]{:S(2)}) %copy-start) | copy-done | bytes 835608
  4.4 0.0 copy-start.1
  4.4 0.7 %copy-done.1 = f32[3,128,128]{2,1,0:T(8,128)} copy-done((f32[3,128,128]{2,1,0:T(8,128)}, f32[3,128,128]{2,1,0:T(8,128)S(1)}, u32[]{:S(2)}) %copy-start.1) | copy-done | bytes 196632
  5.0 3.5 %all-to-all-start.1 = ((f32[2,816,128]{2,1,0:T(8,128)}), f32[2,816,128]{2,1,0:T(8,128)S(1)}, u32[]{:S(2)}, u32[]{:S(2)}) async-start(f32[2,816,128]{2,1,0:T(8,128)} %copy-done), calls=%async_computation.1 | async-start | bytes 1671168 | tf_op jit(solution)/shard_map/all_to_all | solution.py:858
  8.6 1.3 %collective-permute-start = (f32[8,1920]{1,0:T(8,128)S(1)}, f32[8,1920]{1,0:T(8,128)S(1)}, u32[]{:S(2)}, u32[]{:S(2)}) collective-permute-start(f32[8,1920]{1,0:T(8,128)S(1)} %get-tuple-element.71.own), channel_id=1, source_target_pairs={{0,8},{1,9},{2,10},{3,11},{4,12},{5,13},{6,14},{7,15},{16,24},{17,... | collective-permute-start | bytes 184328 | tf_op jit(solution)/shard_map/ppermute | solution.py:814
  9.9 4.9 %collective-permute-done.behind = f32[8,1920]{1,0:T(8,128)S(1)} collective-permute-done((f32[8,1920]{1,0:T(8,128)S(1)}, f32[8,1920]{1,0:T(8,128)S(1)}, u32[]{:S(2)}, u32[]{:S(2)}) %collective-permute-start) | collective-permute-done | bytes 61472 | tf_op jit(solution)/shard_map/ppermute | solution.py:814
  14.7 0.9 %split.1 = f32[8,72,128]{2,1,0:T(8,128)} custom-call(f32[8,1920]{1,0:T(8,128)S(1)} %get-tuple-element.71.own, f32[8,1920]{1,0:T(8,128)S(1)} %collective-permute-done.behind, s32[1,8]{1,0:T(1,128)S(1)} %get-tuple-element.72.cells, f32[16,128]{1,0:T(8,128)S(1)} %get-tuple-element.70.after_this.coef_ref), custom_call_target="tpu_custom_call" | custom-call | flops 1 | bytes 1 | tf_op jit(solution)/shard_map/split/pallas_call | solution.py:776
  15.7 4.4 %all-to-all-done.1.msg = f32[2,816,128]{2,1,0:T(8,128)S(1)} async-done(((f32[2,816,128]{2,1,0:T(8,128)}), f32[2,816,128]{2,1,0:T(8,128)S(1)}, u32[]{:S(2)}, u32[]{:S(2)}) %all-to-all-start.1) | async-done | bytes 835616 | tf_op jit(solution)/shard_map/all_to_all | solution.py:858
  20.1 5.2 %all-to-all-start = ((f32[8,72,128]{2,1,0:T(8,128)}), f32[8,72,128]{2,1,0:T(8,128)S(1)}, u32[]{:S(2)}, u32[]{:S(2)}) async-start(f32[8,72,128]{2,1,0:T(8,128)} %split.1), calls=%async_computation | async-start | bytes 589824 | tf_op jit(solution)/shard_map/all_to_all | solution.py:869
  25.3 0.0 collective-permute-start.1
  25.3 0.1 meet.1.after_this.rest_0_
  25.4 5.5 %all-to-all-done.parts = f32[8,72,128]{2,1,0:T(8,128)S(1)} async-done(((f32[8,72,128]{2,1,0:T(8,128)}), f32[8,72,128]{2,1,0:T(8,128)S(1)}, u32[]{:S(2)}, u32[]{:S(2)}) %all-to-all-start) | async-done | bytes 294944 | tf_op jit(solution)/shard_map/all_to_all | solution.py:869
  30.9 0.6 %prepare.1 = (f32[6,3,4,16,128]{4,3,2,1,0:T(8,128)S(1)}, f32[128,128]{1,0:T(8,128)S(1)}) custom-call(f32[8,72,128]{2,1,0:T(8,128)S(1)} %all-to-all-done.parts, f32[16,128]{1,0:T(8,128)S(1)} %get-tuple-element.65.loads, f32[16,128]{1,0:T(8,128)S(1)} %get-tuple-element.66.steps_table, f32[128,128]{1,0:T(8,128)S(1)} %meet.1.after_this.rest_0_), custom_call_target="tpu_custom_call" | custom-call | flops 1 | bytes 1 | tf_op jit(solution)/shard_map/prepare/pallas_call | solution.py:776
  31.5 0.0 collective-permute-done.1.msg
  31.5 0.3 near0.1
  31.8 0.8 %collective-permute-start.2 = (f32[3,128,128]{2,1,0:T(8,128)S(1)}, f32[3,128,128]{2,1,0:T(8,128)S(1)}, u32[]{:S(2)}, u32[]{:S(2)}) collective-permute-start(f32[3,128,128]{2,1,0:T(8,128)S(1)} %get-tuple-element.83), channel_id=1, source_target_pairs={{0,1},{1,0},{2,3},{3,2},{4,5},{5,4},{6,7},{7,6},{8,9},{9,8},{10,11... | collective-permute-start | bytes 589832 | tf_op jit(solution)/shard_map/ppermute | solution.py:907
  32.6 0.6 %far0.1 = (f32[3,2,144,128]{3,2,1,0:T(8,128)S(1)}, f32[6,2,144,128]{3,2,1,0:T(8,128)S(1)}, f32[6,2,128,128]{3,2,1,0:T(8,128)S(1)}, f32[3,128,128]{2,1,0:T(8,128)S(1)}, f32[3,128,128]{2,1,0:T(8,128)S(1)}) custom-call(f32[3,2,144,128]{3,2,1,0:T(8,128)S(1)} %get-tuple-element.77.V0, ...), custom_call_target="tpu_custom_call", output_to_operand_aliasing={{0}: (0, {}), {1}: (1, {}), {2}: (2, {})} | custom-call | flops 1 | bytes 1 | tf_op jit(solution)/shard_map/far0/pallas_call | solution.py:776
  33.3 0.4 collective-permute-done.2.msg
  33.7 0.3 near1.1
  33.9 0.4 collective-permute-start.3
  34.4 3.2 %collective-permute-start.4 = (f32[3,128,128]{2,1,0:T(8,128)S(1)}, f32[3,128,128]{2,1,0:T(8,128)S(1)}, u32[]{:S(2)}, u32[]{:S(2)}) collective-permute-start(f32[3,128,128]{2,1,0:T(8,128)S(1)} %get-tuple-element.95), channel_id=1, source_target_pairs={{1,2},{3,4},{5,6},{7,8},{9,10},{11,12},{13,14},{2,1},{4,3},{6,5},{... | collective-permute-start | bytes 589832 | tf_op jit(solution)/shard_map/ppermute | solution.py:925
  37.5 0.6 %far1.1 = (f32[3,2,144,128]{3,2,1,0:T(8,128)S(1)}, f32[6,2,144,128]{3,2,1,0:T(8,128)S(1)}, f32[6,2,128,128]{3,2,1,0:T(8,128)S(1)}, f32[3,128,128]{2,1,0:T(8,128)S(1)}, f32[3,128,128]{2,1,0:T(8,128)S(1)}) custom-call(f32[3,2,144,128]{3,2,1,0:T(8,128)S(1)} %get-tuple-element.84.V0, ...), custom_call_target="tpu_custom_call", output_to_operand_aliasing={{0}: (0, {}), {1}: (1, {}), {2}: (2, {})} | custom-call | flops 1 | bytes 1 | tf_op jit(solution)/shard_map/far1/pallas_call | solution.py:776
  38.2 0.0 collective-permute-done.3.msg
  38.2 0.3 near2.1
  38.4 0.1 collective-permute-start.5
  38.5 3.4 %collective-permute-start.6 = (f32[3,128,128]{2,1,0:T(8,128)S(1)}, f32[3,128,128]{2,1,0:T(8,128)S(1)}, u32[]{:S(2)}, u32[]{:S(2)}) collective-permute-start(f32[3,128,128]{2,1,0:T(8,128)S(1)} %get-tuple-element.104), channel_id=1, source_target_pairs={{1,2},{3,4},{5,6},{7,8},{9,10},{11,12},{13,14},{2,1},{4,3},{6,5},{... | collective-permute-start | bytes 589832 | tf_op jit(solution)/shard_map/ppermute | solution.py:925
  41.9 1.5 %collective-permute-done.4.msg = f32[3,128,128]{2,1,0:T(8,128)S(1)} collective-permute-done((f32[3,128,128]{2,1,0:T(8,128)S(1)}, f32[3,128,128]{2,1,0:T(8,128)S(1)}, u32[]{:S(2)}, u32[]{:S(2)}) %collective-permute-start.4) | collective-permute-done | bytes 196640 | tf_op jit(solution)/shard_map/ppermute | solution.py:925
  43.4 0.6 %far2.1 = (f32[3,2,144,128]{3,2,1,0:T(8,128)S(1)}, f32[6,2,144,128]{3,2,1,0:T(8,128)S(1)}, f32[6,2,128,128]{3,2,1,0:T(8,128)S(1)}, f32[3,128,128]{2,1,0:T(8,128)S(1)}, f32[3,128,128]{2,1,0:T(8,128)S(1)}) custom-call(f32[3,2,144,128]{3,2,1,0:T(8,128)S(1)} %get-tuple-element.92.V0, ...), custom_call_target="tpu_custom_call", output_to_operand_aliasing={{0}: (0, {}), {1}: (1, {}), {2}: (2, {})} | custom-call | flops 1 | bytes 1 | tf_op jit(solution)/shard_map/far2/pallas_call | solution.py:776
  44.1 0.0 collective-permute-done.5.msg
  44.1 0.3 near3.1
  44.3 0.1 collective-permute-start.7
  44.4 3.2 %collective-permute-start.8 = (f32[3,128,128]{2,1,0:T(8,128)S(1)}, f32[3,128,128]{2,1,0:T(8,128)S(1)}, u32[]{:S(2)}, u32[]{:S(2)}) collective-permute-start(f32[3,128,128]{2,1,0:T(8,128)S(1)} %get-tuple-element.113), channel_id=1, source_target_pairs={{1,2},{3,4},{5,6},{7,8},{9,10},{11,12},{13,14},{2,1},{4,3},{6,5},{... | collective-permute-start | bytes 589832 | tf_op jit(solution)/shard_map/ppermute | solution.py:925
  47.6 0.0 collective-permute-done.6.msg
  47.6 0.6 %far3.1 = (f32[3,2,144,128]{3,2,1,0:T(8,128)S(1)}, f32[6,2,144,128]{3,2,1,0:T(8,128)S(1)}, f32[6,2,128,128]{3,2,1,0:T(8,128)S(1)}, f32[3,128,128]{2,1,0:T(8,128)S(1)}, f32[3,128,128]{2,1,0:T(8,128)S(1)}) custom-call(f32[3,2,144,128]{3,2,1,0:T(8,128)S(1)} %get-tuple-element.101.V0, ...), custom_call_target="tpu_custom_call", output_to_operand_aliasing={{0}: (0, {}), {1}: (1, {}), {2}: (2, {})} | custom-call | flops 1 | bytes 1 | tf_op jit(solution)/shard_map/far3/pallas_call | solution.py:776
  48.3 0.0 collective-permute-done.7.msg
  48.3 0.3 near4.1
  48.6 0.1 collective-permute-start.9
  48.6 3.7 %collective-permute-start.10 = (f32[3,128,128]{2,1,0:T(8,128)S(1)}, f32[3,128,128]{2,1,0:T(8,128)S(1)}, u32[]{:S(2)}, u32[]{:S(2)}) collective-permute-start(f32[3,128,128]{2,1,0:T(8,128)S(1)} %get-tuple-element.122), channel_id=1, source_target_pairs={{1,2},{3,4},{5,6},{7,8},{9,10},{11,12},{13,14},{2,1},{4,3},{6,5},{... | collective-permute-start | bytes 589832 | tf_op jit(solution)/shard_map/ppermute | solution.py:925
  52.4 1.2 %collective-permute-done.8.msg = f32[3,128,128]{2,1,0:T(8,128)S(1)} collective-permute-done((f32[3,128,128]{2,1,0:T(8,128)S(1)}, f32[3,128,128]{2,1,0:T(8,128)S(1)}, u32[]{:S(2)}, u32[]{:S(2)}) %collective-permute-start.8) | collective-permute-done | bytes 196640 | tf_op jit(solution)/shard_map/ppermute | solution.py:925
  53.5 0.4 far4.1
  54.0 0.0 collective-permute-done.9.msg
  54.0 0.2 near5.1
  54.2 3.6 %collective-permute-done.10.msg = f32[3,128,128]{2,1,0:T(8,128)S(1)} collective-permute-done((f32[3,128,128]{2,1,0:T(8,128)S(1)}, f32[3,128,128]{2,1,0:T(8,128)S(1)}, u32[]{:S(2)}, u32[]{:S(2)}) %collective-permute-start.10) | collective-permute-done | bytes 196640 | tf_op jit(solution)/shard_map/ppermute | solution.py:925
  57.8 1.3 %last.1 = (f32[3,2,144,128]{3,2,1,0:T(8,128)S(1)}, f32[6,2,144,128]{3,2,1,0:T(8,128)S(1)}, f32[6,2,128,128]{3,2,1,0:T(8,128)S(1)}, f32[3,2,128,128]{3,2,1,0:T(8,...) custom-call(f32[3,2,144,128]{3,2,1,0:T(8,128)S(1)} %get-tuple-elemen, ...), custom_call_target="tpu_custom_call", output_to_operand_aliasing={{0}: (0, {}), {1}: (1, {}), {2}: (2, {})} | custom-call | flops 1 | bytes 1 | tf_op jit(solution)/shard_map/last/pallas_call | solution.py:776
Async XLA Ops:
  3.4 0.9 %copy-start = (f32[2,816,128]{2,1,0:T(8,128)}, f32[2,816,128]{2,1,0:T(8,128)S(1)}, u32[]{:S(2)}) copy-start(f32[2,816,128]{2,1,0:T(8,128)S(1)} %get-tuple-element.73) | copy-start | bytes 2506756
  4.4 0.7 %copy-start.1 = (f32[3,128,128]{2,1,0:T(8,128)}, f32[3,128,128]{2,1,0:T(8,128)S(1)}, u32[]{:S(2)}) copy-start(f32[3,128,128]{2,1,0:T(8,128)S(1)} %get-tuple-element.76) | copy-start | bytes 589828
  5.0 15.0 %all-to-all-start.1 = ((f32[2,816,128]{2,1,0:T(8,128)}), f32[2,816,128]{2,1,0:T(8,128)S(1)}, u32[]{:S(2)}, u32[]{:S(2)}) async-start(f32[2,816,128]{2,1,0:T(8,128)} %copy-done), calls=%async_computation.1 | async-start | bytes 1671168 | tf_op jit(solution)/shard_map/all_to_all | solution.py:858
  8.6 6.2 %collective-permute-start = (f32[8,1920]{1,0:T(8,128)S(1)}, f32[8,1920]{1,0:T(8,128)S(1)}, u32[]{:S(2)}, u32[]{:S(2)}) collective-permute-start(f32[8,1920]{1,0:T(8,128)S(1)} %get-tuple-element.71.own), channel_id=1, source_target_pairs={{0,8},{1,9},{2,10},{3,11},{4,12},{5,13},{6,14},{7,15},{16,24},{17,... | collective-permute-start | bytes 184328 | tf_op jit(solution)/shard_map/ppermute | solution.py:814
  20.1 10.8 %all-to-all-start = ((f32[8,72,128]{2,1,0:T(8,128)}), f32[8,72,128]{2,1,0:T(8,128)S(1)}, u32[]{:S(2)}, u32[]{:S(2)}) async-start(f32[8,72,128]{2,1,0:T(8,128)} %split.1), calls=%async_computation | async-start | bytes 589824 | tf_op jit(solution)/shard_map/all_to_all | solution.py:869
  25.3 6.3 %collective-permute-start.1 = (f32[3,128,128]{2,1,0:T(8,128)}, f32[3,128,128]{2,1,0:T(8,128)S(1)}, u32[]{:S(2)}, u32[]{:S(2)}) collective-permute-start(f32[3,128,128]{2,1,0:T(8,128)} %copy-done.1), channel_id=1, source_target_pairs={{0,1},{1,0},{2,3},{3,2},{4,5},{5,4},{6,7},{7,6},{8,9},{9,8},{10,11... | collective-permute-start | bytes 589832 | tf_op jit(solution)/shard_map/ppermute | solution.py:859
  31.8 1.9 %collective-permute-start.2 = (f32[3,128,128]{2,1,0:T(8,128)S(1)}, f32[3,128,128]{2,1,0:T(8,128)S(1)}, u32[]{:S(2)}, u32[]{:S(2)}) collective-permute-start(f32[3,128,128]{2,1,0:T(8,128)S(1)} %get-tuple-element.83), channel_id=1, source_target_pairs={{0,1},{1,0},{2,3},{3,2},{4,5},{5,4},{6,7},{7,6},{8,9},{9,8},{10,11... | collective-permute-start | bytes 589832 | tf_op jit(solution)/shard_map/ppermute | solution.py:907
  33.9 4.2 %collective-permute-start.3 = (f32[3,128,128]{2,1,0:T(8,128)S(1)}, f32[3,128,128]{2,1,0:T(8,128)S(1)}, u32[]{:S(2)}, u32[]{:S(2)}) collective-permute-start(f32[3,128,128]{2,1,0:T(8,128)S(1)} %get-tuple-element.91), channel_id=1, source_target_pairs={{0,1},{1,0},{2,3},{3,2},{4,5},{5,4},{6,7},{7,6},{8,9},{9,8},{10,11... | collective-permute-start | bytes 589832 | tf_op jit(solution)/shard_map/ppermute | solution.py:907
  34.4 9.1 %collective-permute-start.4 = (f32[3,128,128]{2,1,0:T(8,128)S(1)}, f32[3,128,128]{2,1,0:T(8,128)S(1)}, u32[]{:S(2)}, u32[]{:S(2)}) collective-permute-start(f32[3,128,128]{2,1,0:T(8,128)S(1)} %get-tuple-element.95), channel_id=1, source_target_pairs={{1,2},{3,4},{5,6},{7,8},{9,10},{11,12},{13,14},{2,1},{4,3},{6,5},{... | collective-permute-start | bytes 589832 | tf_op jit(solution)/shard_map/ppermute | solution.py:925
  38.4 5.6 %collective-permute-start.5 = (f32[3,128,128]{2,1,0:T(8,128)S(1)}, f32[3,128,128]{2,1,0:T(8,128)S(1)}, u32[]{:S(2)}, u32[]{:S(2)}) collective-permute-start(f32[3,128,128]{2,1,0:T(8,128)S(1)} %get-tuple-element.100), channel_id=1, source_target_pairs={{0,1},{1,0},{2,3},{3,2},{4,5},{5,4},{6,7},{7,6},{8,9},{9,8},{10,11... | collective-permute-start | bytes 589832 | tf_op jit(solution)/shard_map/ppermute | solution.py:907
  38.5 9.1 %collective-permute-start.6 = (f32[3,128,128]{2,1,0:T(8,128)S(1)}, f32[3,128,128]{2,1,0:T(8,128)S(1)}, u32[]{:S(2)}, u32[]{:S(2)}) collective-permute-start(f32[3,128,128]{2,1,0:T(8,128)S(1)} %get-tuple-element.104), channel_id=1, source_target_pairs={{1,2},{3,4},{5,6},{7,8},{9,10},{11,12},{13,14},{2,1},{4,3},{6,5},{... | collective-permute-start | bytes 589832 | tf_op jit(solution)/shard_map/ppermute | solution.py:925
  44.3 3.9 %collective-permute-start.7 = (f32[3,128,128]{2,1,0:T(8,128)S(1)}, f32[3,128,128]{2,1,0:T(8,128)S(1)}, u32[]{:S(2)}, u32[]{:S(2)}) collective-permute-start(f32[3,128,128]{2,1,0:T(8,128)S(1)} %get-tuple-element.109), channel_id=1, source_target_pairs={{0,1},{1,0},{2,3},{3,2},{4,5},{5,4},{6,7},{7,6},{8,9},{9,8},{10,11... | collective-permute-start | bytes 589832 | tf_op jit(solution)/shard_map/ppermute | solution.py:907
  44.4 9.1 %collective-permute-start.8 = (f32[3,128,128]{2,1,0:T(8,128)S(1)}, f32[3,128,128]{2,1,0:T(8,128)S(1)}, u32[]{:S(2)}, u32[]{:S(2)}) collective-permute-start(f32[3,128,128]{2,1,0:T(8,128)S(1)} %get-tuple-element.113), channel_id=1, source_target_pairs={{1,2},{3,4},{5,6},{7,8},{9,10},{11,12},{13,14},{2,1},{4,3},{6,5},{... | collective-permute-start | bytes 589832 | tf_op jit(solution)/shard_map/ppermute | solution.py:925
  48.6 5.4 %collective-permute-start.9 = (f32[3,128,128]{2,1,0:T(8,128)S(1)}, f32[3,128,128]{2,1,0:T(8,128)S(1)}, u32[]{:S(2)}, u32[]{:S(2)}) collective-permute-start(f32[3,128,128]{2,1,0:T(8,128)S(1)} %get-tuple-element.118), channel_id=1, source_target_pairs={{0,1},{1,0},{2,3},{3,2},{4,5},{5,4},{6,7},{7,6},{8,9},{9,8},{10,11... | collective-permute-start | bytes 589832 | tf_op jit(solution)/shard_map/ppermute | solution.py:907
  48.6 9.2 %collective-permute-start.10 = (f32[3,128,128]{2,1,0:T(8,128)S(1)}, f32[3,128,128]{2,1,0:T(8,128)S(1)}, u32[]{:S(2)}, u32[]{:S(2)}) collective-permute-start(f32[3,128,128]{2,1,0:T(8,128)S(1)} %get-tuple-element.122), channel_id=1, source_target_pairs={{1,2},{3,4},{5,6},{7,8},{9,10},{11,12},{13,14},{2,1},{4,3},{6,5},{... | collective-permute-start | bytes 589832 | tf_op jit(solution)/shard_map/ppermute | solution.py:925

commit v9 on v7

--- a/solution.py
+++ b/solution.py
@@ -438,7 +438,7 @@
 
 def start_kernel(
     velocity, stress, memory, layer_in, lam_in, mu_in, buoy_in, rate_in, defect_in, loads, steps_table,
-    V, S, R, coef_ref, msg_near, msg_far, W, table, layer_ref, lam, mu, buoy, rate, defect, sems,
+    V, S, R, coef_ref, msg_near, msg_far, msg_early, W, table, layer_ref, lam, mu, buoy, rate, defect, sems,
 ):
     across = velocity.shape[2]
     inside = pl.ds(PAD, across)
@@ -458,7 +458,7 @@
     table[...] = jnp.zeros(table.shape, jnp.float32)
     table[0:16, :] = steps_table[...]
     columns = table[...].T
-    trucks = 6 * across
+    trucks = 3 * across
     msg_far[trucks : trucks + slots, :] = loads[...]
     for i, at in enumerate((0, 8)):
         first_row = trucks + (1 + i) * slots
@@ -500,7 +500,7 @@
     for copy in copies[6:15]:
         copy.wait()
     even, _, _ = place()
-    now, then = Planes(msg_far, 0, across), Planes(msg_far, 3, across)
+    now = Planes(msg_far, 0, across)
 
     @pl.when(even)
     def _():
@@ -518,11 +518,11 @@
 
     @pl.when(even)
     def _():
-        early_behind(V, S, R, coef_ref, None, 0, then, W, None, 0)
+        early_behind(V, S, R, coef_ref, None, 0, msg_early, W, None, 0)
 
     @pl.when(jnp.logical_not(even))
     def _():
-        early_ahead(V, S, R, coef_ref, then, W, None, 0)
+        early_ahead(V, S, R, coef_ref, msg_early, W, None, 0)
 
 
 def near_kernel(step, window, V0, S0, R0, coef_ref, force, surface, msg, V, S, R, *rest):
@@ -549,7 +549,7 @@
 
 def meet_kernel(across, msg, loads, load, rows_out):
     slots = loads.shape[0]
-    rows, entry, cell = (msg[6 * across + i * slots : 6 * across + (i + 1) * slots, :] for i in range(3))
+    rows, entry, cell = (msg[3 * across + i * slots : 3 * across + (i + 1) * slots, :] for i in range(3))
     for slot in range(slots):
         rows = jnp.where(entry == float(slot), loads[slot : slot + 1, :], rows)
     rows_out[...] = jnp.zeros(rows_out.shape, jnp.float32)
@@ -565,7 +565,7 @@
     across = R.shape[2]
     even, _, _ = place()
     here, then = force.at[step], force.at[step + 1]
-    got = Planes(msg, 3 * step, across) if step < 2 else msg
+    got = Planes(msg, 0, across) if step == 0 else msg
     if step == 0:
         missing, load = None, other
         G, W, A = rest[-3:]
@@ -717,8 +717,7 @@
             out[tile, at : at + 8, :] = jnp.where(passed, own_rows[i], far_rows[i])
 
 
-def prepare_kernel(parts, loads, steps_table, after_this, force, surface, table, rows_out):
-    del after_this
+def prepare_kernel(parts, loads, steps_table, force, surface, table, rows_out):
     steps, comps, width = force.shape[:3]
     lanes = parts.shape[2]
     force[...] = jnp.zeros(force.shape, jnp.float32)
@@ -840,12 +839,12 @@
         behind = jnp.concatenate([record, behind[:, panel:]], axis=1)
         reach *= 2
     tables = (lame_lambda, lame_mu, buoyancy, relax_rate, defect_mu)
-    V, S, R, coef, msg_near, msg_far = call(
+    V, S, R, coef, msg_near, msg_far, early = call(
         start_kernel,
         in_hbm(velocity, stress, memory, layer[None, :], *tables) + (in_vmem(loads), in_vmem(steps_table)),
         (ANYWHERE,) * 9 + (WHOLE,) * 2,
-        (v_type, s_type, r_type, c_type, m_type, pltpu.VMEM((6 * across + 3 * slots, depth), f32)),
-        (WHOLE,) * 6,
+        (v_type, s_type, r_type, c_type, m_type, pltpu.VMEM((3 * across + 3 * slots, depth), f32), m_type),
+        (WHOLE,) * 7,
         scratch=(
             work, pltpu.VMEM((depth, depth), f32), pltpu.VMEM((1, depth), jnp.int32),
             *(pltpu.SMEM(table.shape, f32) for table in tables), dma((21,)),
@@ -854,6 +853,7 @@
         cost=8 * 1024 * 1024,
     )
     msg_far = lax.ppermute(msg_far, "line", far)
+    early = lax.ppermute(early, "line", far)
     msg_near = lax.ppermute(msg_near, "line", near)
     parts = call(
         functools.partial(split_kernel, panel, slots),
@@ -873,12 +873,11 @@
         WHOLE,
         scratch=(pltpu.VMEM((depth, across), f32),),
         name="meet",
-        cost=64 * 1024 * 1024,
     )
     force, surface = call(
         prepare_kernel,
-        (parts, in_vmem(loads), in_vmem(steps_table), load),
-        (WHOLE,) * 3 + (ANYWHERE,),
+        (parts, in_vmem(loads), in_vmem(steps_table)),
+        (WHOLE,) * 3,
         (pltpu.VMEM((STEPS, 3, 4, 16, depth), f32), pltpu.VMEM((across, depth), f32)),
         (WHOLE,) * 2,
         scratch=(pltpu.VMEM((depth, depth), f32), pltpu.VMEM((depth, across), f32)),
@@ -917,8 +916,7 @@
                 aliases=same,
                 name="far" + str(step),
             )
-            if step > 0:
-                msg_far = early
+            msg_far = early
             if msg:
                 early = lax.ppermute(msg[0], "line", far)
     results = call(

time: 57.6 us -> 59.5 us (1.033)
  starting transfers between devices: 24.9 us -> 27.8 us
  local copies, waits for them, and re-layouts: 0.67 us -> 0 us
    ppermute x1, waiting for transfers between devices: 11 us -> 0.01 us  [body(): msg_far = lax.ppermute(msg_far, 'line', far)]
    ppermute x4, waiting for transfers between devices: 6.49 us -> 11.1 us  [body(): early = lax.ppermute(msg[0], 'line', far)]
    ppermute x0 -> x1, waiting for transfers between devices: none -> 4.49 us  [body(): early = lax.ppermute(early, 'line', far)]
    ppermute x5, starting transfers between devices: 0.45 us -> 3.96 us  [body(): msg_near = lax.ppermute(msg[0], 'line', near)]
    ppermute x4, starting transfers between devices: 13.3 us -> 10.6 us  [body(): early = lax.ppermute(msg[0], 'line', far)]
    all_to_all x1, waiting for transfers between devices: 0.01 us -> 1.94 us  [body(): lax.all_to_all(parts, 'line', 0, 0, axis_index_groups=groups, tiled=True)]
    ppermute x0 -> x1, starting transfers between devices: none -> 1.91 us  [body(): early = lax.ppermute(early, 'line', far)]
    ppermute x5, waiting for transfers between devices: 0.79 us -> 0.01 us  [body(): msg_near = lax.ppermute(msg[0], 'line', near)]
  transfers between devices with their start and end apart: 13 -> 14, of which waited for: 7 -> 5; matrix products, arithmetic and copies ran while one was open for 0% -> 0% of each run, Pallas kernels for 12% -> 12%
where the time goes in v9:
time: 59.5 us; the launch traced here: 59.1 us
  starting transfers between devices  27.8 us (47%)
  waiting for transfers between devices  20.2 us (34%)
  Pallas kernels  10.2 us (17%)
  between operations  0.88 us (1%)
    ppermute x4, waiting for transfers between devices, body(): early = lax.ppermute(msg[0], 'line', far)  11.1 us
    ppermute x4, starting transfers between devices, body(): early = lax.ppermute(msg[0], 'line', far)  10.6 us
    pallas_call x17, Pallas kernels, call(): pl.pallas_call(kernel, out_shape=outs, in_specs=specs, out_specs=out_spec...  10.2 us
    all_to_all x1, starting transfers between devices, body(): lax.all_to_all(parts, 'line', 0, 0, axis_index_groups=groups, tiled=True)  6.3 us
    ppermute x1, waiting for transfers between devices, body(): early = lax.ppermute(early, 'line', far)  4.49 us
    ppermute x5, starting transfers between devices, body(): msg_near = lax.ppermute(msg[0], 'line', near)  3.96 us
    ppermute x1, starting transfers between devices, body(): msg_far = lax.ppermute(msg_far, 'line', far)  3.67 us
    ppermute x1, waiting for transfers between devices, ahead_by(): lax.ppermute(x, 'line', [(i, i + distance) for i in range(tiles - distanc...  2.67 us
  transfers between devices with their start and end apart: 14, of which 5 were waited for; matrix products, arithmetic and copies ran while one was open for 0% of the time, Pallas kernels for 12%

profile of v9, /device:TPU:17, one launch (start us, length us, event | category | flops | bytes accessed | tf_op | source)
XLA Modules:
  0.0 59.1 jit_solution(3339816988828507409)
XLA Ops:
  0.6 0.9 %pack.1 = (f32[8,1920]{1,0:T(8,128)S(1)}, f32[16,128]{1,0:T(8,128)S(1)}, f32[16,128]{1,0:T(8,128)S(1)}, s32[1,8]{1,0:T(1,128)S(1)}) custom-call(f32[8,1536]{1,0:T(8,128)} %bitcast.3, f32[16,128]{1,0:T(8,128)} %loads_in.1, s32[6,16]{1,0:T(8,128)} %entries_in.1, s32[6,16]{1,0:T(8,128)} %cells_in.1, s32[1,8]{1,0:T(1,128)} %bitcast.4), custom_call_target="tpu_custom_call" | custom-call | flops 1 | bytes 1 | tf_op jit(solution)/shard_map/pack/pallas_call | solution.py:774
  1.5 1.3 %collective-permute-start = (f32[8,1920]{1,0:T(8,128)S(1)}, f32[8,1920]{1,0:T(8,128)S(1)}, u32[]{:S(2)}, u32[]{:S(2)}) collective-permute-start(f32[8,1920]{1,0:T(8,128)S(1)} %get-tuple-element.72.own), channel_id=1, source_target_pairs={{0,8},{1,9},{2,10},{3,11},{4,12},{5,13},{6,14},{7,15},{16,24},{17,... | collective-permute-start | bytes 184328 | tf_op jit(solution)/shard_map/ppermute | solution.py:812
  2.8 1.9 %start.1 = (f32[3,2,144,128]{3,2,1,0:T(8,128)S(1)}, f32[6,2,144,128]{3,2,1,0:T(8,128)S(1)}, f32[6,2,128,128]{3,2,1,0:T(8,128)S(1)}, f32[16,128]{1,0:T(8,128)S(1)...) custom-call(f32[3,2,128,128]{3,2,1,0:T(8,128)} %velocity.1, ...), custom_call_target="tpu_custom_call" | custom-call | flops 8388608 | bytes 8388608 | tf_op jit(solution)/shard_map/start/pallas_call | solution.py:774
  4.8 2.7 %collective-permute-done.behind = f32[8,1920]{1,0:T(8,128)S(1)} collective-permute-done((f32[8,1920]{1,0:T(8,128)S(1)}, f32[8,1920]{1,0:T(8,128)S(1)}, u32[]{:S(2)}, u32[]{:S(2)}) %collective-permute-start) | collective-permute-done | bytes 61472 | tf_op jit(solution)/shard_map/ppermute | solution.py:812
  7.4 0.9 %split.1 = f32[8,72,128]{2,1,0:T(8,128)} custom-call(f32[8,1920]{1,0:T(8,128)S(1)} %get-tuple-element.72.own, f32[8,1920]{1,0:T(8,128)S(1)} %collective-permute-done.behind, s32[1,8]{1,0:T(1,128)S(1)} %get-tuple-element.73.cells, f32[16,128]{1,0:T(8,128)S(1)} %get-tuple-element.71.after_this.coef_ref), custom_call_target="tpu_custom_call" | custom-call | flops 1 | bytes 1 | tf_op jit(solution)/shard_map/split/pallas_call | solution.py:774
  8.3 6.3 %all-to-all-start = ((f32[8,72,128]{2,1,0:T(8,128)}), f32[8,72,128]{2,1,0:T(8,128)S(1)}, u32[]{:S(2)}, u32[]{:S(2)}) async-start(f32[8,72,128]{2,1,0:T(8,128)} %split.1), calls=%async_computation | async-start | bytes 589824 | tf_op jit(solution)/shard_map/all_to_all | solution.py:867
  14.6 0.0 collective-permute-start.1
  14.7 3.7 %collective-permute-start.2 = (f32[432,128]{1,0:T(8,128)S(1)}, f32[432,128]{1,0:T(8,128)S(1)}, u32[]{:S(2)}, u32[]{:S(2)}) collective-permute-start(f32[432,128]{1,0:T(8,128)S(1)} %get-tuple-element.80), channel_id=1, source_target_pairs={{1,2},{3,4},{5,6},{7,8},{9,10},{11,12},{13,14},{2,1},{4,3},{6,5},{... | collective-permute-start | bytes 663560 | tf_op jit(solution)/shard_map/ppermute | solution.py:855
  18.3 1.9 %all-to-all-done.parts = f32[8,72,128]{2,1,0:T(8,128)S(1)} async-done(((f32[8,72,128]{2,1,0:T(8,128)}), f32[8,72,128]{2,1,0:T(8,128)S(1)}, u32[]{:S(2)}, u32[]{:S(2)}) %all-to-all-start) | async-done | bytes 294944 | tf_op jit(solution)/shard_map/all_to_all | solution.py:867
  20.3 0.6 %prepare.1 = (f32[6,3,4,16,128]{4,3,2,1,0:T(8,128)S(1)}, f32[128,128]{1,0:T(8,128)S(1)}) custom-call(f32[8,72,128]{2,1,0:T(8,128)S(1)} %all-to-all-done.parts, f32[16,128]{1,0:T(8,128)S(1)} %get-tuple-element.66.loads, f32[16,128]{1,0:T(8,128)S(1)} %get-tuple-element.67.steps_table), custom_call_target="tpu_custom_call" | custom-call | flops 1 | bytes 1 | tf_op jit(solution)/shard_map/prepare/pallas_call | solution.py:774
  20.9 0.0 collective-permute-done.1.msg
  20.9 0.3 near0.1
  21.2 3.2 %collective-permute-start.3 = (f32[3,128,128]{2,1,0:T(8,128)S(1)}, f32[3,128,128]{2,1,0:T(8,128)S(1)}, u32[]{:S(2)}, u32[]{:S(2)}) collective-permute-start(f32[3,128,128]{2,1,0:T(8,128)S(1)} %get-tuple-element.84), channel_id=1, source_target_pairs={{0,1},{1,0},{2,3},{3,2},{4,5},{5,4},{6,7},{7,6},{8,9},{9,8},{10,11... | collective-permute-start | bytes 589832 | tf_op jit(solution)/shard_map/ppermute | solution.py:904
  24.3 1.9 %collective-permute-start.4 = (f32[3,128,128]{2,1,0:T(8,128)S(1)}, f32[3,128,128]{2,1,0:T(8,128)S(1)}, u32[]{:S(2)}, u32[]{:S(2)}) collective-permute-start(f32[3,128,128]{2,1,0:T(8,128)S(1)} %get-tuple-element.88), channel_id=1, source_target_pairs={{1,2},{3,4},{5,6},{7,8},{9,10},{11,12},{13,14},{2,1},{4,3},{6,5},{... | collective-permute-start | bytes 589832 | tf_op jit(solution)/shard_map/ppermute | solution.py:856
  26.3 0.0 collective-permute-done.2.msg
  26.3 0.1 meet.1.rest_0_
  26.4 0.6 %far0.1 = (f32[3,2,144,128]{3,2,1,0:T(8,128)S(1)}, f32[6,2,144,128]{3,2,1,0:T(8,128)S(1)}, f32[6,2,128,128]{3,2,1,0:T(8,128)S(1)}, f32[3,128,128]{2,1,0:T(8,128)S(1)}, f32[3,128,128]{2,1,0:T(8,128)S(1)}) custom-call(f32[3,2,144,128]{3,2,1,0:T(8,128)S(1)} %get-tuple-element.77.V0, ...), custom_call_target="tpu_custom_call", output_to_operand_aliasing={{0}: (0, {}), {1}: (1, {}), {2}: (2, {})} | custom-call | flops 1 | bytes 1 | tf_op jit(solution)/shard_map/far0/pallas_call | solution.py:774
  27.0 0.0 collective-permute-done.3.msg
  27.0 0.3 near1.1
  27.3 0.1 collective-permute-start.5
  27.4 3.6 %collective-permute-start.6 = (f32[3,128,128]{2,1,0:T(8,128)S(1)}, f32[3,128,128]{2,1,0:T(8,128)S(1)}, u32[]{:S(2)}, u32[]{:S(2)}) collective-permute-start(f32[3,128,128]{2,1,0:T(8,128)S(1)} %get-tuple-element.97), channel_id=1, source_target_pairs={{1,2},{3,4},{5,6},{7,8},{9,10},{11,12},{13,14},{2,1},{4,3},{6,5},{... | collective-permute-start | bytes 589832 | tf_op jit(solution)/shard_map/ppermute | solution.py:921
  31.0 4.5 %collective-permute-done.4.msg = f32[3,128,128]{2,1,0:T(8,128)S(1)} collective-permute-done((f32[3,128,128]{2,1,0:T(8,128)S(1)}, f32[3,128,128]{2,1,0:T(8,128)S(1)}, u32[]{:S(2)}, u32[]{:S(2)}) %collective-permute-start.4) | collective-permute-done | bytes 196640 | tf_op jit(solution)/shard_map/ppermute | solution.py:856
  35.5 0.6 %far1.1 = (f32[3,2,144,128]{3,2,1,0:T(8,128)S(1)}, f32[6,2,144,128]{3,2,1,0:T(8,128)S(1)}, f32[6,2,128,128]{3,2,1,0:T(8,128)S(1)}, f32[3,128,128]{2,1,0:T(8,128)S(1)}, f32[3,128,128]{2,1,0:T(8,128)S(1)}) custom-call(f32[3,2,144,128]{3,2,1,0:T(8,128)S(1)} %get-tuple-element.85.V0, ...), custom_call_target="tpu_custom_call", output_to_operand_aliasing={{0}: (0, {}), {1}: (1, {}), {2}: (2, {})} | custom-call | flops 1 | bytes 1 | tf_op jit(solution)/shard_map/far1/pallas_call | solution.py:774
  36.1 0.0 collective-permute-done.5.msg
  36.2 0.3 near2.1
  36.4 0.1 collective-permute-start.7
  36.5 1.9 %collective-permute-start.8 = (f32[3,128,128]{2,1,0:T(8,128)S(1)}, f32[3,128,128]{2,1,0:T(8,128)S(1)}, u32[]{:S(2)}, u32[]{:S(2)}) collective-permute-start(f32[3,128,128]{2,1,0:T(8,128)S(1)} %get-tuple-element.106), channel_id=1, source_target_pairs={{1,2},{3,4},{5,6},{7,8},{9,10},{11,12},{13,14},{2,1},{4,3},{6,5},{... | collective-permute-start | bytes 589832 | tf_op jit(solution)/shard_map/ppermute | solution.py:921
  38.4 0.0 collective-permute-done.6.msg
  38.4 0.6 %far2.1 = (f32[3,2,144,128]{3,2,1,0:T(8,128)S(1)}, f32[6,2,144,128]{3,2,1,0:T(8,128)S(1)}, f32[6,2,128,128]{3,2,1,0:T(8,128)S(1)}, f32[3,128,128]{2,1,0:T(8,128)S(1)}, f32[3,128,128]{2,1,0:T(8,128)S(1)}) custom-call(f32[3,2,144,128]{3,2,1,0:T(8,128)S(1)} %get-tuple-element.94.V0, ...), custom_call_target="tpu_custom_call", output_to_operand_aliasing={{0}: (0, {}), {1}: (1, {}), {2}: (2, {})} | custom-call | flops 1 | bytes 1 | tf_op jit(solution)/shard_map/far2/pallas_call | solution.py:774
  39.1 0.0 collective-permute-done.7.msg
  39.1 0.3 near3.1
  39.4 0.6 collective-permute-start.9
  39.9 3.2 %collective-permute-start.10 = (f32[3,128,128]{2,1,0:T(8,128)S(1)}, f32[3,128,128]{2,1,0:T(8,128)S(1)}, u32[]{:S(2)}, u32[]{:S(2)}) collective-permute-start(f32[3,128,128]{2,1,0:T(8,128)S(1)} %get-tuple-element.115), channel_id=1, source_target_pairs={{1,2},{3,4},{5,6},{7,8},{9,10},{11,12},{13,14},{2,1},{4,3},{6,5},{... | collective-permute-start | bytes 589832 | tf_op jit(solution)/shard_map/ppermute | solution.py:921
  43.1 4.6 %collective-permute-done.8.msg = f32[3,128,128]{2,1,0:T(8,128)S(1)} collective-permute-done((f32[3,128,128]{2,1,0:T(8,128)S(1)}, f32[3,128,128]{2,1,0:T(8,128)S(1)}, u32[]{:S(2)}, u32[]{:S(2)}) %collective-permute-start.8) | collective-permute-done | bytes 196640 | tf_op jit(solution)/shard_map/ppermute | solution.py:921
  47.7 0.6 %far3.1 = (f32[3,2,144,128]{3,2,1,0:T(8,128)S(1)}, f32[6,2,144,128]{3,2,1,0:T(8,128)S(1)}, f32[6,2,128,128]{3,2,1,0:T(8,128)S(1)}, f32[3,128,128]{2,1,0:T(8,128)S(1)}, f32[3,128,128]{2,1,0:T(8,128)S(1)}) custom-call(f32[3,2,144,128]{3,2,1,0:T(8,128)S(1)} %get-tuple-element.103.V0, ...), custom_call_target="tpu_custom_call", output_to_operand_aliasing={{0}: (0, {}), {1}: (1, {}), {2}: (2, {})} | custom-call | flops 1 | bytes 1 | tf_op jit(solution)/shard_map/far3/pallas_call | solution.py:774
  48.3 0.0 collective-permute-done.9.msg
  48.3 0.3 near4.1
  48.6 0.1 collective-permute-start.11
  48.7 1.9 %collective-permute-start.12 = (f32[3,128,128]{2,1,0:T(8,128)S(1)}, f32[3,128,128]{2,1,0:T(8,128)S(1)}, u32[]{:S(2)}, u32[]{:S(2)}) collective-permute-start(f32[3,128,128]{2,1,0:T(8,128)S(1)} %get-tuple-element.124), channel_id=1, source_target_pairs={{1,2},{3,4},{5,6},{7,8},{9,10},{11,12},{13,14},{2,1},{4,3},{6,5},{... | collective-permute-start | bytes 589832 | tf_op jit(solution)/shard_map/ppermute | solution.py:921
  50.6 0.0 collective-permute-done.10.msg
  50.6 0.4 far4.1
  51.1 0.0 collective-permute-done.11.msg
  51.1 0.2 near5.1
  51.3 6.5 %collective-permute-done.12.msg = f32[3,128,128]{2,1,0:T(8,128)S(1)} collective-permute-done((f32[3,128,128]{2,1,0:T(8,128)S(1)}, f32[3,128,128]{2,1,0:T(8,128)S(1)}, u32[]{:S(2)}, u32[]{:S(2)}) %collective-permute-start.12) | collective-permute-done | bytes 196640 | tf_op jit(solution)/shard_map/ppermute | solution.py:921
  57.8 1.3 %last.1 = (f32[3,2,144,128]{3,2,1,0:T(8,128)S(1)}, f32[6,2,144,128]{3,2,1,0:T(8,128)S(1)}, f32[6,2,128,128]{3,2,1,0:T(8,128)S(1)}, f32[3,2,128,128]{3,2,1,0:T(8,...) custom-call(f32[3,2,144,128]{3,2,1,0:T(8,128)S(1)} %get-tuple-elemen, ...), custom_call_target="tpu_custom_call", output_to_operand_aliasing={{0}: (0, {}), {1}: (1, {}), {2}: (2, {})} | custom-call | flops 1 | bytes 1 | tf_op jit(solution)/shard_map/last/pallas_call | solution.py:774
Async XLA Ops:
  1.5 5.9 %collective-permute-start = (f32[8,1920]{1,0:T(8,128)S(1)}, f32[8,1920]{1,0:T(8,128)S(1)}, u32[]{:S(2)}, u32[]{:S(2)}) collective-permute-start(f32[8,1920]{1,0:T(8,128)S(1)} %get-tuple-element.72.own), channel_id=1, source_target_pairs={{0,8},{1,9},{2,10},{3,11},{4,12},{5,13},{6,14},{7,15},{16,24},{17,... | collective-permute-start | bytes 184328 | tf_op jit(solution)/shard_map/ppermute | solution.py:812
  8.3 11.9 %all-to-all-start = ((f32[8,72,128]{2,1,0:T(8,128)}), f32[8,72,128]{2,1,0:T(8,128)S(1)}, u32[]{:S(2)}, u32[]{:S(2)}) async-start(f32[8,72,128]{2,1,0:T(8,128)} %split.1), calls=%async_computation | async-start | bytes 589824 | tf_op jit(solution)/shard_map/all_to_all | solution.py:867
  14.6 6.3 %collective-permute-start.1 = (f32[3,128,128]{2,1,0:T(8,128)S(1)}, f32[3,128,128]{2,1,0:T(8,128)S(1)}, u32[]{:S(2)}, u32[]{:S(2)}) collective-permute-start(f32[3,128,128]{2,1,0:T(8,128)S(1)} %get-tuple-element.76), channel_id=1, source_target_pairs={{0,1},{1,0},{2,3},{3,2},{4,5},{5,4},{6,7},{7,6},{8,9},{9,8},{10,11... | collective-permute-start | bytes 589832 | tf_op jit(solution)/shard_map/ppermute | solution.py:857
  14.7 11.6 %collective-permute-start.2 = (f32[432,128]{1,0:T(8,128)S(1)}, f32[432,128]{1,0:T(8,128)S(1)}, u32[]{:S(2)}, u32[]{:S(2)}) collective-permute-start(f32[432,128]{1,0:T(8,128)S(1)} %get-tuple-element.80), channel_id=1, source_target_pairs={{1,2},{3,4},{5,6},{7,8},{9,10},{11,12},{13,14},{2,1},{4,3},{6,5},{... | collective-permute-start | bytes 663560 | tf_op jit(solution)/shard_map/ppermute | solution.py:855
  21.2 5.9 %collective-permute-start.3 = (f32[3,128,128]{2,1,0:T(8,128)S(1)}, f32[3,128,128]{2,1,0:T(8,128)S(1)}, u32[]{:S(2)}, u32[]{:S(2)}) collective-permute-start(f32[3,128,128]{2,1,0:T(8,128)S(1)} %get-tuple-element.84), channel_id=1, source_target_pairs={{0,1},{1,0},{2,3},{3,2},{4,5},{5,4},{6,7},{7,6},{8,9},{9,8},{10,11... | collective-permute-start | bytes 589832 | tf_op jit(solution)/shard_map/ppermute | solution.py:904
  24.3 11.2 %collective-permute-start.4 = (f32[3,128,128]{2,1,0:T(8,128)S(1)}, f32[3,128,128]{2,1,0:T(8,128)S(1)}, u32[]{:S(2)}, u32[]{:S(2)}) collective-permute-start(f32[3,128,128]{2,1,0:T(8,128)S(1)} %get-tuple-element.88), channel_id=1, source_target_pairs={{1,2},{3,4},{5,6},{7,8},{9,10},{11,12},{13,14},{2,1},{4,3},{6,5},{... | collective-permute-start | bytes 589832 | tf_op jit(solution)/shard_map/ppermute | solution.py:856
  27.3 8.8 %collective-permute-start.5 = (f32[3,128,128]{2,1,0:T(8,128)S(1)}, f32[3,128,128]{2,1,0:T(8,128)S(1)}, u32[]{:S(2)}, u32[]{:S(2)}) collective-permute-start(f32[3,128,128]{2,1,0:T(8,128)S(1)} %get-tuple-element.93), channel_id=1, source_target_pairs={{0,1},{1,0},{2,3},{3,2},{4,5},{5,4},{6,7},{7,6},{8,9},{9,8},{10,11... | collective-permute-start | bytes 589832 | tf_op jit(solution)/shard_map/ppermute | solution.py:904
  27.4 11.0 %collective-permute-start.6 = (f32[3,128,128]{2,1,0:T(8,128)S(1)}, f32[3,128,128]{2,1,0:T(8,128)S(1)}, u32[]{:S(2)}, u32[]{:S(2)}) collective-permute-start(f32[3,128,128]{2,1,0:T(8,128)S(1)} %get-tuple-element.97), channel_id=1, source_target_pairs={{1,2},{3,4},{5,6},{7,8},{9,10},{11,12},{13,14},{2,1},{4,3},{6,5},{... | collective-permute-start | bytes 589832 | tf_op jit(solution)/shard_map/ppermute | solution.py:921
  36.4 2.6 %collective-permute-start.7 = (f32[3,128,128]{2,1,0:T(8,128)S(1)}, f32[3,128,128]{2,1,0:T(8,128)S(1)}, u32[]{:S(2)}, u32[]{:S(2)}) collective-permute-start(f32[3,128,128]{2,1,0:T(8,128)S(1)} %get-tuple-element.102), channel_id=1, source_target_pairs={{0,1},{1,0},{2,3},{3,2},{4,5},{5,4},{6,7},{7,6},{8,9},{9,8},{10,11... | collective-permute-start | bytes 589832 | tf_op jit(solution)/shard_map/ppermute | solution.py:904
  36.5 11.2 %collective-permute-start.8 = (f32[3,128,128]{2,1,0:T(8,128)S(1)}, f32[3,128,128]{2,1,0:T(8,128)S(1)}, u32[]{:S(2)}, u32[]{:S(2)}) collective-permute-start(f32[3,128,128]{2,1,0:T(8,128)S(1)} %get-tuple-element.106), channel_id=1, source_target_pairs={{1,2},{3,4},{5,6},{7,8},{9,10},{11,12},{13,14},{2,1},{4,3},{6,5},{... | collective-permute-start | bytes 589832 | tf_op jit(solution)/shard_map/ppermute | solution.py:921
  39.4 9.0 %collective-permute-start.9 = (f32[3,128,128]{2,1,0:T(8,128)S(1)}, f32[3,128,128]{2,1,0:T(8,128)S(1)}, u32[]{:S(2)}, u32[]{:S(2)}) collective-permute-start(f32[3,128,128]{2,1,0:T(8,128)S(1)} %get-tuple-element.111), channel_id=1, source_target_pairs={{0,1},{1,0},{2,3},{3,2},{4,5},{5,4},{6,7},{7,6},{8,9},{9,8},{10,11... | collective-permute-start | bytes 589832 | tf_op jit(solution)/shard_map/ppermute | solution.py:904
  39.9 10.7 %collective-permute-start.10 = (f32[3,128,128]{2,1,0:T(8,128)S(1)}, f32[3,128,128]{2,1,0:T(8,128)S(1)}, u32[]{:S(2)}, u32[]{:S(2)}) collective-permute-start(f32[3,128,128]{2,1,0:T(8,128)S(1)} %get-tuple-element.115), channel_id=1, source_target_pairs={{1,2},{3,4},{5,6},{7,8},{9,10},{11,12},{13,14},{2,1},{4,3},{6,5},{... | collective-permute-start | bytes 589832 | tf_op jit(solution)/shard_map/ppermute | solution.py:921
  48.6 2.5 %collective-permute-start.11 = (f32[3,128,128]{2,1,0:T(8,128)S(1)}, f32[3,128,128]{2,1,0:T(8,128)S(1)}, u32[]{:S(2)}, u32[]{:S(2)}) collective-permute-start(f32[3,128,128]{2,1,0:T(8,128)S(1)} %get-tuple-element.120), channel_id=1, source_target_pairs={{0,1},{1,0},{2,3},{3,2},{4,5},{5,4},{6,7},{7,6},{8,9},{9,8},{10,11... | collective-permute-start | bytes 589832 | tf_op jit(solution)/shard_map/ppermute | solution.py:904
  48.7 9.1 %collective-permute-start.12 = (f32[3,128,128]{2,1,0:T(8,128)S(1)}, f32[3,128,128]{2,1,0:T(8,128)S(1)}, u32[]{:S(2)}, u32[]{:S(2)}) collective-permute-start(f32[3,128,128]{2,1,0:T(8,128)S(1)} %get-tuple-element.124), channel_id=1, source_target_pairs={{1,2},{3,4},{5,6},{7,8},{9,10},{11,12},{13,14},{2,1},{4,3},{6,5},{... | collective-permute-start | bytes 589832 | tf_op jit(solution)/shard_map/ppermute | solution.py:921

commit v10 on v9

--- a/solution.py
+++ b/solution.py
@@ -42,21 +42,6 @@
         return carry
 
     lax.fori_loop(0, count // ROWS, step, 0, unroll=UNROLL)
-
-
-class Planes:
-    def __init__(self, ref, first, across):
-        self.ref, self.first, self.shape = ref, first, (3, across, ref.shape[1])
-
-    def rows(self, at):
-        plane, out = at
-        return pl.ds((self.first + plane) * self.shape[1] + out.start, out.size)
-
-    def __getitem__(self, at):
-        return self.ref[self.rows(at)]
-
-    def __setitem__(self, at, value):
-        self.ref[self.rows(at)] = value
 
 
 def coefs(coef_ref, ids):
@@ -240,82 +225,6 @@
     over_rows(D.shape[1], rest)
 
 
-def first_response_behind(V, S, coef_ref, force, load, D, W, A, window):
-    b, b0, b1, m0, m1, lam, mu2, mu, l0 = coefs(
-        coef_ref, (C_B, C_B0, C_B1, C_M0, C_M1, C_LAM, C_MU2, C_MU, C_L0)
-    )
-    A[...] = jnp.zeros(A.shape, jnp.float32)
-
-    def given(r):
-        here, _, _, _ = spans(r)
-        A[1, here] = -b * S[XY, 1, here]
-        A[2, here] = -b * S[XZ, 1, here]
-
-    over_rows(D.shape[1], given)
-    for i, which in enumerate(((VX, 3), (VY, 2), (VZ, 2), (VY, 3), (VZ, 3))):
-        add_force(A, (i,), force, which, PAD + window)
-
-    def work(r):
-        here, up, down, out = spans(r)
-        vx, vy, vz = A[0, here], A[1, here], A[2, here]
-        exx = vx - V[VX, 1, here]
-        eyy = vy - A[1, up]
-        ezz = vz - m0 * before(vz)
-        volume = lam * (exx + eyy + ezz)
-        dyy = volume + mu2 * eyy
-        dzz = volume + mu2 * ezz + l0 * load[out, :]
-        dxy = mu * (A[0, down] - vx + (A[3, here] - vy))
-        dxz = mu * (m1 * after(vx) - vx + (A[4, here] - vz))
-        dyz = mu * (m1 * after(vy) - vy + (A[2, down] - vz))
-        W[0, here] = dyy
-        W[1, here] = dyz
-        D[0, out] = volume + mu2 * exx
-        D[1, out] = vy + b * (dxy - dyy + dyz) - b0 * before(dyz)
-        D[2, out] = vz + b * (dxz + dyz - dzz) + b1 * after(dzz)
-
-    over_rows(D.shape[1], work)
-
-    def rest(r):
-        _, up, down, out = spans(r)
-        D[1, out] = D[1, out] + b * W[0, down]
-        D[2, out] = D[2, out] - b * W[1, up]
-
-    over_rows(D.shape[1], rest)
-
-
-def first_response_ahead(V, S, coef_ref, force, D, W, A, window):
-    b, b0, m0, m1, lam, mu2, mu = coefs(coef_ref, (C_B, C_B0, C_M0, C_M1, C_LAM, C_MU2, C_MU))
-    A[...] = jnp.zeros(A.shape, jnp.float32)
-
-    def given(r):
-        here, _, _, _ = spans(r)
-        A[0, here] = b * S[XX, 0, here]
-
-    over_rows(D.shape[1], given)
-    for i, which in enumerate(((VX, 2), (VY, 3), (VZ, 3), (VX, 3))):
-        add_force(A, (i,), force, which, PAD + window)
-
-    def work(r):
-        here, up, down, out = spans(r)
-        vx, vy, vz = A[0, here], A[1, here], A[2, here]
-        exx = vx - A[3, here]
-        dxx = lam * (exx + (vy - A[1, up]) + (vz - m0 * before(vz))) + mu2 * exx
-        dxy = mu * (A[0, down] - vx + (V[VY, 0, here] - vy))
-        dxz = mu * (m1 * after(vx) - vx + (V[VZ, 0, here] - vz))
-        W[0, here] = dxy
-        D[0, out] = dxy
-        D[1, out] = dxz
-        D[2, out] = vx + b * (dxy + dxz - dxx) - b0 * before(dxz)
-
-    over_rows(D.shape[1], work)
-
-    def rest(r):
-        _, up, _, out = spans(r)
-        D[2, out] = D[2, out] - b * W[0, up]
-
-    over_rows(D.shape[1], rest)
-
-
 def early_ahead(V, S, R, coef_ref, msg, W, force, window):
     b, b0, m0, m1, lam, mu2, mu = coefs(coef_ref, (C_B, C_B0, C_M0, C_M1, C_LAM, C_MU2, C_MU))
 
@@ -437,9 +346,10 @@
 
 
 def start_kernel(
-    velocity, stress, memory, layer_in, lam_in, mu_in, buoy_in, rate_in, defect_in, loads, steps_table,
-    V, S, R, coef_ref, msg_near, msg_far, msg_early, W, table, layer_ref, lam, mu, buoy, rate, defect, sems,
+    velocity, stress, memory, layer_in, lam_in, mu_in, buoy_in, rate_in, defect_in, after_this,
+    V, S, R, coef_ref, msg_near, msg_far, layer_ref, lam, mu, buoy, rate, defect, sems,
 ):
+    del after_this
     across = velocity.shape[2]
     inside = pl.ds(PAD, across)
     pairs = [
@@ -451,19 +361,8 @@
     copies = [pltpu.make_async_copy(*pair, sems.at[i]) for i, pair in enumerate(pairs)]
     for copy in copies:
         copy.start()
-    slots = loads.shape[0]
     zero_edges(V)
     zero_edges(S)
-    zero_edges(W)
-    table[...] = jnp.zeros(table.shape, jnp.float32)
-    table[0:16, :] = steps_table[...]
-    columns = table[...].T
-    trucks = 3 * across
-    msg_far[trucks : trucks + slots, :] = loads[...]
-    for i, at in enumerate((0, 8)):
-        first_row = trucks + (1 + i) * slots
-        column = columns[0:slots, at : at + 1]
-        msg_far[first_row : first_row + slots, :] = jnp.broadcast_to(column, loads.shape)
     for copy in copies[:6]:
         copy.wait()
     layer = layer_ref[...]
@@ -500,37 +399,53 @@
     for copy in copies[6:15]:
         copy.wait()
     even, _, _ = place()
-    now = Planes(msg_far, 0, across)
 
     @pl.when(even)
     def _():
         pre_ahead(V, S, coef_ref, msg_near, None, 0)
-        pre_behind(V, S, coef_ref, now, None, 0)
+        pre_behind(V, S, coef_ref, msg_far, None, 0)
 
     @pl.when(jnp.logical_not(even))
     def _():
         pre_behind(V, S, coef_ref, msg_near, None, 0)
-        pre_ahead(V, S, coef_ref, now, None, 0)
-
-    inner(V, S, coef_ref, None, 0)
+        pre_ahead(V, S, coef_ref, msg_far, None, 0)
+
     for copy in copies[15:]:
         copy.wait()
 
+
+def first_kernel(window, V0, S, R, coef_ref, force, surface, V, msg, W):
+    even, _, _ = place()
+    zero_edges(W)
+    now, then = force.at[0], force.at[1]
+    add_force(V, (VX, 1), now, (VX, 1), PAD + window)
+    add_force(V, (VY, 0), now, (VY, 0), PAD + window)
+    add_force(V, (VZ, 0), now, (VZ, 0), PAD + window)
+    inner(V, S, coef_ref, now, window)
+
     @pl.when(even)
     def _():
-        early_behind(V, S, R, coef_ref, None, 0, msg_early, W, None, 0)
+        early_behind(V, S, R, coef_ref, surface, 0, msg, W, then, window)
 
     @pl.when(jnp.logical_not(even))
     def _():
-        early_ahead(V, S, R, coef_ref, msg_early, W, None, 0)
+        early_ahead(V, S, R, coef_ref, msg, W, then, window)
+
+
+def write_out(V, S, R, results, sems, cell):
+    inside = pl.ds(PAD, R.shape[2])
+    pairs = [(V.at[:, cell, inside], results[0]), (S.at[:, cell, inside], results[1]), (R.at[:, cell], results[2])]
+    copies = [
+        pltpu.make_async_copy(source, result.at[:, cell], sems.at[i]) for i, (source, result) in enumerate(pairs)
+    ]
+    for copy in copies:
+        copy.start()
+    for copy in copies:
+        copy.wait()
 
 
 def near_kernel(step, window, V0, S0, R0, coef_ref, force, surface, msg, V, S, R, *rest):
     G = rest[-1]
-    if step == 0:
-        for comp in range(3):
-            for cell in range(2):
-                add_force(V, (comp, cell), force, (0, comp, cell), PAD + window)
     even, _, _ = place()
     more = step < STEPS - 1
 
@@ -539,60 +454,41 @@
         ahead_bond(V, S, R, coef_ref, force.at[step], surface, msg, None, G, step, window, 1)
         if more:
             pre_ahead(V, S, coef_ref, rest[0], force.at[step + 1], window)
+        else:
+            write_out(V, S, R, rest[:3], rest[-2], 1)
 
     @pl.when(jnp.logical_not(even))
     def _():
         behind_bond(V, S, R, coef_ref, force.at[step], surface, msg, None, G, step, window, 1)
         if more:
             pre_behind(V, S, coef_ref, rest[0], force.at[step + 1], window)
-
-
-def meet_kernel(across, msg, loads, load, rows_out):
-    slots = loads.shape[0]
-    rows, entry, cell = (msg[3 * across + i * slots : 3 * across + (i + 1) * slots, :] for i in range(3))
-    for slot in range(slots):
-        rows = jnp.where(entry == float(slot), loads[slot : slot + 1, :], rows)
-    rows_out[...] = jnp.zeros(rows_out.shape, jnp.float32)
-    rows_out[0:1, :] = jnp.sum(jnp.where(cell == 0.0, rows, 0.0), axis=0, keepdims=True)
-    load[...] = rows_out[...].T
+        else:
+            write_out(V, S, R, rest[:3], rest[-2], 0)
 
 
 def far_kernel(step, window, V0, S0, R0, coef_ref, force, surface, msg, *rest):
     rest = list(rest)
-    other = rest.pop(0)
+    missing = rest.pop(0) if step > 0 else None
     V, S, R, D = rest[:4]
+    G, W = rest[-2:]
     early = rest[4] if step < STEPS - 2 else None
-    across = R.shape[2]
     even, _, _ = place()
+    zero_edges(W)
     here, then = force.at[step], force.at[step + 1]
-    got = Planes(msg, 0, across) if step == 0 else msg
-    if step == 0:
-        missing, load = None, other
-        G, W, A = rest[-3:]
-    else:
-        missing = other
-        G, W = rest[-2:]
-    zero_edges(W)
 
     @pl.when(even)
     def _():
-        if step == 0:
-            respond = lambda: first_response_ahead(V, S, coef_ref, here, D, W, A, window)
-        else:
-            respond = lambda: response_ahead(V, S, coef_ref, D, W)
         behind_bond(
-            V, S, R, coef_ref, here, surface, got, missing, G, step, window, 2, respond
+            V, S, R, coef_ref, here, surface, msg, missing, G, step, window, 1,
+            lambda: response_ahead(V, S, coef_ref, D, W),
         )
         pre_behind(V, S, coef_ref, None, then, window)
 
     @pl.when(jnp.logical_not(even))
     def _():
-        if step == 0:
-            respond = lambda: first_response_behind(V, S, coef_ref, here, load, D, W, A, window)
-        else:
-            respond = lambda: response_behind(V, S, coef_ref, D, W)
         ahead_bond(
-            V, S, R, coef_ref, here, surface, got, missing, G, step, window, 2, respond
+            V, S, R, coef_ref, here, surface, msg, missing, G, step, window, 1,
+            lambda: response_behind(V, S, coef_ref, D, W),
         )
         pre_ahead(V, S, coef_ref, None, then, window)
 
@@ -609,40 +505,23 @@
             early_ahead(V, S, R, coef_ref, early, W, later, window)
 
 
-def last_kernel(
-    step, window, V0, S0, R0, coef_ref, force, surface, msg, missing, V, S, R, v_out, s_out, r_out, G, sems
-):
+def last_kernel(step, window, V0, S0, R0, coef_ref, force, surface, msg, missing, v0, s0, r0, V, S, R, *rest):
+    *results, G, sems = rest
     even, _, _ = place()
     here = force.at[step]
-    inside = pl.ds(PAD, R.shape[2])
-
-    def copies(cell):
-        return [
-            pltpu.make_async_copy(V.at[:, cell, inside], v_out.at[:, cell], sems.at[cell, 0]),
-            pltpu.make_async_copy(S.at[:, cell, inside], s_out.at[:, cell], sems.at[cell, 1]),
-            pltpu.make_async_copy(R.at[:, cell], r_out.at[:, cell], sems.at[cell, 2]),
-        ]
-
-    def finish(cell, bond):
-        done, other = copies(1 - cell), copies(cell)
-        for copy in done:
-            copy.start()
-        bond(V, S, R, coef_ref, here, surface, msg, missing, G, step, window)
-        for copy in other:
-            copy.start()
-        for copy in done + other:
-            copy.wait()
 
     @pl.when(even)
     def _():
-        finish(0, behind_bond)
+        behind_bond(V, S, R, coef_ref, here, surface, msg, missing, G, step, window)
+        write_out(V, S, R, results, sems, 0)
 
     @pl.when(jnp.logical_not(even))
     def _():
-        finish(1, ahead_bond)
-
-
-ENTRY_ROW, TRUCK_ROW = 48, 56
+        ahead_bond(V, S, R, coef_ref, here, surface, msg, missing, G, step, window)
+        write_out(V, S, R, results, sems, 1)
+
+
+ENTRY_ROW, TRUCK_ROW = 36, 40
 GROUP = 8
 
 
@@ -681,12 +560,10 @@
     me = lax.axis_index("line")
     group, mine = lax.div(me, tiles), lax.rem(me, tiles)
     piers = cell_of.shape[1]
-    row = lax.broadcasted_iota(jnp.int32, (4 * tiles, lanes), 0)
-    tile, j = lax.div(row, 4), lax.rem(row, 4)
-    odd = lax.rem(tile, 2)
-    first = (tile + group * tiles) * 2
-    cell_x = first + jnp.where(j == 2, -1, jnp.where(j == 3, 4 * odd - 2, j))
-    cell_yz = first + jnp.where(j == 3, 4 * odd - 1, j)
+    row = lax.broadcasted_iota(jnp.int32, (3 * tiles, lanes), 0)
+    j = lax.rem(row, 3)
+    first = (lax.div(row, 3) + group * tiles) * 2
+    cell_x, cell_yz = first + jnp.where(j == 2, -1, j), first + j
     record = jnp.where(group == 0, own[:, :panel], behind[:, :panel])
 
     def hits(cell):
@@ -707,9 +584,9 @@
     own_rows, own_entry = trucks(own)
     far_rows, far_entry = trucks(behind)
     for tile in range(tiles):
-        these = slice(4 * tile, 4 * tile + 4)
+        these = slice(3 * tile, 3 * tile + 3)
         for m in range(pieces):
-            out[tile, 4 * m : 4 * m + 4, :] = parts[m][these, :]
+            out[tile, 3 * m : 3 * m + 3, :] = parts[m][these, :]
         passed = mine < tile
         out[tile, ENTRY_ROW : ENTRY_ROW + 1, :] = jnp.where(passed, own_entry, far_entry)
         for i in range(slots // 8):
@@ -806,7 +683,6 @@
     m_type = pltpu.VMEM((3, across, depth), f32)
     ghost = pltpu.VMEM((2, across, depth), f32)
     work = pltpu.VMEM((2, padded, depth), f32)
-    square = pltpu.VMEM((across, depth), f32)
 
     def ahead_by(x, distance):
         return lax.ppermute(x, "line", [(i, i + distance) for i in range(tiles - distance)])
@@ -839,21 +715,19 @@
         behind = jnp.concatenate([record, behind[:, panel:]], axis=1)
         reach *= 2
     tables = (lame_lambda, lame_mu, buoyancy, relax_rate, defect_mu)
-    V, S, R, coef, msg_near, msg_far, early = call(
+    V, S, R, coef, msg_near, msg_far = call(
         start_kernel,
-        in_hbm(velocity, stress, memory, layer[None, :], *tables) + (in_vmem(loads), in_vmem(steps_table)),
-        (ANYWHERE,) * 9 + (WHOLE,) * 2,
-        (v_type, s_type, r_type, c_type, m_type, pltpu.VMEM((3 * across + 3 * slots, depth), f32), m_type),
-        (WHOLE,) * 7,
+        in_hbm(velocity, stress, memory, layer[None, :], *tables) + (steps_table,),
+        (ANYWHERE,) * 10,
+        (v_type, s_type, r_type, c_type, m_type, m_type),
+        (WHOLE,) * 6,
         scratch=(
-            work, pltpu.VMEM((depth, depth), f32), pltpu.VMEM((1, depth), jnp.int32),
-            *(pltpu.SMEM(table.shape, f32) for table in tables), dma((21,)),
+            pltpu.VMEM((1, depth), jnp.int32), *(pltpu.SMEM(table.shape, f32) for table in tables), dma((21,)),
         ),
         name="start",
         cost=8 * 1024 * 1024,
     )
     msg_far = lax.ppermute(msg_far, "line", far)
-    early = lax.ppermute(early, "line", far)
     msg_near = lax.ppermute(msg_near, "line", near)
     parts = call(
         functools.partial(split_kernel, panel, slots),
@@ -865,44 +739,47 @@
     )
     groups = [list(range(at, at + GROUP)) for at in range(0, tiles, GROUP)]
     parts = lax.all_to_all(parts, "line", 0, 0, axis_index_groups=groups, tiled=True)
-    load = call(
-        functools.partial(meet_kernel, across),
-        (in_vmem(msg_far), in_vmem(loads)),
-        (WHOLE,) * 2,
-        square,
-        WHOLE,
-        scratch=(pltpu.VMEM((depth, across), f32),),
-        name="meet",
-    )
     force, surface = call(
         prepare_kernel,
         (parts, in_vmem(loads), in_vmem(steps_table)),
         (WHOLE,) * 3,
-        (pltpu.VMEM((STEPS, 3, 4, 16, depth), f32), pltpu.VMEM((across, depth), f32)),
+        (pltpu.VMEM((STEPS, 3, 3, 16, depth), f32), pltpu.VMEM((across, depth), f32)),
         (WHOLE,) * 2,
         scratch=(pltpu.VMEM((depth, depth), f32), pltpu.VMEM((depth, across), f32)),
         name="prepare",
     )
+    V, early = call(
+        functools.partial(first_kernel, window),
+        tuple(in_vmem(x) for x in (V, S, R, coef, force, surface)),
+        (WHOLE,) * 6,
+        (v_type, m_type),
+        (WHOLE,) * 2,
+        scratch=(work,),
+        aliases={0: 0},
+        name="first",
+    )
+    early = lax.ppermute(early, "line", far)
     state = (v_type, s_type, r_type)
+    results = tuple(jax.ShapeDtypeStruct(x.shape, f32) for x in (velocity, stress, memory))
     same = {0: 0, 1: 1, 2: 2}
     missing = None
     for step in range(STEPS):
         more = step < STEPS - 1
         ins = tuple(in_vmem(x) for x in (V, S, R, coef, force, surface, msg_near))
-        outs = state + ((m_type,) if more else ())
+        outs = state + ((m_type,) if more else results)
         V, S, R, *msg = call(
             functools.partial(near_kernel, step, window),
             ins,
             (WHOLE,) * len(ins),
             outs,
-            (WHOLE,) * len(outs),
-            scratch=(ghost,),
+            (WHOLE,) * 4 if more else (WHOLE,) * 3 + (ANYWHERE,) * 3,
+            scratch=(ghost,) if more else (dma((3,)), ghost),
             aliases=same,
             name="near" + str(step),
         )
         if more:
             msg_near = lax.ppermute(msg[0], "line", near)
-        ins = (V, S, R, coef, force, surface, msg_far, missing if step else load)
+        ins = (V, S, R, coef, force, surface, msg_far) + ((missing,) if step else ())
         ins = tuple(in_vmem(x) for x in ins)
         if more:
             outs = state + (m_type,) + ((m_type,) if step < STEPS - 2 else ())
@@ -912,24 +789,24 @@
                 (WHOLE,) * len(ins),
                 outs,
                 (WHOLE,) * len(outs),
-                scratch=(ghost, work) + (() if step else (pltpu.VMEM((5, padded, depth), f32),)),
+                scratch=(ghost, work),
                 aliases=same,
                 name="far" + str(step),
             )
             msg_far = early
             if msg:
                 early = lax.ppermute(msg[0], "line", far)
-    results = call(
+    ends = call(
         functools.partial(last_kernel, STEPS - 1, window),
-        ins,
-        (WHOLE,) * len(ins),
-        state + tuple(jax.ShapeDtypeStruct(x.shape, f32) for x in (velocity, stress, memory)),
+        ins + tuple(msg),
+        (WHOLE,) * 8 + (ANYWHERE,) * 3,
+        state + results,
         (WHOLE,) * 3 + (ANYWHERE,) * 3,
-        scratch=(ghost, pltpu.SemaphoreType.DMA((2, 3))),
-        aliases=same,
+        scratch=(ghost, dma((3,))),
+        aliases={**same, 8: 3, 9: 4, 10: 5},
         name="last",
     )
-    return results[3:]
+    return ends[3:]
 
 
 def solution(mesh):

time: 59.5 us -> 52.5 us (0.88)
  waiting for transfers between devices: 20.2 us -> 12.2 us
  Pallas kernels: 10.2 us -> 10.8 us
    ppermute x4, waiting for transfers between devices: 11.1 us -> 6.25 us  [body(): early = lax.ppermute(msg[0], 'line', far)]
    ppermute x5, starting transfers between devices: 3.96 us -> 1.22 us  [body(): msg_near = lax.ppermute(msg[0], 'line', near)]
    ppermute x1, waiting for transfers between devices: 4.49 us -> 1.76 us  [body(): early = lax.ppermute(early, 'line', far)]
    ppermute x4, starting transfers between devices: 10.6 us -> 12.8 us  [body(): early = lax.ppermute(msg[0], 'line', far)]
    ppermute x1, starting transfers between devices: 1.91 us -> 2.85 us  [body(): early = lax.ppermute(early, 'line', far)]
    all_to_all x1, waiting for transfers between devices: 1.94 us -> 1.3 us  [body(): lax.all_to_all(parts, 'line', 0, 0, axis_index_groups=groups, tiled=True)]
    pallas_call x17, Pallas kernels: 10.2 us -> 10.8 us  [call(): pl.pallas_call(kernel, out_shape=outs, in_specs=specs, out_specs=out_spec...]
  transfers between devices with their start and end apart: 14 -> 14, of which waited for: 5 -> 7; matrix products, arithmetic and copies ran while one was open for 0% -> 0% of each run, Pallas kernels for 12% -> 15%
where the time goes in v10:
time: 52.5 us; the launch traced here: 52 us
  starting transfers between devices  28.1 us (54%)
  waiting for transfers between devices  12.2 us (23%)
  Pallas kernels  10.8 us (21%)
  between operations  0.88 us (2%)
    ppermute x4, starting transfers between devices, body(): early = lax.ppermute(msg[0], 'line', far)  12.8 us
    pallas_call x17, Pallas kernels, call(): pl.pallas_call(kernel, out_shape=outs, in_specs=specs, out_specs=out_spec...  10.8 us
    all_to_all x1, starting transfers between devices, body(): lax.all_to_all(parts, 'line', 0, 0, axis_index_groups=groups, tiled=True)  6.3 us
    ppermute x4, waiting for transfers between devices, body(): early = lax.ppermute(msg[0], 'line', far)  6.25 us
    ppermute x1, starting transfers between devices, body(): msg_far = lax.ppermute(msg_far, 'line', far)  3.67 us
    ppermute x1, starting transfers between devices, body(): early = lax.ppermute(early, 'line', far)  2.85 us
    ppermute x1, waiting for transfers between devices, ahead_by(): lax.ppermute(x, 'line', [(i, i + distance) for i in range(tiles - distanc...  2.85 us
    ppermute x1, waiting for transfers between devices, body(): early = lax.ppermute(early, 'line', far)  1.76 us
  transfers between devices with their start and end apart: 14, of which 7 were waited for; matrix products, arithmetic and copies ran while one was open for 0% of the time, Pallas kernels for 15%

profile of v10, /device:TPU:17, one launch (start us, length us, event | category | flops | bytes accessed | tf_op | source)
XLA Modules:
  0.0 52.0 jit_solution(6662830733338602059)
XLA Ops:
  0.6 0.9 %pack.1 = (f32[8,1920]{1,0:T(8,128)S(1)}, f32[16,128]{1,0:T(8,128)S(1)}, f32[16,128]{1,0:T(8,128)S(1)}, s32[1,8]{1,0:T(1,128)S(1)}) custom-call(f32[8,1536]{1,0:T(8,128)} %bitcast.3, f32[16,128]{1,0:T(8,128)} %loads_in.1, s32[6,16]{1,0:T(8,128)} %entries_in.1, s32[6,16]{1,0:T(8,128)} %cells_in.1, s32[1,8]{1,0:T(1,128)} %bitcast.4), custom_call_target="tpu_custom_call" | custom-call | flops 1 | bytes 1 | tf_op jit(solution)/shard_map/pack/pallas_call | solution.py:651
  1.5 1.3 %collective-permute-start = (f32[8,1920]{1,0:T(8,128)S(1)}, f32[8,1920]{1,0:T(8,128)S(1)}, u32[]{:S(2)}, u32[]{:S(2)}) collective-permute-start(f32[8,1920]{1,0:T(8,128)S(1)} %get-tuple-element.75.own), channel_id=1, source_target_pairs={{0,8},{1,9},{2,10},{3,11},{4,12},{5,13},{6,14},{7,15},{16,24},{17,... | collective-permute-start | bytes 184328 | tf_op jit(solution)/shard_map/ppermute | solution.py:688
  2.8 1.8 %start.1 = (f32[3,2,144,128]{3,2,1,0:T(8,128)S(1)}, f32[6,2,144,128]{3,2,1,0:T(8,128)S(1)}, f32[6,2,128,128]{3,2,1,0:T(8,128)S(1)}, f32[16,128]{1,0:T(8,128)S(1)...) custom-call(f32[3,2,128,128]{3,2,1,0:T(8,128)} %velocity.1, f32[6,2,128,128]{3,2,1,0:T(8,128)} %stress.1, ...), custom_call_target="tpu_custom_call" | custom-call | flops 8388608 | bytes 8388608 | tf_op jit(solution)/shard_map/start/pallas_call | solution.py:651
  4.6 2.8 %collective-permute-done.behind = f32[8,1920]{1,0:T(8,128)S(1)} collective-permute-done((f32[8,1920]{1,0:T(8,128)S(1)}, f32[8,1920]{1,0:T(8,128)S(1)}, u32[]{:S(2)}, u32[]{:S(2)}) %collective-permute-start) | collective-permute-done | bytes 61472 | tf_op jit(solution)/shard_map/ppermute | solution.py:688
  7.4 0.9 %split.1 = f32[8,56,128]{2,1,0:T(8,128)} custom-call(f32[8,1920]{1,0:T(8,128)S(1)} %get-tuple-element.75.own, f32[8,1920]{1,0:T(8,128)S(1)} %collective-permute-done.behind, s32[1,8]{1,0:T(1,128)S(1)} %get-tuple-element.76.cells, f32[16,128]{1,0:T(8,128)S(1)} %get-tuple-element.74.after_this.coef_ref), custom_call_target="tpu_custom_call" | custom-call | flops 1 | bytes 1 | tf_op jit(solution)/shard_map/split/pallas_call | solution.py:651
  8.3 6.3 %all-to-all-start = ((f32[8,56,128]{2,1,0:T(8,128)}), f32[8,56,128]{2,1,0:T(8,128)S(1)}, u32[]{:S(2)}, u32[]{:S(2)}) async-start(f32[8,56,128]{2,1,0:T(8,128)} %split.1), calls=%async_computation | async-start | bytes 458752 | tf_op jit(solution)/shard_map/all_to_all | solution.py:741
  14.6 0.0 collective-permute-start.1
  14.6 3.7 %collective-permute-start.2 = (f32[3,128,128]{2,1,0:T(8,128)S(1)}, f32[3,128,128]{2,1,0:T(8,128)S(1)}, u32[]{:S(2)}, u32[]{:S(2)}) collective-permute-start(f32[3,128,128]{2,1,0:T(8,128)S(1)} %get-tuple-element.85), channel_id=1, source_target_pairs={{1,2},{3,4},{5,6},{7,8},{9,10},{11,12},{13,14},{2,1},{4,3},{6,5},{... | collective-permute-start | bytes 589832 | tf_op jit(solution)/shard_map/ppermute | solution.py:730
  18.3 1.3 %all-to-all-done.parts = f32[8,56,128]{2,1,0:T(8,128)S(1)} async-done(((f32[8,56,128]{2,1,0:T(8,128)}), f32[8,56,128]{2,1,0:T(8,128)S(1)}, u32[]{:S(2)}, u32[]{:S(2)}) %all-to-all-start) | async-done | bytes 229408 | tf_op jit(solution)/shard_map/all_to_all | solution.py:741
  19.6 0.6 %prepare.1 = (f32[6,3,3,16,128]{4,3,2,1,0:T(8,128)S(1)}, f32[128,128]{1,0:T(8,128)S(1)}) custom-call(f32[8,56,128]{2,1,0:T(8,128)S(1)} %all-to-all-done.parts, f32[16,128]{1,0:T(8,128)S(1)} %get-tuple-element.77.loads, f32[16,128]{1,0:T(8,128)S(1)} %get-tuple-element.70.after_this.steps_table), custom_call_target="tpu_custom_call" | custom-call | flops 1 | bytes 1 | tf_op jit(solution)/shard_map/prepare/pallas_call | solution.py:651
  20.2 0.3 first.1
  20.4 0.0 collective-permute-done.1.msg
  20.5 0.3 near0.1
  20.7 0.9 %collective-permute-start.3 = (f32[3,128,128]{2,1,0:T(8,128)S(1)}, f32[3,128,128]{2,1,0:T(8,128)S(1)}, u32[]{:S(2)}, u32[]{:S(2)}) collective-permute-start(f32[3,128,128]{2,1,0:T(8,128)S(1)} %get-tuple-element.89), channel_id=1, source_target_pairs={{0,1},{1,0},{2,3},{3,2},{4,5},{5,4},{6,7},{7,6},{8,9},{9,8},{10,11... | collective-permute-start | bytes 589832 | tf_op jit(solution)/shard_map/ppermute | solution.py:781
  21.7 2.9 %collective-permute-start.4 = (f32[3,128,128]{2,1,0:T(8,128)S(1)}, f32[3,128,128]{2,1,0:T(8,128)S(1)}, u32[]{:S(2)}, u32[]{:S(2)}) collective-permute-start(f32[3,128,128]{2,1,0:T(8,128)S(1)} %get-tuple-element.93), channel_id=1, source_target_pairs={{1,2},{3,4},{5,6},{7,8},{9,10},{11,12},{13,14},{2,1},{4,3},{6,5},{... | collective-permute-start | bytes 589832 | tf_op jit(solution)/shard_map/ppermute | solution.py:761
  24.5 0.0 collective-permute-done.2.msg
  24.5 0.6 %far0.1 = (f32[3,2,144,128]{3,2,1,0:T(8,128)S(1)}, f32[6,2,144,128]{3,2,1,0:T(8,128)S(1)}, f32[6,2,128,128]{3,2,1,0:T(8,128)S(1)}, f32[3,128,128]{2,1,0:T(8,128)S(1)}, f32[3,128,128]{2,1,0:T(8,128)S(1)}) custom-call(f32[3,2,144,128]{3,2,1,0:T(8,128)S(1)} %get-tuple-element.82.V0, ...), custom_call_target="tpu_custom_call", output_to_operand_aliasing={{0}: (0, {}), {1}: (1, {}), {2}: (2, {})} | custom-call | flops 1 | bytes 1 | tf_op jit(solution)/shard_map/far0/pallas_call | solution.py:651
  25.2 0.0 collective-permute-done.3.msg
  25.2 0.3 near1.1
  25.5 0.1 collective-permute-start.5
  25.5 3.5 %collective-permute-start.6 = (f32[3,128,128]{2,1,0:T(8,128)S(1)}, f32[3,128,128]{2,1,0:T(8,128)S(1)}, u32[]{:S(2)}, u32[]{:S(2)}) collective-permute-start(f32[3,128,128]{2,1,0:T(8,128)S(1)} %get-tuple-element.102), channel_id=1, source_target_pairs={{1,2},{3,4},{5,6},{7,8},{9,10},{11,12},{13,14},{2,1},{4,3},{6,5},{... | collective-permute-start | bytes 589832 | tf_op jit(solution)/shard_map/ppermute | solution.py:798
  29.0 1.8 %collective-permute-done.4.msg = f32[3,128,128]{2,1,0:T(8,128)S(1)} collective-permute-done((f32[3,128,128]{2,1,0:T(8,128)S(1)}, f32[3,128,128]{2,1,0:T(8,128)S(1)}, u32[]{:S(2)}, u32[]{:S(2)}) %collective-permute-start.4) | collective-permute-done | bytes 196640 | tf_op jit(solution)/shard_map/ppermute | solution.py:761
  30.8 0.6 %far1.1 = (f32[3,2,144,128]{3,2,1,0:T(8,128)S(1)}, f32[6,2,144,128]{3,2,1,0:T(8,128)S(1)}, f32[6,2,128,128]{3,2,1,0:T(8,128)S(1)}, f32[3,128,128]{2,1,0:T(8,128)S(1)}, f32[3,128,128]{2,1,0:T(8,128)S(1)}) custom-call(f32[3,2,144,128]{3,2,1,0:T(8,128)S(1)} %get-tuple-element.90.V0, ...), custom_call_target="tpu_custom_call", output_to_operand_aliasing={{0}: (0, {}), {1}: (1, {}), {2}: (2, {})} | custom-call | flops 1 | bytes 1 | tf_op jit(solution)/shard_map/far1/pallas_call | solution.py:651
  31.4 0.0 collective-permute-done.5.msg
  31.4 0.3 near2.1
  31.7 0.1 collective-permute-start.7
  31.7 2.9 %collective-permute-start.8 = (f32[3,128,128]{2,1,0:T(8,128)S(1)}, f32[3,128,128]{2,1,0:T(8,128)S(1)}, u32[]{:S(2)}, u32[]{:S(2)}) collective-permute-start(f32[3,128,128]{2,1,0:T(8,128)S(1)} %get-tuple-element.111), channel_id=1, source_target_pairs={{1,2},{3,4},{5,6},{7,8},{9,10},{11,12},{13,14},{2,1},{4,3},{6,5},{... | collective-permute-start | bytes 589832 | tf_op jit(solution)/shard_map/ppermute | solution.py:798
  34.6 0.3 collective-permute-done.6.msg
  35.0 0.6 %far2.1 = (f32[3,2,144,128]{3,2,1,0:T(8,128)S(1)}, f32[6,2,144,128]{3,2,1,0:T(8,128)S(1)}, f32[6,2,128,128]{3,2,1,0:T(8,128)S(1)}, f32[3,128,128]{2,1,0:T(8,128)S(1)}, f32[3,128,128]{2,1,0:T(8,128)S(1)}) custom-call(f32[3,2,144,128]{3,2,1,0:T(8,128)S(1)} %get-tuple-element.99.V0, ...), custom_call_target="tpu_custom_call", output_to_operand_aliasing={{0}: (0, {}), {1}: (1, {}), {2}: (2, {})} | custom-call | flops 1 | bytes 1 | tf_op jit(solution)/shard_map/far2/pallas_call | solution.py:651
  35.6 0.0 collective-permute-done.7.msg
  35.6 0.3 near3.1
  35.9 0.1 collective-permute-start.9
  36.0 3.6 %collective-permute-start.10 = (f32[3,128,128]{2,1,0:T(8,128)S(1)}, f32[3,128,128]{2,1,0:T(8,128)S(1)}, u32[]{:S(2)}, u32[]{:S(2)}) collective-permute-start(f32[3,128,128]{2,1,0:T(8,128)S(1)} %get-tuple-element.120), channel_id=1, source_target_pairs={{1,2},{3,4},{5,6},{7,8},{9,10},{11,12},{13,14},{2,1},{4,3},{6,5},{... | collective-permute-start | bytes 589832 | tf_op jit(solution)/shard_map/ppermute | solution.py:798
  39.6 1.3 %collective-permute-done.8.msg = f32[3,128,128]{2,1,0:T(8,128)S(1)} collective-permute-done((f32[3,128,128]{2,1,0:T(8,128)S(1)}, f32[3,128,128]{2,1,0:T(8,128)S(1)}, u32[]{:S(2)}, u32[]{:S(2)}) %collective-permute-start.8) | collective-permute-done | bytes 196640 | tf_op jit(solution)/shard_map/ppermute | solution.py:798
  40.8 0.6 %far3.1 = (f32[3,2,144,128]{3,2,1,0:T(8,128)S(1)}, f32[6,2,144,128]{3,2,1,0:T(8,128)S(1)}, f32[6,2,128,128]{3,2,1,0:T(8,128)S(1)}, f32[3,128,128]{2,1,0:T(8,128)S(1)}, f32[3,128,128]{2,1,0:T(8,128)S(1)}) custom-call(f32[3,2,144,128]{3,2,1,0:T(8,128)S(1)} %get-tuple-element.108.V0, ...), custom_call_target="tpu_custom_call", output_to_operand_aliasing={{0}: (0, {}), {1}: (1, {}), {2}: (2, {})} | custom-call | flops 1 | bytes 1 | tf_op jit(solution)/shard_map/far3/pallas_call | solution.py:651
  41.5 0.0 collective-permute-done.9.msg
  41.5 0.3 near4.1
  41.8 0.1 collective-permute-start.11
  41.8 2.9 %collective-permute-start.12 = (f32[3,128,128]{2,1,0:T(8,128)S(1)}, f32[3,128,128]{2,1,0:T(8,128)S(1)}, u32[]{:S(2)}, u32[]{:S(2)}) collective-permute-start(f32[3,128,128]{2,1,0:T(8,128)S(1)} %get-tuple-element.129), channel_id=1, source_target_pairs={{1,2},{3,4},{5,6},{7,8},{9,10},{11,12},{13,14},{2,1},{4,3},{6,5},{... | collective-permute-start | bytes 589832 | tf_op jit(solution)/shard_map/ppermute | solution.py:798
  44.7 0.3 collective-permute-done.10.msg
  45.1 0.4 far4.1
  45.5 0.0 collective-permute-done.11.msg
  45.5 1.1 %near5.1 = (f32[3,2,144,128]{3,2,1,0:T(8,128)S(1)}, f32[6,2,144,128]{3,2,1,0:T(8,128)S(1)}, f32[6,2,128,128]{3,2,1,0:T(8,128)S(1)}, f32[3,2,128,128]{3,2,1,0:T(8...) custom-call(f32[3,2,144,128]{3,2,1,0:T(8,128)S(1)} %get-tuple-elemen, ...), custom_call_target="tpu_custom_call", output_to_operand_aliasing={{0}: (0, {}), {1}: (1, {}), {2}: (2, {})} | custom-call | flops 1 | bytes 1 | tf_op jit(solution)/shard_map/near5/pallas_call | solution.py:651
  46.6 4.3 %collective-permute-done.12.msg = f32[3,128,128]{2,1,0:T(8,128)S(1)} collective-permute-done((f32[3,128,128]{2,1,0:T(8,128)S(1)}, f32[3,128,128]{2,1,0:T(8,128)S(1)}, u32[]{:S(2)}, u32[]{:S(2)}) %collective-permute-start.12) | collective-permute-done | bytes 196640 | tf_op jit(solution)/shard_map/ppermute | solution.py:798
  50.9 1.1 %last.1 = (f32[3,2,144,128]{3,2,1,0:T(8,128)S(1)}, f32[6,2,144,128]{3,2,1,0:T(8,128)S(1)}, f32[6,2,128,128]{3,2,1,0:T(8,128)S(1)}, f32[3,2,128,128]{3,2,1,0:T(8,...) custom-call(f32[3,2,144,128]{3,2,1,0:T(8,128)S(1)} %get-tuple-elemen, ...), custom_call_target="tpu_custom_call", output_to_operand_aliasing={{0}: (0, {}), {1}: (1, {}), {2}: (2, {}), {3}: (8, {}), {4}... | custom-call | flops 1 | bytes 1 | tf_op jit(solution)/shard_map/last/pallas_call | solution.py:651
Async XLA Ops:
  1.5 5.9 %collective-permute-start = (f32[8,1920]{1,0:T(8,128)S(1)}, f32[8,1920]{1,0:T(8,128)S(1)}, u32[]{:S(2)}, u32[]{:S(2)}) collective-permute-start(f32[8,1920]{1,0:T(8,128)S(1)} %get-tuple-element.75.own), channel_id=1, source_target_pairs={{0,8},{1,9},{2,10},{3,11},{4,12},{5,13},{6,14},{7,15},{16,24},{17,... | collective-permute-start | bytes 184328 | tf_op jit(solution)/shard_map/ppermute | solution.py:688
  8.3 11.3 %all-to-all-start = ((f32[8,56,128]{2,1,0:T(8,128)}), f32[8,56,128]{2,1,0:T(8,128)S(1)}, u32[]{:S(2)}, u32[]{:S(2)}) async-start(f32[8,56,128]{2,1,0:T(8,128)} %split.1), calls=%async_computation | async-start | bytes 458752 | tf_op jit(solution)/shard_map/all_to_all | solution.py:741
  14.6 5.9 %collective-permute-start.1 = (f32[3,128,128]{2,1,0:T(8,128)S(1)}, f32[3,128,128]{2,1,0:T(8,128)S(1)}, u32[]{:S(2)}, u32[]{:S(2)}) collective-permute-start(f32[3,128,128]{2,1,0:T(8,128)S(1)} %get-tuple-element.81), channel_id=1, source_target_pairs={{0,1},{1,0},{2,3},{3,2},{4,5},{5,4},{6,7},{7,6},{8,9},{9,8},{10,11... | collective-permute-start | bytes 589832 | tf_op jit(solution)/shard_map/ppermute | solution.py:731
  14.6 9.9 %collective-permute-start.2 = (f32[3,128,128]{2,1,0:T(8,128)S(1)}, f32[3,128,128]{2,1,0:T(8,128)S(1)}, u32[]{:S(2)}, u32[]{:S(2)}) collective-permute-start(f32[3,128,128]{2,1,0:T(8,128)S(1)} %get-tuple-element.85), channel_id=1, source_target_pairs={{1,2},{3,4},{5,6},{7,8},{9,10},{11,12},{13,14},{2,1},{4,3},{6,5},{... | collective-permute-start | bytes 589832 | tf_op jit(solution)/shard_map/ppermute | solution.py:730
  20.7 4.4 %collective-permute-start.3 = (f32[3,128,128]{2,1,0:T(8,128)S(1)}, f32[3,128,128]{2,1,0:T(8,128)S(1)}, u32[]{:S(2)}, u32[]{:S(2)}) collective-permute-start(f32[3,128,128]{2,1,0:T(8,128)S(1)} %get-tuple-element.89), channel_id=1, source_target_pairs={{0,1},{1,0},{2,3},{3,2},{4,5},{5,4},{6,7},{7,6},{8,9},{9,8},{10,11... | collective-permute-start | bytes 589832 | tf_op jit(solution)/shard_map/ppermute | solution.py:781
  21.7 9.1 %collective-permute-start.4 = (f32[3,128,128]{2,1,0:T(8,128)S(1)}, f32[3,128,128]{2,1,0:T(8,128)S(1)}, u32[]{:S(2)}, u32[]{:S(2)}) collective-permute-start(f32[3,128,128]{2,1,0:T(8,128)S(1)} %get-tuple-element.93), channel_id=1, source_target_pairs={{1,2},{3,4},{5,6},{7,8},{9,10},{11,12},{13,14},{2,1},{4,3},{6,5},{... | collective-permute-start | bytes 589832 | tf_op jit(solution)/shard_map/ppermute | solution.py:761
  25.5 5.9 %collective-permute-start.5 = (f32[3,128,128]{2,1,0:T(8,128)S(1)}, f32[3,128,128]{2,1,0:T(8,128)S(1)}, u32[]{:S(2)}, u32[]{:S(2)}) collective-permute-start(f32[3,128,128]{2,1,0:T(8,128)S(1)} %get-tuple-element.98), channel_id=1, source_target_pairs={{0,1},{1,0},{2,3},{3,2},{4,5},{5,4},{6,7},{7,6},{8,9},{9,8},{10,11... | collective-permute-start | bytes 589832 | tf_op jit(solution)/shard_map/ppermute | solution.py:781
  25.5 9.4 %collective-permute-start.6 = (f32[3,128,128]{2,1,0:T(8,128)S(1)}, f32[3,128,128]{2,1,0:T(8,128)S(1)}, u32[]{:S(2)}, u32[]{:S(2)}) collective-permute-start(f32[3,128,128]{2,1,0:T(8,128)S(1)} %get-tuple-element.102), channel_id=1, source_target_pairs={{1,2},{3,4},{5,6},{7,8},{9,10},{11,12},{13,14},{2,1},{4,3},{6,5},{... | collective-permute-start | bytes 589832 | tf_op jit(solution)/shard_map/ppermute | solution.py:798
  31.7 3.9 %collective-permute-start.7 = (f32[3,128,128]{2,1,0:T(8,128)S(1)}, f32[3,128,128]{2,1,0:T(8,128)S(1)}, u32[]{:S(2)}, u32[]{:S(2)}) collective-permute-start(f32[3,128,128]{2,1,0:T(8,128)S(1)} %get-tuple-element.107), channel_id=1, source_target_pairs={{0,1},{1,0},{2,3},{3,2},{4,5},{5,4},{6,7},{7,6},{8,9},{9,8},{10,11... | collective-permute-start | bytes 589832 | tf_op jit(solution)/shard_map/ppermute | solution.py:781
  31.7 9.1 %collective-permute-start.8 = (f32[3,128,128]{2,1,0:T(8,128)S(1)}, f32[3,128,128]{2,1,0:T(8,128)S(1)}, u32[]{:S(2)}, u32[]{:S(2)}) collective-permute-start(f32[3,128,128]{2,1,0:T(8,128)S(1)} %get-tuple-element.111), channel_id=1, source_target_pairs={{1,2},{3,4},{5,6},{7,8},{9,10},{11,12},{13,14},{2,1},{4,3},{6,5},{... | collective-permute-start | bytes 589832 | tf_op jit(solution)/shard_map/ppermute | solution.py:798
  35.9 5.6 %collective-permute-start.9 = (f32[3,128,128]{2,1,0:T(8,128)S(1)}, f32[3,128,128]{2,1,0:T(8,128)S(1)}, u32[]{:S(2)}, u32[]{:S(2)}) collective-permute-start(f32[3,128,128]{2,1,0:T(8,128)S(1)} %get-tuple-element.116), channel_id=1, source_target_pairs={{0,1},{1,0},{2,3},{3,2},{4,5},{5,4},{6,7},{7,6},{8,9},{9,8},{10,11... | collective-permute-start | bytes 589832 | tf_op jit(solution)/shard_map/ppermute | solution.py:781
  36.0 9.1 %collective-permute-start.10 = (f32[3,128,128]{2,1,0:T(8,128)S(1)}, f32[3,128,128]{2,1,0:T(8,128)S(1)}, u32[]{:S(2)}, u32[]{:S(2)}) collective-permute-start(f32[3,128,128]{2,1,0:T(8,128)S(1)} %get-tuple-element.120), channel_id=1, source_target_pairs={{1,2},{3,4},{5,6},{7,8},{9,10},{11,12},{13,14},{2,1},{4,3},{6,5},{... | collective-permute-start | bytes 589832 | tf_op jit(solution)/shard_map/ppermute | solution.py:798
  41.8 3.8 %collective-permute-start.11 = (f32[3,128,128]{2,1,0:T(8,128)S(1)}, f32[3,128,128]{2,1,0:T(8,128)S(1)}, u32[]{:S(2)}, u32[]{:S(2)}) collective-permute-start(f32[3,128,128]{2,1,0:T(8,128)S(1)} %get-tuple-element.125), channel_id=1, source_target_pairs={{0,1},{1,0},{2,3},{3,2},{4,5},{5,4},{6,7},{7,6},{8,9},{9,8},{10,11... | collective-permute-start | bytes 589832 | tf_op jit(solution)/shard_map/ppermute | solution.py:781
  41.8 9.1 %collective-permute-start.12 = (f32[3,128,128]{2,1,0:T(8,128)S(1)}, f32[3,128,128]{2,1,0:T(8,128)S(1)}, u32[]{:S(2)}, u32[]{:S(2)}) collective-permute-start(f32[3,128,128]{2,1,0:T(8,128)S(1)} %get-tuple-element.129), channel_id=1, source_target_pairs={{1,2},{3,4},{5,6},{7,8},{9,10},{11,12},{13,14},{2,1},{4,3},{6,5},{... | collective-permute-start | bytes 589832 | tf_op jit(solution)/shard_map/ppermute | solution.py:798

commit v11 on v10

--- a/solution.py
+++ b/solution.py
@@ -225,7 +225,7 @@
     over_rows(D.shape[1], rest)
 
 
-def early_ahead(V, S, R, coef_ref, msg, W, force, window):
+def early_ahead(V, S, R, coef_ref, msg, W, force, window, ready):
     b, b0, m0, m1, lam, mu2, mu = coefs(coef_ref, (C_B, C_B0, C_M0, C_M1, C_LAM, C_MU2, C_MU))
 
     def work(r):
@@ -242,17 +242,19 @@
         msg[2, out] = vx + b * (sxy + sxz - sxx) - b0 * before(sxz)
 
     over_rows(msg.shape[1], work)
+    ready(0)
+    ready(1)
 
     def rest(r):
         _, up, _, out = spans(r)
         msg[2, out] = msg[2, out] - b * W[0, up]
 
     over_rows(msg.shape[1], rest)
-    if force is not None:
-        add_force(msg, (2,), force, (VX, 1), window)
-
-
-def early_behind(V, S, R, coef_ref, surface, column, msg, W, force, window):
+    add_force(msg, (2,), force, (VX, 1), window)
+    ready(2)
+
+
+def early_behind(V, S, R, coef_ref, surface, column, msg, W, force, window, ready):
     b, b0, b1, m0, m1, lam, mu2, mu, l0 = coefs(
         coef_ref, (C_B, C_B0, C_B1, C_M0, C_M1, C_LAM, C_MU2, C_MU, C_L0)
     )
@@ -266,8 +268,7 @@
         sxx = S[XX, 0, here] + (volume + mu2 * vx) + DT * R[XX, 0, out]
         syy = S[YY, 0, here] + (volume + mu2 * eyy) + DT * R[YY, 0, out]
         szz = S[ZZ, 0, here] + (volume + mu2 * ezz) + DT * R[ZZ, 0, out]
-        if surface is not None:
-            szz = szz + l0 * lane_roll(surface[out, :], -column)
+        szz = szz + l0 * lane_roll(surface[out, :], -column)
         sxy = S[XY, 0, here] + mu * (V[VX, 0, down] - vx + (V[VY, 1, here] - vy)) + DT * R[XY, 0, out]
         sxz = S[XZ, 0, here] + mu * (m1 * after(vx) - vx + (V[VZ, 1, here] - vz)) + DT * R[XZ, 0, out]
         syz = S[YZ, 0, here] + mu * (m1 * after(vy) - vy + (V[VZ, 0, down] - vz)) + DT * R[YZ, 0, out]
@@ -278,6 +279,7 @@
         msg[2, out] = vz + b * (sxz + syz - szz) + b1 * after(szz)
 
     over_rows(msg.shape[1], work)
+    ready(0)
 
     def rest(r):
         _, up, down, out = spans(r)
@@ -285,24 +287,37 @@
         msg[2, out] = msg[2, out] - b * W[1, up]
 
     over_rows(msg.shape[1], rest)
-    if force is not None:
-        add_force(msg, (1,), force, (VY, 0), window)
-        add_force(msg, (2,), force, (VZ, 0), window)
+    add_force(msg, (1,), force, (VY, 0), window)
+    add_force(msg, (2,), force, (VZ, 0), window)
+    ready(1)
+    ready(2)
+
+
+class Outgoing:
+    def __init__(self, msg, out, sems, chunk):
+        self.copies = [pltpu.make_async_copy(msg.at[i], out.at[chunk, i], sems.at[i]) for i in range(3)]
+
+    def ready(self, i):
+        self.copies[i].start()
+
+    def finish(self):
+        for copy in self.copies:
+            copy.wait()
 
 
 def ahead_bond(V, S, R, coef_ref, force, surface, msg, missing, G, step, window, unforced=0, respond=None):
     (b,) = coefs(coef_ref, (C_B,))
     _, _, has_ahead = place()
-    keep = jnp.where(has_ahead, 1.0, 0.0).astype(jnp.float32)
 
     def got(i, out):
-        return msg[i, out] if missing is None else msg[i, out] + missing[i, out]
+        plane = msg[i, out] if missing is None else msg[i, out] + missing[i, out]
+        return jnp.where(has_ahead, plane, 0.0)
 
     def work(r):
         here, _, _, out = spans(r)
-        V[VX, 1, here] = V[VX, 1, here] + (keep * b) * got(0, out)
-        G[0, out] = keep * (got(1, out) - b * S[XY, 1, here])
-        G[1, out] = keep * (got(2, out) - b * S[XZ, 1, here])
+        V[VX, 1, here] = V[VX, 1, here] + b * got(0, out)
+        G[0, out] = jnp.where(has_ahead, got(1, out) - b * S[XY, 1, here], 0.0)
+        G[1, out] = jnp.where(has_ahead, got(2, out) - b * S[XZ, 1, here], 0.0)
 
     over_rows(R.shape[2], work)
     if step < unforced:
@@ -321,16 +336,16 @@
 def behind_bond(V, S, R, coef_ref, force, surface, msg, missing, G, step, window, unforced=0, respond=None):
     (b,) = coefs(coef_ref, (C_B,))
     _, has_behind, _ = place()
-    keep = jnp.where(has_behind, 1.0, 0.0).astype(jnp.float32)
 
     def got(i, out):
-        return msg[i, out] if missing is None else msg[i, out] + missing[i, out]
+        plane = msg[i, out] if missing is None else msg[i, out] + missing[i, out]
+        return jnp.where(has_behind, plane, 0.0)
 
     def work(r):
         here, _, _, out = spans(r)
-        V[VY, 0, here] = V[VY, 0, here] - (keep * b) * got(0, out)
-        V[VZ, 0, here] = V[VZ, 0, here] - (keep * b) * got(1, out)
-        G[0, out] = keep * (got(2, out) + b * S[XX, 0, here])
+        V[VY, 0, here] = V[VY, 0, here] - b * got(0, out)
+        V[VZ, 0, here] = V[VZ, 0, here] - b * got(1, out)
+        G[0, out] = jnp.where(has_behind, got(2, out) + b * S[XX, 0, here], 0.0)
 
     over_rows(R.shape[2], work)
     if step < unforced:
@@ -414,7 +429,7 @@
         copy.wait()
 
 
-def first_kernel(window, V0, S, R, coef_ref, force, surface, V, msg, W):
+def first_kernel(window, V0, S, R, coef_ref, force, surface, V, out, msg, W, sems):
     even, _, _ = place()
     zero_edges(W)
     now, then = force.at[0], force.at[1]
@@ -425,11 +440,15 @@
 
     @pl.when(even)
     def _():
-        early_behind(V, S, R, coef_ref, surface, 0, msg, W, then, window)
+        outgoing = Outgoing(msg, out, sems, 0)
+        early_behind(V, S, R, coef_ref, surface, 0, msg, W, then, window, outgoing.ready)
+        outgoing.finish()
 
     @pl.when(jnp.logical_not(even))
     def _():
-        early_ahead(V, S, R, coef_ref, msg, W, then, window)
+        outgoing = Outgoing(msg, out, sems, 1)
+        early_ahead(V, S, R, coef_ref, msg, W, then, window, outgoing.ready)
+        outgoing.finish()
 
 
 def write_out(V, S, R, results, sems, cell):
@@ -470,8 +489,11 @@
     rest = list(rest)
     missing = rest.pop(0) if step > 0 else None
     V, S, R, D = rest[:4]
-    G, W = rest[-2:]
-    early = rest[4] if step < STEPS - 2 else None
+    more = step < STEPS - 2
+    if more:
+        out, G, W, early, sems = rest[4:]
+    else:
+        G, W = rest[4:]
     even, _, _ = place()
     zero_edges(W)
     here, then = force.at[step], force.at[step + 1]
@@ -479,7 +501,7 @@
     @pl.when(even)
     def _():
         behind_bond(
-            V, S, R, coef_ref, here, surface, msg, missing, G, step, window, 1,
+            V, S, R, coef_ref, here, surface, msg if step == 0 else msg.at[0], missing, G, step, window, 1,
             lambda: response_ahead(V, S, coef_ref, D, W),
         )
         pre_behind(V, S, coef_ref, None, then, window)
@@ -487,22 +509,28 @@
     @pl.when(jnp.logical_not(even))
     def _():
         ahead_bond(
-            V, S, R, coef_ref, here, surface, msg, missing, G, step, window, 1,
+            V, S, R, coef_ref, here, surface, msg if step == 0 else msg.at[1], missing, G, step, window, 1,
             lambda: response_behind(V, S, coef_ref, D, W),
         )
         pre_ahead(V, S, coef_ref, None, then, window)
 
     inner(V, S, coef_ref, then, window)
-    if early is not None:
+    if more:
         later = force.at[step + 2]
 
         @pl.when(even)
         def _():
-            early_behind(V, S, R, coef_ref, surface, 2 * (step + 1), early, W, later, window)
+            outgoing = Outgoing(early, out, sems, 0)
+            early_behind(
+                V, S, R, coef_ref, surface, 2 * (step + 1), early, W, later, window, outgoing.ready
+            )
+            outgoing.finish()
 
         @pl.when(jnp.logical_not(even))
         def _():
-            early_ahead(V, S, R, coef_ref, early, W, later, window)
+            outgoing = Outgoing(early, out, sems, 1)
+            early_ahead(V, S, R, coef_ref, early, W, later, window, outgoing.ready)
+            outgoing.finish()
 
 
 def last_kernel(step, window, V0, S0, R0, coef_ref, force, surface, msg, missing, v0, s0, r0, V, S, R, *rest):
@@ -512,12 +540,12 @@
 
     @pl.when(even)
     def _():
-        behind_bond(V, S, R, coef_ref, here, surface, msg, missing, G, step, window)
+        behind_bond(V, S, R, coef_ref, here, surface, msg.at[0], missing, G, step, window)
         write_out(V, S, R, results, sems, 0)
 
     @pl.when(jnp.logical_not(even))
     def _():
-        ahead_bond(V, S, R, coef_ref, here, surface, msg, missing, G, step, window)
+        ahead_bond(V, S, R, coef_ref, here, surface, msg.at[1], missing, G, step, window)
         write_out(V, S, R, results, sems, 1)
 
 
@@ -687,6 +715,15 @@
     def ahead_by(x, distance):
         return lax.ppermute(x, "line", [(i, i + distance) for i in range(tiles - distance)])
 
+    runs = lax.axis_size("runs")
+    couples = [[run * tiles + i, run * tiles + i + 1] for run in range(runs) for i in range(1, tiles - 1, 2)]
+    couples += [
+        [run * tiles + end, (run + 1) * tiles + end] for run in range(0, runs, 2) for end in (0, tiles - 1)
+    ]
+
+    def swapped(x):
+        return lax.all_to_all(x, ("runs", "line"), 0, 0, axis_index_groups=couples, tiled=True)
+
     def in_hbm(*arrays):
         return tuple(pltpu.with_memory_space_constraint(x, pltpu.HBM) for x in arrays)
 
@@ -748,17 +785,18 @@
         scratch=(pltpu.VMEM((depth, depth), f32), pltpu.VMEM((depth, across), f32)),
         name="prepare",
     )
+    chunks = jax.ShapeDtypeStruct((2, 3, across, depth), f32)
     V, early = call(
         functools.partial(first_kernel, window),
         tuple(in_vmem(x) for x in (V, S, R, coef, force, surface)),
         (WHOLE,) * 6,
-        (v_type, m_type),
-        (WHOLE,) * 2,
-        scratch=(work,),
+        (v_type, chunks),
+        (WHOLE, ANYWHERE),
+        scratch=(m_type, work, dma((3,))),
         aliases={0: 0},
         name="first",
     )
-    early = lax.ppermute(early, "line", far)
+    early = swapped(early)
     state = (v_type, s_type, r_type)
     results = tuple(jax.ShapeDtypeStruct(x.shape, f32) for x in (velocity, stress, memory))
     same = {0: 0, 1: 1, 2: 2}
@@ -782,20 +820,21 @@
         ins = (V, S, R, coef, force, surface, msg_far) + ((missing,) if step else ())
         ins = tuple(in_vmem(x) for x in ins)
         if more:
-            outs = state + (m_type,) + ((m_type,) if step < STEPS - 2 else ())
+            sends = step < STEPS - 2
+            outs = state + (m_type,) + ((chunks,) if sends else ())
             V, S, R, missing, *msg = call(
                 functools.partial(far_kernel, step, window),
                 ins,
                 (WHOLE,) * len(ins),
                 outs,
-                (WHOLE,) * len(outs),
-                scratch=(ghost, work),
+                (WHOLE,) * 4 + ((ANYWHERE,) if sends else ()),
+                scratch=(ghost, work) + ((m_type, dma((3,))) if sends else ()),
                 aliases=same,
                 name="far" + str(step),
             )
             msg_far = early
-            if msg:
-                early = lax.ppermute(msg[0], "line", far)
+            if sends:
+                early = swapped(msg[0])
     ends = call(
         functools.partial(last_kernel, STEPS - 1, window),
         ins + tuple(msg),

time: 52.5 us -> 76.4 us (1.46)
  blocking collectives: 0 us -> 11.1 us
  local copies, waits for them, and re-layouts: 0 us -> 8.44 us
  waiting for transfers between devices: 12.2 us -> 15 us
  Pallas kernels: 10.8 us -> 13.6 us
  starting transfers between devices: 28.1 us -> 26.6 us
    ppermute x5 -> x0, starting transfers between devices: 15.7 us -> none  [the longest x4 12.8 us: body(): early = lax.ppermute(msg[0], 'line', far)]
    all_to_all x0 -> x1, blocking collectives: none -> 11.1 us  [body(): lax.all_to_all(parts, 'line', 0, 0, axis_index_groups=groups, tiled=True)]
    all_to_all x1 -> x5, starting transfers between devices: 6.3 us -> 17.3 us  [swapped(): lax.all_to_all(x, ('runs', 'line'), 0, 0, axis_index_groups=couples, tile...]
    unnamed x0 -> x34, local copies, waits for them, and re-layouts: none -> 8.44 us
    ppermute x5 -> x0, waiting for transfers between devices: 8.01 us -> none  [the longest x4 6.25 us: body(): early = lax.ppermute(msg[0], 'line', far)]
    ppermute x1, waiting for transfers between devices: 0.01 us -> 5.74 us  [body(): msg_far = lax.ppermute(msg_far, 'line', far)]
    ppermute x5, waiting for transfers between devices: 0.01 us -> 4.21 us  [body(): msg_near = lax.ppermute(msg[0], 'line', near)]
    ppermute x5, starting transfers between devices: 1.22 us -> 4.13 us  [body(): msg_near = lax.ppermute(msg[0], 'line', near)]
  transfers between devices with their start and end apart: 14 -> 13, of which waited for: 7 -> 9; matrix products, arithmetic and copies ran while one was open for 0% -> 0% of each run, Pallas kernels for 15% -> 13%
where the time goes in v11:
time: 76.4 us; the launch traced here: 75.6 us
  starting transfers between devices  26.6 us (35%)
  waiting for transfers between devices  15 us (20%)
  Pallas kernels  13.6 us (18%)
  blocking collectives  11.1 us (15%)
  local copies, waits for them, and re-layouts  8.44 us (11%)
  between operations  0.9 us (1%)
    all_to_all x5, starting transfers between devices, swapped(): lax.all_to_all(x, ('runs', 'line'), 0, 0, axis_index_groups=couples, tile...  17.3 us
    pallas_call x17, Pallas kernels, call(): pl.pallas_call(kernel, out_shape=outs, in_specs=specs, out_specs=out_spec...  13.6 us
    all_to_all x1, blocking collectives, body(): lax.all_to_all(parts, 'line', 0, 0, axis_index_groups=groups, tiled=True)  11.1 us
    unnamed x34, local copies, waits for them, and re-layouts  8.44 us
    ppermute x1, waiting for transfers between devices, body(): msg_far = lax.ppermute(msg_far, 'line', far)  5.74 us
    ppermute x5, waiting for transfers between devices, body(): msg_near = lax.ppermute(msg[0], 'line', near)  4.21 us
    ppermute x5, starting transfers between devices, body(): msg_near = lax.ppermute(msg[0], 'line', near)  4.13 us
    ppermute x1, waiting for transfers between devices, ahead_by(): lax.ppermute(x, 'line', [(i, i + distance) for i in range(tiles - distanc...  2.85 us
  transfers between devices with their start and end apart: 13, of which 9 were waited for; matrix products, arithmetic and copies ran while one was open for 0% of the time, Pallas kernels for 13%

profile of v11, /device:TPU:17, one launch (start us, length us, event | category | flops | bytes accessed | tf_op | source)
XLA Modules:
  0.0 75.6 jit_solution(7473999607574851861)
XLA Ops:
  0.6 0.9 %pack.1 = (f32[8,1920]{1,0:T(8,128)S(1)}, f32[16,128]{1,0:T(8,128)S(1)}, f32[16,128]{1,0:T(8,128)S(1)}, s32[1,8]{1,0:T(1,128)S(1)}) custom-call(f32[8,1536]{1,0:T(8,128)} %bitcast.3, f32[16,128]{1,0:T(8,128)} %loads_in.1, s32[6,16]{1,0:T(8,128)} %entries_in.1, s32[6,16]{1,0:T(8,128)} %cells_in.1, s32[1,8]{1,0:T(1,128)} %bitcast.4), custom_call_target="tpu_custom_call" | custom-call | flops 1 | bytes 1 | tf_op jit(solution)/shard_map/pack/pallas_call | solution.py:679
  1.5 1.3 %collective-permute-start = (f32[8,1920]{1,0:T(8,128)S(1)}, f32[8,1920]{1,0:T(8,128)S(1)}, u32[]{:S(2)}, u32[]{:S(2)}) collective-permute-start(f32[8,1920]{1,0:T(8,128)S(1)} %get-tuple-element.75.own), channel_id=1, source_target_pairs={{0,8},{1,9},{2,10},{3,11},{4,12},{5,13},{6,14},{7,15},{16,24},{17,... | collective-permute-start | bytes 184328 | tf_op jit(solution)/shard_map/ppermute | solution.py:716
  2.8 1.8 %start.1 = (f32[3,2,144,128]{3,2,1,0:T(8,128)S(1)}, f32[6,2,144,128]{3,2,1,0:T(8,128)S(1)}, f32[6,2,128,128]{3,2,1,0:T(8,128)S(1)}, f32[16,128]{1,0:T(8,128)S(1)...) custom-call(f32[3,2,128,128]{3,2,1,0:T(8,128)} %velocity.1, f32[6,2,128,128]{3,2,1,0:T(8,128)} %stress.1, ...), custom_call_target="tpu_custom_call" | custom-call | flops 8388608 | bytes 8388608 | tf_op jit(solution)/shard_map/start/pallas_call | solution.py:679
  4.6 2.8 %collective-permute-done.behind = f32[8,1920]{1,0:T(8,128)S(1)} collective-permute-done((f32[8,1920]{1,0:T(8,128)S(1)}, f32[8,1920]{1,0:T(8,128)S(1)}, u32[]{:S(2)}, u32[]{:S(2)}) %collective-permute-start) | collective-permute-done | bytes 61472 | tf_op jit(solution)/shard_map/ppermute | solution.py:716
  7.6 11.1 %all_to_all.30.parts = f32[8,56,128]{2,1,0:T(8,128)S(1)} all-to-all(f32[8,56,128]{2,1,0:T(8,128)S(1)} %split.1), channel_id=1, replica_groups={{0,1,2,3,4,5,6,7},{8,9,10,11,12,13,14,15},{16,17,18,19,20,21,22,23},{24..., dimensions={0} | all-to-all | bytes 458752 | tf_op jit(solution)/shard_map/all_to_all | solution.py:778
  18.7 0.6 prepare.1
  19.3 1.0 %first.1 = (f32[3,2,144,128]{3,2,1,0:T(8,128)S(1)}, f32[2,3,128,128]{3,2,1,0:T(8,128)}) custom-call(f32[3,2,144,128]{3,2,1,0:T(8,128)S(1)} %get-tuple-element.71.V0, f32[6,2,144,128]{3,2,1,0:T(8,128)S(1)} %get-tuple-element.72.S.S0, f32[6,2,128,128]{3,2,1,0:T(8,128)S(1)} %get-tuple-element.73.R.R0, ...), custom_call_target="tpu_custom_call", output_to_operand_aliasing={{0}: (0, {})} | custom-call | flops 1 | bytes 1 | tf_op jit(solution)/shard_map/first/pallas_call | solution.py:679
  20.3 3.5 %all-to-all-start.1 = ((f32[2,3,128,128]{3,2,1,0:T(8,128)}), f32[2,3,128,128]{3,2,1,0:T(8,128)S(1)}, u32[]{:S(2)}, u32[]{:S(2)}) async-start(f32[2,3,128,128]{3,2,1,0:T(8,128)} %get-tuple-element.93), calls=%async_computation.1 | async-start | bytes 786432 | tf_op jit(solution)/shard_map/all_to_all | solution.py:725
  23.8 1.3 %collective-permute-start.1 = (f32[3,128,128]{2,1,0:T(8,128)S(1)}, f32[3,128,128]{2,1,0:T(8,128)S(1)}, u32[]{:S(2)}, u32[]{:S(2)}) collective-permute-start(f32[3,128,128]{2,1,0:T(8,128)S(1)} %get-tuple-element.81), channel_id=1, source_target_pairs={{0,1},{1,0},{2,3},{3,2},{4,5},{5,4},{6,7},{7,6},{8,9},{9,8},{10,11... | collective-permute-start | bytes 589832 | tf_op jit(solution)/shard_map/ppermute | solution.py:768
  25.1 2.5 %collective-permute-start.2 = (f32[3,128,128]{2,1,0:T(8,128)S(1)}, f32[3,128,128]{2,1,0:T(8,128)S(1)}, u32[]{:S(2)}, u32[]{:S(2)}) collective-permute-start(f32[3,128,128]{2,1,0:T(8,128)S(1)} %get-tuple-element.85), channel_id=1, source_target_pairs={{1,2},{3,4},{5,6},{7,8},{9,10},{11,12},{13,14},{2,1},{4,3},{6,5},{... | collective-permute-start | bytes 589832 | tf_op jit(solution)/shard_map/ppermute | solution.py:767
  27.6 0.3 near0.1
  27.9 0.7 copy-done.14
  28.5 5.7 %collective-permute-done.2.msg = f32[3,128,128]{2,1,0:T(8,128)S(1)} collective-permute-done((f32[3,128,128]{2,1,0:T(8,128)S(1)}, f32[3,128,128]{2,1,0:T(8,128)S(1)}, u32[]{:S(2)}, u32[]{:S(2)}) %collective-permute-start.2) | collective-permute-done | bytes 196640 | tf_op jit(solution)/shard_map/ppermute | solution.py:767
  34.3 0.9 %far0.1 = (f32[3,2,144,128]{3,2,1,0:T(8,128)S(1)}, f32[6,2,144,128]{3,2,1,0:T(8,128)S(1)}, f32[6,2,128,128]{3,2,1,0:T(8,128)S(1)}, f32[3,128,128]{2,1,0:T(8,128)S(1)}, f32[2,3,128,128]{3,2,1,0:T(8,128)S(1)}) custom-call(f32[3,2,144,128]{3,2,1,0:T(8,128)S(1)} %get-tuple-element.82.V0, ...), custom_call_target="tpu_custom_call", output_to_operand_aliasing={{0}: (0, {}), {1}: (1, {}), {2}: (2, {})} | custom-call | flops 1 | bytes 1 | tf_op jit(solution)/shard_map/far0/pallas_call | solution.py:679
  35.2 0.7 copy-done.3
  35.9 0.7 copy-done.10
  36.6 3.5 %all-to-all-start.2 = ((f32[2,3,128,128]{3,2,1,0:T(8,128)}), f32[2,3,128,128]{3,2,1,0:T(8,128)S(1)}, u32[]{:S(2)}, u32[]{:S(2)}) async-start(f32[2,3,128,128]{3,2,1,0:T(8,128)} %copy-done.3), calls=%async_computation.2 | async-start | bytes 786432 | tf_op jit(solution)/shard_map/all_to_all | solution.py:725
  40.2 1.6 %collective-permute-done.3.msg = f32[3,128,128]{2,1,0:T(8,128)S(1)} collective-permute-done((f32[3,128,128]{2,1,0:T(8,128)}, f32[3,128,128]{2,1,0:T(8,128)S(1)}, u32[]{:S(2)}, u32[]{:S(2)}) %collective-permute-start.3) | collective-permute-done | bytes 196640 | tf_op jit(solution)/shard_map/ppermute | solution.py:819
  41.8 0.3 near1.1
  42.1 0.7 copy-done.15
  42.8 0.9 %far1.1 = (f32[3,2,144,128]{3,2,1,0:T(8,128)S(1)}, f32[6,2,144,128]{3,2,1,0:T(8,128)S(1)}, f32[6,2,128,128]{3,2,1,0:T(8,128)S(1)}, f32[3,128,128]{2,1,0:T(8,128)S(1)}, f32[2,3,128,128]{3,2,1,0:T(8,128)S(1)}) custom-call(f32[3,2,144,128]{3,2,1,0:T(8,128)S(1)} %get-tuple-element.90.V0, ...), custom_call_target="tpu_custom_call", output_to_operand_aliasing={{0}: (0, {}), {1}: (1, {}), {2}: (2, {})} | custom-call | flops 1 | bytes 1 | tf_op jit(solution)/shard_map/far1/pallas_call | solution.py:679
  43.7 0.7 copy-done.2
  44.4 0.7 copy-done.8
  45.4 3.5 %all-to-all-start.3 = ((f32[2,3,128,128]{3,2,1,0:T(8,128)}), f32[2,3,128,128]{3,2,1,0:T(8,128)S(1)}, u32[]{:S(2)}, u32[]{:S(2)}) async-start(f32[2,3,128,128]{3,2,1,0:T(8,128)} %copy-done.2), calls=%async_computation.3 | async-start | bytes 786432 | tf_op jit(solution)/shard_map/all_to_all | solution.py:725
  48.9 1.3 %collective-permute-start.4 = (f32[3,128,128]{2,1,0:T(8,128)}, f32[3,128,128]{2,1,0:T(8,128)S(1)}, u32[]{:S(2)}, u32[]{:S(2)}) collective-permute-start(f32[3,128,128]{2,1,0:T(8,128)} %copy-done.15), channel_id=1, source_target_pairs={{0,1},{1,0},{2,3},{3,2},{4,5},{5,4},{6,7},{7,6},{8,9},{9,8},{10,11... | collective-permute-start | bytes 589832 | tf_op jit(solution)/shard_map/ppermute | solution.py:819
  50.2 1.3 %collective-permute-done.4.msg = f32[3,128,128]{2,1,0:T(8,128)S(1)} collective-permute-done((f32[3,128,128]{2,1,0:T(8,128)}, f32[3,128,128]{2,1,0:T(8,128)S(1)}, u32[]{:S(2)}, u32[]{:S(2)}) %collective-permute-start.4) | collective-permute-done | bytes 196640 | tf_op jit(solution)/shard_map/ppermute | solution.py:819
  51.5 0.3 near2.1
  51.8 0.7 copy-done.16
  52.4 0.9 %far2.1 = (f32[3,2,144,128]{3,2,1,0:T(8,128)S(1)}, f32[6,2,144,128]{3,2,1,0:T(8,128)S(1)}, f32[6,2,128,128]{3,2,1,0:T(8,128)S(1)}, f32[3,128,128]{2,1,0:T(8,128)S(1)}, f32[2,3,128,128]{3,2,1,0:T(8,128)S(1)}) custom-call(f32[3,2,144,128]{3,2,1,0:T(8,128)S(1)} %get-tuple-element.99.V0, ...), custom_call_target="tpu_custom_call", output_to_operand_aliasing={{0}: (0, {}), {1}: (1, {}), {2}: (2, {})} | custom-call | flops 1 | bytes 1 | tf_op jit(solution)/shard_map/far2/pallas_call | solution.py:679
  53.4 0.7 copy-done.1
  54.1 0.7 copy-done.6
  54.8 0.4 all-to-all-done.3.msg
  55.2 3.5 %all-to-all-start.4 = ((f32[2,3,128,128]{3,2,1,0:T(8,128)}), f32[2,3,128,128]{3,2,1,0:T(8,128)S(1)}, u32[]{:S(2)}, u32[]{:S(2)}) async-start(f32[2,3,128,128]{3,2,1,0:T(8,128)} %copy-done.1), calls=%async_computation.4 | async-start | bytes 786432 | tf_op jit(solution)/shard_map/all_to_all | solution.py:725
  58.7 1.2 %collective-permute-start.5 = (f32[3,128,128]{2,1,0:T(8,128)}, f32[3,128,128]{2,1,0:T(8,128)S(1)}, u32[]{:S(2)}, u32[]{:S(2)}) collective-permute-start(f32[3,128,128]{2,1,0:T(8,128)} %copy-done.16), channel_id=1, source_target_pairs={{0,1},{1,0},{2,3},{3,2},{4,5},{5,4},{6,7},{7,6},{8,9},{9,8},{10,11... | collective-permute-start | bytes 589832 | tf_op jit(solution)/shard_map/ppermute | solution.py:819
  59.9 1.3 %collective-permute-done.5.msg = f32[3,128,128]{2,1,0:T(8,128)S(1)} collective-permute-done((f32[3,128,128]{2,1,0:T(8,128)}, f32[3,128,128]{2,1,0:T(8,128)S(1)}, u32[]{:S(2)}, u32[]{:S(2)}) %collective-permute-start.5) | collective-permute-done | bytes 196640 | tf_op jit(solution)/shard_map/ppermute | solution.py:819
  61.1 0.9 %near3.1 = (f32[3,2,144,128]{3,2,1,0:T(8,128)S(1)}, f32[6,2,144,128]{3,2,1,0:T(8,128)S(1)}, f32[6,2,128,128]{3,2,1,0:T(8,128)S(1)}, f32[3,128,128]{2,1,0:T(8,128)}) custom-call(f32[3,2,144,128]{3,2,1,0:T(8,128)S(1)} %get-tuple-element.104.V0, ...), custom_call_target="tpu_custom_call", output_to_operand_aliasing={{0}: (0, {}), {1}: (1, {}), {2}: (2, {})} | custom-call | flops 1 | bytes 1 | tf_op jit(solution)/shard_map/near3/pallas_call | solution.py:679
  62.1 0.3 collective-permute-start.6
  62.4 0.9 %far3.1 = (f32[3,2,144,128]{3,2,1,0:T(8,128)S(1)}, f32[6,2,144,128]{3,2,1,0:T(8,128)S(1)}, f32[6,2,128,128]{3,2,1,0:T(8,128)S(1)}, f32[3,128,128]{2,1,0:T(8,128)S(1)}, f32[2,3,128,128]{3,2,1,0:T(8,128)S(1)}) custom-call(f32[3,2,144,128]{3,2,1,0:T(8,128)S(1)} %get-tuple-element.108.V0, ...), custom_call_target="tpu_custom_call", output_to_operand_aliasing={{0}: (0, {}), {1}: (1, {}), {2}: (2, {})} | custom-call | flops 1 | bytes 1 | tf_op jit(solution)/shard_map/far3/pallas_call | solution.py:679
  63.3 0.7 copy-done
  64.1 0.7 copy-done.12
  64.8 3.5 %all-to-all-start.5 = ((f32[2,3,128,128]{3,2,1,0:T(8,128)}), f32[2,3,128,128]{3,2,1,0:T(8,128)S(1)}, u32[]{:S(2)}, u32[]{:S(2)}) async-start(f32[2,3,128,128]{3,2,1,0:T(8,128)} %copy-done), calls=%async_computation.5 | async-start | bytes 786432 | tf_op jit(solution)/shard_map/all_to_all | solution.py:725
  68.3 1.2 %near4.1 = (f32[3,2,144,128]{3,2,1,0:T(8,128)S(1)}, f32[6,2,144,128]{3,2,1,0:T(8,128)S(1)}, f32[6,2,128,128]{3,2,1,0:T(8,128)S(1)}, f32[3,128,128]{2,1,0:T(8,128)S(1)}) custom-call(f32[3,2,144,128]{3,2,1,0:T(8,128)S(1)} %get-tuple-element.113.V0, ...), custom_call_target="tpu_custom_call", output_to_operand_aliasing={{0}: (0, {}), {1}: (1, {}), {2}: (2, {})} | custom-call | flops 1 | bytes 1 | tf_op jit(solution)/shard_map/near4/pallas_call | solution.py:679
  69.6 1.2 %collective-permute-start.7 = (f32[3,128,128]{2,1,0:T(8,128)S(1)}, f32[3,128,128]{2,1,0:T(8,128)S(1)}, u32[]{:S(2)}, u32[]{:S(2)}) collective-permute-start(f32[3,128,128]{2,1,0:T(8,128)S(1)} %get-tuple-element.125), channel_id=1, source_target_pairs={{0,1},{1,0},{2,3},{3,2},{4,5},{5,4},{6,7},{7,6},{8,9},{9,8},{10,11... | collective-permute-start | bytes 589832 | tf_op jit(solution)/shard_map/ppermute | solution.py:819
  70.8 0.5 far4.1
  71.2 0.7 copy-done.4
  71.9 1.1 %near5.1 = (f32[3,2,144,128]{3,2,1,0:T(8,128)S(1)}, f32[6,2,144,128]{3,2,1,0:T(8,128)S(1)}, f32[6,2,128,128]{3,2,1,0:T(8,128)S(1)}, f32[3,2,128,128]{3,2,1,0:T(8...) custom-call(f32[3,2,144,128]{3,2,1,0:T(8,128)S(1)} %get-tuple-elemen, ...), custom_call_target="tpu_custom_call", output_to_operand_aliasing={{0}: (0, {}), {1}: (1, {}), {2}: (2, {})} | custom-call | flops 1 | bytes 1 | tf_op jit(solution)/shard_map/near5/pallas_call | solution.py:679
  73.0 1.5 %all-to-all-done.5.msg = f32[2,3,128,128]{3,2,1,0:T(8,128)S(1)} async-done(((f32[2,3,128,128]{3,2,1,0:T(8,128)}), f32[2,3,128,128]{3,2,1,0:T(8,128)S(1)}, u32[]{:S(2)}, u32[]{:S(2)}) %all-to-all-start.5) | async-done | bytes 393248 | tf_op jit(solution)/shard_map/all_to_all | solution.py:725
  74.5 1.1 %last.1 = (f32[3,2,144,128]{3,2,1,0:T(8,128)S(1)}, f32[6,2,144,128]{3,2,1,0:T(8,128)S(1)}, f32[6,2,128,128]{3,2,1,0:T(8,128)S(1)}, f32[3,2,128,128]{3,2,1,0:T(8,...) custom-call(f32[3,2,144,128]{3,2,1,0:T(8,128)S(1)} %get-tuple-elemen, ...), custom_call_target="tpu_custom_call", output_to_operand_aliasing={{0}: (0, {}), {1}: (1, {}), {2}: (2, {}), {3}: (8, {}), {4}... | custom-call | flops 1 | bytes 1 | tf_op jit(solution)/shard_map/last/pallas_call | solution.py:679
  (30 shorter events, 0.7 us)
Async XLA Ops:
  1.5 5.9 %collective-permute-start = (f32[8,1920]{1,0:T(8,128)S(1)}, f32[8,1920]{1,0:T(8,128)S(1)}, u32[]{:S(2)}, u32[]{:S(2)}) collective-permute-start(f32[8,1920]{1,0:T(8,128)S(1)} %get-tuple-element.75.own), channel_id=1, source_target_pairs={{0,8},{1,9},{2,10},{3,11},{4,12},{5,13},{6,14},{7,15},{16,24},{17,... | collective-permute-start | bytes 184328 | tf_op jit(solution)/shard_map/ppermute | solution.py:716
  20.3 16.4 %all-to-all-start.1 = ((f32[2,3,128,128]{3,2,1,0:T(8,128)}), f32[2,3,128,128]{3,2,1,0:T(8,128)S(1)}, u32[]{:S(2)}, u32[]{:S(2)}) async-start(f32[2,3,128,128]{3,2,1,0:T(8,128)} %get-tuple-element.93), calls=%async_computation.1 | async-start | bytes 786432 | tf_op jit(solution)/shard_map/all_to_all | solution.py:725
  23.8 3.8 %collective-permute-start.1 = (f32[3,128,128]{2,1,0:T(8,128)S(1)}, f32[3,128,128]{2,1,0:T(8,128)S(1)}, u32[]{:S(2)}, u32[]{:S(2)}) collective-permute-start(f32[3,128,128]{2,1,0:T(8,128)S(1)} %get-tuple-element.81), channel_id=1, source_target_pairs={{0,1},{1,0},{2,3},{3,2},{4,5},{5,4},{6,7},{7,6},{8,9},{9,8},{10,11... | collective-permute-start | bytes 589832 | tf_op jit(solution)/shard_map/ppermute | solution.py:768
  25.1 9.2 %collective-permute-start.2 = (f32[3,128,128]{2,1,0:T(8,128)S(1)}, f32[3,128,128]{2,1,0:T(8,128)S(1)}, u32[]{:S(2)}, u32[]{:S(2)}) collective-permute-start(f32[3,128,128]{2,1,0:T(8,128)S(1)} %get-tuple-element.85), channel_id=1, source_target_pairs={{1,2},{3,4},{5,6},{7,8},{9,10},{11,12},{13,14},{2,1},{4,3},{6,5},{... | collective-permute-start | bytes 589832 | tf_op jit(solution)/shard_map/ppermute | solution.py:767
  27.9 0.7 copy-start.14
  35.2 0.7 copy-start.3
  35.9 0.7 copy-start.10
  36.6 8.8 %all-to-all-start.2 = ((f32[2,3,128,128]{3,2,1,0:T(8,128)}), f32[2,3,128,128]{3,2,1,0:T(8,128)S(1)}, u32[]{:S(2)}, u32[]{:S(2)}) async-start(f32[2,3,128,128]{3,2,1,0:T(8,128)} %copy-done.3), calls=%async_computation.2 | async-start | bytes 786432 | tf_op jit(solution)/shard_map/all_to_all | solution.py:725
  40.1 1.7 %collective-permute-start.3 = (f32[3,128,128]{2,1,0:T(8,128)}, f32[3,128,128]{2,1,0:T(8,128)S(1)}, u32[]{:S(2)}, u32[]{:S(2)}) collective-permute-start(f32[3,128,128]{2,1,0:T(8,128)} %copy-done.14), channel_id=1, source_target_pairs={{0,1},{1,0},{2,3},{3,2},{4,5},{5,4},{6,7},{7,6},{8,9},{9,8},{10,11... | collective-permute-start | bytes 589832 | tf_op jit(solution)/shard_map/ppermute | solution.py:819
  41.8 0.9 %copy-start.11 = (f32[3,128,128]{2,1,0:T(8,128)S(1)}, f32[3,128,128]{2,1,0:T(8,128)}, u32[]{:S(2)}) copy-start(f32[3,128,128]{2,1,0:T(8,128)} %copy-done.10) | copy-start | bytes 589828
  42.1 0.7 copy-start.15
  43.7 0.7 copy-start.2
  44.4 0.7 copy-start.8
  45.4 9.8 %all-to-all-start.3 = ((f32[2,3,128,128]{3,2,1,0:T(8,128)}), f32[2,3,128,128]{3,2,1,0:T(8,128)S(1)}, u32[]{:S(2)}, u32[]{:S(2)}) async-start(f32[2,3,128,128]{3,2,1,0:T(8,128)} %copy-done.2), calls=%async_computation.3 | async-start | bytes 786432 | tf_op jit(solution)/shard_map/all_to_all | solution.py:725
  48.9 2.6 %collective-permute-start.4 = (f32[3,128,128]{2,1,0:T(8,128)}, f32[3,128,128]{2,1,0:T(8,128)S(1)}, u32[]{:S(2)}, u32[]{:S(2)}) collective-permute-start(f32[3,128,128]{2,1,0:T(8,128)} %copy-done.15), channel_id=1, source_target_pairs={{0,1},{1,0},{2,3},{3,2},{4,5},{5,4},{6,7},{7,6},{8,9},{9,8},{10,11... | collective-permute-start | bytes 589832 | tf_op jit(solution)/shard_map/ppermute | solution.py:819
  51.5 0.9 %copy-start.9 = (f32[3,128,128]{2,1,0:T(8,128)S(1)}, f32[3,128,128]{2,1,0:T(8,128)}, u32[]{:S(2)}) copy-start(f32[3,128,128]{2,1,0:T(8,128)} %copy-done.8) | copy-start | bytes 589828
  51.7 0.7 copy-start.16
  53.3 0.7 copy-start.1
  54.1 0.7 copy-start.6
  55.2 9.7 %all-to-all-start.4 = ((f32[2,3,128,128]{3,2,1,0:T(8,128)}), f32[2,3,128,128]{3,2,1,0:T(8,128)S(1)}, u32[]{:S(2)}, u32[]{:S(2)}) async-start(f32[2,3,128,128]{3,2,1,0:T(8,128)} %copy-done.1), calls=%async_computation.4 | async-start | bytes 786432 | tf_op jit(solution)/shard_map/all_to_all | solution.py:725
  58.7 2.5 %collective-permute-start.5 = (f32[3,128,128]{2,1,0:T(8,128)}, f32[3,128,128]{2,1,0:T(8,128)S(1)}, u32[]{:S(2)}, u32[]{:S(2)}) collective-permute-start(f32[3,128,128]{2,1,0:T(8,128)} %copy-done.16), channel_id=1, source_target_pairs={{0,1},{1,0},{2,3},{3,2},{4,5},{5,4},{6,7},{7,6},{8,9},{9,8},{10,11... | collective-permute-start | bytes 589832 | tf_op jit(solution)/shard_map/ppermute | solution.py:819
  61.1 1.3 %copy-start.7 = (f32[3,128,128]{2,1,0:T(8,128)S(1)}, f32[3,128,128]{2,1,0:T(8,128)}, u32[]{:S(2)}) copy-start(f32[3,128,128]{2,1,0:T(8,128)} %copy-done.6) | copy-start | bytes 589828
  62.1 6.2 %collective-permute-start.6 = (f32[3,128,128]{2,1,0:T(8,128)}, f32[3,128,128]{2,1,0:T(8,128)}, u32[]{:S(2)}, u32[]{:S(2)}) collective-permute-start(f32[3,128,128]{2,1,0:T(8,128)} %get-tuple-element.116), channel_id=1, source_target_pairs={{0,1},{1,0},{2,3},{3,2},{4,5},{5,4},{6,7},{7,6},{8,9},{9,8},{10,11... | collective-permute-start | bytes 589832 | tf_op jit(solution)/shard_map/ppermute | solution.py:819
  63.3 0.7 copy-start
  64.1 0.7 copy-start.12
  64.8 9.7 %all-to-all-start.5 = ((f32[2,3,128,128]{3,2,1,0:T(8,128)}), f32[2,3,128,128]{3,2,1,0:T(8,128)S(1)}, u32[]{:S(2)}, u32[]{:S(2)}) async-start(f32[2,3,128,128]{3,2,1,0:T(8,128)} %copy-done), calls=%async_computation.5 | async-start | bytes 786432 | tf_op jit(solution)/shard_map/all_to_all | solution.py:725
  68.3 2.5 %copy-start.13 = (f32[3,128,128]{2,1,0:T(8,128)S(1)}, f32[3,128,128]{2,1,0:T(8,128)}, u32[]{:S(2)}) copy-start(f32[3,128,128]{2,1,0:T(8,128)} %copy-done.12) | copy-start | bytes 589828
  69.6 2.4 %collective-permute-start.7 = (f32[3,128,128]{2,1,0:T(8,128)S(1)}, f32[3,128,128]{2,1,0:T(8,128)S(1)}, u32[]{:S(2)}, u32[]{:S(2)}) collective-permute-start(f32[3,128,128]{2,1,0:T(8,128)S(1)} %get-tuple-element.125), channel_id=1, source_target_pairs={{0,1},{1,0},{2,3},{3,2},{4,5},{5,4},{6,7},{7,6},{8,9},{9,8},{10,11... | collective-permute-start | bytes 589832 | tf_op jit(solution)/shard_map/ppermute | solution.py:819
  71.2 0.7 copy-start.4
  71.9 2.6 %copy-start.5 = (f32[3,128,128]{2,1,0:T(8,128)S(1)}, f32[3,128,128]{2,1,0:T(8,128)}, u32[]{:S(2)}) copy-start(f32[3,128,128]{2,1,0:T(8,128)} %copy-done.4) | copy-start | bytes 589828

commit v12 on v10

--- a/solution.py
+++ b/solution.py
@@ -63,6 +63,17 @@
     for where in np.ndindex(*ref.shape[:-2]):
         ref[(*where, pl.ds(0, PAD))] = edge
         ref[(*where, pl.ds(PAD + across, PAD))] = edge
+
+
+class Parts:
+    def __init__(self, refs):
+        self.refs = refs
+
+    def __getitem__(self, at):
+        return self.refs[at[0]][at[1]]
+
+    def __setitem__(self, at, value):
+        self.refs[at[0]][at[1]] = value
 
 
 def add_force(ref, index, force, which, first_row):
@@ -347,9 +358,10 @@
 
 def start_kernel(
     velocity, stress, memory, layer_in, lam_in, mu_in, buoy_in, rate_in, defect_in, after_this,
-    V, S, R, coef_ref, msg_near, msg_far, layer_ref, lam, mu, buoy, rate, defect, sems,
+    V, S, R, coef_ref, near_x, near_y, near_z, msg_far, layer_ref, lam, mu, buoy, rate, defect, sems,
 ):
     del after_this
+    msg_near = Parts((near_x, near_y, near_z))
     across = velocity.shape[2]
     inside = pl.ds(PAD, across)
     pairs = [
@@ -432,20 +444,28 @@
         early_ahead(V, S, R, coef_ref, msg, W, then, window)
 
 
-def write_out(V, S, R, results, sems, cell):
+def results_out(V, S, R, results, sems, cell):
     inside = pl.ds(PAD, R.shape[2])
-    pairs = [(V.at[:, cell, inside], results[0]), (S.at[:, cell, inside], results[1]), (R.at[:, cell], results[2])]
-    copies = [
-        pltpu.make_async_copy(source, result.at[:, cell], sems.at[i]) for i, (source, result) in enumerate(pairs)
-    ]
+    pairs = [(V.at[i, cell, inside], results[0].at[i, cell]) for i in range(3)]
+    pairs += [(S.at[i, cell, inside], results[1].at[i, cell]) for i in range(6)]
+    pairs += [(R.at[i, cell], results[2].at[i, cell]) for i in range(6)]
+    return [pltpu.make_async_copy(*pair, sems.at[i]) for i, pair in enumerate(pairs)]
+
+
+def start_all(copies):
     for copy in copies:
         copy.start()
+
+
+def wait_all(copies):
     for copy in copies:
         copy.wait()
 
 
-def near_kernel(step, window, V0, S0, R0, coef_ref, force, surface, msg, V, S, R, *rest):
+def near_kernel(step, window, V0, S0, R0, coef_ref, force, surface, msg_x, msg_y, msg_z, V, S, R, *rest):
     G = rest[-1]
+    msg = Parts((msg_x, msg_y, msg_z))
+    send = Parts(rest[:3])
     even, _, _ = place()
     more = step < STEPS - 1
 
@@ -453,17 +473,21 @@
     def _():
         ahead_bond(V, S, R, coef_ref, force.at[step], surface, msg, None, G, step, window, 1)
         if more:
-            pre_ahead(V, S, coef_ref, rest[0], force.at[step + 1], window)
+            pre_ahead(V, S, coef_ref, send, force.at[step + 1], window)
         else:
-            write_out(V, S, R, rest[:3], rest[-2], 1)
+            copies = results_out(V, S, R, rest[:3], rest[-2], 1)
+            start_all(copies)
+            wait_all(copies)
 
     @pl.when(jnp.logical_not(even))
     def _():
         behind_bond(V, S, R, coef_ref, force.at[step], surface, msg, None, G, step, window, 1)
         if more:
-            pre_behind(V, S, coef_ref, rest[0], force.at[step + 1], window)
+            pre_behind(V, S, coef_ref, send, force.at[step + 1], window)
         else:
-            write_out(V, S, R, rest[:3], rest[-2], 0)
+            copies = results_out(V, S, R, rest[:3], rest[-2], 0)
+            start_all(copies)
+            wait_all(copies)
 
 
 def far_kernel(step, window, V0, S0, R0, coef_ref, force, surface, msg, *rest):
@@ -512,13 +536,21 @@
 
     @pl.when(even)
     def _():
-        behind_bond(V, S, R, coef_ref, here, surface, msg, missing, G, step, window)
-        write_out(V, S, R, results, sems, 0)
+        copies = results_out(V, S, R, results, sems, 0)
+        behind_bond(
+            V, S, R, coef_ref, here, surface, msg, missing, G, step, window, 0, lambda: start_all(copies[:3])
+        )
+        start_all(copies[3:])
+        wait_all(copies)
 
     @pl.when(jnp.logical_not(even))
     def _():
-        ahead_bond(V, S, R, coef_ref, here, surface, msg, missing, G, step, window)
-        write_out(V, S, R, results, sems, 1)
+        copies = results_out(V, S, R, results, sems, 1)
+        ahead_bond(
+            V, S, R, coef_ref, here, surface, msg, missing, G, step, window, 0, lambda: start_all(copies[:3])
+        )
+        start_all(copies[3:])
+        wait_all(copies)
 
 
 ENTRY_ROW, TRUCK_ROW = 36, 40
@@ -681,6 +713,7 @@
     r_type = pltpu.VMEM((6, width_x, across, depth), f32)
     c_type = pltpu.VMEM((N_COEF, depth), f32)
     m_type = pltpu.VMEM((3, across, depth), f32)
+    planes = (pltpu.VMEM((across, depth), f32),) * 3
     ghost = pltpu.VMEM((2, across, depth), f32)
     work = pltpu.VMEM((2, padded, depth), f32)
 
@@ -715,12 +748,12 @@
         behind = jnp.concatenate([record, behind[:, panel:]], axis=1)
         reach *= 2
     tables = (lame_lambda, lame_mu, buoyancy, relax_rate, defect_mu)
-    V, S, R, coef, msg_near, msg_far = call(
+    V, S, R, coef, *msg_near, msg_far = call(
         start_kernel,
         in_hbm(velocity, stress, memory, layer[None, :], *tables) + (steps_table,),
         (ANYWHERE,) * 10,
-        (v_type, s_type, r_type, c_type, m_type, m_type),
-        (WHOLE,) * 6,
+        (v_type, s_type, r_type, c_type, *planes, m_type),
+        (WHOLE,) * 8,
         scratch=(
             pltpu.VMEM((1, depth), jnp.int32), *(pltpu.SMEM(table.shape, f32) for table in tables), dma((21,)),
         ),
@@ -728,12 +761,12 @@
         cost=8 * 1024 * 1024,
     )
     msg_far = lax.ppermute(msg_far, "line", far)
-    msg_near = lax.ppermute(msg_near, "line", near)
+    msg_near = [lax.ppermute(plane, "line", near) for plane in msg_near]
     parts = call(
         functools.partial(split_kernel, panel, slots),
         (own, behind, in_vmem(pier_row), coef),
         (WHOLE,) * 3 + (ANYWHERE,),
-        jax.ShapeDtypeStruct((GROUP, TRUCK_ROW + slots, depth), f32),
+        pltpu.VMEM((GROUP, TRUCK_ROW + slots, depth), f32),
         WHOLE,
         name="split",
     )
@@ -765,20 +798,20 @@
     missing = None
     for step in range(STEPS):
         more = step < STEPS - 1
-        ins = tuple(in_vmem(x) for x in (V, S, R, coef, force, surface, msg_near))
-        outs = state + ((m_type,) if more else results)
+        ins = tuple(in_vmem(x) for x in (V, S, R, coef, force, surface, *msg_near))
+        outs = state + (planes if more else results)
         V, S, R, *msg = call(
             functools.partial(near_kernel, step, window),
             ins,
             (WHOLE,) * len(ins),
             outs,
-            (WHOLE,) * 4 if more else (WHOLE,) * 3 + (ANYWHERE,) * 3,
-            scratch=(ghost,) if more else (dma((3,)), ghost),
+            (WHOLE,) * 6 if more else (WHOLE,) * 3 + (ANYWHERE,) * 3,
+            scratch=(ghost,) if more else (dma((15,)), ghost),
             aliases=same,
             name="near" + str(step),
         )
         if more:
-            msg_near = lax.ppermute(msg[0], "line", near)
+            msg_near = [lax.ppermute(plane, "line", near) for plane in msg]
         ins = (V, S, R, coef, force, surface, msg_far) + ((missing,) if step else ())
         ins = tuple(in_vmem(x) for x in ins)
         if more:
@@ -802,7 +835,7 @@
         (WHOLE,) * 8 + (ANYWHERE,) * 3,
         state + results,
         (WHOLE,) * 3 + (ANYWHERE,) * 3,
-        scratch=(ghost, dma((3,))),
+        scratch=(ghost, dma((15,))),
         aliases={**same, 8: 3, 9: 4, 10: 5},
         name="last",
     )

time: 52.5 us -> 53.7 us (1.023)
  starting transfers between devices: 28.1 us -> 32.7 us
  waiting for transfers between devices: 12.2 us -> 8.64 us
    ppermute x6 -> x18, starting transfers between devices: 1.23 us -> 6.73 us  [the longest x15 6.09 us: body(): msg_near = [lax.ppermute(plane, 'line', near) for plane in msg]]
    ppermute x4, waiting for transfers between devices: 6.25 us -> 0.86 us  [body(): early = lax.ppermute(msg[0], 'line', far)]
    ppermute x6 -> x18, waiting for transfers between devices: 0.02 us -> 3.47 us  [the longest x15 2.3 us: body(): msg_near = [lax.ppermute(plane, 'line', near) for plane in msg]]
    ppermute x1, waiting for transfers between devices: 1.76 us -> 0.01 us  [body(): early = lax.ppermute(early, 'line', far)]
    ppermute x4, starting transfers between devices: 12.8 us -> 11.1 us  [body(): early = lax.ppermute(msg[0], 'line', far)]
    ppermute x1, starting transfers between devices: 2.85 us -> 3.74 us  [body(): early = lax.ppermute(early, 'line', far)]
  transfers between devices with their start and end apart: 14 -> 26, of which waited for: 7 -> 14; matrix products, arithmetic and copies ran while one was open for 0% -> 0% of each run, Pallas kernels for 15% -> 15%
where the time goes in v12:
time: 53.7 us; the launch traced here: 53.2 us
  starting transfers between devices  32.7 us (61%)
  Pallas kernels  11 us (20%)
  waiting for transfers between devices  8.64 us (16%)
  between operations  0.88 us (2%)
    ppermute x4, starting transfers between devices, body(): early = lax.ppermute(msg[0], 'line', far)  11.1 us
    pallas_call x17, Pallas kernels, call(): pl.pallas_call(kernel, out_shape=outs, in_specs=specs, out_specs=out_spec...  11 us
    all_to_all x1, starting transfers between devices, body(): lax.all_to_all(parts, 'line', 0, 0, axis_index_groups=groups, tiled=True)  6.3 us
    ppermute x15, starting transfers between devices, body(): msg_near = [lax.ppermute(plane, 'line', near) for plane in msg]  6.09 us
    ppermute x1, starting transfers between devices, body(): early = lax.ppermute(early, 'line', far)  3.74 us
    ppermute x1, starting transfers between devices, body(): msg_far = lax.ppermute(msg_far, 'line', far)  3.53 us
    ppermute x1, waiting for transfers between devices, ahead_by(): lax.ppermute(x, 'line', [(i, i + distance) for i in range(tiles - distanc...  2.85 us
    ppermute x15, waiting for transfers between devices, body(): msg_near = [lax.ppermute(plane, 'line', near) for plane in msg]  2.3 us
  transfers between devices with their start and end apart: 26, of which 14 were waited for; matrix products, arithmetic and copies ran while one was open for 0% of the time, Pallas kernels for 15%

profile of v12, /device:TPU:17, one launch (start us, length us, event | category | flops | bytes accessed | tf_op | source)
XLA Modules:
  0.0 53.2 jit_solution(15250869324962755204)
XLA Ops:
  0.6 0.9 %pack.1 = (f32[8,1920]{1,0:T(8,128)S(1)}, f32[16,128]{1,0:T(8,128)S(1)}, f32[16,128]{1,0:T(8,128)S(1)}, s32[1,8]{1,0:T(1,128)S(1)}) custom-call(f32[8,1536]{1,0:T(8,128)} %bitcast.3, f32[16,128]{1,0:T(8,128)} %loads_in.1, s32[6,16]{1,0:T(8,128)} %entries_in.1, s32[6,16]{1,0:T(8,128)} %cells_in.1, s32[1,8]{1,0:T(1,128)} %bitcast.4), custom_call_target="tpu_custom_call" | custom-call | flops 1 | bytes 1 | tf_op jit(solution)/shard_map/pack/pallas_call | solution.py:683
  1.5 1.3 %collective-permute-start = (f32[8,1920]{1,0:T(8,128)S(1)}, f32[8,1920]{1,0:T(8,128)S(1)}, u32[]{:S(2)}, u32[]{:S(2)}) collective-permute-start(f32[8,1920]{1,0:T(8,128)S(1)} %get-tuple-element.87.own), channel_id=1, source_target_pairs={{0,8},{1,9},{2,10},{3,11},{4,12},{5,13},{6,14},{7,15},{16,24},{17,... | collective-permute-start | bytes 184328 | tf_op jit(solution)/shard_map/ppermute | solution.py:721
  2.8 1.8 %start.1 = (f32[3,2,144,128]{3,2,1,0:T(8,128)S(1)}, f32[6,2,144,128]{3,2,1,0:T(8,128)S(1)}, f32[6,2,128,128]{3,2,1,0:T(8,128)S(1)}, f32[16,128]{1,0:T(8,128)S(1)...) custom-call(f32[3,2,128,128]{3,2,1,0:T(8,128)} %velocity.1, ...), custom_call_target="tpu_custom_call" | custom-call | flops 8388608 | bytes 8388608 | tf_op jit(solution)/shard_map/start/pallas_call | solution.py:683
  4.6 2.8 %collective-permute-done.behind = f32[8,1920]{1,0:T(8,128)S(1)} collective-permute-done((f32[8,1920]{1,0:T(8,128)S(1)}, f32[8,1920]{1,0:T(8,128)S(1)}, u32[]{:S(2)}, u32[]{:S(2)}) %collective-permute-start) | collective-permute-done | bytes 61472 | tf_op jit(solution)/shard_map/ppermute | solution.py:721
  7.4 0.9 %split.1 = f32[8,56,128]{2,1,0:T(8,128)} custom-call(f32[8,1920]{1,0:T(8,128)S(1)} %get-tuple-element.87.own, f32[8,1920]{1,0:T(8,128)S(1)} %collective-permute-done.behind, s32[1,8]{1,0:T(1,128)S(1)} %get-tuple-element.88.cells, f32[16,128]{1,0:T(8,128)S(1)} %get-tuple-element.86.after_this.coef_ref), custom_call_target="tpu_custom_call" | custom-call | flops 1 | bytes 1 | tf_op jit(solution)/shard_map/split/pallas_call | solution.py:683
  8.3 6.3 %all-to-all-start = ((f32[8,56,128]{2,1,0:T(8,128)}), f32[8,56,128]{2,1,0:T(8,128)S(1)}, u32[]{:S(2)}, u32[]{:S(2)}) async-start(f32[8,56,128]{2,1,0:T(8,128)} %split.1), calls=%async_computation | async-start | bytes 458752 | tf_op jit(solution)/shard_map/all_to_all | solution.py:774
  14.6 3.5 %collective-permute-start.4 = (f32[3,128,128]{2,1,0:T(8,128)S(1)}, f32[3,128,128]{2,1,0:T(8,128)S(1)}, u32[]{:S(2)}, u32[]{:S(2)}) collective-permute-start(f32[3,128,128]{2,1,0:T(8,128)S(1)} %get-tuple-element.99), channel_id=1, source_target_pairs={{1,2},{3,4},{5,6},{7,8},{9,10},{11,12},{13,14},{2,1},{4,3},{6,5},{... | collective-permute-start | bytes 589832 | tf_op jit(solution)/shard_map/ppermute | solution.py:763
  18.1 1.5 %all-to-all-done.parts = f32[8,56,128]{2,1,0:T(8,128)S(1)} async-done(((f32[8,56,128]{2,1,0:T(8,128)}), f32[8,56,128]{2,1,0:T(8,128)S(1)}, u32[]{:S(2)}, u32[]{:S(2)}) %all-to-all-start) | async-done | bytes 229408 | tf_op jit(solution)/shard_map/all_to_all | solution.py:774
  19.6 0.6 %prepare.1 = (f32[6,3,3,16,128]{4,3,2,1,0:T(8,128)S(1)}, f32[128,128]{1,0:T(8,128)S(1)}) custom-call(f32[8,56,128]{2,1,0:T(8,128)S(1)} %all-to-all-done.parts, f32[16,128]{1,0:T(8,128)S(1)} %get-tuple-element.89.loads, f32[16,128]{1,0:T(8,128)S(1)} %get-tuple-element.82.after_this.steps_table), custom_call_target="tpu_custom_call" | custom-call | flops 1 | bytes 1 | tf_op jit(solution)/shard_map/prepare/pallas_call | solution.py:683
  20.2 0.3 first.1
  20.4 3.7 %collective-permute-start.8 = (f32[3,128,128]{2,1,0:T(8,128)S(1)}, f32[3,128,128]{2,1,0:T(8,128)S(1)}, u32[]{:S(2)}, u32[]{:S(2)}) collective-permute-start(f32[3,128,128]{2,1,0:T(8,128)S(1)} %get-tuple-element.109), channel_id=1, source_target_pairs={{1,2},{3,4},{5,6},{7,8},{9,10},{11,12},{13,14},{2,1},{4,3},{6,5},{... | collective-permute-start | bytes 589832 | tf_op jit(solution)/shard_map/ppermute | solution.py:794
  24.3 0.5 collective-permute-start.2
  24.9 0.7 %collective-permute-done.1.msg_x = f32[128,128]{1,0:T(8,128)S(1)} collective-permute-done((f32[128,128]{1,0:T(8,128)S(1)}, f32[128,128]{1,0:T(8,128)S(1)}, u32[]{:S(2)}, u32[]{:S(2)}) %collective-permute-start.1) | collective-permute-done | bytes 65568 | tf_op jit(solution)/shard_map/ppermute | solution.py:764
  25.7 0.4 collective-permute-done.3.msg_z
  26.0 0.3 near0.1
  26.3 0.2 collective-permute-start.5
  26.5 0.4 collective-permute-start.6
  27.0 0.6 %far0.1 = (f32[3,2,144,128]{3,2,1,0:T(8,128)S(1)}, f32[6,2,144,128]{3,2,1,0:T(8,128)S(1)}, f32[6,2,128,128]{3,2,1,0:T(8,128)S(1)}, f32[3,128,128]{2,1,0:T(8,128)S(1)}, f32[3,128,128]{2,1,0:T(8,128)S(1)}) custom-call(f32[3,2,144,128]{3,2,1,0:T(8,128)S(1)} %get-tuple-element.96.V0, ...), custom_call_target="tpu_custom_call", output_to_operand_aliasing={{0}: (0, {}), {1}: (1, {}), {2}: (2, {})} | custom-call | flops 1 | bytes 1 | tf_op jit(solution)/shard_map/far0/pallas_call | solution.py:683
  27.6 3.4 %collective-permute-start.12 = (f32[3,128,128]{2,1,0:T(8,128)S(1)}, f32[3,128,128]{2,1,0:T(8,128)S(1)}, u32[]{:S(2)}, u32[]{:S(2)}) collective-permute-start(f32[3,128,128]{2,1,0:T(8,128)S(1)} %get-tuple-element.120), channel_id=1, source_target_pairs={{1,2},{3,4},{5,6},{7,8},{9,10},{11,12},{13,14},{2,1},{4,3},{6,5},{... | collective-permute-start | bytes 589832 | tf_op jit(solution)/shard_map/ppermute | solution.py:831
  31.0 0.3 near1.1
  31.3 0.6 %far1.1 = (f32[3,2,144,128]{3,2,1,0:T(8,128)S(1)}, f32[6,2,144,128]{3,2,1,0:T(8,128)S(1)}, f32[6,2,128,128]{3,2,1,0:T(8,128)S(1)}, f32[3,128,128]{2,1,0:T(8,128)S(1)}, f32[3,128,128]{2,1,0:T(8,128)S(1)}) custom-call(f32[3,2,144,128]{3,2,1,0:T(8,128)S(1)} %get-tuple-element.106.V0, ...), custom_call_target="tpu_custom_call", output_to_operand_aliasing={{0}: (0, {}), {1}: (1, {}), {2}: (2, {})} | custom-call | flops 1 | bytes 1 | tf_op jit(solution)/shard_map/far1/pallas_call | solution.py:683
  32.0 2.2 %collective-permute-start.16 = (f32[3,128,128]{2,1,0:T(8,128)S(1)}, f32[3,128,128]{2,1,0:T(8,128)S(1)}, u32[]{:S(2)}, u32[]{:S(2)}) collective-permute-start(f32[3,128,128]{2,1,0:T(8,128)S(1)} %get-tuple-element.131), channel_id=1, source_target_pairs={{1,2},{3,4},{5,6},{7,8},{9,10},{11,12},{13,14},{2,1},{4,3},{6,5},{... | collective-permute-start | bytes 589832 | tf_op jit(solution)/shard_map/ppermute | solution.py:831
  34.1 1.4 %collective-permute-start.9 = (f32[128,128]{1,0:T(8,128)S(1)}, f32[128,128]{1,0:T(8,128)S(1)}, u32[]{:S(2)}, u32[]{:S(2)}) collective-permute-start(f32[128,128]{1,0:T(8,128)S(1)} %get-tuple-element.114), channel_id=1, source_target_pairs={{0,1},{1,0},{2,3},{3,2},{4,5},{5,4},{6,7},{7,6},{8,9},{9,8},{10,11... | collective-permute-start | bytes 196616 | tf_op jit(solution)/shard_map/ppermute | solution.py:814
  35.6 0.4 collective-permute-start.11
  36.0 0.4 collective-permute-done.9.msg_x
  36.4 0.4 collective-permute-done.10.msg_y
  36.9 0.3 near2.1
  37.2 0.4 collective-permute-start.13
  37.6 0.2 collective-permute-start.14
  37.8 0.3 collective-permute-start.15
  38.1 0.6 %far2.1 = (f32[3,2,144,128]{3,2,1,0:T(8,128)S(1)}, f32[6,2,144,128]{3,2,1,0:T(8,128)S(1)}, f32[6,2,128,128]{3,2,1,0:T(8,128)S(1)}, f32[3,128,128]{2,1,0:T(8,128)S(1)}, f32[3,128,128]{2,1,0:T(8,128)S(1)}) custom-call(f32[3,2,144,128]{3,2,1,0:T(8,128)S(1)} %get-tuple-element.117.V0, ...), custom_call_target="tpu_custom_call", output_to_operand_aliasing={{0}: (0, {}), {1}: (1, {}), {2}: (2, {})} | custom-call | flops 1 | bytes 1 | tf_op jit(solution)/shard_map/far2/pallas_call | solution.py:683
  38.7 3.2 %collective-permute-start.20 = (f32[3,128,128]{2,1,0:T(8,128)S(1)}, f32[3,128,128]{2,1,0:T(8,128)S(1)}, u32[]{:S(2)}, u32[]{:S(2)}) collective-permute-start(f32[3,128,128]{2,1,0:T(8,128)S(1)} %get-tuple-element.142), channel_id=1, source_target_pairs={{1,2},{3,4},{5,6},{7,8},{9,10},{11,12},{13,14},{2,1},{4,3},{6,5},{... | collective-permute-start | bytes 589832 | tf_op jit(solution)/shard_map/ppermute | solution.py:831
  41.9 0.3 near3.1
  42.2 0.6 %far3.1 = (f32[3,2,144,128]{3,2,1,0:T(8,128)S(1)}, f32[6,2,144,128]{3,2,1,0:T(8,128)S(1)}, f32[6,2,128,128]{3,2,1,0:T(8,128)S(1)}, f32[3,128,128]{2,1,0:T(8,128)S(1)}, f32[3,128,128]{2,1,0:T(8,128)S(1)}) custom-call(f32[3,2,144,128]{3,2,1,0:T(8,128)S(1)} %get-tuple-element.128.V0, ...), custom_call_target="tpu_custom_call", output_to_operand_aliasing={{0}: (0, {}), {1}: (1, {}), {2}: (2, {})} | custom-call | flops 1 | bytes 1 | tf_op jit(solution)/shard_map/far3/pallas_call | solution.py:683
  42.8 2.4 %collective-permute-start.24 = (f32[3,128,128]{2,1,0:T(8,128)S(1)}, f32[3,128,128]{2,1,0:T(8,128)S(1)}, u32[]{:S(2)}, u32[]{:S(2)}) collective-permute-start(f32[3,128,128]{2,1,0:T(8,128)S(1)} %get-tuple-element.153), channel_id=1, source_target_pairs={{1,2},{3,4},{5,6},{7,8},{9,10},{11,12},{13,14},{2,1},{4,3},{6,5},{... | collective-permute-start | bytes 589832 | tf_op jit(solution)/shard_map/ppermute | solution.py:831
  45.3 1.2 %collective-permute-start.17 = (f32[128,128]{1,0:T(8,128)S(1)}, f32[128,128]{1,0:T(8,128)S(1)}, u32[]{:S(2)}, u32[]{:S(2)}) collective-permute-start(f32[128,128]{1,0:T(8,128)S(1)} %get-tuple-element.136), channel_id=1, source_target_pairs={{0,1},{1,0},{2,3},{3,2},{4,5},{5,4},{6,7},{7,6},{8,9},{9,8},{10,11... | collective-permute-start | bytes 196616 | tf_op jit(solution)/shard_map/ppermute | solution.py:814
  46.5 0.4 collective-permute-start.19
  47.0 0.4 collective-permute-done.17.msg_x
  47.4 0.4 collective-permute-done.18.msg_y
  47.9 0.3 near4.1
  48.1 0.4 collective-permute-start.21
  48.5 0.2 collective-permute-start.22
  48.7 0.3 collective-permute-start.23
  49.0 0.4 far4.1
  49.5 0.3 collective-permute-done.22.msg_y
  50.0 1.2 %near5.1 = (f32[3,2,144,128]{3,2,1,0:T(8,128)S(1)}, f32[6,2,144,128]{3,2,1,0:T(8,128)S(1)}, f32[6,2,128,128]{3,2,1,0:T(8,128)S(1)}, f32[3,2,128,128]{3,2,1,0:T(8...) custom-call(f32[3,2,144,128]{3,2,1,0:T(8,128)S(1)} %get-tuple-elemen, ...), custom_call_target="tpu_custom_call", output_to_operand_aliasing={{0}: (0, {}), {1}: (1, {}), {2}: (2, {})} | custom-call | flops 1 | bytes 1 | tf_op jit(solution)/shard_map/near5/pallas_call | solution.py:683
  51.2 0.9 %collective-permute-done.24.msg = f32[3,128,128]{2,1,0:T(8,128)S(1)} collective-permute-done((f32[3,128,128]{2,1,0:T(8,128)S(1)}, f32[3,128,128]{2,1,0:T(8,128)S(1)}, u32[]{:S(2)}, u32[]{:S(2)}) %collective-permute-start.24) | collective-permute-done | bytes 196640 | tf_op jit(solution)/shard_map/ppermute | solution.py:831
  52.0 1.2 %last.1 = (f32[3,2,144,128]{3,2,1,0:T(8,128)S(1)}, f32[6,2,144,128]{3,2,1,0:T(8,128)S(1)}, f32[6,2,128,128]{3,2,1,0:T(8,128)S(1)}, f32[3,2,128,128]{3,2,1,0:T(8,...) custom-call(f32[3,2,144,128]{3,2,1,0:T(8,128)S(1)} %get-tuple-elemen, ...), custom_call_target="tpu_custom_call", output_to_operand_aliasing={{0}: (0, {}), {1}: (1, {}), {2}: (2, {}), {3}: (8, {}), {4}... | custom-call | flops 1 | bytes 1 | tf_op jit(solution)/shard_map/last/pallas_call | solution.py:683
  (21 shorter events, 1.1 us)
Async XLA Ops:
  1.5 5.9 %collective-permute-start = (f32[8,1920]{1,0:T(8,128)S(1)}, f32[8,1920]{1,0:T(8,128)S(1)}, u32[]{:S(2)}, u32[]{:S(2)}) collective-permute-start(f32[8,1920]{1,0:T(8,128)S(1)} %get-tuple-element.87.own), channel_id=1, source_target_pairs={{0,8},{1,9},{2,10},{3,11},{4,12},{5,13},{6,14},{7,15},{16,24},{17,... | collective-permute-start | bytes 184328 | tf_op jit(solution)/shard_map/ppermute | solution.py:721
  8.3 11.3 %all-to-all-start = ((f32[8,56,128]{2,1,0:T(8,128)}), f32[8,56,128]{2,1,0:T(8,128)S(1)}, u32[]{:S(2)}, u32[]{:S(2)}) async-start(f32[8,56,128]{2,1,0:T(8,128)} %split.1), calls=%async_computation | async-start | bytes 458752 | tf_op jit(solution)/shard_map/all_to_all | solution.py:774
  14.6 12.4 %collective-permute-start.4 = (f32[3,128,128]{2,1,0:T(8,128)S(1)}, f32[3,128,128]{2,1,0:T(8,128)S(1)}, u32[]{:S(2)}, u32[]{:S(2)}) collective-permute-start(f32[3,128,128]{2,1,0:T(8,128)S(1)} %get-tuple-element.99), channel_id=1, source_target_pairs={{1,2},{3,4},{5,6},{7,8},{9,10},{11,12},{13,14},{2,1},{4,3},{6,5},{... | collective-permute-start | bytes 589832 | tf_op jit(solution)/shard_map/ppermute | solution.py:763
  20.4 10.9 %collective-permute-start.8 = (f32[3,128,128]{2,1,0:T(8,128)S(1)}, f32[3,128,128]{2,1,0:T(8,128)S(1)}, u32[]{:S(2)}, u32[]{:S(2)}) collective-permute-start(f32[3,128,128]{2,1,0:T(8,128)S(1)} %get-tuple-element.109), channel_id=1, source_target_pairs={{1,2},{3,4},{5,6},{7,8},{9,10},{11,12},{13,14},{2,1},{4,3},{6,5},{... | collective-permute-start | bytes 589832 | tf_op jit(solution)/shard_map/ppermute | solution.py:794
  24.2 1.3 %collective-permute-start.1 = (f32[128,128]{1,0:T(8,128)S(1)}, f32[128,128]{1,0:T(8,128)S(1)}, u32[]{:S(2)}, u32[]{:S(2)}) collective-permute-start(f32[128,128]{1,0:T(8,128)S(1)} %get-tuple-element.93), channel_id=1, source_target_pairs={{0,1},{1,0},{2,3},{3,2},{4,5},{5,4},{6,7},{7,6},{8,9},{9,8},{10,11... | collective-permute-start | bytes 196616 | tf_op jit(solution)/shard_map/ppermute | solution.py:764
  24.3 1.4 %collective-permute-start.2 = (f32[128,128]{1,0:T(8,128)S(1)}, f32[128,128]{1,0:T(8,128)S(1)}, u32[]{:S(2)}, u32[]{:S(2)}) collective-permute-start(f32[128,128]{1,0:T(8,128)S(1)} %get-tuple-element.94), channel_id=1, source_target_pairs={{0,1},{1,0},{2,3},{3,2},{4,5},{5,4},{6,7},{7,6},{8,9},{9,8},{10,11... | collective-permute-start | bytes 196616 | tf_op jit(solution)/shard_map/ppermute | solution.py:764
  24.8 1.3 %collective-permute-start.3 = (f32[128,128]{1,0:T(8,128)S(1)}, f32[128,128]{1,0:T(8,128)S(1)}, u32[]{:S(2)}, u32[]{:S(2)}) collective-permute-start(f32[128,128]{1,0:T(8,128)S(1)} %get-tuple-element.95), channel_id=1, source_target_pairs={{0,1},{1,0},{2,3},{3,2},{4,5},{5,4},{6,7},{7,6},{8,9},{9,8},{10,11... | collective-permute-start | bytes 196616 | tf_op jit(solution)/shard_map/ppermute | solution.py:764
  26.3 4.7 %collective-permute-start.5 = (f32[128,128]{1,0:T(8,128)S(1)}, f32[128,128]{1,0:T(8,128)S(1)}, u32[]{:S(2)}, u32[]{:S(2)}) collective-permute-start(f32[128,128]{1,0:T(8,128)S(1)} %get-tuple-element.103), channel_id=1, source_target_pairs={{0,1},{1,0},{2,3},{3,2},{4,5},{5,4},{6,7},{7,6},{8,9},{9,8},{10,11... | collective-permute-start | bytes 196616 | tf_op jit(solution)/shard_map/ppermute | solution.py:814
  26.5 4.5 %collective-permute-start.6 = (f32[128,128]{1,0:T(8,128)S(1)}, f32[128,128]{1,0:T(8,128)S(1)}, u32[]{:S(2)}, u32[]{:S(2)}) collective-permute-start(f32[128,128]{1,0:T(8,128)S(1)} %get-tuple-element.104), channel_id=1, source_target_pairs={{0,1},{1,0},{2,3},{3,2},{4,5},{5,4},{6,7},{7,6},{8,9},{9,8},{10,11... | collective-permute-start | bytes 196616 | tf_op jit(solution)/shard_map/ppermute | solution.py:814
  26.9 4.2 %collective-permute-start.7 = (f32[128,128]{1,0:T(8,128)S(1)}, f32[128,128]{1,0:T(8,128)S(1)}, u32[]{:S(2)}, u32[]{:S(2)}) collective-permute-start(f32[128,128]{1,0:T(8,128)S(1)} %get-tuple-element.105), channel_id=1, source_target_pairs={{0,1},{1,0},{2,3},{3,2},{4,5},{5,4},{6,7},{7,6},{8,9},{9,8},{10,11... | collective-permute-start | bytes 196616 | tf_op jit(solution)/shard_map/ppermute | solution.py:814
  27.6 10.5 %collective-permute-start.12 = (f32[3,128,128]{2,1,0:T(8,128)S(1)}, f32[3,128,128]{2,1,0:T(8,128)S(1)}, u32[]{:S(2)}, u32[]{:S(2)}) collective-permute-start(f32[3,128,128]{2,1,0:T(8,128)S(1)} %get-tuple-element.120), channel_id=1, source_target_pairs={{1,2},{3,4},{5,6},{7,8},{9,10},{11,12},{13,14},{2,1},{4,3},{6,5},{... | collective-permute-start | bytes 589832 | tf_op jit(solution)/shard_map/ppermute | solution.py:831
  32.0 10.2 %collective-permute-start.16 = (f32[3,128,128]{2,1,0:T(8,128)S(1)}, f32[3,128,128]{2,1,0:T(8,128)S(1)}, u32[]{:S(2)}, u32[]{:S(2)}) collective-permute-start(f32[3,128,128]{2,1,0:T(8,128)S(1)} %get-tuple-element.131), channel_id=1, source_target_pairs={{1,2},{3,4},{5,6},{7,8},{9,10},{11,12},{13,14},{2,1},{4,3},{6,5},{... | collective-permute-start | bytes 589832 | tf_op jit(solution)/shard_map/ppermute | solution.py:831
  34.1 2.3 %collective-permute-start.9 = (f32[128,128]{1,0:T(8,128)S(1)}, f32[128,128]{1,0:T(8,128)S(1)}, u32[]{:S(2)}, u32[]{:S(2)}) collective-permute-start(f32[128,128]{1,0:T(8,128)S(1)} %get-tuple-element.114), channel_id=1, source_target_pairs={{0,1},{1,0},{2,3},{3,2},{4,5},{5,4},{6,7},{7,6},{8,9},{9,8},{10,11... | collective-permute-start | bytes 196616 | tf_op jit(solution)/shard_map/ppermute | solution.py:814
  35.5 1.3 %collective-permute-start.10 = (f32[128,128]{1,0:T(8,128)S(1)}, f32[128,128]{1,0:T(8,128)S(1)}, u32[]{:S(2)}, u32[]{:S(2)}) collective-permute-start(f32[128,128]{1,0:T(8,128)S(1)} %get-tuple-element.115), channel_id=1, source_target_pairs={{0,1},{1,0},{2,3},{3,2},{4,5},{5,4},{6,7},{7,6},{8,9},{9,8},{10,11... | collective-permute-start | bytes 196616 | tf_op jit(solution)/shard_map/ppermute | solution.py:814
  35.6 1.3 %collective-permute-start.11 = (f32[128,128]{1,0:T(8,128)S(1)}, f32[128,128]{1,0:T(8,128)S(1)}, u32[]{:S(2)}, u32[]{:S(2)}) collective-permute-start(f32[128,128]{1,0:T(8,128)S(1)} %get-tuple-element.116), channel_id=1, source_target_pairs={{0,1},{1,0},{2,3},{3,2},{4,5},{5,4},{6,7},{7,6},{8,9},{9,8},{10,11... | collective-permute-start | bytes 196616 | tf_op jit(solution)/shard_map/ppermute | solution.py:814
  37.2 4.7 %collective-permute-start.13 = (f32[128,128]{1,0:T(8,128)S(1)}, f32[128,128]{1,0:T(8,128)S(1)}, u32[]{:S(2)}, u32[]{:S(2)}) collective-permute-start(f32[128,128]{1,0:T(8,128)S(1)} %get-tuple-element.125), channel_id=1, source_target_pairs={{0,1},{1,0},{2,3},{3,2},{4,5},{5,4},{6,7},{7,6},{8,9},{9,8},{10,11... | collective-permute-start | bytes 196616 | tf_op jit(solution)/shard_map/ppermute | solution.py:814
  37.6 4.3 %collective-permute-start.14 = (f32[128,128]{1,0:T(8,128)S(1)}, f32[128,128]{1,0:T(8,128)S(1)}, u32[]{:S(2)}, u32[]{:S(2)}) collective-permute-start(f32[128,128]{1,0:T(8,128)S(1)} %get-tuple-element.126), channel_id=1, source_target_pairs={{0,1},{1,0},{2,3},{3,2},{4,5},{5,4},{6,7},{7,6},{8,9},{9,8},{10,11... | collective-permute-start | bytes 196616 | tf_op jit(solution)/shard_map/ppermute | solution.py:814
  37.8 4.1 %collective-permute-start.15 = (f32[128,128]{1,0:T(8,128)S(1)}, f32[128,128]{1,0:T(8,128)S(1)}, u32[]{:S(2)}, u32[]{:S(2)}) collective-permute-start(f32[128,128]{1,0:T(8,128)S(1)} %get-tuple-element.127), channel_id=1, source_target_pairs={{0,1},{1,0},{2,3},{3,2},{4,5},{5,4},{6,7},{7,6},{8,9},{9,8},{10,11... | collective-permute-start | bytes 196616 | tf_op jit(solution)/shard_map/ppermute | solution.py:814
  38.7 10.3 %collective-permute-start.20 = (f32[3,128,128]{2,1,0:T(8,128)S(1)}, f32[3,128,128]{2,1,0:T(8,128)S(1)}, u32[]{:S(2)}, u32[]{:S(2)}) collective-permute-start(f32[3,128,128]{2,1,0:T(8,128)S(1)} %get-tuple-element.142), channel_id=1, source_target_pairs={{1,2},{3,4},{5,6},{7,8},{9,10},{11,12},{13,14},{2,1},{4,3},{6,5},{... | collective-permute-start | bytes 589832 | tf_op jit(solution)/shard_map/ppermute | solution.py:831
  42.8 9.2 %collective-permute-start.24 = (f32[3,128,128]{2,1,0:T(8,128)S(1)}, f32[3,128,128]{2,1,0:T(8,128)S(1)}, u32[]{:S(2)}, u32[]{:S(2)}) collective-permute-start(f32[3,128,128]{2,1,0:T(8,128)S(1)} %get-tuple-element.153), channel_id=1, source_target_pairs={{1,2},{3,4},{5,6},{7,8},{9,10},{11,12},{13,14},{2,1},{4,3},{6,5},{... | collective-permute-start | bytes 589832 | tf_op jit(solution)/shard_map/ppermute | solution.py:831
  45.3 2.1 %collective-permute-start.17 = (f32[128,128]{1,0:T(8,128)S(1)}, f32[128,128]{1,0:T(8,128)S(1)}, u32[]{:S(2)}, u32[]{:S(2)}) collective-permute-start(f32[128,128]{1,0:T(8,128)S(1)} %get-tuple-element.136), channel_id=1, source_target_pairs={{0,1},{1,0},{2,3},{3,2},{4,5},{5,4},{6,7},{7,6},{8,9},{9,8},{10,11... | collective-permute-start | bytes 196616 | tf_op jit(solution)/shard_map/ppermute | solution.py:814
  46.5 1.3 %collective-permute-start.18 = (f32[128,128]{1,0:T(8,128)S(1)}, f32[128,128]{1,0:T(8,128)S(1)}, u32[]{:S(2)}, u32[]{:S(2)}) collective-permute-start(f32[128,128]{1,0:T(8,128)S(1)} %get-tuple-element.137), channel_id=1, source_target_pairs={{0,1},{1,0},{2,3},{3,2},{4,5},{5,4},{6,7},{7,6},{8,9},{9,8},{10,11... | collective-permute-start | bytes 196616 | tf_op jit(solution)/shard_map/ppermute | solution.py:814
  46.5 1.3 %collective-permute-start.19 = (f32[128,128]{1,0:T(8,128)S(1)}, f32[128,128]{1,0:T(8,128)S(1)}, u32[]{:S(2)}, u32[]{:S(2)}) collective-permute-start(f32[128,128]{1,0:T(8,128)S(1)} %get-tuple-element.138), channel_id=1, source_target_pairs={{0,1},{1,0},{2,3},{3,2},{4,5},{5,4},{6,7},{7,6},{8,9},{9,8},{10,11... | collective-permute-start | bytes 196616 | tf_op jit(solution)/shard_map/ppermute | solution.py:814
  48.1 1.3 %collective-permute-start.21 = (f32[128,128]{1,0:T(8,128)S(1)}, f32[128,128]{1,0:T(8,128)S(1)}, u32[]{:S(2)}, u32[]{:S(2)}) collective-permute-start(f32[128,128]{1,0:T(8,128)S(1)} %get-tuple-element.147), channel_id=1, source_target_pairs={{0,1},{1,0},{2,3},{3,2},{4,5},{5,4},{6,7},{7,6},{8,9},{9,8},{10,11... | collective-permute-start | bytes 196616 | tf_op jit(solution)/shard_map/ppermute | solution.py:814
  48.5 1.3 %collective-permute-start.22 = (f32[128,128]{1,0:T(8,128)S(1)}, f32[128,128]{1,0:T(8,128)S(1)}, u32[]{:S(2)}, u32[]{:S(2)}) collective-permute-start(f32[128,128]{1,0:T(8,128)S(1)} %get-tuple-element.148), channel_id=1, source_target_pairs={{0,1},{1,0},{2,3},{3,2},{4,5},{5,4},{6,7},{7,6},{8,9},{9,8},{10,11... | collective-permute-start | bytes 196616 | tf_op jit(solution)/shard_map/ppermute | solution.py:814
  48.7 1.3 %collective-permute-start.23 = (f32[128,128]{1,0:T(8,128)S(1)}, f32[128,128]{1,0:T(8,128)S(1)}, u32[]{:S(2)}, u32[]{:S(2)}) collective-permute-start(f32[128,128]{1,0:T(8,128)S(1)} %get-tuple-element.149), channel_id=1, source_target_pairs={{0,1},{1,0},{2,3},{3,2},{4,5},{5,4},{6,7},{7,6},{8,9},{9,8},{10,11... | collective-permute-start | bytes 196616 | tf_op jit(solution)/shard_map/ppermute | solution.py:814

commit v13 on v12

--- a/solution.py
+++ b/solution.py
@@ -36,9 +36,9 @@
     return lane_roll(x, -1)
 
 
-def over_rows(count, work):
+def over_rows(count, work, first=0):
     def step(i, carry):
-        work(pl.multiple_of(i * ROWS, ROWS))
+        work(pl.multiple_of(first + i * ROWS, ROWS))
         return carry
 
     lax.fori_loop(0, count // ROWS, step, 0, unroll=UNROLL)
@@ -65,18 +65,39 @@
         ref[(*where, pl.ds(PAD + across, PAD))] = edge
 
 
-class Parts:
-    def __init__(self, refs):
-        self.refs = refs
+class Halves:
+    def __init__(self, *refs):
+        self.refs, self.half, self.rows = refs, 0, refs[0].shape[1]
+
+    def at(self, out):
+        return pl.ds(out.start - self.half * self.rows, out.size)
 
     def __getitem__(self, at):
-        return self.refs[at[0]][at[1]]
+        return self.refs[self.half][at[0], self.at(at[1])]
 
     def __setitem__(self, at, value):
-        self.refs[at[0]][at[1]] = value
+        self.refs[self.half][at[0], self.at(at[1])] = value
+
+    def add_force(self, plane, force, which, first_row):
+        upper, lower = self.refs
+        above = self.rows - first_row
+        upper[plane, pl.ds(first_row, above)] = upper[plane, pl.ds(first_row, above)] + force[which][:above]
+        lower[plane, pl.ds(0, 16 - above)] = lower[plane, pl.ds(0, 16 - above)] + force[which][above:]
+
+
+def over_message(count, work, msg):
+    if not isinstance(msg, Halves):
+        over_rows(count, work)
+        return
+    for half in range(2):
+        msg.half = half
+        over_rows(msg.rows, work, half * msg.rows)
 
 
 def add_force(ref, index, force, which, first_row):
+    if isinstance(ref, Halves):
+        ref.add_force(*index, force, which, first_row)
+        return
     rows = pl.ds(first_row, 16)
     ref[(*index, rows)] = ref[(*index, rows)] + force[which]
 
@@ -94,7 +115,7 @@
             msg[1, out] = sxz
             msg[2, out] = px
 
-    over_rows(V.shape[2] - 2 * PAD, work)
+    over_message(V.shape[2] - 2 * PAD, work, msg)
     if force is not None:
         add_force(V, (VX, 1), force, (VX, 1), PAD + window)
         if msg is not None:
@@ -116,7 +137,7 @@
             msg[1, out] = qy
             msg[2, out] = qz
 
-    over_rows(V.shape[2] - 2 * PAD, work)
+    over_message(V.shape[2] - 2 * PAD, work, msg)
     if force is not None:
         add_force(V, (VY, 0), force, (VY, 0), PAD + window)
         add_force(V, (VZ, 0), force, (VZ, 0), PAD + window)
@@ -315,7 +336,7 @@
         G[0, out] = keep * (got(1, out) - b * S[XY, 1, here])
         G[1, out] = keep * (got(2, out) - b * S[XZ, 1, here])
 
-    over_rows(R.shape[2], work)
+    over_message(R.shape[2], work, msg)
     if step < unforced:
         add_force(G, (0,), force, (VY, 2), window)
         add_force(G, (1,), force, (VZ, 2), window)
@@ -343,7 +364,7 @@
         V[VZ, 0, here] = V[VZ, 0, here] - (keep * b) * got(1, out)
         G[0, out] = keep * (got(2, out) + b * S[XX, 0, here])
 
-    over_rows(R.shape[2], work)
+    over_message(R.shape[2], work, msg)
     if step < unforced:
         add_force(G, (0,), force, (VX, 2), window)
     if respond is not None:
@@ -358,10 +379,10 @@
 
 def start_kernel(
     velocity, stress, memory, layer_in, lam_in, mu_in, buoy_in, rate_in, defect_in, after_this,
-    V, S, R, coef_ref, near_x, near_y, near_z, msg_far, layer_ref, lam, mu, buoy, rate, defect, sems,
+    V, S, R, coef_ref, near_upper, near_lower, msg_far, layer_ref, lam, mu, buoy, rate, defect, sems,
 ):
     del after_this
-    msg_near = Parts((near_x, near_y, near_z))
+    msg_near = Halves(near_upper, near_lower)
     across = velocity.shape[2]
     inside = pl.ds(PAD, across)
     pairs = [
@@ -462,12 +483,12 @@
         copy.wait()
 
 
-def near_kernel(step, window, V0, S0, R0, coef_ref, force, surface, msg_x, msg_y, msg_z, V, S, R, *rest):
+def near_kernel(step, window, V0, S0, R0, coef_ref, force, surface, upper, lower, V, S, R, *rest):
     G = rest[-1]
-    msg = Parts((msg_x, msg_y, msg_z))
-    send = Parts(rest[:3])
+    msg = Halves(upper, lower)
     even, _, _ = place()
     more = step < STEPS - 1
+    send = Halves(*rest[:2]) if more else None
 
     @pl.when(even)
     def _():
@@ -713,7 +734,7 @@
     r_type = pltpu.VMEM((6, width_x, across, depth), f32)
     c_type = pltpu.VMEM((N_COEF, depth), f32)
     m_type = pltpu.VMEM((3, across, depth), f32)
-    planes = (pltpu.VMEM((across, depth), f32),) * 3
+    planes = (pltpu.VMEM((3, across // 2, depth), f32),) * 2
     ghost = pltpu.VMEM((2, across, depth), f32)
     work = pltpu.VMEM((2, padded, depth), f32)
 
@@ -753,7 +774,7 @@
         in_hbm(velocity, stress, memory, layer[None, :], *tables) + (steps_table,),
         (ANYWHERE,) * 10,
         (v_type, s_type, r_type, c_type, *planes, m_type),
-        (WHOLE,) * 8,
+        (WHOLE,) * 7,
         scratch=(
             pltpu.VMEM((1, depth), jnp.int32), *(pltpu.SMEM(table.shape, f32) for table in tables), dma((21,)),
         ),
@@ -805,7 +826,7 @@
             ins,
             (WHOLE,) * len(ins),
             outs,
-            (WHOLE,) * 6 if more else (WHOLE,) * 3 + (ANYWHERE,) * 3,
+            (WHOLE,) * 5 if more else (WHOLE,) * 3 + (ANYWHERE,) * 3,
             scratch=(ghost,) if more else (dma((15,)), ghost),
             aliases=same,
             name="near" + str(step),

time: 53.7 us -> 54.1 us (level)
  Pallas kernels: 11 us -> 14.5 us
  starting transfers between devices: 32.7 us -> 30.5 us
  waiting for transfers between devices: 8.64 us -> 7.79 us
    pallas_call x17, Pallas kernels: 11 us -> 14.5 us  [call(): pl.pallas_call(kernel, out_shape=outs, in_specs=specs, out_specs=out_spec...]
    ppermute x4, waiting for transfers between devices: 0.86 us -> 4.1 us  [body(): early = lax.ppermute(msg[0], 'line', far)]
    ppermute x15 -> x10, starting transfers between devices: 6.09 us -> 3.92 us  [body(): msg_near = [lax.ppermute(plane, 'line', near) for plane in msg]]
    ppermute x15 -> x10, waiting for transfers between devices: 2.3 us -> 0.35 us  [body(): msg_near = [lax.ppermute(plane, 'line', near) for plane in msg]]
    ppermute x3 -> x2, waiting for transfers between devices: 1.17 us -> 0.01 us  [body(): msg_near = [lax.ppermute(plane, 'line', near) for plane in msg_near]]
  transfers between devices with their start and end apart: 26 -> 20, of which waited for: 14 -> 7; matrix products, arithmetic and copies ran while one was open for 0% -> 0% of each run, Pallas kernels for 15% -> 22%
where the time goes in v13:
time: 54.1 us; the launch traced here: 53.7 us
  starting transfers between devices  30.5 us (56%)
  Pallas kernels  14.5 us (27%)
  waiting for transfers between devices  7.79 us (14%)
  between operations  0.88 us (2%)
    pallas_call x17, Pallas kernels, call(): pl.pallas_call(kernel, out_shape=outs, in_specs=specs, out_specs=out_spec...  14.5 us
    ppermute x4, starting transfers between devices, body(): early = lax.ppermute(msg[0], 'line', far)  11.2 us
    all_to_all x1, starting transfers between devices, body(): lax.all_to_all(parts, 'line', 0, 0, axis_index_groups=groups, tiled=True)  6.3 us
    ppermute x4, waiting for transfers between devices, body(): early = lax.ppermute(msg[0], 'line', far)  4.1 us
    ppermute x10, starting transfers between devices, body(): msg_near = [lax.ppermute(plane, 'line', near) for plane in msg]  3.92 us
    ppermute x1, starting transfers between devices, body(): early = lax.ppermute(early, 'line', far)  3.74 us
    ppermute x1, starting transfers between devices, body(): msg_far = lax.ppermute(msg_far, 'line', far)  3.53 us
    ppermute x1, waiting for transfers between devices, ahead_by(): lax.ppermute(x, 'line', [(i, i + distance) for i in range(tiles - distanc...  2.4 us
  transfers between devices with their start and end apart: 20, of which 7 were waited for; matrix products, arithmetic and copies ran while one was open for 0% of the time, Pallas kernels for 22%

profile of v13, /device:TPU:17, one launch (start us, length us, event | category | flops | bytes accessed | tf_op | source)
XLA Modules:
  0.0 53.7 jit_solution(8088046337132722903)
XLA Ops:
  0.6 0.9 %pack.1 = (f32[8,1920]{1,0:T(8,128)S(1)}, f32[16,128]{1,0:T(8,128)S(1)}, f32[16,128]{1,0:T(8,128)S(1)}, s32[1,8]{1,0:T(1,128)S(1)}) custom-call(f32[8,1536]{1,0:T(8,128)} %bitcast.3, f32[16,128]{1,0:T(8,128)} %loads_in.1, s32[6,16]{1,0:T(8,128)} %entries_in.1, s32[6,16]{1,0:T(8,128)} %cells_in.1, s32[1,8]{1,0:T(1,128)} %bitcast.4), custom_call_target="tpu_custom_call" | custom-call | flops 1 | bytes 1 | tf_op jit(solution)/shard_map/pack/pallas_call | solution.py:704
  1.5 1.3 %collective-permute-start = (f32[8,1920]{1,0:T(8,128)S(1)}, f32[8,1920]{1,0:T(8,128)S(1)}, u32[]{:S(2)}, u32[]{:S(2)}) collective-permute-start(f32[8,1920]{1,0:T(8,128)S(1)} %get-tuple-element.81.own), channel_id=1, source_target_pairs={{0,8},{1,9},{2,10},{3,11},{4,12},{5,13},{6,14},{7,15},{16,24},{17,... | collective-permute-start | bytes 184328 | tf_op jit(solution)/shard_map/ppermute | solution.py:742
  2.8 2.2 %start.1 = (f32[3,2,144,128]{3,2,1,0:T(8,128)S(1)}, f32[6,2,144,128]{3,2,1,0:T(8,128)S(1)}, f32[6,2,128,128]{3,2,1,0:T(8,128)S(1)}, f32[16,128]{1,0:T(8,128)S(1)...) custom-call(f32[3,2,128,128]{3,2,1,0:T(8,128)} %velocity.1, ...), custom_call_target="tpu_custom_call" | custom-call | flops 8388608 | bytes 8388608 | tf_op jit(solution)/shard_map/start/pallas_call | solution.py:704
  5.0 2.4 %collective-permute-done.behind = f32[8,1920]{1,0:T(8,128)S(1)} collective-permute-done((f32[8,1920]{1,0:T(8,128)S(1)}, f32[8,1920]{1,0:T(8,128)S(1)}, u32[]{:S(2)}, u32[]{:S(2)}) %collective-permute-start) | collective-permute-done | bytes 61472 | tf_op jit(solution)/shard_map/ppermute | solution.py:742
  7.4 0.9 %split.1 = f32[8,56,128]{2,1,0:T(8,128)} custom-call(f32[8,1920]{1,0:T(8,128)S(1)} %get-tuple-element.81.own, f32[8,1920]{1,0:T(8,128)S(1)} %collective-permute-done.behind, s32[1,8]{1,0:T(1,128)S(1)} %get-tuple-element.82.cells, f32[16,128]{1,0:T(8,128)S(1)} %get-tuple-element.80.after_this.coef_ref), custom_call_target="tpu_custom_call" | custom-call | flops 1 | bytes 1 | tf_op jit(solution)/shard_map/split/pallas_call | solution.py:704
  8.3 6.3 %all-to-all-start = ((f32[8,56,128]{2,1,0:T(8,128)}), f32[8,56,128]{2,1,0:T(8,128)S(1)}, u32[]{:S(2)}, u32[]{:S(2)}) async-start(f32[8,56,128]{2,1,0:T(8,128)} %split.1), calls=%async_computation | async-start | bytes 458752 | tf_op jit(solution)/shard_map/all_to_all | solution.py:795
  14.6 0.0 collective-permute-start.1
  14.6 0.5 collective-permute-start.2
  15.1 3.5 %collective-permute-start.3 = (f32[3,128,128]{2,1,0:T(8,128)S(1)}, f32[3,128,128]{2,1,0:T(8,128)S(1)}, u32[]{:S(2)}, u32[]{:S(2)}) collective-permute-start(f32[3,128,128]{2,1,0:T(8,128)S(1)} %get-tuple-element.92), channel_id=1, source_target_pairs={{1,2},{3,4},{5,6},{7,8},{9,10},{11,12},{13,14},{2,1},{4,3},{6,5},{... | collective-permute-start | bytes 589832 | tf_op jit(solution)/shard_map/ppermute | solution.py:784
  18.6 0.9 %all-to-all-done.parts = f32[8,56,128]{2,1,0:T(8,128)S(1)} async-done(((f32[8,56,128]{2,1,0:T(8,128)}), f32[8,56,128]{2,1,0:T(8,128)S(1)}, u32[]{:S(2)}, u32[]{:S(2)}) %all-to-all-start) | async-done | bytes 229408 | tf_op jit(solution)/shard_map/all_to_all | solution.py:795
  19.6 0.6 %prepare.1 = (f32[6,3,3,16,128]{4,3,2,1,0:T(8,128)S(1)}, f32[128,128]{1,0:T(8,128)S(1)}) custom-call(f32[8,56,128]{2,1,0:T(8,128)S(1)} %all-to-all-done.parts, f32[16,128]{1,0:T(8,128)S(1)} %get-tuple-element.83.loads, f32[16,128]{1,0:T(8,128)S(1)} %get-tuple-element.76.after_this.steps_table), custom_call_target="tpu_custom_call" | custom-call | flops 1 | bytes 1 | tf_op jit(solution)/shard_map/prepare/pallas_call | solution.py:704
  20.2 0.3 first.1
  20.4 3.7 %collective-permute-start.6 = (f32[3,128,128]{2,1,0:T(8,128)S(1)}, f32[3,128,128]{2,1,0:T(8,128)S(1)}, u32[]{:S(2)}, u32[]{:S(2)}) collective-permute-start(f32[3,128,128]{2,1,0:T(8,128)S(1)} %get-tuple-element.101), channel_id=1, source_target_pairs={{1,2},{3,4},{5,6},{7,8},{9,10},{11,12},{13,14},{2,1},{4,3},{6,5},{... | collective-permute-start | bytes 589832 | tf_op jit(solution)/shard_map/ppermute | solution.py:815
  24.2 0.0 collective-permute-done.1.upper
  24.2 0.9 %near0.1 = (f32[3,2,144,128]{3,2,1,0:T(8,128)S(1)}, f32[6,2,144,128]{3,2,1,0:T(8,128)S(1)}, f32[6,2,128,128]{3,2,1,0:T(8,128)S(1)}, f32[3,64,128]{2,1,0:T(8,128)S(1)}, f32[3,64,128]{2,1,0:T(8,128)S(1)}) custom-call(f32[3,2,144,128]{3,2,1,0:T(8,128)S(1)} %get-tuple-element.86.V0, ...), custom_call_target="tpu_custom_call", output_to_operand_aliasing={{0}: (0, {}), {1}: (1, {}), {2}: (2, {})} | custom-call | flops 1 | bytes 1 | tf_op jit(solution)/shard_map/near0/pallas_call | solution.py:704
  25.1 0.1 collective-permute-start.4
  25.2 0.5 collective-permute-start.5
  25.7 0.0 collective-permute-done.3.msg
  25.7 0.6 %far0.1 = (f32[3,2,144,128]{3,2,1,0:T(8,128)S(1)}, f32[6,2,144,128]{3,2,1,0:T(8,128)S(1)}, f32[6,2,128,128]{3,2,1,0:T(8,128)S(1)}, f32[3,128,128]{2,1,0:T(8,128)S(1)}, f32[3,128,128]{2,1,0:T(8,128)S(1)}) custom-call(f32[3,2,144,128]{3,2,1,0:T(8,128)S(1)} %get-tuple-element.89.V0, ...), custom_call_target="tpu_custom_call", output_to_operand_aliasing={{0}: (0, {}), {1}: (1, {}), {2}: (2, {})} | custom-call | flops 1 | bytes 1 | tf_op jit(solution)/shard_map/far0/pallas_call | solution.py:704
  26.3 0.2 collective-permute-done.4.upper
  26.5 0.2 collective-permute-done.5.lower
  26.6 0.8 %near1.1 = (f32[3,2,144,128]{3,2,1,0:T(8,128)S(1)}, f32[6,2,144,128]{3,2,1,0:T(8,128)S(1)}, f32[6,2,128,128]{3,2,1,0:T(8,128)S(1)}, f32[3,64,128]{2,1,0:T(8,128)S(1)}, f32[3,64,128]{2,1,0:T(8,128)S(1)}) custom-call(f32[3,2,144,128]{3,2,1,0:T(8,128)S(1)} %get-tuple-element.93.V0, ...), custom_call_target="tpu_custom_call", output_to_operand_aliasing={{0}: (0, {}), {1}: (1, {}), {2}: (2, {})} | custom-call | flops 1 | bytes 1 | tf_op jit(solution)/shard_map/near1/pallas_call | solution.py:704
  27.5 0.4 collective-permute-start.7
  27.8 0.2 collective-permute-start.8
  28.0 3.3 %collective-permute-start.9 = (f32[3,128,128]{2,1,0:T(8,128)S(1)}, f32[3,128,128]{2,1,0:T(8,128)S(1)}, u32[]{:S(2)}, u32[]{:S(2)}) collective-permute-start(f32[3,128,128]{2,1,0:T(8,128)S(1)} %get-tuple-element.111), channel_id=1, source_target_pairs={{1,2},{3,4},{5,6},{7,8},{9,10},{11,12},{13,14},{2,1},{4,3},{6,5},{... | collective-permute-start | bytes 589832 | tf_op jit(solution)/shard_map/ppermute | solution.py:852
  31.3 0.0 collective-permute-done.6.msg
  31.3 0.6 %far1.1 = (f32[3,2,144,128]{3,2,1,0:T(8,128)S(1)}, f32[6,2,144,128]{3,2,1,0:T(8,128)S(1)}, f32[6,2,128,128]{3,2,1,0:T(8,128)S(1)}, f32[3,128,128]{2,1,0:T(8,128)S(1)}, f32[3,128,128]{2,1,0:T(8,128)S(1)}) custom-call(f32[3,2,144,128]{3,2,1,0:T(8,128)S(1)} %get-tuple-element.98.V0, ...), custom_call_target="tpu_custom_call", output_to_operand_aliasing={{0}: (0, {}), {1}: (1, {}), {2}: (2, {})} | custom-call | flops 1 | bytes 1 | tf_op jit(solution)/shard_map/far1/pallas_call | solution.py:704
  31.9 2.3 %collective-permute-start.12 = (f32[3,128,128]{2,1,0:T(8,128)S(1)}, f32[3,128,128]{2,1,0:T(8,128)S(1)}, u32[]{:S(2)}, u32[]{:S(2)}) collective-permute-start(f32[3,128,128]{2,1,0:T(8,128)S(1)} %get-tuple-element.121), channel_id=1, source_target_pairs={{1,2},{3,4},{5,6},{7,8},{9,10},{11,12},{13,14},{2,1},{4,3},{6,5},{... | collective-permute-start | bytes 589832 | tf_op jit(solution)/shard_map/ppermute | solution.py:852
  34.3 0.0 collective-permute-done.7.upper
  34.3 0.9 %near2.1 = (f32[3,2,144,128]{3,2,1,0:T(8,128)S(1)}, f32[6,2,144,128]{3,2,1,0:T(8,128)S(1)}, f32[6,2,128,128]{3,2,1,0:T(8,128)S(1)}, f32[3,64,128]{2,1,0:T(8,128)S(1)}, f32[3,64,128]{2,1,0:T(8,128)S(1)}) custom-call(f32[3,2,144,128]{3,2,1,0:T(8,128)S(1)} %get-tuple-element.103.V0, ...), custom_call_target="tpu_custom_call", output_to_operand_aliasing={{0}: (0, {}), {1}: (1, {}), {2}: (2, {})} | custom-call | flops 1 | bytes 1 | tf_op jit(solution)/shard_map/near2/pallas_call | solution.py:704
  35.2 1.1 %collective-permute-start.10 = (f32[3,64,128]{2,1,0:T(8,128)S(1)}, f32[3,64,128]{2,1,0:T(8,128)S(1)}, u32[]{:S(2)}, u32[]{:S(2)}) collective-permute-start(f32[3,64,128]{2,1,0:T(8,128)S(1)} %get-tuple-element.116), channel_id=1, source_target_pairs={{0,1},{1,0},{2,3},{3,2},{4,5},{5,4},{6,7},{7,6},{8,9},{9,8},{10,11... | collective-permute-start | bytes 294920 | tf_op jit(solution)/shard_map/ppermute | solution.py:835
  36.3 0.1 collective-permute-start.11
  36.4 0.7 %collective-permute-done.9.msg = f32[3,128,128]{2,1,0:T(8,128)S(1)} collective-permute-done((f32[3,128,128]{2,1,0:T(8,128)S(1)}, f32[3,128,128]{2,1,0:T(8,128)S(1)}, u32[]{:S(2)}, u32[]{:S(2)}) %collective-permute-start.9) | collective-permute-done | bytes 196640 | tf_op jit(solution)/shard_map/ppermute | solution.py:852
  37.1 0.6 %far2.1 = (f32[3,2,144,128]{3,2,1,0:T(8,128)S(1)}, f32[6,2,144,128]{3,2,1,0:T(8,128)S(1)}, f32[6,2,128,128]{3,2,1,0:T(8,128)S(1)}, f32[3,128,128]{2,1,0:T(8,128)S(1)}, f32[3,128,128]{2,1,0:T(8,128)S(1)}) custom-call(f32[3,2,144,128]{3,2,1,0:T(8,128)S(1)} %get-tuple-element.108.V0, ...), custom_call_target="tpu_custom_call", output_to_operand_aliasing={{0}: (0, {}), {1}: (1, {}), {2}: (2, {})} | custom-call | flops 1 | bytes 1 | tf_op jit(solution)/shard_map/far2/pallas_call | solution.py:704
  37.7 0.9 %near3.1 = (f32[3,2,144,128]{3,2,1,0:T(8,128)S(1)}, f32[6,2,144,128]{3,2,1,0:T(8,128)S(1)}, f32[6,2,128,128]{3,2,1,0:T(8,128)S(1)}, f32[3,64,128]{2,1,0:T(8,128)S(1)}, f32[3,64,128]{2,1,0:T(8,128)S(1)}) custom-call(f32[3,2,144,128]{3,2,1,0:T(8,128)S(1)} %get-tuple-element.113.V0, ...), custom_call_target="tpu_custom_call", output_to_operand_aliasing={{0}: (0, {}), {1}: (1, {}), {2}: (2, {})} | custom-call | flops 1 | bytes 1 | tf_op jit(solution)/shard_map/near3/pallas_call | solution.py:704
  38.6 0.1 collective-permute-start.13
  38.7 0.5 collective-permute-start.14
  39.2 3.2 %collective-permute-start.15 = (f32[3,128,128]{2,1,0:T(8,128)S(1)}, f32[3,128,128]{2,1,0:T(8,128)S(1)}, u32[]{:S(2)}, u32[]{:S(2)}) collective-permute-start(f32[3,128,128]{2,1,0:T(8,128)S(1)} %get-tuple-element.131), channel_id=1, source_target_pairs={{1,2},{3,4},{5,6},{7,8},{9,10},{11,12},{13,14},{2,1},{4,3},{6,5},{... | collective-permute-start | bytes 589832 | tf_op jit(solution)/shard_map/ppermute | solution.py:852
  42.5 0.6 %far3.1 = (f32[3,2,144,128]{3,2,1,0:T(8,128)S(1)}, f32[6,2,144,128]{3,2,1,0:T(8,128)S(1)}, f32[6,2,128,128]{3,2,1,0:T(8,128)S(1)}, f32[3,128,128]{2,1,0:T(8,128)S(1)}, f32[3,128,128]{2,1,0:T(8,128)S(1)}) custom-call(f32[3,2,144,128]{3,2,1,0:T(8,128)S(1)} %get-tuple-element.118.V0, ...), custom_call_target="tpu_custom_call", output_to_operand_aliasing={{0}: (0, {}), {1}: (1, {}), {2}: (2, {})} | custom-call | flops 1 | bytes 1 | tf_op jit(solution)/shard_map/far3/pallas_call | solution.py:704
  43.1 2.4 %collective-permute-start.18 = (f32[3,128,128]{2,1,0:T(8,128)S(1)}, f32[3,128,128]{2,1,0:T(8,128)S(1)}, u32[]{:S(2)}, u32[]{:S(2)}) collective-permute-start(f32[3,128,128]{2,1,0:T(8,128)S(1)} %get-tuple-element.141), channel_id=1, source_target_pairs={{1,2},{3,4},{5,6},{7,8},{9,10},{11,12},{13,14},{2,1},{4,3},{6,5},{... | collective-permute-start | bytes 589832 | tf_op jit(solution)/shard_map/ppermute | solution.py:852
  45.5 0.9 %near4.1 = (f32[3,2,144,128]{3,2,1,0:T(8,128)S(1)}, f32[6,2,144,128]{3,2,1,0:T(8,128)S(1)}, f32[6,2,128,128]{3,2,1,0:T(8,128)S(1)}, f32[3,64,128]{2,1,0:T(8,128)S(1)}, f32[3,64,128]{2,1,0:T(8,128)S(1)}) custom-call(f32[3,2,144,128]{3,2,1,0:T(8,128)S(1)} %get-tuple-element.123.V0, ...), custom_call_target="tpu_custom_call", output_to_operand_aliasing={{0}: (0, {}), {1}: (1, {}), {2}: (2, {})} | custom-call | flops 1 | bytes 1 | tf_op jit(solution)/shard_map/near4/pallas_call | solution.py:704
  46.3 0.9 %collective-permute-start.16 = (f32[3,64,128]{2,1,0:T(8,128)S(1)}, f32[3,64,128]{2,1,0:T(8,128)S(1)}, u32[]{:S(2)}, u32[]{:S(2)}) collective-permute-start(f32[3,64,128]{2,1,0:T(8,128)S(1)} %get-tuple-element.136), channel_id=1, source_target_pairs={{0,1},{1,0},{2,3},{3,2},{4,5},{5,4},{6,7},{7,6},{8,9},{9,8},{10,11... | collective-permute-start | bytes 294920 | tf_op jit(solution)/shard_map/ppermute | solution.py:835
  47.3 0.1 collective-permute-start.17
  47.3 0.9 %collective-permute-done.15.msg = f32[3,128,128]{2,1,0:T(8,128)S(1)} collective-permute-done((f32[3,128,128]{2,1,0:T(8,128)S(1)}, f32[3,128,128]{2,1,0:T(8,128)S(1)}, u32[]{:S(2)}, u32[]{:S(2)}) %collective-permute-start.15) | collective-permute-done | bytes 196640 | tf_op jit(solution)/shard_map/ppermute | solution.py:852
  48.3 0.4 far4.1
  48.7 1.3 %near5.1 = (f32[3,2,144,128]{3,2,1,0:T(8,128)S(1)}, f32[6,2,144,128]{3,2,1,0:T(8,128)S(1)}, f32[6,2,128,128]{3,2,1,0:T(8,128)S(1)}, f32[3,2,128,128]{3,2,1,0:T(8...) custom-call(f32[3,2,144,128]{3,2,1,0:T(8,128)S(1)} %get-tuple-elemen, ...), custom_call_target="tpu_custom_call", output_to_operand_aliasing={{0}: (0, {}), {1}: (1, {}), {2}: (2, {})} | custom-call | flops 1 | bytes 1 | tf_op jit(solution)/shard_map/near5/pallas_call | solution.py:704
  50.0 2.5 %collective-permute-done.18.msg = f32[3,128,128]{2,1,0:T(8,128)S(1)} collective-permute-done((f32[3,128,128]{2,1,0:T(8,128)S(1)}, f32[3,128,128]{2,1,0:T(8,128)S(1)}, u32[]{:S(2)}, u32[]{:S(2)}) %collective-permute-start.18) | collective-permute-done | bytes 196640 | tf_op jit(solution)/shard_map/ppermute | solution.py:852
  52.5 1.2 %last.1 = (f32[3,2,144,128]{3,2,1,0:T(8,128)S(1)}, f32[6,2,144,128]{3,2,1,0:T(8,128)S(1)}, f32[6,2,128,128]{3,2,1,0:T(8,128)S(1)}, f32[3,2,128,128]{3,2,1,0:T(8,...) custom-call(f32[3,2,144,128]{3,2,1,0:T(8,128)S(1)} %get-tuple-elemen, ...), custom_call_target="tpu_custom_call", output_to_operand_aliasing={{0}: (0, {}), {1}: (1, {}), {2}: (2, {}), {3}: (8, {}), {4}... | custom-call | flops 1 | bytes 1 | tf_op jit(solution)/shard_map/last/pallas_call | solution.py:704
  (9 shorter events, 0.0 us)
Async XLA Ops:
  1.5 5.9 %collective-permute-start = (f32[8,1920]{1,0:T(8,128)S(1)}, f32[8,1920]{1,0:T(8,128)S(1)}, u32[]{:S(2)}, u32[]{:S(2)}) collective-permute-start(f32[8,1920]{1,0:T(8,128)S(1)} %get-tuple-element.81.own), channel_id=1, source_target_pairs={{0,8},{1,9},{2,10},{3,11},{4,12},{5,13},{6,14},{7,15},{16,24},{17,... | collective-permute-start | bytes 184328 | tf_op jit(solution)/shard_map/ppermute | solution.py:742
  8.3 11.3 %all-to-all-start = ((f32[8,56,128]{2,1,0:T(8,128)}), f32[8,56,128]{2,1,0:T(8,128)S(1)}, u32[]{:S(2)}, u32[]{:S(2)}) async-start(f32[8,56,128]{2,1,0:T(8,128)} %split.1), calls=%async_computation | async-start | bytes 458752 | tf_op jit(solution)/shard_map/all_to_all | solution.py:795
  14.6 9.6 %collective-permute-start.1 = (f32[3,64,128]{2,1,0:T(8,128)S(1)}, f32[3,64,128]{2,1,0:T(8,128)S(1)}, u32[]{:S(2)}, u32[]{:S(2)}) collective-permute-start(f32[3,64,128]{2,1,0:T(8,128)S(1)} %get-tuple-element.87), channel_id=1, source_target_pairs={{0,1},{1,0},{2,3},{3,2},{4,5},{5,4},{6,7},{7,6},{8,9},{9,8},{10,11... | collective-permute-start | bytes 294920 | tf_op jit(solution)/shard_map/ppermute | solution.py:785
  14.6 9.6 %collective-permute-start.2 = (f32[3,64,128]{2,1,0:T(8,128)S(1)}, f32[3,64,128]{2,1,0:T(8,128)S(1)}, u32[]{:S(2)}, u32[]{:S(2)}) collective-permute-start(f32[3,64,128]{2,1,0:T(8,128)S(1)} %get-tuple-element.88), channel_id=1, source_target_pairs={{0,1},{1,0},{2,3},{3,2},{4,5},{5,4},{6,7},{7,6},{8,9},{9,8},{10,11... | collective-permute-start | bytes 294920 | tf_op jit(solution)/shard_map/ppermute | solution.py:785
  15.1 10.6 %collective-permute-start.3 = (f32[3,128,128]{2,1,0:T(8,128)S(1)}, f32[3,128,128]{2,1,0:T(8,128)S(1)}, u32[]{:S(2)}, u32[]{:S(2)}) collective-permute-start(f32[3,128,128]{2,1,0:T(8,128)S(1)} %get-tuple-element.92), channel_id=1, source_target_pairs={{1,2},{3,4},{5,6},{7,8},{9,10},{11,12},{13,14},{2,1},{4,3},{6,5},{... | collective-permute-start | bytes 589832 | tf_op jit(solution)/shard_map/ppermute | solution.py:784
  20.4 10.8 %collective-permute-start.6 = (f32[3,128,128]{2,1,0:T(8,128)S(1)}, f32[3,128,128]{2,1,0:T(8,128)S(1)}, u32[]{:S(2)}, u32[]{:S(2)}) collective-permute-start(f32[3,128,128]{2,1,0:T(8,128)S(1)} %get-tuple-element.101), channel_id=1, source_target_pairs={{1,2},{3,4},{5,6},{7,8},{9,10},{11,12},{13,14},{2,1},{4,3},{6,5},{... | collective-permute-start | bytes 589832 | tf_op jit(solution)/shard_map/ppermute | solution.py:815
  25.1 1.4 %collective-permute-start.4 = (f32[3,64,128]{2,1,0:T(8,128)S(1)}, f32[3,64,128]{2,1,0:T(8,128)S(1)}, u32[]{:S(2)}, u32[]{:S(2)}) collective-permute-start(f32[3,64,128]{2,1,0:T(8,128)S(1)} %get-tuple-element.96), channel_id=1, source_target_pairs={{0,1},{1,0},{2,3},{3,2},{4,5},{5,4},{6,7},{7,6},{8,9},{9,8},{10,11... | collective-permute-start | bytes 294920 | tf_op jit(solution)/shard_map/ppermute | solution.py:835
  25.2 1.4 %collective-permute-start.5 = (f32[3,64,128]{2,1,0:T(8,128)S(1)}, f32[3,64,128]{2,1,0:T(8,128)S(1)}, u32[]{:S(2)}, u32[]{:S(2)}) collective-permute-start(f32[3,64,128]{2,1,0:T(8,128)S(1)} %get-tuple-element.97), channel_id=1, source_target_pairs={{0,1},{1,0},{2,3},{3,2},{4,5},{5,4},{6,7},{7,6},{8,9},{9,8},{10,11... | collective-permute-start | bytes 294920 | tf_op jit(solution)/shard_map/ppermute | solution.py:835
  27.5 6.8 %collective-permute-start.7 = (f32[3,64,128]{2,1,0:T(8,128)S(1)}, f32[3,64,128]{2,1,0:T(8,128)S(1)}, u32[]{:S(2)}, u32[]{:S(2)}) collective-permute-start(f32[3,64,128]{2,1,0:T(8,128)S(1)} %get-tuple-element.106), channel_id=1, source_target_pairs={{0,1},{1,0},{2,3},{3,2},{4,5},{5,4},{6,7},{7,6},{8,9},{9,8},{10,11... | collective-permute-start | bytes 294920 | tf_op jit(solution)/shard_map/ppermute | solution.py:835
  27.8 6.5 %collective-permute-start.8 = (f32[3,64,128]{2,1,0:T(8,128)S(1)}, f32[3,64,128]{2,1,0:T(8,128)S(1)}, u32[]{:S(2)}, u32[]{:S(2)}) collective-permute-start(f32[3,64,128]{2,1,0:T(8,128)S(1)} %get-tuple-element.107), channel_id=1, source_target_pairs={{0,1},{1,0},{2,3},{3,2},{4,5},{5,4},{6,7},{7,6},{8,9},{9,8},{10,11... | collective-permute-start | bytes 294920 | tf_op jit(solution)/shard_map/ppermute | solution.py:835
  28.0 9.1 %collective-permute-start.9 = (f32[3,128,128]{2,1,0:T(8,128)S(1)}, f32[3,128,128]{2,1,0:T(8,128)S(1)}, u32[]{:S(2)}, u32[]{:S(2)}) collective-permute-start(f32[3,128,128]{2,1,0:T(8,128)S(1)} %get-tuple-element.111), channel_id=1, source_target_pairs={{1,2},{3,4},{5,6},{7,8},{9,10},{11,12},{13,14},{2,1},{4,3},{6,5},{... | collective-permute-start | bytes 589832 | tf_op jit(solution)/shard_map/ppermute | solution.py:852
  31.9 10.5 %collective-permute-start.12 = (f32[3,128,128]{2,1,0:T(8,128)S(1)}, f32[3,128,128]{2,1,0:T(8,128)S(1)}, u32[]{:S(2)}, u32[]{:S(2)}) collective-permute-start(f32[3,128,128]{2,1,0:T(8,128)S(1)} %get-tuple-element.121), channel_id=1, source_target_pairs={{1,2},{3,4},{5,6},{7,8},{9,10},{11,12},{13,14},{2,1},{4,3},{6,5},{... | collective-permute-start | bytes 589832 | tf_op jit(solution)/shard_map/ppermute | solution.py:852
  35.2 2.6 %collective-permute-start.10 = (f32[3,64,128]{2,1,0:T(8,128)S(1)}, f32[3,64,128]{2,1,0:T(8,128)S(1)}, u32[]{:S(2)}, u32[]{:S(2)}) collective-permute-start(f32[3,64,128]{2,1,0:T(8,128)S(1)} %get-tuple-element.116), channel_id=1, source_target_pairs={{0,1},{1,0},{2,3},{3,2},{4,5},{5,4},{6,7},{7,6},{8,9},{9,8},{10,11... | collective-permute-start | bytes 294920 | tf_op jit(solution)/shard_map/ppermute | solution.py:835
  36.3 1.4 %collective-permute-start.11 = (f32[3,64,128]{2,1,0:T(8,128)S(1)}, f32[3,64,128]{2,1,0:T(8,128)S(1)}, u32[]{:S(2)}, u32[]{:S(2)}) collective-permute-start(f32[3,64,128]{2,1,0:T(8,128)S(1)} %get-tuple-element.117), channel_id=1, source_target_pairs={{0,1},{1,0},{2,3},{3,2},{4,5},{5,4},{6,7},{7,6},{8,9},{9,8},{10,11... | collective-permute-start | bytes 294920 | tf_op jit(solution)/shard_map/ppermute | solution.py:835
  38.6 6.8 %collective-permute-start.13 = (f32[3,64,128]{2,1,0:T(8,128)S(1)}, f32[3,64,128]{2,1,0:T(8,128)S(1)}, u32[]{:S(2)}, u32[]{:S(2)}) collective-permute-start(f32[3,64,128]{2,1,0:T(8,128)S(1)} %get-tuple-element.126), channel_id=1, source_target_pairs={{0,1},{1,0},{2,3},{3,2},{4,5},{5,4},{6,7},{7,6},{8,9},{9,8},{10,11... | collective-permute-start | bytes 294920 | tf_op jit(solution)/shard_map/ppermute | solution.py:835
  38.7 6.8 %collective-permute-start.14 = (f32[3,64,128]{2,1,0:T(8,128)S(1)}, f32[3,64,128]{2,1,0:T(8,128)S(1)}, u32[]{:S(2)}, u32[]{:S(2)}) collective-permute-start(f32[3,64,128]{2,1,0:T(8,128)S(1)} %get-tuple-element.127), channel_id=1, source_target_pairs={{0,1},{1,0},{2,3},{3,2},{4,5},{5,4},{6,7},{7,6},{8,9},{9,8},{10,11... | collective-permute-start | bytes 294920 | tf_op jit(solution)/shard_map/ppermute | solution.py:835
  39.2 9.1 %collective-permute-start.15 = (f32[3,128,128]{2,1,0:T(8,128)S(1)}, f32[3,128,128]{2,1,0:T(8,128)S(1)}, u32[]{:S(2)}, u32[]{:S(2)}) collective-permute-start(f32[3,128,128]{2,1,0:T(8,128)S(1)} %get-tuple-element.131), channel_id=1, source_target_pairs={{1,2},{3,4},{5,6},{7,8},{9,10},{11,12},{13,14},{2,1},{4,3},{6,5},{... | collective-permute-start | bytes 589832 | tf_op jit(solution)/shard_map/ppermute | solution.py:852
  43.1 9.4 %collective-permute-start.18 = (f32[3,128,128]{2,1,0:T(8,128)S(1)}, f32[3,128,128]{2,1,0:T(8,128)S(1)}, u32[]{:S(2)}, u32[]{:S(2)}) collective-permute-start(f32[3,128,128]{2,1,0:T(8,128)S(1)} %get-tuple-element.141), channel_id=1, source_target_pairs={{1,2},{3,4},{5,6},{7,8},{9,10},{11,12},{13,14},{2,1},{4,3},{6,5},{... | collective-permute-start | bytes 589832 | tf_op jit(solution)/shard_map/ppermute | solution.py:852
  46.3 2.4 %collective-permute-start.16 = (f32[3,64,128]{2,1,0:T(8,128)S(1)}, f32[3,64,128]{2,1,0:T(8,128)S(1)}, u32[]{:S(2)}, u32[]{:S(2)}) collective-permute-start(f32[3,64,128]{2,1,0:T(8,128)S(1)} %get-tuple-element.136), channel_id=1, source_target_pairs={{0,1},{1,0},{2,3},{3,2},{4,5},{5,4},{6,7},{7,6},{8,9},{9,8},{10,11... | collective-permute-start | bytes 294920 | tf_op jit(solution)/shard_map/ppermute | solution.py:835
  47.3 1.5 %collective-permute-start.17 = (f32[3,64,128]{2,1,0:T(8,128)S(1)}, f32[3,64,128]{2,1,0:T(8,128)S(1)}, u32[]{:S(2)}, u32[]{:S(2)}) collective-permute-start(f32[3,64,128]{2,1,0:T(8,128)S(1)} %get-tuple-element.137), channel_id=1, source_target_pairs={{0,1},{1,0},{2,3},{3,2},{4,5},{5,4},{6,7},{7,6},{8,9},{9,8},{10,11... | collective-permute-start | bytes 294920 | tf_op jit(solution)/shard_map/ppermute | solution.py:835

commit v14 on v13

--- a/solution.py
+++ b/solution.py
@@ -14,7 +14,6 @@
 DT = 0.25
 PAD = 8
 ROWS = 16
-UNROLL = 8
 VMEM_LIMIT = 32 * 1024 * 1024
 
 C_B, C_B0, C_B1, C_M0, C_M1, C_LAM, C_MU2, C_MU, C_K1, C_K2, C_K2H, C_L0 = range(12)
@@ -41,7 +40,7 @@
         work(pl.multiple_of(first + i * ROWS, ROWS))
         return carry
 
-    lax.fori_loop(0, count // ROWS, step, 0, unroll=UNROLL)
+    lax.fori_loop(0, count // ROWS, step, 0, unroll=count // ROWS)
 
 
 def coefs(coef_ref, ids):

time: 54.1 us -> 52.4 us (0.969)
  Pallas kernels: 14.5 us -> 11 us
  waiting for transfers between devices: 7.79 us -> 9.25 us
    pallas_call x17, Pallas kernels: 14.5 us -> 11 us  [call(): pl.pallas_call(kernel, out_shape=outs, in_specs=specs, out_specs=out_spec...]
    ppermute x4, starting transfers between devices: 11.2 us -> 12.5 us  [body(): early = lax.ppermute(msg[0], 'line', far)]
    ppermute x10, starting transfers between devices: 3.92 us -> 2.89 us  [body(): msg_near = [lax.ppermute(plane, 'line', near) for plane in msg]]
    ppermute x4, waiting for transfers between devices: 4.1 us -> 5.11 us  [body(): early = lax.ppermute(msg[0], 'line', far)]
  transfers between devices with their start and end apart: 20 -> 20, of which waited for: 7 -> 7; matrix products, arithmetic and copies ran while one was open for 0% -> 0% of each run, Pallas kernels for 22% -> 16%
where the time goes in v14:
time: 52.4 us; the launch traced here: 51.9 us
  starting transfers between devices  30.7 us (59%)
  Pallas kernels  11 us (21%)
  waiting for transfers between devices  9.25 us (18%)
  between operations  0.9 us (2%)
    ppermute x4, starting transfers between devices, body(): early = lax.ppermute(msg[0], 'line', far)  12.5 us
    pallas_call x17, Pallas kernels, call(): pl.pallas_call(kernel, out_shape=outs, in_specs=specs, out_specs=out_spec...  11 us
    all_to_all x1, starting transfers between devices, body(): lax.all_to_all(parts, 'line', 0, 0, axis_index_groups=groups, tiled=True)  6.3 us
    ppermute x4, waiting for transfers between devices, body(): early = lax.ppermute(msg[0], 'line', far)  5.11 us
    ppermute x1, starting transfers between devices, body(): early = lax.ppermute(early, 'line', far)  3.74 us
    ppermute x1, starting transfers between devices, body(): msg_far = lax.ppermute(msg_far, 'line', far)  3.53 us
    ppermute x10, starting transfers between devices, body(): msg_near = [lax.ppermute(plane, 'line', near) for plane in msg]  2.89 us
    ppermute x1, waiting for transfers between devices, ahead_by(): lax.ppermute(x, 'line', [(i, i + distance) for i in range(tiles - distanc...  2.85 us
  transfers between devices with their start and end apart: 20, of which 7 were waited for; matrix products, arithmetic and copies ran while one was open for 0% of the time, Pallas kernels for 16%

profile of v14, /device:TPU:17, one launch (start us, length us, event | category | flops | bytes accessed | tf_op | source)
XLA Modules:
  0.0 51.9 jit_solution(3316485015280826640)
XLA Ops:
  0.6 0.9 %pack.1 = (f32[8,1920]{1,0:T(8,128)S(1)}, f32[16,128]{1,0:T(8,128)S(1)}, f32[16,128]{1,0:T(8,128)S(1)}, s32[1,8]{1,0:T(1,128)S(1)}) custom-call(f32[8,1536]{1,0:T(8,128)} %bitcast.3, f32[16,128]{1,0:T(8,128)} %loads_in.1, s32[6,16]{1,0:T(8,128)} %entries_in.1, s32[6,16]{1,0:T(8,128)} %cells_in.1, s32[1,8]{1,0:T(1,128)} %bitcast.4), custom_call_target="tpu_custom_call" | custom-call | flops 1 | bytes 1 | tf_op jit(solution)/shard_map/pack/pallas_call | solution.py:703
  1.5 1.3 %collective-permute-start = (f32[8,1920]{1,0:T(8,128)S(1)}, f32[8,1920]{1,0:T(8,128)S(1)}, u32[]{:S(2)}, u32[]{:S(2)}) collective-permute-start(f32[8,1920]{1,0:T(8,128)S(1)} %get-tuple-element.81.own), channel_id=1, source_target_pairs={{0,8},{1,9},{2,10},{3,11},{4,12},{5,13},{6,14},{7,15},{16,24},{17,... | collective-permute-start | bytes 184328 | tf_op jit(solution)/shard_map/ppermute | solution.py:741
  2.8 1.8 %start.1 = (f32[3,2,144,128]{3,2,1,0:T(8,128)S(1)}, f32[6,2,144,128]{3,2,1,0:T(8,128)S(1)}, f32[6,2,128,128]{3,2,1,0:T(8,128)S(1)}, f32[16,128]{1,0:T(8,128)S(1)...) custom-call(f32[3,2,128,128]{3,2,1,0:T(8,128)} %velocity.1, ...), custom_call_target="tpu_custom_call" | custom-call | flops 8388608 | bytes 8388608 | tf_op jit(solution)/shard_map/start/pallas_call | solution.py:703
  4.6 2.8 %collective-permute-done.behind = f32[8,1920]{1,0:T(8,128)S(1)} collective-permute-done((f32[8,1920]{1,0:T(8,128)S(1)}, f32[8,1920]{1,0:T(8,128)S(1)}, u32[]{:S(2)}, u32[]{:S(2)}) %collective-permute-start) | collective-permute-done | bytes 61472 | tf_op jit(solution)/shard_map/ppermute | solution.py:741
  7.4 0.9 %split.1 = f32[8,56,128]{2,1,0:T(8,128)} custom-call(f32[8,1920]{1,0:T(8,128)S(1)} %get-tuple-element.81.own, f32[8,1920]{1,0:T(8,128)S(1)} %collective-permute-done.behind, s32[1,8]{1,0:T(1,128)S(1)} %get-tuple-element.82.cells, f32[16,128]{1,0:T(8,128)S(1)} %get-tuple-element.80.after_this.coef_ref), custom_call_target="tpu_custom_call" | custom-call | flops 1 | bytes 1 | tf_op jit(solution)/shard_map/split/pallas_call | solution.py:703
  8.3 6.3 %all-to-all-start = ((f32[8,56,128]{2,1,0:T(8,128)}), f32[8,56,128]{2,1,0:T(8,128)S(1)}, u32[]{:S(2)}, u32[]{:S(2)}) async-start(f32[8,56,128]{2,1,0:T(8,128)} %split.1), calls=%async_computation | async-start | bytes 458752 | tf_op jit(solution)/shard_map/all_to_all | solution.py:794
  14.6 0.0 collective-permute-start.1
  14.6 0.5 collective-permute-start.2
  15.1 3.5 %collective-permute-start.3 = (f32[3,128,128]{2,1,0:T(8,128)S(1)}, f32[3,128,128]{2,1,0:T(8,128)S(1)}, u32[]{:S(2)}, u32[]{:S(2)}) collective-permute-start(f32[3,128,128]{2,1,0:T(8,128)S(1)} %get-tuple-element.92), channel_id=1, source_target_pairs={{1,2},{3,4},{5,6},{7,8},{9,10},{11,12},{13,14},{2,1},{4,3},{6,5},{... | collective-permute-start | bytes 589832 | tf_op jit(solution)/shard_map/ppermute | solution.py:783
  18.6 0.9 %all-to-all-done.parts = f32[8,56,128]{2,1,0:T(8,128)S(1)} async-done(((f32[8,56,128]{2,1,0:T(8,128)}), f32[8,56,128]{2,1,0:T(8,128)S(1)}, u32[]{:S(2)}, u32[]{:S(2)}) %all-to-all-start) | async-done | bytes 229408 | tf_op jit(solution)/shard_map/all_to_all | solution.py:794
  19.6 0.6 %prepare.1 = (f32[6,3,3,16,128]{4,3,2,1,0:T(8,128)S(1)}, f32[128,128]{1,0:T(8,128)S(1)}) custom-call(f32[8,56,128]{2,1,0:T(8,128)S(1)} %all-to-all-done.parts, f32[16,128]{1,0:T(8,128)S(1)} %get-tuple-element.83.loads, f32[16,128]{1,0:T(8,128)S(1)} %get-tuple-element.76.after_this.steps_table), custom_call_target="tpu_custom_call" | custom-call | flops 1 | bytes 1 | tf_op jit(solution)/shard_map/prepare/pallas_call | solution.py:703
  20.2 0.3 first.1
  20.4 3.7 %collective-permute-start.6 = (f32[3,128,128]{2,1,0:T(8,128)S(1)}, f32[3,128,128]{2,1,0:T(8,128)S(1)}, u32[]{:S(2)}, u32[]{:S(2)}) collective-permute-start(f32[3,128,128]{2,1,0:T(8,128)S(1)} %get-tuple-element.101), channel_id=1, source_target_pairs={{1,2},{3,4},{5,6},{7,8},{9,10},{11,12},{13,14},{2,1},{4,3},{6,5},{... | collective-permute-start | bytes 589832 | tf_op jit(solution)/shard_map/ppermute | solution.py:814
  24.2 0.0 collective-permute-done.2.lower
  24.2 0.3 near0.1
  24.5 0.1 collective-permute-start.4
  24.6 0.5 collective-permute-start.5
  25.1 0.6 %far0.1 = (f32[3,2,144,128]{3,2,1,0:T(8,128)S(1)}, f32[6,2,144,128]{3,2,1,0:T(8,128)S(1)}, f32[6,2,128,128]{3,2,1,0:T(8,128)S(1)}, f32[3,128,128]{2,1,0:T(8,128)S(1)}, f32[3,128,128]{2,1,0:T(8,128)S(1)}) custom-call(f32[3,2,144,128]{3,2,1,0:T(8,128)S(1)} %get-tuple-element.89.V0, ...), custom_call_target="tpu_custom_call", output_to_operand_aliasing={{0}: (0, {}), {1}: (1, {}), {2}: (2, {})} | custom-call | flops 1 | bytes 1 | tf_op jit(solution)/shard_map/far0/pallas_call | solution.py:703
  25.7 0.2 collective-permute-done.4.upper
  25.9 0.2 collective-permute-done.5.lower
  26.0 0.2 near1.1
  26.3 0.4 collective-permute-start.7
  26.7 0.2 collective-permute-start.8
  26.9 3.3 %collective-permute-start.9 = (f32[3,128,128]{2,1,0:T(8,128)S(1)}, f32[3,128,128]{2,1,0:T(8,128)S(1)}, u32[]{:S(2)}, u32[]{:S(2)}) collective-permute-start(f32[3,128,128]{2,1,0:T(8,128)S(1)} %get-tuple-element.111), channel_id=1, source_target_pairs={{1,2},{3,4},{5,6},{7,8},{9,10},{11,12},{13,14},{2,1},{4,3},{6,5},{... | collective-permute-start | bytes 589832 | tf_op jit(solution)/shard_map/ppermute | solution.py:851
  30.1 0.0 collective-permute-done.6.msg
  30.2 0.6 %far1.1 = (f32[3,2,144,128]{3,2,1,0:T(8,128)S(1)}, f32[6,2,144,128]{3,2,1,0:T(8,128)S(1)}, f32[6,2,128,128]{3,2,1,0:T(8,128)S(1)}, f32[3,128,128]{2,1,0:T(8,128)S(1)}, f32[3,128,128]{2,1,0:T(8,128)S(1)}) custom-call(f32[3,2,144,128]{3,2,1,0:T(8,128)S(1)} %get-tuple-element.98.V0, ...), custom_call_target="tpu_custom_call", output_to_operand_aliasing={{0}: (0, {}), {1}: (1, {}), {2}: (2, {})} | custom-call | flops 1 | bytes 1 | tf_op jit(solution)/shard_map/far1/pallas_call | solution.py:703
  30.8 3.2 %collective-permute-start.12 = (f32[3,128,128]{2,1,0:T(8,128)S(1)}, f32[3,128,128]{2,1,0:T(8,128)S(1)}, u32[]{:S(2)}, u32[]{:S(2)}) collective-permute-start(f32[3,128,128]{2,1,0:T(8,128)S(1)} %get-tuple-element.121), channel_id=1, source_target_pairs={{1,2},{3,4},{5,6},{7,8},{9,10},{11,12},{13,14},{2,1},{4,3},{6,5},{... | collective-permute-start | bytes 589832 | tf_op jit(solution)/shard_map/ppermute | solution.py:851
  34.0 0.0 collective-permute-done.7.upper
  34.0 0.3 near2.1
  34.3 0.3 collective-permute-start.10
  34.6 0.2 collective-permute-start.11
  34.8 1.1 %collective-permute-done.9.msg = f32[3,128,128]{2,1,0:T(8,128)S(1)} collective-permute-done((f32[3,128,128]{2,1,0:T(8,128)S(1)}, f32[3,128,128]{2,1,0:T(8,128)S(1)}, u32[]{:S(2)}, u32[]{:S(2)}) %collective-permute-start.9) | collective-permute-done | bytes 196640 | tf_op jit(solution)/shard_map/ppermute | solution.py:851
  35.9 0.6 %far2.1 = (f32[3,2,144,128]{3,2,1,0:T(8,128)S(1)}, f32[6,2,144,128]{3,2,1,0:T(8,128)S(1)}, f32[6,2,128,128]{3,2,1,0:T(8,128)S(1)}, f32[3,128,128]{2,1,0:T(8,128)S(1)}, f32[3,128,128]{2,1,0:T(8,128)S(1)}) custom-call(f32[3,2,144,128]{3,2,1,0:T(8,128)S(1)} %get-tuple-element.108.V0, ...), custom_call_target="tpu_custom_call", output_to_operand_aliasing={{0}: (0, {}), {1}: (1, {}), {2}: (2, {})} | custom-call | flops 1 | bytes 1 | tf_op jit(solution)/shard_map/far2/pallas_call | solution.py:703
  36.6 0.0 collective-permute-done.10.upper
  36.6 0.3 near3.1
  36.9 0.1 collective-permute-start.13
  36.9 0.5 collective-permute-start.14
  37.4 3.3 %collective-permute-start.15 = (f32[3,128,128]{2,1,0:T(8,128)S(1)}, f32[3,128,128]{2,1,0:T(8,128)S(1)}, u32[]{:S(2)}, u32[]{:S(2)}) collective-permute-start(f32[3,128,128]{2,1,0:T(8,128)S(1)} %get-tuple-element.131), channel_id=1, source_target_pairs={{1,2},{3,4},{5,6},{7,8},{9,10},{11,12},{13,14},{2,1},{4,3},{6,5},{... | collective-permute-start | bytes 589832 | tf_op jit(solution)/shard_map/ppermute | solution.py:851
  40.7 0.6 %far3.1 = (f32[3,2,144,128]{3,2,1,0:T(8,128)S(1)}, f32[6,2,144,128]{3,2,1,0:T(8,128)S(1)}, f32[6,2,128,128]{3,2,1,0:T(8,128)S(1)}, f32[3,128,128]{2,1,0:T(8,128)S(1)}, f32[3,128,128]{2,1,0:T(8,128)S(1)}) custom-call(f32[3,2,144,128]{3,2,1,0:T(8,128)S(1)} %get-tuple-element.118.V0, ...), custom_call_target="tpu_custom_call", output_to_operand_aliasing={{0}: (0, {}), {1}: (1, {}), {2}: (2, {})} | custom-call | flops 1 | bytes 1 | tf_op jit(solution)/shard_map/far3/pallas_call | solution.py:703
  41.4 2.7 %collective-permute-start.18 = (f32[3,128,128]{2,1,0:T(8,128)S(1)}, f32[3,128,128]{2,1,0:T(8,128)S(1)}, u32[]{:S(2)}, u32[]{:S(2)}) collective-permute-start(f32[3,128,128]{2,1,0:T(8,128)S(1)} %get-tuple-element.141), channel_id=1, source_target_pairs={{1,2},{3,4},{5,6},{7,8},{9,10},{11,12},{13,14},{2,1},{4,3},{6,5},{... | collective-permute-start | bytes 589832 | tf_op jit(solution)/shard_map/ppermute | solution.py:851
  44.1 0.3 near4.1
  44.4 0.5 %collective-permute-start.16 = (f32[3,64,128]{2,1,0:T(8,128)S(1)}, f32[3,64,128]{2,1,0:T(8,128)S(1)}, u32[]{:S(2)}, u32[]{:S(2)}) collective-permute-start(f32[3,64,128]{2,1,0:T(8,128)S(1)} %get-tuple-element.136), channel_id=1, source_target_pairs={{0,1},{1,0},{2,3},{3,2},{4,5},{5,4},{6,7},{7,6},{8,9},{9,8},{10,11... | collective-permute-start | bytes 294920 | tf_op jit(solution)/shard_map/ppermute | solution.py:834
  44.9 0.1 collective-permute-start.17
  45.0 1.5 %collective-permute-done.15.msg = f32[3,128,128]{2,1,0:T(8,128)S(1)} collective-permute-done((f32[3,128,128]{2,1,0:T(8,128)S(1)}, f32[3,128,128]{2,1,0:T(8,128)S(1)}, u32[]{:S(2)}, u32[]{:S(2)}) %collective-permute-start.15) | collective-permute-done | bytes 196640 | tf_op jit(solution)/shard_map/ppermute | solution.py:851
  46.5 0.4 far4.1
  47.0 1.2 %near5.1 = (f32[3,2,144,128]{3,2,1,0:T(8,128)S(1)}, f32[6,2,144,128]{3,2,1,0:T(8,128)S(1)}, f32[6,2,128,128]{3,2,1,0:T(8,128)S(1)}, f32[3,2,128,128]{3,2,1,0:T(8...) custom-call(f32[3,2,144,128]{3,2,1,0:T(8,128)S(1)} %get-tuple-elemen, ...), custom_call_target="tpu_custom_call", output_to_operand_aliasing={{0}: (0, {}), {1}: (1, {}), {2}: (2, {})} | custom-call | flops 1 | bytes 1 | tf_op jit(solution)/shard_map/near5/pallas_call | solution.py:703
  48.2 2.5 %collective-permute-done.18.msg = f32[3,128,128]{2,1,0:T(8,128)S(1)} collective-permute-done((f32[3,128,128]{2,1,0:T(8,128)S(1)}, f32[3,128,128]{2,1,0:T(8,128)S(1)}, u32[]{:S(2)}, u32[]{:S(2)}) %collective-permute-start.18) | collective-permute-done | bytes 196640 | tf_op jit(solution)/shard_map/ppermute | solution.py:851
  50.7 1.2 %last.1 = (f32[3,2,144,128]{3,2,1,0:T(8,128)S(1)}, f32[6,2,144,128]{3,2,1,0:T(8,128)S(1)}, f32[6,2,128,128]{3,2,1,0:T(8,128)S(1)}, f32[3,2,128,128]{3,2,1,0:T(8,...) custom-call(f32[3,2,144,128]{3,2,1,0:T(8,128)S(1)} %get-tuple-elemen, ...), custom_call_target="tpu_custom_call", output_to_operand_aliasing={{0}: (0, {}), {1}: (1, {}), {2}: (2, {}), {3}: (8, {}), {4}... | custom-call | flops 1 | bytes 1 | tf_op jit(solution)/shard_map/last/pallas_call | solution.py:703
  (9 shorter events, 0.0 us)
Async XLA Ops:
  1.5 5.9 %collective-permute-start = (f32[8,1920]{1,0:T(8,128)S(1)}, f32[8,1920]{1,0:T(8,128)S(1)}, u32[]{:S(2)}, u32[]{:S(2)}) collective-permute-start(f32[8,1920]{1,0:T(8,128)S(1)} %get-tuple-element.81.own), channel_id=1, source_target_pairs={{0,8},{1,9},{2,10},{3,11},{4,12},{5,13},{6,14},{7,15},{16,24},{17,... | collective-permute-start | bytes 184328 | tf_op jit(solution)/shard_map/ppermute | solution.py:741
  8.3 11.3 %all-to-all-start = ((f32[8,56,128]{2,1,0:T(8,128)}), f32[8,56,128]{2,1,0:T(8,128)S(1)}, u32[]{:S(2)}, u32[]{:S(2)}) async-start(f32[8,56,128]{2,1,0:T(8,128)} %split.1), calls=%async_computation | async-start | bytes 458752 | tf_op jit(solution)/shard_map/all_to_all | solution.py:794
  14.6 9.6 %collective-permute-start.1 = (f32[3,64,128]{2,1,0:T(8,128)S(1)}, f32[3,64,128]{2,1,0:T(8,128)S(1)}, u32[]{:S(2)}, u32[]{:S(2)}) collective-permute-start(f32[3,64,128]{2,1,0:T(8,128)S(1)} %get-tuple-element.87), channel_id=1, source_target_pairs={{0,1},{1,0},{2,3},{3,2},{4,5},{5,4},{6,7},{7,6},{8,9},{9,8},{10,11... | collective-permute-start | bytes 294920 | tf_op jit(solution)/shard_map/ppermute | solution.py:784
  14.6 9.6 %collective-permute-start.2 = (f32[3,64,128]{2,1,0:T(8,128)S(1)}, f32[3,64,128]{2,1,0:T(8,128)S(1)}, u32[]{:S(2)}, u32[]{:S(2)}) collective-permute-start(f32[3,64,128]{2,1,0:T(8,128)S(1)} %get-tuple-element.88), channel_id=1, source_target_pairs={{0,1},{1,0},{2,3},{3,2},{4,5},{5,4},{6,7},{7,6},{8,9},{9,8},{10,11... | collective-permute-start | bytes 294920 | tf_op jit(solution)/shard_map/ppermute | solution.py:784
  15.1 10.0 %collective-permute-start.3 = (f32[3,128,128]{2,1,0:T(8,128)S(1)}, f32[3,128,128]{2,1,0:T(8,128)S(1)}, u32[]{:S(2)}, u32[]{:S(2)}) collective-permute-start(f32[3,128,128]{2,1,0:T(8,128)S(1)} %get-tuple-element.92), channel_id=1, source_target_pairs={{1,2},{3,4},{5,6},{7,8},{9,10},{11,12},{13,14},{2,1},{4,3},{6,5},{... | collective-permute-start | bytes 589832 | tf_op jit(solution)/shard_map/ppermute | solution.py:783
  20.4 9.7 %collective-permute-start.6 = (f32[3,128,128]{2,1,0:T(8,128)S(1)}, f32[3,128,128]{2,1,0:T(8,128)S(1)}, u32[]{:S(2)}, u32[]{:S(2)}) collective-permute-start(f32[3,128,128]{2,1,0:T(8,128)S(1)} %get-tuple-element.101), channel_id=1, source_target_pairs={{1,2},{3,4},{5,6},{7,8},{9,10},{11,12},{13,14},{2,1},{4,3},{6,5},{... | collective-permute-start | bytes 589832 | tf_op jit(solution)/shard_map/ppermute | solution.py:814
  24.5 1.4 %collective-permute-start.4 = (f32[3,64,128]{2,1,0:T(8,128)S(1)}, f32[3,64,128]{2,1,0:T(8,128)S(1)}, u32[]{:S(2)}, u32[]{:S(2)}) collective-permute-start(f32[3,64,128]{2,1,0:T(8,128)S(1)} %get-tuple-element.96), channel_id=1, source_target_pairs={{0,1},{1,0},{2,3},{3,2},{4,5},{5,4},{6,7},{7,6},{8,9},{9,8},{10,11... | collective-permute-start | bytes 294920 | tf_op jit(solution)/shard_map/ppermute | solution.py:834
  24.6 1.4 %collective-permute-start.5 = (f32[3,64,128]{2,1,0:T(8,128)S(1)}, f32[3,64,128]{2,1,0:T(8,128)S(1)}, u32[]{:S(2)}, u32[]{:S(2)}) collective-permute-start(f32[3,64,128]{2,1,0:T(8,128)S(1)} %get-tuple-element.97), channel_id=1, source_target_pairs={{0,1},{1,0},{2,3},{3,2},{4,5},{5,4},{6,7},{7,6},{8,9},{9,8},{10,11... | collective-permute-start | bytes 294920 | tf_op jit(solution)/shard_map/ppermute | solution.py:834
  26.3 7.7 %collective-permute-start.7 = (f32[3,64,128]{2,1,0:T(8,128)S(1)}, f32[3,64,128]{2,1,0:T(8,128)S(1)}, u32[]{:S(2)}, u32[]{:S(2)}) collective-permute-start(f32[3,64,128]{2,1,0:T(8,128)S(1)} %get-tuple-element.106), channel_id=1, source_target_pairs={{0,1},{1,0},{2,3},{3,2},{4,5},{5,4},{6,7},{7,6},{8,9},{9,8},{10,11... | collective-permute-start | bytes 294920 | tf_op jit(solution)/shard_map/ppermute | solution.py:834
  26.7 7.3 %collective-permute-start.8 = (f32[3,64,128]{2,1,0:T(8,128)S(1)}, f32[3,64,128]{2,1,0:T(8,128)S(1)}, u32[]{:S(2)}, u32[]{:S(2)}) collective-permute-start(f32[3,64,128]{2,1,0:T(8,128)S(1)} %get-tuple-element.107), channel_id=1, source_target_pairs={{0,1},{1,0},{2,3},{3,2},{4,5},{5,4},{6,7},{7,6},{8,9},{9,8},{10,11... | collective-permute-start | bytes 294920 | tf_op jit(solution)/shard_map/ppermute | solution.py:834
  26.9 9.1 %collective-permute-start.9 = (f32[3,128,128]{2,1,0:T(8,128)S(1)}, f32[3,128,128]{2,1,0:T(8,128)S(1)}, u32[]{:S(2)}, u32[]{:S(2)}) collective-permute-start(f32[3,128,128]{2,1,0:T(8,128)S(1)} %get-tuple-element.111), channel_id=1, source_target_pairs={{1,2},{3,4},{5,6},{7,8},{9,10},{11,12},{13,14},{2,1},{4,3},{6,5},{... | collective-permute-start | bytes 589832 | tf_op jit(solution)/shard_map/ppermute | solution.py:851
  30.8 9.9 %collective-permute-start.12 = (f32[3,128,128]{2,1,0:T(8,128)S(1)}, f32[3,128,128]{2,1,0:T(8,128)S(1)}, u32[]{:S(2)}, u32[]{:S(2)}) collective-permute-start(f32[3,128,128]{2,1,0:T(8,128)S(1)} %get-tuple-element.121), channel_id=1, source_target_pairs={{1,2},{3,4},{5,6},{7,8},{9,10},{11,12},{13,14},{2,1},{4,3},{6,5},{... | collective-permute-start | bytes 589832 | tf_op jit(solution)/shard_map/ppermute | solution.py:851
  34.3 2.3 %collective-permute-start.10 = (f32[3,64,128]{2,1,0:T(8,128)S(1)}, f32[3,64,128]{2,1,0:T(8,128)S(1)}, u32[]{:S(2)}, u32[]{:S(2)}) collective-permute-start(f32[3,64,128]{2,1,0:T(8,128)S(1)} %get-tuple-element.116), channel_id=1, source_target_pairs={{0,1},{1,0},{2,3},{3,2},{4,5},{5,4},{6,7},{7,6},{8,9},{9,8},{10,11... | collective-permute-start | bytes 294920 | tf_op jit(solution)/shard_map/ppermute | solution.py:834
  34.6 2.0 %collective-permute-start.11 = (f32[3,64,128]{2,1,0:T(8,128)S(1)}, f32[3,64,128]{2,1,0:T(8,128)S(1)}, u32[]{:S(2)}, u32[]{:S(2)}) collective-permute-start(f32[3,64,128]{2,1,0:T(8,128)S(1)} %get-tuple-element.117), channel_id=1, source_target_pairs={{0,1},{1,0},{2,3},{3,2},{4,5},{5,4},{6,7},{7,6},{8,9},{9,8},{10,11... | collective-permute-start | bytes 294920 | tf_op jit(solution)/shard_map/ppermute | solution.py:834
  36.9 7.3 %collective-permute-start.13 = (f32[3,64,128]{2,1,0:T(8,128)S(1)}, f32[3,64,128]{2,1,0:T(8,128)S(1)}, u32[]{:S(2)}, u32[]{:S(2)}) collective-permute-start(f32[3,64,128]{2,1,0:T(8,128)S(1)} %get-tuple-element.126), channel_id=1, source_target_pairs={{0,1},{1,0},{2,3},{3,2},{4,5},{5,4},{6,7},{7,6},{8,9},{9,8},{10,11... | collective-permute-start | bytes 294920 | tf_op jit(solution)/shard_map/ppermute | solution.py:834
  36.9 7.2 %collective-permute-start.14 = (f32[3,64,128]{2,1,0:T(8,128)S(1)}, f32[3,64,128]{2,1,0:T(8,128)S(1)}, u32[]{:S(2)}, u32[]{:S(2)}) collective-permute-start(f32[3,64,128]{2,1,0:T(8,128)S(1)} %get-tuple-element.127), channel_id=1, source_target_pairs={{0,1},{1,0},{2,3},{3,2},{4,5},{5,4},{6,7},{7,6},{8,9},{9,8},{10,11... | collective-permute-start | bytes 294920 | tf_op jit(solution)/shard_map/ppermute | solution.py:834
  37.4 9.1 %collective-permute-start.15 = (f32[3,128,128]{2,1,0:T(8,128)S(1)}, f32[3,128,128]{2,1,0:T(8,128)S(1)}, u32[]{:S(2)}, u32[]{:S(2)}) collective-permute-start(f32[3,128,128]{2,1,0:T(8,128)S(1)} %get-tuple-element.131), channel_id=1, source_target_pairs={{1,2},{3,4},{5,6},{7,8},{9,10},{11,12},{13,14},{2,1},{4,3},{6,5},{... | collective-permute-start | bytes 589832 | tf_op jit(solution)/shard_map/ppermute | solution.py:851
  41.4 9.3 %collective-permute-start.18 = (f32[3,128,128]{2,1,0:T(8,128)S(1)}, f32[3,128,128]{2,1,0:T(8,128)S(1)}, u32[]{:S(2)}, u32[]{:S(2)}) collective-permute-start(f32[3,128,128]{2,1,0:T(8,128)S(1)} %get-tuple-element.141), channel_id=1, source_target_pairs={{1,2},{3,4},{5,6},{7,8},{9,10},{11,12},{13,14},{2,1},{4,3},{6,5},{... | collective-permute-start | bytes 589832 | tf_op jit(solution)/shard_map/ppermute | solution.py:851
  44.4 2.5 %collective-permute-start.16 = (f32[3,64,128]{2,1,0:T(8,128)S(1)}, f32[3,64,128]{2,1,0:T(8,128)S(1)}, u32[]{:S(2)}, u32[]{:S(2)}) collective-permute-start(f32[3,64,128]{2,1,0:T(8,128)S(1)} %get-tuple-element.136), channel_id=1, source_target_pairs={{0,1},{1,0},{2,3},{3,2},{4,5},{5,4},{6,7},{7,6},{8,9},{9,8},{10,11... | collective-permute-start | bytes 294920 | tf_op jit(solution)/shard_map/ppermute | solution.py:834
  44.9 2.0 %collective-permute-start.17 = (f32[3,64,128]{2,1,0:T(8,128)S(1)}, f32[3,64,128]{2,1,0:T(8,128)S(1)}, u32[]{:S(2)}, u32[]{:S(2)}) collective-permute-start(f32[3,64,128]{2,1,0:T(8,128)S(1)} %get-tuple-element.137), channel_id=1, source_target_pairs={{0,1},{1,0},{2,3},{3,2},{4,5},{5,4},{6,7},{7,6},{8,9},{9,8},{10,11... | collective-permute-start | bytes 294920 | tf_op jit(solution)/shard_map/ppermute | solution.py:834

commit v15 on v10

--- a/solution.py
+++ b/solution.py
@@ -551,7 +551,7 @@
     return sum(lane_roll(table[s : s + 1, :], s * width) for s in range(STEPS))
 
 
-def split_kernel(panel, slots, own, behind, cells, after_this, out):
+def split_kernel(panel, slots, own, behind, cells, after_this, result, out, sems):
     del after_this
     tiles, _, lanes = out.shape
     pieces = panel // lanes
@@ -581,6 +581,7 @@
         blocks = [source[0:8, panel + i * lanes : panel + (i + 1) * lanes] for i in range(slots // 8 + 1)]
         return blocks[:-1], lane_blocks(blocks[-1], slots)
 
+    copies = []
     own_rows, own_entry = trucks(own)
     far_rows, far_entry = trucks(behind)
     for tile in range(tiles):
@@ -592,6 +593,10 @@
         for i in range(slots // 8):
             at = TRUCK_ROW + 8 * i
             out[tile, at : at + 8, :] = jnp.where(passed, own_rows[i], far_rows[i])
+        copies.append(pltpu.make_async_copy(out.at[tile], result.at[tile], sems.at[tile]))
+        copies[-1].start()
+    for copy in copies:
+        copy.wait()
 
 
 def prepare_kernel(parts, loads, steps_table, force, surface, table, rows_out):
@@ -607,31 +612,38 @@
                 panel = parts[s, pl.ds(comp * per * width + cell, per, stride=width), :]
                 force[s, comp, cell, pl.ds(4, per, stride=2), :] = scale * panel
                 force[s, comp, cell, pl.ds(5, per, stride=2), :] = scale * lane_roll(panel, FZ)
-
+    surface_loads(1, parts, loads, steps_table, surface, table, rows_out)
+
+
+def surface_kernel(parts, loads, steps_table, surface, table, rows_out):
+    surface_loads(STEPS, parts, loads, steps_table, surface, table, rows_out)
+
+
+def surface_loads(steps, parts, loads, steps_table, surface, table, rows_out):
     slots = loads.shape[0]
     tiles = parts.shape[0]
     mine = lax.rem(lax.axis_index("line"), tiles)
     table[...] = jnp.zeros(table.shape, jnp.float32)
     table[0:1, :] = lane_blocks(steps_table[0:8, :], slots)
-    table[STEPS + 1 : STEPS + 2, :] = lane_blocks(steps_table[8:16, :], slots)
+    table[steps + 1 : steps + 2, :] = lane_blocks(steps_table[8:16, :], slots)
     rows = [loads[...]]
-    for k in range(1, STEPS + 1):
+    for k in range(1, steps + 1):
         source = lax.rem(mine + (tiles - k), tiles)
         rows.append(parts[source, TRUCK_ROW : TRUCK_ROW + slots, :])
         table[k : k + 1, :] = parts[source, ENTRY_ROW : ENTRY_ROW + 1, :]
     columns = table[...].T
     rows_out[...] = jnp.zeros(rows_out.shape, jnp.float32)
-    for s in range(STEPS):
+    for s in range(steps):
         block = slice(s * slots, (s + 1) * slots)
         moved = []
-        for k in range(STEPS - s):
+        for k in range(steps - s):
             entry = jnp.broadcast_to(columns[block, k : k + 1], rows[k].shape)
             new = rows[k]
             for slot in range(slots):
                 new = jnp.where(entry == float(slot), rows[k + 1][slot : slot + 1, :], new)
             moved.append(new)
         rows = moved
-        cell = jnp.broadcast_to(columns[block, STEPS + 1 : STEPS + 2], rows[0].shape)
+        cell = jnp.broadcast_to(columns[block, steps + 1 : steps + 2], rows[0].shape)
         for c in range(2):
             load = jnp.sum(jnp.where(cell == float(c), rows[0], 0.0), axis=0, keepdims=True)
             rows_out[2 * s + c : 2 * s + c + 1, :] = load
@@ -734,20 +746,25 @@
         (own, behind, in_vmem(pier_row), coef),
         (WHOLE,) * 3 + (ANYWHERE,),
         jax.ShapeDtypeStruct((GROUP, TRUCK_ROW + slots, depth), f32),
-        WHOLE,
+        ANYWHERE,
+        scratch=(pltpu.VMEM((GROUP, TRUCK_ROW + slots, depth), f32), dma((GROUP,))),
         name="split",
     )
     groups = [list(range(at, at + GROUP)) for at in range(0, tiles, GROUP)]
     parts = lax.all_to_all(parts, "line", 0, 0, axis_index_groups=groups, tiled=True)
+    square = pltpu.VMEM((across, depth), f32)
+    turned = (pltpu.VMEM((depth, depth), f32), pltpu.VMEM((depth, across), f32))
+    ins = (parts, in_vmem(loads), in_vmem(steps_table))
     force, surface = call(
         prepare_kernel,
-        (parts, in_vmem(loads), in_vmem(steps_table)),
+        ins,
         (WHOLE,) * 3,
-        (pltpu.VMEM((STEPS, 3, 3, 16, depth), f32), pltpu.VMEM((across, depth), f32)),
+        (pltpu.VMEM((STEPS, 3, 3, 16, depth), f32), square),
         (WHOLE,) * 2,
-        scratch=(pltpu.VMEM((depth, depth), f32), pltpu.VMEM((depth, across), f32)),
+        scratch=turned,
         name="prepare",
     )
+    later = call(surface_kernel, ins, (WHOLE,) * 3, square, WHOLE, scratch=turned, name="surface")
     V, early = call(
         functools.partial(first_kernel, window),
         tuple(in_vmem(x) for x in (V, S, R, coef, force, surface)),
@@ -779,6 +796,8 @@
         )
         if more:
             msg_near = lax.ppermute(msg[0], "line", near)
+        if step == 0:
+            surface = later
         ins = (V, S, R, coef, force, surface, msg_far) + ((missing,) if step else ())
         ins = tuple(in_vmem(x) for x in ins)
         if more:

time: 52.5 us -> 52.3 us (level)
    ppermute x1, waiting for transfers between devices: 1.76 us -> 1.18 us  [body(): early = lax.ppermute(early, 'line', far)]
    pallas_call x17 -> x18, Pallas kernels: 10.8 us -> 11.2 us  [call(): pl.pallas_call(kernel, out_shape=outs, in_specs=specs, out_specs=out_spec...]
  transfers between devices with their start and end apart: 14 -> 14, of which waited for: 7 -> 7; matrix products, arithmetic and copies ran while one was open for 0% -> 0% of each run, Pallas kernels for 15% -> 16%
where the time goes in v15:
time: 52.3 us; the launch traced here: 51.8 us
  starting transfers between devices  28 us (54%)
  waiting for transfers between devices  11.7 us (22%)
  Pallas kernels  11.2 us (21%)
  between operations  0.88 us (2%)
    ppermute x4, starting transfers between devices, body(): early = lax.ppermute(msg[0], 'line', far)  12.7 us
    pallas_call x18, Pallas kernels, call(): pl.pallas_call(kernel, out_shape=outs, in_specs=specs, out_specs=out_spec...  11.2 us
    ppermute x4, waiting for transfers between devices, body(): early = lax.ppermute(msg[0], 'line', far)  6.36 us
    all_to_all x1, starting transfers between devices, body(): lax.all_to_all(parts, 'line', 0, 0, axis_index_groups=groups, tiled=True)  6.31 us
    ppermute x1, starting transfers between devices, body(): msg_far = lax.ppermute(msg_far, 'line', far)  3.67 us
    ppermute x1, waiting for transfers between devices, ahead_by(): lax.ppermute(x, 'line', [(i, i + distance) for i in range(tiles - distanc...  2.85 us
    ppermute x1, starting transfers between devices, body(): early = lax.ppermute(early, 'line', far)  2.85 us
    all_to_all x1, waiting for transfers between devices, body(): lax.all_to_all(parts, 'line', 0, 0, axis_index_groups=groups, tiled=True)  1.3 us
  transfers between devices with their start and end apart: 14, of which 7 were waited for; matrix products, arithmetic and copies ran while one was open for 0% of the time, Pallas kernels for 16%

profile of v15, /device:TPU:17, one launch (start us, length us, event | category | flops | bytes accessed | tf_op | source)
XLA Modules:
  0.0 51.8 jit_solution(9638261172903429617)
XLA Ops:
  0.6 0.9 %pack.1 = (f32[8,1920]{1,0:T(8,128)S(1)}, f32[16,128]{1,0:T(8,128)S(1)}, f32[16,128]{1,0:T(8,128)S(1)}, s32[1,8]{1,0:T(1,128)S(1)}) custom-call(f32[8,1536]{1,0:T(8,128)} %bitcast.3, f32[16,128]{1,0:T(8,128)} %loads_in.1, s32[6,16]{1,0:T(8,128)} %entries_in.1, s32[6,16]{1,0:T(8,128)} %cells_in.1, s32[1,8]{1,0:T(1,128)} %bitcast.4), custom_call_target="tpu_custom_call" | custom-call | flops 1 | bytes 1 | tf_op jit(solution)/shard_map/pack/pallas_call | solution.py:663
  1.5 1.3 %collective-permute-start = (f32[8,1920]{1,0:T(8,128)S(1)}, f32[8,1920]{1,0:T(8,128)S(1)}, u32[]{:S(2)}, u32[]{:S(2)}) collective-permute-start(f32[8,1920]{1,0:T(8,128)S(1)} %get-tuple-element.75.own), channel_id=1, source_target_pairs={{0,8},{1,9},{2,10},{3,11},{4,12},{5,13},{6,14},{7,15},{16,24},{17,... | collective-permute-start | bytes 184328 | tf_op jit(solution)/shard_map/ppermute | solution.py:700
  2.8 1.8 %start.1 = (f32[3,2,144,128]{3,2,1,0:T(8,128)S(1)}, f32[6,2,144,128]{3,2,1,0:T(8,128)S(1)}, f32[6,2,128,128]{3,2,1,0:T(8,128)S(1)}, f32[16,128]{1,0:T(8,128)S(1)...) custom-call(f32[3,2,128,128]{3,2,1,0:T(8,128)} %velocity.1, f32[6,2,128,128]{3,2,1,0:T(8,128)} %stress.1, ...), custom_call_target="tpu_custom_call" | custom-call | flops 8388608 | bytes 8388608 | tf_op jit(solution)/shard_map/start/pallas_call | solution.py:663
  4.6 2.8 %collective-permute-done.behind = f32[8,1920]{1,0:T(8,128)S(1)} collective-permute-done((f32[8,1920]{1,0:T(8,128)S(1)}, f32[8,1920]{1,0:T(8,128)S(1)}, u32[]{:S(2)}, u32[]{:S(2)}) %collective-permute-start) | collective-permute-done | bytes 61472 | tf_op jit(solution)/shard_map/ppermute | solution.py:700
  7.4 0.9 %split.1 = f32[8,56,128]{2,1,0:T(8,128)} custom-call(f32[8,1920]{1,0:T(8,128)S(1)} %get-tuple-element.75.own, f32[8,1920]{1,0:T(8,128)S(1)} %collective-permute-done.behind, s32[1,8]{1,0:T(1,128)S(1)} %get-tuple-element.76.cells, f32[16,128]{1,0:T(8,128)S(1)} %get-tuple-element.74.after_this.coef_ref), custom_call_target="tpu_custom_call" | custom-call | flops 1 | bytes 1 | tf_op jit(solution)/shard_map/split/pallas_call | solution.py:663
  8.3 6.3 %all-to-all-start = ((f32[8,56,128]{2,1,0:T(8,128)}), f32[8,56,128]{2,1,0:T(8,128)S(1)}, u32[]{:S(2)}, u32[]{:S(2)}) async-start(f32[8,56,128]{2,1,0:T(8,128)} %split.1), calls=%async_computation | async-start | bytes 458752 | tf_op jit(solution)/shard_map/all_to_all | solution.py:754
  14.6 0.0 collective-permute-start.1
  14.6 3.7 %collective-permute-start.2 = (f32[3,128,128]{2,1,0:T(8,128)S(1)}, f32[3,128,128]{2,1,0:T(8,128)S(1)}, u32[]{:S(2)}, u32[]{:S(2)}) collective-permute-start(f32[3,128,128]{2,1,0:T(8,128)S(1)} %get-tuple-element.85), channel_id=1, source_target_pairs={{1,2},{3,4},{5,6},{7,8},{9,10},{11,12},{13,14},{2,1},{4,3},{6,5},{... | collective-permute-start | bytes 589832 | tf_op jit(solution)/shard_map/ppermute | solution.py:742
  18.3 1.3 %all-to-all-done.parts = f32[8,56,128]{2,1,0:T(8,128)S(1)} async-done(((f32[8,56,128]{2,1,0:T(8,128)}), f32[8,56,128]{2,1,0:T(8,128)S(1)}, u32[]{:S(2)}, u32[]{:S(2)}) %all-to-all-start) | async-done | bytes 229408 | tf_op jit(solution)/shard_map/all_to_all | solution.py:754
  19.6 0.3 prepare.1
  20.0 0.3 first.1
  20.3 0.0 collective-permute-done.1.msg
  20.3 0.3 near0.1
  20.6 0.9 %collective-permute-start.3 = (f32[3,128,128]{2,1,0:T(8,128)S(1)}, f32[3,128,128]{2,1,0:T(8,128)S(1)}, u32[]{:S(2)}, u32[]{:S(2)}) collective-permute-start(f32[3,128,128]{2,1,0:T(8,128)S(1)} %get-tuple-element.89), channel_id=1, source_target_pairs={{0,1},{1,0},{2,3},{3,2},{4,5},{5,4},{6,7},{7,6},{8,9},{9,8},{10,11... | collective-permute-start | bytes 589832 | tf_op jit(solution)/shard_map/ppermute | solution.py:798
  21.5 2.8 %collective-permute-start.4 = (f32[3,128,128]{2,1,0:T(8,128)S(1)}, f32[3,128,128]{2,1,0:T(8,128)S(1)}, u32[]{:S(2)}, u32[]{:S(2)}) collective-permute-start(f32[3,128,128]{2,1,0:T(8,128)S(1)} %get-tuple-element.93), channel_id=1, source_target_pairs={{1,2},{3,4},{5,6},{7,8},{9,10},{11,12},{13,14},{2,1},{4,3},{6,5},{... | collective-permute-start | bytes 589832 | tf_op jit(solution)/shard_map/ppermute | solution.py:778
  24.3 0.6 %surface.1 = f32[128,128]{1,0:T(8,128)S(1)} custom-call(f32[8,56,128]{2,1,0:T(8,128)S(1)} %all-to-all-done.parts, f32[16,128]{1,0:T(8,128)S(1)} %get-tuple-element.77.loads, f32[16,128]{1,0:T(8,128)S(1)} %get-tuple-element.70.after_this.steps_table), custom_call_target="tpu_custom_call" | custom-call | flops 1 | bytes 1 | tf_op jit(solution)/shard_map/surface/pallas_call | solution.py:663
  24.9 0.0 collective-permute-done.2.msg
  24.9 0.6 %far0.1 = (f32[3,2,144,128]{3,2,1,0:T(8,128)S(1)}, f32[6,2,144,128]{3,2,1,0:T(8,128)S(1)}, f32[6,2,128,128]{3,2,1,0:T(8,128)S(1)}, f32[3,128,128]{2,1,0:T(8,128)S(1)}, f32[3,128,128]{2,1,0:T(8,128)S(1)}) custom-call(f32[3,2,144,128]{3,2,1,0:T(8,128)S(1)} %get-tuple-element.82.V0, ...), custom_call_target="tpu_custom_call", output_to_operand_aliasing={{0}: (0, {}), {1}: (1, {}), {2}: (2, {})} | custom-call | flops 1 | bytes 1 | tf_op jit(solution)/shard_map/far0/pallas_call | solution.py:663
  25.6 0.0 collective-permute-done.3.msg
  25.6 0.3 near1.1
  25.8 0.1 collective-permute-start.5
  25.9 3.5 %collective-permute-start.6 = (f32[3,128,128]{2,1,0:T(8,128)S(1)}, f32[3,128,128]{2,1,0:T(8,128)S(1)}, u32[]{:S(2)}, u32[]{:S(2)}) collective-permute-start(f32[3,128,128]{2,1,0:T(8,128)S(1)} %get-tuple-element.102), channel_id=1, source_target_pairs={{1,2},{3,4},{5,6},{7,8},{9,10},{11,12},{13,14},{2,1},{4,3},{6,5},{... | collective-permute-start | bytes 589832 | tf_op jit(solution)/shard_map/ppermute | solution.py:817
  29.4 1.2 %collective-permute-done.4.msg = f32[3,128,128]{2,1,0:T(8,128)S(1)} collective-permute-done((f32[3,128,128]{2,1,0:T(8,128)S(1)}, f32[3,128,128]{2,1,0:T(8,128)S(1)}, u32[]{:S(2)}, u32[]{:S(2)}) %collective-permute-start.4) | collective-permute-done | bytes 196640 | tf_op jit(solution)/shard_map/ppermute | solution.py:778
  30.6 0.6 %far1.1 = (f32[3,2,144,128]{3,2,1,0:T(8,128)S(1)}, f32[6,2,144,128]{3,2,1,0:T(8,128)S(1)}, f32[6,2,128,128]{3,2,1,0:T(8,128)S(1)}, f32[3,128,128]{2,1,0:T(8,128)S(1)}, f32[3,128,128]{2,1,0:T(8,128)S(1)}) custom-call(f32[3,2,144,128]{3,2,1,0:T(8,128)S(1)} %get-tuple-element.90.V0, ...), custom_call_target="tpu_custom_call", output_to_operand_aliasing={{0}: (0, {}), {1}: (1, {}), {2}: (2, {})} | custom-call | flops 1 | bytes 1 | tf_op jit(solution)/shard_map/far1/pallas_call | solution.py:663
  31.2 0.0 collective-permute-done.5.msg
  31.2 0.3 near2.1
  31.5 0.1 collective-permute-start.7
  31.6 2.9 %collective-permute-start.8 = (f32[3,128,128]{2,1,0:T(8,128)S(1)}, f32[3,128,128]{2,1,0:T(8,128)S(1)}, u32[]{:S(2)}, u32[]{:S(2)}) collective-permute-start(f32[3,128,128]{2,1,0:T(8,128)S(1)} %get-tuple-element.111), channel_id=1, source_target_pairs={{1,2},{3,4},{5,6},{7,8},{9,10},{11,12},{13,14},{2,1},{4,3},{6,5},{... | collective-permute-start | bytes 589832 | tf_op jit(solution)/shard_map/ppermute | solution.py:817
  34.4 0.6 %collective-permute-done.6.msg = f32[3,128,128]{2,1,0:T(8,128)S(1)} collective-permute-done((f32[3,128,128]{2,1,0:T(8,128)S(1)}, f32[3,128,128]{2,1,0:T(8,128)S(1)}, u32[]{:S(2)}, u32[]{:S(2)}) %collective-permute-start.6) | collective-permute-done | bytes 196640 | tf_op jit(solution)/shard_map/ppermute | solution.py:817
  35.0 0.6 %far2.1 = (f32[3,2,144,128]{3,2,1,0:T(8,128)S(1)}, f32[6,2,144,128]{3,2,1,0:T(8,128)S(1)}, f32[6,2,128,128]{3,2,1,0:T(8,128)S(1)}, f32[3,128,128]{2,1,0:T(8,128)S(1)}, f32[3,128,128]{2,1,0:T(8,128)S(1)}) custom-call(f32[3,2,144,128]{3,2,1,0:T(8,128)S(1)} %get-tuple-element.99.V0, ...), custom_call_target="tpu_custom_call", output_to_operand_aliasing={{0}: (0, {}), {1}: (1, {}), {2}: (2, {})} | custom-call | flops 1 | bytes 1 | tf_op jit(solution)/shard_map/far2/pallas_call | solution.py:663
  35.6 0.0 collective-permute-done.7.msg
  35.6 0.3 near3.1
  35.9 0.1 collective-permute-start.9
  36.0 3.5 %collective-permute-start.10 = (f32[3,128,128]{2,1,0:T(8,128)S(1)}, f32[3,128,128]{2,1,0:T(8,128)S(1)}, u32[]{:S(2)}, u32[]{:S(2)}) collective-permute-start(f32[3,128,128]{2,1,0:T(8,128)S(1)} %get-tuple-element.120), channel_id=1, source_target_pairs={{1,2},{3,4},{5,6},{7,8},{9,10},{11,12},{13,14},{2,1},{4,3},{6,5},{... | collective-permute-start | bytes 589832 | tf_op jit(solution)/shard_map/ppermute | solution.py:817
  39.5 1.2 %collective-permute-done.8.msg = f32[3,128,128]{2,1,0:T(8,128)S(1)} collective-permute-done((f32[3,128,128]{2,1,0:T(8,128)S(1)}, f32[3,128,128]{2,1,0:T(8,128)S(1)}, u32[]{:S(2)}, u32[]{:S(2)}) %collective-permute-start.8) | collective-permute-done | bytes 196640 | tf_op jit(solution)/shard_map/ppermute | solution.py:817
  40.7 0.6 %far3.1 = (f32[3,2,144,128]{3,2,1,0:T(8,128)S(1)}, f32[6,2,144,128]{3,2,1,0:T(8,128)S(1)}, f32[6,2,128,128]{3,2,1,0:T(8,128)S(1)}, f32[3,128,128]{2,1,0:T(8,128)S(1)}, f32[3,128,128]{2,1,0:T(8,128)S(1)}) custom-call(f32[3,2,144,128]{3,2,1,0:T(8,128)S(1)} %get-tuple-element.108.V0, ...), custom_call_target="tpu_custom_call", output_to_operand_aliasing={{0}: (0, {}), {1}: (1, {}), {2}: (2, {})} | custom-call | flops 1 | bytes 1 | tf_op jit(solution)/shard_map/far3/pallas_call | solution.py:663
  41.3 0.0 collective-permute-done.9.msg
  41.3 0.3 near4.1
  41.6 0.1 collective-permute-start.11
  41.6 2.9 %collective-permute-start.12 = (f32[3,128,128]{2,1,0:T(8,128)S(1)}, f32[3,128,128]{2,1,0:T(8,128)S(1)}, u32[]{:S(2)}, u32[]{:S(2)}) collective-permute-start(f32[3,128,128]{2,1,0:T(8,128)S(1)} %get-tuple-element.129), channel_id=1, source_target_pairs={{1,2},{3,4},{5,6},{7,8},{9,10},{11,12},{13,14},{2,1},{4,3},{6,5},{... | collective-permute-start | bytes 589832 | tf_op jit(solution)/shard_map/ppermute | solution.py:817
  44.5 0.6 %collective-permute-done.10.msg = f32[3,128,128]{2,1,0:T(8,128)S(1)} collective-permute-done((f32[3,128,128]{2,1,0:T(8,128)S(1)}, f32[3,128,128]{2,1,0:T(8,128)S(1)}, u32[]{:S(2)}, u32[]{:S(2)}) %collective-permute-start.10) | collective-permute-done | bytes 196640 | tf_op jit(solution)/shard_map/ppermute | solution.py:817
  45.1 0.5 far4.1
  45.6 0.0 collective-permute-done.11.msg
  45.6 1.1 %near5.1 = (f32[3,2,144,128]{3,2,1,0:T(8,128)S(1)}, f32[6,2,144,128]{3,2,1,0:T(8,128)S(1)}, f32[6,2,128,128]{3,2,1,0:T(8,128)S(1)}, f32[3,2,128,128]{3,2,1,0:T(8...) custom-call(f32[3,2,144,128]{3,2,1,0:T(8,128)S(1)} %get-tuple-elemen, ...), custom_call_target="tpu_custom_call", output_to_operand_aliasing={{0}: (0, {}), {1}: (1, {}), {2}: (2, {})} | custom-call | flops 1 | bytes 1 | tf_op jit(solution)/shard_map/near5/pallas_call | solution.py:663
  46.7 4.0 %collective-permute-done.12.msg = f32[3,128,128]{2,1,0:T(8,128)S(1)} collective-permute-done((f32[3,128,128]{2,1,0:T(8,128)S(1)}, f32[3,128,128]{2,1,0:T(8,128)S(1)}, u32[]{:S(2)}, u32[]{:S(2)}) %collective-permute-start.12) | collective-permute-done | bytes 196640 | tf_op jit(solution)/shard_map/ppermute | solution.py:817
  50.7 1.1 %last.1 = (f32[3,2,144,128]{3,2,1,0:T(8,128)S(1)}, f32[6,2,144,128]{3,2,1,0:T(8,128)S(1)}, f32[6,2,128,128]{3,2,1,0:T(8,128)S(1)}, f32[3,2,128,128]{3,2,1,0:T(8,...) custom-call(f32[3,2,144,128]{3,2,1,0:T(8,128)S(1)} %get-tuple-elemen, ...), custom_call_target="tpu_custom_call", output_to_operand_aliasing={{0}: (0, {}), {1}: (1, {}), {2}: (2, {}), {3}: (8, {}), {4}... | custom-call | flops 1 | bytes 1 | tf_op jit(solution)/shard_map/last/pallas_call | solution.py:663
Async XLA Ops:
  1.5 5.9 %collective-permute-start = (f32[8,1920]{1,0:T(8,128)S(1)}, f32[8,1920]{1,0:T(8,128)S(1)}, u32[]{:S(2)}, u32[]{:S(2)}) collective-permute-start(f32[8,1920]{1,0:T(8,128)S(1)} %get-tuple-element.75.own), channel_id=1, source_target_pairs={{0,8},{1,9},{2,10},{3,11},{4,12},{5,13},{6,14},{7,15},{16,24},{17,... | collective-permute-start | bytes 184328 | tf_op jit(solution)/shard_map/ppermute | solution.py:700
  8.3 11.3 %all-to-all-start = ((f32[8,56,128]{2,1,0:T(8,128)}), f32[8,56,128]{2,1,0:T(8,128)S(1)}, u32[]{:S(2)}, u32[]{:S(2)}) async-start(f32[8,56,128]{2,1,0:T(8,128)} %split.1), calls=%async_computation | async-start | bytes 458752 | tf_op jit(solution)/shard_map/all_to_all | solution.py:754
  14.6 5.6 %collective-permute-start.1 = (f32[3,128,128]{2,1,0:T(8,128)S(1)}, f32[3,128,128]{2,1,0:T(8,128)S(1)}, u32[]{:S(2)}, u32[]{:S(2)}) collective-permute-start(f32[3,128,128]{2,1,0:T(8,128)S(1)} %get-tuple-element.81), channel_id=1, source_target_pairs={{0,1},{1,0},{2,3},{3,2},{4,5},{5,4},{6,7},{7,6},{8,9},{9,8},{10,11... | collective-permute-start | bytes 589832 | tf_op jit(solution)/shard_map/ppermute | solution.py:743
  14.6 10.3 %collective-permute-start.2 = (f32[3,128,128]{2,1,0:T(8,128)S(1)}, f32[3,128,128]{2,1,0:T(8,128)S(1)}, u32[]{:S(2)}, u32[]{:S(2)}) collective-permute-start(f32[3,128,128]{2,1,0:T(8,128)S(1)} %get-tuple-element.85), channel_id=1, source_target_pairs={{1,2},{3,4},{5,6},{7,8},{9,10},{11,12},{13,14},{2,1},{4,3},{6,5},{... | collective-permute-start | bytes 589832 | tf_op jit(solution)/shard_map/ppermute | solution.py:742
  20.6 5.0 %collective-permute-start.3 = (f32[3,128,128]{2,1,0:T(8,128)S(1)}, f32[3,128,128]{2,1,0:T(8,128)S(1)}, u32[]{:S(2)}, u32[]{:S(2)}) collective-permute-start(f32[3,128,128]{2,1,0:T(8,128)S(1)} %get-tuple-element.89), channel_id=1, source_target_pairs={{0,1},{1,0},{2,3},{3,2},{4,5},{5,4},{6,7},{7,6},{8,9},{9,8},{10,11... | collective-permute-start | bytes 589832 | tf_op jit(solution)/shard_map/ppermute | solution.py:798
  21.5 9.1 %collective-permute-start.4 = (f32[3,128,128]{2,1,0:T(8,128)S(1)}, f32[3,128,128]{2,1,0:T(8,128)S(1)}, u32[]{:S(2)}, u32[]{:S(2)}) collective-permute-start(f32[3,128,128]{2,1,0:T(8,128)S(1)} %get-tuple-element.93), channel_id=1, source_target_pairs={{1,2},{3,4},{5,6},{7,8},{9,10},{11,12},{13,14},{2,1},{4,3},{6,5},{... | collective-permute-start | bytes 589832 | tf_op jit(solution)/shard_map/ppermute | solution.py:778
  25.8 5.3 %collective-permute-start.5 = (f32[3,128,128]{2,1,0:T(8,128)S(1)}, f32[3,128,128]{2,1,0:T(8,128)S(1)}, u32[]{:S(2)}, u32[]{:S(2)}) collective-permute-start(f32[3,128,128]{2,1,0:T(8,128)S(1)} %get-tuple-element.98), channel_id=1, source_target_pairs={{0,1},{1,0},{2,3},{3,2},{4,5},{5,4},{6,7},{7,6},{8,9},{9,8},{10,11... | collective-permute-start | bytes 589832 | tf_op jit(solution)/shard_map/ppermute | solution.py:798
  25.9 9.1 %collective-permute-start.6 = (f32[3,128,128]{2,1,0:T(8,128)S(1)}, f32[3,128,128]{2,1,0:T(8,128)S(1)}, u32[]{:S(2)}, u32[]{:S(2)}) collective-permute-start(f32[3,128,128]{2,1,0:T(8,128)S(1)} %get-tuple-element.102), channel_id=1, source_target_pairs={{1,2},{3,4},{5,6},{7,8},{9,10},{11,12},{13,14},{2,1},{4,3},{6,5},{... | collective-permute-start | bytes 589832 | tf_op jit(solution)/shard_map/ppermute | solution.py:817
  31.5 4.2 %collective-permute-start.7 = (f32[3,128,128]{2,1,0:T(8,128)S(1)}, f32[3,128,128]{2,1,0:T(8,128)S(1)}, u32[]{:S(2)}, u32[]{:S(2)}) collective-permute-start(f32[3,128,128]{2,1,0:T(8,128)S(1)} %get-tuple-element.107), channel_id=1, source_target_pairs={{0,1},{1,0},{2,3},{3,2},{4,5},{5,4},{6,7},{7,6},{8,9},{9,8},{10,11... | collective-permute-start | bytes 589832 | tf_op jit(solution)/shard_map/ppermute | solution.py:798
  31.6 9.1 %collective-permute-start.8 = (f32[3,128,128]{2,1,0:T(8,128)S(1)}, f32[3,128,128]{2,1,0:T(8,128)S(1)}, u32[]{:S(2)}, u32[]{:S(2)}) collective-permute-start(f32[3,128,128]{2,1,0:T(8,128)S(1)} %get-tuple-element.111), channel_id=1, source_target_pairs={{1,2},{3,4},{5,6},{7,8},{9,10},{11,12},{13,14},{2,1},{4,3},{6,5},{... | collective-permute-start | bytes 589832 | tf_op jit(solution)/shard_map/ppermute | solution.py:817
  35.9 5.4 %collective-permute-start.9 = (f32[3,128,128]{2,1,0:T(8,128)S(1)}, f32[3,128,128]{2,1,0:T(8,128)S(1)}, u32[]{:S(2)}, u32[]{:S(2)}) collective-permute-start(f32[3,128,128]{2,1,0:T(8,128)S(1)} %get-tuple-element.116), channel_id=1, source_target_pairs={{0,1},{1,0},{2,3},{3,2},{4,5},{5,4},{6,7},{7,6},{8,9},{9,8},{10,11... | collective-permute-start | bytes 589832 | tf_op jit(solution)/shard_map/ppermute | solution.py:798
  36.0 9.1 %collective-permute-start.10 = (f32[3,128,128]{2,1,0:T(8,128)S(1)}, f32[3,128,128]{2,1,0:T(8,128)S(1)}, u32[]{:S(2)}, u32[]{:S(2)}) collective-permute-start(f32[3,128,128]{2,1,0:T(8,128)S(1)} %get-tuple-element.120), channel_id=1, source_target_pairs={{1,2},{3,4},{5,6},{7,8},{9,10},{11,12},{13,14},{2,1},{4,3},{6,5},{... | collective-permute-start | bytes 589832 | tf_op jit(solution)/shard_map/ppermute | solution.py:817
  41.6 4.0 %collective-permute-start.11 = (f32[3,128,128]{2,1,0:T(8,128)S(1)}, f32[3,128,128]{2,1,0:T(8,128)S(1)}, u32[]{:S(2)}, u32[]{:S(2)}) collective-permute-start(f32[3,128,128]{2,1,0:T(8,128)S(1)} %get-tuple-element.125), channel_id=1, source_target_pairs={{0,1},{1,0},{2,3},{3,2},{4,5},{5,4},{6,7},{7,6},{8,9},{9,8},{10,11... | collective-permute-start | bytes 589832 | tf_op jit(solution)/shard_map/ppermute | solution.py:798
  41.6 9.1 %collective-permute-start.12 = (f32[3,128,128]{2,1,0:T(8,128)S(1)}, f32[3,128,128]{2,1,0:T(8,128)S(1)}, u32[]{:S(2)}, u32[]{:S(2)}) collective-permute-start(f32[3,128,128]{2,1,0:T(8,128)S(1)} %get-tuple-element.129), channel_id=1, source_target_pairs={{1,2},{3,4},{5,6},{7,8},{9,10},{11,12},{13,14},{2,1},{4,3},{6,5},{... | collective-permute-start | bytes 589832 | tf_op jit(solution)/shard_map/ppermute | solution.py:817

commit v16 on v15

--- a/solution.py
+++ b/solution.py
@@ -9,6 +9,7 @@
 from jax.sharding import PartitionSpec as P
 
 STEPS = 6
+SOON = 3
 FY = 8
 FZ = 64
 DT = 0.25
@@ -612,7 +613,7 @@
                 panel = parts[s, pl.ds(comp * per * width + cell, per, stride=width), :]
                 force[s, comp, cell, pl.ds(4, per, stride=2), :] = scale * panel
                 force[s, comp, cell, pl.ds(5, per, stride=2), :] = scale * lane_roll(panel, FZ)
-    surface_loads(1, parts, loads, steps_table, surface, table, rows_out)
+    surface_loads(SOON, parts, loads, steps_table, surface, table, rows_out)
 
 
 def surface_kernel(parts, loads, steps_table, surface, table, rows_out):
@@ -796,7 +797,7 @@
         )
         if more:
             msg_near = lax.ppermute(msg[0], "line", near)
-        if step == 0:
+        if step == SOON - 1:
             surface = later
         ins = (V, S, R, coef, force, surface, msg_far) + ((missing,) if step else ())
         ins = tuple(in_vmem(x) for x in ins)

time: 52.3 us -> 52.9 us (1.011)
    ppermute x1, waiting for transfers between devices: 1.18 us -> 1.75 us  [body(): early = lax.ppermute(early, 'line', far)]
  transfers between devices with their start and end apart: 14 -> 14, of which waited for: 7 -> 6; matrix products, arithmetic and copies ran while one was open for 0% -> 0% of each run, Pallas kernels for 16% -> 16%
where the time goes in v16:
time: 52.9 us; the launch traced here: 52.5 us
  starting transfers between devices  28.5 us (54%)
  waiting for transfers between devices  11.8 us (22%)
  Pallas kernels  11.3 us (21%)
  between operations  0.9 us (2%)
    ppermute x4, starting transfers between devices, body(): early = lax.ppermute(msg[0], 'line', far)  13.1 us
    pallas_call x18, Pallas kernels, call(): pl.pallas_call(kernel, out_shape=outs, in_specs=specs, out_specs=out_spec...  11.3 us
    all_to_all x1, starting transfers between devices, body(): lax.all_to_all(parts, 'line', 0, 0, axis_index_groups=groups, tiled=True)  6.31 us
    ppermute x4, waiting for transfers between devices, body(): early = lax.ppermute(msg[0], 'line', far)  5.89 us
    ppermute x1, starting transfers between devices, body(): msg_far = lax.ppermute(msg_far, 'line', far)  3.67 us
    ppermute x1, waiting for transfers between devices, ahead_by(): lax.ppermute(x, 'line', [(i, i + distance) for i in range(tiles - distanc...  2.85 us
    ppermute x1, starting transfers between devices, body(): early = lax.ppermute(early, 'line', far)  2.85 us
    ppermute x1, waiting for transfers between devices, body(): early = lax.ppermute(early, 'line', far)  1.75 us
  transfers between devices with their start and end apart: 14, of which 6 were waited for; matrix products, arithmetic and copies ran while one was open for 0% of the time, Pallas kernels for 16%

profile of v16, /device:TPU:17, one launch (start us, length us, event | category | flops | bytes accessed | tf_op | source)
XLA Modules:
  0.0 52.5 jit_solution(16336454538632476795)
XLA Ops:
  0.6 0.9 %pack.1 = (f32[8,1920]{1,0:T(8,128)S(1)}, f32[16,128]{1,0:T(8,128)S(1)}, f32[16,128]{1,0:T(8,128)S(1)}, s32[1,8]{1,0:T(1,128)S(1)}) custom-call(f32[8,1536]{1,0:T(8,128)} %bitcast.3, f32[16,128]{1,0:T(8,128)} %loads_in.1, s32[6,16]{1,0:T(8,128)} %entries_in.1, s32[6,16]{1,0:T(8,128)} %cells_in.1, s32[1,8]{1,0:T(1,128)} %bitcast.4), custom_call_target="tpu_custom_call" | custom-call | flops 1 | bytes 1 | tf_op jit(solution)/shard_map/pack/pallas_call | solution.py:664
  1.5 1.3 %collective-permute-start = (f32[8,1920]{1,0:T(8,128)S(1)}, f32[8,1920]{1,0:T(8,128)S(1)}, u32[]{:S(2)}, u32[]{:S(2)}) collective-permute-start(f32[8,1920]{1,0:T(8,128)S(1)} %get-tuple-element.75.own), channel_id=1, source_target_pairs={{0,8},{1,9},{2,10},{3,11},{4,12},{5,13},{6,14},{7,15},{16,24},{17,... | collective-permute-start | bytes 184328 | tf_op jit(solution)/shard_map/ppermute | solution.py:701
  2.8 1.8 %start.1 = (f32[3,2,144,128]{3,2,1,0:T(8,128)S(1)}, f32[6,2,144,128]{3,2,1,0:T(8,128)S(1)}, f32[6,2,128,128]{3,2,1,0:T(8,128)S(1)}, f32[16,128]{1,0:T(8,128)S(1)...) custom-call(f32[3,2,128,128]{3,2,1,0:T(8,128)} %velocity.1, f32[6,2,128,128]{3,2,1,0:T(8,128)} %stress.1, ...), custom_call_target="tpu_custom_call" | custom-call | flops 8388608 | bytes 8388608 | tf_op jit(solution)/shard_map/start/pallas_call | solution.py:664
  4.6 2.8 %collective-permute-done.behind = f32[8,1920]{1,0:T(8,128)S(1)} collective-permute-done((f32[8,1920]{1,0:T(8,128)S(1)}, f32[8,1920]{1,0:T(8,128)S(1)}, u32[]{:S(2)}, u32[]{:S(2)}) %collective-permute-start) | collective-permute-done | bytes 61472 | tf_op jit(solution)/shard_map/ppermute | solution.py:701
  7.4 0.9 %split.1 = f32[8,56,128]{2,1,0:T(8,128)} custom-call(f32[8,1920]{1,0:T(8,128)S(1)} %get-tuple-element.75.own, f32[8,1920]{1,0:T(8,128)S(1)} %collective-permute-done.behind, s32[1,8]{1,0:T(1,128)S(1)} %get-tuple-element.76.cells, f32[16,128]{1,0:T(8,128)S(1)} %get-tuple-element.74.after_this.coef_ref), custom_call_target="tpu_custom_call" | custom-call | flops 1 | bytes 1 | tf_op jit(solution)/shard_map/split/pallas_call | solution.py:664
  8.3 6.3 %all-to-all-start = ((f32[8,56,128]{2,1,0:T(8,128)}), f32[8,56,128]{2,1,0:T(8,128)S(1)}, u32[]{:S(2)}, u32[]{:S(2)}) async-start(f32[8,56,128]{2,1,0:T(8,128)} %split.1), calls=%async_computation | async-start | bytes 458752 | tf_op jit(solution)/shard_map/all_to_all | solution.py:755
  14.6 0.0 collective-permute-start.1
  14.6 3.7 %collective-permute-start.2 = (f32[3,128,128]{2,1,0:T(8,128)S(1)}, f32[3,128,128]{2,1,0:T(8,128)S(1)}, u32[]{:S(2)}, u32[]{:S(2)}) collective-permute-start(f32[3,128,128]{2,1,0:T(8,128)S(1)} %get-tuple-element.85), channel_id=1, source_target_pairs={{1,2},{3,4},{5,6},{7,8},{9,10},{11,12},{13,14},{2,1},{4,3},{6,5},{... | collective-permute-start | bytes 589832 | tf_op jit(solution)/shard_map/ppermute | solution.py:743
  18.3 1.3 %all-to-all-done.parts = f32[8,56,128]{2,1,0:T(8,128)S(1)} async-done(((f32[8,56,128]{2,1,0:T(8,128)}), f32[8,56,128]{2,1,0:T(8,128)S(1)}, u32[]{:S(2)}, u32[]{:S(2)}) %all-to-all-start) | async-done | bytes 229408 | tf_op jit(solution)/shard_map/all_to_all | solution.py:755
  19.6 0.4 prepare.1
  20.0 0.3 first.1
  20.3 0.0 collective-permute-done.1.msg
  20.3 0.3 near0.1
  20.6 0.9 %collective-permute-start.3 = (f32[3,128,128]{2,1,0:T(8,128)S(1)}, f32[3,128,128]{2,1,0:T(8,128)S(1)}, u32[]{:S(2)}, u32[]{:S(2)}) collective-permute-start(f32[3,128,128]{2,1,0:T(8,128)S(1)} %get-tuple-element.89), channel_id=1, source_target_pairs={{0,1},{1,0},{2,3},{3,2},{4,5},{5,4},{6,7},{7,6},{8,9},{9,8},{10,11... | collective-permute-start | bytes 589832 | tf_op jit(solution)/shard_map/ppermute | solution.py:799
  21.6 2.8 %collective-permute-start.4 = (f32[3,128,128]{2,1,0:T(8,128)S(1)}, f32[3,128,128]{2,1,0:T(8,128)S(1)}, u32[]{:S(2)}, u32[]{:S(2)}) collective-permute-start(f32[3,128,128]{2,1,0:T(8,128)S(1)} %get-tuple-element.93), channel_id=1, source_target_pairs={{1,2},{3,4},{5,6},{7,8},{9,10},{11,12},{13,14},{2,1},{4,3},{6,5},{... | collective-permute-start | bytes 589832 | tf_op jit(solution)/shard_map/ppermute | solution.py:779
  24.4 0.0 collective-permute-done.2.msg
  24.4 0.6 %far0.1 = (f32[3,2,144,128]{3,2,1,0:T(8,128)S(1)}, f32[6,2,144,128]{3,2,1,0:T(8,128)S(1)}, f32[6,2,128,128]{3,2,1,0:T(8,128)S(1)}, f32[3,128,128]{2,1,0:T(8,128)S(1)}, f32[3,128,128]{2,1,0:T(8,128)S(1)}) custom-call(f32[3,2,144,128]{3,2,1,0:T(8,128)S(1)} %get-tuple-element.82.V0, ...), custom_call_target="tpu_custom_call", output_to_operand_aliasing={{0}: (0, {}), {1}: (1, {}), {2}: (2, {})} | custom-call | flops 1 | bytes 1 | tf_op jit(solution)/shard_map/far0/pallas_call | solution.py:664
  25.0 0.0 collective-permute-done.3.msg
  25.1 0.3 near1.1
  25.3 0.1 collective-permute-start.5
  25.4 3.5 %collective-permute-start.6 = (f32[3,128,128]{2,1,0:T(8,128)S(1)}, f32[3,128,128]{2,1,0:T(8,128)S(1)}, u32[]{:S(2)}, u32[]{:S(2)}) collective-permute-start(f32[3,128,128]{2,1,0:T(8,128)S(1)} %get-tuple-element.102), channel_id=1, source_target_pairs={{1,2},{3,4},{5,6},{7,8},{9,10},{11,12},{13,14},{2,1},{4,3},{6,5},{... | collective-permute-start | bytes 589832 | tf_op jit(solution)/shard_map/ppermute | solution.py:818
  28.9 1.8 %collective-permute-done.4.msg = f32[3,128,128]{2,1,0:T(8,128)S(1)} collective-permute-done((f32[3,128,128]{2,1,0:T(8,128)S(1)}, f32[3,128,128]{2,1,0:T(8,128)S(1)}, u32[]{:S(2)}, u32[]{:S(2)}) %collective-permute-start.4) | collective-permute-done | bytes 196640 | tf_op jit(solution)/shard_map/ppermute | solution.py:779
  30.6 0.6 %far1.1 = (f32[3,2,144,128]{3,2,1,0:T(8,128)S(1)}, f32[6,2,144,128]{3,2,1,0:T(8,128)S(1)}, f32[6,2,128,128]{3,2,1,0:T(8,128)S(1)}, f32[3,128,128]{2,1,0:T(8,128)S(1)}, f32[3,128,128]{2,1,0:T(8,128)S(1)}) custom-call(f32[3,2,144,128]{3,2,1,0:T(8,128)S(1)} %get-tuple-element.90.V0, ...), custom_call_target="tpu_custom_call", output_to_operand_aliasing={{0}: (0, {}), {1}: (1, {}), {2}: (2, {})} | custom-call | flops 1 | bytes 1 | tf_op jit(solution)/shard_map/far1/pallas_call | solution.py:664
  31.3 0.0 collective-permute-done.5.msg
  31.3 0.3 near2.1
  31.5 0.1 collective-permute-start.7
  31.6 0.6 %surface.1 = f32[128,128]{1,0:T(8,128)S(1)} custom-call(f32[8,56,128]{2,1,0:T(8,128)S(1)} %all-to-all-done.parts, f32[16,128]{1,0:T(8,128)S(1)} %get-tuple-element.77.loads, f32[16,128]{1,0:T(8,128)S(1)} %get-tuple-element.70.after_this.steps_table), custom_call_target="tpu_custom_call" | custom-call | flops 1 | bytes 1 | tf_op jit(solution)/shard_map/surface/pallas_call | solution.py:664
  32.2 2.9 %collective-permute-start.8 = (f32[3,128,128]{2,1,0:T(8,128)S(1)}, f32[3,128,128]{2,1,0:T(8,128)S(1)}, u32[]{:S(2)}, u32[]{:S(2)}) collective-permute-start(f32[3,128,128]{2,1,0:T(8,128)S(1)} %get-tuple-element.111), channel_id=1, source_target_pairs={{1,2},{3,4},{5,6},{7,8},{9,10},{11,12},{13,14},{2,1},{4,3},{6,5},{... | collective-permute-start | bytes 589832 | tf_op jit(solution)/shard_map/ppermute | solution.py:818
  35.1 0.0 collective-permute-done.6.msg
  35.1 0.6 %far2.1 = (f32[3,2,144,128]{3,2,1,0:T(8,128)S(1)}, f32[6,2,144,128]{3,2,1,0:T(8,128)S(1)}, f32[6,2,128,128]{3,2,1,0:T(8,128)S(1)}, f32[3,128,128]{2,1,0:T(8,128)S(1)}, f32[3,128,128]{2,1,0:T(8,128)S(1)}) custom-call(f32[3,2,144,128]{3,2,1,0:T(8,128)S(1)} %get-tuple-element.99.V0, ...), custom_call_target="tpu_custom_call", output_to_operand_aliasing={{0}: (0, {}), {1}: (1, {}), {2}: (2, {})} | custom-call | flops 1 | bytes 1 | tf_op jit(solution)/shard_map/far2/pallas_call | solution.py:664
  35.7 0.0 collective-permute-done.7.msg
  35.7 0.3 near3.1
  36.0 0.1 collective-permute-start.9
  36.1 3.9 %collective-permute-start.10 = (f32[3,128,128]{2,1,0:T(8,128)S(1)}, f32[3,128,128]{2,1,0:T(8,128)S(1)}, u32[]{:S(2)}, u32[]{:S(2)}) collective-permute-start(f32[3,128,128]{2,1,0:T(8,128)S(1)} %get-tuple-element.120), channel_id=1, source_target_pairs={{1,2},{3,4},{5,6},{7,8},{9,10},{11,12},{13,14},{2,1},{4,3},{6,5},{... | collective-permute-start | bytes 589832 | tf_op jit(solution)/shard_map/ppermute | solution.py:818
  40.0 1.3 %collective-permute-done.8.msg = f32[3,128,128]{2,1,0:T(8,128)S(1)} collective-permute-done((f32[3,128,128]{2,1,0:T(8,128)S(1)}, f32[3,128,128]{2,1,0:T(8,128)S(1)}, u32[]{:S(2)}, u32[]{:S(2)}) %collective-permute-start.8) | collective-permute-done | bytes 196640 | tf_op jit(solution)/shard_map/ppermute | solution.py:818
  41.3 0.6 %far3.1 = (f32[3,2,144,128]{3,2,1,0:T(8,128)S(1)}, f32[6,2,144,128]{3,2,1,0:T(8,128)S(1)}, f32[6,2,128,128]{3,2,1,0:T(8,128)S(1)}, f32[3,128,128]{2,1,0:T(8,128)S(1)}, f32[3,128,128]{2,1,0:T(8,128)S(1)}) custom-call(f32[3,2,144,128]{3,2,1,0:T(8,128)S(1)} %get-tuple-element.108.V0, ...), custom_call_target="tpu_custom_call", output_to_operand_aliasing={{0}: (0, {}), {1}: (1, {}), {2}: (2, {})} | custom-call | flops 1 | bytes 1 | tf_op jit(solution)/shard_map/far3/pallas_call | solution.py:664
  41.9 0.0 collective-permute-done.9.msg
  41.9 0.3 near4.1
  42.2 0.1 collective-permute-start.11
  42.3 2.9 %collective-permute-start.12 = (f32[3,128,128]{2,1,0:T(8,128)S(1)}, f32[3,128,128]{2,1,0:T(8,128)S(1)}, u32[]{:S(2)}, u32[]{:S(2)}) collective-permute-start(f32[3,128,128]{2,1,0:T(8,128)S(1)} %get-tuple-element.129), channel_id=1, source_target_pairs={{1,2},{3,4},{5,6},{7,8},{9,10},{11,12},{13,14},{2,1},{4,3},{6,5},{... | collective-permute-start | bytes 589832 | tf_op jit(solution)/shard_map/ppermute | solution.py:818
  45.2 0.3 collective-permute-done.10.msg
  45.5 0.5 far4.1
  46.0 0.0 collective-permute-done.11.msg
  46.0 1.1 %near5.1 = (f32[3,2,144,128]{3,2,1,0:T(8,128)S(1)}, f32[6,2,144,128]{3,2,1,0:T(8,128)S(1)}, f32[6,2,128,128]{3,2,1,0:T(8,128)S(1)}, f32[3,2,128,128]{3,2,1,0:T(8...) custom-call(f32[3,2,144,128]{3,2,1,0:T(8,128)S(1)} %get-tuple-elemen, ...), custom_call_target="tpu_custom_call", output_to_operand_aliasing={{0}: (0, {}), {1}: (1, {}), {2}: (2, {})} | custom-call | flops 1 | bytes 1 | tf_op jit(solution)/shard_map/near5/pallas_call | solution.py:664
  47.1 4.3 %collective-permute-done.12.msg = f32[3,128,128]{2,1,0:T(8,128)S(1)} collective-permute-done((f32[3,128,128]{2,1,0:T(8,128)S(1)}, f32[3,128,128]{2,1,0:T(8,128)S(1)}, u32[]{:S(2)}, u32[]{:S(2)}) %collective-permute-start.12) | collective-permute-done | bytes 196640 | tf_op jit(solution)/shard_map/ppermute | solution.py:818
  51.4 1.1 %last.1 = (f32[3,2,144,128]{3,2,1,0:T(8,128)S(1)}, f32[6,2,144,128]{3,2,1,0:T(8,128)S(1)}, f32[6,2,128,128]{3,2,1,0:T(8,128)S(1)}, f32[3,2,128,128]{3,2,1,0:T(8,...) custom-call(f32[3,2,144,128]{3,2,1,0:T(8,128)S(1)} %get-tuple-elemen, ...), custom_call_target="tpu_custom_call", output_to_operand_aliasing={{0}: (0, {}), {1}: (1, {}), {2}: (2, {}), {3}: (8, {}), {4}... | custom-call | flops 1 | bytes 1 | tf_op jit(solution)/shard_map/last/pallas_call | solution.py:664
Async XLA Ops:
  1.5 5.9 %collective-permute-start = (f32[8,1920]{1,0:T(8,128)S(1)}, f32[8,1920]{1,0:T(8,128)S(1)}, u32[]{:S(2)}, u32[]{:S(2)}) collective-permute-start(f32[8,1920]{1,0:T(8,128)S(1)} %get-tuple-element.75.own), channel_id=1, source_target_pairs={{0,8},{1,9},{2,10},{3,11},{4,12},{5,13},{6,14},{7,15},{16,24},{17,... | collective-permute-start | bytes 184328 | tf_op jit(solution)/shard_map/ppermute | solution.py:701
  8.3 11.3 %all-to-all-start = ((f32[8,56,128]{2,1,0:T(8,128)}), f32[8,56,128]{2,1,0:T(8,128)S(1)}, u32[]{:S(2)}, u32[]{:S(2)}) async-start(f32[8,56,128]{2,1,0:T(8,128)} %split.1), calls=%async_computation | async-start | bytes 458752 | tf_op jit(solution)/shard_map/all_to_all | solution.py:755
  14.6 5.7 %collective-permute-start.1 = (f32[3,128,128]{2,1,0:T(8,128)S(1)}, f32[3,128,128]{2,1,0:T(8,128)S(1)}, u32[]{:S(2)}, u32[]{:S(2)}) collective-permute-start(f32[3,128,128]{2,1,0:T(8,128)S(1)} %get-tuple-element.81), channel_id=1, source_target_pairs={{0,1},{1,0},{2,3},{3,2},{4,5},{5,4},{6,7},{7,6},{8,9},{9,8},{10,11... | collective-permute-start | bytes 589832 | tf_op jit(solution)/shard_map/ppermute | solution.py:744
  14.6 9.8 %collective-permute-start.2 = (f32[3,128,128]{2,1,0:T(8,128)S(1)}, f32[3,128,128]{2,1,0:T(8,128)S(1)}, u32[]{:S(2)}, u32[]{:S(2)}) collective-permute-start(f32[3,128,128]{2,1,0:T(8,128)S(1)} %get-tuple-element.85), channel_id=1, source_target_pairs={{1,2},{3,4},{5,6},{7,8},{9,10},{11,12},{13,14},{2,1},{4,3},{6,5},{... | collective-permute-start | bytes 589832 | tf_op jit(solution)/shard_map/ppermute | solution.py:743
  20.6 4.4 %collective-permute-start.3 = (f32[3,128,128]{2,1,0:T(8,128)S(1)}, f32[3,128,128]{2,1,0:T(8,128)S(1)}, u32[]{:S(2)}, u32[]{:S(2)}) collective-permute-start(f32[3,128,128]{2,1,0:T(8,128)S(1)} %get-tuple-element.89), channel_id=1, source_target_pairs={{0,1},{1,0},{2,3},{3,2},{4,5},{5,4},{6,7},{7,6},{8,9},{9,8},{10,11... | collective-permute-start | bytes 589832 | tf_op jit(solution)/shard_map/ppermute | solution.py:799
  21.6 9.1 %collective-permute-start.4 = (f32[3,128,128]{2,1,0:T(8,128)S(1)}, f32[3,128,128]{2,1,0:T(8,128)S(1)}, u32[]{:S(2)}, u32[]{:S(2)}) collective-permute-start(f32[3,128,128]{2,1,0:T(8,128)S(1)} %get-tuple-element.93), channel_id=1, source_target_pairs={{1,2},{3,4},{5,6},{7,8},{9,10},{11,12},{13,14},{2,1},{4,3},{6,5},{... | collective-permute-start | bytes 589832 | tf_op jit(solution)/shard_map/ppermute | solution.py:779
  25.3 5.9 %collective-permute-start.5 = (f32[3,128,128]{2,1,0:T(8,128)S(1)}, f32[3,128,128]{2,1,0:T(8,128)S(1)}, u32[]{:S(2)}, u32[]{:S(2)}) collective-permute-start(f32[3,128,128]{2,1,0:T(8,128)S(1)} %get-tuple-element.98), channel_id=1, source_target_pairs={{0,1},{1,0},{2,3},{3,2},{4,5},{5,4},{6,7},{7,6},{8,9},{9,8},{10,11... | collective-permute-start | bytes 589832 | tf_op jit(solution)/shard_map/ppermute | solution.py:799
  25.4 9.7 %collective-permute-start.6 = (f32[3,128,128]{2,1,0:T(8,128)S(1)}, f32[3,128,128]{2,1,0:T(8,128)S(1)}, u32[]{:S(2)}, u32[]{:S(2)}) collective-permute-start(f32[3,128,128]{2,1,0:T(8,128)S(1)} %get-tuple-element.102), channel_id=1, source_target_pairs={{1,2},{3,4},{5,6},{7,8},{9,10},{11,12},{13,14},{2,1},{4,3},{6,5},{... | collective-permute-start | bytes 589832 | tf_op jit(solution)/shard_map/ppermute | solution.py:818
  31.5 4.2 %collective-permute-start.7 = (f32[3,128,128]{2,1,0:T(8,128)S(1)}, f32[3,128,128]{2,1,0:T(8,128)S(1)}, u32[]{:S(2)}, u32[]{:S(2)}) collective-permute-start(f32[3,128,128]{2,1,0:T(8,128)S(1)} %get-tuple-element.107), channel_id=1, source_target_pairs={{0,1},{1,0},{2,3},{3,2},{4,5},{5,4},{6,7},{7,6},{8,9},{9,8},{10,11... | collective-permute-start | bytes 589832 | tf_op jit(solution)/shard_map/ppermute | solution.py:799
  32.2 9.1 %collective-permute-start.8 = (f32[3,128,128]{2,1,0:T(8,128)S(1)}, f32[3,128,128]{2,1,0:T(8,128)S(1)}, u32[]{:S(2)}, u32[]{:S(2)}) collective-permute-start(f32[3,128,128]{2,1,0:T(8,128)S(1)} %get-tuple-element.111), channel_id=1, source_target_pairs={{1,2},{3,4},{5,6},{7,8},{9,10},{11,12},{13,14},{2,1},{4,3},{6,5},{... | collective-permute-start | bytes 589832 | tf_op jit(solution)/shard_map/ppermute | solution.py:818
  36.0 5.9 %collective-permute-start.9 = (f32[3,128,128]{2,1,0:T(8,128)S(1)}, f32[3,128,128]{2,1,0:T(8,128)S(1)}, u32[]{:S(2)}, u32[]{:S(2)}) collective-permute-start(f32[3,128,128]{2,1,0:T(8,128)S(1)} %get-tuple-element.116), channel_id=1, source_target_pairs={{0,1},{1,0},{2,3},{3,2},{4,5},{5,4},{6,7},{7,6},{8,9},{9,8},{10,11... | collective-permute-start | bytes 589832 | tf_op jit(solution)/shard_map/ppermute | solution.py:799
  36.1 9.4 %collective-permute-start.10 = (f32[3,128,128]{2,1,0:T(8,128)S(1)}, f32[3,128,128]{2,1,0:T(8,128)S(1)}, u32[]{:S(2)}, u32[]{:S(2)}) collective-permute-start(f32[3,128,128]{2,1,0:T(8,128)S(1)} %get-tuple-element.120), channel_id=1, source_target_pairs={{1,2},{3,4},{5,6},{7,8},{9,10},{11,12},{13,14},{2,1},{4,3},{6,5},{... | collective-permute-start | bytes 589832 | tf_op jit(solution)/shard_map/ppermute | solution.py:818
  42.2 3.8 %collective-permute-start.11 = (f32[3,128,128]{2,1,0:T(8,128)S(1)}, f32[3,128,128]{2,1,0:T(8,128)S(1)}, u32[]{:S(2)}, u32[]{:S(2)}) collective-permute-start(f32[3,128,128]{2,1,0:T(8,128)S(1)} %get-tuple-element.125), channel_id=1, source_target_pairs={{0,1},{1,0},{2,3},{3,2},{4,5},{5,4},{6,7},{7,6},{8,9},{9,8},{10,11... | collective-permute-start | bytes 589832 | tf_op jit(solution)/shard_map/ppermute | solution.py:799
  42.3 9.1 %collective-permute-start.12 = (f32[3,128,128]{2,1,0:T(8,128)S(1)}, f32[3,128,128]{2,1,0:T(8,128)S(1)}, u32[]{:S(2)}, u32[]{:S(2)}) collective-permute-start(f32[3,128,128]{2,1,0:T(8,128)S(1)} %get-tuple-element.129), channel_id=1, source_target_pairs={{1,2},{3,4},{5,6},{7,8},{9,10},{11,12},{13,14},{2,1},{4,3},{6,5},{... | collective-permute-start | bytes 589832 | tf_op jit(solution)/shard_map/ppermute | solution.py:818

commit v17 on v14

--- a/solution.py
+++ b/solution.py
@@ -466,10 +466,10 @@
 
 def results_out(V, S, R, results, sems, cell):
     inside = pl.ds(PAD, R.shape[2])
-    pairs = [(V.at[i, cell, inside], results[0].at[i, cell]) for i in range(3)]
-    pairs += [(S.at[i, cell, inside], results[1].at[i, cell]) for i in range(6)]
-    pairs += [(R.at[i, cell], results[2].at[i, cell]) for i in range(6)]
-    return [pltpu.make_async_copy(*pair, sems.at[i]) for i, pair in enumerate(pairs)]
+    pairs = [(V.at[:, cell, inside], results[0]), (S.at[:, cell, inside], results[1]), (R.at[:, cell], results[2])]
+    return [
+        pltpu.make_async_copy(source, result.at[:, cell], sems.at[i]) for i, (source, result) in enumerate(pairs)
+    ]
 
 
 def start_all(copies):
@@ -558,18 +558,18 @@
     def _():
         copies = results_out(V, S, R, results, sems, 0)
         behind_bond(
-            V, S, R, coef_ref, here, surface, msg, missing, G, step, window, 0, lambda: start_all(copies[:3])
+            V, S, R, coef_ref, here, surface, msg, missing, G, step, window, 0, lambda: start_all(copies[:1])
         )
-        start_all(copies[3:])
+        start_all(copies[1:])
         wait_all(copies)
 
     @pl.when(jnp.logical_not(even))
     def _():
         copies = results_out(V, S, R, results, sems, 1)
         ahead_bond(
-            V, S, R, coef_ref, here, surface, msg, missing, G, step, window, 0, lambda: start_all(copies[:3])
+            V, S, R, coef_ref, here, surface, msg, missing, G, step, window, 0, lambda: start_all(copies[:1])
         )
-        start_all(copies[3:])
+        start_all(copies[1:])
         wait_all(copies)
 
 
@@ -659,31 +659,38 @@
                 panel = parts[s, pl.ds(comp * per * width + cell, per, stride=width), :]
                 force[s, comp, cell, pl.ds(4, per, stride=2), :] = scale * panel
                 force[s, comp, cell, pl.ds(5, per, stride=2), :] = scale * lane_roll(panel, FZ)
-
+    surface_loads(1, parts, loads, steps_table, surface, table, rows_out)
+
+
+def surface_kernel(parts, loads, steps_table, surface, table, rows_out):
+    surface_loads(STEPS, parts, loads, steps_table, surface, table, rows_out)
+
+
+def surface_loads(steps, parts, loads, steps_table, surface, table, rows_out):
     slots = loads.shape[0]
     tiles = parts.shape[0]
     mine = lax.rem(lax.axis_index("line"), tiles)
     table[...] = jnp.zeros(table.shape, jnp.float32)
     table[0:1, :] = lane_blocks(steps_table[0:8, :], slots)
-    table[STEPS + 1 : STEPS + 2, :] = lane_blocks(steps_table[8:16, :], slots)
+    table[steps + 1 : steps + 2, :] = lane_blocks(steps_table[8:16, :], slots)
     rows = [loads[...]]
-    for k in range(1, STEPS + 1):
+    for k in range(1, steps + 1):
         source = lax.rem(mine + (tiles - k), tiles)
         rows.append(parts[source, TRUCK_ROW : TRUCK_ROW + slots, :])
         table[k : k + 1, :] = parts[source, ENTRY_ROW : ENTRY_ROW + 1, :]
     columns = table[...].T
     rows_out[...] = jnp.zeros(rows_out.shape, jnp.float32)
-    for s in range(STEPS):
+    for s in range(steps):
         block = slice(s * slots, (s + 1) * slots)
         moved = []
-        for k in range(STEPS - s):
+        for k in range(steps - s):
             entry = jnp.broadcast_to(columns[block, k : k + 1], rows[k].shape)
             new = rows[k]
             for slot in range(slots):
                 new = jnp.where(entry == float(slot), rows[k + 1][slot : slot + 1, :], new)
             moved.append(new)
         rows = moved
-        cell = jnp.broadcast_to(columns[block, STEPS + 1 : STEPS + 2], rows[0].shape)
+        cell = jnp.broadcast_to(columns[block, steps + 1 : steps + 2], rows[0].shape)
         for c in range(2):
             load = jnp.sum(jnp.where(cell == float(c), rows[0], 0.0), axis=0, keepdims=True)
             rows_out[2 * s + c : 2 * s + c + 1, :] = load
@@ -792,15 +799,19 @@
     )
     groups = [list(range(at, at + GROUP)) for at in range(0, tiles, GROUP)]
     parts = lax.all_to_all(parts, "line", 0, 0, axis_index_groups=groups, tiled=True)
+    square = pltpu.VMEM((across, depth), f32)
+    turned = (pltpu.VMEM((depth, depth), f32), pltpu.VMEM((depth, across), f32))
+    ins = (parts, in_vmem(loads), in_vmem(steps_table))
     force, surface = call(
         prepare_kernel,
-        (parts, in_vmem(loads), in_vmem(steps_table)),
+        ins,
         (WHOLE,) * 3,
-        (pltpu.VMEM((STEPS, 3, 3, 16, depth), f32), pltpu.VMEM((across, depth), f32)),
+        (pltpu.VMEM((STEPS, 3, 3, 16, depth), f32), square),
         (WHOLE,) * 2,
-        scratch=(pltpu.VMEM((depth, depth), f32), pltpu.VMEM((depth, across), f32)),
+        scratch=turned,
         name="prepare",
     )
+    later = call(surface_kernel, ins, (WHOLE,) * 3, square, WHOLE, scratch=turned, name="surface")
     V, early = call(
         functools.partial(first_kernel, window),
         tuple(in_vmem(x) for x in (V, S, R, coef, force, surface)),
@@ -826,12 +837,14 @@
             (WHOLE,) * len(ins),
             outs,
             (WHOLE,) * 5 if more else (WHOLE,) * 3 + (ANYWHERE,) * 3,
-            scratch=(ghost,) if more else (dma((15,)), ghost),
+            scratch=(ghost,) if more else (dma((3,)), ghost),
             aliases=same,
             name="near" + str(step),
         )
         if more:
             msg_near = [lax.ppermute(plane, "line", near) for plane in msg]
+        if step == 0:
+            surface = later
         ins = (V, S, R, coef, force, surface, msg_far) + ((missing,) if step else ())
         ins = tuple(in_vmem(x) for x in ins)
         if more:
@@ -855,7 +868,7 @@
         (WHOLE,) * 8 + (ANYWHERE,) * 3,
         state + results,
         (WHOLE,) * 3 + (ANYWHERE,) * 3,
-        scratch=(ghost, dma((15,))),
+        scratch=(ghost, dma((3,))),
         aliases={**same, 8: 3, 9: 4, 10: 5},
         name="last",
     )

time: 52.4 us -> 52.3 us (level)
    ppermute x4, starting transfers between devices: 12.5 us -> 11.9 us  [body(): early = lax.ppermute(msg[0], 'line', far)]
    pallas_call x17 -> x18, Pallas kernels: 11 us -> 11.2 us  [call(): pl.pallas_call(kernel, out_shape=outs, in_specs=specs, out_specs=out_spec...]
  transfers between devices with their start and end apart: 20 -> 20, of which waited for: 7 -> 5; matrix products, arithmetic and copies ran while one was open for 0% -> 0% of each run, Pallas kernels for 16% -> 16%
where the time goes in v17:
time: 52.3 us; the launch traced here: 51.9 us
  starting transfers between devices  30.4 us (58%)
  Pallas kernels  11.2 us (21%)
  waiting for transfers between devices  9.33 us (18%)
  between operations  0.93 us (2%)
    ppermute x4, starting transfers between devices, body(): early = lax.ppermute(msg[0], 'line', far)  11.9 us
    pallas_call x18, Pallas kernels, call(): pl.pallas_call(kernel, out_shape=outs, in_specs=specs, out_specs=out_spec...  11.2 us
    all_to_all x1, starting transfers between devices, body(): lax.all_to_all(parts, 'line', 0, 0, axis_index_groups=groups, tiled=True)  6.3 us
    ppermute x4, waiting for transfers between devices, body(): early = lax.ppermute(msg[0], 'line', far)  5.51 us
    ppermute x1, starting transfers between devices, body(): early = lax.ppermute(early, 'line', far)  3.74 us
    ppermute x1, starting transfers between devices, body(): msg_far = lax.ppermute(msg_far, 'line', far)  3.53 us
    ppermute x10, starting transfers between devices, body(): msg_near = [lax.ppermute(plane, 'line', near) for plane in msg]  3.13 us
    ppermute x1, waiting for transfers between devices, ahead_by(): lax.ppermute(x, 'line', [(i, i + distance) for i in range(tiles - distanc...  2.85 us
  transfers between devices with their start and end apart: 20, of which 5 were waited for; matrix products, arithmetic and copies ran while one was open for 0% of the time, Pallas kernels for 16%

profile of v17, /device:TPU:17, one launch (start us, length us, event | category | flops | bytes accessed | tf_op | source)
XLA Modules:
  0.0 51.9 jit_solution(144586001326431970)
XLA Ops:
  0.6 0.9 %pack.1 = (f32[8,1920]{1,0:T(8,128)S(1)}, f32[16,128]{1,0:T(8,128)S(1)}, f32[16,128]{1,0:T(8,128)S(1)}, s32[1,8]{1,0:T(1,128)S(1)}) custom-call(f32[8,1536]{1,0:T(8,128)} %bitcast.3, f32[16,128]{1,0:T(8,128)} %loads_in.1, s32[6,16]{1,0:T(8,128)} %entries_in.1, s32[6,16]{1,0:T(8,128)} %cells_in.1, s32[1,8]{1,0:T(1,128)} %bitcast.4), custom_call_target="tpu_custom_call" | custom-call | flops 1 | bytes 1 | tf_op jit(solution)/shard_map/pack/pallas_call | solution.py:710
  1.5 1.3 %collective-permute-start = (f32[8,1920]{1,0:T(8,128)S(1)}, f32[8,1920]{1,0:T(8,128)S(1)}, u32[]{:S(2)}, u32[]{:S(2)}) collective-permute-start(f32[8,1920]{1,0:T(8,128)S(1)} %get-tuple-element.81.own), channel_id=1, source_target_pairs={{0,8},{1,9},{2,10},{3,11},{4,12},{5,13},{6,14},{7,15},{16,24},{17,... | collective-permute-start | bytes 184328 | tf_op jit(solution)/shard_map/ppermute | solution.py:748
  2.8 1.8 %start.1 = (f32[3,2,144,128]{3,2,1,0:T(8,128)S(1)}, f32[6,2,144,128]{3,2,1,0:T(8,128)S(1)}, f32[6,2,128,128]{3,2,1,0:T(8,128)S(1)}, f32[16,128]{1,0:T(8,128)S(1)...) custom-call(f32[3,2,128,128]{3,2,1,0:T(8,128)} %velocity.1, ...), custom_call_target="tpu_custom_call" | custom-call | flops 8388608 | bytes 8388608 | tf_op jit(solution)/shard_map/start/pallas_call | solution.py:710
  4.6 2.8 %collective-permute-done.behind = f32[8,1920]{1,0:T(8,128)S(1)} collective-permute-done((f32[8,1920]{1,0:T(8,128)S(1)}, f32[8,1920]{1,0:T(8,128)S(1)}, u32[]{:S(2)}, u32[]{:S(2)}) %collective-permute-start) | collective-permute-done | bytes 61472 | tf_op jit(solution)/shard_map/ppermute | solution.py:748
  7.4 0.9 %split.1 = f32[8,56,128]{2,1,0:T(8,128)} custom-call(f32[8,1920]{1,0:T(8,128)S(1)} %get-tuple-element.81.own, f32[8,1920]{1,0:T(8,128)S(1)} %collective-permute-done.behind, s32[1,8]{1,0:T(1,128)S(1)} %get-tuple-element.82.cells, f32[16,128]{1,0:T(8,128)S(1)} %get-tuple-element.80.after_this.coef_ref), custom_call_target="tpu_custom_call" | custom-call | flops 1 | bytes 1 | tf_op jit(solution)/shard_map/split/pallas_call | solution.py:710
  8.3 6.3 %all-to-all-start = ((f32[8,56,128]{2,1,0:T(8,128)}), f32[8,56,128]{2,1,0:T(8,128)S(1)}, u32[]{:S(2)}, u32[]{:S(2)}) async-start(f32[8,56,128]{2,1,0:T(8,128)} %split.1), calls=%async_computation | async-start | bytes 458752 | tf_op jit(solution)/shard_map/all_to_all | solution.py:801
  14.6 0.0 collective-permute-start.1
  14.6 0.5 collective-permute-start.2
  15.1 3.5 %collective-permute-start.3 = (f32[3,128,128]{2,1,0:T(8,128)S(1)}, f32[3,128,128]{2,1,0:T(8,128)S(1)}, u32[]{:S(2)}, u32[]{:S(2)}) collective-permute-start(f32[3,128,128]{2,1,0:T(8,128)S(1)} %get-tuple-element.92), channel_id=1, source_target_pairs={{1,2},{3,4},{5,6},{7,8},{9,10},{11,12},{13,14},{2,1},{4,3},{6,5},{... | collective-permute-start | bytes 589832 | tf_op jit(solution)/shard_map/ppermute | solution.py:790
  18.6 0.9 %all-to-all-done.parts = f32[8,56,128]{2,1,0:T(8,128)S(1)} async-done(((f32[8,56,128]{2,1,0:T(8,128)}), f32[8,56,128]{2,1,0:T(8,128)S(1)}, u32[]{:S(2)}, u32[]{:S(2)}) %all-to-all-start) | async-done | bytes 229408 | tf_op jit(solution)/shard_map/all_to_all | solution.py:801
  19.6 0.3 prepare.1
  19.9 0.3 first.1
  20.2 3.7 %collective-permute-start.6 = (f32[3,128,128]{2,1,0:T(8,128)S(1)}, f32[3,128,128]{2,1,0:T(8,128)S(1)}, u32[]{:S(2)}, u32[]{:S(2)}) collective-permute-start(f32[3,128,128]{2,1,0:T(8,128)S(1)} %get-tuple-element.101), channel_id=1, source_target_pairs={{1,2},{3,4},{5,6},{7,8},{9,10},{11,12},{13,14},{2,1},{4,3},{6,5},{... | collective-permute-start | bytes 589832 | tf_op jit(solution)/shard_map/ppermute | solution.py:825
  24.0 0.0 collective-permute-done.1.upper
  24.0 0.3 near0.1
  24.3 0.1 collective-permute-start.4
  24.3 0.5 collective-permute-start.5
  24.8 0.6 %surface.1 = f32[128,128]{1,0:T(8,128)S(1)} custom-call(f32[8,56,128]{2,1,0:T(8,128)S(1)} %all-to-all-done.parts, f32[16,128]{1,0:T(8,128)S(1)} %get-tuple-element.83.loads, f32[16,128]{1,0:T(8,128)S(1)} %get-tuple-element.76.after_this.steps_table), custom_call_target="tpu_custom_call" | custom-call | flops 1 | bytes 1 | tf_op jit(solution)/shard_map/surface/pallas_call | solution.py:710
  25.4 0.0 collective-permute-done.3.msg
  25.4 0.6 %far0.1 = (f32[3,2,144,128]{3,2,1,0:T(8,128)S(1)}, f32[6,2,144,128]{3,2,1,0:T(8,128)S(1)}, f32[6,2,128,128]{3,2,1,0:T(8,128)S(1)}, f32[3,128,128]{2,1,0:T(8,128)S(1)}, f32[3,128,128]{2,1,0:T(8,128)S(1)}) custom-call(f32[3,2,144,128]{3,2,1,0:T(8,128)S(1)} %get-tuple-element.89.V0, ...), custom_call_target="tpu_custom_call", output_to_operand_aliasing={{0}: (0, {}), {1}: (1, {}), {2}: (2, {})} | custom-call | flops 1 | bytes 1 | tf_op jit(solution)/shard_map/far0/pallas_call | solution.py:710
  26.0 0.0 collective-permute-done.4.upper
  26.1 0.3 near1.1
  26.3 0.1 collective-permute-start.7
  26.5 0.4 collective-permute-start.8
  26.9 3.0 %collective-permute-start.9 = (f32[3,128,128]{2,1,0:T(8,128)S(1)}, f32[3,128,128]{2,1,0:T(8,128)S(1)}, u32[]{:S(2)}, u32[]{:S(2)}) collective-permute-start(f32[3,128,128]{2,1,0:T(8,128)S(1)} %get-tuple-element.111), channel_id=1, source_target_pairs={{1,2},{3,4},{5,6},{7,8},{9,10},{11,12},{13,14},{2,1},{4,3},{6,5},{... | collective-permute-start | bytes 589832 | tf_op jit(solution)/shard_map/ppermute | solution.py:864
  30.0 0.0 collective-permute-done.6.msg
  30.0 0.6 %far1.1 = (f32[3,2,144,128]{3,2,1,0:T(8,128)S(1)}, f32[6,2,144,128]{3,2,1,0:T(8,128)S(1)}, f32[6,2,128,128]{3,2,1,0:T(8,128)S(1)}, f32[3,128,128]{2,1,0:T(8,128)S(1)}, f32[3,128,128]{2,1,0:T(8,128)S(1)}) custom-call(f32[3,2,144,128]{3,2,1,0:T(8,128)S(1)} %get-tuple-element.98.V0, ...), custom_call_target="tpu_custom_call", output_to_operand_aliasing={{0}: (0, {}), {1}: (1, {}), {2}: (2, {})} | custom-call | flops 1 | bytes 1 | tf_op jit(solution)/shard_map/far1/pallas_call | solution.py:710
  30.6 3.1 %collective-permute-start.12 = (f32[3,128,128]{2,1,0:T(8,128)S(1)}, f32[3,128,128]{2,1,0:T(8,128)S(1)}, u32[]{:S(2)}, u32[]{:S(2)}) collective-permute-start(f32[3,128,128]{2,1,0:T(8,128)S(1)} %get-tuple-element.121), channel_id=1, source_target_pairs={{1,2},{3,4},{5,6},{7,8},{9,10},{11,12},{13,14},{2,1},{4,3},{6,5},{... | collective-permute-start | bytes 589832 | tf_op jit(solution)/shard_map/ppermute | solution.py:864
  33.7 0.0 collective-permute-done.8.lower
  33.7 0.3 near2.1
  34.0 0.4 collective-permute-start.10
  34.4 0.2 collective-permute-start.11
  34.6 1.4 %collective-permute-done.9.msg = f32[3,128,128]{2,1,0:T(8,128)S(1)} collective-permute-done((f32[3,128,128]{2,1,0:T(8,128)S(1)}, f32[3,128,128]{2,1,0:T(8,128)S(1)}, u32[]{:S(2)}, u32[]{:S(2)}) %collective-permute-start.9) | collective-permute-done | bytes 196640 | tf_op jit(solution)/shard_map/ppermute | solution.py:864
  36.0 0.6 %far2.1 = (f32[3,2,144,128]{3,2,1,0:T(8,128)S(1)}, f32[6,2,144,128]{3,2,1,0:T(8,128)S(1)}, f32[6,2,128,128]{3,2,1,0:T(8,128)S(1)}, f32[3,128,128]{2,1,0:T(8,128)S(1)}, f32[3,128,128]{2,1,0:T(8,128)S(1)}) custom-call(f32[3,2,144,128]{3,2,1,0:T(8,128)S(1)} %get-tuple-element.108.V0, ...), custom_call_target="tpu_custom_call", output_to_operand_aliasing={{0}: (0, {}), {1}: (1, {}), {2}: (2, {})} | custom-call | flops 1 | bytes 1 | tf_op jit(solution)/shard_map/far2/pallas_call | solution.py:710
  36.6 0.3 near3.1
  36.9 0.1 collective-permute-start.13
  37.0 0.5 collective-permute-start.14
  37.5 3.1 %collective-permute-start.15 = (f32[3,128,128]{2,1,0:T(8,128)S(1)}, f32[3,128,128]{2,1,0:T(8,128)S(1)}, u32[]{:S(2)}, u32[]{:S(2)}) collective-permute-start(f32[3,128,128]{2,1,0:T(8,128)S(1)} %get-tuple-element.131), channel_id=1, source_target_pairs={{1,2},{3,4},{5,6},{7,8},{9,10},{11,12},{13,14},{2,1},{4,3},{6,5},{... | collective-permute-start | bytes 589832 | tf_op jit(solution)/shard_map/ppermute | solution.py:864
  40.6 0.6 %far3.1 = (f32[3,2,144,128]{3,2,1,0:T(8,128)S(1)}, f32[6,2,144,128]{3,2,1,0:T(8,128)S(1)}, f32[6,2,128,128]{3,2,1,0:T(8,128)S(1)}, f32[3,128,128]{2,1,0:T(8,128)S(1)}, f32[3,128,128]{2,1,0:T(8,128)S(1)}) custom-call(f32[3,2,144,128]{3,2,1,0:T(8,128)S(1)} %get-tuple-element.118.V0, ...), custom_call_target="tpu_custom_call", output_to_operand_aliasing={{0}: (0, {}), {1}: (1, {}), {2}: (2, {})} | custom-call | flops 1 | bytes 1 | tf_op jit(solution)/shard_map/far3/pallas_call | solution.py:710
  41.2 2.7 %collective-permute-start.18 = (f32[3,128,128]{2,1,0:T(8,128)S(1)}, f32[3,128,128]{2,1,0:T(8,128)S(1)}, u32[]{:S(2)}, u32[]{:S(2)}) collective-permute-start(f32[3,128,128]{2,1,0:T(8,128)S(1)} %get-tuple-element.141), channel_id=1, source_target_pairs={{1,2},{3,4},{5,6},{7,8},{9,10},{11,12},{13,14},{2,1},{4,3},{6,5},{... | collective-permute-start | bytes 589832 | tf_op jit(solution)/shard_map/ppermute | solution.py:864
  44.0 0.3 near4.1
  44.2 0.8 %collective-permute-start.16 = (f32[3,64,128]{2,1,0:T(8,128)S(1)}, f32[3,64,128]{2,1,0:T(8,128)S(1)}, u32[]{:S(2)}, u32[]{:S(2)}) collective-permute-start(f32[3,64,128]{2,1,0:T(8,128)S(1)} %get-tuple-element.136), channel_id=1, source_target_pairs={{0,1},{1,0},{2,3},{3,2},{4,5},{5,4},{6,7},{7,6},{8,9},{9,8},{10,11... | collective-permute-start | bytes 294920 | tf_op jit(solution)/shard_map/ppermute | solution.py:845
  45.0 0.1 collective-permute-start.17
  45.1 1.8 %collective-permute-done.15.msg = f32[3,128,128]{2,1,0:T(8,128)S(1)} collective-permute-done((f32[3,128,128]{2,1,0:T(8,128)S(1)}, f32[3,128,128]{2,1,0:T(8,128)S(1)}, u32[]{:S(2)}, u32[]{:S(2)}) %collective-permute-start.15) | collective-permute-done | bytes 196640 | tf_op jit(solution)/shard_map/ppermute | solution.py:864
  46.9 0.5 far4.1
  47.4 1.1 %near5.1 = (f32[3,2,144,128]{3,2,1,0:T(8,128)S(1)}, f32[6,2,144,128]{3,2,1,0:T(8,128)S(1)}, f32[6,2,128,128]{3,2,1,0:T(8,128)S(1)}, f32[3,2,128,128]{3,2,1,0:T(8...) custom-call(f32[3,2,144,128]{3,2,1,0:T(8,128)S(1)} %get-tuple-elemen, ...), custom_call_target="tpu_custom_call", output_to_operand_aliasing={{0}: (0, {}), {1}: (1, {}), {2}: (2, {})} | custom-call | flops 1 | bytes 1 | tf_op jit(solution)/shard_map/near5/pallas_call | solution.py:710
  48.5 2.3 %collective-permute-done.18.msg = f32[3,128,128]{2,1,0:T(8,128)S(1)} collective-permute-done((f32[3,128,128]{2,1,0:T(8,128)S(1)}, f32[3,128,128]{2,1,0:T(8,128)S(1)}, u32[]{:S(2)}, u32[]{:S(2)}) %collective-permute-start.18) | collective-permute-done | bytes 196640 | tf_op jit(solution)/shard_map/ppermute | solution.py:864
  50.8 1.1 %last.1 = (f32[3,2,144,128]{3,2,1,0:T(8,128)S(1)}, f32[6,2,144,128]{3,2,1,0:T(8,128)S(1)}, f32[6,2,128,128]{3,2,1,0:T(8,128)S(1)}, f32[3,2,128,128]{3,2,1,0:T(8,...) custom-call(f32[3,2,144,128]{3,2,1,0:T(8,128)S(1)} %get-tuple-elemen, ...), custom_call_target="tpu_custom_call", output_to_operand_aliasing={{0}: (0, {}), {1}: (1, {}), {2}: (2, {}), {3}: (8, {}), {4}... | custom-call | flops 1 | bytes 1 | tf_op jit(solution)/shard_map/last/pallas_call | solution.py:710
  (10 shorter events, 0.0 us)
Async XLA Ops:
  1.5 5.9 %collective-permute-start = (f32[8,1920]{1,0:T(8,128)S(1)}, f32[8,1920]{1,0:T(8,128)S(1)}, u32[]{:S(2)}, u32[]{:S(2)}) collective-permute-start(f32[8,1920]{1,0:T(8,128)S(1)} %get-tuple-element.81.own), channel_id=1, source_target_pairs={{0,8},{1,9},{2,10},{3,11},{4,12},{5,13},{6,14},{7,15},{16,24},{17,... | collective-permute-start | bytes 184328 | tf_op jit(solution)/shard_map/ppermute | solution.py:748
  8.3 11.3 %all-to-all-start = ((f32[8,56,128]{2,1,0:T(8,128)}), f32[8,56,128]{2,1,0:T(8,128)S(1)}, u32[]{:S(2)}, u32[]{:S(2)}) async-start(f32[8,56,128]{2,1,0:T(8,128)} %split.1), calls=%async_computation | async-start | bytes 458752 | tf_op jit(solution)/shard_map/all_to_all | solution.py:801
  14.6 9.4 %collective-permute-start.1 = (f32[3,64,128]{2,1,0:T(8,128)S(1)}, f32[3,64,128]{2,1,0:T(8,128)S(1)}, u32[]{:S(2)}, u32[]{:S(2)}) collective-permute-start(f32[3,64,128]{2,1,0:T(8,128)S(1)} %get-tuple-element.87), channel_id=1, source_target_pairs={{0,1},{1,0},{2,3},{3,2},{4,5},{5,4},{6,7},{7,6},{8,9},{9,8},{10,11... | collective-permute-start | bytes 294920 | tf_op jit(solution)/shard_map/ppermute | solution.py:791
  14.6 9.4 %collective-permute-start.2 = (f32[3,64,128]{2,1,0:T(8,128)S(1)}, f32[3,64,128]{2,1,0:T(8,128)S(1)}, u32[]{:S(2)}, u32[]{:S(2)}) collective-permute-start(f32[3,64,128]{2,1,0:T(8,128)S(1)} %get-tuple-element.88), channel_id=1, source_target_pairs={{0,1},{1,0},{2,3},{3,2},{4,5},{5,4},{6,7},{7,6},{8,9},{9,8},{10,11... | collective-permute-start | bytes 294920 | tf_op jit(solution)/shard_map/ppermute | solution.py:791
  15.1 10.3 %collective-permute-start.3 = (f32[3,128,128]{2,1,0:T(8,128)S(1)}, f32[3,128,128]{2,1,0:T(8,128)S(1)}, u32[]{:S(2)}, u32[]{:S(2)}) collective-permute-start(f32[3,128,128]{2,1,0:T(8,128)S(1)} %get-tuple-element.92), channel_id=1, source_target_pairs={{1,2},{3,4},{5,6},{7,8},{9,10},{11,12},{13,14},{2,1},{4,3},{6,5},{... | collective-permute-start | bytes 589832 | tf_op jit(solution)/shard_map/ppermute | solution.py:790
  20.2 9.8 %collective-permute-start.6 = (f32[3,128,128]{2,1,0:T(8,128)S(1)}, f32[3,128,128]{2,1,0:T(8,128)S(1)}, u32[]{:S(2)}, u32[]{:S(2)}) collective-permute-start(f32[3,128,128]{2,1,0:T(8,128)S(1)} %get-tuple-element.101), channel_id=1, source_target_pairs={{1,2},{3,4},{5,6},{7,8},{9,10},{11,12},{13,14},{2,1},{4,3},{6,5},{... | collective-permute-start | bytes 589832 | tf_op jit(solution)/shard_map/ppermute | solution.py:825
  24.3 1.8 %collective-permute-start.4 = (f32[3,64,128]{2,1,0:T(8,128)S(1)}, f32[3,64,128]{2,1,0:T(8,128)S(1)}, u32[]{:S(2)}, u32[]{:S(2)}) collective-permute-start(f32[3,64,128]{2,1,0:T(8,128)S(1)} %get-tuple-element.96), channel_id=1, source_target_pairs={{0,1},{1,0},{2,3},{3,2},{4,5},{5,4},{6,7},{7,6},{8,9},{9,8},{10,11... | collective-permute-start | bytes 294920 | tf_op jit(solution)/shard_map/ppermute | solution.py:845
  24.3 1.7 %collective-permute-start.5 = (f32[3,64,128]{2,1,0:T(8,128)S(1)}, f32[3,64,128]{2,1,0:T(8,128)S(1)}, u32[]{:S(2)}, u32[]{:S(2)}) collective-permute-start(f32[3,64,128]{2,1,0:T(8,128)S(1)} %get-tuple-element.97), channel_id=1, source_target_pairs={{0,1},{1,0},{2,3},{3,2},{4,5},{5,4},{6,7},{7,6},{8,9},{9,8},{10,11... | collective-permute-start | bytes 294920 | tf_op jit(solution)/shard_map/ppermute | solution.py:845
  26.3 7.4 %collective-permute-start.7 = (f32[3,64,128]{2,1,0:T(8,128)S(1)}, f32[3,64,128]{2,1,0:T(8,128)S(1)}, u32[]{:S(2)}, u32[]{:S(2)}) collective-permute-start(f32[3,64,128]{2,1,0:T(8,128)S(1)} %get-tuple-element.106), channel_id=1, source_target_pairs={{0,1},{1,0},{2,3},{3,2},{4,5},{5,4},{6,7},{7,6},{8,9},{9,8},{10,11... | collective-permute-start | bytes 294920 | tf_op jit(solution)/shard_map/ppermute | solution.py:845
  26.5 7.3 %collective-permute-start.8 = (f32[3,64,128]{2,1,0:T(8,128)S(1)}, f32[3,64,128]{2,1,0:T(8,128)S(1)}, u32[]{:S(2)}, u32[]{:S(2)}) collective-permute-start(f32[3,64,128]{2,1,0:T(8,128)S(1)} %get-tuple-element.107), channel_id=1, source_target_pairs={{0,1},{1,0},{2,3},{3,2},{4,5},{5,4},{6,7},{7,6},{8,9},{9,8},{10,11... | collective-permute-start | bytes 294920 | tf_op jit(solution)/shard_map/ppermute | solution.py:845
  26.9 9.1 %collective-permute-start.9 = (f32[3,128,128]{2,1,0:T(8,128)S(1)}, f32[3,128,128]{2,1,0:T(8,128)S(1)}, u32[]{:S(2)}, u32[]{:S(2)}) collective-permute-start(f32[3,128,128]{2,1,0:T(8,128)S(1)} %get-tuple-element.111), channel_id=1, source_target_pairs={{1,2},{3,4},{5,6},{7,8},{9,10},{11,12},{13,14},{2,1},{4,3},{6,5},{... | collective-permute-start | bytes 589832 | tf_op jit(solution)/shard_map/ppermute | solution.py:864
  30.6 9.9 %collective-permute-start.12 = (f32[3,128,128]{2,1,0:T(8,128)S(1)}, f32[3,128,128]{2,1,0:T(8,128)S(1)}, u32[]{:S(2)}, u32[]{:S(2)}) collective-permute-start(f32[3,128,128]{2,1,0:T(8,128)S(1)} %get-tuple-element.121), channel_id=1, source_target_pairs={{1,2},{3,4},{5,6},{7,8},{9,10},{11,12},{13,14},{2,1},{4,3},{6,5},{... | collective-permute-start | bytes 589832 | tf_op jit(solution)/shard_map/ppermute | solution.py:864
  34.0 2.6 %collective-permute-start.10 = (f32[3,64,128]{2,1,0:T(8,128)S(1)}, f32[3,64,128]{2,1,0:T(8,128)S(1)}, u32[]{:S(2)}, u32[]{:S(2)}) collective-permute-start(f32[3,64,128]{2,1,0:T(8,128)S(1)} %get-tuple-element.116), channel_id=1, source_target_pairs={{0,1},{1,0},{2,3},{3,2},{4,5},{5,4},{6,7},{7,6},{8,9},{9,8},{10,11... | collective-permute-start | bytes 294920 | tf_op jit(solution)/shard_map/ppermute | solution.py:845
  34.4 2.2 %collective-permute-start.11 = (f32[3,64,128]{2,1,0:T(8,128)S(1)}, f32[3,64,128]{2,1,0:T(8,128)S(1)}, u32[]{:S(2)}, u32[]{:S(2)}) collective-permute-start(f32[3,64,128]{2,1,0:T(8,128)S(1)} %get-tuple-element.117), channel_id=1, source_target_pairs={{0,1},{1,0},{2,3},{3,2},{4,5},{5,4},{6,7},{7,6},{8,9},{9,8},{10,11... | collective-permute-start | bytes 294920 | tf_op jit(solution)/shard_map/ppermute | solution.py:845
  36.9 7.0 %collective-permute-start.13 = (f32[3,64,128]{2,1,0:T(8,128)S(1)}, f32[3,64,128]{2,1,0:T(8,128)S(1)}, u32[]{:S(2)}, u32[]{:S(2)}) collective-permute-start(f32[3,64,128]{2,1,0:T(8,128)S(1)} %get-tuple-element.126), channel_id=1, source_target_pairs={{0,1},{1,0},{2,3},{3,2},{4,5},{5,4},{6,7},{7,6},{8,9},{9,8},{10,11... | collective-permute-start | bytes 294920 | tf_op jit(solution)/shard_map/ppermute | solution.py:845
  37.0 7.0 %collective-permute-start.14 = (f32[3,64,128]{2,1,0:T(8,128)S(1)}, f32[3,64,128]{2,1,0:T(8,128)S(1)}, u32[]{:S(2)}, u32[]{:S(2)}) collective-permute-start(f32[3,64,128]{2,1,0:T(8,128)S(1)} %get-tuple-element.127), channel_id=1, source_target_pairs={{0,1},{1,0},{2,3},{3,2},{4,5},{5,4},{6,7},{7,6},{8,9},{9,8},{10,11... | collective-permute-start | bytes 294920 | tf_op jit(solution)/shard_map/ppermute | solution.py:845
  37.5 9.4 %collective-permute-start.15 = (f32[3,128,128]{2,1,0:T(8,128)S(1)}, f32[3,128,128]{2,1,0:T(8,128)S(1)}, u32[]{:S(2)}, u32[]{:S(2)}) collective-permute-start(f32[3,128,128]{2,1,0:T(8,128)S(1)} %get-tuple-element.131), channel_id=1, source_target_pairs={{1,2},{3,4},{5,6},{7,8},{9,10},{11,12},{13,14},{2,1},{4,3},{6,5},{... | collective-permute-start | bytes 589832 | tf_op jit(solution)/shard_map/ppermute | solution.py:864
  41.2 9.6 %collective-permute-start.18 = (f32[3,128,128]{2,1,0:T(8,128)S(1)}, f32[3,128,128]{2,1,0:T(8,128)S(1)}, u32[]{:S(2)}, u32[]{:S(2)}) collective-permute-start(f32[3,128,128]{2,1,0:T(8,128)S(1)} %get-tuple-element.141), channel_id=1, source_target_pairs={{1,2},{3,4},{5,6},{7,8},{9,10},{11,12},{13,14},{2,1},{4,3},{6,5},{... | collective-permute-start | bytes 589832 | tf_op jit(solution)/shard_map/ppermute | solution.py:864
  44.2 3.1 %collective-permute-start.16 = (f32[3,64,128]{2,1,0:T(8,128)S(1)}, f32[3,64,128]{2,1,0:T(8,128)S(1)}, u32[]{:S(2)}, u32[]{:S(2)}) collective-permute-start(f32[3,64,128]{2,1,0:T(8,128)S(1)} %get-tuple-element.136), channel_id=1, source_target_pairs={{0,1},{1,0},{2,3},{3,2},{4,5},{5,4},{6,7},{7,6},{8,9},{9,8},{10,11... | collective-permute-start | bytes 294920 | tf_op jit(solution)/shard_map/ppermute | solution.py:845
  45.0 2.3 %collective-permute-start.17 = (f32[3,64,128]{2,1,0:T(8,128)S(1)}, f32[3,64,128]{2,1,0:T(8,128)S(1)}, u32[]{:S(2)}, u32[]{:S(2)}) collective-permute-start(f32[3,64,128]{2,1,0:T(8,128)S(1)} %get-tuple-element.137), channel_id=1, source_target_pairs={{0,1},{1,0},{2,3},{3,2},{4,5},{5,4},{6,7},{7,6},{8,9},{9,8},{10,11... | collective-permute-start | bytes 294920 | tf_op jit(solution)/shard_map/ppermute | solution.py:845

commit v18 on v17

--- a/solution.py
+++ b/solution.py
@@ -9,6 +9,7 @@
 from jax.sharding import PartitionSpec as P
 
 STEPS = 6
+SOON = 3
 FY = 8
 FZ = 64
 DT = 0.25
@@ -659,7 +660,7 @@
                 panel = parts[s, pl.ds(comp * per * width + cell, per, stride=width), :]
                 force[s, comp, cell, pl.ds(4, per, stride=2), :] = scale * panel
                 force[s, comp, cell, pl.ds(5, per, stride=2), :] = scale * lane_roll(panel, FZ)
-    surface_loads(1, parts, loads, steps_table, surface, table, rows_out)
+    surface_loads(SOON, parts, loads, steps_table, surface, table, rows_out)
 
 
 def surface_kernel(parts, loads, steps_table, surface, table, rows_out):
@@ -843,7 +844,7 @@
         )
         if more:
             msg_near = [lax.ppermute(plane, "line", near) for plane in msg]
-        if step == 0:
+        if step == SOON - 1:
             surface = later
         ins = (V, S, R, coef, force, surface, msg_far) + ((missing,) if step else ())
         ins = tuple(in_vmem(x) for x in ins)

time: 52.3 us -> 52.1 us (level)
  waiting for transfers between devices: 9.33 us -> 8.78 us
    ppermute x4, waiting for transfers between devices: 5.51 us -> 4.63 us  [body(): early = lax.ppermute(msg[0], 'line', far)]
    ppermute x4, starting transfers between devices: 11.9 us -> 12.5 us  [body(): early = lax.ppermute(msg[0], 'line', far)]
  transfers between devices with their start and end apart: 20 -> 20, of which waited for: 5 -> 7; matrix products, arithmetic and copies ran while one was open for 0% -> 0% of each run, Pallas kernels for 16% -> 16%
where the time goes in v18:
time: 52.1 us; the launch traced here: 51.6 us
  starting transfers between devices  30.7 us (59%)
  Pallas kernels  11.2 us (21%)
  waiting for transfers between devices  8.78 us (17%)
  between operations  0.91 us (2%)
    ppermute x4, starting transfers between devices, body(): early = lax.ppermute(msg[0], 'line', far)  12.5 us
    pallas_call x18, Pallas kernels, call(): pl.pallas_call(kernel, out_shape=outs, in_specs=specs, out_specs=out_spec...  11.2 us
    all_to_all x1, starting transfers between devices, body(): lax.all_to_all(parts, 'line', 0, 0, axis_index_groups=groups, tiled=True)  6.3 us
    ppermute x4, waiting for transfers between devices, body(): early = lax.ppermute(msg[0], 'line', far)  4.63 us
    ppermute x1, starting transfers between devices, body(): early = lax.ppermute(early, 'line', far)  3.74 us
    ppermute x1, starting transfers between devices, body(): msg_far = lax.ppermute(msg_far, 'line', far)  3.53 us
    ppermute x10, starting transfers between devices, body(): msg_near = [lax.ppermute(plane, 'line', near) for plane in msg]  2.89 us
    ppermute x1, waiting for transfers between devices, ahead_by(): lax.ppermute(x, 'line', [(i, i + distance) for i in range(tiles - distanc...  2.85 us
  transfers between devices with their start and end apart: 20, of which 7 were waited for; matrix products, arithmetic and copies ran while one was open for 0% of the time, Pallas kernels for 16%

profile of v18, /device:TPU:17, one launch (start us, length us, event | category | flops | bytes accessed | tf_op | source)
XLA Modules:
  0.0 51.6 jit_solution(16514100446326846218)
XLA Ops:
  0.6 0.9 %pack.1 = (f32[8,1920]{1,0:T(8,128)S(1)}, f32[16,128]{1,0:T(8,128)S(1)}, f32[16,128]{1,0:T(8,128)S(1)}, s32[1,8]{1,0:T(1,128)S(1)}) custom-call(f32[8,1536]{1,0:T(8,128)} %bitcast.3, f32[16,128]{1,0:T(8,128)} %loads_in.1, s32[6,16]{1,0:T(8,128)} %entries_in.1, s32[6,16]{1,0:T(8,128)} %cells_in.1, s32[1,8]{1,0:T(1,128)} %bitcast.4), custom_call_target="tpu_custom_call" | custom-call | flops 1 | bytes 1 | tf_op jit(solution)/shard_map/pack/pallas_call | solution.py:711
  1.5 1.3 %collective-permute-start = (f32[8,1920]{1,0:T(8,128)S(1)}, f32[8,1920]{1,0:T(8,128)S(1)}, u32[]{:S(2)}, u32[]{:S(2)}) collective-permute-start(f32[8,1920]{1,0:T(8,128)S(1)} %get-tuple-element.81.own), channel_id=1, source_target_pairs={{0,8},{1,9},{2,10},{3,11},{4,12},{5,13},{6,14},{7,15},{16,24},{17,... | collective-permute-start | bytes 184328 | tf_op jit(solution)/shard_map/ppermute | solution.py:749
  2.8 1.8 %start.1 = (f32[3,2,144,128]{3,2,1,0:T(8,128)S(1)}, f32[6,2,144,128]{3,2,1,0:T(8,128)S(1)}, f32[6,2,128,128]{3,2,1,0:T(8,128)S(1)}, f32[16,128]{1,0:T(8,128)S(1)...) custom-call(f32[3,2,128,128]{3,2,1,0:T(8,128)} %velocity.1, ...), custom_call_target="tpu_custom_call" | custom-call | flops 8388608 | bytes 8388608 | tf_op jit(solution)/shard_map/start/pallas_call | solution.py:711
  4.6 2.8 %collective-permute-done.behind = f32[8,1920]{1,0:T(8,128)S(1)} collective-permute-done((f32[8,1920]{1,0:T(8,128)S(1)}, f32[8,1920]{1,0:T(8,128)S(1)}, u32[]{:S(2)}, u32[]{:S(2)}) %collective-permute-start) | collective-permute-done | bytes 61472 | tf_op jit(solution)/shard_map/ppermute | solution.py:749
  7.4 0.9 %split.1 = f32[8,56,128]{2,1,0:T(8,128)} custom-call(f32[8,1920]{1,0:T(8,128)S(1)} %get-tuple-element.81.own, f32[8,1920]{1,0:T(8,128)S(1)} %collective-permute-done.behind, s32[1,8]{1,0:T(1,128)S(1)} %get-tuple-element.82.cells, f32[16,128]{1,0:T(8,128)S(1)} %get-tuple-element.80.after_this.coef_ref), custom_call_target="tpu_custom_call" | custom-call | flops 1 | bytes 1 | tf_op jit(solution)/shard_map/split/pallas_call | solution.py:711
  8.3 6.3 %all-to-all-start = ((f32[8,56,128]{2,1,0:T(8,128)}), f32[8,56,128]{2,1,0:T(8,128)S(1)}, u32[]{:S(2)}, u32[]{:S(2)}) async-start(f32[8,56,128]{2,1,0:T(8,128)} %split.1), calls=%async_computation | async-start | bytes 458752 | tf_op jit(solution)/shard_map/all_to_all | solution.py:802
  14.6 0.0 collective-permute-start.1
  14.6 0.5 collective-permute-start.2
  15.1 3.5 %collective-permute-start.3 = (f32[3,128,128]{2,1,0:T(8,128)S(1)}, f32[3,128,128]{2,1,0:T(8,128)S(1)}, u32[]{:S(2)}, u32[]{:S(2)}) collective-permute-start(f32[3,128,128]{2,1,0:T(8,128)S(1)} %get-tuple-element.92), channel_id=1, source_target_pairs={{1,2},{3,4},{5,6},{7,8},{9,10},{11,12},{13,14},{2,1},{4,3},{6,5},{... | collective-permute-start | bytes 589832 | tf_op jit(solution)/shard_map/ppermute | solution.py:791
  18.6 0.9 %all-to-all-done.parts = f32[8,56,128]{2,1,0:T(8,128)S(1)} async-done(((f32[8,56,128]{2,1,0:T(8,128)}), f32[8,56,128]{2,1,0:T(8,128)S(1)}, u32[]{:S(2)}, u32[]{:S(2)}) %all-to-all-start) | async-done | bytes 229408 | tf_op jit(solution)/shard_map/all_to_all | solution.py:802
  19.6 0.4 prepare.1
  20.0 0.3 first.1
  20.3 3.7 %collective-permute-start.6 = (f32[3,128,128]{2,1,0:T(8,128)S(1)}, f32[3,128,128]{2,1,0:T(8,128)S(1)}, u32[]{:S(2)}, u32[]{:S(2)}) collective-permute-start(f32[3,128,128]{2,1,0:T(8,128)S(1)} %get-tuple-element.101), channel_id=1, source_target_pairs={{1,2},{3,4},{5,6},{7,8},{9,10},{11,12},{13,14},{2,1},{4,3},{6,5},{... | collective-permute-start | bytes 589832 | tf_op jit(solution)/shard_map/ppermute | solution.py:826
  24.0 0.0 collective-permute-done.2.lower
  24.0 0.3 near0.1
  24.3 0.1 collective-permute-start.4
  24.4 0.5 collective-permute-start.5
  24.9 0.6 %far0.1 = (f32[3,2,144,128]{3,2,1,0:T(8,128)S(1)}, f32[6,2,144,128]{3,2,1,0:T(8,128)S(1)}, f32[6,2,128,128]{3,2,1,0:T(8,128)S(1)}, f32[3,128,128]{2,1,0:T(8,128)S(1)}, f32[3,128,128]{2,1,0:T(8,128)S(1)}) custom-call(f32[3,2,144,128]{3,2,1,0:T(8,128)S(1)} %get-tuple-element.89.V0, ...), custom_call_target="tpu_custom_call", output_to_operand_aliasing={{0}: (0, {}), {1}: (1, {}), {2}: (2, {})} | custom-call | flops 1 | bytes 1 | tf_op jit(solution)/shard_map/far0/pallas_call | solution.py:711
  25.5 0.2 collective-permute-done.4.upper
  25.7 0.2 collective-permute-done.5.lower
  25.8 0.2 near1.1
  26.1 0.4 collective-permute-start.7
  26.5 0.2 collective-permute-start.8
  26.7 3.3 %collective-permute-start.9 = (f32[3,128,128]{2,1,0:T(8,128)S(1)}, f32[3,128,128]{2,1,0:T(8,128)S(1)}, u32[]{:S(2)}, u32[]{:S(2)}) collective-permute-start(f32[3,128,128]{2,1,0:T(8,128)S(1)} %get-tuple-element.111), channel_id=1, source_target_pairs={{1,2},{3,4},{5,6},{7,8},{9,10},{11,12},{13,14},{2,1},{4,3},{6,5},{... | collective-permute-start | bytes 589832 | tf_op jit(solution)/shard_map/ppermute | solution.py:865
  30.0 0.6 %far1.1 = (f32[3,2,144,128]{3,2,1,0:T(8,128)S(1)}, f32[6,2,144,128]{3,2,1,0:T(8,128)S(1)}, f32[6,2,128,128]{3,2,1,0:T(8,128)S(1)}, f32[3,128,128]{2,1,0:T(8,128)S(1)}, f32[3,128,128]{2,1,0:T(8,128)S(1)}) custom-call(f32[3,2,144,128]{3,2,1,0:T(8,128)S(1)} %get-tuple-element.98.V0, ...), custom_call_target="tpu_custom_call", output_to_operand_aliasing={{0}: (0, {}), {1}: (1, {}), {2}: (2, {})} | custom-call | flops 1 | bytes 1 | tf_op jit(solution)/shard_map/far1/pallas_call | solution.py:711
  30.6 3.2 %collective-permute-start.12 = (f32[3,128,128]{2,1,0:T(8,128)S(1)}, f32[3,128,128]{2,1,0:T(8,128)S(1)}, u32[]{:S(2)}, u32[]{:S(2)}) collective-permute-start(f32[3,128,128]{2,1,0:T(8,128)S(1)} %get-tuple-element.121), channel_id=1, source_target_pairs={{1,2},{3,4},{5,6},{7,8},{9,10},{11,12},{13,14},{2,1},{4,3},{6,5},{... | collective-permute-start | bytes 589832 | tf_op jit(solution)/shard_map/ppermute | solution.py:865
  33.8 0.0 collective-permute-done.7.upper
  33.8 0.3 near2.1
  34.1 0.3 collective-permute-start.10
  34.4 0.2 collective-permute-start.11
  34.7 0.6 %surface.1 = f32[128,128]{1,0:T(8,128)S(1)} custom-call(f32[8,56,128]{2,1,0:T(8,128)S(1)} %all-to-all-done.parts, f32[16,128]{1,0:T(8,128)S(1)} %get-tuple-element.83.loads, f32[16,128]{1,0:T(8,128)S(1)} %get-tuple-element.76.after_this.steps_table), custom_call_target="tpu_custom_call" | custom-call | flops 1 | bytes 1 | tf_op jit(solution)/shard_map/surface/pallas_call | solution.py:711
  35.2 0.5 %collective-permute-done.9.msg = f32[3,128,128]{2,1,0:T(8,128)S(1)} collective-permute-done((f32[3,128,128]{2,1,0:T(8,128)S(1)}, f32[3,128,128]{2,1,0:T(8,128)S(1)}, u32[]{:S(2)}, u32[]{:S(2)}) %collective-permute-start.9) | collective-permute-done | bytes 196640 | tf_op jit(solution)/shard_map/ppermute | solution.py:865
  35.8 0.6 %far2.1 = (f32[3,2,144,128]{3,2,1,0:T(8,128)S(1)}, f32[6,2,144,128]{3,2,1,0:T(8,128)S(1)}, f32[6,2,128,128]{3,2,1,0:T(8,128)S(1)}, f32[3,128,128]{2,1,0:T(8,128)S(1)}, f32[3,128,128]{2,1,0:T(8,128)S(1)}) custom-call(f32[3,2,144,128]{3,2,1,0:T(8,128)S(1)} %get-tuple-element.108.V0, ...), custom_call_target="tpu_custom_call", output_to_operand_aliasing={{0}: (0, {}), {1}: (1, {}), {2}: (2, {})} | custom-call | flops 1 | bytes 1 | tf_op jit(solution)/shard_map/far2/pallas_call | solution.py:711
  36.4 0.0 collective-permute-done.11.lower
  36.4 0.3 near3.1
  36.7 0.1 collective-permute-start.13
  36.7 0.5 collective-permute-start.14
  37.2 3.3 %collective-permute-start.15 = (f32[3,128,128]{2,1,0:T(8,128)S(1)}, f32[3,128,128]{2,1,0:T(8,128)S(1)}, u32[]{:S(2)}, u32[]{:S(2)}) collective-permute-start(f32[3,128,128]{2,1,0:T(8,128)S(1)} %get-tuple-element.131), channel_id=1, source_target_pairs={{1,2},{3,4},{5,6},{7,8},{9,10},{11,12},{13,14},{2,1},{4,3},{6,5},{... | collective-permute-start | bytes 589832 | tf_op jit(solution)/shard_map/ppermute | solution.py:865
  40.6 0.6 %far3.1 = (f32[3,2,144,128]{3,2,1,0:T(8,128)S(1)}, f32[6,2,144,128]{3,2,1,0:T(8,128)S(1)}, f32[6,2,128,128]{3,2,1,0:T(8,128)S(1)}, f32[3,128,128]{2,1,0:T(8,128)S(1)}, f32[3,128,128]{2,1,0:T(8,128)S(1)}) custom-call(f32[3,2,144,128]{3,2,1,0:T(8,128)S(1)} %get-tuple-element.118.V0, ...), custom_call_target="tpu_custom_call", output_to_operand_aliasing={{0}: (0, {}), {1}: (1, {}), {2}: (2, {})} | custom-call | flops 1 | bytes 1 | tf_op jit(solution)/shard_map/far3/pallas_call | solution.py:711
  41.2 2.7 %collective-permute-start.18 = (f32[3,128,128]{2,1,0:T(8,128)S(1)}, f32[3,128,128]{2,1,0:T(8,128)S(1)}, u32[]{:S(2)}, u32[]{:S(2)}) collective-permute-start(f32[3,128,128]{2,1,0:T(8,128)S(1)} %get-tuple-element.141), channel_id=1, source_target_pairs={{1,2},{3,4},{5,6},{7,8},{9,10},{11,12},{13,14},{2,1},{4,3},{6,5},{... | collective-permute-start | bytes 589832 | tf_op jit(solution)/shard_map/ppermute | solution.py:865
  44.0 0.3 near4.1
  44.2 0.5 %collective-permute-start.16 = (f32[3,64,128]{2,1,0:T(8,128)S(1)}, f32[3,64,128]{2,1,0:T(8,128)S(1)}, u32[]{:S(2)}, u32[]{:S(2)}) collective-permute-start(f32[3,64,128]{2,1,0:T(8,128)S(1)} %get-tuple-element.136), channel_id=1, source_target_pairs={{0,1},{1,0},{2,3},{3,2},{4,5},{5,4},{6,7},{7,6},{8,9},{9,8},{10,11... | collective-permute-start | bytes 294920 | tf_op jit(solution)/shard_map/ppermute | solution.py:846
  44.8 0.1 collective-permute-start.17
  44.8 1.5 %collective-permute-done.15.msg = f32[3,128,128]{2,1,0:T(8,128)S(1)} collective-permute-done((f32[3,128,128]{2,1,0:T(8,128)S(1)}, f32[3,128,128]{2,1,0:T(8,128)S(1)}, u32[]{:S(2)}, u32[]{:S(2)}) %collective-permute-start.15) | collective-permute-done | bytes 196640 | tf_op jit(solution)/shard_map/ppermute | solution.py:865
  46.3 0.5 far4.1
  46.8 1.1 %near5.1 = (f32[3,2,144,128]{3,2,1,0:T(8,128)S(1)}, f32[6,2,144,128]{3,2,1,0:T(8,128)S(1)}, f32[6,2,128,128]{3,2,1,0:T(8,128)S(1)}, f32[3,2,128,128]{3,2,1,0:T(8...) custom-call(f32[3,2,144,128]{3,2,1,0:T(8,128)S(1)} %get-tuple-elemen, ...), custom_call_target="tpu_custom_call", output_to_operand_aliasing={{0}: (0, {}), {1}: (1, {}), {2}: (2, {})} | custom-call | flops 1 | bytes 1 | tf_op jit(solution)/shard_map/near5/pallas_call | solution.py:711
  47.9 2.6 %collective-permute-done.18.msg = f32[3,128,128]{2,1,0:T(8,128)S(1)} collective-permute-done((f32[3,128,128]{2,1,0:T(8,128)S(1)}, f32[3,128,128]{2,1,0:T(8,128)S(1)}, u32[]{:S(2)}, u32[]{:S(2)}) %collective-permute-start.18) | collective-permute-done | bytes 196640 | tf_op jit(solution)/shard_map/ppermute | solution.py:865
  50.5 1.1 %last.1 = (f32[3,2,144,128]{3,2,1,0:T(8,128)S(1)}, f32[6,2,144,128]{3,2,1,0:T(8,128)S(1)}, f32[6,2,128,128]{3,2,1,0:T(8,128)S(1)}, f32[3,2,128,128]{3,2,1,0:T(8,...) custom-call(f32[3,2,144,128]{3,2,1,0:T(8,128)S(1)} %get-tuple-elemen, ...), custom_call_target="tpu_custom_call", output_to_operand_aliasing={{0}: (0, {}), {1}: (1, {}), {2}: (2, {}), {3}: (8, {}), {4}... | custom-call | flops 1 | bytes 1 | tf_op jit(solution)/shard_map/last/pallas_call | solution.py:711
  (10 shorter events, 0.0 us)
Async XLA Ops:
  1.5 5.9 %collective-permute-start = (f32[8,1920]{1,0:T(8,128)S(1)}, f32[8,1920]{1,0:T(8,128)S(1)}, u32[]{:S(2)}, u32[]{:S(2)}) collective-permute-start(f32[8,1920]{1,0:T(8,128)S(1)} %get-tuple-element.81.own), channel_id=1, source_target_pairs={{0,8},{1,9},{2,10},{3,11},{4,12},{5,13},{6,14},{7,15},{16,24},{17,... | collective-permute-start | bytes 184328 | tf_op jit(solution)/shard_map/ppermute | solution.py:749
  8.3 11.3 %all-to-all-start = ((f32[8,56,128]{2,1,0:T(8,128)}), f32[8,56,128]{2,1,0:T(8,128)S(1)}, u32[]{:S(2)}, u32[]{:S(2)}) async-start(f32[8,56,128]{2,1,0:T(8,128)} %split.1), calls=%async_computation | async-start | bytes 458752 | tf_op jit(solution)/shard_map/all_to_all | solution.py:802
  14.6 9.4 %collective-permute-start.1 = (f32[3,64,128]{2,1,0:T(8,128)S(1)}, f32[3,64,128]{2,1,0:T(8,128)S(1)}, u32[]{:S(2)}, u32[]{:S(2)}) collective-permute-start(f32[3,64,128]{2,1,0:T(8,128)S(1)} %get-tuple-element.87), channel_id=1, source_target_pairs={{0,1},{1,0},{2,3},{3,2},{4,5},{5,4},{6,7},{7,6},{8,9},{9,8},{10,11... | collective-permute-start | bytes 294920 | tf_op jit(solution)/shard_map/ppermute | solution.py:792
  14.6 9.4 %collective-permute-start.2 = (f32[3,64,128]{2,1,0:T(8,128)S(1)}, f32[3,64,128]{2,1,0:T(8,128)S(1)}, u32[]{:S(2)}, u32[]{:S(2)}) collective-permute-start(f32[3,64,128]{2,1,0:T(8,128)S(1)} %get-tuple-element.88), channel_id=1, source_target_pairs={{0,1},{1,0},{2,3},{3,2},{4,5},{5,4},{6,7},{7,6},{8,9},{9,8},{10,11... | collective-permute-start | bytes 294920 | tf_op jit(solution)/shard_map/ppermute | solution.py:792
  15.1 9.8 %collective-permute-start.3 = (f32[3,128,128]{2,1,0:T(8,128)S(1)}, f32[3,128,128]{2,1,0:T(8,128)S(1)}, u32[]{:S(2)}, u32[]{:S(2)}) collective-permute-start(f32[3,128,128]{2,1,0:T(8,128)S(1)} %get-tuple-element.92), channel_id=1, source_target_pairs={{1,2},{3,4},{5,6},{7,8},{9,10},{11,12},{13,14},{2,1},{4,3},{6,5},{... | collective-permute-start | bytes 589832 | tf_op jit(solution)/shard_map/ppermute | solution.py:791
  20.3 9.7 %collective-permute-start.6 = (f32[3,128,128]{2,1,0:T(8,128)S(1)}, f32[3,128,128]{2,1,0:T(8,128)S(1)}, u32[]{:S(2)}, u32[]{:S(2)}) collective-permute-start(f32[3,128,128]{2,1,0:T(8,128)S(1)} %get-tuple-element.101), channel_id=1, source_target_pairs={{1,2},{3,4},{5,6},{7,8},{9,10},{11,12},{13,14},{2,1},{4,3},{6,5},{... | collective-permute-start | bytes 589832 | tf_op jit(solution)/shard_map/ppermute | solution.py:826
  24.3 1.4 %collective-permute-start.4 = (f32[3,64,128]{2,1,0:T(8,128)S(1)}, f32[3,64,128]{2,1,0:T(8,128)S(1)}, u32[]{:S(2)}, u32[]{:S(2)}) collective-permute-start(f32[3,64,128]{2,1,0:T(8,128)S(1)} %get-tuple-element.96), channel_id=1, source_target_pairs={{0,1},{1,0},{2,3},{3,2},{4,5},{5,4},{6,7},{7,6},{8,9},{9,8},{10,11... | collective-permute-start | bytes 294920 | tf_op jit(solution)/shard_map/ppermute | solution.py:846
  24.4 1.4 %collective-permute-start.5 = (f32[3,64,128]{2,1,0:T(8,128)S(1)}, f32[3,64,128]{2,1,0:T(8,128)S(1)}, u32[]{:S(2)}, u32[]{:S(2)}) collective-permute-start(f32[3,64,128]{2,1,0:T(8,128)S(1)} %get-tuple-element.97), channel_id=1, source_target_pairs={{0,1},{1,0},{2,3},{3,2},{4,5},{5,4},{6,7},{7,6},{8,9},{9,8},{10,11... | collective-permute-start | bytes 294920 | tf_op jit(solution)/shard_map/ppermute | solution.py:846
  26.1 7.7 %collective-permute-start.7 = (f32[3,64,128]{2,1,0:T(8,128)S(1)}, f32[3,64,128]{2,1,0:T(8,128)S(1)}, u32[]{:S(2)}, u32[]{:S(2)}) collective-permute-start(f32[3,64,128]{2,1,0:T(8,128)S(1)} %get-tuple-element.106), channel_id=1, source_target_pairs={{0,1},{1,0},{2,3},{3,2},{4,5},{5,4},{6,7},{7,6},{8,9},{9,8},{10,11... | collective-permute-start | bytes 294920 | tf_op jit(solution)/shard_map/ppermute | solution.py:846
  26.5 7.3 %collective-permute-start.8 = (f32[3,64,128]{2,1,0:T(8,128)S(1)}, f32[3,64,128]{2,1,0:T(8,128)S(1)}, u32[]{:S(2)}, u32[]{:S(2)}) collective-permute-start(f32[3,64,128]{2,1,0:T(8,128)S(1)} %get-tuple-element.107), channel_id=1, source_target_pairs={{0,1},{1,0},{2,3},{3,2},{4,5},{5,4},{6,7},{7,6},{8,9},{9,8},{10,11... | collective-permute-start | bytes 294920 | tf_op jit(solution)/shard_map/ppermute | solution.py:846
  26.7 9.1 %collective-permute-start.9 = (f32[3,128,128]{2,1,0:T(8,128)S(1)}, f32[3,128,128]{2,1,0:T(8,128)S(1)}, u32[]{:S(2)}, u32[]{:S(2)}) collective-permute-start(f32[3,128,128]{2,1,0:T(8,128)S(1)} %get-tuple-element.111), channel_id=1, source_target_pairs={{1,2},{3,4},{5,6},{7,8},{9,10},{11,12},{13,14},{2,1},{4,3},{6,5},{... | collective-permute-start | bytes 589832 | tf_op jit(solution)/shard_map/ppermute | solution.py:865
  30.6 9.9 %collective-permute-start.12 = (f32[3,128,128]{2,1,0:T(8,128)S(1)}, f32[3,128,128]{2,1,0:T(8,128)S(1)}, u32[]{:S(2)}, u32[]{:S(2)}) collective-permute-start(f32[3,128,128]{2,1,0:T(8,128)S(1)} %get-tuple-element.121), channel_id=1, source_target_pairs={{1,2},{3,4},{5,6},{7,8},{9,10},{11,12},{13,14},{2,1},{4,3},{6,5},{... | collective-permute-start | bytes 589832 | tf_op jit(solution)/shard_map/ppermute | solution.py:865
  34.1 2.3 %collective-permute-start.10 = (f32[3,64,128]{2,1,0:T(8,128)S(1)}, f32[3,64,128]{2,1,0:T(8,128)S(1)}, u32[]{:S(2)}, u32[]{:S(2)}) collective-permute-start(f32[3,64,128]{2,1,0:T(8,128)S(1)} %get-tuple-element.116), channel_id=1, source_target_pairs={{0,1},{1,0},{2,3},{3,2},{4,5},{5,4},{6,7},{7,6},{8,9},{9,8},{10,11... | collective-permute-start | bytes 294920 | tf_op jit(solution)/shard_map/ppermute | solution.py:846
  34.4 1.9 %collective-permute-start.11 = (f32[3,64,128]{2,1,0:T(8,128)S(1)}, f32[3,64,128]{2,1,0:T(8,128)S(1)}, u32[]{:S(2)}, u32[]{:S(2)}) collective-permute-start(f32[3,64,128]{2,1,0:T(8,128)S(1)} %get-tuple-element.117), channel_id=1, source_target_pairs={{0,1},{1,0},{2,3},{3,2},{4,5},{5,4},{6,7},{7,6},{8,9},{9,8},{10,11... | collective-permute-start | bytes 294920 | tf_op jit(solution)/shard_map/ppermute | solution.py:846
  36.7 7.3 %collective-permute-start.13 = (f32[3,64,128]{2,1,0:T(8,128)S(1)}, f32[3,64,128]{2,1,0:T(8,128)S(1)}, u32[]{:S(2)}, u32[]{:S(2)}) collective-permute-start(f32[3,64,128]{2,1,0:T(8,128)S(1)} %get-tuple-element.126), channel_id=1, source_target_pairs={{0,1},{1,0},{2,3},{3,2},{4,5},{5,4},{6,7},{7,6},{8,9},{9,8},{10,11... | collective-permute-start | bytes 294920 | tf_op jit(solution)/shard_map/ppermute | solution.py:846
  36.7 7.2 %collective-permute-start.14 = (f32[3,64,128]{2,1,0:T(8,128)S(1)}, f32[3,64,128]{2,1,0:T(8,128)S(1)}, u32[]{:S(2)}, u32[]{:S(2)}) collective-permute-start(f32[3,64,128]{2,1,0:T(8,128)S(1)} %get-tuple-element.127), channel_id=1, source_target_pairs={{0,1},{1,0},{2,3},{3,2},{4,5},{5,4},{6,7},{7,6},{8,9},{9,8},{10,11... | collective-permute-start | bytes 294920 | tf_op jit(solution)/shard_map/ppermute | solution.py:846
  37.2 9.1 %collective-permute-start.15 = (f32[3,128,128]{2,1,0:T(8,128)S(1)}, f32[3,128,128]{2,1,0:T(8,128)S(1)}, u32[]{:S(2)}, u32[]{:S(2)}) collective-permute-start(f32[3,128,128]{2,1,0:T(8,128)S(1)} %get-tuple-element.131), channel_id=1, source_target_pairs={{1,2},{3,4},{5,6},{7,8},{9,10},{11,12},{13,14},{2,1},{4,3},{6,5},{... | collective-permute-start | bytes 589832 | tf_op jit(solution)/shard_map/ppermute | solution.py:865
  41.2 9.3 %collective-permute-start.18 = (f32[3,128,128]{2,1,0:T(8,128)S(1)}, f32[3,128,128]{2,1,0:T(8,128)S(1)}, u32[]{:S(2)}, u32[]{:S(2)}) collective-permute-start(f32[3,128,128]{2,1,0:T(8,128)S(1)} %get-tuple-element.141), channel_id=1, source_target_pairs={{1,2},{3,4},{5,6},{7,8},{9,10},{11,12},{13,14},{2,1},{4,3},{6,5},{... | collective-permute-start | bytes 589832 | tf_op jit(solution)/shard_map/ppermute | solution.py:865
  44.2 2.6 %collective-permute-start.16 = (f32[3,64,128]{2,1,0:T(8,128)S(1)}, f32[3,64,128]{2,1,0:T(8,128)S(1)}, u32[]{:S(2)}, u32[]{:S(2)}) collective-permute-start(f32[3,64,128]{2,1,0:T(8,128)S(1)} %get-tuple-element.136), channel_id=1, source_target_pairs={{0,1},{1,0},{2,3},{3,2},{4,5},{5,4},{6,7},{7,6},{8,9},{9,8},{10,11... | collective-permute-start | bytes 294920 | tf_op jit(solution)/shard_map/ppermute | solution.py:846
  44.8 2.0 %collective-permute-start.17 = (f32[3,64,128]{2,1,0:T(8,128)S(1)}, f32[3,64,128]{2,1,0:T(8,128)S(1)}, u32[]{:S(2)}, u32[]{:S(2)}) collective-permute-start(f32[3,64,128]{2,1,0:T(8,128)S(1)} %get-tuple-element.137), channel_id=1, source_target_pairs={{0,1},{1,0},{2,3},{3,2},{4,5},{5,4},{6,7},{7,6},{8,9},{9,8},{10,11... | collective-permute-start | bytes 294920 | tf_op jit(solution)/shard_map/ppermute | solution.py:846

commit v19 on v17

--- a/solution.py
+++ b/solution.py
@@ -175,7 +175,7 @@
         add_force(V, (VZ, 1), force, (VZ, 1), PAD + window)
 
 
-def post(V, S, R, coef_ref, surface, cell, column, behind_x, ahead_y, ahead_z):
+def post(V, S, R, coef_ref, surface, cell, column, behind_x, ahead_y, ahead_z, done=None):
     m0, m1, lam, mu2, mu, k1, k2, k2h, l0 = coefs(
         coef_ref, (C_M0, C_M1, C_LAM, C_MU2, C_MU, C_K1, C_K2, C_K2H, C_L0)
     )
@@ -202,7 +202,13 @@
             S[comp, cell, here] = S[comp, cell, here] + mu * e + DT * old
             R[comp, cell, out] = k1 * old - k2h * e
 
-    over_rows(R.shape[2], work)
+    if done is None:
+        over_rows(R.shape[2], work)
+        return
+    half = R.shape[2] // 2
+    for first in (0, half):
+        over_rows(half, work, first)
+        done(first, half)
 
 
 def response_behind(V, S, coef_ref, D, W):
@@ -321,7 +327,7 @@
         add_force(msg, (2,), force, (VZ, 0), window)
 
 
-def ahead_bond(V, S, R, coef_ref, force, surface, msg, missing, G, step, window, unforced=0, respond=None):
+def ahead_bond(V, S, R, coef_ref, force, surface, msg, missing, G, step, window, unforced=0, respond=None, done=None):
     (b,) = coefs(coef_ref, (C_B,))
     _, _, has_ahead = place()
     keep = jnp.where(has_ahead, 1.0, 0.0).astype(jnp.float32)
@@ -346,10 +352,11 @@
         lambda r: V[VX, 0, pl.ds(PAD + r, ROWS)],
         lambda r: G[0, pl.ds(r, ROWS)],
         lambda r: G[1, pl.ds(r, ROWS)],
-    )
-
-
-def behind_bond(V, S, R, coef_ref, force, surface, msg, missing, G, step, window, unforced=0, respond=None):
+        done,
+    )
+
+
+def behind_bond(V, S, R, coef_ref, force, surface, msg, missing, G, step, window, unforced=0, respond=None, done=None):
     (b,) = coefs(coef_ref, (C_B,))
     _, has_behind, _ = place()
     keep = jnp.where(has_behind, 1.0, 0.0).astype(jnp.float32)
@@ -373,6 +380,7 @@
         lambda r: G[0, pl.ds(r, ROWS)],
         lambda r: V[VY, 1, pl.ds(PAD + r, ROWS)],
         lambda r: V[VZ, 1, pl.ds(PAD + r, ROWS)],
+        done,
     )
 
 
@@ -554,23 +562,31 @@
     even, _, _ = place()
     here = force.at[step]
 
+    def finish(cell, bond):
+        copies = []
+
+        def send(source, result):
+            copies.append(pltpu.make_async_copy(source, result, sems.at[len(copies)]))
+            copies[-1].start()
+
+        def velocities():
+            send(V.at[:, cell, pl.ds(PAD, R.shape[2])], results[0].at[:, cell])
+
+        def done(first, count):
+            out = pl.ds(first, count)
+            send(S.at[:, cell, pl.ds(PAD + first, count)], results[1].at[:, cell, out])
+            send(R.at[:, cell, out], results[2].at[:, cell, out])
+
+        bond(V, S, R, coef_ref, here, surface, msg, missing, G, step, window, 0, velocities, done)
+        wait_all(copies)
+
     @pl.when(even)
     def _():
-        copies = results_out(V, S, R, results, sems, 0)
-        behind_bond(
-            V, S, R, coef_ref, here, surface, msg, missing, G, step, window, 0, lambda: start_all(copies[:1])
-        )
-        start_all(copies[1:])
-        wait_all(copies)
+        finish(0, behind_bond)
 
     @pl.when(jnp.logical_not(even))
     def _():
-        copies = results_out(V, S, R, results, sems, 1)
-        ahead_bond(
-            V, S, R, coef_ref, here, surface, msg, missing, G, step, window, 0, lambda: start_all(copies[:1])
-        )
-        start_all(copies[1:])
-        wait_all(copies)
+        finish(1, ahead_bond)
 
 
 ENTRY_ROW, TRUCK_ROW = 36, 40
@@ -868,7 +884,7 @@
         (WHOLE,) * 8 + (ANYWHERE,) * 3,
         state + results,
         (WHOLE,) * 3 + (ANYWHERE,) * 3,
-        scratch=(ghost, dma((3,))),
+        scratch=(ghost, dma((5,))),
         aliases={**same, 8: 3, 9: 4, 10: 5},
         name="last",
     )

time: 52.3 us -> 52.3 us (level)
  no operation moved by 1% of the time
where the time goes in v19:
time: 52.3 us; the launch traced here: 51.9 us
  starting transfers between devices  30.4 us (58%)
  Pallas kernels  11.2 us (21%)
  waiting for transfers between devices  9.33 us (18%)
  between operations  0.93 us (2%)
    ppermute x4, starting transfers between devices, body(): early = lax.ppermute(msg[0], 'line', far)  11.9 us
    pallas_call x18, Pallas kernels, call(): pl.pallas_call(kernel, out_shape=outs, in_specs=specs, out_specs=out_spec...  11.2 us
    all_to_all x1, starting transfers between devices, body(): lax.all_to_all(parts, 'line', 0, 0, axis_index_groups=groups, tiled=True)  6.3 us
    ppermute x4, waiting for transfers between devices, body(): early = lax.ppermute(msg[0], 'line', far)  5.51 us
    ppermute x1, starting transfers between devices, body(): early = lax.ppermute(early, 'line', far)  3.74 us
    ppermute x1, starting transfers between devices, body(): msg_far = lax.ppermute(msg_far, 'line', far)  3.53 us
    ppermute x10, starting transfers between devices, body(): msg_near = [lax.ppermute(plane, 'line', near) for plane in msg]  3.13 us
    ppermute x1, waiting for transfers between devices, ahead_by(): lax.ppermute(x, 'line', [(i, i + distance) for i in range(tiles - distanc...  2.85 us
  transfers between devices with their start and end apart: 20, of which 5 were waited for; matrix products, arithmetic and copies ran while one was open for 0% of the time, Pallas kernels for 16%

profile of v19, /device:TPU:17, one launch (start us, length us, event | category | flops | bytes accessed | tf_op | source)
XLA Modules:
  0.0 51.9 jit_solution(896262524164826557)
XLA Ops:
  0.6 0.9 %pack.1 = (f32[8,1920]{1,0:T(8,128)S(1)}, f32[16,128]{1,0:T(8,128)S(1)}, f32[16,128]{1,0:T(8,128)S(1)}, s32[1,8]{1,0:T(1,128)S(1)}) custom-call(f32[8,1536]{1,0:T(8,128)} %bitcast.3, f32[16,128]{1,0:T(8,128)} %loads_in.1, s32[6,16]{1,0:T(8,128)} %entries_in.1, s32[6,16]{1,0:T(8,128)} %cells_in.1, s32[1,8]{1,0:T(1,128)} %bitcast.4), custom_call_target="tpu_custom_call" | custom-call | flops 1 | bytes 1 | tf_op jit(solution)/shard_map/pack/pallas_call | solution.py:726
  1.5 1.3 %collective-permute-start = (f32[8,1920]{1,0:T(8,128)S(1)}, f32[8,1920]{1,0:T(8,128)S(1)}, u32[]{:S(2)}, u32[]{:S(2)}) collective-permute-start(f32[8,1920]{1,0:T(8,128)S(1)} %get-tuple-element.81.own), channel_id=1, source_target_pairs={{0,8},{1,9},{2,10},{3,11},{4,12},{5,13},{6,14},{7,15},{16,24},{17,... | collective-permute-start | bytes 184328 | tf_op jit(solution)/shard_map/ppermute | solution.py:764
  2.8 1.8 %start.1 = (f32[3,2,144,128]{3,2,1,0:T(8,128)S(1)}, f32[6,2,144,128]{3,2,1,0:T(8,128)S(1)}, f32[6,2,128,128]{3,2,1,0:T(8,128)S(1)}, f32[16,128]{1,0:T(8,128)S(1)...) custom-call(f32[3,2,128,128]{3,2,1,0:T(8,128)} %velocity.1, ...), custom_call_target="tpu_custom_call" | custom-call | flops 8388608 | bytes 8388608 | tf_op jit(solution)/shard_map/start/pallas_call | solution.py:726
  4.6 2.8 %collective-permute-done.behind = f32[8,1920]{1,0:T(8,128)S(1)} collective-permute-done((f32[8,1920]{1,0:T(8,128)S(1)}, f32[8,1920]{1,0:T(8,128)S(1)}, u32[]{:S(2)}, u32[]{:S(2)}) %collective-permute-start) | collective-permute-done | bytes 61472 | tf_op jit(solution)/shard_map/ppermute | solution.py:764
  7.4 0.9 %split.1 = f32[8,56,128]{2,1,0:T(8,128)} custom-call(f32[8,1920]{1,0:T(8,128)S(1)} %get-tuple-element.81.own, f32[8,1920]{1,0:T(8,128)S(1)} %collective-permute-done.behind, s32[1,8]{1,0:T(1,128)S(1)} %get-tuple-element.82.cells, f32[16,128]{1,0:T(8,128)S(1)} %get-tuple-element.80.after_this.coef_ref), custom_call_target="tpu_custom_call" | custom-call | flops 1 | bytes 1 | tf_op jit(solution)/shard_map/split/pallas_call | solution.py:726
  8.3 6.3 %all-to-all-start = ((f32[8,56,128]{2,1,0:T(8,128)}), f32[8,56,128]{2,1,0:T(8,128)S(1)}, u32[]{:S(2)}, u32[]{:S(2)}) async-start(f32[8,56,128]{2,1,0:T(8,128)} %split.1), calls=%async_computation | async-start | bytes 458752 | tf_op jit(solution)/shard_map/all_to_all | solution.py:817
  14.6 0.0 collective-permute-start.1
  14.6 0.5 collective-permute-start.2
  15.1 3.5 %collective-permute-start.3 = (f32[3,128,128]{2,1,0:T(8,128)S(1)}, f32[3,128,128]{2,1,0:T(8,128)S(1)}, u32[]{:S(2)}, u32[]{:S(2)}) collective-permute-start(f32[3,128,128]{2,1,0:T(8,128)S(1)} %get-tuple-element.92), channel_id=1, source_target_pairs={{1,2},{3,4},{5,6},{7,8},{9,10},{11,12},{13,14},{2,1},{4,3},{6,5},{... | collective-permute-start | bytes 589832 | tf_op jit(solution)/shard_map/ppermute | solution.py:806
  18.6 0.9 %all-to-all-done.parts = f32[8,56,128]{2,1,0:T(8,128)S(1)} async-done(((f32[8,56,128]{2,1,0:T(8,128)}), f32[8,56,128]{2,1,0:T(8,128)S(1)}, u32[]{:S(2)}, u32[]{:S(2)}) %all-to-all-start) | async-done | bytes 229408 | tf_op jit(solution)/shard_map/all_to_all | solution.py:817
  19.6 0.3 prepare.1
  19.9 0.3 first.1
  20.2 3.7 %collective-permute-start.6 = (f32[3,128,128]{2,1,0:T(8,128)S(1)}, f32[3,128,128]{2,1,0:T(8,128)S(1)}, u32[]{:S(2)}, u32[]{:S(2)}) collective-permute-start(f32[3,128,128]{2,1,0:T(8,128)S(1)} %get-tuple-element.101), channel_id=1, source_target_pairs={{1,2},{3,4},{5,6},{7,8},{9,10},{11,12},{13,14},{2,1},{4,3},{6,5},{... | collective-permute-start | bytes 589832 | tf_op jit(solution)/shard_map/ppermute | solution.py:841
  24.0 0.0 collective-permute-done.2.lower
  24.0 0.3 near0.1
  24.3 0.1 collective-permute-start.4
  24.3 0.5 collective-permute-start.5
  24.8 0.6 %surface.1 = f32[128,128]{1,0:T(8,128)S(1)} custom-call(f32[8,56,128]{2,1,0:T(8,128)S(1)} %all-to-all-done.parts, f32[16,128]{1,0:T(8,128)S(1)} %get-tuple-element.83.loads, f32[16,128]{1,0:T(8,128)S(1)} %get-tuple-element.76.after_this.steps_table), custom_call_target="tpu_custom_call" | custom-call | flops 1 | bytes 1 | tf_op jit(solution)/shard_map/surface/pallas_call | solution.py:726
  25.4 0.6 %far0.1 = (f32[3,2,144,128]{3,2,1,0:T(8,128)S(1)}, f32[6,2,144,128]{3,2,1,0:T(8,128)S(1)}, f32[6,2,128,128]{3,2,1,0:T(8,128)S(1)}, f32[3,128,128]{2,1,0:T(8,128)S(1)}, f32[3,128,128]{2,1,0:T(8,128)S(1)}) custom-call(f32[3,2,144,128]{3,2,1,0:T(8,128)S(1)} %get-tuple-element.89.V0, ...), custom_call_target="tpu_custom_call", output_to_operand_aliasing={{0}: (0, {}), {1}: (1, {}), {2}: (2, {})} | custom-call | flops 1 | bytes 1 | tf_op jit(solution)/shard_map/far0/pallas_call | solution.py:726
  26.1 0.0 collective-permute-done.5.lower
  26.1 0.3 near1.1
  26.3 0.1 collective-permute-start.7
  26.5 0.4 collective-permute-start.8
  26.9 3.0 %collective-permute-start.9 = (f32[3,128,128]{2,1,0:T(8,128)S(1)}, f32[3,128,128]{2,1,0:T(8,128)S(1)}, u32[]{:S(2)}, u32[]{:S(2)}) collective-permute-start(f32[3,128,128]{2,1,0:T(8,128)S(1)} %get-tuple-element.111), channel_id=1, source_target_pairs={{1,2},{3,4},{5,6},{7,8},{9,10},{11,12},{13,14},{2,1},{4,3},{6,5},{... | collective-permute-start | bytes 589832 | tf_op jit(solution)/shard_map/ppermute | solution.py:880
  30.0 0.6 %far1.1 = (f32[3,2,144,128]{3,2,1,0:T(8,128)S(1)}, f32[6,2,144,128]{3,2,1,0:T(8,128)S(1)}, f32[6,2,128,128]{3,2,1,0:T(8,128)S(1)}, f32[3,128,128]{2,1,0:T(8,128)S(1)}, f32[3,128,128]{2,1,0:T(8,128)S(1)}) custom-call(f32[3,2,144,128]{3,2,1,0:T(8,128)S(1)} %get-tuple-element.98.V0, ...), custom_call_target="tpu_custom_call", output_to_operand_aliasing={{0}: (0, {}), {1}: (1, {}), {2}: (2, {})} | custom-call | flops 1 | bytes 1 | tf_op jit(solution)/shard_map/far1/pallas_call | solution.py:726
  30.6 3.1 %collective-permute-start.12 = (f32[3,128,128]{2,1,0:T(8,128)S(1)}, f32[3,128,128]{2,1,0:T(8,128)S(1)}, u32[]{:S(2)}, u32[]{:S(2)}) collective-permute-start(f32[3,128,128]{2,1,0:T(8,128)S(1)} %get-tuple-element.121), channel_id=1, source_target_pairs={{1,2},{3,4},{5,6},{7,8},{9,10},{11,12},{13,14},{2,1},{4,3},{6,5},{... | collective-permute-start | bytes 589832 | tf_op jit(solution)/shard_map/ppermute | solution.py:880
  33.7 0.0 collective-permute-done.7.upper
  33.7 0.3 near2.1
  34.0 0.4 collective-permute-start.10
  34.4 0.2 collective-permute-start.11
  34.6 1.4 %collective-permute-done.9.msg = f32[3,128,128]{2,1,0:T(8,128)S(1)} collective-permute-done((f32[3,128,128]{2,1,0:T(8,128)S(1)}, f32[3,128,128]{2,1,0:T(8,128)S(1)}, u32[]{:S(2)}, u32[]{:S(2)}) %collective-permute-start.9) | collective-permute-done | bytes 196640 | tf_op jit(solution)/shard_map/ppermute | solution.py:880
  36.0 0.6 %far2.1 = (f32[3,2,144,128]{3,2,1,0:T(8,128)S(1)}, f32[6,2,144,128]{3,2,1,0:T(8,128)S(1)}, f32[6,2,128,128]{3,2,1,0:T(8,128)S(1)}, f32[3,128,128]{2,1,0:T(8,128)S(1)}, f32[3,128,128]{2,1,0:T(8,128)S(1)}) custom-call(f32[3,2,144,128]{3,2,1,0:T(8,128)S(1)} %get-tuple-element.108.V0, ...), custom_call_target="tpu_custom_call", output_to_operand_aliasing={{0}: (0, {}), {1}: (1, {}), {2}: (2, {})} | custom-call | flops 1 | bytes 1 | tf_op jit(solution)/shard_map/far2/pallas_call | solution.py:726
  36.6 0.0 collective-permute-done.10.upper
  36.6 0.0 collective-permute-done.11.lower
  36.6 0.3 near3.1
  36.9 0.1 collective-permute-start.13
  37.0 0.5 collective-permute-start.14
  37.5 3.1 %collective-permute-start.15 = (f32[3,128,128]{2,1,0:T(8,128)S(1)}, f32[3,128,128]{2,1,0:T(8,128)S(1)}, u32[]{:S(2)}, u32[]{:S(2)}) collective-permute-start(f32[3,128,128]{2,1,0:T(8,128)S(1)} %get-tuple-element.131), channel_id=1, source_target_pairs={{1,2},{3,4},{5,6},{7,8},{9,10},{11,12},{13,14},{2,1},{4,3},{6,5},{... | collective-permute-start | bytes 589832 | tf_op jit(solution)/shard_map/ppermute | solution.py:880
  40.6 0.6 %far3.1 = (f32[3,2,144,128]{3,2,1,0:T(8,128)S(1)}, f32[6,2,144,128]{3,2,1,0:T(8,128)S(1)}, f32[6,2,128,128]{3,2,1,0:T(8,128)S(1)}, f32[3,128,128]{2,1,0:T(8,128)S(1)}, f32[3,128,128]{2,1,0:T(8,128)S(1)}) custom-call(f32[3,2,144,128]{3,2,1,0:T(8,128)S(1)} %get-tuple-element.118.V0, ...), custom_call_target="tpu_custom_call", output_to_operand_aliasing={{0}: (0, {}), {1}: (1, {}), {2}: (2, {})} | custom-call | flops 1 | bytes 1 | tf_op jit(solution)/shard_map/far3/pallas_call | solution.py:726
  41.2 2.7 %collective-permute-start.18 = (f32[3,128,128]{2,1,0:T(8,128)S(1)}, f32[3,128,128]{2,1,0:T(8,128)S(1)}, u32[]{:S(2)}, u32[]{:S(2)}) collective-permute-start(f32[3,128,128]{2,1,0:T(8,128)S(1)} %get-tuple-element.141), channel_id=1, source_target_pairs={{1,2},{3,4},{5,6},{7,8},{9,10},{11,12},{13,14},{2,1},{4,3},{6,5},{... | collective-permute-start | bytes 589832 | tf_op jit(solution)/shard_map/ppermute | solution.py:880
  44.0 0.3 near4.1
  44.2 0.8 %collective-permute-start.16 = (f32[3,64,128]{2,1,0:T(8,128)S(1)}, f32[3,64,128]{2,1,0:T(8,128)S(1)}, u32[]{:S(2)}, u32[]{:S(2)}) collective-permute-start(f32[3,64,128]{2,1,0:T(8,128)S(1)} %get-tuple-element.136), channel_id=1, source_target_pairs={{0,1},{1,0},{2,3},{3,2},{4,5},{5,4},{6,7},{7,6},{8,9},{9,8},{10,11... | collective-permute-start | bytes 294920 | tf_op jit(solution)/shard_map/ppermute | solution.py:861
  45.0 0.1 collective-permute-start.17
  45.1 1.8 %collective-permute-done.15.msg = f32[3,128,128]{2,1,0:T(8,128)S(1)} collective-permute-done((f32[3,128,128]{2,1,0:T(8,128)S(1)}, f32[3,128,128]{2,1,0:T(8,128)S(1)}, u32[]{:S(2)}, u32[]{:S(2)}) %collective-permute-start.15) | collective-permute-done | bytes 196640 | tf_op jit(solution)/shard_map/ppermute | solution.py:880
  46.9 0.5 far4.1
  47.4 1.1 %near5.1 = (f32[3,2,144,128]{3,2,1,0:T(8,128)S(1)}, f32[6,2,144,128]{3,2,1,0:T(8,128)S(1)}, f32[6,2,128,128]{3,2,1,0:T(8,128)S(1)}, f32[3,2,128,128]{3,2,1,0:T(8...) custom-call(f32[3,2,144,128]{3,2,1,0:T(8,128)S(1)} %get-tuple-elemen, ...), custom_call_target="tpu_custom_call", output_to_operand_aliasing={{0}: (0, {}), {1}: (1, {}), {2}: (2, {})} | custom-call | flops 1 | bytes 1 | tf_op jit(solution)/shard_map/near5/pallas_call | solution.py:726
  48.5 2.3 %collective-permute-done.18.msg = f32[3,128,128]{2,1,0:T(8,128)S(1)} collective-permute-done((f32[3,128,128]{2,1,0:T(8,128)S(1)}, f32[3,128,128]{2,1,0:T(8,128)S(1)}, u32[]{:S(2)}, u32[]{:S(2)}) %collective-permute-start.18) | collective-permute-done | bytes 196640 | tf_op jit(solution)/shard_map/ppermute | solution.py:880
  50.8 1.1 %last.1 = (f32[3,2,144,128]{3,2,1,0:T(8,128)S(1)}, f32[6,2,144,128]{3,2,1,0:T(8,128)S(1)}, f32[6,2,128,128]{3,2,1,0:T(8,128)S(1)}, f32[3,2,128,128]{3,2,1,0:T(8,...) custom-call(f32[3,2,144,128]{3,2,1,0:T(8,128)S(1)} %get-tuple-elemen, ...), custom_call_target="tpu_custom_call", output_to_operand_aliasing={{0}: (0, {}), {1}: (1, {}), {2}: (2, {}), {3}: (8, {}), {4}... | custom-call | flops 1 | bytes 1 | tf_op jit(solution)/shard_map/last/pallas_call | solution.py:726
  (10 shorter events, 0.0 us)
Async XLA Ops:
  1.5 5.9 %collective-permute-start = (f32[8,1920]{1,0:T(8,128)S(1)}, f32[8,1920]{1,0:T(8,128)S(1)}, u32[]{:S(2)}, u32[]{:S(2)}) collective-permute-start(f32[8,1920]{1,0:T(8,128)S(1)} %get-tuple-element.81.own), channel_id=1, source_target_pairs={{0,8},{1,9},{2,10},{3,11},{4,12},{5,13},{6,14},{7,15},{16,24},{17,... | collective-permute-start | bytes 184328 | tf_op jit(solution)/shard_map/ppermute | solution.py:764
  8.3 11.3 %all-to-all-start = ((f32[8,56,128]{2,1,0:T(8,128)}), f32[8,56,128]{2,1,0:T(8,128)S(1)}, u32[]{:S(2)}, u32[]{:S(2)}) async-start(f32[8,56,128]{2,1,0:T(8,128)} %split.1), calls=%async_computation | async-start | bytes 458752 | tf_op jit(solution)/shard_map/all_to_all | solution.py:817
  14.6 9.4 %collective-permute-start.1 = (f32[3,64,128]{2,1,0:T(8,128)S(1)}, f32[3,64,128]{2,1,0:T(8,128)S(1)}, u32[]{:S(2)}, u32[]{:S(2)}) collective-permute-start(f32[3,64,128]{2,1,0:T(8,128)S(1)} %get-tuple-element.87), channel_id=1, source_target_pairs={{0,1},{1,0},{2,3},{3,2},{4,5},{5,4},{6,7},{7,6},{8,9},{9,8},{10,11... | collective-permute-start | bytes 294920 | tf_op jit(solution)/shard_map/ppermute | solution.py:807
  14.6 9.4 %collective-permute-start.2 = (f32[3,64,128]{2,1,0:T(8,128)S(1)}, f32[3,64,128]{2,1,0:T(8,128)S(1)}, u32[]{:S(2)}, u32[]{:S(2)}) collective-permute-start(f32[3,64,128]{2,1,0:T(8,128)S(1)} %get-tuple-element.88), channel_id=1, source_target_pairs={{0,1},{1,0},{2,3},{3,2},{4,5},{5,4},{6,7},{7,6},{8,9},{9,8},{10,11... | collective-permute-start | bytes 294920 | tf_op jit(solution)/shard_map/ppermute | solution.py:807
  15.1 10.3 %collective-permute-start.3 = (f32[3,128,128]{2,1,0:T(8,128)S(1)}, f32[3,128,128]{2,1,0:T(8,128)S(1)}, u32[]{:S(2)}, u32[]{:S(2)}) collective-permute-start(f32[3,128,128]{2,1,0:T(8,128)S(1)} %get-tuple-element.92), channel_id=1, source_target_pairs={{1,2},{3,4},{5,6},{7,8},{9,10},{11,12},{13,14},{2,1},{4,3},{6,5},{... | collective-permute-start | bytes 589832 | tf_op jit(solution)/shard_map/ppermute | solution.py:806
  20.2 9.8 %collective-permute-start.6 = (f32[3,128,128]{2,1,0:T(8,128)S(1)}, f32[3,128,128]{2,1,0:T(8,128)S(1)}, u32[]{:S(2)}, u32[]{:S(2)}) collective-permute-start(f32[3,128,128]{2,1,0:T(8,128)S(1)} %get-tuple-element.101), channel_id=1, source_target_pairs={{1,2},{3,4},{5,6},{7,8},{9,10},{11,12},{13,14},{2,1},{4,3},{6,5},{... | collective-permute-start | bytes 589832 | tf_op jit(solution)/shard_map/ppermute | solution.py:841
  24.3 1.8 %collective-permute-start.4 = (f32[3,64,128]{2,1,0:T(8,128)S(1)}, f32[3,64,128]{2,1,0:T(8,128)S(1)}, u32[]{:S(2)}, u32[]{:S(2)}) collective-permute-start(f32[3,64,128]{2,1,0:T(8,128)S(1)} %get-tuple-element.96), channel_id=1, source_target_pairs={{0,1},{1,0},{2,3},{3,2},{4,5},{5,4},{6,7},{7,6},{8,9},{9,8},{10,11... | collective-permute-start | bytes 294920 | tf_op jit(solution)/shard_map/ppermute | solution.py:861
  24.3 1.7 %collective-permute-start.5 = (f32[3,64,128]{2,1,0:T(8,128)S(1)}, f32[3,64,128]{2,1,0:T(8,128)S(1)}, u32[]{:S(2)}, u32[]{:S(2)}) collective-permute-start(f32[3,64,128]{2,1,0:T(8,128)S(1)} %get-tuple-element.97), channel_id=1, source_target_pairs={{0,1},{1,0},{2,3},{3,2},{4,5},{5,4},{6,7},{7,6},{8,9},{9,8},{10,11... | collective-permute-start | bytes 294920 | tf_op jit(solution)/shard_map/ppermute | solution.py:861
  26.3 7.4 %collective-permute-start.7 = (f32[3,64,128]{2,1,0:T(8,128)S(1)}, f32[3,64,128]{2,1,0:T(8,128)S(1)}, u32[]{:S(2)}, u32[]{:S(2)}) collective-permute-start(f32[3,64,128]{2,1,0:T(8,128)S(1)} %get-tuple-element.106), channel_id=1, source_target_pairs={{0,1},{1,0},{2,3},{3,2},{4,5},{5,4},{6,7},{7,6},{8,9},{9,8},{10,11... | collective-permute-start | bytes 294920 | tf_op jit(solution)/shard_map/ppermute | solution.py:861
  26.5 7.3 %collective-permute-start.8 = (f32[3,64,128]{2,1,0:T(8,128)S(1)}, f32[3,64,128]{2,1,0:T(8,128)S(1)}, u32[]{:S(2)}, u32[]{:S(2)}) collective-permute-start(f32[3,64,128]{2,1,0:T(8,128)S(1)} %get-tuple-element.107), channel_id=1, source_target_pairs={{0,1},{1,0},{2,3},{3,2},{4,5},{5,4},{6,7},{7,6},{8,9},{9,8},{10,11... | collective-permute-start | bytes 294920 | tf_op jit(solution)/shard_map/ppermute | solution.py:861
  26.9 9.1 %collective-permute-start.9 = (f32[3,128,128]{2,1,0:T(8,128)S(1)}, f32[3,128,128]{2,1,0:T(8,128)S(1)}, u32[]{:S(2)}, u32[]{:S(2)}) collective-permute-start(f32[3,128,128]{2,1,0:T(8,128)S(1)} %get-tuple-element.111), channel_id=1, source_target_pairs={{1,2},{3,4},{5,6},{7,8},{9,10},{11,12},{13,14},{2,1},{4,3},{6,5},{... | collective-permute-start | bytes 589832 | tf_op jit(solution)/shard_map/ppermute | solution.py:880
  30.6 9.9 %collective-permute-start.12 = (f32[3,128,128]{2,1,0:T(8,128)S(1)}, f32[3,128,128]{2,1,0:T(8,128)S(1)}, u32[]{:S(2)}, u32[]{:S(2)}) collective-permute-start(f32[3,128,128]{2,1,0:T(8,128)S(1)} %get-tuple-element.121), channel_id=1, source_target_pairs={{1,2},{3,4},{5,6},{7,8},{9,10},{11,12},{13,14},{2,1},{4,3},{6,5},{... | collective-permute-start | bytes 589832 | tf_op jit(solution)/shard_map/ppermute | solution.py:880
  34.0 2.6 %collective-permute-start.10 = (f32[3,64,128]{2,1,0:T(8,128)S(1)}, f32[3,64,128]{2,1,0:T(8,128)S(1)}, u32[]{:S(2)}, u32[]{:S(2)}) collective-permute-start(f32[3,64,128]{2,1,0:T(8,128)S(1)} %get-tuple-element.116), channel_id=1, source_target_pairs={{0,1},{1,0},{2,3},{3,2},{4,5},{5,4},{6,7},{7,6},{8,9},{9,8},{10,11... | collective-permute-start | bytes 294920 | tf_op jit(solution)/shard_map/ppermute | solution.py:861
  34.4 2.2 %collective-permute-start.11 = (f32[3,64,128]{2,1,0:T(8,128)S(1)}, f32[3,64,128]{2,1,0:T(8,128)S(1)}, u32[]{:S(2)}, u32[]{:S(2)}) collective-permute-start(f32[3,64,128]{2,1,0:T(8,128)S(1)} %get-tuple-element.117), channel_id=1, source_target_pairs={{0,1},{1,0},{2,3},{3,2},{4,5},{5,4},{6,7},{7,6},{8,9},{9,8},{10,11... | collective-permute-start | bytes 294920 | tf_op jit(solution)/shard_map/ppermute | solution.py:861
  36.9 7.0 %collective-permute-start.13 = (f32[3,64,128]{2,1,0:T(8,128)S(1)}, f32[3,64,128]{2,1,0:T(8,128)S(1)}, u32[]{:S(2)}, u32[]{:S(2)}) collective-permute-start(f32[3,64,128]{2,1,0:T(8,128)S(1)} %get-tuple-element.126), channel_id=1, source_target_pairs={{0,1},{1,0},{2,3},{3,2},{4,5},{5,4},{6,7},{7,6},{8,9},{9,8},{10,11... | collective-permute-start | bytes 294920 | tf_op jit(solution)/shard_map/ppermute | solution.py:861
  37.0 7.0 %collective-permute-start.14 = (f32[3,64,128]{2,1,0:T(8,128)S(1)}, f32[3,64,128]{2,1,0:T(8,128)S(1)}, u32[]{:S(2)}, u32[]{:S(2)}) collective-permute-start(f32[3,64,128]{2,1,0:T(8,128)S(1)} %get-tuple-element.127), channel_id=1, source_target_pairs={{0,1},{1,0},{2,3},{3,2},{4,5},{5,4},{6,7},{7,6},{8,9},{9,8},{10,11... | collective-permute-start | bytes 294920 | tf_op jit(solution)/shard_map/ppermute | solution.py:861
  37.5 9.4 %collective-permute-start.15 = (f32[3,128,128]{2,1,0:T(8,128)S(1)}, f32[3,128,128]{2,1,0:T(8,128)S(1)}, u32[]{:S(2)}, u32[]{:S(2)}) collective-permute-start(f32[3,128,128]{2,1,0:T(8,128)S(1)} %get-tuple-element.131), channel_id=1, source_target_pairs={{1,2},{3,4},{5,6},{7,8},{9,10},{11,12},{13,14},{2,1},{4,3},{6,5},{... | collective-permute-start | bytes 589832 | tf_op jit(solution)/shard_map/ppermute | solution.py:880
  41.2 9.6 %collective-permute-start.18 = (f32[3,128,128]{2,1,0:T(8,128)S(1)}, f32[3,128,128]{2,1,0:T(8,128)S(1)}, u32[]{:S(2)}, u32[]{:S(2)}) collective-permute-start(f32[3,128,128]{2,1,0:T(8,128)S(1)} %get-tuple-element.141), channel_id=1, source_target_pairs={{1,2},{3,4},{5,6},{7,8},{9,10},{11,12},{13,14},{2,1},{4,3},{6,5},{... | collective-permute-start | bytes 589832 | tf_op jit(solution)/shard_map/ppermute | solution.py:880
  44.2 3.1 %collective-permute-start.16 = (f32[3,64,128]{2,1,0:T(8,128)S(1)}, f32[3,64,128]{2,1,0:T(8,128)S(1)}, u32[]{:S(2)}, u32[]{:S(2)}) collective-permute-start(f32[3,64,128]{2,1,0:T(8,128)S(1)} %get-tuple-element.136), channel_id=1, source_target_pairs={{0,1},{1,0},{2,3},{3,2},{4,5},{5,4},{6,7},{7,6},{8,9},{9,8},{10,11... | collective-permute-start | bytes 294920 | tf_op jit(solution)/shard_map/ppermute | solution.py:861
  45.0 2.3 %collective-permute-start.17 = (f32[3,64,128]{2,1,0:T(8,128)S(1)}, f32[3,64,128]{2,1,0:T(8,128)S(1)}, u32[]{:S(2)}, u32[]{:S(2)}) collective-permute-start(f32[3,64,128]{2,1,0:T(8,128)S(1)} %get-tuple-element.137), channel_id=1, source_target_pairs={{0,1},{1,0},{2,3},{3,2},{4,5},{5,4},{6,7},{7,6},{8,9},{9,8},{10,11... | collective-permute-start | bytes 294920 | tf_op jit(solution)/shard_map/ppermute | solution.py:861

commit v20 on v17

--- a/solution.py
+++ b/solution.py
@@ -660,6 +660,13 @@
                 force[s, comp, cell, pl.ds(4, per, stride=2), :] = scale * panel
                 force[s, comp, cell, pl.ds(5, per, stride=2), :] = scale * lane_roll(panel, FZ)
     surface_loads(1, parts, loads, steps_table, surface, table, rows_out)
+
+
+def opening_kernel(
+    window, parts, loads, steps_table, V0, S, R, coef_ref, force, surface, V, msg, table, rows_out, W
+):
+    prepare_kernel(parts, loads, steps_table, force, surface, table, rows_out)
+    first_kernel(window, V0, S, R, coef_ref, force, surface, V, msg, W)
 
 
 def surface_kernel(parts, loads, steps_table, surface, table, rows_out):
@@ -802,25 +809,16 @@
     square = pltpu.VMEM((across, depth), f32)
     turned = (pltpu.VMEM((depth, depth), f32), pltpu.VMEM((depth, across), f32))
     ins = (parts, in_vmem(loads), in_vmem(steps_table))
-    force, surface = call(
-        prepare_kernel,
-        ins,
-        (WHOLE,) * 3,
-        (pltpu.VMEM((STEPS, 3, 3, 16, depth), f32), square),
-        (WHOLE,) * 2,
-        scratch=turned,
-        name="prepare",
-    )
     later = call(surface_kernel, ins, (WHOLE,) * 3, square, WHOLE, scratch=turned, name="surface")
-    V, early = call(
-        functools.partial(first_kernel, window),
-        tuple(in_vmem(x) for x in (V, S, R, coef, force, surface)),
-        (WHOLE,) * 6,
-        (v_type, m_type),
-        (WHOLE,) * 2,
-        scratch=(work,),
-        aliases={0: 0},
-        name="first",
+    force, surface, V, early = call(
+        functools.partial(opening_kernel, window),
+        ins + tuple(in_vmem(x) for x in (V, S, R, coef)),
+        (WHOLE,) * 7,
+        (pltpu.VMEM((STEPS, 3, 3, 16, depth), f32), square, v_type, m_type),
+        (WHOLE,) * 4,
+        scratch=(*turned, work),
+        aliases={3: 2},
+        name="opening",
     )
     early = lax.ppermute(early, "line", far)
     state = (v_type, s_type, r_type)

time: 52.3 us -> 52.2 us (level)
    pallas_call x18 -> x17, Pallas kernels: 11.2 us -> 11.1 us  [call(): pl.pallas_call(kernel, out_shape=outs, in_specs=specs, out_specs=out_spec...]
where the time goes in v20:
time: 52.2 us; the launch traced here: 51.8 us
  starting transfers between devices  30.5 us (58%)
  Pallas kernels  11.1 us (21%)
  waiting for transfers between devices  9.36 us (18%)
  between operations  0.93 us (2%)
    ppermute x4, starting transfers between devices, body(): early = lax.ppermute(msg[0], 'line', far)  12 us
    pallas_call x17, Pallas kernels, call(): pl.pallas_call(kernel, out_shape=outs, in_specs=specs, out_specs=out_spec...  11.1 us
    all_to_all x1, starting transfers between devices, body(): lax.all_to_all(parts, 'line', 0, 0, axis_index_groups=groups, tiled=True)  6.3 us
    ppermute x4, waiting for transfers between devices, body(): early = lax.ppermute(msg[0], 'line', far)  5.54 us
    ppermute x1, starting transfers between devices, body(): early = lax.ppermute(early, 'line', far)  3.74 us
    ppermute x1, starting transfers between devices, body(): msg_far = lax.ppermute(msg_far, 'line', far)  3.53 us
    ppermute x10, starting transfers between devices, body(): msg_near = [lax.ppermute(plane, 'line', near) for plane in msg]  3.12 us
    ppermute x1, waiting for transfers between devices, ahead_by(): lax.ppermute(x, 'line', [(i, i + distance) for i in range(tiles - distanc...  2.85 us
  transfers between devices with their start and end apart: 20, of which 5 were waited for; matrix products, arithmetic and copies ran while one was open for 0% of the time, Pallas kernels for 16%

profile of v20, /device:TPU:17, one launch (start us, length us, event | category | flops | bytes accessed | tf_op | source)
XLA Modules:
  0.0 51.8 jit_solution(771432252290121457)
XLA Ops:
  0.6 0.9 %pack.1 = (f32[8,1920]{1,0:T(8,128)S(1)}, f32[16,128]{1,0:T(8,128)S(1)}, f32[16,128]{1,0:T(8,128)S(1)}, s32[1,8]{1,0:T(1,128)S(1)}) custom-call(f32[8,1536]{1,0:T(8,128)} %bitcast.3, f32[16,128]{1,0:T(8,128)} %loads_in.1, s32[6,16]{1,0:T(8,128)} %entries_in.1, s32[6,16]{1,0:T(8,128)} %cells_in.1, s32[1,8]{1,0:T(1,128)} %bitcast.4), custom_call_target="tpu_custom_call" | custom-call | flops 1 | bytes 1 | tf_op jit(solution)/shard_map/pack/pallas_call | solution.py:717
  1.5 1.3 %collective-permute-start = (f32[8,1920]{1,0:T(8,128)S(1)}, f32[8,1920]{1,0:T(8,128)S(1)}, u32[]{:S(2)}, u32[]{:S(2)}) collective-permute-start(f32[8,1920]{1,0:T(8,128)S(1)} %get-tuple-element.76.own), channel_id=1, source_target_pairs={{0,8},{1,9},{2,10},{3,11},{4,12},{5,13},{6,14},{7,15},{16,24},{17,... | collective-permute-start | bytes 184328 | tf_op jit(solution)/shard_map/ppermute | solution.py:755
  2.8 1.8 %start.1 = (f32[3,2,144,128]{3,2,1,0:T(8,128)S(1)}, f32[6,2,144,128]{3,2,1,0:T(8,128)S(1)}, f32[6,2,128,128]{3,2,1,0:T(8,128)S(1)}, f32[16,128]{1,0:T(8,128)S(1)...) custom-call(f32[3,2,128,128]{3,2,1,0:T(8,128)} %velocity.1, ...), custom_call_target="tpu_custom_call" | custom-call | flops 8388608 | bytes 8388608 | tf_op jit(solution)/shard_map/start/pallas_call | solution.py:717
  4.6 2.8 %collective-permute-done.behind = f32[8,1920]{1,0:T(8,128)S(1)} collective-permute-done((f32[8,1920]{1,0:T(8,128)S(1)}, f32[8,1920]{1,0:T(8,128)S(1)}, u32[]{:S(2)}, u32[]{:S(2)}) %collective-permute-start) | collective-permute-done | bytes 61472 | tf_op jit(solution)/shard_map/ppermute | solution.py:755
  7.4 0.9 %split.1 = f32[8,56,128]{2,1,0:T(8,128)} custom-call(f32[8,1920]{1,0:T(8,128)S(1)} %get-tuple-element.76.own, f32[8,1920]{1,0:T(8,128)S(1)} %collective-permute-done.behind, s32[1,8]{1,0:T(1,128)S(1)} %get-tuple-element.77.cells, f32[16,128]{1,0:T(8,128)S(1)} %get-tuple-element.79.after_this.coef_ref), custom_call_target="tpu_custom_call" | custom-call | flops 1 | bytes 1 | tf_op jit(solution)/shard_map/split/pallas_call | solution.py:717
  8.3 6.3 %all-to-all-start = ((f32[8,56,128]{2,1,0:T(8,128)}), f32[8,56,128]{2,1,0:T(8,128)S(1)}, u32[]{:S(2)}, u32[]{:S(2)}) async-start(f32[8,56,128]{2,1,0:T(8,128)} %split.1), calls=%async_computation | async-start | bytes 458752 | tf_op jit(solution)/shard_map/all_to_all | solution.py:808
  14.6 0.0 collective-permute-start.1
  14.6 0.5 collective-permute-start.2
  15.1 3.5 %collective-permute-start.3 = (f32[3,128,128]{2,1,0:T(8,128)S(1)}, f32[3,128,128]{2,1,0:T(8,128)S(1)}, u32[]{:S(2)}, u32[]{:S(2)}) collective-permute-start(f32[3,128,128]{2,1,0:T(8,128)S(1)} %get-tuple-element.92), channel_id=1, source_target_pairs={{1,2},{3,4},{5,6},{7,8},{9,10},{11,12},{13,14},{2,1},{4,3},{6,5},{... | collective-permute-start | bytes 589832 | tf_op jit(solution)/shard_map/ppermute | solution.py:797
  18.6 0.9 %all-to-all-done.parts = f32[8,56,128]{2,1,0:T(8,128)S(1)} async-done(((f32[8,56,128]{2,1,0:T(8,128)}), f32[8,56,128]{2,1,0:T(8,128)S(1)}, u32[]{:S(2)}, u32[]{:S(2)}) %all-to-all-start) | async-done | bytes 229408 | tf_op jit(solution)/shard_map/all_to_all | solution.py:808
  19.6 0.6 %opening.1 = (f32[6,3,3,16,128]{4,3,2,1,0:T(8,128)S(1)}, f32[128,128]{1,0:T(8,128)S(1)}, f32[3,2,144,128]{3,2,1,0:T(8,128)S(1)}, f32[3,128,128]{2,1,0:T(8,128)S(1)}) custom-call(f32[8,56,128]{2,1,0:T(8,128)S(1)} %all-to-all-done.parts, f32[16,128]{1,0:T(8,128)S(1)} %get-tuple-element.80.loads, ...), custom_call_target="tpu_custom_call", output_to_operand_aliasing={{2}: (3, {})} | custom-call | flops 1 | bytes 1 | tf_op jit(solution)/shard_map/opening/pallas_call | solution.py:717
  20.1 3.7 %collective-permute-start.6 = (f32[3,128,128]{2,1,0:T(8,128)S(1)}, f32[3,128,128]{2,1,0:T(8,128)S(1)}, u32[]{:S(2)}, u32[]{:S(2)}) collective-permute-start(f32[3,128,128]{2,1,0:T(8,128)S(1)} %get-tuple-element.101), channel_id=1, source_target_pairs={{1,2},{3,4},{5,6},{7,8},{9,10},{11,12},{13,14},{2,1},{4,3},{6,5},{... | collective-permute-start | bytes 589832 | tf_op jit(solution)/shard_map/ppermute | solution.py:823
  23.9 0.0 collective-permute-done.1.upper
  23.9 0.0 collective-permute-done.2.lower
  23.9 0.3 near0.1
  24.2 0.1 collective-permute-start.4
  24.3 0.5 collective-permute-start.5
  24.8 0.6 %surface.1 = f32[128,128]{1,0:T(8,128)S(1)} custom-call(f32[8,56,128]{2,1,0:T(8,128)S(1)} %all-to-all-done.parts, f32[16,128]{1,0:T(8,128)S(1)} %get-tuple-element.80.loads, f32[16,128]{1,0:T(8,128)S(1)} %get-tuple-element.78.after_this.steps_table), custom_call_target="tpu_custom_call" | custom-call | flops 1 | bytes 1 | tf_op jit(solution)/shard_map/surface/pallas_call | solution.py:717
  25.3 0.0 collective-permute-done.3.msg
  25.3 0.6 %far0.1 = (f32[3,2,144,128]{3,2,1,0:T(8,128)S(1)}, f32[6,2,144,128]{3,2,1,0:T(8,128)S(1)}, f32[6,2,128,128]{3,2,1,0:T(8,128)S(1)}, f32[3,128,128]{2,1,0:T(8,128)S(1)}, f32[3,128,128]{2,1,0:T(8,128)S(1)}) custom-call(f32[3,2,144,128]{3,2,1,0:T(8,128)S(1)} %get-tuple-element.89.V0, ...), custom_call_target="tpu_custom_call", output_to_operand_aliasing={{0}: (0, {}), {1}: (1, {}), {2}: (2, {})} | custom-call | flops 1 | bytes 1 | tf_op jit(solution)/shard_map/far0/pallas_call | solution.py:717
  26.0 0.0 collective-permute-done.5.lower
  26.0 0.3 near1.1
  26.3 0.1 collective-permute-start.7
  26.4 0.4 collective-permute-start.8
  26.8 3.0 %collective-permute-start.9 = (f32[3,128,128]{2,1,0:T(8,128)S(1)}, f32[3,128,128]{2,1,0:T(8,128)S(1)}, u32[]{:S(2)}, u32[]{:S(2)}) collective-permute-start(f32[3,128,128]{2,1,0:T(8,128)S(1)} %get-tuple-element.111), channel_id=1, source_target_pairs={{1,2},{3,4},{5,6},{7,8},{9,10},{11,12},{13,14},{2,1},{4,3},{6,5},{... | collective-permute-start | bytes 589832 | tf_op jit(solution)/shard_map/ppermute | solution.py:862
  29.9 0.0 collective-permute-done.6.msg
  29.9 0.6 %far1.1 = (f32[3,2,144,128]{3,2,1,0:T(8,128)S(1)}, f32[6,2,144,128]{3,2,1,0:T(8,128)S(1)}, f32[6,2,128,128]{3,2,1,0:T(8,128)S(1)}, f32[3,128,128]{2,1,0:T(8,128)S(1)}, f32[3,128,128]{2,1,0:T(8,128)S(1)}) custom-call(f32[3,2,144,128]{3,2,1,0:T(8,128)S(1)} %get-tuple-element.98.V0, ...), custom_call_target="tpu_custom_call", output_to_operand_aliasing={{0}: (0, {}), {1}: (1, {}), {2}: (2, {})} | custom-call | flops 1 | bytes 1 | tf_op jit(solution)/shard_map/far1/pallas_call | solution.py:717
  30.5 3.1 %collective-permute-start.12 = (f32[3,128,128]{2,1,0:T(8,128)S(1)}, f32[3,128,128]{2,1,0:T(8,128)S(1)}, u32[]{:S(2)}, u32[]{:S(2)}) collective-permute-start(f32[3,128,128]{2,1,0:T(8,128)S(1)} %get-tuple-element.121), channel_id=1, source_target_pairs={{1,2},{3,4},{5,6},{7,8},{9,10},{11,12},{13,14},{2,1},{4,3},{6,5},{... | collective-permute-start | bytes 589832 | tf_op jit(solution)/shard_map/ppermute | solution.py:862
  33.6 0.0 collective-permute-done.7.upper
  33.7 0.3 near2.1
  33.9 0.4 collective-permute-start.10
  34.3 0.2 collective-permute-start.11
  34.5 1.4 %collective-permute-done.9.msg = f32[3,128,128]{2,1,0:T(8,128)S(1)} collective-permute-done((f32[3,128,128]{2,1,0:T(8,128)S(1)}, f32[3,128,128]{2,1,0:T(8,128)S(1)}, u32[]{:S(2)}, u32[]{:S(2)}) %collective-permute-start.9) | collective-permute-done | bytes 196640 | tf_op jit(solution)/shard_map/ppermute | solution.py:862
  35.9 0.6 %far2.1 = (f32[3,2,144,128]{3,2,1,0:T(8,128)S(1)}, f32[6,2,144,128]{3,2,1,0:T(8,128)S(1)}, f32[6,2,128,128]{3,2,1,0:T(8,128)S(1)}, f32[3,128,128]{2,1,0:T(8,128)S(1)}, f32[3,128,128]{2,1,0:T(8,128)S(1)}) custom-call(f32[3,2,144,128]{3,2,1,0:T(8,128)S(1)} %get-tuple-element.108.V0, ...), custom_call_target="tpu_custom_call", output_to_operand_aliasing={{0}: (0, {}), {1}: (1, {}), {2}: (2, {})} | custom-call | flops 1 | bytes 1 | tf_op jit(solution)/shard_map/far2/pallas_call | solution.py:717
  36.5 0.3 near3.1
  36.8 0.1 collective-permute-start.13
  36.9 0.5 collective-permute-start.14
  37.4 3.1 %collective-permute-start.15 = (f32[3,128,128]{2,1,0:T(8,128)S(1)}, f32[3,128,128]{2,1,0:T(8,128)S(1)}, u32[]{:S(2)}, u32[]{:S(2)}) collective-permute-start(f32[3,128,128]{2,1,0:T(8,128)S(1)} %get-tuple-element.131), channel_id=1, source_target_pairs={{1,2},{3,4},{5,6},{7,8},{9,10},{11,12},{13,14},{2,1},{4,3},{6,5},{... | collective-permute-start | bytes 589832 | tf_op jit(solution)/shard_map/ppermute | solution.py:862
  40.5 0.6 %far3.1 = (f32[3,2,144,128]{3,2,1,0:T(8,128)S(1)}, f32[6,2,144,128]{3,2,1,0:T(8,128)S(1)}, f32[6,2,128,128]{3,2,1,0:T(8,128)S(1)}, f32[3,128,128]{2,1,0:T(8,128)S(1)}, f32[3,128,128]{2,1,0:T(8,128)S(1)}) custom-call(f32[3,2,144,128]{3,2,1,0:T(8,128)S(1)} %get-tuple-element.118.V0, ...), custom_call_target="tpu_custom_call", output_to_operand_aliasing={{0}: (0, {}), {1}: (1, {}), {2}: (2, {})} | custom-call | flops 1 | bytes 1 | tf_op jit(solution)/shard_map/far3/pallas_call | solution.py:717
  41.1 2.7 %collective-permute-start.18 = (f32[3,128,128]{2,1,0:T(8,128)S(1)}, f32[3,128,128]{2,1,0:T(8,128)S(1)}, u32[]{:S(2)}, u32[]{:S(2)}) collective-permute-start(f32[3,128,128]{2,1,0:T(8,128)S(1)} %get-tuple-element.141), channel_id=1, source_target_pairs={{1,2},{3,4},{5,6},{7,8},{9,10},{11,12},{13,14},{2,1},{4,3},{6,5},{... | collective-permute-start | bytes 589832 | tf_op jit(solution)/shard_map/ppermute | solution.py:862
  43.9 0.3 near4.1
  44.1 0.8 %collective-permute-start.16 = (f32[3,64,128]{2,1,0:T(8,128)S(1)}, f32[3,64,128]{2,1,0:T(8,128)S(1)}, u32[]{:S(2)}, u32[]{:S(2)}) collective-permute-start(f32[3,64,128]{2,1,0:T(8,128)S(1)} %get-tuple-element.136), channel_id=1, source_target_pairs={{0,1},{1,0},{2,3},{3,2},{4,5},{5,4},{6,7},{7,6},{8,9},{9,8},{10,11... | collective-permute-start | bytes 294920 | tf_op jit(solution)/shard_map/ppermute | solution.py:843
  44.9 0.1 collective-permute-start.17
  45.0 1.8 %collective-permute-done.15.msg = f32[3,128,128]{2,1,0:T(8,128)S(1)} collective-permute-done((f32[3,128,128]{2,1,0:T(8,128)S(1)}, f32[3,128,128]{2,1,0:T(8,128)S(1)}, u32[]{:S(2)}, u32[]{:S(2)}) %collective-permute-start.15) | collective-permute-done | bytes 196640 | tf_op jit(solution)/shard_map/ppermute | solution.py:862
  46.8 0.4 far4.1
  47.3 1.1 %near5.1 = (f32[3,2,144,128]{3,2,1,0:T(8,128)S(1)}, f32[6,2,144,128]{3,2,1,0:T(8,128)S(1)}, f32[6,2,128,128]{3,2,1,0:T(8,128)S(1)}, f32[3,2,128,128]{3,2,1,0:T(8...) custom-call(f32[3,2,144,128]{3,2,1,0:T(8,128)S(1)} %get-tuple-elemen, ...), custom_call_target="tpu_custom_call", output_to_operand_aliasing={{0}: (0, {}), {1}: (1, {}), {2}: (2, {})} | custom-call | flops 1 | bytes 1 | tf_op jit(solution)/shard_map/near5/pallas_call | solution.py:717
  48.4 2.3 %collective-permute-done.18.msg = f32[3,128,128]{2,1,0:T(8,128)S(1)} collective-permute-done((f32[3,128,128]{2,1,0:T(8,128)S(1)}, f32[3,128,128]{2,1,0:T(8,128)S(1)}, u32[]{:S(2)}, u32[]{:S(2)}) %collective-permute-start.18) | collective-permute-done | bytes 196640 | tf_op jit(solution)/shard_map/ppermute | solution.py:862
  50.7 1.1 %last.1 = (f32[3,2,144,128]{3,2,1,0:T(8,128)S(1)}, f32[6,2,144,128]{3,2,1,0:T(8,128)S(1)}, f32[6,2,128,128]{3,2,1,0:T(8,128)S(1)}, f32[3,2,128,128]{3,2,1,0:T(8,...) custom-call(f32[3,2,144,128]{3,2,1,0:T(8,128)S(1)} %get-tuple-elemen, ...), custom_call_target="tpu_custom_call", output_to_operand_aliasing={{0}: (0, {}), {1}: (1, {}), {2}: (2, {}), {3}: (8, {}), {4}... | custom-call | flops 1 | bytes 1 | tf_op jit(solution)/shard_map/last/pallas_call | solution.py:717
  (9 shorter events, 0.0 us)
Async XLA Ops:
  1.5 5.9 %collective-permute-start = (f32[8,1920]{1,0:T(8,128)S(1)}, f32[8,1920]{1,0:T(8,128)S(1)}, u32[]{:S(2)}, u32[]{:S(2)}) collective-permute-start(f32[8,1920]{1,0:T(8,128)S(1)} %get-tuple-element.76.own), channel_id=1, source_target_pairs={{0,8},{1,9},{2,10},{3,11},{4,12},{5,13},{6,14},{7,15},{16,24},{17,... | collective-permute-start | bytes 184328 | tf_op jit(solution)/shard_map/ppermute | solution.py:755
  8.3 11.3 %all-to-all-start = ((f32[8,56,128]{2,1,0:T(8,128)}), f32[8,56,128]{2,1,0:T(8,128)S(1)}, u32[]{:S(2)}, u32[]{:S(2)}) async-start(f32[8,56,128]{2,1,0:T(8,128)} %split.1), calls=%async_computation | async-start | bytes 458752 | tf_op jit(solution)/shard_map/all_to_all | solution.py:808
  14.6 9.3 %collective-permute-start.1 = (f32[3,64,128]{2,1,0:T(8,128)S(1)}, f32[3,64,128]{2,1,0:T(8,128)S(1)}, u32[]{:S(2)}, u32[]{:S(2)}) collective-permute-start(f32[3,64,128]{2,1,0:T(8,128)S(1)} %get-tuple-element.87), channel_id=1, source_target_pairs={{0,1},{1,0},{2,3},{3,2},{4,5},{5,4},{6,7},{7,6},{8,9},{9,8},{10,11... | collective-permute-start | bytes 294920 | tf_op jit(solution)/shard_map/ppermute | solution.py:798
  14.6 9.3 %collective-permute-start.2 = (f32[3,64,128]{2,1,0:T(8,128)S(1)}, f32[3,64,128]{2,1,0:T(8,128)S(1)}, u32[]{:S(2)}, u32[]{:S(2)}) collective-permute-start(f32[3,64,128]{2,1,0:T(8,128)S(1)} %get-tuple-element.88), channel_id=1, source_target_pairs={{0,1},{1,0},{2,3},{3,2},{4,5},{5,4},{6,7},{7,6},{8,9},{9,8},{10,11... | collective-permute-start | bytes 294920 | tf_op jit(solution)/shard_map/ppermute | solution.py:798
  15.1 10.2 %collective-permute-start.3 = (f32[3,128,128]{2,1,0:T(8,128)S(1)}, f32[3,128,128]{2,1,0:T(8,128)S(1)}, u32[]{:S(2)}, u32[]{:S(2)}) collective-permute-start(f32[3,128,128]{2,1,0:T(8,128)S(1)} %get-tuple-element.92), channel_id=1, source_target_pairs={{1,2},{3,4},{5,6},{7,8},{9,10},{11,12},{13,14},{2,1},{4,3},{6,5},{... | collective-permute-start | bytes 589832 | tf_op jit(solution)/shard_map/ppermute | solution.py:797
  20.1 9.7 %collective-permute-start.6 = (f32[3,128,128]{2,1,0:T(8,128)S(1)}, f32[3,128,128]{2,1,0:T(8,128)S(1)}, u32[]{:S(2)}, u32[]{:S(2)}) collective-permute-start(f32[3,128,128]{2,1,0:T(8,128)S(1)} %get-tuple-element.101), channel_id=1, source_target_pairs={{1,2},{3,4},{5,6},{7,8},{9,10},{11,12},{13,14},{2,1},{4,3},{6,5},{... | collective-permute-start | bytes 589832 | tf_op jit(solution)/shard_map/ppermute | solution.py:823
  24.2 1.8 %collective-permute-start.4 = (f32[3,64,128]{2,1,0:T(8,128)S(1)}, f32[3,64,128]{2,1,0:T(8,128)S(1)}, u32[]{:S(2)}, u32[]{:S(2)}) collective-permute-start(f32[3,64,128]{2,1,0:T(8,128)S(1)} %get-tuple-element.96), channel_id=1, source_target_pairs={{0,1},{1,0},{2,3},{3,2},{4,5},{5,4},{6,7},{7,6},{8,9},{9,8},{10,11... | collective-permute-start | bytes 294920 | tf_op jit(solution)/shard_map/ppermute | solution.py:843
  24.3 1.7 %collective-permute-start.5 = (f32[3,64,128]{2,1,0:T(8,128)S(1)}, f32[3,64,128]{2,1,0:T(8,128)S(1)}, u32[]{:S(2)}, u32[]{:S(2)}) collective-permute-start(f32[3,64,128]{2,1,0:T(8,128)S(1)} %get-tuple-element.97), channel_id=1, source_target_pairs={{0,1},{1,0},{2,3},{3,2},{4,5},{5,4},{6,7},{7,6},{8,9},{9,8},{10,11... | collective-permute-start | bytes 294920 | tf_op jit(solution)/shard_map/ppermute | solution.py:843
  26.3 7.4 %collective-permute-start.7 = (f32[3,64,128]{2,1,0:T(8,128)S(1)}, f32[3,64,128]{2,1,0:T(8,128)S(1)}, u32[]{:S(2)}, u32[]{:S(2)}) collective-permute-start(f32[3,64,128]{2,1,0:T(8,128)S(1)} %get-tuple-element.106), channel_id=1, source_target_pairs={{0,1},{1,0},{2,3},{3,2},{4,5},{5,4},{6,7},{7,6},{8,9},{9,8},{10,11... | collective-permute-start | bytes 294920 | tf_op jit(solution)/shard_map/ppermute | solution.py:843
  26.4 7.3 %collective-permute-start.8 = (f32[3,64,128]{2,1,0:T(8,128)S(1)}, f32[3,64,128]{2,1,0:T(8,128)S(1)}, u32[]{:S(2)}, u32[]{:S(2)}) collective-permute-start(f32[3,64,128]{2,1,0:T(8,128)S(1)} %get-tuple-element.107), channel_id=1, source_target_pairs={{0,1},{1,0},{2,3},{3,2},{4,5},{5,4},{6,7},{7,6},{8,9},{9,8},{10,11... | collective-permute-start | bytes 294920 | tf_op jit(solution)/shard_map/ppermute | solution.py:843
  26.8 9.1 %collective-permute-start.9 = (f32[3,128,128]{2,1,0:T(8,128)S(1)}, f32[3,128,128]{2,1,0:T(8,128)S(1)}, u32[]{:S(2)}, u32[]{:S(2)}) collective-permute-start(f32[3,128,128]{2,1,0:T(8,128)S(1)} %get-tuple-element.111), channel_id=1, source_target_pairs={{1,2},{3,4},{5,6},{7,8},{9,10},{11,12},{13,14},{2,1},{4,3},{6,5},{... | collective-permute-start | bytes 589832 | tf_op jit(solution)/shard_map/ppermute | solution.py:862
  30.5 9.9 %collective-permute-start.12 = (f32[3,128,128]{2,1,0:T(8,128)S(1)}, f32[3,128,128]{2,1,0:T(8,128)S(1)}, u32[]{:S(2)}, u32[]{:S(2)}) collective-permute-start(f32[3,128,128]{2,1,0:T(8,128)S(1)} %get-tuple-element.121), channel_id=1, source_target_pairs={{1,2},{3,4},{5,6},{7,8},{9,10},{11,12},{13,14},{2,1},{4,3},{6,5},{... | collective-permute-start | bytes 589832 | tf_op jit(solution)/shard_map/ppermute | solution.py:862
  33.9 2.6 %collective-permute-start.10 = (f32[3,64,128]{2,1,0:T(8,128)S(1)}, f32[3,64,128]{2,1,0:T(8,128)S(1)}, u32[]{:S(2)}, u32[]{:S(2)}) collective-permute-start(f32[3,64,128]{2,1,0:T(8,128)S(1)} %get-tuple-element.116), channel_id=1, source_target_pairs={{0,1},{1,0},{2,3},{3,2},{4,5},{5,4},{6,7},{7,6},{8,9},{9,8},{10,11... | collective-permute-start | bytes 294920 | tf_op jit(solution)/shard_map/ppermute | solution.py:843
  34.3 2.2 %collective-permute-start.11 = (f32[3,64,128]{2,1,0:T(8,128)S(1)}, f32[3,64,128]{2,1,0:T(8,128)S(1)}, u32[]{:S(2)}, u32[]{:S(2)}) collective-permute-start(f32[3,64,128]{2,1,0:T(8,128)S(1)} %get-tuple-element.117), channel_id=1, source_target_pairs={{0,1},{1,0},{2,3},{3,2},{4,5},{5,4},{6,7},{7,6},{8,9},{9,8},{10,11... | collective-permute-start | bytes 294920 | tf_op jit(solution)/shard_map/ppermute | solution.py:843
  36.8 7.0 %collective-permute-start.13 = (f32[3,64,128]{2,1,0:T(8,128)S(1)}, f32[3,64,128]{2,1,0:T(8,128)S(1)}, u32[]{:S(2)}, u32[]{:S(2)}) collective-permute-start(f32[3,64,128]{2,1,0:T(8,128)S(1)} %get-tuple-element.126), channel_id=1, source_target_pairs={{0,1},{1,0},{2,3},{3,2},{4,5},{5,4},{6,7},{7,6},{8,9},{9,8},{10,11... | collective-permute-start | bytes 294920 | tf_op jit(solution)/shard_map/ppermute | solution.py:843
  36.9 7.0 %collective-permute-start.14 = (f32[3,64,128]{2,1,0:T(8,128)S(1)}, f32[3,64,128]{2,1,0:T(8,128)S(1)}, u32[]{:S(2)}, u32[]{:S(2)}) collective-permute-start(f32[3,64,128]{2,1,0:T(8,128)S(1)} %get-tuple-element.127), channel_id=1, source_target_pairs={{0,1},{1,0},{2,3},{3,2},{4,5},{5,4},{6,7},{7,6},{8,9},{9,8},{10,11... | collective-permute-start | bytes 294920 | tf_op jit(solution)/shard_map/ppermute | solution.py:843
  37.4 9.4 %collective-permute-start.15 = (f32[3,128,128]{2,1,0:T(8,128)S(1)}, f32[3,128,128]{2,1,0:T(8,128)S(1)}, u32[]{:S(2)}, u32[]{:S(2)}) collective-permute-start(f32[3,128,128]{2,1,0:T(8,128)S(1)} %get-tuple-element.131), channel_id=1, source_target_pairs={{1,2},{3,4},{5,6},{7,8},{9,10},{11,12},{13,14},{2,1},{4,3},{6,5},{... | collective-permute-start | bytes 589832 | tf_op jit(solution)/shard_map/ppermute | solution.py:862
  41.1 9.6 %collective-permute-start.18 = (f32[3,128,128]{2,1,0:T(8,128)S(1)}, f32[3,128,128]{2,1,0:T(8,128)S(1)}, u32[]{:S(2)}, u32[]{:S(2)}) collective-permute-start(f32[3,128,128]{2,1,0:T(8,128)S(1)} %get-tuple-element.141), channel_id=1, source_target_pairs={{1,2},{3,4},{5,6},{7,8},{9,10},{11,12},{13,14},{2,1},{4,3},{6,5},{... | collective-permute-start | bytes 589832 | tf_op jit(solution)/shard_map/ppermute | solution.py:862
  44.1 3.1 %collective-permute-start.16 = (f32[3,64,128]{2,1,0:T(8,128)S(1)}, f32[3,64,128]{2,1,0:T(8,128)S(1)}, u32[]{:S(2)}, u32[]{:S(2)}) collective-permute-start(f32[3,64,128]{2,1,0:T(8,128)S(1)} %get-tuple-element.136), channel_id=1, source_target_pairs={{0,1},{1,0},{2,3},{3,2},{4,5},{5,4},{6,7},{7,6},{8,9},{9,8},{10,11... | collective-permute-start | bytes 294920 | tf_op jit(solution)/shard_map/ppermute | solution.py:843
  44.9 2.4 %collective-permute-start.17 = (f32[3,64,128]{2,1,0:T(8,128)S(1)}, f32[3,64,128]{2,1,0:T(8,128)S(1)}, u32[]{:S(2)}, u32[]{:S(2)}) collective-permute-start(f32[3,64,128]{2,1,0:T(8,128)S(1)} %get-tuple-element.137), channel_id=1, source_target_pairs={{0,1},{1,0},{2,3},{3,2},{4,5},{5,4},{6,7},{7,6},{8,9},{9,8},{10,11... | collective-permute-start | bytes 294920 | tf_op jit(solution)/shard_map/ppermute | solution.py:843
